TPU v7x, 32 devices: a whole 2x2x4 slice. The times are simulated.
32 devices in a mesh: dp: 2 (over y), view: 4 (over x, core), head: 4 (over z).
Axes of the slice: x: 2, y: 2, z: 4, core: 2. Of those that a mesh axis runs over, the one named last changes fastest.
Arguments:
- normed: bfloat16 [2, 4, 256, 3072], P('dp', 'view'), may hold values from -6 to 6
- queries: bfloat16 [2, 4, 256, 3072], P('dp', 'view', None, 'head'), may hold values from -180 to 180
- saved_keys: bfloat16 [2, 4, 256, 3072], P('dp', 'view', None, 'head'), may hold values from -4.5 to 4.5
- saved_values: bfloat16 [2, 4, 256, 3072], P('dp', 'view', None, 'head'), may hold values from -6 to 6
- output_grad: bfloat16 [2, 4, 256, 3072], P('dp', 'view', None, 'head'), may hold values from -200 to 200
- view_links: int32 [4, 2], P('view'), may hold values from -1 to 3, as said below
- query_weight: bfloat16 [3072, 3072], P(('dp', 'view'), 'head'), may hold values from -0.109375 to 0.109375
- key_weight: bfloat16 [3072, 3072], P(('dp', 'view'), 'head'), may hold values from -0.109375 to 0.109375
- value_weight: bfloat16 [3072, 3072], P(('dp', 'view'), 'head'), may hold values from -0.109375 to 0.109375
Outputs:
- input_grad: bfloat16 [2, 4, 256, 3072], P('dp', 'view', None, 'head')
- grad_query: float32 [3072, 3072], P(('dp', 'view'), 'head')
- grad_key: float32 [3072, 3072], P(('dp', 'view'), 'head')
- grad_value: float32 [3072, 3072], P(('dp', 'view'), 'head')
Inputs may be any that keep to these rules, and one draw needn't show every extreme that they name: `view_links`: row v holds (v - 1) mod 4 or -1 and then (v + 1) mod 4 or -1; -1 marks a link that view v does not attend.
All inputs are finite; a program needn't handle non-finite values.
Results may differ from a plain program's by a relative error of at most 0.0057.
Values may be sent and summed in bfloat16 or wider, within the bound.
No kernel may reach another device: no remote copies, remote signals or barrier semaphores. Data moves between devices by JAX's collectives and lax.ppermute only.
A program may use at most 128 MiB of HBM per device.

v0:
```python
import jax
import jax.numpy as jnp
from jax import lax
from jax.sharding import PartitionSpec as P

HD = 128


def shifted(value, axis, steps):
    count = lax.axis_size(axis)
    pairs = [(source, (source + steps) % count) for source in range(count)]
    return lax.ppermute(value, axis, pairs)


def attend(query_rows, grad_rows, blocks, usable, scaling):
    batch_size, length, col_count = query_rows.shape
    heads_here = col_count // HD
    key_heads = blocks[..., :col_count].reshape(batch_size, 3 * length, heads_here, HD)
    value_heads = blocks[..., col_count:].reshape(batch_size, 3 * length, heads_here, HD)
    query_heads = query_rows.reshape(batch_size, length, heads_here, HD)
    grad_heads = grad_rows.reshape(batch_size, length, heads_here, HD)
    scores = (
        jnp.einsum("bshd,bthd->bhst", query_heads, key_heads, preferred_element_type=jnp.float32)
        * scaling
    )
    scores = jnp.where(usable, scores, -1e30)
    largest = jnp.max(scores, axis=-1, keepdims=True)
    powers = jnp.exp(scores - largest)
    attn_probs = powers / jnp.sum(powers, axis=-1, keepdims=True)
    probs_half = attn_probs.astype(jnp.bfloat16)
    prob_grad = jnp.einsum(
        "bshd,bthd->bhst", grad_heads, value_heads, preferred_element_type=jnp.float32
    )
    row_delta = jnp.sum(attn_probs * prob_grad, axis=-1, keepdims=True)
    score_grad = (scaling * attn_probs * (prob_grad - row_delta)).astype(jnp.bfloat16)
    query_grad = jnp.einsum(
        "bhst,bthd->bshd", score_grad, key_heads, preferred_element_type=jnp.float32
    )
    key_grad = jnp.einsum(
        "bhst,bshd->bthd", score_grad, query_heads, preferred_element_type=jnp.float32
    )
    value_grad = jnp.einsum(
        "bhst,bshd->bthd", probs_half, grad_heads, preferred_element_type=jnp.float32
    )
    query_grad = query_grad.reshape(batch_size, length, col_count)
    key_grad = key_grad.reshape(batch_size, 3, length, col_count)
    value_grad = value_grad.reshape(batch_size, 3, length, col_count)
    return (query_grad, jnp.concatenate([key_grad, value_grad], axis=-1))


def body(
    normed,
    queries,
    saved_keys,
    saved_values,
    output_grad,
    view_links,
    query_weight,
    key_weight,
    value_weight,
):
    scaling = HD ** (-0.5)
    batch_size, view_count, length, col_count = queries.shape
    model_width = normed.shape[-1]
    pairs = jnp.concatenate([saved_keys, saved_values], axis=-1)
    from_lower = shifted(pairs, "view", 1)
    from_upper = shifted(pairs, "view", -1)
    extended = jnp.concatenate([from_lower, pairs, from_upper], axis=1)
    block_index = jnp.arange(3 * length) // length
    pair_grads = jnp.zeros(extended.shape, jnp.float32)
    link_flags = view_links[0] >= 0
    usable = jnp.where(
        block_index == 0, link_flags[0], jnp.where(block_index == 2, link_flags[1], True)
    )
    query_grad, block_grad = attend(queries[:, 0], output_grad[:, 0], extended, usable, scaling)
    query_grads = [query_grad]
    pair_grads = pair_grads.at[:, 0:3].add(block_grad)
    row_count = batch_size * view_count * length
    query_half = jnp.stack(query_grads, axis=1).astype(jnp.bfloat16).reshape(row_count, col_count)
    flat_input = normed.reshape(row_count, model_width)
    mean_scale = 1.0 / (lax.axis_size("dp") * batch_size * lax.axis_size("view") * view_count)
    from_lower_grads = shifted(pair_grads[:, -1:], "view", 1)
    from_upper_grads = shifted(pair_grads[:, :1], "view", -1)
    own_grads = pair_grads[:, 1 : view_count + 1]
    own_grads = own_grads.at[:, :1].add(from_lower_grads)
    own_grads = own_grads.at[:, -1:].add(from_upper_grads)
    key_half = own_grads[..., :col_count].astype(jnp.bfloat16).reshape(row_count, col_count)
    value_half = own_grads[..., col_count:].astype(jnp.bfloat16).reshape(row_count, col_count)
    all_grads = jnp.concatenate([query_half, key_half, value_half], axis=-1)
    grads_three = all_grads.reshape(row_count, 3, col_count)
    stacked = jnp.stack([query_weight, key_weight, value_weight])
    partial_input = jnp.einsum(
        "ric,ipc->rp",
        grads_three,
        lax.all_gather(stacked, ("dp", "view"), axis=1, tiled=True),
        preferred_element_type=jnp.float32,
    )
    summed_input = lax.psum_scatter(partial_input, "head", scatter_dimension=1, tiled=True)
    input_grad = summed_input.astype(jnp.bfloat16).reshape(
        batch_size, view_count, length, model_width // lax.axis_size("head")
    )
    product = lax.dot_general(
        flat_input, all_grads, (((0,), (0,)), ((), ())), preferred_element_type=jnp.float32
    )
    together = lax.psum_scatter(
        product * mean_scale, ("dp", "view"), scatter_dimension=0, tiled=True
    )
    grad_query = together[:, :col_count]
    grad_key = together[:, col_count : 2 * col_count]
    grad_value = together[:, 2 * col_count :]
    return (input_grad, grad_query, grad_key, grad_value)


def solution(mesh):
    placed = (
        P("dp", "view", None, None),
        P("dp", "view", None, "head"),
        P("dp", "view", None, "head"),
        P("dp", "view", None, "head"),
        P("dp", "view", None, "head"),
        P("view", None),
        P(("dp", "view"), "head"),
        P(("dp", "view"), "head"),
        P(("dp", "view"), "head"),
    )
    return jax.shard_map(
        body,
        mesh=mesh,
        in_specs=placed,
        out_specs=(
            P("dp", "view", None, "head"),
            P(("dp", "view"), "head"),
            P(("dp", "view"), "head"),
            P(("dp", "view"), "head"),
        ),
        check_vma=False,
    )
```

profile of v0, /device:TPU:16, one launch (start us, length us, event | category | flops | bytes accessed | tf_op | source)
XLA Modules:
  0.0 397.3 jit_solution(5199153229653786730)
XLA Ops:
  7.2 0.0 copy-start
  7.2 0.0 all-gather.2.cloned.1.call-start
  7.2 0.0 copy-start.8
  7.2 0.0 copy-start.9
  7.2 3.0 pad_maximum_fusion.1
  10.2 0.0 all-gather.2.cloned.1.call-update
  10.2 0.0 reduce-scatter.3.cloned.1.call-start
  10.3 0.0 copy-done.8
  10.3 0.0 copy-done.9
  10.4 1.0 collective-permute-start.1
  11.4 0.0 collective-permute-start
  11.4 0.0 copy-done.10
  11.4 0.9 copy.24
  12.3 1.9 copy.27
  14.2 0.0 copy-done.11
  14.2 0.6 fusion.47
  14.8 1.3 fusion.37
  16.1 21.4 %collective-permute-done.1 = bf16[1,1,256,1536]{3,2,1,0:T(8,128)(2,1)S(1)} collective-permute-done((bf16[1,1,256,1536]{3,2,1,0:T(8,128)(2,1)S(1)}, bf16[1,1,256,1536]{3,2,1,0:T(8,128)(2,1)S(1)}, u32[]{:S(2)}, u32[]{:S(2)}) %collective-permute-start.1) | collective-permute-done | bytes 786464 | tf_op jit(solution)/shard_map/ppermute | solution.py:12
  37.5 1.2 collective-permute-done
  38.7 1.4 pad_maximum_fusion
  40.1 1.6 fusion.46
  41.6 2.8 reshape.229
  44.5 1.7 copy.30
  46.2 3.9 reshape.231
  50.1 4.0 fusion.48
  54.0 3.2 fusion.13
  57.3 3.1 copy.35
  60.4 4.2 %reshape.234 = f32[1,3,256,768]{3,2,1,0:T(8,128)} reshape(f32[1,768,6,128]{3,2,1,0:T(8,128)} %copy.35) | data formatting | bytes 4718592 | tf_op jit(solution)/shard_map/reshape | solution.py:47
  64.6 3.9 fusion.1
  68.4 0.3 slice-done.1
  68.7 0.8 fusion.3
  69.5 0.2 copy-done.7
  69.7 0.8 convolution_bitcast_fusion.1
  70.4 0.6 copy-done.1
  71.1 3.0 copy.33
  74.1 4.1 %reshape.233 = f32[1,3,256,768]{3,2,1,0:T(8,128)} reshape(f32[1,768,6,128]{3,2,1,0:T(8,128)} %copy.33) | data formatting | bytes 4718592 | tf_op jit(solution)/shard_map/reshape | solution.py:46
  78.2 2.2 constant_dynamic-update-slice_fusion.3
  80.4 0.2 copy-done.4
  80.6 0.3 constant_dynamic-update-slice_fusion.2
  80.9 1.9 fusion.44
  82.8 1.5 copy-done.3
  84.3 0.0 collective-permute-start.2
  84.3 1.7 collective-permute-start.3
  86.0 0.0 copy-done.2
  86.0 0.5 convolution_convert_fusion
  86.5 0.9 copy.36
  87.5 41.7 %collective-permute-done.2 = f32[1,1,256,1536]{3,2,1,0:T(8,128)} collective-permute-done((f32[1,1,256,1536]{3,2,1,0:T(8,128)}, f32[1,1,256,1536]{3,2,1,0:T(8,128)}, u32[]{:S(2)}, u32[]{:S(2)}) %collective-permute-start.2) | collective-permute-done | bytes 1572896 | tf_op jit(solution)/shard_map/ppermute | solution.py:12
  129.1 0.0 collective-permute-done.3
  129.1 2.7 fusion.17
  131.8 0.1 slice_bitcast_fusion.2
  131.9 0.0 all-gather.2.cloned.1.call-done
  131.9 10.7 %convolution_bitcast_fusion = f32[256,3072]{1,0:T(8,128)} fusion(bf16[3,3072,768]{2,1,0:T(8,128)(2,1)} %all-gather.2.cloned.1.call-done, bf16[256,1,768]{2,0,1:T(8,128)(2,1)S(1)} %get-tuple-element.81, bf16[256,1,768]{2,0,1:T(8,128)(2,1)S(1)} %get-tuple-element.82, bf16[256,1,768]{2,0,1:T(8,128)(2,1)} %copy.36), kind=kOutput, calls=%fused_computation.12 | convolution fusion | flops 3625058304 | bytes 18481152 | tf_op jit(solution)/shard_map/ric,ipc->rp/dot_general | solution.py:92
  142.6 0.0 reduce-scatter.3.cloned.1.call-update
  142.6 0.0 reduce-scatter.5.cloned.1.call-start
  142.7 0.2 copy.37
  142.9 11.9 %multiply_bitcast_fusion = f32[3072,2304]{0,1:T(8,128)} fusion(bf16[1,1,256,3072]{3,2,1,0:T(8,128)(2,1)S(1)} %copy-done, bf16[256,768]{1,0:T(8,128)(2,1)S(1)} %get-tuple-element.80, bf16[256,768]{1,0:T(8,128)(2,1)S(1)} %get-tuple-element.79, bf16[256,768]{1,0:T(8,128)(2,1)S(1)} %copy.37), kind=kOutput, calls=%fused_computation.1 | convolution fusion | flops 3634495488 | bytes 31064064 | tf_op jit(solution)/shard_map/dot_general | solution.py:102
  154.8 0.0 reduce-scatter.5.cloned.1.call-update
  154.8 48.7 %reduce-scatter.3.cloned.1.call-done = f32[256,768]{1,0:T(8,128)} async-done(((f32[256,3072]{1,0:T(8,128)}), f32[256,768]{1,0:T(8,128)}) %reduce-scatter.3.cloned.1.call-update) | async-done | bytes 786448 | tf_op jit(solution)/shard_map/reduce_scatter | solution.py:98
  203.5 1.9 convert_bitcast_fusion
  205.4 175.1 %reduce-scatter.5.cloned.1.call-done = f32[384,2304]{0,1:T(8,128)} async-done(((f32[3072,2304]{0,1:T(8,128)}), f32[384,2304]{0,1:T(8,128)}) %reduce-scatter.5.cloned.1.call-update) | async-done | bytes 3538960 | tf_op jit(solution)/shard_map/reduce_scatter | solution.py:105
  380.5 3.6 fusion.45
  384.1 2.7 copy.40
  386.7 2.7 copy.39
  389.4 1.4 copy.38
  (19 shorter events, 0.1 us)
Async XLA Ops:
  7.2 135.7 %copy-start = (bf16[1,1,256,3072]{3,2,1,0:T(8,128)(2,1)S(1)}, bf16[1,1,256,3072]{3,2,1,0:T(8,128)(2,1)}, u32[]{:S(2)}) copy-start(bf16[1,1,256,3072]{3,2,1,0:T(8,128)(2,1)} %param.21) | copy-start | bytes 4718596
  7.2 124.7 %all-gather.2.cloned.1.call-start = ((), (), s32[]{:S(2)}) async-start(), calls=%async_computation.2 | async-start | bytes 15925248 | tf_op jit(solution)/shard_map/all_gather | solution.py:95
  7.2 3.1 copy-start.8
  7.2 3.1 copy-start.9
  10.2 1.2 copy-start.10
  10.2 4.0 %copy-start.11 = (s32[1,2]{1,0:T(1,128)S(1)}, s32[1,2]{1,0:T(1,128)}, u32[]{:S(2)}) copy-start(s32[1,2]{1,0:T(1,128)} %param.26) | copy-start | bytes 28
  10.2 193.2 %reduce-scatter.3.cloned.1.call-start = ((), (), s32[]{:S(2)}) async-start(), calls=%async_computation.3 | async-start | bytes 3932160 | tf_op jit(solution)/shard_map/reduce_scatter | solution.py:98
  10.4 27.1 %collective-permute-start.1 = (bf16[1,1,256,1536]{3,2,1,0:T(8,128)(2,1)S(1)}, bf16[1,1,256,1536]{3,2,1,0:T(8,128)(2,1)S(1)}, u32[]{:S(2)}, u32[]{:S(2)}) collective-permute-start(bf16[1,1,256,1536]{3,2,1,0:T(8,128)(2,1)S(1)} %constant_dynamic-update-slice_fusion), channel_id=1, source_target_pairs={{0,12},{4,0},{8,4},{12,8},{1,13},{5,1},{9,5},{13,9},{2,14},{6,2},{... | collective-permute-start | bytes 2359304 | tf_op jit(solution)/shard_map/ppermute | solution.py:12
  11.4 27.3 %collective-permute-start = (bf16[1,1,256,1536]{3,2,1,0:T(8,128)(2,1)S(1)}, bf16[1,1,256,1536]{3,2,1,0:T(8,128)(2,1)}, u32[]{:S(2)}, u32[]{:S(2)}) collective-permute-start(bf16[1,1,256,1536]{3,2,1,0:T(8,128)(2,1)S(1)} %constant_dynamic-update-slice_fusion), channel_id=1, source_target_pairs={{0,4},{4,8},{8,12},{12,0},{1,5},{5,9},{9,13},{13,1},{2,6},{6,10},{... | collective-permute-start | bytes 2359304 | tf_op jit(solution)/shard_map/ppermute | solution.py:12
  46.2 3.9 copy-start.5
  46.2 3.9 copy-start.6
  60.4 8.0 %slice-start = ((s8[4718592]{0:T(1024)(128)(4,1)}), s8[524288]{0:T(1024)(128)(4,1)S(1)}, s32[]{:S(2)}) async-start(s8[4718592]{0:T(1024)(128)(4,1)} %bitcast.78), calls=%async_computation.5 | async-start | bytes 1048576
  64.5 4.1 %slice-start.1 = ((s8[4718592]{0:T(1024)(128)(4,1)}), s8[4194304]{0:T(1024)(128)(4,1)S(1)}, s32[]{:S(2)}) async-start(s8[4718592]{0:T(1024)(128)(4,1)} %bitcast.78), calls=%async_computation.6 | async-start | bytes 8388608
  68.7 1.0 copy-start.7
  69.7 1.4 copy-start.1
  78.2 2.4 copy-start.4
  80.9 3.4 copy-start.3
  80.9 5.1 %copy-start.2 = (bf16[6,256,768]{1,2,0:T(8,128)(2,1)S(1)}, bf16[6,256,768]{1,2,0:T(8,128)(2,1)}, u32[]{:S(2)}) copy-start(bf16[6,256,768]{1,2,0:T(8,128)(2,1)} %copy-done.1) | copy-start | bytes 7077892
  84.3 44.8 %collective-permute-start.2 = (f32[1,1,256,1536]{3,2,1,0:T(8,128)}, f32[1,1,256,1536]{3,2,1,0:T(8,128)}, u32[]{:S(2)}, u32[]{:S(2)}) collective-permute-start(f32[1,1,256,1536]{3,2,1,0:T(8,128)} %get-tuple-element.72), channel_id=1, source_target_pairs={{0,4},{4,8},{8,12},{12,0},{1,5},{5,9},{9,13},{13,1},{2,6},{6,10},{... | collective-permute-start | bytes 4718600 | tf_op jit(solution)/shard_map/ppermute | solution.py:12
  84.3 44.8 %collective-permute-start.3 = (f32[1,1,256,1536]{3,2,1,0:T(8,128)}, f32[1,1,256,1536]{3,2,1,0:T(8,128)}, u32[]{:S(2)}, u32[]{:S(2)}) collective-permute-start(f32[1,1,256,1536]{3,2,1,0:T(8,128)} %get-tuple-element.73), channel_id=1, source_target_pairs={{0,12},{4,0},{8,4},{12,8},{1,13},{5,1},{9,5},{13,9},{2,14},{6,2},{... | collective-permute-start | bytes 4718600 | tf_op jit(solution)/shard_map/ppermute | solution.py:12
  142.6 237.9 %reduce-scatter.5.cloned.1.call-start = ((), (), s32[]{:S(2)}) async-start(), calls=%async_computation.4 | async-start | bytes 31850496 | tf_op jit(solution)/shard_map/reduce_scatter | solution.py:105
Sparse Core Ops, SparseCore 0:
  10.4 95.3 all-gather.1
  142.7 60.6 reduce-scatter.2
  207.2 173.2 reduce-scatter.4
where the time goes:
time: 400 us; the launch traced here: 397 us
  waiting for transfers between devices  288 us (72%)
  local copies, waits for them, and re-layouts  46.5 us (12%)
  matrix products  34.9 us (9%)
  between operations  13.9 us (3%)
  other arithmetic  11.1 us (3%)
    reduce_scatter x1, waiting for transfers between devices, body(): lax.psum_scatter(product * mean_scale, ('dp', 'view'), scatter_dimension=...  175 us
    ppermute x4, waiting for transfers between devices, shifted(): return lax.ppermute(value, axis, pairs)  64.2 us
    reduce_scatter x1, waiting for transfers between devices, body(): lax.psum_scatter(partial_input, 'head', scatter_dimension=1, tiled=True)  48.7 us
    unnamed x35, local copies, waits for them, and re-layouts  14.5 us
    dot_general x1, matrix products, body(): lax.dot_general(flat_input, all_grads, (((0,), (0,)), ((), ())), preferre...  11.9 us
    dot_general x1, matrix products, body(): jnp.einsum('ric,ipc->rp', grads_three, lax.all_gather(stacked, ('dp', 'vi...  10.7 us
    another operation x3, local copies, waits for them, and re-layouts  8.4 us
  transfers between devices with their start and end apart: 7, of which 5 were waited for; matrix products, arithmetic and copies ran while one was open for 17% of the time, Pallas kernels for 0%

commit v1 on v0

--- a/solution.py
+++ b/solution.py
@@ -1,9 +1,15 @@
+import functools
+
 import jax
 import jax.numpy as jnp
 from jax import lax
+from jax.experimental import pallas as pl
+from jax.experimental.pallas import tpu as pltpu
 from jax.sharding import PartitionSpec as P
 
 HD = 128
+LOG2E = 1.4426950408889634
+MIB = 1024 * 1024
 
 
 def shifted(value, axis, steps):
@@ -48,7 +54,7 @@
     return (query_grad, jnp.concatenate([key_grad, value_grad], axis=-1))
 
 
-def body(
+def halo_body(
     normed,
     queries,
     saved_keys,
@@ -111,7 +117,355 @@
     return (input_grad, grad_query, grad_key, grad_value)
 
 
+MATE, XSAME, XCROSS = (0, 1), (0, 2), (0, 3)
+YSAME, YCROSS, DIAGONAL = (1, 0), (1, 1), (1, 2)
+
+
+def flipped(value, flip):
+    prompts, views = lax.axis_size("dp"), lax.axis_size("view")
+    pairs = [
+        (y * views + v, (y ^ flip[0]) * views + (v ^ flip[1]))
+        for y in range(prompts)
+        for v in range(views)
+    ]
+    return lax.ppermute(value, ("dp", "view"), pairs)
+
+
+def core_of():
+    return lax.rem(lax.axis_index("view"), 2)
+
+
+def lanes(start, size):
+    return pl.ds(pl.multiple_of(start, HD), size)
+
+
+def whole(space=pltpu.VMEM):
+    return pl.BlockSpec(memory_space=space)
+
+
+def pack_kernel(per_core, core_ref, q_ref, k_ref, v_ref, g_ref, *out_refs):
+    core = core_ref[0]
+    width = per_core * HD
+    for part, half in enumerate((core, 1 - core)):
+        for head in range(per_core):
+            out = out_refs[part * per_core + head]
+            for place, source in enumerate((q_ref, k_ref, v_ref, g_ref)):
+                out[:, place * HD : (place + 1) * HD] = source[
+                    :, lanes(half * width + head * HD, HD)
+                ]
+
+
+def pack(core, q, k, v, g):
+    length, cols = q.shape
+    per_core = cols // HD // 2
+    out = jax.ShapeDtypeStruct((length, 4 * HD), q.dtype)
+    packed = pl.pallas_call(
+        functools.partial(pack_kernel, per_core),
+        out_shape=[out] * (2 * per_core),
+        in_specs=[whole(pltpu.SMEM)] + [whole()] * 4,
+        out_specs=[whole()] * (2 * per_core),
+        name="pack_heads",
+    )(core, q, k, v, g)
+    return packed[:per_core], packed[per_core:]
+
+
+def dot_last(a, b):
+    return lax.dot_general(a, b, (((1,), (1,)), ((), ())), preferred_element_type=jnp.float32)
+
+
+def dot_first(a, b):
+    return lax.dot_general(a, b, (((0,), (0,)), ((), ())), preferred_element_type=jnp.float32)
+
+
+def attention_kernel(scaling, links_ref, view_ref, x0, x1, x2, x3, keep_ref, send_ref, kacc, vacc):
+    xs = (x0, x1, x2, x3)
+    view = view_ref[0]
+    odd = lax.rem(view, 2)
+    factor = scaling * LOG2E
+    seen = set()
+    for e in range(4):
+        place = jnp.bitwise_xor(view, e)
+        below = links_ref[place, odd]
+        above = links_ref[place, 1 - odd]
+        far_below = jnp.where(below >= 0, 0.0, 1e30).astype(jnp.float32)
+        far_above = jnp.where(above >= 0, 0.0, 1e30).astype(jnp.float32)
+        blocks = ((e + 3) % 4, e, (e + 1) % 4)
+        q = xs[e][:, 0:HD]
+        g = xs[e][:, 3 * HD : 4 * HD]
+        scores = [dot_last(xs[f][:, HD : 2 * HD], q) for f in blocks]
+        tops = [jnp.max(s, axis=0, keepdims=True) for s in scores]
+        top = jnp.maximum(tops[1], jnp.maximum(tops[0] - far_below, tops[2] - far_above))
+        offsets = (top + far_below, top, top + far_above)
+        powers = [jnp.exp2((s - o) * factor) for s, o in zip(scores, offsets)]
+        total = sum(jnp.sum(p, axis=0, keepdims=True) for p in powers)
+        inverse = 1.0 / total
+        prob_grads = [dot_last(xs[f][:, 2 * HD : 3 * HD], g) for f in blocks]
+        delta = inverse * sum(
+            jnp.sum(p * d, axis=0, keepdims=True) for p, d in zip(powers, prob_grads)
+        )
+        query_grad = None
+        for f, p, d in zip(blocks, powers, prob_grads):
+            probs = p * inverse
+            score_grad = (probs * (d - delta)).astype(jnp.bfloat16)
+            probs_half = probs.astype(jnp.bfloat16)
+            part = dot_first(score_grad, xs[f][:, HD : 2 * HD])
+            query_grad = part if query_grad is None else query_grad + part
+            key_part = jnp.dot(score_grad, q, preferred_element_type=jnp.float32)
+            value_part = jnp.dot(probs_half, g, preferred_element_type=jnp.float32)
+            if f in seen:
+                kacc[f] += key_part
+                vacc[f] += value_part
+            else:
+                seen.add(f)
+                kacc[f] = key_part
+                vacc[f] = value_part
+        out = (keep_ref, send_ref)[e % 2]
+        out[e // 2, :, 0:HD] = (query_grad * scaling).astype(out.dtype)
+    for f in range(4):
+        out = (keep_ref, send_ref)[f % 2]
+        out[f // 2, :, HD : 2 * HD] = (kacc[f] * scaling).astype(out.dtype)
+        out[f // 2, :, 2 * HD : 3 * HD] = vacc[f].astype(out.dtype)
+
+
+def attention(links, view, blocks):
+    length = blocks[0].shape[0]
+    out = jax.ShapeDtypeStruct((2, length, 3 * HD), jnp.bfloat16)
+    return pl.pallas_call(
+        functools.partial(attention_kernel, HD ** (-0.5)),
+        out_shape=[out, out],
+        in_specs=[whole(pltpu.SMEM)] * 2 + [whole()] * 4,
+        out_specs=[whole()] * 2,
+        scratch_shapes=[pltpu.VMEM((4, length, HD), jnp.float32)] * 2,
+        compiler_params=pltpu.CompilerParams(vmem_limit_bytes=32 * MIB),
+        cost_estimate=pl.CostEstimate(
+            flops=4 * 5 * 2 * length * 3 * length * HD * 2,
+            bytes_accessed=2 * length * 7 * HD * 4,
+            transcendentals=12 * length * length,
+        ),
+        name="attention_gradients",
+    )(links, view, *blocks)
+
+
+def input_kernel(per_core, core_ref, *refs):
+    own_refs = refs[:per_core]
+    other_refs = refs[per_core : 2 * per_core]
+    own_weights = refs[2 * per_core : 2 * per_core + 3]
+    mate_weights = refs[2 * per_core + 3 : 2 * per_core + 6]
+    out_ref = refs[2 * per_core + 6]
+    core = core_ref[0]
+    width = per_core * HD
+    rows = own_weights[0].shape[0]
+    blocks, length, depth = own_refs[0].shape
+    for weights, place in ((own_weights, core), (mate_weights, 1 - core)):
+        total = None
+        for grads, half in ((own_refs, core), (other_refs, 1 - core)):
+            left = jnp.concatenate([g[...].reshape(blocks * length, depth) for g in grads], axis=1)
+            right = jnp.concatenate(
+                [
+                    w[:, lanes(half * width + head * HD, HD)]
+                    for head in range(per_core)
+                    for w in weights
+                ],
+                axis=1,
+            )
+            part = dot_last(left, right)
+            total = part if total is None else total + part
+        out_ref[:, lanes(place * rows, rows)] = total.astype(out_ref.dtype)
+
+
+def input_product(core, own, other, own_weights, mate_weights):
+    per_core = len(own)
+    blocks, length, _ = own[0].shape
+    rows, cols = own_weights[0].shape
+    return pl.pallas_call(
+        functools.partial(input_kernel, per_core),
+        out_shape=jax.ShapeDtypeStruct((blocks * length, 2 * rows), jnp.bfloat16),
+        in_specs=[whole(pltpu.SMEM)] + [whole()] * (2 * per_core + 6),
+        out_specs=whole(),
+        compiler_params=pltpu.CompilerParams(vmem_limit_bytes=32 * MIB),
+        cost_estimate=pl.CostEstimate(
+            flops=2 * blocks * length * 2 * rows * 3 * cols,
+            bytes_accessed=2 * (blocks * length * (2 * rows + 3 * cols) + 6 * rows * cols),
+            transcendentals=0,
+        ),
+        name="input_gradient",
+    )(core, *own, *other, *own_weights, *mate_weights)
+
+
+def token_blocks(per_core, grad_refs):
+    for prompt in range(2):
+        for e in range(4):
+            yield prompt * 4 + e, [
+                grad_refs[(prompt * per_core + head) * 2 + e % 2][e // 2]
+                for head in range(per_core)
+            ]
+
+
+def weight_kernel(per_core, mean_scale, core_ref, *refs):
+    normed_refs = refs[:8]
+    grad_refs = refs[8 : 8 + 4 * per_core]
+    out_ref = refs[8 + 4 * per_core]
+    rows = out_ref.shape[0]
+    start = (1 - core_ref[0]) * rows
+    total = None
+    for block, grads in token_blocks(per_core, grad_refs):
+        part = dot_first(normed_refs[block][:, lanes(start, rows)], jnp.concatenate(grads, axis=1))
+        total = part if total is None else total + part
+    out_ref[...] = total * mean_scale
+
+
+def weight_final_kernel(per_core, mean_scale, core_ref, *refs):
+    normed_refs = refs[:8]
+    grad_refs = refs[8 : 8 + 4 * per_core]
+    mate_ref = refs[8 + 4 * per_core]
+    out_refs = refs[9 + 4 * per_core : 12 + 4 * per_core]
+    core = core_ref[0]
+    rows = mate_ref.shape[0]
+    width = per_core * HD
+    total = None
+    for block, grads in token_blocks(per_core, grad_refs):
+        part = dot_first(
+            normed_refs[block][:, lanes(core * rows, rows)], jnp.concatenate(grads, axis=1)
+        )
+        total = part if total is None else total + part
+    total = total * mean_scale
+    for head in range(per_core):
+        for kind in range(3):
+            column = (head * 3 + kind) * HD
+            out_refs[kind][:, lanes(core * width + head * HD, HD)] = total[:, column : column + HD]
+            out_refs[kind][:, lanes((1 - core) * width + head * HD, HD)] = mate_ref[
+                :, column : column + HD
+            ]
+
+
+def weight_cost(rows, cols, tokens):
+    return pl.CostEstimate(
+        flops=2 * rows * cols * tokens,
+        bytes_accessed=2 * tokens * (2 * rows + cols) + 4 * rows * cols,
+        transcendentals=0,
+    )
+
+
+def gather_body(
+    normed,
+    queries,
+    saved_keys,
+    saved_values,
+    output_grad,
+    view_links,
+    query_weight,
+    key_weight,
+    value_weight,
+):
+    length, cols = queries.shape[2:]
+    model_width = normed.shape[-1]
+    rows = query_weight.shape[0]
+    per_core = cols // HD // 2
+    prompts, views, groups = (lax.axis_size(name) for name in ("dp", "view", "head"))
+    mean_scale = 1.0 / (prompts * views)
+    view = lax.axis_index("view")
+    core = core_of()
+    view_word = view.reshape(1).astype(jnp.int32)
+    core_word = core.reshape(1).astype(jnp.int32)
+    links = lax.all_gather(view_links, "view", axis=0, tiled=True)
+
+    own_packs, mate_packs = pack(
+        core_word, *(a.reshape(length, cols) for a in (queries, saved_keys, saved_values, output_grad))
+    )
+    own_sets, other_sets = [], []
+    for head in range(per_core):
+        mine, theirs = own_packs[head], mate_packs[head]
+        across = flipped(theirs, XCROSS)
+        beside = flipped(mine, YSAME)
+        own_sets.append((mine, flipped(theirs, MATE), flipped(mine, XSAME), across))
+        other_sets.append(
+            (beside, flipped(theirs, YCROSS), flipped(beside, XSAME), flipped(across, YSAME))
+        )
+
+    own_weights = (query_weight, key_weight, value_weight)
+    mate_weights = tuple(flipped(w, MATE) for w in own_weights)
+
+    pieces, grads = [], []
+    for sets in (own_sets, other_sets):
+        kept, received = [], []
+        for blocks in sets:
+            keep, send = attention(links, view_word, blocks)
+            kept.append(keep)
+            received.append(flipped(send, MATE))
+            grads += [keep, send]
+        partial = input_product(core_word, kept, received, own_weights, mate_weights)
+        pieces.append(lax.psum_scatter(partial, "head", scatter_dimension=0, tiled=True))
+
+    def place(y, v, z):
+        return (y * views + v) * groups + z
+
+    halves = []
+    for part in range(2):
+        landed = []
+        for other, piece in enumerate(pieces):
+            pairs = [
+                (
+                    place(y, v, z),
+                    place(y ^ other, v ^ (2 * (z // 2)), y * (views // 2) + v // 2),
+                )
+                for y in range(prompts)
+                for v in range(views)
+                for z in range(groups)
+                if z % 2 == part
+            ]
+            landed.append(lax.ppermute(piece, ("dp", "view", "head"), pairs))
+        halves.append(landed[0] + landed[1])
+    input_grad = jnp.concatenate(halves, axis=0).reshape(
+        1, 1, length, model_width // groups
+    )
+
+    chip = lax.axis_index("dp") * (views // 2) + view // 2
+    flat = normed.reshape(length, model_width)
+
+    def columns(of_chip):
+        return lax.dynamic_slice_in_dim(flat, of_chip * (2 * rows), 2 * rows, axis=1)
+
+    near = [columns(chip)]
+    for shift, flip in ((1, XSAME), (2, YSAME), (3, DIAGONAL)):
+        near.append(flipped(columns(jnp.bitwise_xor(chip, shift)), flip))
+    far = [flipped(n, MATE) for n in near]
+    tokens = [near[0], far[0], near[1], far[1], near[2], far[2], near[3], far[3]]
+    half_cols = 3 * per_core * HD
+    cost = weight_cost(rows, half_cols, 8 * length)
+    params = pltpu.CompilerParams(vmem_limit_bytes=40 * MIB)
+    for_mate = pl.pallas_call(
+        functools.partial(weight_kernel, per_core, mean_scale),
+        out_shape=jax.ShapeDtypeStruct((rows, half_cols), jnp.float32),
+        in_specs=[whole(pltpu.SMEM)] + [whole()] * (8 + len(grads)),
+        out_specs=whole(),
+        compiler_params=params,
+        cost_estimate=cost,
+        name="weight_gradient_mate",
+    )(core_word, *tokens, *grads)
+    from_mate = flipped(for_mate, MATE)
+    weight_grads = pl.pallas_call(
+        functools.partial(weight_final_kernel, per_core, mean_scale),
+        out_shape=[jax.ShapeDtypeStruct((rows, cols), jnp.float32)] * 3,
+        in_specs=[whole(pltpu.SMEM)] + [whole()] * (9 + len(grads)),
+        out_specs=[whole()] * 3,
+        compiler_params=params,
+        cost_estimate=cost,
+        name="weight_gradient_own",
+    )(core_word, *tokens, *grads, from_mate)
+    return (input_grad, *weight_grads)
+
+
 def solution(mesh):
+    prompts, views, groups = (mesh.shape[name] for name in ("dp", "view", "head"))
+    loop_of_four = prompts * 2 == views and prompts * views == 2 * groups and views == groups
+
+    def choose(*arrays):
+        heads_here = arrays[1].shape[-1] // HD
+        one_view_each = arrays[1].shape[:2] == (1, 1)
+        if loop_of_four and one_view_each and heads_here % 2 == 0:
+            return gather_body(*arrays)
+        return halo_body(*arrays)
+
     placed = (
         P("dp", "view", None, None),
         P("dp", "view", None, "head"),
@@ -124,7 +478,7 @@
         P(("dp", "view"), "head"),
     )
     return jax.shard_map(
-        body,
+        choose,
         mesh=mesh,
         in_specs=placed,
         out_specs=(

time: 400 us -> 217 us (0.54)
  waiting for transfers between devices: 288 us -> 68.4 us
  Pallas kernels: 0 us -> 47.5 us
  starting transfers between devices: 2.85 us -> 47.1 us
  matrix products: 34.9 us -> 0 us
  local copies, waits for them, and re-layouts: 46.5 us -> 23.6 us
  blocking collectives: 0 us -> 12 us
  other arithmetic: 11.1 us -> 0.87 us
    reduce_scatter x2, waiting for transfers between devices: 224 us -> 19.8 us  [gather_body(): lax.psum_scatter(partial, 'head', scatter_dimension=0, tiled=True)]
    pallas_call x0 -> x11, Pallas kernels: none -> 47.5 us  [the longest x6 27.1 us: attention(): pl.pallas_call(functools.partial(attention_kernel, HD ** (-0.5)), out_sha...]
    ppermute x4 -> x42, starting transfers between devices: 2.73 us -> 47.1 us  [the longest x38 30 us: flipped(): return lax.ppermute(value, ('dp', 'view'), pairs)]
    dot_general x6 -> x0, matrix products: 30.9 us -> none  [the longest x1 11.9 us: body(): lax.dot_general(flat_input, all_grads, (((0,), (0,)), ((), ())), preferre...]
    ppermute x4 -> x42, waiting for transfers between devices: 64.2 us -> 48.6 us  [the longest x38 48.6 us: flipped(): return lax.ppermute(value, ('dp', 'view'), pairs)]
    all_gather x0 -> x1, blocking collectives: none -> 12 us  [gather_body(): links = lax.all_gather(view_links, 'view', axis=0, tiled=True)]
    another operation x3 -> x0, local copies, waits for them, and re-layouts: 8.4 us -> none
    reshape x3 -> x0, local copies, waits for them, and re-layouts: 8.38 us -> none  [the longest x1 4.16 us: attend(): value_grad = value_grad.reshape(batch_size, 3, length, col_count)]
  transfers between devices with their start and end apart: 7 -> 44, of which waited for: 5 -> 11; matrix products, arithmetic and copies ran while one was open for 17% -> 1% of each run, Pallas kernels for 0% -> 21%
where the time goes in v1:
time: 217 us; the launch traced here: 214 us
  waiting for transfers between devices  68.4 us (32%)
  Pallas kernels  47.5 us (22%)
  starting transfers between devices  47.1 us (22%)
  local copies, waits for them, and re-layouts  23.6 us (11%)
  between operations  14.6 us (7%)
  blocking collectives  12 us (6%)
    ppermute x38, waiting for transfers between devices, flipped(): return lax.ppermute(value, ('dp', 'view'), pairs)  48.6 us
    ppermute x38, starting transfers between devices, flipped(): return lax.ppermute(value, ('dp', 'view'), pairs)  30 us
    pallas_call x6, Pallas kernels, attention(): pl.pallas_call(functools.partial(attention_kernel, HD ** (-0.5)), out_sha...  27.1 us
    unnamed x94, local copies, waits for them, and re-layouts  21.2 us
    reduce_scatter x2, waiting for transfers between devices, gather_body(): lax.psum_scatter(partial, 'head', scatter_dimension=0, tiled=True)  19.8 us
    ppermute x4, starting transfers between devices, gather_body(): landed.append(lax.ppermute(piece, ('dp', 'view', 'head'), pairs))  17.1 us
    all_gather x1, blocking collectives, gather_body(): links = lax.all_gather(view_links, 'view', axis=0, tiled=True)  12 us
    pallas_call x2, Pallas kernels, input_product(): pl.pallas_call(functools.partial(input_kernel, per_core), out_shape=jax.S...  9.67 us
  transfers between devices with their start and end apart: 44, of which 11 were waited for; matrix products, arithmetic and copies ran while one was open for 1% of the time, Pallas kernels for 21%

profile of v1, /device:TPU:16, one launch (start us, length us, event | category | flops | bytes accessed | tf_op | source)
XLA Modules:
  0.0 214.2 jit_solution(10589063918760187017)
XLA Ops:
  7.2 2.8 %pack_heads.1 = (bf16[256,512]{1,0:T(8,128)(2,1)}, bf16[256,512]{1,0:T(8,128)(2,1)}, bf16[256,512]{1,0:T(8,128)(2,1)}, bf16[256,512]{1,0:T(8,128)(2,1)}, bf16[25...) custom-call(s32[1]{0:T(128)} %bitcast.core_ref, bf16[256,768]{1,0:T(8,128)(2,1)} %bitcast.24, bf16[256,768]{1,0:T(8,128)(2,1)} %bitcast.25, ...), custom_call_target="tpu_custom_call" | custom-call | tf_op jit(solution)/shard_map/pack_heads/pallas_call | solution.py:162
  10.0 0.9 collective-permute-start.2
  10.9 0.8 collective-permute-start.5
  11.8 0.9 collective-permute-start.8
  13.9 4.9 %collective-permute-done.2.x3 = bf16[256,512]{1,0:T(8,128)(2,1)S(1)} collective-permute-done((bf16[256,512]{1,0:T(8,128)(2,1)}, bf16[256,512]{1,0:T(8,128)(2,1)S(1)}, u32[]{:S(2)}, u32[]{:S(2)}) %collective-permute-start.2) | collective-permute-done | bytes 262176 | tf_op jit(solution)/shard_map/ppermute | solution.py:131
  19.0 5.4 %collective-permute-done.5.x3 = bf16[256,512]{1,0:T(8,128)(2,1)S(1)} collective-permute-done((bf16[256,512]{1,0:T(8,128)(2,1)}, bf16[256,512]{1,0:T(8,128)(2,1)S(1)}, u32[]{:S(2)}, u32[]{:S(2)}) %collective-permute-start.5) | collective-permute-done | bytes 262176 | tf_op jit(solution)/shard_map/ppermute | solution.py:131
  24.4 1.5 collective-permute-start.4
  25.9 4.1 %collective-permute-done.8.x3 = bf16[256,512]{1,0:T(8,128)(2,1)S(1)} collective-permute-done((bf16[256,512]{1,0:T(8,128)(2,1)}, bf16[256,512]{1,0:T(8,128)(2,1)S(1)}, u32[]{:S(2)}, u32[]{:S(2)}) %collective-permute-start.8) | collective-permute-done | bytes 262176 | tf_op jit(solution)/shard_map/ppermute | solution.py:131
  30.1 1.6 collective-permute-start.1
  31.7 4.0 %collective-permute-done.7.x2 = bf16[256,512]{1,0:T(8,128)(2,1)S(1)} collective-permute-done((bf16[256,512]{1,0:T(8,128)(2,1)}, bf16[256,512]{1,0:T(8,128)(2,1)S(1)}, u32[]{:S(2)}, u32[]{:S(2)}) %collective-permute-start.7) | collective-permute-done | bytes 262176 | tf_op jit(solution)/shard_map/ppermute | solution.py:131
  35.7 12.0 %all-gather = s32[4,1,2]{2,1,0:T(1,128)S(1)} all-gather(s32[1,1,2]{2,1,0:T(1,128)S(1)} %bitcast.28), channel_id=1, replica_groups=mesh['dp'=2,'view'=4,'head'=4] {'view'}, dimensions={0}, use_global_device_ids=true | all-gather | bytes 40 | tf_op jit(solution)/shard_map/all_gather | solution.py:370
  48.1 4.6 %attention_gradients.8 = (bf16[2,256,384]{2,1,0:T(8,128)(2,1)S(1)}, bf16[2,256,384]{2,1,0:T(8,128)(2,1)S(1)}) custom-call(s32[4,2]{1,0:T(4,128)S(1)} %bitcast.18, s32[1]{0:T(128)} %bitcast.3.view_ref, bf16[256,512]{1,0:T(8,128)(2,1)} %get-tuple-element.31.x0, bf16[256,512]{1,0:T(8,128)(2,1)S(1)} %collective-permute-done.6.x1, ...), custom_call_target="tpu_custom_call" | custom-call | flops 2013265920 | bytes 1835008 | tf_op jit(solution)/shard_map/attention_gradients/pallas_call | solution.py:233
  52.7 1.6 collective-permute-start.16
  55.0 4.6 %attention_gradients.7 = (bf16[2,256,384]{2,1,0:T(8,128)(2,1)S(1)}, bf16[2,256,384]{2,1,0:T(8,128)(2,1)S(1)}) custom-call(s32[4,2]{1,0:T(4,128)S(1)} %bitcast.19, s32[1]{0:T(128)} %bitcast.3.view_ref, bf16[256,512]{1,0:T(8,128)(2,1)} %get-tuple-element.28.x0, bf16[256,512]{1,0:T(8,128)(2,1)S(1)} %collective-permute-done.3.x1, ...), custom_call_target="tpu_custom_call" | custom-call | flops 2013265920 | bytes 1835008 | tf_op jit(solution)/shard_map/attention_gradients/pallas_call | solution.py:233
  59.6 4.2 %attention_gradients.6 = (bf16[2,256,384]{2,1,0:T(8,128)(2,1)S(1)}, bf16[2,256,384]{2,1,0:T(8,128)(2,1)S(1)}) custom-call(s32[4,2]{1,0:T(4,128)S(1)} %bitcast.20, s32[1]{0:T(128)} %bitcast.3.view_ref, bf16[256,512]{1,0:T(8,128)(2,1)S(1)} %copy-done.44, bf16[256,512]{1,0:T(8,128)(2,1)S(1)} %collective-permute-done.x1, ...), custom_call_target="tpu_custom_call" | custom-call | flops 2013265920 | bytes 1835008 | tf_op jit(solution)/shard_map/attention_gradients/pallas_call | solution.py:233
  63.8 2.3 %collective-permute-done.17.x1 = bf16[256,512]{1,0:T(8,128)(2,1)S(1)} collective-permute-done((bf16[256,512]{1,0:T(8,128)(2,1)S(1)}, bf16[256,512]{1,0:T(8,128)(2,1)S(1)}, u32[]{:S(2)}, u32[]{:S(2)}) %collective-permute-start.17) | collective-permute-done | bytes 262176 | tf_op jit(solution)/shard_map/ppermute | solution.py:131
  67.4 0.8 copy-done.34
  68.2 1.6 collective-permute-start.20
  69.8 2.4 %dynamic-slice_bitcast_fusion = (bf16[256,768]{1,0:T(8,128)(2,1)}, bf16[256,768]{1,0:T(8,128)(2,1)}, bf16[256,768]{1,0:T(8,128)(2,1)S(1)}, bf16[256,768]{1,0:T(8,128)(2,1)}) fusion(bf16[1,1,256,3072]{3,2,1,0:T(8,128)(2,1)} %param.9, s32[]{:T(128)S(6)} %select_n.21, s32[]{:T(128)S(6)} %select_n.19, s32[]{:T(128)S(6)} %select_n.18, s32[]{:T(128)S(6)} %select_n.20), kind=kLoop, calls=%fused_computation.1 | loop fusion | bytes 3145744 | tf_op jit(solution)/shard_map/dynamic_slice | solution.py:426
  72.2 1.5 collective-permute-start.35
  73.7 1.5 collective-permute-start.24
  75.7 5.1 %input_gradient.2 = bf16[512,768]{1,0:T(8,128)(2,1)S(1)} custom-call(s32[1]{0:T(128)} %bitcast.core_ref, bf16[2,256,384]{2,1,0:T(8,128)(2,1)S(1)} %get-tuple-element.27.refs_0_.refs_8_, bf16[2,256,384]{2,1,0:T(8,128)(2,1)S(1)} %get-tuple-element.30.refs_1_.refs_10_, bf16[2,256,384]{2,1,0:T(8,128)(2,1)S(1)} %get-tuple-element.33.refs_2_.refs_12_, ...), custom_call_target="tpu_custom_call" | custom-call | flops 1811939328 | bytes 6684672 | tf_op jit(solution)/shard_map/input_gradient/pallas_call | solution.py:280
  80.8 0.9 copy-done.32
  81.8 1.6 collective-permute-start.37
  83.9 4.8 %collective-permute-done.24.x0 = bf16[256,512]{1,0:T(8,128)(2,1)} collective-permute-done((bf16[256,512]{1,0:T(8,128)(2,1)}, bf16[256,512]{1,0:T(8,128)(2,1)}, u32[]{:S(2)}, u32[]{:S(2)}) %collective-permute-start.24) | collective-permute-done | bytes 262176 | tf_op jit(solution)/shard_map/ppermute | solution.py:131
  88.7 1.8 collective-permute-start.19
  90.5 3.5 %collective-permute-done.25.x1 = bf16[256,512]{1,0:T(8,128)(2,1)} collective-permute-done((bf16[256,512]{1,0:T(8,128)(2,1)}, bf16[256,512]{1,0:T(8,128)(2,1)}, u32[]{:S(2)}, u32[]{:S(2)}) %collective-permute-start.25) | collective-permute-done | bytes 262176 | tf_op jit(solution)/shard_map/ppermute | solution.py:131
  93.9 1.2 collective-permute-start.22
  95.1 1.5 collective-permute-start.23
  96.7 6.0 %collective-permute-done.37.refs_4_ = bf16[256,768]{1,0:T(8,128)(2,1)S(1)} collective-permute-done((bf16[256,768]{1,0:T(8,128)(2,1)}, bf16[256,768]{1,0:T(8,128)(2,1)S(1)}, u32[]{:S(2)}, u32[]{:S(2)}) %collective-permute-start.37) | collective-permute-done | bytes 393248 | tf_op jit(solution)/shard_map/ppermute | solution.py:131
  102.6 2.7 %collective-permute-start.39 = (bf16[256,768]{1,0:T(8,128)(2,1)}, bf16[256,768]{1,0:T(8,128)(2,1)S(1)}, u32[]{:S(2)}, u32[]{:S(2)}) collective-permute-start(bf16[256,768]{1,0:T(8,128)(2,1)} %get-tuple-element.46), channel_id=1, source_target_pairs={{0,24},{4,28},{8,16},{12,20},{16,8},{20,12},{24,0},{28,4},{1,25},{... | collective-permute-start | bytes 1179656 | tf_op jit(solution)/shard_map/ppermute | solution.py:131
  105.3 11.3 %collective-permute-done.19.x3 = bf16[256,512]{1,0:T(8,128)(2,1)S(1)} collective-permute-done((bf16[256,512]{1,0:T(8,128)(2,1)}, bf16[256,512]{1,0:T(8,128)(2,1)S(1)}, u32[]{:S(2)}, u32[]{:S(2)}) %collective-permute-start.19) | collective-permute-done | bytes 262176 | tf_op jit(solution)/shard_map/ppermute | solution.py:131
  116.7 1.8 collective-permute-start.27
  118.5 1.5 collective-permute-start.26
  119.9 2.3 %collective-permute-done.23.x3 = bf16[256,512]{1,0:T(8,128)(2,1)S(1)} collective-permute-done((bf16[256,512]{1,0:T(8,128)(2,1)}, bf16[256,512]{1,0:T(8,128)(2,1)S(1)}, u32[]{:S(2)}, u32[]{:S(2)}) %collective-permute-start.23) | collective-permute-done | bytes 262176 | tf_op jit(solution)/shard_map/ppermute | solution.py:131
  122.3 0.9 copy-done.41
  123.2 0.9 copy-done.43
  124.2 4.2 %attention_gradients.9 = (bf16[2,256,384]{2,1,0:T(8,128)(2,1)S(1)}, bf16[2,256,384]{2,1,0:T(8,128)(2,1)S(1)}) custom-call(s32[4,2]{1,0:T(4,128)S(1)} %bitcast.21, s32[1]{0:T(128)} %bitcast.3.view_ref, bf16[256,512]{1,0:T(8,128)(2,1)S(1)} %copy-done.41, bf16[256,512]{1,0:T(8,128)(2,1)S(1)} %copy-done.43, bf16[256,512]{1,0:T(8,128)(2,1)S(1)} %collective-permute-done.18.x2, ...), custom_call_target="tpu_custom_call" | custom-call | flops 2013265920 | bytes 1835008 | tf_op jit(solution)/shard_map/attention_gradients/pallas_call | solution.py:233
  128.4 5.0 %attention_gradients.10 = (bf16[2,256,384]{2,1,0:T(8,128)(2,1)S(1)}, bf16[2,256,384]{2,1,0:T(8,128)(2,1)S(1)}) custom-call(s32[4,2]{1,0:T(4,128)S(1)} %bitcast.22, s32[1]{0:T(128)} %bitcast.3.view_ref, bf16[256,512]{1,0:T(8,128)(2,1)} %collective-permute-done.20.x0, bf16[256,512]{1,0:T(8,128)(2,1)} %collective-permute-done.21.x1, ...), custom_call_target="tpu_custom_call" | custom-call | flops 2013265920 | bytes 1835008 | tf_op jit(solution)/shard_map/attention_gradients/pallas_call | solution.py:233
  134.5 4.7 %attention_gradients.11 = (bf16[2,256,384]{2,1,0:T(8,128)(2,1)S(1)}, bf16[2,256,384]{2,1,0:T(8,128)(2,1)S(1)}) custom-call(s32[4,2]{1,0:T(4,128)S(1)} %bitcast.23, s32[1]{0:T(128)} %bitcast.3.view_ref, bf16[256,512]{1,0:T(8,128)(2,1)} %collective-permute-done.24.x0, bf16[256,512]{1,0:T(8,128)(2,1)} %collective-permute-done.25.x1, ...), custom_call_target="tpu_custom_call" | custom-call | flops 2013265920 | bytes 1835008 | tf_op jit(solution)/shard_map/attention_gradients/pallas_call | solution.py:233
  139.9 3.7 %weight_gradient_mate.1 = f32[384,1152]{1,0:T(8,128)} custom-call(s32[1]{0:T(128)} %bitcast.core_ref, bf16[256,768]{1,0:T(8,128)(2,1)S(1)} %get-tuple-element.48.refs_0_, bf16[256,768]{1,0:T(8,128)(2,1)S(1)} %collective-permute-done.34.refs_1_, bf16[256,768]{1,0:T(8,128)(2,1)S(1)} %collective-permute-done.35.refs_2_, ...), custom_call_target="tpu_custom_call" | custom-call | flops 1811939328 | bytes 9633792 | tf_op jit(solution)/shard_map/weight_gradient_mate/pallas_call | solution.py:436
  143.9 4.6 %input_gradient.3 = bf16[512,768]{1,0:T(8,128)(2,1)S(1)} custom-call(s32[1]{0:T(128)} %bitcast.core_ref, bf16[2,256,384]{2,1,0:T(8,128)(2,1)S(1)} %get-tuple-element.37.refs_0_.refs_14_, bf16[2,256,384]{2,1,0:T(8,128)(2,1)S(1)} %get-tuple-element.38.refs_1_.refs_16_, bf16[2,256,384]{2,1,0:T(8,128)(2,1)S(1)} %get-tuple-element.39.refs_2_.refs_18_, ...), custom_call_target="tpu_custom_call" | custom-call | flops 1811939328 | bytes 6684672 | tf_op jit(solution)/shard_map/input_gradient/pallas_call | solution.py:280
  148.5 0.9 copy-done.33
  149.4 3.4 %collective-permute-start.15 = (bf16[128,768]{1,0:T(8,128)(2,1)}, bf16[128,768]{1,0:T(8,128)(2,1)S(1)}, u32[]{:S(2)}, u32[]{:S(2)}) collective-permute-start(bf16[128,768]{1,0:T(8,128)(2,1)} %reduce-scatter.3.cloned.1.call-done), channel_id=1, source_target_pairs={{0,0},{2,8},{4,4},{6,12},{8,9},{10,1},{12,13},{14,5},{16,18},{18,2... | collective-permute-start | bytes 589832 | tf_op jit(solution)/shard_map/ppermute | solution.py:416
  152.8 19.7 %reduce-scatter.5.cloned.1.call-done = bf16[128,768]{1,0:T(8,128)(2,1)} async-done(((bf16[512,768]{1,0:T(8,128)(2,1)}), bf16[128,768]{1,0:T(8,128)(2,1)}) %reduce-scatter.5.cloned.1.call-update) | async-done | bytes 196624 | tf_op jit(solution)/shard_map/reduce_scatter | solution.py:397
  172.6 11.7 %collective-permute-start.31 = (bf16[128,768]{1,0:T(8,128)(2,1)}, bf16[128,768]{1,0:T(8,128)(2,1)S(1)}, u32[]{:S(2)}, u32[]{:S(2)}) collective-permute-start(bf16[128,768]{1,0:T(8,128)(2,1)} %reduce-scatter.5.cloned.1.call-done), channel_id=1, source_target_pairs={{0,16},{2,24},{4,20},{6,28},{8,25},{10,17},{12,29},{14,21},{16,2},... | collective-permute-start | bytes 589832 | tf_op jit(solution)/shard_map/ppermute | solution.py:416
  185.0 1.3 collective-permute-start.33
  186.3 1.0 copy-done.1
  187.3 1.0 copy-done.3
  188.3 1.0 copy-done.5
  189.3 1.0 copy-done.7
  190.3 1.0 copy-done.9
  191.3 1.0 copy-done.11
  192.3 1.0 copy-done.13
  193.3 1.0 copy-done.15
  194.2 1.0 copy-done.17
  195.2 1.0 copy-done.19
  196.2 1.0 copy-done.21
  197.2 1.0 copy-done.23
  198.2 1.0 copy-done.25
  199.2 1.0 copy-done.27
  200.2 1.0 copy-done.29
  201.2 1.0 copy-done.31
  202.2 4.2 %weight_gradient_own.1 = (f32[384,768]{1,0:T(8,128)}, f32[384,768]{1,0:T(8,128)}, f32[384,768]{1,0:T(8,128)}) custom-call(s32[1]{0:T(128)} %bitcast.core_ref, bf16[256,768]{1,0:T(8,128)(2,1)S(1)} %get-tuple-element.48.refs_0_, bf16[256,768]{1,0:T(8,128)(2,1)S(1)} %copy-done.13, bf16[256,768]{1,0:T(8,128)(2,1)S(1)} %copy-done.7, ...), custom_call_target="tpu_custom_call" | custom-call | flops 1811939328 | bytes 9633792 | tf_op jit(solution)/shard_map/weight_gradient_own/pallas_call | solution.py:446
  (136 shorter events, 8.6 us)
Async XLA Ops:
  7.2 28.6 %copy-start.45 = (s32[1,2]{1,0:T(1,128)S(1)}, s32[1,2]{1,0:T(1,128)}, u32[]{:S(2)}) copy-start(s32[1,2]{1,0:T(1,128)} %param.14) | copy-start | bytes 28
  7.2 142.2 %reduce-scatter.3.cloned.1.call-start = ((), (), s32[]{:S(2)}) async-start(), calls=%async_computation.2 | async-start | bytes 983040 | tf_op jit(solution)/shard_map/reduce_scatter | solution.py:397
  10.0 8.8 %collective-permute-start.2 = (bf16[256,512]{1,0:T(8,128)(2,1)}, bf16[256,512]{1,0:T(8,128)(2,1)S(1)}, u32[]{:S(2)}, u32[]{:S(2)}) collective-permute-start(bf16[256,512]{1,0:T(8,128)(2,1)} %get-tuple-element.26), channel_id=1, source_target_pairs={{0,12},{4,8},{8,4},{12,0},{16,28},{20,24},{24,20},{28,16},{1,13},{... | collective-permute-start | bytes 786440 | tf_op jit(solution)/shard_map/ppermute | solution.py:131
  10.9 13.5 %collective-permute-start.5 = (bf16[256,512]{1,0:T(8,128)(2,1)}, bf16[256,512]{1,0:T(8,128)(2,1)S(1)}, u32[]{:S(2)}, u32[]{:S(2)}) collective-permute-start(bf16[256,512]{1,0:T(8,128)(2,1)} %get-tuple-element.29), channel_id=1, source_target_pairs={{0,12},{4,8},{8,4},{12,0},{16,28},{20,24},{24,20},{28,16},{1,13},{... | collective-permute-start | bytes 786440 | tf_op jit(solution)/shard_map/ppermute | solution.py:131
  11.8 18.3 %collective-permute-start.8 = (bf16[256,512]{1,0:T(8,128)(2,1)}, bf16[256,512]{1,0:T(8,128)(2,1)S(1)}, u32[]{:S(2)}, u32[]{:S(2)}) collective-permute-start(bf16[256,512]{1,0:T(8,128)(2,1)} %get-tuple-element.32), channel_id=1, source_target_pairs={{0,12},{4,8},{8,4},{12,0},{16,28},{20,24},{24,20},{28,16},{1,13},{... | collective-permute-start | bytes 786440 | tf_op jit(solution)/shard_map/ppermute | solution.py:131
  12.7 17.5 %collective-permute-start.6 = (bf16[256,512]{1,0:T(8,128)(2,1)}, bf16[256,512]{1,0:T(8,128)(2,1)S(1)}, u32[]{:S(2)}, u32[]{:S(2)}) collective-permute-start(bf16[256,512]{1,0:T(8,128)(2,1)} %get-tuple-element.32), channel_id=1, source_target_pairs={{0,4},{4,0},{8,12},{12,8},{16,20},{20,16},{24,28},{28,24},{1,5},{5... | collective-permute-start | bytes 786440 | tf_op jit(solution)/shard_map/ppermute | solution.py:131
  13.4 22.4 %collective-permute-start.7 = (bf16[256,512]{1,0:T(8,128)(2,1)}, bf16[256,512]{1,0:T(8,128)(2,1)S(1)}, u32[]{:S(2)}, u32[]{:S(2)}) collective-permute-start(bf16[256,512]{1,0:T(8,128)(2,1)} %get-tuple-element.31.x0), channel_id=1, source_target_pairs={{0,8},{4,12},{8,0},{12,4},{16,24},{20,28},{24,16},{28,20},{1,9},{5... | collective-permute-start | bytes 786440 | tf_op jit(solution)/shard_map/ppermute | solution.py:131
  18.8 40.7 %copy-start.39 = (bf16[256,512]{1,0:T(8,128)(2,1)}, bf16[256,512]{1,0:T(8,128)(2,1)S(1)}, u32[]{:S(2)}) copy-start(bf16[256,512]{1,0:T(8,128)(2,1)S(1)} %collective-permute-done.2.x3) | copy-start | bytes 786436
  18.8 29.0 %collective-permute-start.3 = (bf16[256,512]{1,0:T(8,128)(2,1)}, bf16[256,512]{1,0:T(8,128)(2,1)S(1)}, u32[]{:S(2)}, u32[]{:S(2)}) collective-permute-start(bf16[256,512]{1,0:T(8,128)(2,1)} %get-tuple-element.29), channel_id=1, source_target_pairs={{0,4},{4,0},{8,12},{12,8},{16,20},{20,16},{24,28},{28,24},{1,5},{5... | collective-permute-start | bytes 786440 | tf_op jit(solution)/shard_map/ppermute | solution.py:131
  24.4 30.6 %copy-start.38 = (bf16[256,512]{1,0:T(8,128)(2,1)}, bf16[256,512]{1,0:T(8,128)(2,1)S(1)}, u32[]{:S(2)}) copy-start(bf16[256,512]{1,0:T(8,128)(2,1)S(1)} %collective-permute-done.5.x3) | copy-start | bytes 786436
  24.4 28.3 %collective-permute-start.4 = (bf16[256,512]{1,0:T(8,128)(2,1)}, bf16[256,512]{1,0:T(8,128)(2,1)S(1)}, u32[]{:S(2)}, u32[]{:S(2)}) collective-permute-start(bf16[256,512]{1,0:T(8,128)(2,1)} %get-tuple-element.28.x0), channel_id=1, source_target_pairs={{0,8},{4,12},{8,0},{12,4},{16,24},{20,28},{24,16},{28,20},{1,9},{5... | collective-permute-start | bytes 786440 | tf_op jit(solution)/shard_map/ppermute | solution.py:131
  30.0 29.5 %copy-start.37 = (bf16[256,512]{1,0:T(8,128)(2,1)}, bf16[256,512]{1,0:T(8,128)(2,1)S(1)}, u32[]{:S(2)}) copy-start(bf16[256,512]{1,0:T(8,128)(2,1)S(1)} %collective-permute-done.8.x3) | copy-start | bytes 786436
  30.0 24.3 %collective-permute-start = (bf16[256,512]{1,0:T(8,128)(2,1)}, bf16[256,512]{1,0:T(8,128)(2,1)S(1)}, u32[]{:S(2)}, u32[]{:S(2)}) collective-permute-start(bf16[256,512]{1,0:T(8,128)(2,1)} %get-tuple-element.26), channel_id=1, source_target_pairs={{0,4},{4,0},{8,12},{12,8},{16,20},{20,16},{24,28},{28,24},{1,5},{5... | collective-permute-start | bytes 786440 | tf_op jit(solution)/shard_map/ppermute | solution.py:131
  30.1 24.2 %collective-permute-start.1 = (bf16[256,512]{1,0:T(8,128)(2,1)}, bf16[256,512]{1,0:T(8,128)(2,1)S(1)}, u32[]{:S(2)}, u32[]{:S(2)}) collective-permute-start(bf16[256,512]{1,0:T(8,128)(2,1)} %get-tuple-element.25.x0), channel_id=1, source_target_pairs={{0,8},{4,12},{8,0},{12,4},{16,24},{20,28},{24,16},{28,20},{1,9},{5... | collective-permute-start | bytes 786440 | tf_op jit(solution)/shard_map/ppermute | solution.py:131
  35.7 31.7 %collective-permute-start.12 = (bf16[384,768]{1,0:T(8,128)(2,1)}, bf16[384,768]{1,0:T(8,128)(2,1)S(1)}, u32[]{:S(2)}, u32[]{:S(2)}) collective-permute-start(bf16[384,768]{1,0:T(8,128)(2,1)} %refs_6_.3), channel_id=1, source_target_pairs={{0,4},{4,0},{8,12},{12,8},{16,20},{20,16},{24,28},{28,24},{1,5},{5... | collective-permute-start | bytes 1769480 | tf_op jit(solution)/shard_map/ppermute | solution.py:131
  47.8 20.4 %collective-permute-start.13 = (bf16[384,768]{1,0:T(8,128)(2,1)}, bf16[384,768]{1,0:T(8,128)(2,1)}, u32[]{:S(2)}, u32[]{:S(2)}) collective-permute-start(bf16[384,768]{1,0:T(8,128)(2,1)} %refs_7_.3), channel_id=1, source_target_pairs={{0,4},{4,0},{8,12},{12,8},{16,20},{20,16},{24,28},{28,24},{1,5},{5... | collective-permute-start | bytes 1769480 | tf_op jit(solution)/shard_map/ppermute | solution.py:131
  48.1 4.6 %copy-start.44 = (bf16[256,512]{1,0:T(8,128)(2,1)S(1)}, bf16[256,512]{1,0:T(8,128)(2,1)}, u32[]{:S(2)}) copy-start(bf16[256,512]{1,0:T(8,128)(2,1)} %get-tuple-element.25.x0) | copy-start | bytes 786436
  48.1 6.2 %copy-start.46 = (bf16[256,512]{1,0:T(8,128)(2,1)S(1)}, bf16[256,512]{1,0:T(8,128)(2,1)}, u32[]{:S(2)}) copy-start(bf16[256,512]{1,0:T(8,128)(2,1)} %get-tuple-element.26) | copy-start | bytes 786436
  52.7 11.0 %collective-permute-start.16 = (bf16[256,512]{1,0:T(8,128)(2,1)S(1)}, bf16[256,512]{1,0:T(8,128)(2,1)S(1)}, u32[]{:S(2)}, u32[]{:S(2)}) collective-permute-start(bf16[256,512]{1,0:T(8,128)(2,1)S(1)} %copy-done.44), channel_id=1, source_target_pairs={{0,16},{4,20},{8,24},{12,28},{16,0},{20,4},{24,8},{28,12},{1,17},{... | collective-permute-start | bytes 786440 | tf_op jit(solution)/shard_map/ppermute | solution.py:131
  54.3 11.8 %collective-permute-start.17 = (bf16[256,512]{1,0:T(8,128)(2,1)S(1)}, bf16[256,512]{1,0:T(8,128)(2,1)S(1)}, u32[]{:S(2)}, u32[]{:S(2)}) collective-permute-start(bf16[256,512]{1,0:T(8,128)(2,1)S(1)} %copy-done.46), channel_id=1, source_target_pairs={{0,20},{4,16},{8,28},{12,24},{16,4},{20,0},{24,12},{28,8},{1,21},{... | collective-permute-start | bytes 786440 | tf_op jit(solution)/shard_map/ppermute | solution.py:131
  54.4 17.8 %collective-permute-start.14 = (bf16[384,768]{1,0:T(8,128)(2,1)}, bf16[384,768]{1,0:T(8,128)(2,1)}, u32[]{:S(2)}, u32[]{:S(2)}) collective-permute-start(bf16[384,768]{1,0:T(8,128)(2,1)} %refs_8_.3), channel_id=1, source_target_pairs={{0,4},{4,0},{8,12},{12,8},{16,20},{20,16},{24,28},{28,24},{1,5},{5... | collective-permute-start | bytes 1769480 | tf_op jit(solution)/shard_map/ppermute | solution.py:131
  59.5 80.3 %copy-start = (bf16[2,256,384]{2,1,0:T(8,128)(2,1)}, bf16[2,256,384]{2,1,0:T(8,128)(2,1)S(1)}, u32[]{:S(2)}) copy-start(bf16[2,256,384]{2,1,0:T(8,128)(2,1)S(1)} %get-tuple-element.35.refs_11_) | copy-start | bytes 1179652
  63.7 76.1 %copy-start.2 = (bf16[2,256,384]{2,1,0:T(8,128)(2,1)}, bf16[2,256,384]{2,1,0:T(8,128)(2,1)S(1)}, u32[]{:S(2)}) copy-start(bf16[2,256,384]{2,1,0:T(8,128)(2,1)S(1)} %get-tuple-element.27.refs_0_.refs_8_) | copy-start | bytes 1179652
  63.7 76.1 %copy-start.4 = (bf16[2,256,384]{2,1,0:T(8,128)(2,1)}, bf16[2,256,384]{2,1,0:T(8,128)(2,1)S(1)}, u32[]{:S(2)}) copy-start(bf16[2,256,384]{2,1,0:T(8,128)(2,1)S(1)} %get-tuple-element.34.refs_9_) | copy-start | bytes 1179652
  63.8 10.0 %collective-permute-start.11 = (bf16[2,256,384]{2,1,0:T(8,128)(2,1)S(1)}, bf16[2,256,384]{2,1,0:T(8,128)(2,1)}, u32[]{:S(2)}, u32[]{:S(2)}) collective-permute-start(bf16[2,256,384]{2,1,0:T(8,128)(2,1)S(1)} %get-tuple-element.36.refs_13_), channel_id=1, source_target_pairs={{0,4},{4,0},{8,12},{12,8},{16,20},{20,16},{24,28},{28,24},{1,5},{5... | collective-permute-start | bytes 1179656 | tf_op jit(solution)/shard_map/ppermute | solution.py:131
  66.8 6.9 %collective-permute-start.10 = (bf16[2,256,384]{2,1,0:T(8,128)(2,1)S(1)}, bf16[2,256,384]{2,1,0:T(8,128)(2,1)}, u32[]{:S(2)}, u32[]{:S(2)}) collective-permute-start(bf16[2,256,384]{2,1,0:T(8,128)(2,1)S(1)} %get-tuple-element.35.refs_11_), channel_id=1, source_target_pairs={{0,4},{4,0},{8,12},{12,8},{16,20},{20,16},{24,28},{28,24},{1,5},{5... | collective-permute-start | bytes 1179656 | tf_op jit(solution)/shard_map/ppermute | solution.py:131
  68.2 7.0 %collective-permute-start.9 = (bf16[2,256,384]{2,1,0:T(8,128)(2,1)S(1)}, bf16[2,256,384]{2,1,0:T(8,128)(2,1)}, u32[]{:S(2)}, u32[]{:S(2)}) collective-permute-start(bf16[2,256,384]{2,1,0:T(8,128)(2,1)S(1)} %get-tuple-element.34.refs_9_), channel_id=1, source_target_pairs={{0,4},{4,0},{8,12},{12,8},{16,20},{20,16},{24,28},{28,24},{1,5},{5... | collective-permute-start | bytes 1179656 | tf_op jit(solution)/shard_map/ppermute | solution.py:131
  68.2 7.5 %copy-start.35 = (bf16[384,768]{1,0:T(8,128)(2,1)S(1)}, bf16[384,768]{1,0:T(8,128)(2,1)}, u32[]{:S(2)}) copy-start(bf16[384,768]{1,0:T(8,128)(2,1)} %copy-done.34) | copy-start | bytes 1769476
  68.2 13.5 %collective-permute-start.20 = (bf16[256,512]{1,0:T(8,128)(2,1)}, bf16[256,512]{1,0:T(8,128)(2,1)}, u32[]{:S(2)}, u32[]{:S(2)}) collective-permute-start(bf16[256,512]{1,0:T(8,128)(2,1)} %get-tuple-element.28.x0), channel_id=1, source_target_pairs={{0,16},{4,20},{8,24},{12,28},{16,0},{20,4},{24,8},{28,12},{1,17},{... | collective-permute-start | bytes 786440 | tf_op jit(solution)/shard_map/ppermute | solution.py:131
  72.2 22.9 %collective-permute-start.35 = (bf16[256,768]{1,0:T(8,128)(2,1)}, bf16[256,768]{1,0:T(8,128)(2,1)S(1)}, u32[]{:S(2)}, u32[]{:S(2)}) collective-permute-start(bf16[256,768]{1,0:T(8,128)(2,1)} %get-tuple-element.47), channel_id=1, source_target_pairs={{0,8},{4,12},{8,0},{12,4},{16,24},{20,28},{24,16},{28,20},{1,9},{5... | collective-permute-start | bytes 1179656 | tf_op jit(solution)/shard_map/ppermute | solution.py:131
  73.7 9.6 %collective-permute-start.21 = (bf16[256,512]{1,0:T(8,128)(2,1)}, bf16[256,512]{1,0:T(8,128)(2,1)}, u32[]{:S(2)}, u32[]{:S(2)}) collective-permute-start(bf16[256,512]{1,0:T(8,128)(2,1)} %get-tuple-element.29), channel_id=1, source_target_pairs={{0,20},{4,16},{8,28},{12,24},{16,4},{20,0},{24,12},{28,8},{1,21},{... | collective-permute-start | bytes 786440 | tf_op jit(solution)/shard_map/ppermute | solution.py:131
  73.7 15.0 %collective-permute-start.24 = (bf16[256,512]{1,0:T(8,128)(2,1)}, bf16[256,512]{1,0:T(8,128)(2,1)}, u32[]{:S(2)}, u32[]{:S(2)}) collective-permute-start(bf16[256,512]{1,0:T(8,128)(2,1)} %get-tuple-element.31.x0), channel_id=1, source_target_pairs={{0,16},{4,20},{8,24},{12,28},{16,0},{20,4},{24,8},{28,12},{1,17},{... | collective-permute-start | bytes 786440 | tf_op jit(solution)/shard_map/ppermute | solution.py:131
  75.2 18.7 %collective-permute-start.25 = (bf16[256,512]{1,0:T(8,128)(2,1)}, bf16[256,512]{1,0:T(8,128)(2,1)}, u32[]{:S(2)}, u32[]{:S(2)}) collective-permute-start(bf16[256,512]{1,0:T(8,128)(2,1)} %get-tuple-element.32), channel_id=1, source_target_pairs={{0,20},{4,16},{8,28},{12,24},{16,4},{20,0},{24,12},{28,8},{1,21},{... | collective-permute-start | bytes 786440 | tf_op jit(solution)/shard_map/ppermute | solution.py:131
  81.7 90.9 %reduce-scatter.5.cloned.1.call-start = ((), (), s32[]{:S(2)}) async-start(), calls=%async_computation.3 | async-start | bytes 983040 | tf_op jit(solution)/shard_map/reduce_scatter | solution.py:397
  81.8 20.9 %collective-permute-start.37 = (bf16[256,768]{1,0:T(8,128)(2,1)}, bf16[256,768]{1,0:T(8,128)(2,1)S(1)}, u32[]{:S(2)}, u32[]{:S(2)}) collective-permute-start(bf16[256,768]{1,0:T(8,128)(2,1)} %get-tuple-element.49), channel_id=1, source_target_pairs={{0,16},{4,20},{8,24},{12,28},{16,0},{20,4},{24,8},{28,12},{1,17},{... | collective-permute-start | bytes 1179656 | tf_op jit(solution)/shard_map/ppermute | solution.py:131
  83.3 22.0 %collective-permute-start.18 = (bf16[256,512]{1,0:T(8,128)(2,1)}, bf16[256,512]{1,0:T(8,128)(2,1)S(1)}, u32[]{:S(2)}, u32[]{:S(2)}) collective-permute-start(bf16[256,512]{1,0:T(8,128)(2,1)} %copy-done.40), channel_id=1, source_target_pairs={{0,8},{4,12},{8,0},{12,4},{16,24},{20,28},{24,16},{28,20},{1,9},{5... | collective-permute-start | bytes 786440 | tf_op jit(solution)/shard_map/ppermute | solution.py:131
  88.7 28.0 %collective-permute-start.19 = (bf16[256,512]{1,0:T(8,128)(2,1)}, bf16[256,512]{1,0:T(8,128)(2,1)S(1)}, u32[]{:S(2)}, u32[]{:S(2)}) collective-permute-start(bf16[256,512]{1,0:T(8,128)(2,1)} %copy-done.39), channel_id=1, source_target_pairs={{0,16},{4,20},{8,24},{12,28},{16,0},{20,4},{24,8},{28,12},{1,17},{... | collective-permute-start | bytes 786440 | tf_op jit(solution)/shard_map/ppermute | solution.py:131
  93.9 24.5 %collective-permute-start.22 = (bf16[256,512]{1,0:T(8,128)(2,1)}, bf16[256,512]{1,0:T(8,128)(2,1)S(1)}, u32[]{:S(2)}, u32[]{:S(2)}) collective-permute-start(bf16[256,512]{1,0:T(8,128)(2,1)} %collective-permute-done.20.x0), channel_id=1, source_target_pairs={{0,8},{4,12},{8,0},{12,4},{16,24},{20,28},{24,16},{28,20},{1,9},{5... | collective-permute-start | bytes 786440 | tf_op jit(solution)/shard_map/ppermute | solution.py:131
  95.1 44.7 %copy-start.6 = (bf16[256,768]{1,0:T(8,128)(2,1)}, bf16[256,768]{1,0:T(8,128)(2,1)S(1)}, u32[]{:S(2)}) copy-start(bf16[256,768]{1,0:T(8,128)(2,1)S(1)} %collective-permute-done.35.refs_2_) | copy-start | bytes 1179652
  95.1 27.1 %collective-permute-start.23 = (bf16[256,512]{1,0:T(8,128)(2,1)}, bf16[256,512]{1,0:T(8,128)(2,1)S(1)}, u32[]{:S(2)}, u32[]{:S(2)}) collective-permute-start(bf16[256,512]{1,0:T(8,128)(2,1)} %copy-done.38), channel_id=1, source_target_pairs={{0,16},{4,20},{8,24},{12,28},{16,0},{20,4},{24,8},{28,12},{1,17},{... | collective-permute-start | bytes 786440 | tf_op jit(solution)/shard_map/ppermute | solution.py:131
  102.6 37.2 %copy-start.8 = (bf16[256,768]{1,0:T(8,128)(2,1)}, bf16[256,768]{1,0:T(8,128)(2,1)S(1)}, u32[]{:S(2)}) copy-start(bf16[256,768]{1,0:T(8,128)(2,1)S(1)} %collective-permute-done.37.refs_4_) | copy-start | bytes 1179652
  102.6 30.8 %collective-permute-start.39 = (bf16[256,768]{1,0:T(8,128)(2,1)}, bf16[256,768]{1,0:T(8,128)(2,1)S(1)}, u32[]{:S(2)}, u32[]{:S(2)}) collective-permute-start(bf16[256,768]{1,0:T(8,128)(2,1)} %get-tuple-element.46), channel_id=1, source_target_pairs={{0,24},{4,28},{8,16},{12,20},{16,8},{20,12},{24,0},{28,4},{1,25},{... | collective-permute-start | bytes 1179656 | tf_op jit(solution)/shard_map/ppermute | solution.py:131
  105.3 33.9 %collective-permute-start.34 = (bf16[256,768]{1,0:T(8,128)(2,1)S(1)}, bf16[256,768]{1,0:T(8,128)(2,1)S(1)}, u32[]{:S(2)}, u32[]{:S(2)}) collective-permute-start(bf16[256,768]{1,0:T(8,128)(2,1)S(1)} %get-tuple-element.48.refs_0_), channel_id=1, source_target_pairs={{0,4},{4,0},{8,12},{12,8},{16,20},{20,16},{24,28},{28,24},{1,5},{5... | collective-permute-start | bytes 1179656 | tf_op jit(solution)/shard_map/ppermute | solution.py:131
  116.7 17.4 %collective-permute-start.27 = (bf16[256,512]{1,0:T(8,128)(2,1)}, bf16[256,512]{1,0:T(8,128)(2,1)S(1)}, u32[]{:S(2)}, u32[]{:S(2)}) collective-permute-start(bf16[256,512]{1,0:T(8,128)(2,1)} %copy-done.37), channel_id=1, source_target_pairs={{0,16},{4,20},{8,24},{12,28},{16,0},{20,4},{24,8},{28,12},{1,17},{... | collective-permute-start | bytes 786440 | tf_op jit(solution)/shard_map/ppermute | solution.py:131
  118.5 15.5 %collective-permute-start.26 = (bf16[256,512]{1,0:T(8,128)(2,1)}, bf16[256,512]{1,0:T(8,128)(2,1)S(1)}, u32[]{:S(2)}, u32[]{:S(2)}) collective-permute-start(bf16[256,512]{1,0:T(8,128)(2,1)} %collective-permute-done.24.x0), channel_id=1, source_target_pairs={{0,8},{4,12},{8,0},{12,4},{16,24},{20,28},{24,16},{28,20},{1,9},{5... | collective-permute-start | bytes 786440 | tf_op jit(solution)/shard_map/ppermute | solution.py:131
  122.3 17.1 %collective-permute-start.36 = (bf16[256,768]{1,0:T(8,128)(2,1)S(1)}, bf16[256,768]{1,0:T(8,128)(2,1)S(1)}, u32[]{:S(2)}, u32[]{:S(2)}) collective-permute-start(bf16[256,768]{1,0:T(8,128)(2,1)S(1)} %collective-permute-done.35.refs_2_), channel_id=1, source_target_pairs={{0,4},{4,0},{8,12},{12,8},{16,20},{20,16},{24,28},{28,24},{1,5},{5... | collective-permute-start | bytes 1179656 | tf_op jit(solution)/shard_map/ppermute | solution.py:131
  128.4 11.5 %copy-start.18 = (bf16[2,256,384]{2,1,0:T(8,128)(2,1)}, bf16[2,256,384]{2,1,0:T(8,128)(2,1)S(1)}, u32[]{:S(2)}) copy-start(bf16[2,256,384]{2,1,0:T(8,128)(2,1)S(1)} %get-tuple-element.40.refs_15_) | copy-start | bytes 1179652
  128.4 15.5 %copy-start.16 = (bf16[2,256,384]{2,1,0:T(8,128)(2,1)}, bf16[2,256,384]{2,1,0:T(8,128)(2,1)S(1)}, u32[]{:S(2)}) copy-start(bf16[2,256,384]{2,1,0:T(8,128)(2,1)S(1)} %get-tuple-element.37.refs_0_.refs_14_) | copy-start | bytes 1179652
  133.3 6.5 %copy-start.22 = (bf16[2,256,384]{2,1,0:T(8,128)(2,1)}, bf16[2,256,384]{2,1,0:T(8,128)(2,1)S(1)}, u32[]{:S(2)}) copy-start(bf16[2,256,384]{2,1,0:T(8,128)(2,1)S(1)} %get-tuple-element.41.refs_17_) | copy-start | bytes 1179652
  133.4 10.5 %copy-start.20 = (bf16[2,256,384]{2,1,0:T(8,128)(2,1)}, bf16[2,256,384]{2,1,0:T(8,128)(2,1)S(1)}, u32[]{:S(2)}) copy-start(bf16[2,256,384]{2,1,0:T(8,128)(2,1)S(1)} %get-tuple-element.38.refs_1_.refs_16_) | copy-start | bytes 1179652
  133.4 6.5 %copy-start.10 = (bf16[256,768]{1,0:T(8,128)(2,1)}, bf16[256,768]{1,0:T(8,128)(2,1)S(1)}, u32[]{:S(2)}) copy-start(bf16[256,768]{1,0:T(8,128)(2,1)S(1)} %collective-permute-done.39.refs_6_) | copy-start | bytes 1179652
  133.4 6.4 %collective-permute-start.38 = (bf16[256,768]{1,0:T(8,128)(2,1)S(1)}, bf16[256,768]{1,0:T(8,128)(2,1)S(1)}, u32[]{:S(2)}, u32[]{:S(2)}) collective-permute-start(bf16[256,768]{1,0:T(8,128)(2,1)S(1)} %collective-permute-done.37.refs_4_), channel_id=1, source_target_pairs={{0,4},{4,0},{8,12},{12,8},{16,20},{20,16},{24,28},{28,24},{1,5},{5... | collective-permute-start | bytes 1179656 | tf_op jit(solution)/shard_map/ppermute | solution.py:131
  134.0 5.8 %collective-permute-start.40 = (bf16[256,768]{1,0:T(8,128)(2,1)S(1)}, bf16[256,768]{1,0:T(8,128)(2,1)S(1)}, u32[]{:S(2)}, u32[]{:S(2)}) collective-permute-start(bf16[256,768]{1,0:T(8,128)(2,1)S(1)} %collective-permute-done.39.refs_6_), channel_id=1, source_target_pairs={{0,4},{4,0},{8,12},{12,8},{16,20},{20,16},{24,28},{28,24},{1,5},{5... | collective-permute-start | bytes 1179656 | tf_op jit(solution)/shard_map/ppermute | solution.py:131
  134.1 9.8 %collective-permute-start.28 = (bf16[2,256,384]{2,1,0:T(8,128)(2,1)S(1)}, bf16[2,256,384]{2,1,0:T(8,128)(2,1)S(1)}, u32[]{:S(2)}, u32[]{:S(2)}) collective-permute-start(bf16[2,256,384]{2,1,0:T(8,128)(2,1)S(1)} %get-tuple-element.40.refs_15_), channel_id=1, source_target_pairs={{0,4},{4,0},{8,12},{12,8},{16,20},{20,16},{24,28},{28,24},{1,5},{5... | collective-permute-start | bytes 1179656 | tf_op jit(solution)/shard_map/ppermute | solution.py:131
  139.2 4.5 %copy-start.30 = (bf16[2,256,384]{2,1,0:T(8,128)(2,1)}, bf16[2,256,384]{2,1,0:T(8,128)(2,1)S(1)}, u32[]{:S(2)}) copy-start(bf16[2,256,384]{2,1,0:T(8,128)(2,1)S(1)} %get-tuple-element.42.refs_19_) | copy-start | bytes 1179652
  139.2 4.7 %copy-start.28 = (bf16[2,256,384]{2,1,0:T(8,128)(2,1)}, bf16[2,256,384]{2,1,0:T(8,128)(2,1)S(1)}, u32[]{:S(2)}) copy-start(bf16[2,256,384]{2,1,0:T(8,128)(2,1)S(1)} %get-tuple-element.39.refs_2_.refs_18_) | copy-start | bytes 1179652
  139.2 4.4 %copy-start.12 = (bf16[256,768]{1,0:T(8,128)(2,1)}, bf16[256,768]{1,0:T(8,128)(2,1)S(1)}, u32[]{:S(2)}) copy-start(bf16[256,768]{1,0:T(8,128)(2,1)S(1)} %collective-permute-done.34.refs_1_) | copy-start | bytes 1179652
  139.2 4.6 %collective-permute-start.29 = (bf16[2,256,384]{2,1,0:T(8,128)(2,1)S(1)}, bf16[2,256,384]{2,1,0:T(8,128)(2,1)S(1)}, u32[]{:S(2)}, u32[]{:S(2)}) collective-permute-start(bf16[2,256,384]{2,1,0:T(8,128)(2,1)S(1)} %get-tuple-element.41.refs_17_), channel_id=1, source_target_pairs={{0,4},{4,0},{8,12},{12,8},{16,20},{20,16},{24,28},{28,24},{1,5},{5... | collective-permute-start | bytes 1179656 | tf_op jit(solution)/shard_map/ppermute | solution.py:131
  139.4 4.5 %collective-permute-start.30 = (bf16[2,256,384]{2,1,0:T(8,128)(2,1)S(1)}, bf16[2,256,384]{2,1,0:T(8,128)(2,1)S(1)}, u32[]{:S(2)}, u32[]{:S(2)}) collective-permute-start(bf16[2,256,384]{2,1,0:T(8,128)(2,1)S(1)} %get-tuple-element.42.refs_19_), channel_id=1, source_target_pairs={{0,4},{4,0},{8,12},{12,8},{16,20},{20,16},{24,28},{28,24},{1,5},{5... | collective-permute-start | bytes 1179656 | tf_op jit(solution)/shard_map/ppermute | solution.py:131
  143.7 42.6 %collective-permute-start.41 = (f32[384,1152]{1,0:T(8,128)}, f32[384,1152]{1,0:T(8,128)S(1)}, u32[]{:S(2)}, u32[]{:S(2)}) collective-permute-start(f32[384,1152]{1,0:T(8,128)} %weight_gradient_mate.1), channel_id=1, source_target_pairs={{0,4},{4,0},{8,12},{12,8},{16,20},{20,16},{24,28},{28,24},{1,5},{5... | collective-permute-start | bytes 5308424 | tf_op jit(solution)/shard_map/ppermute | solution.py:131
  149.4 57.1 %collective-permute-start.15 = (bf16[128,768]{1,0:T(8,128)(2,1)}, bf16[128,768]{1,0:T(8,128)(2,1)S(1)}, u32[]{:S(2)}, u32[]{:S(2)}) collective-permute-start(bf16[128,768]{1,0:T(8,128)(2,1)} %reduce-scatter.3.cloned.1.call-done), channel_id=1, source_target_pairs={{0,0},{2,8},{4,4},{6,12},{8,9},{10,1},{12,13},{14,5},{16,18},{18,2... | collective-permute-start | bytes 589832 | tf_op jit(solution)/shard_map/ppermute | solution.py:416
  172.6 33.9 %collective-permute-start.31 = (bf16[128,768]{1,0:T(8,128)(2,1)}, bf16[128,768]{1,0:T(8,128)(2,1)S(1)}, u32[]{:S(2)}, u32[]{:S(2)}) collective-permute-start(bf16[128,768]{1,0:T(8,128)(2,1)} %reduce-scatter.5.cloned.1.call-done), channel_id=1, source_target_pairs={{0,16},{2,24},{4,20},{6,28},{8,25},{10,17},{12,29},{14,21},{16,2},... | collective-permute-start | bytes 589832 | tf_op jit(solution)/shard_map/ppermute | solution.py:416
  184.3 22.2 %collective-permute-start.32 = (bf16[128,768]{1,0:T(8,128)(2,1)}, bf16[128,768]{1,0:T(8,128)(2,1)S(1)}, u32[]{:S(2)}, u32[]{:S(2)}) collective-permute-start(bf16[128,768]{1,0:T(8,128)(2,1)} %reduce-scatter.3.cloned.1.call-done), channel_id=1, source_target_pairs={{1,0},{3,8},{5,4},{7,12},{9,9},{11,1},{13,13},{15,5},{17,18},{19,2... | collective-permute-start | bytes 589832 | tf_op jit(solution)/shard_map/ppermute | solution.py:416
  185.0 21.5 %collective-permute-start.33 = (bf16[128,768]{1,0:T(8,128)(2,1)}, bf16[128,768]{1,0:T(8,128)(2,1)S(1)}, u32[]{:S(2)}, u32[]{:S(2)}) collective-permute-start(bf16[128,768]{1,0:T(8,128)(2,1)} %reduce-scatter.5.cloned.1.call-done), channel_id=1, source_target_pairs={{1,16},{3,24},{5,20},{7,28},{9,25},{11,17},{13,29},{15,21},{17,2},... | collective-permute-start | bytes 589832 | tf_op jit(solution)/shard_map/ppermute | solution.py:416
  (27 other events, 40.7 us)
Sparse Core Ops, SparseCore 0:
  81.8 21.8 reduce-scatter.2
  149.5 23.0 reduce-scatter.4

commit v2 on v0

--- a/solution.py
+++ b/solution.py
@@ -1,9 +1,15 @@
+import functools
+
 import jax
 import jax.numpy as jnp
 from jax import lax
+from jax.experimental import pallas as pl
+from jax.experimental.pallas import tpu as pltpu
 from jax.sharding import PartitionSpec as P
 
 HD = 128
+LOG2E = 1.4426950408889634
+MIB = 1024 * 1024
 
 
 def shifted(value, axis, steps):
@@ -48,7 +54,7 @@
     return (query_grad, jnp.concatenate([key_grad, value_grad], axis=-1))
 
 
-def body(
+def halo_body(
     normed,
     queries,
     saved_keys,
@@ -111,7 +117,501 @@
     return (input_grad, grad_query, grad_key, grad_value)
 
 
+def moved(value, target):
+    prompts, views = lax.axis_size("dp"), lax.axis_size("view")
+    pairs = []
+    for y in range(prompts):
+        for v in range(views):
+            goal = target(y, v)
+            if goal is not None:
+                pairs.append((y * views + v, goal[0] * views + goal[1]))
+    return lax.ppermute(value, ("dp", "view"), pairs)
+
+
+def straight(y, v):
+    return (y, v ^ 2) if v % 2 == 0 else (y ^ 1, v)
+
+
+def crossed(y, v):
+    return (y ^ 1, v ^ 1) if v % 2 == 0 else (y, v ^ 3)
+
+
+def inwards(y, v):
+    return None if v % 2 == 0 else (y, v ^ 1)
+
+
+def relay_x(y, v):
+    return None if v % 2 == 0 else (y, v ^ 2)
+
+
+def relay_y(y, v):
+    return (y ^ 1, v ^ 1) if v % 2 == 0 else None
+
+
+def corner_same(y, v):
+    return None if v % 2 == 0 else (y ^ 1, v ^ 2)
+
+
+def corner_cross(y, v):
+    return (y ^ 1, v ^ 3) if v % 2 == 0 else None
+
+
+def mate(y, v):
+    return (y, v ^ 1)
+
+
+def lanes(start, size):
+    return pl.ds(pl.multiple_of(start, HD), size)
+
+
+def whole(space=pltpu.VMEM):
+    return pl.BlockSpec(memory_space=space)
+
+
+def dot_last(a, b):
+    return lax.dot_general(a, b, (((1,), (1,)), ((), ())), preferred_element_type=jnp.float32)
+
+
+def dot_first(a, b):
+    return lax.dot_general(a, b, (((0,), (0,)), ((), ())), preferred_element_type=jnp.float32)
+
+
+def dot(a, b):
+    return jnp.dot(a, b, preferred_element_type=jnp.float32)
+
+
+def run_copies(copies):
+    for copy in copies:
+        copy.start()
+    for copy in copies:
+        copy.wait()
+
+
+FLAG_ROWS = 16
+
+
+def pack_first_kernel(width, links_ref, q_ref, k_ref, v_ref, g_ref, out_ref, flags, sems):
+    length = q_ref.shape[0]
+    half = FLAG_ROWS // 2
+    row = lax.broadcasted_iota(jnp.int32, (FLAG_ROWS, width), 0)
+    gaps = [jnp.where(links_ref[0, side] >= 0, 0.0, 1.0).astype(jnp.float32) for side in range(2)]
+    flags[...] = jnp.where(row < half, gaps[0], gaps[1]).astype(jnp.bfloat16)
+    run_copies(
+        [
+            pltpu.make_async_copy(
+                source.at[:, 0:width],
+                out_ref.at[kind * length : (kind + 1) * length],
+                sems.at[kind],
+            )
+            for kind, source in enumerate((q_ref, k_ref, v_ref, g_ref))
+        ]
+        + [pltpu.make_async_copy(flags, out_ref.at[4 * length : 4 * length + FLAG_ROWS], sems.at[4])]
+    )
+
+
+def pack_next_kernel(first, width, q_ref, k_ref, v_ref, g_ref, out_ref, sems):
+    length = q_ref.shape[0]
+    run_copies(
+        [
+            pltpu.make_async_copy(
+                source.at[:, first : first + width],
+                out_ref.at[kind * length : (kind + 1) * length],
+                sems.at[kind],
+            )
+            for kind, source in enumerate((q_ref, k_ref, v_ref, g_ref))
+        ]
+    )
+
+
+def pack(first, width, links, arrays):
+    length = arrays[0].shape[0]
+    any_space = [whole(pl.ANY)] * 4
+    if first == 0:
+        return pl.pallas_call(
+            functools.partial(pack_first_kernel, width),
+            out_shape=jax.ShapeDtypeStruct((4 * length + FLAG_ROWS, width), jnp.bfloat16),
+            in_specs=[whole(pltpu.SMEM)] + any_space,
+            out_specs=whole(pl.ANY),
+            scratch_shapes=[
+                pltpu.VMEM((FLAG_ROWS, width), jnp.bfloat16),
+                pltpu.SemaphoreType.DMA((5,)),
+            ],
+            name="pack_first",
+        )(links, *arrays)
+    return pl.pallas_call(
+        functools.partial(pack_next_kernel, first, width),
+        out_shape=jax.ShapeDtypeStruct((4 * length, width), jnp.bfloat16),
+        in_specs=any_space,
+        out_specs=whole(pl.ANY),
+        scratch_shapes=[pltpu.SemaphoreType.DMA((4,))],
+        name="pack_next",
+    )(*arrays)
+
+
+def attention_kernel(scaling, opening, place_ref, *refs):
+    sources = refs[:6]
+    if opening:
+        out_ref, flags_out, x, flags, kacc, vacc, sems = refs[6:]
+    else:
+        flags_in, out_ref, x, flags, kacc, vacc, sems = refs[6:]
+    core, odd = place_ref[0], place_ref[1]
+    _, length, width = out_ref.shape
+    width = width // 3
+    own, mate_in, first, second, relayed_x, relayed_y = sources
+    chosen = ((own, mate_in, first, second), (first, second, relayed_x, relayed_y))
+
+    for which in range(2):
+
+        @pl.when(core == which)
+        def _():
+            copies = [
+                pltpu.make_async_copy(source.at[0 : 4 * length], x.at[e], sems.at[e])
+                for e, source in enumerate(chosen[which])
+            ]
+            if opening:
+                copies += [
+                    pltpu.make_async_copy(
+                        source.at[4 * length : 4 * length + FLAG_ROWS], flags.at[e], sems.at[4 + e]
+                    )
+                    for e, source in enumerate(chosen[which])
+                ]
+            run_copies(copies)
+
+    if opening:
+        flags_out[...] = flags[...]
+    else:
+        flags[...] = flags_in[...]
+    factor = scaling * LOG2E
+    kacc[...] = jnp.zeros_like(kacc)
+    vacc[...] = jnp.zeros_like(vacc)
+
+    def rows(e, kind, head):
+        return x[e, kind * length : (kind + 1) * length, head * HD : (head + 1) * HD]
+
+    def one_view(e, carry):
+        blocks = (jnp.bitwise_and(e + 3, 3), e, jnp.bitwise_and(e + 1, 3))
+        gaps = flags[e].astype(jnp.float32) * 1e30
+        before, after = gaps[0:1, :length], gaps[FLAG_ROWS // 2 : FLAG_ROWS // 2 + 1, :length]
+        far_below = jnp.where(odd == 0, before, after)
+        far_above = jnp.where(odd == 0, after, before)
+        for head in range(width // HD):
+            q = rows(e, 0, head)
+            g = rows(e, 3, head)
+            scores = [dot_last(rows(f, 1, head), q) for f in blocks]
+            tops = [jnp.max(s, axis=0, keepdims=True) for s in scores]
+            top = jnp.maximum(tops[1], jnp.maximum(tops[0] - far_below, tops[2] - far_above))
+            offsets = (top + far_below, top, top + far_above)
+            powers = [jnp.exp2((s - o) * factor) for s, o in zip(scores, offsets)]
+            inverse = 1.0 / sum(jnp.sum(p, axis=0, keepdims=True) for p in powers)
+            prob_grads = [dot_last(rows(f, 2, head), g) for f in blocks]
+            delta = inverse * sum(
+                jnp.sum(p * d, axis=0, keepdims=True) for p, d in zip(powers, prob_grads)
+            )
+            query_grad = None
+            here = slice(head * HD, (head + 1) * HD)
+            for f, p, d in zip(blocks, powers, prob_grads):
+                probs = p * inverse
+                score_grad = (probs * scaling * (d - delta)).astype(jnp.bfloat16)
+                part = dot_first(score_grad, rows(f, 1, head))
+                query_grad = part if query_grad is None else query_grad + part
+                kacc[f, :, here] += dot(score_grad, q)
+                vacc[f, :, here] += dot(probs.astype(jnp.bfloat16), g)
+            out_ref[e, :, here] = query_grad.astype(out_ref.dtype)
+        return carry
+
+    lax.fori_loop(0, 4, one_view, 0)
+    out_ref[:, :, width : 2 * width] = kacc[...].astype(out_ref.dtype)
+    out_ref[:, :, 2 * width : 3 * width] = vacc[...].astype(out_ref.dtype)
+
+
+def attention(place, sources, flags, length):
+    width = sources[0].shape[1]
+    opening = flags is None
+    out = jax.ShapeDtypeStruct((4, length, 3 * width), jnp.bfloat16)
+    flag_shape = (4, FLAG_ROWS, width)
+    flag_out = jax.ShapeDtypeStruct(flag_shape, jnp.bfloat16)
+    result = pl.pallas_call(
+        functools.partial(attention_kernel, HD ** (-0.5), opening),
+        out_shape=[out, flag_out] if opening else [out],
+        in_specs=[whole(pltpu.SMEM)] + [whole(pl.ANY)] * 6 + ([] if opening else [whole()]),
+        out_specs=[whole()] * (2 if opening else 1),
+        scratch_shapes=[
+            pltpu.VMEM((4, 4 * length, width), jnp.bfloat16),
+            pltpu.VMEM(flag_shape, jnp.bfloat16),
+            pltpu.VMEM((4, length, width), jnp.float32),
+            pltpu.VMEM((4, length, width), jnp.float32),
+            pltpu.SemaphoreType.DMA((8,)),
+        ],
+        compiler_params=pltpu.CompilerParams(vmem_limit_bytes=32 * MIB),
+        cost_estimate=pl.CostEstimate(
+            flops=4 * 5 * 2 * length * 3 * length * width * 2,
+            bytes_accessed=2 * length * 7 * width * 4,
+            transcendentals=12 * length * length * (width // HD),
+        ),
+        name="attention_gradients",
+    )(place, *sources, *([] if opening else [flags]))
+    return result if opening else (result[0], flags)
+
+
+def input_kernel(place_ref, *refs):
+    chunks = (len(refs) - 10) // 1
+    grads = refs[:chunks]
+    own_weights = refs[chunks : chunks + 3]
+    mate_weights = refs[chunks + 3 : chunks + 6]
+    out_refs = refs[chunks + 6 :]
+    core = place_ref[0]
+    rows = own_weights[0].shape[0]
+    width = grads[0].shape[2] // 3
+    slot = pl.program_id(0)
+    parts = []
+    for weights in (own_weights, mate_weights):
+        total = None
+        for chunk, grad in enumerate(grads):
+            left = grad[0]
+            right = jnp.concatenate(
+                [w[:, chunk * width : (chunk + 1) * width] for w in weights], axis=1
+            )
+            part = dot_last(left, right)
+            total = part if total is None else total + part
+        parts.append(total.astype(jnp.bfloat16))
+    for s, out_ref in enumerate(out_refs):
+
+        @pl.when(slot == s)
+        def _():
+            for part, at in zip(parts, (core, 1 - core)):
+                out_ref[:, lanes(at * rows, rows)] = part
+
+
+def input_product(place, grads, own_weights, mate_weights):
+    blocks, length, triple = grads[0].shape
+    rows, cols = own_weights[0].shape
+    fixed = pl.BlockSpec((rows, cols), lambda s, place: (0, 0))
+    out = jax.ShapeDtypeStruct((length, 2 * rows), jnp.bfloat16)
+    return pl.pallas_call(
+        input_kernel,
+        grid_spec=pltpu.PrefetchScalarGridSpec(
+            num_scalar_prefetch=1,
+            grid=(blocks,),
+            in_specs=[
+                pl.BlockSpec(
+                    (1, length, triple), lambda s, place: (jnp.bitwise_xor(s, place[2]), 0, 0)
+                )
+            ]
+            * len(grads)
+            + [fixed] * 6,
+            out_specs=[pl.BlockSpec((length, 2 * rows), lambda s, place: (0, 0))] * blocks,
+        ),
+        out_shape=[out] * blocks,
+        compiler_params=pltpu.CompilerParams(vmem_limit_bytes=32 * MIB),
+        cost_estimate=pl.CostEstimate(
+            flops=2 * blocks * length * 2 * rows * 3 * cols,
+            bytes_accessed=2 * (blocks * length * (2 * rows + 3 * cols) + 6 * rows * cols),
+            transcendentals=0,
+        ),
+        name="input_gradient",
+    )(place, *grads, *own_weights, *mate_weights)
+
+
+def columns_kernel(place_ref, normed_ref, *refs):
+    out_refs, sems = refs[:-1], refs[-1]
+    width = out_refs[0].shape[1]
+    run_copies(
+        [
+            pltpu.make_async_copy(
+                normed_ref.at[:, lanes(place_ref[3 + at] * width, width)], out, sems.at[at]
+            )
+            for at, out in enumerate(out_refs)
+        ]
+    )
+
+
+def columns(place, flat, width):
+    out = jax.ShapeDtypeStruct((flat.shape[0], width), flat.dtype)
+    return pl.pallas_call(
+        columns_kernel,
+        out_shape=[out] * 4,
+        in_specs=[whole(pltpu.SMEM), whole(pl.ANY)],
+        out_specs=[whole(pl.ANY)] * 4,
+        scratch_shapes=[pltpu.SemaphoreType.DMA((4,))],
+        name="normed_columns",
+    )(place, flat)
+
+
+def weight_kernel(mine, mean_scale, place_ref, *refs):
+    sources, grad_refs = refs[:6], refs[6:9]
+    if mine:
+        received, out_refs, scratch = refs[9:12], refs[12:15], refs[15:]
+    else:
+        received, out_refs, scratch = None, refs[9:12], refs[12:]
+    tokens, turned, grads, sems = scratch
+    core = place_ref[0]
+    rows = out_refs[0].shape[0]
+    chunks, blocks, length, triple = grads.shape
+    width = triple // 3
+    start = (core if mine else 1 - core) * rows
+    own, mate_in, first, second, corner, corner_far = sources
+    chosen = ((own, mate_in, first, second), (first, second, corner, corner_far))
+    loads = [
+        pltpu.make_async_copy(source, grads.at[chunk], sems.at[4 + chunk])
+        for chunk, source in enumerate(grad_refs)
+    ]
+    for which in range(2):
+
+        @pl.when(core == which)
+        def _():
+            for e, source in enumerate(chosen[which]):
+                pltpu.make_async_copy(
+                    source.at[:, lanes(start, rows)], tokens.at[e], sems.at[e]
+                ).start()
+
+    for load in loads:
+        load.start()
+    for e in range(blocks):
+        pltpu.make_async_copy(first.at[:, lanes(start, rows)], tokens.at[e], sems.at[e]).wait()
+        turned[:, e * length : (e + 1) * length] = tokens[e].T
+    for chunk, load in enumerate(loads):
+        load.wait()
+        for kind, out in enumerate(out_refs):
+            right = grads[chunk, :, :, kind * width : (kind + 1) * width]
+            here = slice(chunk * width, (chunk + 1) * width)
+            total = dot(turned[...], right.reshape(blocks * length, width))
+            if mine:
+                total = (total + received[kind][:, here]) * mean_scale
+            out[:, here] = total
+
+
+def weight_product(place, mine, mean_scale, tokens, grads, received=()):
+    blocks, length, triple = grads[0].shape
+    width = triple // 3
+    rows = tokens[0].shape[1] // 2
+    cols = width * len(grads)
+    return pl.pallas_call(
+        functools.partial(weight_kernel, mine, mean_scale),
+        out_shape=[jax.ShapeDtypeStruct((rows, cols), jnp.float32)] * 3,
+        in_specs=[whole(pltpu.SMEM)] + [whole(pl.ANY)] * 9 + [whole()] * len(received),
+        out_specs=[whole()] * 3,
+        scratch_shapes=[
+            pltpu.VMEM((blocks, length, rows), jnp.bfloat16),
+            pltpu.VMEM((rows, blocks * length), jnp.bfloat16),
+            pltpu.VMEM((len(grads), blocks, length, triple), jnp.bfloat16),
+            pltpu.SemaphoreType.DMA((4 + len(grads),)),
+        ],
+        compiler_params=pltpu.CompilerParams(vmem_limit_bytes=40 * MIB),
+        cost_estimate=pl.CostEstimate(
+            flops=2 * rows * 3 * cols * blocks * length,
+            bytes_accessed=2 * blocks * length * (rows + 3 * cols) + 12 * rows * cols,
+            transcendentals=0,
+        ),
+        name="weight_gradient_own" if mine else "weight_gradient_mate",
+    )(place, *tokens, *grads, *received)
+
+
+def after(values, *earlier):
+    return lax.optimization_barrier((tuple(values), tuple(earlier)))[0]
+
+
+def gather_body(
+    normed,
+    queries,
+    saved_keys,
+    saved_values,
+    output_grad,
+    view_links,
+    query_weight,
+    key_weight,
+    value_weight,
+):
+    length, cols = queries.shape[2:]
+    model_width = normed.shape[-1]
+    rows = query_weight.shape[0]
+    prompts, views, groups = (lax.axis_size(name) for name in ("dp", "view", "head"))
+    mean_scale = 1.0 / (prompts * views)
+    width = length
+    view = lax.axis_index("view")
+    core = lax.rem(view, 2)
+    chip = lax.axis_index("dp") * (views // 2) + view // 2
+    toward_x, toward_y = jnp.bitwise_xor(chip, 1), jnp.bitwise_xor(chip, 2)
+    place = jnp.stack(
+        [
+            core,
+            core,
+            lax.axis_index("head"),
+            jnp.where(core == 0, toward_x, toward_y),
+            jnp.where(core == 0, toward_y, toward_x),
+            chip,
+            jnp.bitwise_xor(chip, 3),
+        ]
+    ).astype(jnp.int32)
+
+    arrays = tuple(a.reshape(length, cols) for a in (queries, saved_keys, saved_values, output_grad))
+    sets = []
+    for first in range(0, cols, width):
+        if sets:
+            arrays = after(arrays, sets[-1][2])
+        own = pack(first, width, view_links, arrays)
+        straight_in = moved(own, straight)
+        crossed_in = moved(own, crossed)
+        mate_in = moved(own, inwards)
+        sets.append(
+            (own, mate_in, straight_in, crossed_in)
+            + (moved(straight_in, relay_x), moved(straight_in, relay_y))
+        )
+
+    own_weights = after((query_weight, key_weight, value_weight), sets[0][1])
+    mate_weights = tuple(moved(w, mate) for w in own_weights)
+
+    grads, flags = [], None
+    for sources in sets:
+        grad, flags = attention(place, sources, flags, length)
+        grads.append(grad)
+
+    slots = input_product(place, grads, own_weights, mate_weights)
+    total = slots[0].astype(jnp.float32)
+    for s in range(1, groups):
+        total += lax.ppermute(slots[s], "head", [(z, z ^ s) for z in range(groups)]).astype(
+            jnp.float32
+        )
+
+    def spot(y, v, z):
+        return (y * views + v) * groups + z
+
+    pairs = [
+        (spot(y, v, z), spot(y ^ (v % 2), v ^ z, y * (views // 2) + v // 2))
+        for y in range(prompts)
+        for v in range(views)
+        for z in range(groups)
+    ]
+    input_grad = lax.ppermute(total.astype(jnp.bfloat16), ("dp", "view", "head"), pairs)
+
+    (flat,) = after((normed.reshape(length, model_width),), sets[-1][3])
+    to_straight, to_crossed, here, to_corner = columns(place, flat, 2 * rows)
+    tokens = (
+        here,
+        moved(here, inwards),
+        moved(to_straight, straight),
+        moved(to_crossed, crossed),
+        moved(to_corner, corner_same),
+        moved(to_corner, corner_cross),
+    )
+    for_mate = weight_product(place, False, mean_scale, tokens, grads)
+    from_mate = [moved(w, mate) for w in for_mate]
+    weight_grads = weight_product(place, True, mean_scale, tokens, grads, from_mate)
+    return (
+        input_grad.reshape(1, 1, length, model_width // groups),
+        *weight_grads,
+    )
+
+
 def solution(mesh):
+    prompts, views, groups = (mesh.shape[name] for name in ("dp", "view", "head"))
+    loop_of_four = prompts * 2 == views and prompts * views == 2 * groups and views == groups
+
+    def choose(*arrays):
+        batch, held, length, cols = arrays[1].shape
+        if loop_of_four and batch == held == 1 and length % HD == 0 and cols == 3 * length:
+            return gather_body(*arrays)
+        return halo_body(*arrays)
+
     placed = (
         P("dp", "view", None, None),
         P("dp", "view", None, "head"),
@@ -124,7 +624,7 @@
         P(("dp", "view"), "head"),
     )
     return jax.shard_map(
-        body,
+        choose,
         mesh=mesh,
         in_specs=placed,
         out_specs=(

time: 400 us -> 283 us (0.71)
  the two profiles are of different devices: /device:TPU:16 before, /device:TPU:25 now
where the time goes in v2:
time: 283 us
  Pallas kernels  147 us (52%)
  waiting for transfers between devices  70.1 us (25%)
  starting transfers between devices  55.2 us (20%)
  local copies, waits for them, and re-layouts  9.32 us (3%)
    pallas_call x1, Pallas kernels, columns(): pl.pallas_call(columns_kernel, out_shape=[out] * 4, in_specs=[whole(pltpu...  49.6 us
    ppermute x26, starting transfers between devices, moved(): return lax.ppermute(value, ('dp', 'view'), pairs)  47.7 us
    pallas_call x2, Pallas kernels, pack(): pl.pallas_call(functools.partial(pack_next_kernel, first, width), out_sha...  34 us
    ppermute x1, waiting for transfers between devices, gather_body(): lax.ppermute(total.astype(jnp.bfloat16), ('dp', 'view', 'head'), pairs)  32.3 us
    pallas_call x3, Pallas kernels, attention(): pl.pallas_call(functools.partial(attention_kernel, HD ** (-0.5), opening)...  29.2 us
    ppermute x3, waiting for transfers between devices, gather_body(): lax.ppermute(slots[s], 'head', [(z, z ^ s) for z in range(groups)])  26.5 us
    pallas_call x1, Pallas kernels, pack(): pl.pallas_call(functools.partial(pack_first_kernel, width), out_shape=jax...  17.7 us
    ppermute x26, waiting for transfers between devices, moved(): return lax.ppermute(value, ('dp', 'view'), pairs)  11.3 us
  transfers between devices with their start and end apart: 30, of which 7 were waited for; matrix products, arithmetic and copies ran while one was open for 0% of the time, Pallas kernels for 44%

profile of v2, /device:TPU:25, one launch (start us, length us, event | category | flops | bytes accessed | tf_op | source)
XLA Modules:
  0.0 282.8 jit_solution(6009246777123006980)
XLA Ops:
  0.6 17.7 %pack_first.1.refs_0_ = bf16[1040,256]{1,0:T(8,128)(2,1)} custom-call(s32[1,2]{1,0:T(1,128)} %links_ref.1, bf16[256,768]{1,0:T(8,128)(2,1)} %bitcast.12, bf16[256,768]{1,0:T(8,128)(2,1)} %bitcast.15, bf16[256,768]{1,0:T(8,128)(2,1)} %bitcast.18, bf16[256,768]{1,0:T(8,128)(2,1)} %bitcast.21), custom_call_target="tpu_custom_call" | custom-call | tf_op jit(solution)/shard_map/pack_first/pallas_call | solution.py:230
  18.3 0.0 copy-start.1
  18.4 1.3 collective-permute-start.1
  19.7 1.1 collective-permute-start.2
  20.7 10.0 %collective-permute-done.1.refs_2_ = bf16[1040,256]{1,0:T(8,128)(2,1)S(1)} collective-permute-done((bf16[1040,256]{1,0:T(8,128)(2,1)}, bf16[1040,256]{1,0:T(8,128)(2,1)S(1)}, u32[]{:S(2)}, u32[]{:S(2)}) %collective-permute-start.1) | collective-permute-done | bytes 532512 | tf_op jit(solution)/shard_map/ppermute | solution.py:128
  30.7 17.0 %pack_next.2.refs_0_ = bf16[1024,256]{1,0:T(8,128)(2,1)} custom-call(bf16[256,768]{1,0:T(8,128)(2,1)} %bitcast.13, bf16[256,768]{1,0:T(8,128)(2,1)} %bitcast.16, bf16[256,768]{1,0:T(8,128)(2,1)} %bitcast.19, bf16[256,768]{1,0:T(8,128)(2,1)} %bitcast.22), custom_call_target="tpu_custom_call" | custom-call | tf_op jit(solution)/shard_map/pack_next/pallas_call | solution.py:241
  47.8 2.2 collective-permute-start.6
  49.9 4.8 %collective-permute-start = (bf16[1040,256]{1,0:T(8,128)(2,1)S(1)}, bf16[1040,256]{1,0:T(8,128)(2,1)S(1)}, u32[]{:S(2)}, u32[]{:S(2)}) collective-permute-start(bf16[1040,256]{1,0:T(8,128)(2,1)S(1)} %copy-done.1), channel_id=1, source_target_pairs={{4,0},{12,8},{20,16},{28,24},{5,1},{13,9},{21,17},{29,25},{6,2},{1... | collective-permute-start | bytes 1597448 | tf_op jit(solution)/shard_map/ppermute | solution.py:128
  54.8 0.1 collective-permute-start.7
  54.8 1.3 collective-permute-start.4
  56.1 0.0 copy-start.11
  56.1 2.6 collective-permute-start.3
  58.8 7.5 %collective-permute-start.5 = (bf16[1024,256]{1,0:T(8,128)(2,1)}, bf16[1024,256]{1,0:T(8,128)(2,1)}, u32[]{:S(2)}, u32[]{:S(2)}) collective-permute-start(bf16[1024,256]{1,0:T(8,128)(2,1)} %pack_next.2.refs_0_), channel_id=1, source_target_pairs={{4,0},{12,8},{20,16},{28,24},{5,1},{13,9},{21,17},{29,25},{6,2},{1... | collective-permute-start | bytes 1572872 | tf_op jit(solution)/shard_map/ppermute | solution.py:128
  66.3 17.0 %pack_next.3.refs_0_ = bf16[1024,256]{1,0:T(8,128)(2,1)} custom-call(bf16[256,768]{1,0:T(8,128)(2,1)} %bitcast.14, bf16[256,768]{1,0:T(8,128)(2,1)} %bitcast.17, bf16[256,768]{1,0:T(8,128)(2,1)} %bitcast.20, bf16[256,768]{1,0:T(8,128)(2,1)} %bitcast.23), custom_call_target="tpu_custom_call" | custom-call | tf_op jit(solution)/shard_map/pack_next/pallas_call | solution.py:241
  83.3 0.0 copy-start.13
  83.3 0.8 copy-done.13
  84.1 1.2 collective-permute-start.11
  85.4 3.3 %collective-permute-start.10 = (bf16[1024,256]{1,0:T(8,128)(2,1)}, bf16[1024,256]{1,0:T(8,128)(2,1)}, u32[]{:S(2)}, u32[]{:S(2)}) collective-permute-start(bf16[1024,256]{1,0:T(8,128)(2,1)} %pack_next.3.refs_0_), channel_id=1, source_target_pairs={{4,0},{12,8},{20,16},{28,24},{5,1},{13,9},{21,17},{29,25},{6,2},{1... | collective-permute-start | bytes 1572872 | tf_op jit(solution)/shard_map/ppermute | solution.py:128
  88.7 0.8 copy-done.15
  89.5 1.3 collective-permute-start.9
  90.8 0.8 copy-done.17
  91.6 4.1 %collective-permute-start.8 = (bf16[1024,256]{1,0:T(8,128)(2,1)}, bf16[1024,256]{1,0:T(8,128)(2,1)}, u32[]{:S(2)}, u32[]{:S(2)}) collective-permute-start(bf16[1024,256]{1,0:T(8,128)(2,1)} %collective-permute-done.6.refs_2_), channel_id=1, source_target_pairs={{4,12},{12,4},{20,28},{28,20},{5,13},{13,5},{21,29},{29,21},{6,14}... | collective-permute-start | bytes 1572872 | tf_op jit(solution)/shard_map/ppermute | solution.py:128
  95.7 0.1 stack.28.place_ref
  95.8 0.8 collective-permute-done.11.refs_2_
  96.6 1.3 collective-permute-start.14
  97.9 0.1 collective-permute-done.12.refs_3_
  98.0 0.8 copy-done.19
  98.8 4.1 %collective-permute-start.13 = (bf16[1024,256]{1,0:T(8,128)(2,1)}, bf16[1024,256]{1,0:T(8,128)(2,1)}, u32[]{:S(2)}, u32[]{:S(2)}) collective-permute-start(bf16[1024,256]{1,0:T(8,128)(2,1)} %collective-permute-done.11.refs_2_), channel_id=1, source_target_pairs={{4,12},{12,4},{20,28},{28,20},{5,13},{13,5},{21,29},{29,21},{6,14}... | collective-permute-start | bytes 1572872 | tf_op jit(solution)/shard_map/ppermute | solution.py:128
  102.9 0.0 copy-start.10
  102.9 1.0 copy-done.10
  104.0 1.0 copy-done.12
  105.0 1.0 copy-done.14
  106.0 1.0 copy-done.16
  107.1 1.0 copy-done.18
  108.1 8.9 %attention_gradients.3 = (bf16[4,256,768]{2,1,0:T(8,128)(2,1)S(1)}, bf16[4,16,256]{2,1,0:T(8,128)(2,1)S(1)}) custom-call(s32[7]{0:T(128)S(1)} %stack.28.place_ref, bf16[1040,256]{1,0:T(8,128)(2,1)S(1)} %copy-done.1, bf16[1040,256]{1,0:T(8,128)(2,1)S(1)} %copy-done.14, bf16[1040,256]{1,0:T(8,128)(2,1)S(1)} %copy-done.10, bf16[1040,256]{1,0:T(8,128)(2,1)S(1)} %copy-done.12, ...), custom_call_target="tpu_custom_call" | custom-call | flops 4026531840 | bytes 3670016 | tf_op jit(solution)/shard_map/attention_gradients/pallas_call | solution.py:333
  117.1 0.0 copy-start.6
  117.1 49.6 %normed_columns.1 = (bf16[256,768]{1,0:T(8,128)(2,1)}, bf16[256,768]{1,0:T(8,128)(2,1)}, bf16[256,768]{1,0:T(8,128)(2,1)}, bf16[256,768]{1,0:T(8,128)(2,1)}) custom-call(s32[7]{0:T(128)} %copy-done.4, bf16[256,3072]{1,0:T(8,128)(2,1)} %bitcast.24), custom_call_target="tpu_custom_call" | custom-call | tf_op jit(solution)/shard_map/normed_columns/pallas_call | solution.py:430
  166.7 1.3 collective-permute-start.15
  168.0 0.1 collective-permute-start.16
  168.1 0.4 collective-permute-start.17
  168.6 10.2 %attention_gradients.4.refs_1_.refs_7_ = bf16[4,256,768]{2,1,0:T(8,128)(2,1)S(1)} custom-call(s32[7]{0:T(128)S(1)} %copy-done.5, bf16[1024,256]{1,0:T(8,128)(2,1)S(1)} %copy-done.2, bf16[1024,256]{1,0:T(8,128)(2,1)} %collective-permute-done.5.refs_1_, bf16[1024,256]{1,0:T(8,128)(2,1)} %collective-permute-done.6.refs_2_, ...), custom_call_target="tpu_custom_call" | custom-call | flops 4026531840 | bytes 3670016 | tf_op jit(solution)/shard_map/attention_gradients/pallas_call | solution.py:333
  178.8 0.8 collective-permute-start.23
  179.6 0.0 copy-start.8
  179.6 1.4 collective-permute-start.26
  181.1 10.1 %attention_gradients.5.refs_2_.refs_8_ = bf16[4,256,768]{2,1,0:T(8,128)(2,1)S(1)} custom-call(s32[7]{0:T(128)S(1)} %copy-done.5, bf16[1024,256]{1,0:T(8,128)(2,1)S(1)} %copy-done.3, bf16[1024,256]{1,0:T(8,128)(2,1)} %collective-permute-done.10.refs_1_, bf16[1024,256]{1,0:T(8,128)(2,1)} %collective-permute-done.11.refs_2_, bf16[1024,256]{1,0:T(8,128)(2,1)S(1)} %copy-done.20, ...), custom_call_target="tpu_custom_call" | custom-call | flops 4026531840 | bytes 3670016 | tf_op jit(solution)/shard_map/attention_gradients/pallas_call | solution.py:333
  191.2 4.4 %collective-permute-start.25 = (bf16[256,768]{1,0:T(8,128)(2,1)S(1)}, bf16[256,768]{1,0:T(8,128)(2,1)S(1)}, u32[]{:S(2)}, u32[]{:S(2)}) collective-permute-start(bf16[256,768]{1,0:T(8,128)(2,1)S(1)} %copy-done.21), channel_id=1, source_target_pairs={{4,28},{12,20},{20,12},{28,4},{5,29},{13,21},{21,13},{29,5},{6,30}... | collective-permute-start | bytes 1179656 | tf_op jit(solution)/shard_map/ppermute | solution.py:128
  195.6 0.1 collective-permute-start.24
  195.7 2.3 collective-permute-start.22
  198.0 6.3 %input_gradient.1 = (bf16[256,768]{1,0:T(8,128)(2,1)S(1)}, bf16[256,768]{1,0:T(8,128)(2,1)S(1)}, bf16[256,768]{1,0:T(8,128)(2,1)S(1)}, bf16[256,768]{1,0:T(8,128)(2,1)S(1)}) custom-call(s32[7]{0:T(128)S(1)} %copy-done.5, bf16[4,256,768]{2,1,0:T(8,128)(2,1)S(1)} %get-tuple-element.32.refs_0_.refs_6_, ...), custom_call_target="tpu_custom_call" | custom-call | flops 3623878656 | bytes 9830400 | tf_op jit(solution)/shard_map/input_gradient/pallas_call | solution.py:390
  204.4 0.2 collective-permute-start.18
  204.6 0.4 collective-permute-done.24.refs_3_
  204.9 4.3 %weight_gradient_mate.1 = (f32[384,768]{1,0:T(8,128)S(1)}, f32[384,768]{1,0:T(8,128)S(1)}, f32[384,768]{1,0:T(8,128)S(1)}) custom-call(s32[7]{0:T(128)S(1)} %copy-done.5, bf16[256,768]{1,0:T(8,128)(2,1)S(1)} %copy-done, bf16[256,768]{1,0:T(8,128)(2,1)S(1)} %collective-permute-done.22.refs_1_, bf16[256,768]{1,0:T(8,128)(2,1)S(1)} %collective-permute-done.23.refs_2_, ...), custom_call_target="tpu_custom_call" | custom-call | flops 1811939328 | bytes 9043968 | tf_op jit(solution)/shard_map/weight_gradient_mate/pallas_call | solution.py:488
  209.3 0.2 collective-permute-start.27
  209.5 0.3 collective-permute-start.28
  209.8 0.2 collective-permute-start.29
  210.0 0.1 collective-permute-start.19
  210.1 6.9 %collective-permute-done.18 = bf16[256,768]{1,0:T(8,128)(2,1)S(1)} collective-permute-done((bf16[256,768]{1,0:T(8,128)(2,1)S(1)}, bf16[256,768]{1,0:T(8,128)(2,1)S(1)}, u32[]{:S(2)}, u32[]{:S(2)}) %collective-permute-start.18) | collective-permute-done | bytes 393248 | tf_op jit(solution)/shard_map/ppermute | solution.py:571
  217.0 1.6 collective-permute-start.20
  218.6 19.6 %collective-permute-done.19 = bf16[256,768]{1,0:T(8,128)(2,1)S(1)} collective-permute-done((bf16[256,768]{1,0:T(8,128)(2,1)S(1)}, bf16[256,768]{1,0:T(8,128)(2,1)S(1)}, u32[]{:S(2)}, u32[]{:S(2)}) %collective-permute-start.19) | collective-permute-done | bytes 393248 | tf_op jit(solution)/shard_map/ppermute | solution.py:571
  238.2 0.2 add_convert_fusion
  238.4 5.7 %collective-permute-start.21 = (bf16[256,768]{1,0:T(8,128)(2,1)S(1)}, bf16[256,768]{1,0:T(8,128)(2,1)S(1)}, u32[]{:S(2)}, u32[]{:S(2)}) collective-permute-start(bf16[256,768]{1,0:T(8,128)(2,1)S(1)} %add_convert_fusion), channel_id=1, source_target_pairs={{0,0},{1,4},{2,8},{3,12},{4,20},{5,16},{6,28},{7,24},{8,9},{9,13},... | collective-permute-start | bytes 1179656 | tf_op jit(solution)/shard_map/ppermute | solution.py:584
  244.1 32.3 %collective-permute-done.21 = bf16[256,768]{1,0:T(8,128)(2,1)S(1)} collective-permute-done((bf16[256,768]{1,0:T(8,128)(2,1)S(1)}, bf16[256,768]{1,0:T(8,128)(2,1)S(1)}, u32[]{:S(2)}, u32[]{:S(2)}) %collective-permute-start.21) | collective-permute-done | bytes 393248 | tf_op jit(solution)/shard_map/ppermute | solution.py:584
  276.5 5.5 %weight_gradient_own.1 = (f32[384,768]{1,0:T(8,128)}, f32[384,768]{1,0:T(8,128)}, f32[384,768]{1,0:T(8,128)}) custom-call(s32[7]{0:T(128)S(1)} %copy-done.5, bf16[256,768]{1,0:T(8,128)(2,1)S(1)} %copy-done, bf16[256,768]{1,0:T(8,128)(2,1)S(1)} %collective-permute-done.22.refs_1_, bf16[256,768]{1,0:T(8,128)(2,1)S(1)} %collective-permute-done.23.refs_2_, ...), custom_call_target="tpu_custom_call" | custom-call | flops 1811939328 | bytes 9043968 | tf_op jit(solution)/shard_map/weight_gradient_own/pallas_call | solution.py:488
  282.0 0.7 copy.14
  (57 shorter events, 0.1 us)
Async XLA Ops:
  18.3 31.6 %copy-start.1 = (bf16[1040,256]{1,0:T(8,128)(2,1)S(1)}, bf16[1040,256]{1,0:T(8,128)(2,1)}, u32[]{:S(2)}) copy-start(bf16[1040,256]{1,0:T(8,128)(2,1)} %pack_first.1.refs_0_) | copy-start | bytes 1597444
  18.4 12.4 %collective-permute-start.1 = (bf16[1040,256]{1,0:T(8,128)(2,1)}, bf16[1040,256]{1,0:T(8,128)(2,1)S(1)}, u32[]{:S(2)}, u32[]{:S(2)}) collective-permute-start(bf16[1040,256]{1,0:T(8,128)(2,1)} %pack_first.1.refs_0_), channel_id=1, source_target_pairs={{0,8},{4,20},{8,0},{12,28},{16,24},{20,4},{24,16},{28,12},{1,9},{5... | collective-permute-start | bytes 1597448 | tf_op jit(solution)/shard_map/ppermute | solution.py:128
  19.7 36.5 %collective-permute-start.2 = (bf16[1040,256]{1,0:T(8,128)(2,1)}, bf16[1040,256]{1,0:T(8,128)(2,1)S(1)}, u32[]{:S(2)}, u32[]{:S(2)}) collective-permute-start(bf16[1040,256]{1,0:T(8,128)(2,1)} %pack_first.1.refs_0_), channel_id=1, source_target_pairs={{0,20},{4,8},{8,28},{12,0},{16,4},{20,24},{24,12},{28,16},{1,21},{... | collective-permute-start | bytes 1597448 | tf_op jit(solution)/shard_map/ppermute | solution.py:128
  30.7 52.6 %copy-start.9 = (bf16[1040,256]{1,0:T(8,128)(2,1)}, bf16[1040,256]{1,0:T(8,128)(2,1)S(1)}, u32[]{:S(2)}) copy-start(bf16[1040,256]{1,0:T(8,128)(2,1)S(1)} %collective-permute-done.1.refs_2_) | copy-start | bytes 1597444
  47.8 11.0 %collective-permute-start.6 = (bf16[1024,256]{1,0:T(8,128)(2,1)}, bf16[1024,256]{1,0:T(8,128)(2,1)}, u32[]{:S(2)}, u32[]{:S(2)}) collective-permute-start(bf16[1024,256]{1,0:T(8,128)(2,1)} %pack_next.2.refs_0_), channel_id=1, source_target_pairs={{0,8},{4,20},{8,0},{12,28},{16,24},{20,4},{24,16},{28,12},{1,9},{5... | collective-permute-start | bytes 1572872 | tf_op jit(solution)/shard_map/ppermute | solution.py:128
  49.9 33.4 %collective-permute-start = (bf16[1040,256]{1,0:T(8,128)(2,1)S(1)}, bf16[1040,256]{1,0:T(8,128)(2,1)S(1)}, u32[]{:S(2)}, u32[]{:S(2)}) collective-permute-start(bf16[1040,256]{1,0:T(8,128)(2,1)S(1)} %copy-done.1), channel_id=1, source_target_pairs={{4,0},{12,8},{20,16},{28,24},{5,1},{13,9},{21,17},{29,25},{6,2},{1... | collective-permute-start | bytes 1597448 | tf_op jit(solution)/shard_map/ppermute | solution.py:128
  54.8 30.6 %collective-permute-start.7 = (bf16[1024,256]{1,0:T(8,128)(2,1)}, bf16[1024,256]{1,0:T(8,128)(2,1)}, u32[]{:S(2)}, u32[]{:S(2)}) collective-permute-start(bf16[1024,256]{1,0:T(8,128)(2,1)} %pack_next.2.refs_0_), channel_id=1, source_target_pairs={{0,20},{4,8},{8,28},{12,0},{16,4},{20,24},{24,12},{28,16},{1,21},{... | collective-permute-start | bytes 1572872 | tf_op jit(solution)/shard_map/ppermute | solution.py:128
  54.8 33.9 %collective-permute-start.4 = (bf16[1040,256]{1,0:T(8,128)(2,1)S(1)}, bf16[1040,256]{1,0:T(8,128)(2,1)S(1)}, u32[]{:S(2)}, u32[]{:S(2)}) collective-permute-start(bf16[1040,256]{1,0:T(8,128)(2,1)S(1)} %collective-permute-done.1.refs_2_), channel_id=1, source_target_pairs={{0,20},{8,28},{16,4},{24,12},{1,21},{9,29},{17,5},{25,13},{2,22},{... | collective-permute-start | bytes 1597448 | tf_op jit(solution)/shard_map/ppermute | solution.py:128
  56.1 41.8 %copy-start.11 = (bf16[1040,256]{1,0:T(8,128)(2,1)}, bf16[1040,256]{1,0:T(8,128)(2,1)S(1)}, u32[]{:S(2)}) copy-start(bf16[1040,256]{1,0:T(8,128)(2,1)S(1)} %collective-permute-done.2.refs_3_) | copy-start | bytes 1597444
  56.1 34.6 %collective-permute-start.3 = (bf16[1040,256]{1,0:T(8,128)(2,1)S(1)}, bf16[1040,256]{1,0:T(8,128)(2,1)S(1)}, u32[]{:S(2)}, u32[]{:S(2)}) collective-permute-start(bf16[1040,256]{1,0:T(8,128)(2,1)S(1)} %collective-permute-done.1.refs_2_), channel_id=1, source_target_pairs={{4,12},{12,4},{20,28},{28,20},{5,13},{13,5},{21,29},{29,21},{6,14}... | collective-permute-start | bytes 1597448 | tf_op jit(solution)/shard_map/ppermute | solution.py:128
  58.8 26.6 %collective-permute-start.5 = (bf16[1024,256]{1,0:T(8,128)(2,1)}, bf16[1024,256]{1,0:T(8,128)(2,1)}, u32[]{:S(2)}, u32[]{:S(2)}) collective-permute-start(bf16[1024,256]{1,0:T(8,128)(2,1)} %pack_next.2.refs_0_), channel_id=1, source_target_pairs={{4,0},{12,8},{20,16},{28,24},{5,1},{13,9},{21,17},{29,25},{6,2},{1... | collective-permute-start | bytes 1572872 | tf_op jit(solution)/shard_map/ppermute | solution.py:128
  83.3 0.8 copy-start.13
  84.1 12.5 %collective-permute-start.11 = (bf16[1024,256]{1,0:T(8,128)(2,1)}, bf16[1024,256]{1,0:T(8,128)(2,1)}, u32[]{:S(2)}, u32[]{:S(2)}) collective-permute-start(bf16[1024,256]{1,0:T(8,128)(2,1)} %pack_next.3.refs_0_), channel_id=1, source_target_pairs={{0,8},{4,20},{8,0},{12,28},{16,24},{20,4},{24,16},{28,12},{1,9},{5... | collective-permute-start | bytes 1572872 | tf_op jit(solution)/shard_map/ppermute | solution.py:128
  85.4 12.6 %collective-permute-start.12 = (bf16[1024,256]{1,0:T(8,128)(2,1)}, bf16[1024,256]{1,0:T(8,128)(2,1)S(1)}, u32[]{:S(2)}, u32[]{:S(2)}) collective-permute-start(bf16[1024,256]{1,0:T(8,128)(2,1)} %pack_next.3.refs_0_), channel_id=1, source_target_pairs={{0,20},{4,8},{8,28},{12,0},{16,4},{20,24},{24,12},{28,16},{1,21},{... | collective-permute-start | bytes 1572872 | tf_op jit(solution)/shard_map/ppermute | solution.py:128
  85.4 81.3 %collective-permute-start.10 = (bf16[1024,256]{1,0:T(8,128)(2,1)}, bf16[1024,256]{1,0:T(8,128)(2,1)}, u32[]{:S(2)}, u32[]{:S(2)}) collective-permute-start(bf16[1024,256]{1,0:T(8,128)(2,1)} %pack_next.3.refs_0_), channel_id=1, source_target_pairs={{4,0},{12,8},{20,16},{28,24},{5,1},{13,9},{21,17},{29,25},{6,2},{1... | collective-permute-start | bytes 1572872 | tf_op jit(solution)/shard_map/ppermute | solution.py:128
  88.7 0.8 copy-start.15
  89.5 78.5 %collective-permute-start.9 = (bf16[1024,256]{1,0:T(8,128)(2,1)}, bf16[1024,256]{1,0:T(8,128)(2,1)}, u32[]{:S(2)}, u32[]{:S(2)}) collective-permute-start(bf16[1024,256]{1,0:T(8,128)(2,1)} %collective-permute-done.6.refs_2_), channel_id=1, source_target_pairs={{0,20},{8,28},{16,4},{24,12},{1,21},{9,29},{17,5},{25,13},{2,22},{... | collective-permute-start | bytes 1572872 | tf_op jit(solution)/shard_map/ppermute | solution.py:128
  90.8 0.8 copy-start.17
  91.6 76.5 %collective-permute-start.8 = (bf16[1024,256]{1,0:T(8,128)(2,1)}, bf16[1024,256]{1,0:T(8,128)(2,1)}, u32[]{:S(2)}, u32[]{:S(2)}) collective-permute-start(bf16[1024,256]{1,0:T(8,128)(2,1)} %collective-permute-done.6.refs_2_), channel_id=1, source_target_pairs={{4,12},{12,4},{20,28},{28,20},{5,13},{13,5},{21,29},{29,21},{6,14}... | collective-permute-start | bytes 1572872 | tf_op jit(solution)/shard_map/ppermute | solution.py:128
  95.8 21.3 %copy-start.4 = (s32[7]{0:T(128)}, s32[7]{0:T(128)S(1)}, u32[]{:S(2)}) copy-start(s32[7]{0:T(128)S(1)} %stack.28.place_ref) | copy-start | bytes 88
  96.6 82.2 %collective-permute-start.14 = (bf16[1024,256]{1,0:T(8,128)(2,1)}, bf16[1024,256]{1,0:T(8,128)(2,1)}, u32[]{:S(2)}, u32[]{:S(2)}) collective-permute-start(bf16[1024,256]{1,0:T(8,128)(2,1)} %collective-permute-done.11.refs_2_), channel_id=1, source_target_pairs={{0,20},{8,28},{16,4},{24,12},{1,21},{9,29},{17,5},{25,13},{2,22},{... | collective-permute-start | bytes 1572872 | tf_op jit(solution)/shard_map/ppermute | solution.py:128
  98.0 0.8 copy-start.19
  98.8 80.8 %collective-permute-start.13 = (bf16[1024,256]{1,0:T(8,128)(2,1)}, bf16[1024,256]{1,0:T(8,128)(2,1)}, u32[]{:S(2)}, u32[]{:S(2)}) collective-permute-start(bf16[1024,256]{1,0:T(8,128)(2,1)} %collective-permute-done.11.refs_2_), channel_id=1, source_target_pairs={{4,12},{12,4},{20,28},{28,20},{5,13},{13,5},{21,29},{29,21},{6,14}... | collective-permute-start | bytes 1572872 | tf_op jit(solution)/shard_map/ppermute | solution.py:128
  102.9 1.0 copy-start.10
  104.0 1.0 copy-start.12
  105.0 1.0 copy-start.14
  106.0 1.0 copy-start.16
  107.1 1.0 copy-start.18
  108.1 59.9 %copy-start.7 = (bf16[384,768]{1,0:T(8,128)(2,1)S(1)}, bf16[384,768]{1,0:T(8,128)(2,1)}, u32[]{:S(2)}) copy-start(bf16[384,768]{1,0:T(8,128)(2,1)} %refs_4_) | copy-start | bytes 1769476
  117.1 49.6 %copy-start.6 = (bf16[384,768]{1,0:T(8,128)(2,1)S(1)}, bf16[384,768]{1,0:T(8,128)(2,1)}, u32[]{:S(2)}) copy-start(bf16[384,768]{1,0:T(8,128)(2,1)} %refs_3_) | copy-start | bytes 1769476
  117.1 51.4 %copy-start.2 = (bf16[1024,256]{1,0:T(8,128)(2,1)S(1)}, bf16[1024,256]{1,0:T(8,128)(2,1)}, u32[]{:S(2)}) copy-start(bf16[1024,256]{1,0:T(8,128)(2,1)} %pack_next.2.refs_0_) | copy-start | bytes 1572868
  117.1 51.4 %copy-start.5 = (s32[7]{0:T(128)S(1)}, s32[7]{0:T(128)}, u32[]{:S(2)}) copy-start(s32[7]{0:T(128)} %copy-done.4) | copy-start | bytes 88
  166.7 24.5 %collective-permute-start.15 = (bf16[384,768]{1,0:T(8,128)(2,1)S(1)}, bf16[384,768]{1,0:T(8,128)(2,1)S(1)}, u32[]{:S(2)}, u32[]{:S(2)}) collective-permute-start(bf16[384,768]{1,0:T(8,128)(2,1)S(1)} %copy-done.6), channel_id=1, source_target_pairs={{0,4},{4,0},{8,12},{12,8},{16,20},{20,16},{24,28},{28,24},{1,5},{5... | collective-permute-start | bytes 1769480 | tf_op jit(solution)/shard_map/ppermute | solution.py:128
  168.0 27.6 %collective-permute-start.16 = (bf16[384,768]{1,0:T(8,128)(2,1)S(1)}, bf16[384,768]{1,0:T(8,128)(2,1)S(1)}, u32[]{:S(2)}, u32[]{:S(2)}) collective-permute-start(bf16[384,768]{1,0:T(8,128)(2,1)S(1)} %copy-done.7), channel_id=1, source_target_pairs={{0,4},{4,0},{8,12},{12,8},{16,20},{20,16},{24,28},{28,24},{1,5},{5... | collective-permute-start | bytes 1769480 | tf_op jit(solution)/shard_map/ppermute | solution.py:128
  168.1 27.6 %collective-permute-start.17 = (bf16[384,768]{1,0:T(8,128)(2,1)}, bf16[384,768]{1,0:T(8,128)(2,1)S(1)}, u32[]{:S(2)}, u32[]{:S(2)}) collective-permute-start(bf16[384,768]{1,0:T(8,128)(2,1)} %refs_5_), channel_id=1, source_target_pairs={{0,4},{4,0},{8,12},{12,8},{16,20},{20,16},{24,28},{28,24},{1,5},{5... | collective-permute-start | bytes 1769480 | tf_op jit(solution)/shard_map/ppermute | solution.py:128
  168.5 10.3 %copy-start.23 = (bf16[256,768]{1,0:T(8,128)(2,1)S(1)}, bf16[256,768]{1,0:T(8,128)(2,1)}, u32[]{:S(2)}) copy-start(bf16[256,768]{1,0:T(8,128)(2,1)} %get-tuple-element.51) | copy-start | bytes 1179652
  168.5 11.1 %copy-start.21 = (bf16[256,768]{1,0:T(8,128)(2,1)S(1)}, bf16[256,768]{1,0:T(8,128)(2,1)}, u32[]{:S(2)}) copy-start(bf16[256,768]{1,0:T(8,128)(2,1)} %get-tuple-element.53) | copy-start | bytes 1179652
  168.5 12.6 %copy-start.3 = (bf16[1024,256]{1,0:T(8,128)(2,1)S(1)}, bf16[1024,256]{1,0:T(8,128)(2,1)}, u32[]{:S(2)}) copy-start(bf16[1024,256]{1,0:T(8,128)(2,1)} %pack_next.3.refs_0_) | copy-start | bytes 1572868
  168.5 12.6 %copy-start.20 = (bf16[1024,256]{1,0:T(8,128)(2,1)S(1)}, bf16[1024,256]{1,0:T(8,128)(2,1)}, u32[]{:S(2)}) copy-start(bf16[1024,256]{1,0:T(8,128)(2,1)} %copy-done.19) | copy-start | bytes 1572868
  178.8 25.5 %collective-permute-start.23 = (bf16[256,768]{1,0:T(8,128)(2,1)S(1)}, bf16[256,768]{1,0:T(8,128)(2,1)S(1)}, u32[]{:S(2)}, u32[]{:S(2)}) collective-permute-start(bf16[256,768]{1,0:T(8,128)(2,1)S(1)} %copy-done.23), channel_id=1, source_target_pairs={{0,8},{4,20},{8,0},{12,28},{16,24},{20,4},{24,16},{28,12},{1,9},{5... | collective-permute-start | bytes 1179656 | tf_op jit(solution)/shard_map/ppermute | solution.py:128
  179.6 15.9 %copy-start.22 = (bf16[256,768]{1,0:T(8,128)(2,1)S(1)}, bf16[256,768]{1,0:T(8,128)(2,1)}, u32[]{:S(2)}) copy-start(bf16[256,768]{1,0:T(8,128)(2,1)} %get-tuple-element.52) | copy-start | bytes 1179652
  179.6 16.0 %copy-start = (bf16[256,768]{1,0:T(8,128)(2,1)S(1)}, bf16[256,768]{1,0:T(8,128)(2,1)}, u32[]{:S(2)}) copy-start(bf16[256,768]{1,0:T(8,128)(2,1)} %get-tuple-element.50.refs_0_) | copy-start | bytes 1179652
  179.6 18.4 %copy-start.8 = (bf16[384,768]{1,0:T(8,128)(2,1)S(1)}, bf16[384,768]{1,0:T(8,128)(2,1)}, u32[]{:S(2)}) copy-start(bf16[384,768]{1,0:T(8,128)(2,1)} %refs_5_) | copy-start | bytes 1769476
  179.6 25.3 %collective-permute-start.26 = (bf16[256,768]{1,0:T(8,128)(2,1)S(1)}, bf16[256,768]{1,0:T(8,128)(2,1)S(1)}, u32[]{:S(2)}, u32[]{:S(2)}) collective-permute-start(bf16[256,768]{1,0:T(8,128)(2,1)S(1)} %copy-done.21), channel_id=1, source_target_pairs={{0,28},{8,20},{16,12},{24,4},{1,29},{9,21},{17,13},{25,5},{2,30},{... | collective-permute-start | bytes 1179656 | tf_op jit(solution)/shard_map/ppermute | solution.py:128
  191.2 13.7 %collective-permute-start.25 = (bf16[256,768]{1,0:T(8,128)(2,1)S(1)}, bf16[256,768]{1,0:T(8,128)(2,1)S(1)}, u32[]{:S(2)}, u32[]{:S(2)}) collective-permute-start(bf16[256,768]{1,0:T(8,128)(2,1)S(1)} %copy-done.21), channel_id=1, source_target_pairs={{4,28},{12,20},{20,12},{28,4},{5,29},{13,21},{21,13},{29,5},{6,30}... | collective-permute-start | bytes 1179656 | tf_op jit(solution)/shard_map/ppermute | solution.py:128
  195.6 9.3 %collective-permute-start.24 = (bf16[256,768]{1,0:T(8,128)(2,1)S(1)}, bf16[256,768]{1,0:T(8,128)(2,1)S(1)}, u32[]{:S(2)}, u32[]{:S(2)}) collective-permute-start(bf16[256,768]{1,0:T(8,128)(2,1)S(1)} %copy-done.22), channel_id=1, source_target_pairs={{0,20},{4,8},{8,28},{12,0},{16,4},{20,24},{24,12},{28,16},{1,21},{... | collective-permute-start | bytes 1179656 | tf_op jit(solution)/shard_map/ppermute | solution.py:128
  195.7 9.3 %collective-permute-start.22 = (bf16[256,768]{1,0:T(8,128)(2,1)S(1)}, bf16[256,768]{1,0:T(8,128)(2,1)S(1)}, u32[]{:S(2)}, u32[]{:S(2)}) collective-permute-start(bf16[256,768]{1,0:T(8,128)(2,1)S(1)} %copy-done), channel_id=1, source_target_pairs={{4,0},{12,8},{20,16},{28,24},{5,1},{13,9},{21,17},{29,25},{6,2},{1... | collective-permute-start | bytes 1179656 | tf_op jit(solution)/shard_map/ppermute | solution.py:128
  204.4 12.6 %collective-permute-start.18 = (bf16[256,768]{1,0:T(8,128)(2,1)S(1)}, bf16[256,768]{1,0:T(8,128)(2,1)S(1)}, u32[]{:S(2)}, u32[]{:S(2)}) collective-permute-start(bf16[256,768]{1,0:T(8,128)(2,1)S(1)} %get-tuple-element.46), channel_id=1, source_target_pairs={{0,1},{1,0},{2,3},{3,2},{4,5},{5,4},{6,7},{7,6},{8,9},{9,8},{10,11... | collective-permute-start | bytes 1179656 | tf_op jit(solution)/shard_map/ppermute | solution.py:571
  209.3 67.2 %collective-permute-start.27 = (f32[384,768]{1,0:T(8,128)S(1)}, f32[384,768]{1,0:T(8,128)S(1)}, u32[]{:S(2)}, u32[]{:S(2)}) collective-permute-start(f32[384,768]{1,0:T(8,128)S(1)} %get-tuple-element.54), channel_id=1, source_target_pairs={{0,4},{4,0},{8,12},{12,8},{16,20},{20,16},{24,28},{28,24},{1,5},{5... | collective-permute-start | bytes 3538952 | tf_op jit(solution)/shard_map/ppermute | solution.py:128
  209.5 66.9 %collective-permute-start.28 = (f32[384,768]{1,0:T(8,128)S(1)}, f32[384,768]{1,0:T(8,128)S(1)}, u32[]{:S(2)}, u32[]{:S(2)}) collective-permute-start(f32[384,768]{1,0:T(8,128)S(1)} %get-tuple-element.55), channel_id=1, source_target_pairs={{0,4},{4,0},{8,12},{12,8},{16,20},{20,16},{24,28},{28,24},{1,5},{5... | collective-permute-start | bytes 3538952 | tf_op jit(solution)/shard_map/ppermute | solution.py:128
  209.8 66.6 %collective-permute-start.29 = (f32[384,768]{1,0:T(8,128)S(1)}, f32[384,768]{1,0:T(8,128)S(1)}, u32[]{:S(2)}, u32[]{:S(2)}) collective-permute-start(f32[384,768]{1,0:T(8,128)S(1)} %get-tuple-element.56), channel_id=1, source_target_pairs={{0,4},{4,0},{8,12},{12,8},{16,20},{20,16},{24,28},{28,24},{1,5},{5... | collective-permute-start | bytes 3538952 | tf_op jit(solution)/shard_map/ppermute | solution.py:128
  210.0 28.2 %collective-permute-start.19 = (bf16[256,768]{1,0:T(8,128)(2,1)S(1)}, bf16[256,768]{1,0:T(8,128)(2,1)S(1)}, u32[]{:S(2)}, u32[]{:S(2)}) collective-permute-start(bf16[256,768]{1,0:T(8,128)(2,1)S(1)} %get-tuple-element.47), channel_id=1, source_target_pairs={{0,2},{1,3},{2,0},{3,1},{4,6},{5,7},{6,4},{7,5},{8,10},{9,11},{10,... | collective-permute-start | bytes 1179656 | tf_op jit(solution)/shard_map/ppermute | solution.py:571
  217.0 21.2 %collective-permute-start.20 = (bf16[256,768]{1,0:T(8,128)(2,1)S(1)}, bf16[256,768]{1,0:T(8,128)(2,1)S(1)}, u32[]{:S(2)}, u32[]{:S(2)}) collective-permute-start(bf16[256,768]{1,0:T(8,128)(2,1)S(1)} %get-tuple-element.48), channel_id=1, source_target_pairs={{0,3},{1,2},{2,1},{3,0},{4,7},{5,6},{6,5},{7,4},{8,11},{9,10},{10,... | collective-permute-start | bytes 1179656 | tf_op jit(solution)/shard_map/ppermute | solution.py:571
  238.4 38.0 %collective-permute-start.21 = (bf16[256,768]{1,0:T(8,128)(2,1)S(1)}, bf16[256,768]{1,0:T(8,128)(2,1)S(1)}, u32[]{:S(2)}, u32[]{:S(2)}) collective-permute-start(bf16[256,768]{1,0:T(8,128)(2,1)S(1)} %add_convert_fusion), channel_id=1, source_target_pairs={{0,0},{1,4},{2,8},{3,12},{4,20},{5,16},{6,28},{7,24},{8,9},{9,13},... | collective-permute-start | bytes 1179656 | tf_op jit(solution)/shard_map/ppermute | solution.py:584

commit v3 on v0

--- a/solution.py
+++ b/solution.py
@@ -1,9 +1,15 @@
+import functools
+
 import jax
 import jax.numpy as jnp
 from jax import lax
+from jax.experimental import pallas as pl
+from jax.experimental.pallas import tpu as pltpu
 from jax.sharding import PartitionSpec as P
 
 HD = 128
+LOG2E = 1.4426950408889634
+MIB = 1024 * 1024
 
 
 def shifted(value, axis, steps):
@@ -48,7 +54,7 @@
     return (query_grad, jnp.concatenate([key_grad, value_grad], axis=-1))
 
 
-def body(
+def halo_body(
     normed,
     queries,
     saved_keys,
@@ -111,7 +117,486 @@
     return (input_grad, grad_query, grad_key, grad_value)
 
 
+def moved(value, target):
+    prompts, views = lax.axis_size("dp"), lax.axis_size("view")
+    pairs = []
+    for y in range(prompts):
+        for v in range(views):
+            goal = target(y, v)
+            if goal is not None:
+                pairs.append((y * views + v, goal[0] * views + goal[1]))
+    return lax.ppermute(value, ("dp", "view"), pairs)
+
+
+def straight(y, v):
+    return (y, v ^ 2) if v % 2 == 0 else (y ^ 1, v)
+
+
+def crossed(y, v):
+    return (y ^ 1, v ^ 1) if v % 2 == 0 else (y, v ^ 3)
+
+
+def inwards(y, v):
+    return None if v % 2 == 0 else (y, v ^ 1)
+
+
+def relay_x(y, v):
+    return None if v % 2 == 0 else (y, v ^ 2)
+
+
+def relay_y(y, v):
+    return (y ^ 1, v ^ 1) if v % 2 == 0 else None
+
+
+def corner_same(y, v):
+    return None if v % 2 == 0 else (y ^ 1, v ^ 2)
+
+
+def corner_cross(y, v):
+    return (y ^ 1, v ^ 3) if v % 2 == 0 else None
+
+
+def mate(y, v):
+    return (y, v ^ 1)
+
+
+def lanes(start, size):
+    return pl.ds(pl.multiple_of(start, HD), size)
+
+
+def whole(space=pltpu.VMEM):
+    return pl.BlockSpec(memory_space=space)
+
+
+def dot_last(a, b):
+    return lax.dot_general(a, b, (((1,), (1,)), ((), ())), preferred_element_type=jnp.float32)
+
+
+def dot_first(a, b):
+    return lax.dot_general(a, b, (((0,), (0,)), ((), ())), preferred_element_type=jnp.float32)
+
+
+def dot(a, b):
+    return jnp.dot(a, b, preferred_element_type=jnp.float32)
+
+
+def run_copies(copies):
+    for copy in copies:
+        copy.start()
+    for copy in copies:
+        copy.wait()
+
+
+FLAG_ROWS = 16
+
+
+def pack_kernel(opening, links_ref, q_ref, k_ref, v_ref, g_ref, out_ref):
+    length, width = q_ref.shape
+    for kind, source in enumerate((q_ref, k_ref, v_ref, g_ref)):
+        out_ref[kind * length : (kind + 1) * length] = source[...]
+    if opening:
+        row = lax.broadcasted_iota(jnp.int32, (FLAG_ROWS, width), 0)
+        gaps = [
+            jnp.where(links_ref[0, side] >= 0, 0.0, 1.0).astype(jnp.float32) for side in range(2)
+        ]
+        flags = jnp.where(row < FLAG_ROWS // 2, gaps[0], gaps[1])
+        out_ref[4 * length : 4 * length + FLAG_ROWS] = flags.astype(out_ref.dtype)
+
+
+def pack(chunk, width, links, arrays):
+    length = arrays[0].shape[0]
+    height = 4 * length + (FLAG_ROWS if chunk == 0 else 0)
+    return pl.pallas_call(
+        functools.partial(pack_kernel, chunk == 0),
+        grid=(1,),
+        out_shape=jax.ShapeDtypeStruct((height, width), jnp.bfloat16),
+        in_specs=[whole(pltpu.SMEM)] + [pl.BlockSpec((length, width), lambda i: (0, chunk))] * 4,
+        out_specs=pl.BlockSpec((height, width), lambda i: (0, 0)),
+        name="pack_heads",
+    )(links, *arrays)
+
+
+def attention_kernel(scaling, role, place_ref, *refs):
+    sources, openers, out_ref = refs[:4], refs[4:8], refs[8]
+    x, flags, kacc, vacc, out, sems = refs[9:]
+    odd = place_ref[1]
+    _, length, triple = out.shape
+    width = triple // 3
+    factor = scaling * LOG2E
+
+    def rows(e, kind, head):
+        return x[e, kind * length : (kind + 1) * length, lanes(head * HD, HD)]
+
+    def one_head(head, carry):
+        seen = set()
+        here = lanes(head * HD, HD)
+        for e in range(4):
+            blocks = ((e + 3) % 4, e, (e + 1) % 4)
+            gaps = flags[e].astype(jnp.float32) * 1e30
+            before, after = gaps[0:1, :length], gaps[FLAG_ROWS // 2 : FLAG_ROWS // 2 + 1, :length]
+            far_below = jnp.where(odd == 0, before, after)
+            far_above = jnp.where(odd == 0, after, before)
+            q = rows(e, 0, head)
+            g = rows(e, 3, head)
+            scores = [dot_last(rows(f, 1, head), q) for f in blocks]
+            tops = [jnp.max(s, axis=0, keepdims=True) for s in scores]
+            top = jnp.maximum(tops[1], jnp.maximum(tops[0] - far_below, tops[2] - far_above))
+            offsets = (top + far_below, top, top + far_above)
+            powers = [jnp.exp2((s - o) * factor) for s, o in zip(scores, offsets)]
+            inverse = 1.0 / sum(jnp.sum(p, axis=0, keepdims=True) for p in powers)
+            prob_grads = [dot_last(rows(f, 2, head), g) for f in blocks]
+            delta = inverse * sum(
+                jnp.sum(p * d, axis=0, keepdims=True) for p, d in zip(powers, prob_grads)
+            )
+            query_grad = None
+            for f, p, d in zip(blocks, powers, prob_grads):
+                probs = p * inverse
+                score_grad = (probs * scaling * (d - delta)).astype(jnp.bfloat16)
+                part = dot_first(score_grad, rows(f, 1, head))
+                query_grad = part if query_grad is None else query_grad + part
+                key_part = dot(score_grad, q)
+                value_part = dot(probs.astype(jnp.bfloat16), g)
+                if f in seen:
+                    kacc[f] += key_part
+                    vacc[f] += value_part
+                else:
+                    seen.add(f)
+                    kacc[f] = key_part
+                    vacc[f] = value_part
+            out[e, :, here] = query_grad.astype(out.dtype)
+        for f in range(4):
+            out[f, :, lanes(width + head * HD, HD)] = kacc[f].astype(out.dtype)
+            out[f, :, lanes(2 * width + head * HD, HD)] = vacc[f].astype(out.dtype)
+        return carry
+
+    @pl.when(place_ref[0] == role)
+    def _():
+        run_copies(
+            [
+                pltpu.make_async_copy(source.at[0 : 4 * length], x.at[e], sems.at[e])
+                for e, source in enumerate(sources)
+            ]
+            + [
+                pltpu.make_async_copy(
+                    opener.at[4 * length : 4 * length + FLAG_ROWS], flags.at[e], sems.at[4 + e]
+                )
+                for e, opener in enumerate(openers)
+            ]
+        )
+        lax.fori_loop(0, width // HD, one_head, 0)
+        run_copies([pltpu.make_async_copy(out, out_ref, sems.at[8])])
+
+
+def attention(place, role, sources, openers, length):
+    width = sources[0].shape[1]
+    out = jax.ShapeDtypeStruct((4, length, 3 * width), jnp.bfloat16)
+    return pl.pallas_call(
+        functools.partial(attention_kernel, HD ** (-0.5), role),
+        out_shape=out,
+        in_specs=[whole(pltpu.SMEM)] + [whole(pltpu.HBM)] * 8,
+        out_specs=whole(pltpu.HBM),
+        scratch_shapes=[
+            pltpu.VMEM((4, 4 * length, width), jnp.bfloat16),
+            pltpu.VMEM((4, FLAG_ROWS, width), jnp.bfloat16),
+            pltpu.VMEM((4, length, HD), jnp.float32),
+            pltpu.VMEM((4, length, HD), jnp.float32),
+            pltpu.VMEM(out.shape, out.dtype),
+            pltpu.SemaphoreType.DMA((9,)),
+        ],
+        compiler_params=pltpu.CompilerParams(vmem_limit_bytes=32 * MIB),
+        cost_estimate=pl.CostEstimate(
+            flops=4 * 5 * 2 * length * 3 * length * width * 2,
+            bytes_accessed=2 * length * 7 * width * 4,
+            transcendentals=12 * length * length * (width // HD),
+        ),
+        name="attention_gradients",
+    )(place, *sources, *openers)
+
+
+def input_kernel(role, chunks, place_ref, *refs):
+    grad_refs, weight_refs, out_refs = refs[:chunks], refs[chunks : chunks + 2], refs[chunks + 2 : -4]
+    grads, weights, outs, sems = refs[-4:]
+    core, plane = place_ref[0], place_ref[2]
+    rows = weights.shape[2]
+    width = grads.shape[3] // 3
+    slots = len(out_refs)
+    order = list(range(1, slots)) + [0]
+
+    @pl.when(core == role)
+    def _():
+        fetches = [
+            pltpu.make_async_copy(ref, weights.at[side], sems.at[side])
+            for side, ref in enumerate(weight_refs)
+        ]
+        loads = {
+            s: [
+                pltpu.make_async_copy(
+                    ref.at[jnp.bitwise_xor(plane, s)], grads.at[s, chunk], sems.at[2 + s * chunks + chunk]
+                )
+                for chunk, ref in enumerate(grad_refs)
+            ]
+            for s in order
+        }
+        stores = [
+            pltpu.make_async_copy(outs.at[s], out, sems.at[2 + slots * chunks + s])
+            for s, out in enumerate(out_refs)
+        ]
+        for copy in fetches + [load for s in order for load in loads[s]]:
+            copy.start()
+        for copy in fetches:
+            copy.wait()
+        for s in order:
+            for load in loads[s]:
+                load.wait()
+            for side, at in ((0, core), (1, 1 - core)):
+                total = None
+                for chunk in range(chunks):
+                    right = jnp.concatenate(
+                        [
+                            weights[side, kind, :, chunk * width : (chunk + 1) * width]
+                            for kind in range(3)
+                        ],
+                        axis=1,
+                    )
+                    part = dot_last(grads[s, chunk], right)
+                    total = part if total is None else total + part
+                outs[s, :, lanes(at * rows, rows)] = total.astype(outs.dtype)
+            stores[s].start()
+        for store in stores:
+            store.wait()
+
+
+def input_product(place, role, grads, own_weights, mate_weights):
+    blocks, length, triple = grads[0].shape
+    _, rows, cols = own_weights.shape
+    chunks = len(grads)
+    out = jax.ShapeDtypeStruct((length, 2 * rows), jnp.bfloat16)
+    return pl.pallas_call(
+        functools.partial(input_kernel, role, chunks),
+        out_shape=[out] * blocks,
+        in_specs=[whole(pltpu.SMEM)] + [whole(pltpu.HBM)] * (chunks + 2),
+        out_specs=[whole(pltpu.HBM)] * blocks,
+        scratch_shapes=[
+            pltpu.VMEM((blocks, chunks, length, triple), jnp.bfloat16),
+            pltpu.VMEM((2, 3, rows, cols), jnp.bfloat16),
+            pltpu.VMEM((blocks, length, 2 * rows), jnp.bfloat16),
+            pltpu.SemaphoreType.DMA((2 + blocks * (chunks + 1),)),
+        ],
+        compiler_params=pltpu.CompilerParams(vmem_limit_bytes=32 * MIB),
+        cost_estimate=pl.CostEstimate(
+            flops=2 * blocks * length * 2 * rows * 3 * cols,
+            bytes_accessed=2 * (blocks * length * (2 * rows + 3 * cols) + 6 * rows * cols),
+            transcendentals=0,
+        ),
+        name="input_gradient",
+    )(place, *grads, own_weights, mate_weights)
+
+
+def weight_kernel(mine, mean_scale, chunks, place_ref, *refs):
+    sources, refs = refs[:6], refs[6:]
+    grad_refs, refs = (refs[:chunks], refs[chunks : 2 * chunks]), refs[2 * chunks :]
+    received, refs = (refs[:3], refs[3:]) if mine else ((), refs)
+    out_refs = refs[:3]
+    tokens, turned, grads, sems = refs[3:]
+    core = place_ref[0]
+    rows = out_refs[0].shape[0]
+    _, blocks, length, triple = grads.shape
+    width = triple // 3
+    start = (core if mine else 1 - core) * rows
+    own, mate_in, first, second, corner, corner_far = sources
+    chosen = ((own, mate_in, first, second), (first, second, corner, corner_far))
+
+    def copies(which):
+        return [
+            pltpu.make_async_copy(source.at[:, lanes(start, rows)], tokens.at[e], sems.at[e])
+            for e, source in enumerate(chosen[which])
+        ] + [
+            pltpu.make_async_copy(ref, grads.at[chunk], sems.at[blocks + chunk])
+            for chunk, ref in enumerate(grad_refs[which])
+        ]
+
+    for which in range(2):
+
+        @pl.when(core == which)
+        def _():
+            for copy in copies(which):
+                copy.start()
+
+    waits = copies(0)
+    for e in range(blocks):
+        waits[e].wait()
+        turned[:, e * length : (e + 1) * length] = tokens[e].T
+    for chunk in range(chunks):
+        waits[blocks + chunk].wait()
+        for kind, out in enumerate(out_refs):
+            right = grads[chunk, :, :, kind * width : (kind + 1) * width]
+            here = slice(chunk * width, (chunk + 1) * width)
+            total = dot(turned[...], right.reshape(blocks * length, width))
+            if mine:
+                total = (total + received[kind][:, here]) * mean_scale
+            out[:, here] = total
+
+
+def weight_product(place, mine, mean_scale, tokens, grads, received=()):
+    chunks = len(grads[0])
+    blocks, length, triple = grads[0][0].shape
+    rows = tokens[0].shape[1] // 2
+    cols = triple // 3 * chunks
+    return pl.pallas_call(
+        functools.partial(weight_kernel, mine, mean_scale, chunks),
+        out_shape=[jax.ShapeDtypeStruct((rows, cols), jnp.float32)] * 3,
+        in_specs=[whole(pltpu.SMEM)]
+        + [whole(pltpu.HBM)] * (6 + 2 * chunks)
+        + [whole()] * len(received),
+        out_specs=[whole()] * 3,
+        scratch_shapes=[
+            pltpu.VMEM((blocks, length, rows), jnp.bfloat16),
+            pltpu.VMEM((rows, blocks * length), jnp.bfloat16),
+            pltpu.VMEM((chunks, blocks, length, triple), jnp.bfloat16),
+            pltpu.SemaphoreType.DMA((blocks + chunks,)),
+        ],
+        compiler_params=pltpu.CompilerParams(vmem_limit_bytes=40 * MIB),
+        cost_estimate=pl.CostEstimate(
+            flops=2 * rows * 3 * cols * blocks * length,
+            bytes_accessed=2 * blocks * length * (rows + 3 * cols) + 12 * rows * cols,
+            transcendentals=0,
+        ),
+        name="weight_gradient_own" if mine else "weight_gradient_mate",
+    )(place, *tokens, *grads[0], *grads[1], *received)
+
+
+def after(values, *earlier):
+    return lax.optimization_barrier((tuple(values), tuple(earlier)))[0]
+
+
+def gather_body(
+    normed,
+    queries,
+    saved_keys,
+    saved_values,
+    output_grad,
+    view_links,
+    query_weight,
+    key_weight,
+    value_weight,
+):
+    length, cols = queries.shape[2:]
+    model_width = normed.shape[-1]
+    rows = query_weight.shape[0]
+    prompts, views, groups = (lax.axis_size(name) for name in ("dp", "view", "head"))
+    mean_scale = 1.0 / (prompts * views)
+    width = cols // 2
+    view = lax.axis_index("view")
+    core = lax.rem(view, 2)
+    chip = lax.axis_index("dp") * (views // 2) + view // 2
+    place = jnp.stack([core, core, lax.axis_index("head")]).astype(jnp.int32)
+
+    arrays = tuple(a.reshape(length, cols) for a in (queries, saved_keys, saved_values, output_grad))
+    packs, straights, crosseds, mates = [], [], [], []
+    for chunk in range(cols // width):
+        packs.append(pack(chunk, width, view_links, after(arrays, *mates[-1:])))
+        straights.append(moved(packs[-1], straight))
+        crosseds.append(moved(packs[-1], crossed))
+        (sent,) = after((packs[-1],), *mates[-1:])
+        mates.append(moved(sent, inwards))
+    relays_x, relays_y = [], []
+    for chunk, sent in enumerate(straights):
+        (sent,) = after((sent,), *straights[chunk + 1 :], *crosseds[chunk + 1 :], *relays_x[-1:])
+        relays_x.append(moved(sent, relay_x))
+        relays_y.append(moved(sent, relay_y))
+    sets = (
+        list(zip(packs, mates, straights, crosseds)),
+        list(zip(straights, crosseds, relays_x, relays_y)),
+    )
+
+    own_weights = jnp.stack(after((query_weight, key_weight, value_weight), mates[0]))
+    mate_weights = moved(own_weights, mate)
+
+    def exchange(role, slots):
+        total = slots[0].astype(jnp.float32)
+        for s in range(1, groups):
+            pairs = [
+                ((y * views + v) * groups + z, (y * views + v) * groups + (z ^ s))
+                for y in range(prompts)
+                for v in range(role, views, 2)
+                for z in range(groups)
+            ]
+            total += lax.ppermute(slots[s], ("dp", "view", "head"), pairs).astype(jnp.float32)
+        return total.astype(jnp.bfloat16)
+
+    def deliver(role, total):
+        pairs = [
+            (
+                (y * views + v) * groups + z,
+                ((y ^ role) * views + (v ^ z)) * groups + y * (views // 2) + v // 2,
+            )
+            for y in range(prompts)
+            for v in range(role, views, 2)
+            for z in range(groups)
+        ]
+        return lax.ppermute(total, ("dp", "view", "head"), pairs)
+
+    def attend_all(role, turn):
+        results = []
+        for sources in sets[role]:
+            results.append(attention(turn, role, sources, sets[role][0], length))
+            (turn,) = after((turn,), results[-1])
+        return results
+
+    first = attend_all(0, place)
+    first_slots = input_product(place, 0, first, own_weights, mate_weights)
+    (turn,) = after((place,), *first_slots)
+    second = attend_all(1, turn)
+    gate = (relays_x[-1], relays_y[-1], second[0])
+    first_total = exchange(0, after(first_slots, *gate))
+    (turn,) = after((place,), first_total)
+    second_slots = input_product(turn, 1, second, own_weights, mate_weights)
+    second_total = exchange(1, second_slots)
+    grads = (first, second)
+    landed = (deliver(0, first_total), deliver(1, second_total))
+    from_first = lax.axis_index("head") // (views // 2) == lax.axis_index("dp")
+    input_grad = jnp.where(from_first, landed[0], landed[1])
+
+    flat = normed.reshape(length, model_width)
+
+    def columns(of_chip):
+        return lax.dynamic_slice_in_dim(flat, of_chip * (2 * rows), 2 * rows, axis=1)
+
+    toward_x, toward_y = jnp.bitwise_xor(chip, 1), jnp.bitwise_xor(chip, 2)
+    here = columns(chip)
+    to_straight = columns(jnp.where(core == 0, toward_x, toward_y))
+    to_crossed = columns(jnp.where(core == 0, toward_y, toward_x))
+    to_corner = columns(jnp.bitwise_xor(chip, 3))
+    (sent,) = after((here,), mates[0])
+    (to_corner,) = after((to_corner,), *gate)
+    to_straight, to_crossed = after((to_straight, to_crossed), first_total)
+    tokens = (
+        here,
+        moved(sent, inwards),
+        moved(to_straight, straight),
+        moved(to_crossed, crossed),
+        moved(to_corner, corner_same),
+        moved(to_corner, corner_cross),
+    )
+    for_mate = weight_product(place, False, mean_scale, tokens, grads)
+    from_mate = [moved(w, mate) for w in for_mate]
+    weight_grads = weight_product(place, True, mean_scale, tokens, grads, from_mate)
+    return (
+        input_grad.reshape(1, 1, length, model_width // groups),
+        *weight_grads,
+    )
+
+
 def solution(mesh):
+    prompts, views, groups = (mesh.shape[name] for name in ("dp", "view", "head"))
+    loop_of_four = prompts * 2 == views and prompts * views == 2 * groups and views == groups
+
+    def choose(*arrays):
+        batch, held, length, cols = arrays[1].shape
+        if loop_of_four and batch == held == 1 and cols % (2 * HD) == 0 and cols >= 2 * length:
+            return gather_body(*arrays)
+        return halo_body(*arrays)
+
     placed = (
         P("dp", "view", None, None),
         P("dp", "view", None, "head"),
@@ -124,7 +609,7 @@
         P(("dp", "view"), "head"),
     )
     return jax.shard_map(
-        body,
+        choose,
         mesh=mesh,
         in_specs=placed,
         out_specs=(

time: 400 us -> 192 us (0.48)
  the two profiles are of different devices: /device:TPU:16 before, /device:TPU:1 now
where the time goes in v3:
time: 192 us; the launch traced here: 191 us
  starting transfers between devices  59.9 us (31%)
  waiting for transfers between devices  56 us (29%)
  Pallas kernels  54.5 us (28%)
  local copies, waits for them, and re-layouts  12.7 us (7%)
  other arithmetic  6.32 us (3%)
    ppermute x19, starting transfers between devices, moved(): return lax.ppermute(value, ('dp', 'view'), pairs)  43.6 us
    ppermute x19, waiting for transfers between devices, moved(): return lax.ppermute(value, ('dp', 'view'), pairs)  29.5 us
    pallas_call x4, Pallas kernels, attention(): pl.pallas_call(functools.partial(attention_kernel, HD ** (-0.5), role), o...  28.3 us
    ppermute x2, waiting for transfers between devices, deliver(): return lax.ppermute(total, ('dp', 'view', 'head'), pairs)  20.6 us
    pallas_call x2, Pallas kernels, weight_product(): pl.pallas_call(functools.partial(weight_kernel, mine, mean_scale, chunks)...  11.6 us
    ppermute x6, starting transfers between devices, exchange(): lax.ppermute(slots[s], ('dp', 'view', 'head'), pairs).astype(jnp.float32)  11.3 us
    unnamed x44, local copies, waits for them, and re-layouts  11.3 us
    pallas_call x2, Pallas kernels, input_product(): pl.pallas_call(functools.partial(input_kernel, role, chunks), out_shape=[...  10.2 us
  transfers between devices with their start and end apart: 27, of which 7 were waited for; matrix products, arithmetic and copies ran while one was open for 4% of the time, Pallas kernels for 24%

profile of v3, /device:TPU:1, one launch (start us, length us, event | category | flops | bytes accessed | tf_op | source)
XLA Modules:
  0.0 190.8 jit_solution(2653836852478470926)
XLA Ops:
  0.6 2.2 %pack_heads.2.refs_0_.refs_4_ = bf16[1040,384]{1,0:T(8,128)(2,1)} custom-call(s32[1,2]{1,0:T(1,128)} %links_ref.3, bf16[256,768]{1,0:T(8,128)(2,1)} %bitcast.19, bf16[256,768]{1,0:T(8,128)(2,1)} %bitcast.21, bf16[256,768]{1,0:T(8,128)(2,1)} %bitcast.23, bf16[256,768]{1,0:T(8,128)(2,1)} %bitcast.25), custom_call_target="tpu_custom_call" | custom-call | tf_op jit(solution)/shard_map/pack_heads/pallas_call | solution.py:209
  2.8 2.1 %collective-permute-start = (bf16[1040,384]{1,0:T(8,128)(2,1)}, bf16[1040,384]{1,0:T(8,128)(2,1)S(1)}, u32[]{:S(2)}, u32[]{:S(2)}) collective-permute-start(bf16[1040,384]{1,0:T(8,128)(2,1)} %pack_heads.2.refs_0_.refs_4_), channel_id=1, source_target_pairs={{4,0},{12,8},{20,16},{28,24},{5,1},{13,9},{21,17},{29,25},{6,2},{1... | collective-permute-start | bytes 2396168 | tf_op jit(solution)/shard_map/ppermute | solution.py:128
  5.0 2.8 %collective-permute-start.1 = (bf16[1040,384]{1,0:T(8,128)(2,1)}, bf16[1040,384]{1,0:T(8,128)(2,1)}, u32[]{:S(2)}, u32[]{:S(2)}) collective-permute-start(bf16[1040,384]{1,0:T(8,128)(2,1)} %pack_heads.2.refs_0_.refs_4_), channel_id=1, source_target_pairs={{0,8},{4,20},{8,0},{12,28},{16,24},{20,4},{24,16},{28,12},{1,9},{5... | collective-permute-start | bytes 2396168 | tf_op jit(solution)/shard_map/ppermute | solution.py:128
  7.7 0.0 collective-permute-start.2
  7.7 0.0 collective-permute-done.refs_1_.refs_5_
  7.7 0.9 copy-done.16
  8.6 2.2 %pack_heads.3.refs_0_ = bf16[1024,384]{1,0:T(8,128)(2,1)} custom-call(s32[1,2]{1,0:T(1,128)} %links_ref.3, bf16[256,768]{1,0:T(8,128)(2,1)} %bitcast.20, bf16[256,768]{1,0:T(8,128)(2,1)} %bitcast.22, bf16[256,768]{1,0:T(8,128)(2,1)} %bitcast.24, bf16[256,768]{1,0:T(8,128)(2,1)} %bitcast.26), custom_call_target="tpu_custom_call" | custom-call | tf_op jit(solution)/shard_map/pack_heads/pallas_call | solution.py:209
  10.8 2.0 %collective-permute-start.4 = (bf16[1024,384]{1,0:T(8,128)(2,1)}, bf16[1024,384]{1,0:T(8,128)(2,1)S(1)}, u32[]{:S(2)}, u32[]{:S(2)}) collective-permute-start(bf16[1024,384]{1,0:T(8,128)(2,1)} %pack_heads.3.refs_0_), channel_id=1, source_target_pairs={{0,8},{4,20},{8,0},{12,28},{16,24},{20,4},{24,16},{28,12},{1,9},{5... | collective-permute-start | bytes 2359304 | tf_op jit(solution)/shard_map/ppermute | solution.py:128
  12.8 0.3 collective-permute-start.5
  13.1 2.5 %pad_maximum_fusion.refs_2_ = bf16[3,384,768]{2,1,0:T(8,128)(2,1)} fusion(bf16[1,384,768]{2,1,0:T(8,128)(2,1)S(1)} %bitcast.27, bf16[1,384,768]{2,1,0:T(8,128)(2,1)S(1)} %bitcast.28, bf16[1,384,768]{2,1,0:T(8,128)(2,1)} %bitcast.29), kind=kLoop, calls=%fused_computation | loop fusion | flops 1769472 | bytes 3538944 | tf_op jit(solution)/shard_map/stack | solution.py:512
  15.6 0.4 collective-permute-start.6
  16.0 9.1 %collective-permute-done.1.refs_2_.refs_6_.refs_0_.refs_4_ = bf16[1040,384]{1,0:T(8,128)(2,1)} collective-permute-done((bf16[1040,384]{1,0:T(8,128)(2,1)}, bf16[1040,384]{1,0:T(8,128)(2,1)}, u32[]{:S(2)}, u32[]{:S(2)}) %collective-permute-start.1) | collective-permute-done | bytes 798752 | tf_op jit(solution)/shard_map/ppermute | solution.py:128
  25.1 2.4 %collective-permute-start.3 = (bf16[1024,384]{1,0:T(8,128)(2,1)}, bf16[1024,384]{1,0:T(8,128)(2,1)S(1)}, u32[]{:S(2)}, u32[]{:S(2)}) collective-permute-start(bf16[1024,384]{1,0:T(8,128)(2,1)} %pack_heads.3.refs_0_), channel_id=1, source_target_pairs={{4,0},{12,8},{20,16},{28,24},{5,1},{13,9},{21,17},{29,25},{6,2},{1... | collective-permute-start | bytes 2359304 | tf_op jit(solution)/shard_map/ppermute | solution.py:128
  27.5 0.1 pad_add_fusion.place_ref
  27.6 1.5 dynamic-slice_bitcast_fusion
  29.0 0.0 copy-start.12
  29.0 12.9 %collective-permute-done.4.refs_2_.refs_0_ = bf16[1024,384]{1,0:T(8,128)(2,1)S(1)} collective-permute-done((bf16[1024,384]{1,0:T(8,128)(2,1)}, bf16[1024,384]{1,0:T(8,128)(2,1)S(1)}, u32[]{:S(2)}, u32[]{:S(2)}) %collective-permute-start.4) | collective-permute-done | bytes 786464 | tf_op jit(solution)/shard_map/ppermute | solution.py:128
  41.9 0.9 copy-done.18
  42.8 0.2 collective-permute-done.5.refs_3_.refs_1_
  43.0 3.4 %collective-permute-start.7 = (bf16[1040,384]{1,0:T(8,128)(2,1)}, bf16[1040,384]{1,0:T(8,128)(2,1)S(1)}, u32[]{:S(2)}, u32[]{:S(2)}) collective-permute-start(bf16[1040,384]{1,0:T(8,128)(2,1)} %collective-permute-done.1.refs_2_.refs_6_.refs_0_.refs_4_), channel_id=1, source_target_pairs={{4,12},{12,4},{20,28},{28,20},{5,13},{13,5},{21,29},{29,21},{6,14}... | collective-permute-start | bytes 2396168 | tf_op jit(solution)/shard_map/ppermute | solution.py:128
  46.4 0.0 collective-permute-done.2.refs_3_.refs_7_.refs_1_.refs_5_
  46.4 0.0 copy-start.13
  46.4 0.9 copy-done.13
  47.3 1.1 copy-done.14
  48.4 1.1 copy-done.17
  49.6 0.6 attention_gradients.4.refs_0_.refs_6_
  50.2 12.4 %collective-permute-start.19 = (bf16[256,768]{1,0:T(8,128)(2,1)S(1)}, bf16[256,768]{1,0:T(8,128)(2,1)S(1)}, u32[]{:S(2)}, u32[]{:S(2)}) collective-permute-start(bf16[256,768]{1,0:T(8,128)(2,1)S(1)} %get-tuple-element.74.refs_0_), channel_id=1, source_target_pairs={{4,0},{12,8},{20,16},{28,24},{5,1},{13,9},{21,17},{29,25},{6,2},{1... | collective-permute-start | bytes 1179656 | tf_op jit(solution)/shard_map/ppermute | solution.py:128
  62.6 1.3 collective-permute-start.10
  64.0 0.6 attention_gradients.5.refs_1_.refs_7_
  64.6 0.0 copy-start.15
  64.6 4.3 %collective-permute-start.8 = (bf16[1024,384]{1,0:T(8,128)(2,1)S(1)}, bf16[1024,384]{1,0:T(8,128)(2,1)S(1)}, u32[]{:S(2)}, u32[]{:S(2)}) collective-permute-start(bf16[1024,384]{1,0:T(8,128)(2,1)S(1)} %copy-done.19), channel_id=1, source_target_pairs={{4,12},{12,4},{20,28},{28,20},{5,13},{13,5},{21,29},{29,21},{6,14}... | collective-permute-start | bytes 2359304 | tf_op jit(solution)/shard_map/ppermute | solution.py:128
  68.9 1.3 collective-permute-start.9
  70.2 0.9 input_gradient.2
  71.1 5.2 %collective-permute-done.10.refs_3_.refs_7_ = bf16[1040,384]{1,0:T(8,128)(2,1)S(1)} collective-permute-done((bf16[1040,384]{1,0:T(8,128)(2,1)}, bf16[1040,384]{1,0:T(8,128)(2,1)S(1)}, u32[]{:S(2)}, u32[]{:S(2)}) %collective-permute-start.10) | collective-permute-done | bytes 798752 | tf_op jit(solution)/shard_map/ppermute | solution.py:128
  76.3 13.4 %attention_gradients.6.refs_0_.refs_8_ = bf16[4,256,1152]{2,1,0:T(8,128)(2,1)S(1)} custom-call(s32[3]{0:T(128)S(1)} %pad_add_fusion.place_ref, bf16[1040,384]{1,0:T(8,128)(2,1)} %collective-permute-done.1.refs_2_.refs_6_.refs_0_.refs_4_, bf16[1040,384]{1,0:T(8,128)(2,1)S(1)} %copy-done.15, bf16[1040,384]{1,0:T(8,128)(2,1)S(1)} %collective-permute-done.7.refs_2_.refs_6_, ...), custom_call_target="tpu_custom_call" | custom-call | flops 6039797760 | bytes 5505024 | tf_op jit(solution)/shard_map/attention_gradients/pallas_call | solution.py:293
  89.7 2.2 %collective-permute-done.9.refs_3_ = bf16[1024,384]{1,0:T(8,128)(2,1)S(1)} collective-permute-done((bf16[1024,384]{1,0:T(8,128)(2,1)S(1)}, bf16[1024,384]{1,0:T(8,128)(2,1)S(1)}, u32[]{:S(2)}, u32[]{:S(2)}) %collective-permute-start.9) | collective-permute-done | bytes 786464 | tf_op jit(solution)/shard_map/ppermute | solution.py:128
  91.9 0.7 collective-permute-start.13
  92.5 0.7 collective-permute-start.12
  93.2 0.7 collective-permute-start.11
  93.9 5.2 %collective-permute-start.22 = (bf16[256,768]{1,0:T(8,128)(2,1)S(1)}, bf16[256,768]{1,0:T(8,128)(2,1)S(1)}, u32[]{:S(2)}, u32[]{:S(2)}) collective-permute-start(bf16[256,768]{1,0:T(8,128)(2,1)S(1)} %get-tuple-element.77), channel_id=1, source_target_pairs={{4,28},{12,20},{20,12},{28,4},{5,29},{13,21},{21,13},{29,5},{6,30}... | collective-permute-start | bytes 1179656 | tf_op jit(solution)/shard_map/ppermute | solution.py:128
  99.1 13.7 %attention_gradients.7.refs_1_.refs_9_ = bf16[4,256,1152]{2,1,0:T(8,128)(2,1)S(1)} custom-call(s32[3]{0:T(128)S(1)} %pad_add_fusion.place_ref, bf16[1024,384]{1,0:T(8,128)(2,1)S(1)} %copy-done.19, bf16[1024,384]{1,0:T(8,128)(2,1)} %collective-permute-done.5.refs_3_.refs_1_, bf16[1024,384]{1,0:T(8,128)(2,1)S(1)} %collective-permute-done.8.refs_2_, ...), custom_call_target="tpu_custom_call" | custom-call | flops 6039797760 | bytes 5505024 | tf_op jit(solution)/shard_map/attention_gradients/pallas_call | solution.py:293
  112.8 1.3 collective-permute-start.23
  114.2 0.9 add_convert_fusion.1
  115.1 3.8 %collective-permute-start.21 = (bf16[256,768]{1,0:T(8,128)(2,1)S(1)}, bf16[256,768]{1,0:T(8,128)(2,1)S(1)}, u32[]{:S(2)}, u32[]{:S(2)}) collective-permute-start(bf16[256,768]{1,0:T(8,128)(2,1)S(1)} %get-tuple-element.76), channel_id=1, source_target_pairs={{0,20},{4,8},{8,28},{12,0},{16,4},{20,24},{24,12},{28,16},{1,21},{... | collective-permute-start | bytes 1179656 | tf_op jit(solution)/shard_map/ppermute | solution.py:128
  118.9 9.4 %input_gradient.3 = (bf16[256,768]{1,0:T(8,128)(2,1)S(1)}, bf16[256,768]{1,0:T(8,128)(2,1)S(1)}, bf16[256,768]{1,0:T(8,128)(2,1)S(1)}, bf16[256,768]{1,0:T(8,128)(2,1)S(1)}) custom-call(s32[3]{0:T(128)S(1)} %pad_add_fusion.place_ref, bf16[4,256,1152]{2,1,0:T(8,128)(2,1)S(1)} %attention_gradients.6.refs_0_.refs_8_, ...), custom_call_target="tpu_custom_call" | custom-call | flops 3623878656 | bytes 9830400 | tf_op jit(solution)/shard_map/input_gradient/pallas_call | solution.py:374
  128.3 4.1 %collective-permute-start.17 = (bf16[256,768]{1,0:T(8,128)(2,1)S(1)}, bf16[256,768]{1,0:T(8,128)(2,1)S(1)}, u32[]{:S(2)}, u32[]{:S(2)}) collective-permute-start(bf16[256,768]{1,0:T(8,128)(2,1)S(1)} %get-tuple-element.73), channel_id=1, source_target_pairs={{4,7},{5,6},{6,5},{7,4},{12,15},{13,14},{14,13},{15,12},{20,23},{2... | collective-permute-start | bytes 1179656 | tf_op jit(solution)/shard_map/ppermute | solution.py:524
  132.4 1.9 %collective-permute-start.16 = (bf16[256,768]{1,0:T(8,128)(2,1)S(1)}, bf16[256,768]{1,0:T(8,128)(2,1)S(1)}, u32[]{:S(2)}, u32[]{:S(2)}) collective-permute-start(bf16[256,768]{1,0:T(8,128)(2,1)S(1)} %get-tuple-element.72), channel_id=1, source_target_pairs={{4,6},{5,7},{6,4},{7,5},{12,14},{13,15},{14,12},{15,13},{20,22},{2... | collective-permute-start | bytes 1179656 | tf_op jit(solution)/shard_map/ppermute | solution.py:524
  134.4 3.2 %collective-permute-start.15 = (bf16[256,768]{1,0:T(8,128)(2,1)S(1)}, bf16[256,768]{1,0:T(8,128)(2,1)S(1)}, u32[]{:S(2)}, u32[]{:S(2)}) collective-permute-start(bf16[256,768]{1,0:T(8,128)(2,1)S(1)} %get-tuple-element.71), channel_id=1, source_target_pairs={{4,5},{5,4},{6,7},{7,6},{12,13},{13,12},{14,15},{15,14},{20,21},{2... | collective-permute-start | bytes 1179656 | tf_op jit(solution)/shard_map/ppermute | solution.py:524
  137.7 5.1 %weight_gradient_mate.1 = (f32[384,768]{1,0:T(8,128)}, f32[384,768]{1,0:T(8,128)}, f32[384,768]{1,0:T(8,128)}) custom-call(s32[3]{0:T(128)S(1)} %pad_add_fusion.place_ref, bf16[256,768]{1,0:T(8,128)(2,1)S(1)} %get-tuple-element.74.refs_0_, bf16[256,768]{1,0:T(8,128)(2,1)S(1)} %collective-permute-done.19.refs_1_, ...), custom_call_target="tpu_custom_call" | custom-call | flops 1811939328 | bytes 9043968 | tf_op jit(solution)/shard_map/weight_gradient_mate/pallas_call | solution.py:445
  142.8 0.1 collective-permute-start.24
  142.9 0.5 collective-permute-start.25
  143.4 0.1 collective-permute-start.26
  143.4 5.9 %collective-permute-done.16 = bf16[256,768]{1,0:T(8,128)(2,1)S(1)} collective-permute-done((bf16[256,768]{1,0:T(8,128)(2,1)S(1)}, bf16[256,768]{1,0:T(8,128)(2,1)S(1)}, u32[]{:S(2)}, u32[]{:S(2)}) %collective-permute-start.16) | collective-permute-done | bytes 393248 | tf_op jit(solution)/shard_map/ppermute | solution.py:524
  149.3 1.5 collective-permute-start.14
  150.9 1.0 add_convert_fusion
  151.9 3.5 %collective-permute-start.18 = (bf16[256,768]{1,0:T(8,128)(2,1)}, bf16[256,768]{1,0:T(8,128)(2,1)}, u32[]{:S(2)}, u32[]{:S(2)}) collective-permute-start(bf16[256,768]{1,0:T(8,128)(2,1)} %add_convert_fusion), channel_id=1, source_target_pairs={{4,20},{5,16},{6,28},{7,24},{12,29},{13,25},{14,21},{15,17},{20,6}... | collective-permute-start | bytes 1179656 | tf_op jit(solution)/shard_map/ppermute | solution.py:537
  155.4 20.6 %collective-permute-done.14 = bf16[256,768]{1,0:T(8,128)(2,1)} collective-permute-done((bf16[256,768]{1,0:T(8,128)(2,1)}, bf16[256,768]{1,0:T(8,128)(2,1)}, u32[]{:S(2)}, u32[]{:S(2)}) %collective-permute-start.14) | collective-permute-done | bytes 393248 | tf_op jit(solution)/shard_map/ppermute | solution.py:537
  176.0 1.8 select_bitcast_fusion
  177.8 1.7 copy-done.1
  179.5 1.7 copy-done.3
  181.1 1.0 copy-done.6
  182.1 1.0 copy-done.8
  183.1 1.0 copy-done.10
  184.1 6.5 %weight_gradient_own.1 = (f32[384,768]{1,0:T(8,128)}, f32[384,768]{1,0:T(8,128)}, f32[384,768]{1,0:T(8,128)}) custom-call(s32[3]{0:T(128)S(1)} %pad_add_fusion.place_ref, bf16[256,768]{1,0:T(8,128)(2,1)S(1)} %get-tuple-element.74.refs_0_, bf16[256,768]{1,0:T(8,128)(2,1)S(1)} %collective-permute-done.19.refs_1_, bf16[256,768]{1,0:T(8,128)(2,1)S(1)} %copy-done.8, ...), custom_call_target="tpu_custom_call" | custom-call | flops 1811939328 | bytes 9043968 | tf_op jit(solution)/shard_map/weight_gradient_own/pallas_call | solution.py:445
  (50 shorter events, 0.1 us)
Async XLA Ops:
  2.8 10.2 %copy-start.20 = (bf16[384,768]{1,0:T(8,128)(2,1)S(1)}, bf16[384,768]{1,0:T(8,128)(2,1)}, u32[]{:S(2)}) copy-start(bf16[384,768]{1,0:T(8,128)(2,1)} %param.17) | copy-start | bytes 1769476
  2.8 10.2 %copy-start.21 = (bf16[384,768]{1,0:T(8,128)(2,1)S(1)}, bf16[384,768]{1,0:T(8,128)(2,1)}, u32[]{:S(2)}) copy-start(bf16[384,768]{1,0:T(8,128)(2,1)} %param.16) | copy-start | bytes 1769476
  2.8 4.9 %collective-permute-start = (bf16[1040,384]{1,0:T(8,128)(2,1)}, bf16[1040,384]{1,0:T(8,128)(2,1)S(1)}, u32[]{:S(2)}, u32[]{:S(2)}) collective-permute-start(bf16[1040,384]{1,0:T(8,128)(2,1)} %pack_heads.2.refs_0_.refs_4_), channel_id=1, source_target_pairs={{4,0},{12,8},{20,16},{28,24},{5,1},{13,9},{21,17},{29,25},{6,2},{1... | collective-permute-start | bytes 2396168 | tf_op jit(solution)/shard_map/ppermute | solution.py:128
  5.0 20.1 %collective-permute-start.1 = (bf16[1040,384]{1,0:T(8,128)(2,1)}, bf16[1040,384]{1,0:T(8,128)(2,1)}, u32[]{:S(2)}, u32[]{:S(2)}) collective-permute-start(bf16[1040,384]{1,0:T(8,128)(2,1)} %pack_heads.2.refs_0_.refs_4_), channel_id=1, source_target_pairs={{0,8},{4,20},{8,0},{12,28},{16,24},{20,4},{24,16},{28,12},{1,9},{5... | collective-permute-start | bytes 2396168 | tf_op jit(solution)/shard_map/ppermute | solution.py:128
  7.7 38.7 %collective-permute-start.2 = (bf16[1040,384]{1,0:T(8,128)(2,1)}, bf16[1040,384]{1,0:T(8,128)(2,1)S(1)}, u32[]{:S(2)}, u32[]{:S(2)}) collective-permute-start(bf16[1040,384]{1,0:T(8,128)(2,1)} %pack_heads.2.refs_0_.refs_4_), channel_id=1, source_target_pairs={{0,20},{4,8},{8,28},{12,0},{16,4},{20,24},{24,12},{28,16},{1,21},{... | collective-permute-start | bytes 2396168 | tf_op jit(solution)/shard_map/ppermute | solution.py:128
  7.7 0.9 copy-start.16
  10.8 31.1 %collective-permute-start.4 = (bf16[1024,384]{1,0:T(8,128)(2,1)}, bf16[1024,384]{1,0:T(8,128)(2,1)S(1)}, u32[]{:S(2)}, u32[]{:S(2)}) collective-permute-start(bf16[1024,384]{1,0:T(8,128)(2,1)} %pack_heads.3.refs_0_), channel_id=1, source_target_pairs={{0,8},{4,20},{8,0},{12,28},{16,24},{20,4},{24,16},{28,12},{1,9},{5... | collective-permute-start | bytes 2359304 | tf_op jit(solution)/shard_map/ppermute | solution.py:128
  12.8 30.2 %collective-permute-start.5 = (bf16[1024,384]{1,0:T(8,128)(2,1)}, bf16[1024,384]{1,0:T(8,128)(2,1)}, u32[]{:S(2)}, u32[]{:S(2)}) collective-permute-start(bf16[1024,384]{1,0:T(8,128)(2,1)} %pack_heads.3.refs_0_), channel_id=1, source_target_pairs={{0,20},{4,8},{8,28},{12,0},{16,4},{20,24},{24,12},{28,16},{1,21},{... | collective-permute-start | bytes 2359304 | tf_op jit(solution)/shard_map/ppermute | solution.py:128
  15.6 31.7 %copy-start.11 = (bf16[1040,384]{1,0:T(8,128)(2,1)S(1)}, bf16[1040,384]{1,0:T(8,128)(2,1)}, u32[]{:S(2)}) copy-start(bf16[1040,384]{1,0:T(8,128)(2,1)} %pack_heads.2.refs_0_.refs_4_) | copy-start | bytes 2396164
  15.6 54.6 %collective-permute-start.6 = (bf16[3,384,768]{2,1,0:T(8,128)(2,1)}, bf16[3,384,768]{2,1,0:T(8,128)(2,1)}, u32[]{:S(2)}, u32[]{:S(2)}) collective-permute-start(bf16[3,384,768]{2,1,0:T(8,128)(2,1)} %pad_maximum_fusion.refs_2_), channel_id=1, source_target_pairs={{0,4},{4,0},{8,12},{12,8},{16,20},{20,16},{24,28},{28,24},{1,5},{5... | collective-permute-start | bytes 5308424 | tf_op jit(solution)/shard_map/ppermute | solution.py:128
  25.1 38.9 %collective-permute-start.3 = (bf16[1024,384]{1,0:T(8,128)(2,1)}, bf16[1024,384]{1,0:T(8,128)(2,1)S(1)}, u32[]{:S(2)}, u32[]{:S(2)}) collective-permute-start(bf16[1024,384]{1,0:T(8,128)(2,1)} %pack_heads.3.refs_0_), channel_id=1, source_target_pairs={{4,0},{12,8},{20,16},{28,24},{5,1},{13,9},{21,17},{29,25},{6,2},{1... | collective-permute-start | bytes 2359304 | tf_op jit(solution)/shard_map/ppermute | solution.py:128
  29.0 34.9 %copy-start.12 = (bf16[1040,384]{1,0:T(8,128)(2,1)S(1)}, bf16[1040,384]{1,0:T(8,128)(2,1)}, u32[]{:S(2)}) copy-start(bf16[1040,384]{1,0:T(8,128)(2,1)} %pack_heads.2.refs_0_.refs_4_) | copy-start | bytes 2396164
  41.9 0.9 copy-start.18
  43.0 21.7 %collective-permute-start.7 = (bf16[1040,384]{1,0:T(8,128)(2,1)}, bf16[1040,384]{1,0:T(8,128)(2,1)S(1)}, u32[]{:S(2)}, u32[]{:S(2)}) collective-permute-start(bf16[1040,384]{1,0:T(8,128)(2,1)} %collective-permute-done.1.refs_2_.refs_6_.refs_0_.refs_4_), channel_id=1, source_target_pairs={{4,12},{12,4},{20,28},{28,20},{5,13},{13,5},{21,29},{29,21},{6,14}... | collective-permute-start | bytes 2396168 | tf_op jit(solution)/shard_map/ppermute | solution.py:128
  46.4 0.9 copy-start.13
  47.3 1.1 copy-start.14
  48.4 1.1 copy-start.17
  49.6 14.4 %copy-start.19 = (bf16[1024,384]{1,0:T(8,128)(2,1)S(1)}, bf16[1024,384]{1,0:T(8,128)(2,1)}, u32[]{:S(2)}) copy-start(bf16[1024,384]{1,0:T(8,128)(2,1)} %copy-done.18) | copy-start | bytes 2359300
  50.2 78.1 %collective-permute-start.19 = (bf16[256,768]{1,0:T(8,128)(2,1)S(1)}, bf16[256,768]{1,0:T(8,128)(2,1)S(1)}, u32[]{:S(2)}, u32[]{:S(2)}) collective-permute-start(bf16[256,768]{1,0:T(8,128)(2,1)S(1)} %get-tuple-element.74.refs_0_), channel_id=1, source_target_pairs={{4,0},{12,8},{20,16},{28,24},{5,1},{13,9},{21,17},{29,25},{6,2},{1... | collective-permute-start | bytes 1179656 | tf_op jit(solution)/shard_map/ppermute | solution.py:128
  62.6 13.7 %collective-permute-start.10 = (bf16[1040,384]{1,0:T(8,128)(2,1)}, bf16[1040,384]{1,0:T(8,128)(2,1)S(1)}, u32[]{:S(2)}, u32[]{:S(2)}) collective-permute-start(bf16[1040,384]{1,0:T(8,128)(2,1)} %collective-permute-done.1.refs_2_.refs_6_.refs_0_.refs_4_), channel_id=1, source_target_pairs={{0,20},{8,28},{16,4},{24,12},{1,21},{9,29},{17,5},{25,13},{2,22},{... | collective-permute-start | bytes 2396168 | tf_op jit(solution)/shard_map/ppermute | solution.py:128
  64.6 73.1 %copy-start = (bf16[4,256,1152]{2,1,0:T(8,128)(2,1)}, bf16[4,256,1152]{2,1,0:T(8,128)(2,1)S(1)}, u32[]{:S(2)}) copy-start(bf16[4,256,1152]{2,1,0:T(8,128)(2,1)S(1)} %attention_gradients.5.refs_1_.refs_7_) | copy-start | bytes 7077892
  64.6 11.7 %copy-start.15 = (bf16[1040,384]{1,0:T(8,128)(2,1)S(1)}, bf16[1040,384]{1,0:T(8,128)(2,1)}, u32[]{:S(2)}) copy-start(bf16[1040,384]{1,0:T(8,128)(2,1)} %copy-done.13) | copy-start | bytes 2396164
  64.6 25.1 %collective-permute-start.8 = (bf16[1024,384]{1,0:T(8,128)(2,1)S(1)}, bf16[1024,384]{1,0:T(8,128)(2,1)S(1)}, u32[]{:S(2)}, u32[]{:S(2)}) collective-permute-start(bf16[1024,384]{1,0:T(8,128)(2,1)S(1)} %copy-done.19), channel_id=1, source_target_pairs={{4,12},{12,4},{20,28},{28,20},{5,13},{13,5},{21,29},{29,21},{6,14}... | collective-permute-start | bytes 2359304 | tf_op jit(solution)/shard_map/ppermute | solution.py:128
  68.9 23.0 %collective-permute-start.9 = (bf16[1024,384]{1,0:T(8,128)(2,1)S(1)}, bf16[1024,384]{1,0:T(8,128)(2,1)S(1)}, u32[]{:S(2)}, u32[]{:S(2)}) collective-permute-start(bf16[1024,384]{1,0:T(8,128)(2,1)S(1)} %copy-done.19), channel_id=1, source_target_pairs={{0,20},{8,28},{16,4},{24,12},{1,21},{9,29},{17,5},{25,13},{2,22},{... | collective-permute-start | bytes 2359304 | tf_op jit(solution)/shard_map/ppermute | solution.py:128
  89.7 48.0 %copy-start.2 = (bf16[4,256,1152]{2,1,0:T(8,128)(2,1)}, bf16[4,256,1152]{2,1,0:T(8,128)(2,1)S(1)}, u32[]{:S(2)}) copy-start(bf16[4,256,1152]{2,1,0:T(8,128)(2,1)S(1)} %attention_gradients.6.refs_0_.refs_8_) | copy-start | bytes 7077892
  91.9 21.0 %collective-permute-start.13 = (bf16[256,768]{1,0:T(8,128)(2,1)S(1)}, bf16[256,768]{1,0:T(8,128)(2,1)S(1)}, u32[]{:S(2)}, u32[]{:S(2)}) collective-permute-start(bf16[256,768]{1,0:T(8,128)(2,1)S(1)} %get-tuple-element.67), channel_id=1, source_target_pairs={{0,3},{1,2},{2,1},{3,0},{8,11},{9,10},{10,9},{11,8},{16,19},{17,18... | collective-permute-start | bytes 1179656 | tf_op jit(solution)/shard_map/ppermute | solution.py:524
  92.5 21.6 %collective-permute-start.12 = (bf16[256,768]{1,0:T(8,128)(2,1)S(1)}, bf16[256,768]{1,0:T(8,128)(2,1)S(1)}, u32[]{:S(2)}, u32[]{:S(2)}) collective-permute-start(bf16[256,768]{1,0:T(8,128)(2,1)S(1)} %get-tuple-element.66), channel_id=1, source_target_pairs={{0,2},{1,3},{2,0},{3,1},{8,10},{9,11},{10,8},{11,9},{16,18},{17,19... | collective-permute-start | bytes 1179656 | tf_op jit(solution)/shard_map/ppermute | solution.py:524
  93.2 20.9 %collective-permute-start.11 = (bf16[256,768]{1,0:T(8,128)(2,1)S(1)}, bf16[256,768]{1,0:T(8,128)(2,1)S(1)}, u32[]{:S(2)}, u32[]{:S(2)}) collective-permute-start(bf16[256,768]{1,0:T(8,128)(2,1)S(1)} %get-tuple-element.65), channel_id=1, source_target_pairs={{0,1},{1,0},{2,3},{3,2},{8,9},{9,8},{10,11},{11,10},{16,17},{17,16... | collective-permute-start | bytes 1179656 | tf_op jit(solution)/shard_map/ppermute | solution.py:524
  93.9 38.5 %collective-permute-start.22 = (bf16[256,768]{1,0:T(8,128)(2,1)S(1)}, bf16[256,768]{1,0:T(8,128)(2,1)S(1)}, u32[]{:S(2)}, u32[]{:S(2)}) collective-permute-start(bf16[256,768]{1,0:T(8,128)(2,1)S(1)} %get-tuple-element.77), channel_id=1, source_target_pairs={{4,28},{12,20},{20,12},{28,4},{5,29},{13,21},{21,13},{29,5},{6,30}... | collective-permute-start | bytes 1179656 | tf_op jit(solution)/shard_map/ppermute | solution.py:128
  112.8 15.5 %copy-start.4 = (bf16[4,256,1152]{2,1,0:T(8,128)(2,1)}, bf16[4,256,1152]{2,1,0:T(8,128)(2,1)S(1)}, u32[]{:S(2)}) copy-start(bf16[4,256,1152]{2,1,0:T(8,128)(2,1)S(1)} %attention_gradients.7.refs_1_.refs_9_) | copy-start | bytes 7077892
  112.8 21.5 %collective-permute-start.23 = (bf16[256,768]{1,0:T(8,128)(2,1)S(1)}, bf16[256,768]{1,0:T(8,128)(2,1)S(1)}, u32[]{:S(2)}, u32[]{:S(2)}) collective-permute-start(bf16[256,768]{1,0:T(8,128)(2,1)S(1)} %get-tuple-element.77), channel_id=1, source_target_pairs={{0,28},{8,20},{16,12},{24,4},{1,29},{9,21},{17,13},{25,5},{2,30},{... | collective-permute-start | bytes 1179656 | tf_op jit(solution)/shard_map/ppermute | solution.py:128
  115.1 22.5 %collective-permute-start.20 = (bf16[256,768]{1,0:T(8,128)(2,1)S(1)}, bf16[256,768]{1,0:T(8,128)(2,1)S(1)}, u32[]{:S(2)}, u32[]{:S(2)}) collective-permute-start(bf16[256,768]{1,0:T(8,128)(2,1)S(1)} %get-tuple-element.75), channel_id=1, source_target_pairs={{0,8},{4,20},{8,0},{12,28},{16,24},{20,4},{24,16},{28,12},{1,9},{5... | collective-permute-start | bytes 1179656 | tf_op jit(solution)/shard_map/ppermute | solution.py:128
  115.1 22.5 %collective-permute-start.21 = (bf16[256,768]{1,0:T(8,128)(2,1)S(1)}, bf16[256,768]{1,0:T(8,128)(2,1)S(1)}, u32[]{:S(2)}, u32[]{:S(2)}) collective-permute-start(bf16[256,768]{1,0:T(8,128)(2,1)S(1)} %get-tuple-element.76), channel_id=1, source_target_pairs={{0,20},{4,8},{8,28},{12,0},{16,4},{20,24},{24,12},{28,16},{1,21},{... | collective-permute-start | bytes 1179656 | tf_op jit(solution)/shard_map/ppermute | solution.py:128
  128.3 15.1 %collective-permute-start.17 = (bf16[256,768]{1,0:T(8,128)(2,1)S(1)}, bf16[256,768]{1,0:T(8,128)(2,1)S(1)}, u32[]{:S(2)}, u32[]{:S(2)}) collective-permute-start(bf16[256,768]{1,0:T(8,128)(2,1)S(1)} %get-tuple-element.73), channel_id=1, source_target_pairs={{4,7},{5,6},{6,5},{7,4},{12,15},{13,14},{14,13},{15,12},{20,23},{2... | collective-permute-start | bytes 1179656 | tf_op jit(solution)/shard_map/ppermute | solution.py:524
  132.4 16.9 %collective-permute-start.16 = (bf16[256,768]{1,0:T(8,128)(2,1)S(1)}, bf16[256,768]{1,0:T(8,128)(2,1)S(1)}, u32[]{:S(2)}, u32[]{:S(2)}) collective-permute-start(bf16[256,768]{1,0:T(8,128)(2,1)S(1)} %get-tuple-element.72), channel_id=1, source_target_pairs={{4,6},{5,7},{6,4},{7,5},{12,14},{13,15},{14,12},{15,13},{20,22},{2... | collective-permute-start | bytes 1179656 | tf_op jit(solution)/shard_map/ppermute | solution.py:524
  134.4 8.4 %copy-start.5 = (bf16[256,768]{1,0:T(8,128)(2,1)}, bf16[256,768]{1,0:T(8,128)(2,1)S(1)}, u32[]{:S(2)}) copy-start(bf16[256,768]{1,0:T(8,128)(2,1)S(1)} %collective-permute-done.23.refs_5_) | copy-start | bytes 1179652
  134.4 16.5 %collective-permute-start.15 = (bf16[256,768]{1,0:T(8,128)(2,1)S(1)}, bf16[256,768]{1,0:T(8,128)(2,1)S(1)}, u32[]{:S(2)}, u32[]{:S(2)}) collective-permute-start(bf16[256,768]{1,0:T(8,128)(2,1)S(1)} %get-tuple-element.71), channel_id=1, source_target_pairs={{4,5},{5,4},{6,7},{7,6},{12,13},{13,12},{14,15},{15,14},{20,21},{2... | collective-permute-start | bytes 1179656 | tf_op jit(solution)/shard_map/ppermute | solution.py:524
  137.6 5.1 %copy-start.7 = (bf16[256,768]{1,0:T(8,128)(2,1)}, bf16[256,768]{1,0:T(8,128)(2,1)S(1)}, u32[]{:S(2)}) copy-start(bf16[256,768]{1,0:T(8,128)(2,1)S(1)} %collective-permute-done.20.refs_2_) | copy-start | bytes 1179652
  137.7 5.1 %copy-start.9 = (bf16[256,768]{1,0:T(8,128)(2,1)}, bf16[256,768]{1,0:T(8,128)(2,1)S(1)}, u32[]{:S(2)}) copy-start(bf16[256,768]{1,0:T(8,128)(2,1)S(1)} %collective-permute-done.21.refs_3_) | copy-start | bytes 1179652
  142.8 35.0 %collective-permute-start.24 = (f32[384,768]{1,0:T(8,128)}, f32[384,768]{1,0:T(8,128)}, u32[]{:S(2)}, u32[]{:S(2)}) collective-permute-start(f32[384,768]{1,0:T(8,128)} %get-tuple-element.78), channel_id=1, source_target_pairs={{0,4},{4,0},{8,12},{12,8},{16,20},{20,16},{24,28},{28,24},{1,5},{5... | collective-permute-start | bytes 3538952 | tf_op jit(solution)/shard_map/ppermute | solution.py:128
  142.9 34.9 %collective-permute-start.25 = (f32[384,768]{1,0:T(8,128)}, f32[384,768]{1,0:T(8,128)}, u32[]{:S(2)}, u32[]{:S(2)}) collective-permute-start(f32[384,768]{1,0:T(8,128)} %get-tuple-element.79), channel_id=1, source_target_pairs={{0,4},{4,0},{8,12},{12,8},{16,20},{20,16},{24,28},{28,24},{1,5},{5... | collective-permute-start | bytes 3538952 | tf_op jit(solution)/shard_map/ppermute | solution.py:128
  143.4 34.4 %collective-permute-start.26 = (f32[384,768]{1,0:T(8,128)}, f32[384,768]{1,0:T(8,128)}, u32[]{:S(2)}, u32[]{:S(2)}) collective-permute-start(f32[384,768]{1,0:T(8,128)} %get-tuple-element.80), channel_id=1, source_target_pairs={{0,4},{4,0},{8,12},{12,8},{16,20},{20,16},{24,28},{28,24},{1,5},{5... | collective-permute-start | bytes 3538952 | tf_op jit(solution)/shard_map/ppermute | solution.py:128
  149.3 26.7 %collective-permute-start.14 = (bf16[256,768]{1,0:T(8,128)(2,1)}, bf16[256,768]{1,0:T(8,128)(2,1)}, u32[]{:S(2)}, u32[]{:S(2)}) collective-permute-start(bf16[256,768]{1,0:T(8,128)(2,1)} %add_convert_fusion.1), channel_id=1, source_target_pairs={{0,0},{1,4},{2,8},{3,12},{8,9},{9,13},{10,1},{11,5},{16,18},{17,22... | collective-permute-start | bytes 1179656 | tf_op jit(solution)/shard_map/ppermute | solution.py:537
  151.9 24.1 %collective-permute-start.18 = (bf16[256,768]{1,0:T(8,128)(2,1)}, bf16[256,768]{1,0:T(8,128)(2,1)}, u32[]{:S(2)}, u32[]{:S(2)}) collective-permute-start(bf16[256,768]{1,0:T(8,128)(2,1)} %add_convert_fusion), channel_id=1, source_target_pairs={{4,20},{5,16},{6,28},{7,24},{12,29},{13,25},{14,21},{15,17},{20,6}... | collective-permute-start | bytes 1179656 | tf_op jit(solution)/shard_map/ppermute | solution.py:537
  177.8 1.7 copy-start.1
  179.5 1.7 copy-start.3
  181.1 1.0 copy-start.6
  182.1 1.0 copy-start.8
  183.1 1.0 copy-start.10

commit v4 on v3

v4 whole, which is shorter than its diff:
```python
import functools

import jax
import jax.numpy as jnp
from jax import lax
from jax.experimental import pallas as pl
from jax.experimental.pallas import tpu as pltpu
from jax.sharding import PartitionSpec as P

HD = 128
LOG2E = 1.4426950408889634
MIB = 1024 * 1024


def shifted(value, axis, steps):
    count = lax.axis_size(axis)
    pairs = [(source, (source + steps) % count) for source in range(count)]
    return lax.ppermute(value, axis, pairs)


def attend(query_rows, grad_rows, blocks, usable, scaling):
    batch_size, length, col_count = query_rows.shape
    heads_here = col_count // HD
    key_heads = blocks[..., :col_count].reshape(batch_size, 3 * length, heads_here, HD)
    value_heads = blocks[..., col_count:].reshape(batch_size, 3 * length, heads_here, HD)
    query_heads = query_rows.reshape(batch_size, length, heads_here, HD)
    grad_heads = grad_rows.reshape(batch_size, length, heads_here, HD)
    scores = (
        jnp.einsum("bshd,bthd->bhst", query_heads, key_heads, preferred_element_type=jnp.float32)
        * scaling
    )
    scores = jnp.where(usable, scores, -1e30)
    largest = jnp.max(scores, axis=-1, keepdims=True)
    powers = jnp.exp(scores - largest)
    attn_probs = powers / jnp.sum(powers, axis=-1, keepdims=True)
    probs_half = attn_probs.astype(jnp.bfloat16)
    prob_grad = jnp.einsum(
        "bshd,bthd->bhst", grad_heads, value_heads, preferred_element_type=jnp.float32
    )
    row_delta = jnp.sum(attn_probs * prob_grad, axis=-1, keepdims=True)
    score_grad = (scaling * attn_probs * (prob_grad - row_delta)).astype(jnp.bfloat16)
    query_grad = jnp.einsum(
        "bhst,bthd->bshd", score_grad, key_heads, preferred_element_type=jnp.float32
    )
    key_grad = jnp.einsum(
        "bhst,bshd->bthd", score_grad, query_heads, preferred_element_type=jnp.float32
    )
    value_grad = jnp.einsum(
        "bhst,bshd->bthd", probs_half, grad_heads, preferred_element_type=jnp.float32
    )
    query_grad = query_grad.reshape(batch_size, length, col_count)
    key_grad = key_grad.reshape(batch_size, 3, length, col_count)
    value_grad = value_grad.reshape(batch_size, 3, length, col_count)
    return (query_grad, jnp.concatenate([key_grad, value_grad], axis=-1))


def halo_body(
    normed,
    queries,
    saved_keys,
    saved_values,
    output_grad,
    view_links,
    query_weight,
    key_weight,
    value_weight,
):
    scaling = HD ** (-0.5)
    batch_size, view_count, length, col_count = queries.shape
    model_width = normed.shape[-1]
    pairs = jnp.concatenate([saved_keys, saved_values], axis=-1)
    from_lower = shifted(pairs, "view", 1)
    from_upper = shifted(pairs, "view", -1)
    extended = jnp.concatenate([from_lower, pairs, from_upper], axis=1)
    block_index = jnp.arange(3 * length) // length
    pair_grads = jnp.zeros(extended.shape, jnp.float32)
    link_flags = view_links[0] >= 0
    usable = jnp.where(
        block_index == 0, link_flags[0], jnp.where(block_index == 2, link_flags[1], True)
    )
    query_grad, block_grad = attend(queries[:, 0], output_grad[:, 0], extended, usable, scaling)
    query_grads = [query_grad]
    pair_grads = pair_grads.at[:, 0:3].add(block_grad)
    row_count = batch_size * view_count * length
    query_half = jnp.stack(query_grads, axis=1).astype(jnp.bfloat16).reshape(row_count, col_count)
    flat_input = normed.reshape(row_count, model_width)
    mean_scale = 1.0 / (lax.axis_size("dp") * batch_size * lax.axis_size("view") * view_count)
    from_lower_grads = shifted(pair_grads[:, -1:], "view", 1)
    from_upper_grads = shifted(pair_grads[:, :1], "view", -1)
    own_grads = pair_grads[:, 1 : view_count + 1]
    own_grads = own_grads.at[:, :1].add(from_lower_grads)
    own_grads = own_grads.at[:, -1:].add(from_upper_grads)
    key_half = own_grads[..., :col_count].astype(jnp.bfloat16).reshape(row_count, col_count)
    value_half = own_grads[..., col_count:].astype(jnp.bfloat16).reshape(row_count, col_count)
    all_grads = jnp.concatenate([query_half, key_half, value_half], axis=-1)
    grads_three = all_grads.reshape(row_count, 3, col_count)
    stacked = jnp.stack([query_weight, key_weight, value_weight])
    partial_input = jnp.einsum(
        "ric,ipc->rp",
        grads_three,
        lax.all_gather(stacked, ("dp", "view"), axis=1, tiled=True),
        preferred_element_type=jnp.float32,
    )
    summed_input = lax.psum_scatter(partial_input, "head", scatter_dimension=1, tiled=True)
    input_grad = summed_input.astype(jnp.bfloat16).reshape(
        batch_size, view_count, length, model_width // lax.axis_size("head")
    )
    product = lax.dot_general(
        flat_input, all_grads, (((0,), (0,)), ((), ())), preferred_element_type=jnp.float32
    )
    together = lax.psum_scatter(
        product * mean_scale, ("dp", "view"), scatter_dimension=0, tiled=True
    )
    grad_query = together[:, :col_count]
    grad_key = together[:, col_count : 2 * col_count]
    grad_value = together[:, 2 * col_count :]
    return (input_grad, grad_query, grad_key, grad_value)


def moved(value, target):
    prompts, views = lax.axis_size("dp"), lax.axis_size("view")
    pairs = []
    for y in range(prompts):
        for v in range(views):
            goal = target(y, v)
            if goal is not None:
                pairs.append((y * views + v, goal[0] * views + goal[1]))
    return lax.ppermute(value, ("dp", "view"), pairs)


def mate(y, v):
    return (y, v ^ 1)


def along_x(y, v):
    return (y, v ^ 2)


def across_x(y, v):
    return (y, v ^ 3)


def only(core, target):
    return lambda y, v: target(y, v) if v % 2 == core else None


def along_y(y, v):
    return (y ^ 1, v)


def across_y(y, v):
    return (y ^ 1, v ^ 1)


def straight(y, v):
    return along_x(y, v) if v % 2 == 0 else along_y(y, v)


def crossed(y, v):
    return across_y(y, v) if v % 2 == 0 else across_x(y, v)


def corner_same(y, v):
    return None if v % 2 == 0 else (y ^ 1, v ^ 2)


def corner_cross(y, v):
    return (y ^ 1, v ^ 3) if v % 2 == 0 else None


def lanes(start, size):
    return pl.ds(pl.multiple_of(start, HD), size)


def whole(space=pltpu.VMEM):
    return pl.BlockSpec(memory_space=space)


def dot_last(a, b):
    return lax.dot_general(a, b, (((1,), (1,)), ((), ())), preferred_element_type=jnp.float32)


def dot_first(a, b):
    return lax.dot_general(a, b, (((0,), (0,)), ((), ())), preferred_element_type=jnp.float32)


def dot(a, b):
    return jnp.dot(a, b, preferred_element_type=jnp.float32)


def after(values, *earlier):
    return lax.optimization_barrier((tuple(values), tuple(earlier)))[0]


CORE, PLANE, HERE, BESIDE = range(4)
FLAG_ROWS = 16


def pack_kernel(picks, place_ref, links_ref, q_ref, k_ref, v_ref, g_ref, *out_refs):
    length = q_ref.shape[0]
    core = place_ref[CORE]
    for pick, out_ref in zip(picks, out_refs):
        start = pick(core, place_ref[HERE], place_ref[BESIDE]) * HD
        for kind, source in enumerate((q_ref, k_ref, v_ref, g_ref)):
            out_ref[kind * length : (kind + 1) * length] = source[:, lanes(start, HD)]
        row = lax.broadcasted_iota(jnp.int32, (FLAG_ROWS, HD), 0)
        gaps = [
            jnp.where(links_ref[0, side] >= 0, 0.0, 1.0).astype(jnp.float32) for side in range(2)
        ]
        flags = jnp.where(row < FLAG_ROWS // 2, gaps[0], gaps[1])
        out_ref[4 * length : 4 * length + FLAG_ROWS] = flags.astype(out_ref.dtype)


def pack(picks, place, links, arrays):
    length = arrays[0].shape[0]
    out = jax.ShapeDtypeStruct((4 * length + FLAG_ROWS, HD), jnp.bfloat16)
    return pl.pallas_call(
        functools.partial(pack_kernel, picks),
        out_shape=[out] * len(picks),
        in_specs=[whole(pltpu.SMEM)] * 2 + [whole()] * 4,
        out_specs=[whole()] * len(picks),
        name="pack_heads",
    )(place, links, *arrays)


def attention_kernel(scaling, both, place_ref, x0, x1, x2, x3, out_ref, kacc, vacc):
    xs = (x0, x1, x2, x3)
    core = place_ref[CORE]
    length = out_ref.shape[1]
    factor = scaling * LOG2E

    def rows(e, kind):
        return xs[e][kind * length : (kind + 1) * length]

    def gap(e, side):
        at = 4 * length + side * (FLAG_ROWS // 2)
        flags = xs[e][at : at + FLAG_ROWS // 2].astype(jnp.float32)[0:1]
        return jnp.concatenate([flags] * (length // HD), axis=1) * 1e30

    def compute():
        seen = set()
        for e in range(4):
            blocks = ((e + 3) % 4, e, (e + 1) % 4)
            before, behind = gap(e, 0), gap(e, 1)
            far_below = jnp.where(core == 0, before, behind)
            far_above = jnp.where(core == 0, behind, before)
            q, g = rows(e, 0), rows(e, 3)
            scores = [dot_last(rows(f, 1), q) for f in blocks]
            tops = [jnp.max(s, axis=0, keepdims=True) for s in scores]
            top = jnp.maximum(tops[1], jnp.maximum(tops[0] - far_below, tops[2] - far_above))
            offsets = (top + far_below, top, top + far_above)
            powers = [jnp.exp2((s - o) * factor) for s, o in zip(scores, offsets)]
            inverse = 1.0 / sum(jnp.sum(p, axis=0, keepdims=True) for p in powers)
            prob_grads = [dot_last(rows(f, 2), g) for f in blocks]
            delta = inverse * sum(
                jnp.sum(p * d, axis=0, keepdims=True) for p, d in zip(powers, prob_grads)
            )
            query_grad = None
            for f, p, d in zip(blocks, powers, prob_grads):
                probs = p * inverse
                score_grad = (probs * scaling * (d - delta)).astype(jnp.bfloat16)
                part = dot_first(score_grad, rows(f, 1))
                query_grad = part if query_grad is None else query_grad + part
                key_part = dot(score_grad, q)
                value_part = dot(probs.astype(jnp.bfloat16), g)
                if f in seen:
                    kacc[f] += key_part
                    vacc[f] += value_part
                else:
                    seen.add(f)
                    kacc[f] = key_part
                    vacc[f] = value_part
            out_ref[e, :, 0:HD] = query_grad.astype(out_ref.dtype)
        out_ref[:, :, HD : 2 * HD] = kacc[...].astype(out_ref.dtype)
        out_ref[:, :, 2 * HD : 3 * HD] = vacc[...].astype(out_ref.dtype)

    if both:
        compute()
    else:
        pl.when(core == 0)(compute)


def attention(place, both, sources):
    length = (sources[0].shape[0] - FLAG_ROWS) // 4
    return pl.pallas_call(
        functools.partial(attention_kernel, HD ** (-0.5), both),
        out_shape=jax.ShapeDtypeStruct((4, length, 3 * HD), jnp.bfloat16),
        in_specs=[whole(pltpu.SMEM)] + [whole()] * 4,
        out_specs=whole(),
        scratch_shapes=[pltpu.VMEM((4, length, HD), jnp.float32)] * 2,
        compiler_params=pltpu.CompilerParams(vmem_limit_bytes=32 * MIB),
        cost_estimate=pl.CostEstimate(
            flops=4 * 5 * 2 * length * 3 * length * HD * 2,
            bytes_accessed=2 * length * 7 * HD * 4,
            transcendentals=12 * length * length,
        ),
        name="attention_gradients",
    )(place, *sources)


def turn_kernel(q_ref, k_ref, v_ref, out_ref):
    for head in range(q_ref.shape[1] // HD):
        for kind, source in enumerate((q_ref, k_ref, v_ref)):
            at = (head * 3 + kind) * HD
            out_ref[at : at + HD] = source[:, head * HD : (head + 1) * HD].T


def turned_weights(weights):
    rows, cols = weights[0].shape
    return pl.pallas_call(
        turn_kernel,
        out_shape=jax.ShapeDtypeStruct((3 * cols, rows), jnp.bfloat16),
        in_specs=[whole()] * 3,
        out_specs=whole(),
        compiler_params=pltpu.CompilerParams(vmem_limit_bytes=16 * MIB),
        name="turn_weights",
    )(*weights)


def input_kernel(role, marks, place_ref, *refs):
    count = len(marks)
    grad_refs, weight_refs, out_refs = refs[:count], refs[count : count + 2], refs[count + 2 : -4]
    grads, weights, outs, sems = refs[-4:]
    core, plane = place_ref[CORE], place_ref[PLANE]
    rows = weights.shape[2]
    triple = grad_refs[0].shape[2]
    slots = len(out_refs)
    order = list(range(1, slots)) + [0]

    @pl.when(core == role)
    def _():
        fetches = [
            pltpu.make_async_copy(ref, weights.at[side], sems.at[side])
            for side, ref in enumerate(weight_refs)
        ]
        loads = {
            s: [
                pltpu.make_async_copy(
                    ref.at[jnp.bitwise_xor(plane, s ^ flip)],
                    grads.at[s, :, lanes((place_ref[base] + step) * triple, triple)],
                    sems.at[2 + s * count + at],
                )
                for at, (ref, (base, step, flip)) in enumerate(zip(grad_refs, marks))
            ]
            for s in order
        }
        stores = [
            pltpu.make_async_copy(outs.at[s], out, sems.at[2 + slots * count + s])
            for s, out in enumerate(out_refs)
        ]
        for copy in loads[order[0]] + fetches + [load for s in order[1:] for load in loads[s]]:
            copy.start()
        for copy in fetches:
            copy.wait()
        for s in order:
            for load in loads[s]:
                load.wait()
            for side, at in ((0, core), (1, 1 - core)):
                total = dot(grads[s], weights[side])
                outs[s, :, lanes(at * rows, rows)] = total.astype(outs.dtype)
            stores[s].start()
        for store in stores:
            store.wait()


def input_product(place, role, grads, own_weights, mate_weights):
    blocks, length, triple = grads[0][0].shape
    depth, rows = own_weights.shape
    count = len(grads)
    out = jax.ShapeDtypeStruct((length, 2 * rows), jnp.bfloat16)
    return pl.pallas_call(
        functools.partial(input_kernel, role, [mark for _, mark in grads]),
        out_shape=[out] * blocks,
        in_specs=[whole(pltpu.SMEM)] + [whole(pltpu.HBM)] * (count + 2),
        out_specs=[whole(pltpu.HBM)] * blocks,
        scratch_shapes=[
            pltpu.VMEM((blocks, length, depth), jnp.bfloat16),
            pltpu.VMEM((2, depth, rows), jnp.bfloat16),
            pltpu.VMEM((blocks, length, 2 * rows), jnp.bfloat16),
            pltpu.SemaphoreType.DMA((2 + blocks * (count + 1),)),
        ],
        compiler_params=pltpu.CompilerParams(vmem_limit_bytes=32 * MIB),
        cost_estimate=pl.CostEstimate(
            flops=2 * blocks * length * 2 * rows * depth,
            bytes_accessed=2 * (blocks * length * (2 * rows + depth) + 2 * rows * depth),
            transcendentals=0,
        ),
        name="input_gradient",
    )(place, *[array for array, _ in grads], own_weights, mate_weights)


def weight_kernel(mine, mean_scale, marks, place_ref, *refs):
    sources, refs = refs[:6], refs[6:]
    count = len(marks[0])
    grad_refs, refs = (refs[:count], refs[count : 2 * count]), refs[2 * count :]
    received, refs = (refs[:3], refs[3:]) if mine else ((), refs)
    out_refs = refs[:3]
    if mine:
        tokens, turned, grads, sums, sems = refs[3:]
    else:
        tokens, turned, grads, sems = refs[3:]
    core = place_ref[CORE]
    rows = out_refs[0].shape[0]
    blocks, length, triple = grad_refs[0][0].shape
    start = (core if mine else 1 - core) * rows
    own, mate_in, first, second, corner, corner_far = sources
    chosen = ((own, mate_in, first, second), (first, second, corner, corner_far))

    def copies(which):
        return [
            pltpu.make_async_copy(source.at[:, lanes(start, rows)], tokens.at[e], sems.at[e])
            for e, source in enumerate(chosen[which])
        ] + [
            pltpu.make_async_copy(
                ref.at[e ^ flip],
                grads.at[
                    e * length : (e + 1) * length,
                    lanes((place_ref[base] + step) * triple, triple),
                ],
                sems.at[blocks + at * blocks + e],
            )
            for at, (ref, (base, step, flip)) in enumerate(zip(grad_refs[which], marks[which]))
            for e in range(blocks)
        ]

    for which in range(2):

        @pl.when(core == which)
        def _():
            for copy in copies(which):
                copy.start()

    arrivals = [
        pltpu.make_async_copy(ref, sums.at[kind], sems.at[blocks * (count + 1) + kind])
        for kind, ref in enumerate(received)
    ]
    for copy in arrivals:
        copy.start()
    waits = copies(0)
    for e in range(blocks):
        waits[e].wait()
        turned[:, e * length : (e + 1) * length] = tokens[e].T
    for copy in waits[blocks:] + arrivals:
        copy.wait()
    for pair in range(count // 2):
        total = dot(turned[...], grads[:, pair * 2 * triple : (pair + 1) * 2 * triple])
        for head in range(2):
            here = slice((2 * pair + head) * HD, (2 * pair + head + 1) * HD)
            for kind, out in enumerate(out_refs):
                at = (head * 3 + kind) * HD
                part = total[:, at : at + HD]
                if mine:
                    part = (part + sums[kind, :, here]) * mean_scale
                out[:, here] = part


def weight_product(place, mine, mean_scale, tokens, grads, received=()):
    blocks, length, triple = grads[0][0][0].shape
    count = len(grads[0])
    rows = tokens[0].shape[1] // 2
    cols = HD * count
    return pl.pallas_call(
        functools.partial(
            weight_kernel, mine, mean_scale, [[mark for _, mark in part] for part in grads]
        ),
        out_shape=[jax.ShapeDtypeStruct((rows, cols), jnp.float32)] * 3,
        in_specs=[whole(pltpu.SMEM)] + [whole(pltpu.HBM)] * (6 + 2 * count + len(received)),
        out_specs=[whole()] * 3,
        scratch_shapes=[
            pltpu.VMEM((blocks, length, rows), jnp.bfloat16),
            pltpu.VMEM((rows, blocks * length), jnp.bfloat16),
            pltpu.VMEM((blocks * length, count * triple), jnp.bfloat16),
        ]
        + ([pltpu.VMEM((3, rows, cols), jnp.float32)] if mine else [])
        + [pltpu.SemaphoreType.DMA((blocks * (count + 1) + 3,))],
        compiler_params=pltpu.CompilerParams(vmem_limit_bytes=40 * MIB),
        cost_estimate=pl.CostEstimate(
            flops=2 * rows * 3 * cols * blocks * length,
            bytes_accessed=2 * blocks * length * (rows + 3 * cols) + 12 * rows * cols,
            transcendentals=0,
        ),
        name="weight_gradient_own" if mine else "weight_gradient_mate",
    )(place, *tokens, *[array for part in grads for array, _ in part], *received)


def gather_body(
    normed,
    queries,
    saved_keys,
    saved_values,
    output_grad,
    view_links,
    query_weight,
    key_weight,
    value_weight,
):
    length, cols = queries.shape[2:]
    model_width = normed.shape[-1]
    rows = query_weight.shape[0]
    prompts, views, groups = (lax.axis_size(name) for name in ("dp", "view", "head"))
    mean_scale = 1.0 / (prompts * views)
    half = cols // HD // 2
    view = lax.axis_index("view")
    core = lax.rem(view, 2)
    side = view // 2
    chip = lax.axis_index("dp") * (views // 2) + side
    place = jnp.stack([core, lax.axis_index("head"), side * half, (1 - side) * half])
    place = place.astype(jnp.int32)
    arrays = tuple(a.reshape(length, cols) for a in (queries, saved_keys, saved_values, output_grad))

    ready = []
    for step in range(0, half, 2):
        if step + 1 < half:
            picks = (
                lambda c, here, beside, step=step: here + step + c,
                lambda c, here, beside, step=step: here + step + 1 - c,
                lambda c, here, beside, step=step: beside + step + c,
                lambda c, here, beside, step=step: beside + step + 1 - c,
            )
            own, to_mate, to_x, to_cross = pack(picks, place, view_links, arrays)
            sources = (own, moved(to_mate, mate), moved(to_x, along_x), moved(to_cross, across_x))
        else:
            picks = (
                lambda c, here, beside, step=step: here + step,
                lambda c, here, beside, step=step: beside + step,
            )
            own, to_x = pack(picks, place, view_links, arrays)
            sources = (
                own,
                moved(own, only(1, mate)),
                moved(to_x, only(0, along_x)),
                moved(to_x, only(1, across_x)),
            )
        arrays = after(arrays, own)
        ready.append((step, step + 1 < half, sources))

    own_weights = turned_weights(after((query_weight, key_weight, value_weight), arrays[0]))
    mate_weights = moved(own_weights, mate)

    first, second = [], []
    turn = place
    for step, both, sources in ready:
        made = attention(turn, both, sources)
        (turn,) = after((place,), made)
        if both:
            inward = moved(made, only(1, mate))
            ahead = moved(made, straight)
            aside = moved(made, crossed)
            first += [
                (made, (HERE, step, 0)),
                (inward, (HERE, step + 1, 1)),
                (ahead, (BESIDE, step, 2)),
                (aside, (BESIDE, step + 1, 3)),
            ]
            second += [
                (ahead, (HERE, step + 1, 0)),
                (aside, (HERE, step, 1)),
                (moved(ahead, only(1, along_x)), (BESIDE, step + 1, 2)),
                (moved(ahead, only(0, across_y)), (BESIDE, step, 3)),
            ]
        else:
            ahead = moved(made, only(0, along_x))
            aside = moved(made, only(0, across_y))
            first += [(made, (HERE, step, 0)), (ahead, (BESIDE, step, 2))]
            second += [
                (aside, (HERE, step, 1)),
                (moved(ahead, only(0, across_y)), (BESIDE, step, 3)),
            ]

    def exchange(role, slots):
        total = slots[0].astype(jnp.float32)
        for s in range(1, groups):
            pairs = [
                ((y * views + v) * groups + z, (y * views + v) * groups + (z ^ s))
                for y in range(prompts)
                for v in range(role, views, 2)
                for z in range(groups)
            ]
            total += lax.ppermute(slots[s], ("dp", "view", "head"), pairs).astype(jnp.float32)
        return total.astype(jnp.bfloat16)

    def deliver(role, total):
        pairs = [
            (
                (y * views + v) * groups + z,
                ((y ^ role) * views + (v ^ z)) * groups + y * (views // 2) + v // 2,
            )
            for y in range(prompts)
            for v in range(role, views, 2)
            for z in range(groups)
        ]
        return lax.ppermute(total, ("dp", "view", "head"), pairs)

    first_slots = input_product(turn, 0, first, own_weights, mate_weights)
    first_total = exchange(0, first_slots)
    (turn,) = after((place,), first_total)
    second_slots = input_product(turn, 1, second, own_weights, mate_weights)
    second_total = exchange(1, second_slots)
    landed = (deliver(0, first_total), deliver(1, second_total))
    from_first = lax.axis_index("head") // (views // 2) == lax.axis_index("dp")
    input_grad = jnp.where(from_first, landed[0], landed[1])

    flat = normed.reshape(length, model_width)

    def columns(of_chip):
        return lax.dynamic_slice_in_dim(flat, of_chip * (2 * rows), 2 * rows, axis=1)

    toward_x, toward_y = jnp.bitwise_xor(chip, 1), jnp.bitwise_xor(chip, 2)
    here = columns(chip)
    to_straight = columns(jnp.where(core == 0, toward_x, toward_y))
    to_crossed = columns(jnp.where(core == 0, toward_y, toward_x))
    to_corner = columns(jnp.bitwise_xor(chip, 3))
    (sent,) = after((here,), ready[0][2][1])
    to_straight, to_crossed, to_corner = after(
        (to_straight, to_crossed, to_corner), second[2][0], second[3][0]
    )
    tokens = (
        here,
        moved(sent, only(1, mate)),
        moved(to_straight, straight),
        moved(to_crossed, crossed),
        moved(to_corner, corner_same),
        moved(to_corner, corner_cross),
    )
    for_mate = weight_product(place, False, mean_scale, tokens, (first, second))
    from_mate = [moved(w, mate) for w in for_mate]
    weight_grads = weight_product(place, True, mean_scale, tokens, (first, second), from_mate)
    return (
        input_grad.reshape(1, 1, length, model_width // groups),
        *weight_grads,
    )


def solution(mesh):
    prompts, views, groups = (mesh.shape[name] for name in ("dp", "view", "head"))
    loop_of_four = prompts * 2 == views and prompts * views == 2 * groups and views == groups

    def choose(*arrays):
        batch, held, length, cols = arrays[1].shape
        if loop_of_four and batch == held == 1 and length % HD == 0 and cols % (2 * HD) == 0:
            return gather_body(*arrays)
        return halo_body(*arrays)

    placed = (
        P("dp", "view", None, None),
        P("dp", "view", None, "head"),
        P("dp", "view", None, "head"),
        P("dp", "view", None, "head"),
        P("dp", "view", None, "head"),
        P("view", None),
        P(("dp", "view"), "head"),
        P(("dp", "view"), "head"),
        P(("dp", "view"), "head"),
    )
    return jax.shard_map(
        choose,
        mesh=mesh,
        in_specs=placed,
        out_specs=(
            P("dp", "view", None, "head"),
            P(("dp", "view"), "head"),
            P(("dp", "view"), "head"),
            P(("dp", "view"), "head"),
        ),
        check_vma=False,
    )
```

time: 192 us -> 176 us (0.917)
  Pallas kernels: 54.5 us -> 36.3 us
  starting transfers between devices: 59.9 us -> 76.9 us
  waiting for transfers between devices: 56 us -> 43.3 us
    pallas_call x10 -> x9, Pallas kernels: 54.5 us -> 36.3 us  [the longest x2 14.2 us: weight_product(): pl.pallas_call(functools.partial(weight_kernel, mine, mean_scale, [[mark...]
    ppermute x19 -> x23, waiting for transfers between devices: 29.5 us -> 15.6 us  [moved(): return lax.ppermute(value, ('dp', 'view'), pairs)]
    ppermute x19 -> x23, starting transfers between devices: 43.6 us -> 55.6 us  [moved(): return lax.ppermute(value, ('dp', 'view'), pairs)]
    ppermute x6, starting transfers between devices: 11.3 us -> 16 us  [exchange(): lax.ppermute(slots[s], ('dp', 'view', 'head'), pairs).astype(jnp.float32)]
    ppermute x2, waiting for transfers between devices: 20.6 us -> 23.1 us  [deliver(): return lax.ppermute(total, ('dp', 'view', 'head'), pairs)]
    another operation x2 -> x1, other arithmetic: 2.62 us -> 0.65 us  [gather_body(): jnp.stack([core, lax.axis_index('head'), side * half, (1 - side) * half])]
    unnamed x44 -> x54, local copies, waits for them, and re-layouts: 11.3 us -> 9.99 us
  transfers between devices with their start and end apart: 27 -> 31, of which waited for: 7 -> 6; matrix products, arithmetic and copies ran while one was open for 4% -> 4% of each run, Pallas kernels for 24% -> 15%
where the time goes in v4:
time: 176 us; the launch traced here: 175 us
  starting transfers between devices  76.9 us (44%)
  waiting for transfers between devices  43.3 us (25%)
  Pallas kernels  36.3 us (21%)
  local copies, waits for them, and re-layouts  11.5 us (7%)
  other arithmetic  5.55 us (3%)
    ppermute x23, starting transfers between devices, moved(): return lax.ppermute(value, ('dp', 'view'), pairs)  55.6 us
    ppermute x2, waiting for transfers between devices, deliver(): return lax.ppermute(total, ('dp', 'view', 'head'), pairs)  23.1 us
    ppermute x6, starting transfers between devices, exchange(): lax.ppermute(slots[s], ('dp', 'view', 'head'), pairs).astype(jnp.float32)  16 us
    ppermute x23, waiting for transfers between devices, moved(): return lax.ppermute(value, ('dp', 'view'), pairs)  15.6 us
    pallas_call x2, Pallas kernels, weight_product(): pl.pallas_call(functools.partial(weight_kernel, mine, mean_scale, [[mark...  14.2 us
    pallas_call x2, Pallas kernels, input_product(): pl.pallas_call(functools.partial(input_kernel, role, [mark for _, mark in...  10.9 us
    unnamed x54, local copies, waits for them, and re-layouts  9.99 us
    ppermute x2, starting transfers between devices, deliver(): return lax.ppermute(total, ('dp', 'view', 'head'), pairs)  5.31 us
  transfers between devices with their start and end apart: 31, of which 6 were waited for; matrix products, arithmetic and copies ran while one was open for 4% of the time, Pallas kernels for 15%

profile of v4, /device:TPU:1, one launch (start us, length us, event | category | flops | bytes accessed | tf_op | source)
XLA Modules:
  0.0 175.0 jit_solution(6817206669986465687)
XLA Ops:
  0.7 0.7 pad_add_fusion.place_ref
  1.3 2.5 %pack_heads.2 = (bf16[1040,128]{1,0:T(8,128)(2,1)}, bf16[1040,128]{1,0:T(8,128)(2,1)}, bf16[1040,128]{1,0:T(8,128)(2,1)}, bf16[1040,128]{1,0:T(8,128)(2,1)}) custom-call(s32[4]{0:T(128)} %pad_add_fusion.place_ref, s32[1,2]{1,0:T(1,128)} %links_ref.3, bf16[256,768]{1,0:T(8,128)(2,1)} %bitcast.18, bf16[256,768]{1,0:T(8,128)(2,1)} %bitcast.20, ...), custom_call_target="tpu_custom_call" | custom-call | tf_op jit(solution)/shard_map/pack_heads/pallas_call | solution.py:217
  3.8 0.1 collective-permute-start
  3.9 2.7 %collective-permute-start.1 = (bf16[1040,128]{1,0:T(8,128)(2,1)}, bf16[1040,128]{1,0:T(8,128)(2,1)S(1)}, u32[]{:S(2)}, u32[]{:S(2)}) collective-permute-start(bf16[1040,128]{1,0:T(8,128)(2,1)} %get-tuple-element.40), channel_id=1, source_target_pairs={{0,8},{4,12},{8,0},{12,4},{16,24},{20,28},{24,16},{28,20},{1,9},{5... | collective-permute-start | bytes 798728 | tf_op jit(solution)/shard_map/ppermute | solution.py:128
  6.6 0.0 collective-permute-start.2
  6.6 0.0 copy-start.21
  6.6 1.1 copy-done.21
  7.7 1.8 %turn_weights.1.refs_6_ = bf16[2304,384]{1,0:T(8,128)(2,1)} custom-call(bf16[384,768]{1,0:T(8,128)(2,1)S(1)} %copy-done.19, bf16[384,768]{1,0:T(8,128)(2,1)S(1)} %copy-done.20, bf16[384,768]{1,0:T(8,128)(2,1)S(1)} %copy-done.21), custom_call_target="tpu_custom_call" | custom-call | tf_op jit(solution)/shard_map/turn_weights/pallas_call | solution.py:310
  9.4 0.4 collective-permute-start.10
  9.8 2.3 %pack_heads.3 = (bf16[1040,128]{1,0:T(8,128)(2,1)}, bf16[1040,128]{1,0:T(8,128)(2,1)}) custom-call(s32[4]{0:T(128)} %pad_add_fusion.place_ref, s32[1,2]{1,0:T(1,128)} %links_ref.3, bf16[256,768]{1,0:T(8,128)(2,1)} %bitcast.19, bf16[256,768]{1,0:T(8,128)(2,1)} %bitcast.21, bf16[256,768]{1,0:T(8,128)(2,1)} %bitcast.23, bf16[256,768]{1,0:T(8,128)(2,1)} %bitcast.25), custom_call_target="tpu_custom_call" | custom-call | tf_op jit(solution)/shard_map/pack_heads/pallas_call | solution.py:217
  12.1 2.0 %collective-permute-start.3 = (bf16[1040,128]{1,0:T(8,128)(2,1)}, bf16[1040,128]{1,0:T(8,128)(2,1)S(1)}, u32[]{:S(2)}, u32[]{:S(2)}) collective-permute-start(bf16[1040,128]{1,0:T(8,128)(2,1)} %get-tuple-element.47.x0), channel_id=1, source_target_pairs={{4,0},{12,8},{20,16},{28,24},{5,1},{13,9},{21,17},{29,25},{6,2},{1... | collective-permute-start | bytes 798728 | tf_op jit(solution)/shard_map/ppermute | solution.py:128
  14.1 0.0 collective-permute-done.x1
  14.1 0.8 collective-permute-start.4
  15.0 4.2 %collective-permute-start.5 = (bf16[1040,128]{1,0:T(8,128)(2,1)}, bf16[1040,128]{1,0:T(8,128)(2,1)S(1)}, u32[]{:S(2)}, u32[]{:S(2)}) collective-permute-start(bf16[1040,128]{1,0:T(8,128)(2,1)} %get-tuple-element.48), channel_id=1, source_target_pairs={{4,8},{12,0},{20,24},{28,16},{5,9},{13,1},{21,25},{29,17},{6,10},{... | collective-permute-start | bytes 798728 | tf_op jit(solution)/shard_map/ppermute | solution.py:128
  19.1 0.1 collective-permute-done.2.x3
  19.2 4.2 %attention_gradients.2.refs_0_.refs_6_ = bf16[4,256,384]{2,1,0:T(8,128)(2,1)S(1)} custom-call(s32[4]{0:T(128)S(1)} %copy-done.24, bf16[1040,128]{1,0:T(8,128)(2,1)S(1)} %copy-done.25, bf16[1040,128]{1,0:T(8,128)(2,1)S(1)} %collective-permute-done.x1, bf16[1040,128]{1,0:T(8,128)(2,1)S(1)} %collective-permute-done.1.x2, ...), custom_call_target="tpu_custom_call" | custom-call | flops 2013265920 | bytes 1835008 | tf_op jit(solution)/shard_map/attention_gradients/pallas_call | solution.py:285
  23.5 1.6 collective-permute-start.7
  25.1 0.6 attention_gradients.3.refs_4_.refs_10_
  25.7 1.5 collective-permute-start.9
  27.2 8.2 %collective-permute-start.6 = (bf16[4,256,384]{2,1,0:T(8,128)(2,1)S(1)}, bf16[4,256,384]{2,1,0:T(8,128)(2,1)S(1)}, u32[]{:S(2)}, u32[]{:S(2)}) collective-permute-start(bf16[4,256,384]{2,1,0:T(8,128)(2,1)S(1)} %attention_gradients.2.refs_0_.refs_6_), channel_id=1, source_target_pairs={{4,0},{12,8},{20,16},{28,24},{5,1},{13,9},{21,17},{29,25},{6,2},{1... | collective-permute-start | bytes 2359304 | tf_op jit(solution)/shard_map/ppermute | solution.py:128
  35.5 0.1 collective-permute-start.8
  35.5 2.6 %collective-permute-start.15 = (bf16[4,256,384]{2,1,0:T(8,128)(2,1)S(1)}, bf16[4,256,384]{2,1,0:T(8,128)(2,1)S(1)}, u32[]{:S(2)}, u32[]{:S(2)}) collective-permute-start(bf16[4,256,384]{2,1,0:T(8,128)(2,1)S(1)} %collective-permute-done.7.refs_2_.refs_0_.refs_8_.refs_12_), channel_id=1, source_target_pairs={{4,12},{12,4},{20,28},{28,20},{5,13},{13,5},{21,29},{29,21},{6,14}... | collective-permute-start | bytes 2359304 | tf_op jit(solution)/shard_map/ppermute | solution.py:128
  38.1 1.3 collective-permute-start.16
  39.5 1.3 collective-permute-start.17
  40.8 10.7 %collective-permute-done.8.refs_3_.refs_1_.refs_9_.refs_13_ = bf16[4,256,384]{2,1,0:T(8,128)(2,1)S(1)} collective-permute-done((bf16[4,256,384]{2,1,0:T(8,128)(2,1)S(1)}, bf16[4,256,384]{2,1,0:T(8,128)(2,1)S(1)}, u32[]{:S(2)}, u32[]{:S(2)}) %collective-permute-start.8) | collective-permute-done | bytes 786464 | tf_op jit(solution)/shard_map/ppermute | solution.py:128
  51.5 1.3 collective-permute-start.18
  52.8 1.0 input_gradient.2
  53.8 0.0 copy-start.22
  53.8 0.7 copy-done.22
  54.6 1.4 collective-permute-start.11
  56.0 4.5 %collective-permute-done.15.refs_2_.refs_14_ = bf16[4,256,384]{2,1,0:T(8,128)(2,1)S(1)} collective-permute-done((bf16[4,256,384]{2,1,0:T(8,128)(2,1)S(1)}, bf16[4,256,384]{2,1,0:T(8,128)(2,1)S(1)}, u32[]{:S(2)}, u32[]{:S(2)}) %collective-permute-start.15) | collective-permute-done | bytes 786464 | tf_op jit(solution)/shard_map/ppermute | solution.py:128
  60.5 0.9 copy-done.3
  61.5 1.4 collective-permute-start.12
  62.9 0.2 collective-permute-done.16.refs_3_.refs_15_
  63.1 0.9 copy-done.6
  64.0 1.4 collective-permute-start.13
  65.5 1.5 dynamic-slice_bitcast_fusion
  67.0 15.2 %collective-permute-start.23 = (bf16[256,768]{1,0:T(8,128)(2,1)S(1)}, bf16[256,768]{1,0:T(8,128)(2,1)S(1)}, u32[]{:S(2)}, u32[]{:S(2)}) collective-permute-start(bf16[256,768]{1,0:T(8,128)(2,1)S(1)} %get-tuple-element.62.refs_0_), channel_id=1, source_target_pairs={{4,0},{12,8},{20,16},{28,24},{5,1},{13,9},{21,17},{29,25},{6,2},{1... | collective-permute-start | bytes 1179656 | tf_op jit(solution)/shard_map/ppermute | solution.py:128
  82.2 4.6 %collective-permute-start.26 = (bf16[256,768]{1,0:T(8,128)(2,1)S(1)}, bf16[256,768]{1,0:T(8,128)(2,1)S(1)}, u32[]{:S(2)}, u32[]{:S(2)}) collective-permute-start(bf16[256,768]{1,0:T(8,128)(2,1)S(1)} %get-tuple-element.65), channel_id=1, source_target_pairs={{4,28},{12,20},{20,12},{28,4},{5,29},{13,21},{21,13},{29,5},{6,30}... | collective-permute-start | bytes 1179656 | tf_op jit(solution)/shard_map/ppermute | solution.py:128
  86.9 1.3 collective-permute-start.27
  88.2 2.2 %add_convert_fusion.1 = bf16[256,768]{1,0:T(8,128)(2,1)} fusion(bf16[256,768]{1,0:T(8,128)(2,1)} %collective-permute-done.13, bf16[256,768]{1,0:T(8,128)(2,1)} %collective-permute-done.12, bf16[256,768]{1,0:T(8,128)(2,1)} %collective-permute-done.11, bf16[256,768]{1,0:T(8,128)(2,1)S(1)} %copy-done.23), kind=kLoop, calls=%fused_computation.1 | loop fusion | flops 1572864 | bytes 1966080 | tf_op jit(solution)/shard_map/convert_element_type | solution.py:580
  90.3 0.3 collective-permute-start.24
  90.6 5.6 %collective-permute-start.25 = (bf16[256,768]{1,0:T(8,128)(2,1)S(1)}, bf16[256,768]{1,0:T(8,128)(2,1)S(1)}, u32[]{:S(2)}, u32[]{:S(2)}) collective-permute-start(bf16[256,768]{1,0:T(8,128)(2,1)S(1)} %get-tuple-element.64), channel_id=1, source_target_pairs={{0,20},{4,8},{8,28},{12,0},{16,4},{20,24},{24,12},{28,16},{1,21},{... | collective-permute-start | bytes 1179656 | tf_op jit(solution)/shard_map/ppermute | solution.py:128
  96.2 9.9 %input_gradient.3 = (bf16[256,768]{1,0:T(8,128)(2,1)S(1)}, bf16[256,768]{1,0:T(8,128)(2,1)S(1)}, bf16[256,768]{1,0:T(8,128)(2,1)S(1)}, bf16[256,768]{1,0:T(8,128)(2,1)S(1)}) custom-call(s32[4]{0:T(128)S(1)} %copy-done.24, bf16[4,256,384]{2,1,0:T(8,128)(2,1)S(1)} %collective-permute-done.7.refs_2_.refs_0_.refs_8_.refs_12_, ...), custom_call_target="tpu_custom_call" | custom-call | flops 3623878656 | bytes 9830400 | tf_op jit(solution)/shard_map/input_gradient/pallas_call | solution.py:371
  106.1 5.7 %collective-permute-start.19 = (bf16[256,768]{1,0:T(8,128)(2,1)S(1)}, bf16[256,768]{1,0:T(8,128)(2,1)S(1)}, u32[]{:S(2)}, u32[]{:S(2)}) collective-permute-start(bf16[256,768]{1,0:T(8,128)(2,1)S(1)} %get-tuple-element.59), channel_id=1, source_target_pairs={{4,5},{5,4},{6,7},{7,6},{12,13},{13,12},{14,15},{15,14},{20,21},{2... | collective-permute-start | bytes 1179656 | tf_op jit(solution)/shard_map/ppermute | solution.py:579
  111.8 2.9 %collective-permute-start.20 = (bf16[256,768]{1,0:T(8,128)(2,1)S(1)}, bf16[256,768]{1,0:T(8,128)(2,1)S(1)}, u32[]{:S(2)}, u32[]{:S(2)}) collective-permute-start(bf16[256,768]{1,0:T(8,128)(2,1)S(1)} %get-tuple-element.60), channel_id=1, source_target_pairs={{4,6},{5,7},{6,4},{7,5},{12,14},{13,15},{14,12},{15,13},{20,22},{2... | collective-permute-start | bytes 1179656 | tf_op jit(solution)/shard_map/ppermute | solution.py:579
  114.8 3.1 %collective-permute-start.21 = (bf16[256,768]{1,0:T(8,128)(2,1)S(1)}, bf16[256,768]{1,0:T(8,128)(2,1)S(1)}, u32[]{:S(2)}, u32[]{:S(2)}) collective-permute-start(bf16[256,768]{1,0:T(8,128)(2,1)S(1)} %get-tuple-element.61), channel_id=1, source_target_pairs={{4,7},{5,6},{6,5},{7,4},{12,15},{13,14},{14,13},{15,12},{20,23},{2... | collective-permute-start | bytes 1179656 | tf_op jit(solution)/shard_map/ppermute | solution.py:579
  117.9 6.5 %weight_gradient_mate.1 = (f32[384,768]{1,0:T(8,128)}, f32[384,768]{1,0:T(8,128)}, f32[384,768]{1,0:T(8,128)}) custom-call(s32[4]{0:T(128)S(1)} %copy-done.24, bf16[256,768]{1,0:T(8,128)(2,1)S(1)} %get-tuple-element.62.refs_0_, bf16[256,768]{1,0:T(8,128)(2,1)S(1)} %collective-permute-done.23.refs_1_, bf16[256,768]{1,0:T(8,128)(2,1)S(1)} %collective-permute-done.24.refs_2_, ...), custom_call_target="tpu_custom_call" | custom-call | flops 1811939328 | bytes 9043968 | tf_op jit(solution)/shard_map/weight_gradient_mate/pallas_call | solution.py:462
  124.5 0.1 collective-permute-start.28
  124.6 0.5 collective-permute-start.29
  125.1 0.1 collective-permute-start.30
  125.2 4.5 %collective-permute-done.20 = bf16[256,768]{1,0:T(8,128)(2,1)S(1)} collective-permute-done((bf16[256,768]{1,0:T(8,128)(2,1)S(1)}, bf16[256,768]{1,0:T(8,128)(2,1)S(1)}, u32[]{:S(2)}, u32[]{:S(2)}) %collective-permute-start.20) | collective-permute-done | bytes 393248 | tf_op jit(solution)/shard_map/ppermute | solution.py:579
  129.7 1.3 collective-permute-start.14
  131.0 0.9 add_convert_fusion
  131.9 4.0 %collective-permute-start.22 = (bf16[256,768]{1,0:T(8,128)(2,1)}, bf16[256,768]{1,0:T(8,128)(2,1)}, u32[]{:S(2)}, u32[]{:S(2)}) collective-permute-start(bf16[256,768]{1,0:T(8,128)(2,1)} %add_convert_fusion), channel_id=1, source_target_pairs={{4,20},{5,16},{6,28},{7,24},{12,29},{13,25},{14,21},{15,17},{20,6}... | collective-permute-start | bytes 1179656 | tf_op jit(solution)/shard_map/ppermute | solution.py:592
  135.9 23.1 %collective-permute-done.14 = bf16[256,768]{1,0:T(8,128)(2,1)} collective-permute-done((bf16[256,768]{1,0:T(8,128)(2,1)}, bf16[256,768]{1,0:T(8,128)(2,1)}, u32[]{:S(2)}, u32[]{:S(2)}) %collective-permute-start.14) | collective-permute-done | bytes 393248 | tf_op jit(solution)/shard_map/ppermute | solution.py:592
  159.1 1.8 %select_bitcast_fusion = bf16[1,1,256,768]{3,2,1,0:T(8,128)(2,1)} fusion(bf16[256,768]{1,0:T(8,128)(2,1)} %collective-permute-done.14, bf16[256,768]{1,0:T(8,128)(2,1)} %collective-permute-done.22, pred[]{:T(512)S(6)} %eq.7), kind=kLoop, calls=%fused_computation.6 | loop fusion | flops 196608 | bytes 1179649 | tf_op jit(solution)/shard_map/reshape | solution.py:629
  160.9 1.1 copy-done.5
  162.0 1.1 copy-done.8
  163.2 1.0 copy-done.12
  164.2 1.0 copy-done.14
  165.2 1.0 copy-done.16
  166.2 1.0 copy-done.18
  167.2 7.6 %weight_gradient_own.1 = (f32[384,768]{1,0:T(8,128)}, f32[384,768]{1,0:T(8,128)}, f32[384,768]{1,0:T(8,128)}) custom-call(s32[4]{0:T(128)S(1)} %copy-done.24, bf16[256,768]{1,0:T(8,128)(2,1)S(1)} %get-tuple-element.62.refs_0_, bf16[256,768]{1,0:T(8,128)(2,1)S(1)} %copy-done.10, bf16[256,768]{1,0:T(8,128)(2,1)S(1)} %copy-done.16, ...), custom_call_target="tpu_custom_call" | custom-call | flops 1811939328 | bytes 9043968 | tf_op jit(solution)/shard_map/weight_gradient_own/pallas_call | solution.py:462
  (66 shorter events, 0.1 us)
Async XLA Ops:
  0.6 6.0 %copy-start.19 = (bf16[384,768]{1,0:T(8,128)(2,1)S(1)}, bf16[384,768]{1,0:T(8,128)(2,1)}, u32[]{:S(2)}) copy-start(bf16[384,768]{1,0:T(8,128)(2,1)} %q_ref) | copy-start | bytes 1769476
  0.6 5.9 %copy-start.20 = (bf16[384,768]{1,0:T(8,128)(2,1)S(1)}, bf16[384,768]{1,0:T(8,128)(2,1)}, u32[]{:S(2)}) copy-start(bf16[384,768]{1,0:T(8,128)(2,1)} %k_ref) | copy-start | bytes 1769476
  3.8 10.3 %collective-permute-start = (bf16[1040,128]{1,0:T(8,128)(2,1)}, bf16[1040,128]{1,0:T(8,128)(2,1)S(1)}, u32[]{:S(2)}, u32[]{:S(2)}) collective-permute-start(bf16[1040,128]{1,0:T(8,128)(2,1)} %get-tuple-element.39), channel_id=1, source_target_pairs={{0,4},{4,0},{8,12},{12,8},{16,20},{20,16},{24,28},{28,24},{1,5},{5... | collective-permute-start | bytes 798728 | tf_op jit(solution)/shard_map/ppermute | solution.py:128
  3.9 11.0 %collective-permute-start.1 = (bf16[1040,128]{1,0:T(8,128)(2,1)}, bf16[1040,128]{1,0:T(8,128)(2,1)S(1)}, u32[]{:S(2)}, u32[]{:S(2)}) collective-permute-start(bf16[1040,128]{1,0:T(8,128)(2,1)} %get-tuple-element.40), channel_id=1, source_target_pairs={{0,8},{4,12},{8,0},{12,4},{16,24},{20,28},{24,16},{28,20},{1,9},{5... | collective-permute-start | bytes 798728 | tf_op jit(solution)/shard_map/ppermute | solution.py:128
  6.6 12.6 %collective-permute-start.2 = (bf16[1040,128]{1,0:T(8,128)(2,1)}, bf16[1040,128]{1,0:T(8,128)(2,1)S(1)}, u32[]{:S(2)}, u32[]{:S(2)}) collective-permute-start(bf16[1040,128]{1,0:T(8,128)(2,1)} %get-tuple-element.41), channel_id=1, source_target_pairs={{0,12},{4,8},{8,4},{12,0},{16,28},{20,24},{24,20},{28,16},{1,13},{... | collective-permute-start | bytes 798728 | tf_op jit(solution)/shard_map/ppermute | solution.py:128
  6.6 1.1 copy-start.21
  9.4 9.8 %copy-start.24 = (s32[4]{0:T(128)S(1)}, s32[4]{0:T(128)}, u32[]{:S(2)}) copy-start(s32[4]{0:T(128)} %pad_add_fusion.place_ref) | copy-start | bytes 52
  9.4 9.8 %copy-start.25 = (bf16[1040,128]{1,0:T(8,128)(2,1)S(1)}, bf16[1040,128]{1,0:T(8,128)(2,1)}, u32[]{:S(2)}) copy-start(bf16[1040,128]{1,0:T(8,128)(2,1)} %get-tuple-element.38.x0) | copy-start | bytes 798724
  9.4 43.4 %collective-permute-start.10 = (bf16[2304,384]{1,0:T(8,128)(2,1)}, bf16[2304,384]{1,0:T(8,128)(2,1)}, u32[]{:S(2)}, u32[]{:S(2)}) collective-permute-start(bf16[2304,384]{1,0:T(8,128)(2,1)} %turn_weights.1.refs_6_), channel_id=1, source_target_pairs={{0,4},{4,0},{8,12},{12,8},{16,20},{20,16},{24,28},{28,24},{1,5},{5... | collective-permute-start | bytes 5308424 | tf_op jit(solution)/shard_map/ppermute | solution.py:128
  12.1 13.0 %collective-permute-start.3 = (bf16[1040,128]{1,0:T(8,128)(2,1)}, bf16[1040,128]{1,0:T(8,128)(2,1)S(1)}, u32[]{:S(2)}, u32[]{:S(2)}) collective-permute-start(bf16[1040,128]{1,0:T(8,128)(2,1)} %get-tuple-element.47.x0), channel_id=1, source_target_pairs={{4,0},{12,8},{20,16},{28,24},{5,1},{13,9},{21,17},{29,25},{6,2},{1... | collective-permute-start | bytes 798728 | tf_op jit(solution)/shard_map/ppermute | solution.py:128
  14.1 11.0 %copy-start.26 = (bf16[1040,128]{1,0:T(8,128)(2,1)S(1)}, bf16[1040,128]{1,0:T(8,128)(2,1)}, u32[]{:S(2)}) copy-start(bf16[1040,128]{1,0:T(8,128)(2,1)} %get-tuple-element.47.x0) | copy-start | bytes 798724
  14.1 11.0 %collective-permute-start.4 = (bf16[1040,128]{1,0:T(8,128)(2,1)}, bf16[1040,128]{1,0:T(8,128)(2,1)S(1)}, u32[]{:S(2)}, u32[]{:S(2)}) collective-permute-start(bf16[1040,128]{1,0:T(8,128)(2,1)} %get-tuple-element.48), channel_id=1, source_target_pairs={{0,8},{8,0},{16,24},{24,16},{1,9},{9,1},{17,25},{25,17},{2,10},{10... | collective-permute-start | bytes 798728 | tf_op jit(solution)/shard_map/ppermute | solution.py:128
  15.0 10.2 %collective-permute-start.5 = (bf16[1040,128]{1,0:T(8,128)(2,1)}, bf16[1040,128]{1,0:T(8,128)(2,1)S(1)}, u32[]{:S(2)}, u32[]{:S(2)}) collective-permute-start(bf16[1040,128]{1,0:T(8,128)(2,1)} %get-tuple-element.48), channel_id=1, source_target_pairs={{4,8},{12,0},{20,24},{28,16},{5,9},{13,1},{21,25},{29,17},{6,10},{... | collective-permute-start | bytes 798728 | tf_op jit(solution)/shard_map/ppermute | solution.py:128
  23.5 12.0 %collective-permute-start.7 = (bf16[4,256,384]{2,1,0:T(8,128)(2,1)S(1)}, bf16[4,256,384]{2,1,0:T(8,128)(2,1)S(1)}, u32[]{:S(2)}, u32[]{:S(2)}) collective-permute-start(bf16[4,256,384]{2,1,0:T(8,128)(2,1)S(1)} %attention_gradients.2.refs_0_.refs_6_), channel_id=1, source_target_pairs={{0,8},{4,20},{8,0},{12,28},{16,24},{20,4},{24,16},{28,12},{1,9},{5... | collective-permute-start | bytes 2359304 | tf_op jit(solution)/shard_map/ppermute | solution.py:128
  25.7 12.4 %collective-permute-start.9 = (bf16[4,256,384]{2,1,0:T(8,128)(2,1)S(1)}, bf16[4,256,384]{2,1,0:T(8,128)(2,1)}, u32[]{:S(2)}, u32[]{:S(2)}) collective-permute-start(bf16[4,256,384]{2,1,0:T(8,128)(2,1)S(1)} %attention_gradients.3.refs_4_.refs_10_), channel_id=1, source_target_pairs={{0,8},{8,0},{16,24},{24,16},{1,9},{9,1},{17,25},{25,17},{2,10},{10... | collective-permute-start | bytes 2359304 | tf_op jit(solution)/shard_map/ppermute | solution.py:128
  27.2 12.2 %collective-permute-start.6 = (bf16[4,256,384]{2,1,0:T(8,128)(2,1)S(1)}, bf16[4,256,384]{2,1,0:T(8,128)(2,1)S(1)}, u32[]{:S(2)}, u32[]{:S(2)}) collective-permute-start(bf16[4,256,384]{2,1,0:T(8,128)(2,1)S(1)} %attention_gradients.2.refs_0_.refs_6_), channel_id=1, source_target_pairs={{4,0},{12,8},{20,16},{28,24},{5,1},{13,9},{21,17},{29,25},{6,2},{1... | collective-permute-start | bytes 2359304 | tf_op jit(solution)/shard_map/ppermute | solution.py:128
  35.5 16.0 %collective-permute-start.8 = (bf16[4,256,384]{2,1,0:T(8,128)(2,1)S(1)}, bf16[4,256,384]{2,1,0:T(8,128)(2,1)S(1)}, u32[]{:S(2)}, u32[]{:S(2)}) collective-permute-start(bf16[4,256,384]{2,1,0:T(8,128)(2,1)S(1)} %attention_gradients.2.refs_0_.refs_6_), channel_id=1, source_target_pairs={{0,20},{4,8},{8,28},{12,0},{16,4},{20,24},{24,12},{28,16},{1,21},{... | collective-permute-start | bytes 2359304 | tf_op jit(solution)/shard_map/ppermute | solution.py:128
  35.5 25.0 %collective-permute-start.15 = (bf16[4,256,384]{2,1,0:T(8,128)(2,1)S(1)}, bf16[4,256,384]{2,1,0:T(8,128)(2,1)S(1)}, u32[]{:S(2)}, u32[]{:S(2)}) collective-permute-start(bf16[4,256,384]{2,1,0:T(8,128)(2,1)S(1)} %collective-permute-done.7.refs_2_.refs_0_.refs_8_.refs_12_), channel_id=1, source_target_pairs={{4,12},{12,4},{20,28},{28,20},{5,13},{13,5},{21,29},{29,21},{6,14}... | collective-permute-start | bytes 2359304 | tf_op jit(solution)/shard_map/ppermute | solution.py:128
  38.1 24.9 %collective-permute-start.16 = (bf16[4,256,384]{2,1,0:T(8,128)(2,1)S(1)}, bf16[4,256,384]{2,1,0:T(8,128)(2,1)S(1)}, u32[]{:S(2)}, u32[]{:S(2)}) collective-permute-start(bf16[4,256,384]{2,1,0:T(8,128)(2,1)S(1)} %collective-permute-done.7.refs_2_.refs_0_.refs_8_.refs_12_), channel_id=1, source_target_pairs={{0,20},{8,28},{16,4},{24,12},{1,21},{9,29},{17,5},{25,13},{2,22},{... | collective-permute-start | bytes 2359304 | tf_op jit(solution)/shard_map/ppermute | solution.py:128
  39.5 14.3 %copy-start = (bf16[4,256,384]{2,1,0:T(8,128)(2,1)}, bf16[4,256,384]{2,1,0:T(8,128)(2,1)S(1)}, u32[]{:S(2)}) copy-start(bf16[4,256,384]{2,1,0:T(8,128)(2,1)S(1)} %collective-permute-done.6.refs_1_.refs_7_) | copy-start | bytes 2359300
  39.5 50.9 %collective-permute-start.17 = (bf16[4,256,384]{2,1,0:T(8,128)(2,1)S(1)}, bf16[4,256,384]{2,1,0:T(8,128)(2,1)}, u32[]{:S(2)}, u32[]{:S(2)}) collective-permute-start(bf16[4,256,384]{2,1,0:T(8,128)(2,1)S(1)} %attention_gradients.3.refs_4_.refs_10_), channel_id=1, source_target_pairs={{0,20},{8,28},{16,4},{24,12},{1,21},{9,29},{17,5},{25,13},{2,22},{... | collective-permute-start | bytes 2359304 | tf_op jit(solution)/shard_map/ppermute | solution.py:128
  51.5 39.2 %collective-permute-start.18 = (bf16[4,256,384]{2,1,0:T(8,128)(2,1)}, bf16[4,256,384]{2,1,0:T(8,128)(2,1)}, u32[]{:S(2)}, u32[]{:S(2)}) collective-permute-start(bf16[4,256,384]{2,1,0:T(8,128)(2,1)} %collective-permute-done.9.refs_5_.refs_11_), channel_id=1, source_target_pairs={{0,20},{8,28},{16,4},{24,12},{1,21},{9,29},{17,5},{25,13},{2,22},{... | collective-permute-start | bytes 2359304 | tf_op jit(solution)/shard_map/ppermute | solution.py:128
  53.8 0.7 copy-start.22
  54.6 12.4 %collective-permute-start.11 = (bf16[256,768]{1,0:T(8,128)(2,1)}, bf16[256,768]{1,0:T(8,128)(2,1)}, u32[]{:S(2)}, u32[]{:S(2)}) collective-permute-start(bf16[256,768]{1,0:T(8,128)(2,1)} %get-tuple-element.54), channel_id=1, source_target_pairs={{0,1},{1,0},{2,3},{3,2},{8,9},{9,8},{10,11},{11,10},{16,17},{17,16... | collective-permute-start | bytes 1179656 | tf_op jit(solution)/shard_map/ppermute | solution.py:579
  60.5 0.9 copy-start.3
  61.5 20.8 %collective-permute-start.12 = (bf16[256,768]{1,0:T(8,128)(2,1)}, bf16[256,768]{1,0:T(8,128)(2,1)}, u32[]{:S(2)}, u32[]{:S(2)}) collective-permute-start(bf16[256,768]{1,0:T(8,128)(2,1)} %get-tuple-element.55), channel_id=1, source_target_pairs={{0,2},{1,3},{2,0},{3,1},{8,10},{9,11},{10,8},{11,9},{16,18},{17,19... | collective-permute-start | bytes 1179656 | tf_op jit(solution)/shard_map/ppermute | solution.py:579
  63.1 0.9 copy-start.6
  64.0 22.8 %collective-permute-start.13 = (bf16[256,768]{1,0:T(8,128)(2,1)}, bf16[256,768]{1,0:T(8,128)(2,1)}, u32[]{:S(2)}, u32[]{:S(2)}) collective-permute-start(bf16[256,768]{1,0:T(8,128)(2,1)} %get-tuple-element.56), channel_id=1, source_target_pairs={{0,3},{1,2},{2,1},{3,0},{8,11},{9,10},{10,9},{11,8},{16,19},{17,18... | collective-permute-start | bytes 1179656 | tf_op jit(solution)/shard_map/ppermute | solution.py:579
  65.4 22.7 %copy-start.23 = (bf16[256,768]{1,0:T(8,128)(2,1)S(1)}, bf16[256,768]{1,0:T(8,128)(2,1)}, u32[]{:S(2)}) copy-start(bf16[256,768]{1,0:T(8,128)(2,1)} %copy-done.22) | copy-start | bytes 1179652
  67.0 29.2 %copy-start.4 = (bf16[4,256,384]{2,1,0:T(8,128)(2,1)S(1)}, bf16[4,256,384]{2,1,0:T(8,128)(2,1)}, u32[]{:S(2)}) copy-start(bf16[4,256,384]{2,1,0:T(8,128)(2,1)} %copy-done.3) | copy-start | bytes 2359300
  67.0 29.2 %copy-start.7 = (bf16[4,256,384]{2,1,0:T(8,128)(2,1)S(1)}, bf16[4,256,384]{2,1,0:T(8,128)(2,1)}, u32[]{:S(2)}) copy-start(bf16[4,256,384]{2,1,0:T(8,128)(2,1)} %copy-done.6) | copy-start | bytes 2359300
  67.0 39.1 %collective-permute-start.23 = (bf16[256,768]{1,0:T(8,128)(2,1)S(1)}, bf16[256,768]{1,0:T(8,128)(2,1)S(1)}, u32[]{:S(2)}, u32[]{:S(2)}) collective-permute-start(bf16[256,768]{1,0:T(8,128)(2,1)S(1)} %get-tuple-element.62.refs_0_), channel_id=1, source_target_pairs={{4,0},{12,8},{20,16},{28,24},{5,1},{13,9},{21,17},{29,25},{6,2},{1... | collective-permute-start | bytes 1179656 | tf_op jit(solution)/shard_map/ppermute | solution.py:128
  82.2 35.7 %collective-permute-start.26 = (bf16[256,768]{1,0:T(8,128)(2,1)S(1)}, bf16[256,768]{1,0:T(8,128)(2,1)S(1)}, u32[]{:S(2)}, u32[]{:S(2)}) collective-permute-start(bf16[256,768]{1,0:T(8,128)(2,1)S(1)} %get-tuple-element.65), channel_id=1, source_target_pairs={{4,28},{12,20},{20,12},{28,4},{5,29},{13,21},{21,13},{29,5},{6,30}... | collective-permute-start | bytes 1179656 | tf_op jit(solution)/shard_map/ppermute | solution.py:128
  86.9 31.1 %collective-permute-start.27 = (bf16[256,768]{1,0:T(8,128)(2,1)S(1)}, bf16[256,768]{1,0:T(8,128)(2,1)S(1)}, u32[]{:S(2)}, u32[]{:S(2)}) collective-permute-start(bf16[256,768]{1,0:T(8,128)(2,1)S(1)} %get-tuple-element.65), channel_id=1, source_target_pairs={{0,28},{8,20},{16,12},{24,4},{1,29},{9,21},{17,13},{25,5},{2,30},{... | collective-permute-start | bytes 1179656 | tf_op jit(solution)/shard_map/ppermute | solution.py:128
  90.3 27.6 %copy-start.1 = (bf16[4,256,384]{2,1,0:T(8,128)(2,1)S(1)}, bf16[4,256,384]{2,1,0:T(8,128)(2,1)}, u32[]{:S(2)}) copy-start(bf16[4,256,384]{2,1,0:T(8,128)(2,1)} %copy-done) | copy-start | bytes 2359300
  90.3 21.5 %collective-permute-start.24 = (bf16[256,768]{1,0:T(8,128)(2,1)S(1)}, bf16[256,768]{1,0:T(8,128)(2,1)S(1)}, u32[]{:S(2)}, u32[]{:S(2)}) collective-permute-start(bf16[256,768]{1,0:T(8,128)(2,1)S(1)} %get-tuple-element.63), channel_id=1, source_target_pairs={{0,8},{4,20},{8,0},{12,28},{16,24},{20,4},{24,16},{28,12},{1,9},{5... | collective-permute-start | bytes 1179656 | tf_op jit(solution)/shard_map/ppermute | solution.py:128
  90.6 24.1 %collective-permute-start.25 = (bf16[256,768]{1,0:T(8,128)(2,1)S(1)}, bf16[256,768]{1,0:T(8,128)(2,1)S(1)}, u32[]{:S(2)}, u32[]{:S(2)}) collective-permute-start(bf16[256,768]{1,0:T(8,128)(2,1)S(1)} %get-tuple-element.64), channel_id=1, source_target_pairs={{0,20},{4,8},{8,28},{12,0},{16,4},{20,24},{24,12},{28,16},{1,21},{... | collective-permute-start | bytes 1179656 | tf_op jit(solution)/shard_map/ppermute | solution.py:128
  106.1 18.4 %copy-start.9 = (bf16[256,768]{1,0:T(8,128)(2,1)}, bf16[256,768]{1,0:T(8,128)(2,1)S(1)}, u32[]{:S(2)}) copy-start(bf16[256,768]{1,0:T(8,128)(2,1)S(1)} %collective-permute-done.23.refs_1_) | copy-start | bytes 1179652
  106.1 19.0 %collective-permute-start.19 = (bf16[256,768]{1,0:T(8,128)(2,1)S(1)}, bf16[256,768]{1,0:T(8,128)(2,1)S(1)}, u32[]{:S(2)}, u32[]{:S(2)}) collective-permute-start(bf16[256,768]{1,0:T(8,128)(2,1)S(1)} %get-tuple-element.59), channel_id=1, source_target_pairs={{4,5},{5,4},{6,7},{7,6},{12,13},{13,12},{14,15},{15,14},{20,21},{2... | collective-permute-start | bytes 1179656 | tf_op jit(solution)/shard_map/ppermute | solution.py:579
  111.8 12.7 %copy-start.15 = (bf16[256,768]{1,0:T(8,128)(2,1)}, bf16[256,768]{1,0:T(8,128)(2,1)S(1)}, u32[]{:S(2)}) copy-start(bf16[256,768]{1,0:T(8,128)(2,1)S(1)} %collective-permute-done.24.refs_2_) | copy-start | bytes 1179652
  111.8 17.8 %collective-permute-start.20 = (bf16[256,768]{1,0:T(8,128)(2,1)S(1)}, bf16[256,768]{1,0:T(8,128)(2,1)S(1)}, u32[]{:S(2)}, u32[]{:S(2)}) collective-permute-start(bf16[256,768]{1,0:T(8,128)(2,1)S(1)} %get-tuple-element.60), channel_id=1, source_target_pairs={{4,6},{5,7},{6,4},{7,5},{12,14},{13,15},{14,12},{15,13},{20,22},{2... | collective-permute-start | bytes 1179656 | tf_op jit(solution)/shard_map/ppermute | solution.py:579
  114.8 9.7 %copy-start.17 = (bf16[256,768]{1,0:T(8,128)(2,1)}, bf16[256,768]{1,0:T(8,128)(2,1)S(1)}, u32[]{:S(2)}) copy-start(bf16[256,768]{1,0:T(8,128)(2,1)S(1)} %collective-permute-done.25.refs_3_) | copy-start | bytes 1179652
  114.8 16.2 %collective-permute-start.21 = (bf16[256,768]{1,0:T(8,128)(2,1)S(1)}, bf16[256,768]{1,0:T(8,128)(2,1)S(1)}, u32[]{:S(2)}, u32[]{:S(2)}) collective-permute-start(bf16[256,768]{1,0:T(8,128)(2,1)S(1)} %get-tuple-element.61), channel_id=1, source_target_pairs={{4,7},{5,6},{6,5},{7,4},{12,15},{13,14},{14,13},{15,12},{20,23},{2... | collective-permute-start | bytes 1179656 | tf_op jit(solution)/shard_map/ppermute | solution.py:579
  117.9 6.6 %copy-start.11 = (bf16[256,768]{1,0:T(8,128)(2,1)}, bf16[256,768]{1,0:T(8,128)(2,1)S(1)}, u32[]{:S(2)}) copy-start(bf16[256,768]{1,0:T(8,128)(2,1)S(1)} %collective-permute-done.26.refs_4_) | copy-start | bytes 1179652
  117.9 6.6 %copy-start.13 = (bf16[256,768]{1,0:T(8,128)(2,1)}, bf16[256,768]{1,0:T(8,128)(2,1)S(1)}, u32[]{:S(2)}) copy-start(bf16[256,768]{1,0:T(8,128)(2,1)S(1)} %collective-permute-done.27.refs_5_) | copy-start | bytes 1179652
  124.5 36.4 %collective-permute-start.28 = (f32[384,768]{1,0:T(8,128)}, f32[384,768]{1,0:T(8,128)}, u32[]{:S(2)}, u32[]{:S(2)}) collective-permute-start(f32[384,768]{1,0:T(8,128)} %get-tuple-element.66), channel_id=1, source_target_pairs={{0,4},{4,0},{8,12},{12,8},{16,20},{20,16},{24,28},{28,24},{1,5},{5... | collective-permute-start | bytes 3538952 | tf_op jit(solution)/shard_map/ppermute | solution.py:128
  124.6 36.3 %collective-permute-start.29 = (f32[384,768]{1,0:T(8,128)}, f32[384,768]{1,0:T(8,128)}, u32[]{:S(2)}, u32[]{:S(2)}) collective-permute-start(f32[384,768]{1,0:T(8,128)} %get-tuple-element.67), channel_id=1, source_target_pairs={{0,4},{4,0},{8,12},{12,8},{16,20},{20,16},{24,28},{28,24},{1,5},{5... | collective-permute-start | bytes 3538952 | tf_op jit(solution)/shard_map/ppermute | solution.py:128
  125.1 35.8 %collective-permute-start.30 = (f32[384,768]{1,0:T(8,128)}, f32[384,768]{1,0:T(8,128)}, u32[]{:S(2)}, u32[]{:S(2)}) collective-permute-start(f32[384,768]{1,0:T(8,128)} %get-tuple-element.68), channel_id=1, source_target_pairs={{0,4},{4,0},{8,12},{12,8},{16,20},{20,16},{24,28},{28,24},{1,5},{5... | collective-permute-start | bytes 3538952 | tf_op jit(solution)/shard_map/ppermute | solution.py:128
  129.7 29.4 %collective-permute-start.14 = (bf16[256,768]{1,0:T(8,128)(2,1)}, bf16[256,768]{1,0:T(8,128)(2,1)}, u32[]{:S(2)}, u32[]{:S(2)}) collective-permute-start(bf16[256,768]{1,0:T(8,128)(2,1)} %add_convert_fusion.1), channel_id=1, source_target_pairs={{0,0},{1,4},{2,8},{3,12},{8,9},{9,13},{10,1},{11,5},{16,18},{17,22... | collective-permute-start | bytes 1179656 | tf_op jit(solution)/shard_map/ppermute | solution.py:592
  131.9 27.2 %collective-permute-start.22 = (bf16[256,768]{1,0:T(8,128)(2,1)}, bf16[256,768]{1,0:T(8,128)(2,1)}, u32[]{:S(2)}, u32[]{:S(2)}) collective-permute-start(bf16[256,768]{1,0:T(8,128)(2,1)} %add_convert_fusion), channel_id=1, source_target_pairs={{4,20},{5,16},{6,28},{7,24},{12,29},{13,25},{14,21},{15,17},{20,6}... | collective-permute-start | bytes 1179656 | tf_op jit(solution)/shard_map/ppermute | solution.py:592
  135.9 25.0 %copy-start.2 = (bf16[4,256,384]{2,1,0:T(8,128)(2,1)S(1)}, bf16[4,256,384]{2,1,0:T(8,128)(2,1)}, u32[]{:S(2)}) copy-start(bf16[4,256,384]{2,1,0:T(8,128)(2,1)} %copy-done) | copy-start | bytes 2359300
  135.9 25.0 %copy-start.10 = (bf16[256,768]{1,0:T(8,128)(2,1)S(1)}, bf16[256,768]{1,0:T(8,128)(2,1)}, u32[]{:S(2)}) copy-start(bf16[256,768]{1,0:T(8,128)(2,1)} %copy-done.9) | copy-start | bytes 1179652
  160.9 1.1 copy-start.5
  162.0 1.1 copy-start.8
  163.2 1.0 copy-start.12
  164.2 1.0 copy-start.14
  165.2 1.0 copy-start.16
  166.2 1.0 copy-start.18

commit v5 on v4

--- a/solution.py
+++ b/solution.py
@@ -196,31 +196,41 @@
 FLAG_ROWS = 16
 
 
-def pack_kernel(picks, place_ref, links_ref, q_ref, k_ref, v_ref, g_ref, *out_refs):
-    length = q_ref.shape[0]
-    core = place_ref[CORE]
-    for pick, out_ref in zip(picks, out_refs):
-        start = pick(core, place_ref[HERE], place_ref[BESIDE]) * HD
-        for kind, source in enumerate((q_ref, k_ref, v_ref, g_ref)):
-            out_ref[kind * length : (kind + 1) * length] = source[:, lanes(start, HD)]
-        row = lax.broadcasted_iota(jnp.int32, (FLAG_ROWS, HD), 0)
-        gaps = [
-            jnp.where(links_ref[0, side] >= 0, 0.0, 1.0).astype(jnp.float32) for side in range(2)
-        ]
-        flags = jnp.where(row < FLAG_ROWS // 2, gaps[0], gaps[1])
+def pack_kernel(count, place_ref, links_ref, *refs):
+    del place_ref
+    sources, out_refs = refs[: 4 * count], refs[4 * count :]
+    length = sources[0].shape[0]
+    row = lax.broadcasted_iota(jnp.int32, (FLAG_ROWS, HD), 0)
+    gaps = [jnp.where(links_ref[0, side] >= 0, 0.0, 1.0).astype(jnp.float32) for side in range(2)]
+    flags = jnp.where(row < FLAG_ROWS // 2, gaps[0], gaps[1])
+    for at, out_ref in enumerate(out_refs):
+        for kind in range(4):
+            out_ref[kind * length : (kind + 1) * length] = sources[4 * at + kind][...]
         out_ref[4 * length : 4 * length + FLAG_ROWS] = flags.astype(out_ref.dtype)
 
 
 def pack(picks, place, links, arrays):
     length = arrays[0].shape[0]
-    out = jax.ShapeDtypeStruct((4 * length + FLAG_ROWS, HD), jnp.bfloat16)
+    height = 4 * length + FLAG_ROWS
     return pl.pallas_call(
-        functools.partial(pack_kernel, picks),
-        out_shape=[out] * len(picks),
-        in_specs=[whole(pltpu.SMEM)] * 2 + [whole()] * 4,
-        out_specs=[whole()] * len(picks),
+        functools.partial(pack_kernel, len(picks)),
+        grid_spec=pltpu.PrefetchScalarGridSpec(
+            num_scalar_prefetch=1,
+            grid=(1,),
+            in_specs=[whole(pltpu.SMEM)]
+            + [
+                pl.BlockSpec(
+                    (length, HD),
+                    lambda i, place, pick=pick: (0, pick(place[CORE], place[HERE], place[BESIDE])),
+                )
+                for pick in picks
+                for _ in arrays
+            ],
+            out_specs=[pl.BlockSpec((height, HD), lambda i, place: (0, 0))] * len(picks),
+        ),
+        out_shape=[jax.ShapeDtypeStruct((height, HD), jnp.bfloat16)] * len(picks),
         name="pack_heads",
-    )(place, links, *arrays)
+    )(place, links, *(arrays * len(picks)))
 
 
 def attention_kernel(scaling, both, place_ref, x0, x1, x2, x3, out_ref, kacc, vacc):
@@ -288,7 +298,7 @@
         in_specs=[whole(pltpu.SMEM)] + [whole()] * 4,
         out_specs=whole(),
         scratch_shapes=[pltpu.VMEM((4, length, HD), jnp.float32)] * 2,
-        compiler_params=pltpu.CompilerParams(vmem_limit_bytes=32 * MIB),
+        compiler_params=pltpu.CompilerParams(vmem_limit_bytes=12 * MIB),
         cost_estimate=pl.CostEstimate(
             flops=4 * 5 * 2 * length * 3 * length * HD * 2,
             bytes_accessed=2 * length * 7 * HD * 4,
@@ -312,52 +322,47 @@
         out_shape=jax.ShapeDtypeStruct((3 * cols, rows), jnp.bfloat16),
         in_specs=[whole()] * 3,
         out_specs=whole(),
-        compiler_params=pltpu.CompilerParams(vmem_limit_bytes=16 * MIB),
+        compiler_params=pltpu.CompilerParams(vmem_limit_bytes=8 * MIB),
         name="turn_weights",
     )(*weights)
 
 
 def input_kernel(role, marks, place_ref, *refs):
     count = len(marks)
-    grad_refs, weight_refs, out_refs = refs[:count], refs[count : count + 2], refs[count + 2 : -4]
-    grads, weights, outs, sems = refs[-4:]
+    grad_refs, weight_refs, out_refs = refs[:count], refs[count : count + 2], refs[count + 2 : -3]
+    grads, outs, sems = refs[-3:]
     core, plane = place_ref[CORE], place_ref[PLANE]
-    rows = weights.shape[2]
+    rows = weight_refs[0].shape[1]
     triple = grad_refs[0].shape[2]
     slots = len(out_refs)
     order = list(range(1, slots)) + [0]
 
     @pl.when(core == role)
     def _():
-        fetches = [
-            pltpu.make_async_copy(ref, weights.at[side], sems.at[side])
-            for side, ref in enumerate(weight_refs)
-        ]
         loads = {
             s: [
                 pltpu.make_async_copy(
                     ref.at[jnp.bitwise_xor(plane, s ^ flip)],
-                    grads.at[s, :, lanes((place_ref[base] + step) * triple, triple)],
-                    sems.at[2 + s * count + at],
+                    grads.at[s, place_ref[base] + step],
+                    sems.at[s * count + at],
                 )
                 for at, (ref, (base, step, flip)) in enumerate(zip(grad_refs, marks))
             ]
             for s in order
         }
         stores = [
-            pltpu.make_async_copy(outs.at[s], out, sems.at[2 + slots * count + s])
+            pltpu.make_async_copy(outs.at[s], out, sems.at[slots * count + s])
             for s, out in enumerate(out_refs)
         ]
-        for copy in loads[order[0]] + fetches + [load for s in order[1:] for load in loads[s]]:
-            copy.start()
-        for copy in fetches:
-            copy.wait()
+        for s in order:
+            for load in loads[s]:
+                load.start()
         for s in order:
             for load in loads[s]:
                 load.wait()
-            for side, at in ((0, core), (1, 1 - core)):
-                total = dot(grads[s], weights[side])
-                outs[s, :, lanes(at * rows, rows)] = total.astype(outs.dtype)
+            left = jnp.concatenate([grads[s, head] for head in range(count)], axis=1)
+            for weights, at in zip(weight_refs, (core, 1 - core)):
+                outs[s, :, lanes(at * rows, rows)] = dot(left, weights[...]).astype(outs.dtype)
             stores[s].start()
         for store in stores:
             store.wait()
@@ -371,15 +376,14 @@
     return pl.pallas_call(
         functools.partial(input_kernel, role, [mark for _, mark in grads]),
         out_shape=[out] * blocks,
-        in_specs=[whole(pltpu.SMEM)] + [whole(pltpu.HBM)] * (count + 2),
+        in_specs=[whole(pltpu.SMEM)] + [whole(pltpu.HBM)] * count + [whole()] * 2,
         out_specs=[whole(pltpu.HBM)] * blocks,
         scratch_shapes=[
-            pltpu.VMEM((blocks, length, depth), jnp.bfloat16),
-            pltpu.VMEM((2, depth, rows), jnp.bfloat16),
+            pltpu.VMEM((blocks, count, length, triple), jnp.bfloat16),
             pltpu.VMEM((blocks, length, 2 * rows), jnp.bfloat16),
-            pltpu.SemaphoreType.DMA((2 + blocks * (count + 1),)),
+            pltpu.SemaphoreType.DMA((blocks * (count + 1),)),
         ],
-        compiler_params=pltpu.CompilerParams(vmem_limit_bytes=32 * MIB),
+        compiler_params=pltpu.CompilerParams(vmem_limit_bytes=12 * MIB),
         cost_estimate=pl.CostEstimate(
             flops=2 * blocks * length * 2 * rows * depth,
             bytes_accessed=2 * (blocks * length * (2 * rows + depth) + 2 * rows * depth),
@@ -402,21 +406,18 @@
     core = place_ref[CORE]
     rows = out_refs[0].shape[0]
     blocks, length, triple = grad_refs[0][0].shape
-    start = (core if mine else 1 - core) * rows
+    part = core if mine else 1 - core
     own, mate_in, first, second, corner, corner_far = sources
     chosen = ((own, mate_in, first, second), (first, second, corner, corner_far))
 
     def copies(which):
         return [
-            pltpu.make_async_copy(source.at[:, lanes(start, rows)], tokens.at[e], sems.at[e])
+            pltpu.make_async_copy(source.at[part], tokens.at[e], sems.at[e])
             for e, source in enumerate(chosen[which])
         ] + [
             pltpu.make_async_copy(
                 ref.at[e ^ flip],
-                grads.at[
-                    e * length : (e + 1) * length,
-                    lanes((place_ref[base] + step) * triple, triple),
-                ],
+                grads.at[place_ref[base] + step, e],
                 sems.at[blocks + at * blocks + e],
             )
             for at, (ref, (base, step, flip)) in enumerate(zip(grad_refs[which], marks[which]))
@@ -443,21 +444,22 @@
     for copy in waits[blocks:] + arrivals:
         copy.wait()
     for pair in range(count // 2):
-        total = dot(turned[...], grads[:, pair * 2 * triple : (pair + 1) * 2 * triple])
+        right = [grads[2 * pair + head].reshape(blocks * length, triple) for head in range(2)]
+        total = dot(turned[...], jnp.concatenate(right, axis=1))
         for head in range(2):
             here = slice((2 * pair + head) * HD, (2 * pair + head + 1) * HD)
             for kind, out in enumerate(out_refs):
                 at = (head * 3 + kind) * HD
-                part = total[:, at : at + HD]
+                value = total[:, at : at + HD]
                 if mine:
-                    part = (part + sums[kind, :, here]) * mean_scale
-                out[:, here] = part
+                    value = (value + sums[kind, :, here]) * mean_scale
+                out[:, here] = value
 
 
 def weight_product(place, mine, mean_scale, tokens, grads, received=()):
     blocks, length, triple = grads[0][0][0].shape
     count = len(grads[0])
-    rows = tokens[0].shape[1] // 2
+    rows = tokens[0].shape[2]
     cols = HD * count
     return pl.pallas_call(
         functools.partial(
@@ -469,11 +471,11 @@
         scratch_shapes=[
             pltpu.VMEM((blocks, length, rows), jnp.bfloat16),
             pltpu.VMEM((rows, blocks * length), jnp.bfloat16),
-            pltpu.VMEM((blocks * length, count * triple), jnp.bfloat16),
+            pltpu.VMEM((count, blocks, length, triple), jnp.bfloat16),
         ]
         + ([pltpu.VMEM((3, rows, cols), jnp.float32)] if mine else [])
         + [pltpu.SemaphoreType.DMA((blocks * (count + 1) + 3,))],
-        compiler_params=pltpu.CompilerParams(vmem_limit_bytes=40 * MIB),
+        compiler_params=pltpu.CompilerParams(vmem_limit_bytes=20 * MIB),
         cost_estimate=pl.CostEstimate(
             flops=2 * rows * 3 * cols * blocks * length,
             bytes_accessed=2 * blocks * length * (rows + 3 * cols) + 12 * rows * cols,
@@ -481,6 +483,27 @@
         ),
         name="weight_gradient_own" if mine else "weight_gradient_mate",
     )(place, *tokens, *[array for part in grads for array, _ in part], *received)
+
+
+def choose_kernel(which_ref, first_ref, second_ref, out_ref, sem):
+    for which, ref in enumerate((first_ref, second_ref)):
+
+        @pl.when(which_ref[0] == which)
+        def _():
+            copy = pltpu.make_async_copy(ref, out_ref, sem)
+            copy.start()
+            copy.wait()
+
+
+def chosen_of(which, first, second):
+    return pl.pallas_call(
+        choose_kernel,
+        out_shape=jax.ShapeDtypeStruct(first.shape, first.dtype),
+        in_specs=[whole(pltpu.SMEM)] + [whole(pltpu.HBM)] * 2,
+        out_specs=whole(),
+        scratch_shapes=[pltpu.SemaphoreType.DMA],
+        name="choose_block",
+    )(which, first, second)
 
 
 def gather_body(
@@ -509,22 +532,22 @@
     arrays = tuple(a.reshape(length, cols) for a in (queries, saved_keys, saved_values, output_grad))
 
     ready = []
-    for step in range(0, half, 2):
+    for step in sorted(range(0, half, 2), key=lambda step: step + 1 < half):
         if step + 1 < half:
             picks = (
+                lambda c, here, beside, step=step: beside + step + c,
+                lambda c, here, beside, step=step: beside + step + 1 - c,
                 lambda c, here, beside, step=step: here + step + c,
                 lambda c, here, beside, step=step: here + step + 1 - c,
-                lambda c, here, beside, step=step: beside + step + c,
-                lambda c, here, beside, step=step: beside + step + 1 - c,
             )
-            own, to_mate, to_x, to_cross = pack(picks, place, view_links, arrays)
+            to_x, to_cross, own, to_mate = pack(picks, place, view_links, arrays)
             sources = (own, moved(to_mate, mate), moved(to_x, along_x), moved(to_cross, across_x))
         else:
             picks = (
+                lambda c, here, beside, step=step: beside + step,
                 lambda c, here, beside, step=step: here + step,
-                lambda c, here, beside, step=step: beside + step,
             )
-            own, to_x = pack(picks, place, view_links, arrays)
+            to_x, own = pack(picks, place, view_links, arrays)
             sources = (
                 own,
                 moved(own, only(1, mate)),
@@ -579,31 +602,35 @@
             total += lax.ppermute(slots[s], ("dp", "view", "head"), pairs).astype(jnp.float32)
         return total.astype(jnp.bfloat16)
 
-    def deliver(role, total):
+    def deliver(role, total, *earlier):
+        def spot(y, v, z):
+            return (y * views + v) * groups + z
+
+        corners = [
+            (y, v, z) for y in range(prompts) for v in range(role, views, 2) for z in range(groups)
+        ]
+        pairs = [(spot(y, v, z), spot(y ^ role, v ^ z, z)) for y, v, z in corners]
+        beside = lax.ppermute(total, ("dp", "view", "head"), pairs)
         pairs = [
-            (
-                (y * views + v) * groups + z,
-                ((y ^ role) * views + (v ^ z)) * groups + y * (views // 2) + v // 2,
-            )
-            for y in range(prompts)
-            for v in range(role, views, 2)
-            for z in range(groups)
+            (spot(y ^ role, v ^ z, z), spot(y ^ role, v ^ z, y * (views // 2) + v // 2))
+            for y, v, z in corners
         ]
-        return lax.ppermute(total, ("dp", "view", "head"), pairs)
+        (beside,) = after((beside,), *earlier)
+        return lax.ppermute(beside, ("dp", "view", "head"), pairs)
 
     first_slots = input_product(turn, 0, first, own_weights, mate_weights)
     first_total = exchange(0, first_slots)
     (turn,) = after((place,), first_total)
     second_slots = input_product(turn, 1, second, own_weights, mate_weights)
     second_total = exchange(1, second_slots)
-    landed = (deliver(0, first_total), deliver(1, second_total))
-    from_first = lax.axis_index("head") // (views // 2) == lax.axis_index("dp")
-    input_grad = jnp.where(from_first, landed[0], landed[1])
-
     flat = normed.reshape(length, model_width)
 
     def columns(of_chip):
-        return lax.dynamic_slice_in_dim(flat, of_chip * (2 * rows), 2 * rows, axis=1)
+        parts = [
+            lax.dynamic_slice_in_dim(flat, (2 * of_chip + part) * rows, rows, axis=1)
+            for part in range(2)
+        ]
+        return jnp.stack(parts)
 
     toward_x, toward_y = jnp.bitwise_xor(chip, 1), jnp.bitwise_xor(chip, 2)
     here = columns(chip)
@@ -612,7 +639,7 @@
     to_corner = columns(jnp.bitwise_xor(chip, 3))
     (sent,) = after((here,), ready[0][2][1])
     to_straight, to_crossed, to_corner = after(
-        (to_straight, to_crossed, to_corner), second[2][0], second[3][0]
+        (to_straight, to_crossed, to_corner), *[array for array, _ in second]
     )
     tokens = (
         here,
@@ -625,6 +652,9 @@
     for_mate = weight_product(place, False, mean_scale, tokens, (first, second))
     from_mate = [moved(w, mate) for w in for_mate]
     weight_grads = weight_product(place, True, mean_scale, tokens, (first, second), from_mate)
+    landed = (deliver(0, first_total), deliver(1, second_total, *weight_grads))
+    which = jnp.bitwise_xor(lax.axis_index("head") // (views // 2), lax.axis_index("dp"))
+    input_grad = chosen_of(which.reshape(1).astype(jnp.int32), *landed)
     return (
         input_grad.reshape(1, 1, length, model_width // groups),
         *weight_grads,

time: 176 us -> 199 us (1.13)
  the two profiles are of different devices: /device:TPU:1 before, /device:TPU:6 now
where the time goes in v5:
time: 199 us; the launch traced here: 198 us
  starting transfers between devices  88.5 us (44%)
  Pallas kernels  52.6 us (26%)
  waiting for transfers between devices  51.9 us (26%)
  local copies, waits for them, and re-layouts  2.7 us (1%)
    ppermute x23, starting transfers between devices, moved(): return lax.ppermute(value, ('dp', 'view'), pairs)  38.9 us
    ppermute x23, waiting for transfers between devices, moved(): return lax.ppermute(value, ('dp', 'view'), pairs)  38.3 us
    ppermute x2, starting transfers between devices, deliver(): return lax.ppermute(beside, ('dp', 'view', 'head'), pairs)  34.7 us
    pallas_call x2, Pallas kernels, weight_product(): pl.pallas_call(functools.partial(weight_kernel, mine, mean_scale, [[mark...  19.5 us
    pallas_call x2, Pallas kernels, input_product(): pl.pallas_call(functools.partial(input_kernel, role, [mark for _, mark in...  15.4 us
    ppermute x6, starting transfers between devices, exchange(): lax.ppermute(slots[s], ('dp', 'view', 'head'), pairs).astype(jnp.float32)  12.2 us
    ppermute x2, waiting for transfers between devices, deliver(): return lax.ppermute(beside, ('dp', 'view', 'head'), pairs)  10.3 us
    pallas_call x2, Pallas kernels, attention(): pl.pallas_call(functools.partial(attention_kernel, HD ** (-0.5), both), o...  8.5 us
  transfers between devices with their start and end apart: 33, of which 7 were waited for; matrix products, arithmetic and copies ran while one was open for 0% of the time, Pallas kernels for 24%

profile of v5, /device:TPU:6, one launch (start us, length us, event | category | flops | bytes accessed | tf_op | source)
XLA Modules:
  0.0 198.2 jit_solution(16620356854007877665)
XLA Ops:
  0.7 0.6 pad_add_fusion.place_ref
  1.3 2.7 %pack_heads.2 = (bf16[1040,128]{1,0:T(8,128)(2,1)}, bf16[1040,128]{1,0:T(8,128)(2,1)}) custom-call(s32[4]{0:T(128)} %pad_add_fusion.place_ref, s32[1,2]{1,0:T(1,128)} %links_ref.3, bf16[256,768]{1,0:T(8,128)(2,1)} %bitcast.26, bf16[256,768]{1,0:T(8,128)(2,1)} %bitcast.32, bf16[256,768]{1,0:T(8,128)(2,1)} %bitcast.38, bf16[256,768]{1,0:T(8,128)(2,1)} %bitcast.44, ...), custom_call_target="tpu_custom_call" | custom-call | tf_op jit(solution)/shard_map/pack_heads/pallas_call | solution.py:215
  4.0 1.3 collective-permute-start
  5.3 2.4 %collective-permute-start.1 = (bf16[1040,128]{1,0:T(8,128)(2,1)}, bf16[1040,128]{1,0:T(8,128)(2,1)S(1)}, u32[]{:S(2)}, u32[]{:S(2)}) collective-permute-start(bf16[1040,128]{1,0:T(8,128)(2,1)} %get-tuple-element.40), channel_id=1, source_target_pairs={{0,8},{8,0},{16,24},{24,16},{1,9},{9,1},{17,25},{25,17},{2,10},{10... | collective-permute-start | bytes 798728 | tf_op jit(solution)/shard_map/ppermute | solution.py:128
  7.7 1.3 collective-permute-start.2
  9.0 1.8 turn_weights.1.refs_6_
  10.8 2.2 %collective-permute-start.10 = (bf16[2304,384]{1,0:T(8,128)(2,1)}, bf16[2304,384]{1,0:T(8,128)(2,1)}, u32[]{:S(2)}, u32[]{:S(2)}) collective-permute-start(bf16[2304,384]{1,0:T(8,128)(2,1)} %turn_weights.1.refs_6_), channel_id=1, source_target_pairs={{0,4},{4,0},{8,12},{12,8},{16,20},{20,16},{24,28},{28,24},{1,5},{5... | collective-permute-start | bytes 5308424 | tf_op jit(solution)/shard_map/ppermute | solution.py:128
  13.0 2.9 %pack_heads.3 = (bf16[1040,128]{1,0:T(8,128)(2,1)}, bf16[1040,128]{1,0:T(8,128)(2,1)}, bf16[1040,128]{1,0:T(8,128)(2,1)}, bf16[1040,128]{1,0:T(8,128)(2,1)}) custom-call(s32[4]{0:T(128)} %pad_add_fusion.place_ref, s32[1,2]{1,0:T(1,128)} %links_ref.3, bf16[256,768]{1,0:T(8,128)(2,1)} %bitcast.28, bf16[256,768]{1,0:T(8,128)(2,1)} %bitcast.34, ...), custom_call_target="tpu_custom_call" | custom-call | tf_op jit(solution)/shard_map/pack_heads/pallas_call | solution.py:215
  16.0 0.1 collective-permute-start.3
  16.1 0.5 collective-permute-start.4
  16.7 0.0 collective-permute-done.1.x2
  16.7 1.2 collective-permute-start.5
  17.8 0.0 collective-permute-done.2.x3
  17.8 0.7 copy-done.6
  18.6 1.0 copy-done.7
  19.5 4.3 %attention_gradients.2.refs_0_.refs_6_ = bf16[4,256,384]{2,1,0:T(8,128)(2,1)S(1)} custom-call(s32[4]{0:T(128)S(1)} %copy-done.3, bf16[1040,128]{1,0:T(8,128)(2,1)S(1)} %copy-done.4, bf16[1040,128]{1,0:T(8,128)(2,1)S(1)} %collective-permute-done.x1, bf16[1040,128]{1,0:T(8,128)(2,1)S(1)} %collective-permute-done.1.x2, bf16[1040,128]{1,0:T(8,128)(2,1)S(1)} %copy-done.7), custom_call_target="tpu_custom_call" | custom-call | flops 2013265920 | bytes 1835008 | tf_op jit(solution)/shard_map/attention_gradients/pallas_call | solution.py:295
  23.8 0.0 collective-permute-done.3.x1
  23.8 1.8 collective-permute-done.4.x2
  25.5 4.6 %collective-permute-done.5.x3 = bf16[1040,128]{1,0:T(8,128)(2,1)S(1)} collective-permute-done((bf16[1040,128]{1,0:T(8,128)(2,1)}, bf16[1040,128]{1,0:T(8,128)(2,1)S(1)}, u32[]{:S(2)}, u32[]{:S(2)}) %collective-permute-start.5) | collective-permute-done | bytes 266272 | tf_op jit(solution)/shard_map/ppermute | solution.py:128
  30.1 4.2 %attention_gradients.3.refs_2_.refs_8_ = bf16[4,256,384]{2,1,0:T(8,128)(2,1)S(1)} custom-call(s32[4]{0:T(128)S(1)} %copy-done.3, bf16[1040,128]{1,0:T(8,128)(2,1)S(1)} %copy-done.5, bf16[1040,128]{1,0:T(8,128)(2,1)S(1)} %collective-permute-done.3.x1, bf16[1040,128]{1,0:T(8,128)(2,1)S(1)} %collective-permute-done.4.x2, ...), custom_call_target="tpu_custom_call" | custom-call | flops 2013265920 | bytes 1835008 | tf_op jit(solution)/shard_map/attention_gradients/pallas_call | solution.py:295
  34.4 0.6 collective-permute-start.8
  35.0 1.2 collective-permute-start.9
  36.2 2.4 %collective-permute-start.6 = (bf16[4,256,384]{2,1,0:T(8,128)(2,1)S(1)}, bf16[4,256,384]{2,1,0:T(8,128)(2,1)}, u32[]{:S(2)}, u32[]{:S(2)}) collective-permute-start(bf16[4,256,384]{2,1,0:T(8,128)(2,1)S(1)} %attention_gradients.2.refs_0_.refs_6_), channel_id=1, source_target_pairs={{0,8},{8,0},{16,24},{24,16},{1,9},{9,1},{17,25},{25,17},{2,10},{10... | collective-permute-start | bytes 2359304 | tf_op jit(solution)/shard_map/ppermute | solution.py:128
  38.6 1.3 collective-permute-start.7
  39.9 14.9 %collective-permute-done.8.refs_4_.refs_2_.refs_10_.refs_14_ = bf16[4,256,384]{2,1,0:T(8,128)(2,1)S(1)} collective-permute-done((bf16[4,256,384]{2,1,0:T(8,128)(2,1)S(1)}, bf16[4,256,384]{2,1,0:T(8,128)(2,1)S(1)}, u32[]{:S(2)}, u32[]{:S(2)}) %collective-permute-start.8) | collective-permute-done | bytes 786464 | tf_op jit(solution)/shard_map/ppermute | solution.py:128
  54.8 2.2 %collective-permute-start.16 = (bf16[4,256,384]{2,1,0:T(8,128)(2,1)S(1)}, bf16[4,256,384]{2,1,0:T(8,128)(2,1)}, u32[]{:S(2)}, u32[]{:S(2)}) collective-permute-start(bf16[4,256,384]{2,1,0:T(8,128)(2,1)S(1)} %attention_gradients.2.refs_0_.refs_6_), channel_id=1, source_target_pairs={{0,20},{8,28},{16,4},{24,12},{1,21},{9,29},{17,5},{25,13},{2,22},{... | collective-permute-start | bytes 2359304 | tf_op jit(solution)/shard_map/ppermute | solution.py:128
  57.0 0.0 collective-permute-done.9.refs_5_.refs_3_.refs_11_.refs_15_
  57.0 1.5 collective-permute-start.18
  58.6 8.6 %collective-permute-done.6.refs_1_.refs_7_ = bf16[4,256,384]{2,1,0:T(8,128)(2,1)} collective-permute-done((bf16[4,256,384]{2,1,0:T(8,128)(2,1)S(1)}, bf16[4,256,384]{2,1,0:T(8,128)(2,1)}, u32[]{:S(2)}, u32[]{:S(2)}) %collective-permute-start.6) | collective-permute-done | bytes 786464 | tf_op jit(solution)/shard_map/ppermute | solution.py:128
  67.2 1.3 collective-permute-start.19
  68.5 1.3 collective-permute-start.17
  69.9 0.0 collective-permute-done.10.refs_7_
  69.9 12.9 %input_gradient.2 = (bf16[256,768]{1,0:T(8,128)(2,1)S(1)}, bf16[256,768]{1,0:T(8,128)(2,1)S(1)}, bf16[256,768]{1,0:T(8,128)(2,1)S(1)}, bf16[256,768]{1,0:T(8,128)(2,1)S(1)}) custom-call(s32[4]{0:T(128)S(1)} %copy-done.3, bf16[4,256,384]{2,1,0:T(8,128)(2,1)S(1)} %attention_gradients.2.refs_0_.refs_6_, ...), custom_call_target="tpu_custom_call" | custom-call | flops 3623878656 | bytes 9830400 | tf_op jit(solution)/shard_map/input_gradient/pallas_call | solution.py:376
  82.8 3.5 %collective-permute-start.11 = (bf16[256,768]{1,0:T(8,128)(2,1)S(1)}, bf16[256,768]{1,0:T(8,128)(2,1)S(1)}, u32[]{:S(2)}, u32[]{:S(2)}) collective-permute-start(bf16[256,768]{1,0:T(8,128)(2,1)S(1)} %get-tuple-element.55), channel_id=1, source_target_pairs={{0,1},{1,0},{2,3},{3,2},{8,9},{9,8},{10,11},{11,10},{16,17},{17,16... | collective-permute-start | bytes 1179656 | tf_op jit(solution)/shard_map/ppermute | solution.py:602
  86.3 4.5 %collective-permute-start.12 = (bf16[256,768]{1,0:T(8,128)(2,1)S(1)}, bf16[256,768]{1,0:T(8,128)(2,1)S(1)}, u32[]{:S(2)}, u32[]{:S(2)}) collective-permute-start(bf16[256,768]{1,0:T(8,128)(2,1)S(1)} %get-tuple-element.56), channel_id=1, source_target_pairs={{0,2},{1,3},{2,0},{3,1},{8,10},{9,11},{10,8},{11,9},{16,18},{17,19... | collective-permute-start | bytes 1179656 | tf_op jit(solution)/shard_map/ppermute | solution.py:602
  90.8 0.0 collective-permute-done.18.refs_4_.refs_16_
  90.8 2.1 %collective-permute-start.13 = (bf16[256,768]{1,0:T(8,128)(2,1)S(1)}, bf16[256,768]{1,0:T(8,128)(2,1)S(1)}, u32[]{:S(2)}, u32[]{:S(2)}) collective-permute-start(bf16[256,768]{1,0:T(8,128)(2,1)S(1)} %get-tuple-element.57), channel_id=1, source_target_pairs={{0,3},{1,2},{2,1},{3,0},{8,11},{9,10},{10,9},{11,8},{16,19},{17,18... | collective-permute-start | bytes 1179656 | tf_op jit(solution)/shard_map/ppermute | solution.py:602
  93.0 0.3 dynamic-slice_bitcast_fusion.1
  93.3 0.1 pad_maximum_fusion.1
  93.5 1.3 collective-permute-start.24
  94.8 0.0 collective-permute-done.17.refs_1_.refs_13_
  94.8 0.7 collective-permute-start.27
  95.5 6.5 %collective-permute-start.28 = (bf16[2,256,384]{2,1,0:T(8,128)(2,1)S(1)}, bf16[2,256,384]{2,1,0:T(8,128)(2,1)S(1)}, u32[]{:S(2)}, u32[]{:S(2)}) collective-permute-start(bf16[2,256,384]{2,1,0:T(8,128)(2,1)S(1)} %pad_maximum_fusion.3), channel_id=1, source_target_pairs={{0,28},{8,20},{16,12},{24,4},{1,29},{9,21},{17,13},{25,5},{2,30},{... | collective-permute-start | bytes 1179656 | tf_op jit(solution)/shard_map/ppermute | solution.py:128
  102.0 3.3 %collective-permute-done.12 = bf16[256,768]{1,0:T(8,128)(2,1)S(1)} collective-permute-done((bf16[256,768]{1,0:T(8,128)(2,1)S(1)}, bf16[256,768]{1,0:T(8,128)(2,1)S(1)}, u32[]{:S(2)}, u32[]{:S(2)}) %collective-permute-start.12) | collective-permute-done | bytes 393248 | tf_op jit(solution)/shard_map/ppermute | solution.py:602
  105.3 0.6 collective-permute-start.25
  105.9 0.2 add_convert_fusion.1
  106.1 2.5 %input_gradient.3 = (bf16[256,768]{1,0:T(8,128)(2,1)S(1)}, bf16[256,768]{1,0:T(8,128)(2,1)S(1)}, bf16[256,768]{1,0:T(8,128)(2,1)S(1)}, bf16[256,768]{1,0:T(8,128)(2,1)S(1)}) custom-call(s32[4]{0:T(128)S(1)} %copy-done.3, bf16[4,256,384]{2,1,0:T(8,128)(2,1)} %collective-permute-done.16.refs_0_.refs_12_, ...), custom_call_target="tpu_custom_call" | custom-call | flops 3623878656 | bytes 9830400 | tf_op jit(solution)/shard_map/input_gradient/pallas_call | solution.py:376
  108.6 0.7 collective-permute-start.20
  109.3 8.4 %collective-permute-done.25.refs_2_ = bf16[2,256,384]{2,1,0:T(8,128)(2,1)S(1)} collective-permute-done((bf16[2,256,384]{2,1,0:T(8,128)(2,1)S(1)}, bf16[2,256,384]{2,1,0:T(8,128)(2,1)S(1)}, u32[]{:S(2)}, u32[]{:S(2)}) %collective-permute-start.25) | collective-permute-done | bytes 393248 | tf_op jit(solution)/shard_map/ppermute | solution.py:128
  117.7 8.4 %weight_gradient_mate.1 = (f32[384,768]{1,0:T(8,128)S(1)}, f32[384,768]{1,0:T(8,128)S(1)}, f32[384,768]{1,0:T(8,128)S(1)}) custom-call(s32[4]{0:T(128)S(1)} %copy-done.3, bf16[2,256,384]{2,1,0:T(8,128)(2,1)S(1)} %pad_maximum_fusion.refs_0_, bf16[2,256,384]{2,1,0:T(8,128)(2,1)S(1)} %collective-permute-done.24.refs_1_, ...), custom_call_target="tpu_custom_call" | custom-call | flops 1811939328 | bytes 9043968 | tf_op jit(solution)/shard_map/weight_gradient_mate/pallas_call | solution.py:464
  126.1 8.2 %collective-permute-start.29 = (f32[384,768]{1,0:T(8,128)S(1)}, f32[384,768]{1,0:T(8,128)S(1)}, u32[]{:S(2)}, u32[]{:S(2)}) collective-permute-start(f32[384,768]{1,0:T(8,128)S(1)} %get-tuple-element.67), channel_id=1, source_target_pairs={{0,4},{4,0},{8,12},{12,8},{16,20},{20,16},{24,28},{28,24},{1,5},{5... | collective-permute-start | bytes 3538952 | tf_op jit(solution)/shard_map/ppermute | solution.py:128
  134.3 0.1 collective-permute-start.30
  134.4 0.4 collective-permute-start.31
  134.8 0.7 collective-permute-start.21
  135.5 0.7 collective-permute-start.22
  136.2 1.4 collective-permute-start.14
  137.7 0.2 add_convert_fusion
  137.9 1.4 collective-permute-start.23
  139.3 33.4 %collective-permute-start.15 = (bf16[256,768]{1,0:T(8,128)(2,1)}, bf16[256,768]{1,0:T(8,128)(2,1)S(1)}, u32[]{:S(2)}, u32[]{:S(2)}) collective-permute-start(bf16[256,768]{1,0:T(8,128)(2,1)} %collective-permute-done.14), channel_id=1, source_target_pairs={{0,0},{5,4},{10,8},{15,12},{8,9},{13,13},{2,1},{7,5},{16,18},{21,2... | collective-permute-start | bytes 1179656 | tf_op jit(solution)/shard_map/ppermute | solution.py:619
  172.7 11.2 %weight_gradient_own.1 = (f32[384,768]{1,0:T(8,128)}, f32[384,768]{1,0:T(8,128)}, f32[384,768]{1,0:T(8,128)}) custom-call(s32[4]{0:T(128)S(1)} %copy-done.3, bf16[2,256,384]{2,1,0:T(8,128)(2,1)S(1)} %pad_maximum_fusion.refs_0_, bf16[2,256,384]{2,1,0:T(8,128)(2,1)S(1)} %collective-permute-done.24.refs_1_, ...), custom_call_target="tpu_custom_call" | custom-call | flops 1811939328 | bytes 9043968 | tf_op jit(solution)/shard_map/weight_gradient_own/pallas_call | solution.py:464
  183.9 1.3 collective-permute-start.32
  185.2 10.3 %collective-permute-done.32.second_ref = bf16[256,768]{1,0:T(8,128)(2,1)S(1)} collective-permute-done((bf16[256,768]{1,0:T(8,128)(2,1)}, bf16[256,768]{1,0:T(8,128)(2,1)S(1)}, u32[]{:S(2)}, u32[]{:S(2)}) %collective-permute-start.32) | collective-permute-done | bytes 393248 | tf_op jit(solution)/shard_map/ppermute | solution.py:619
  195.6 0.7 copy-done.10
  196.3 1.7 choose_block.1
  (41 shorter events, 0.2 us)
Async XLA Ops:
  1.3 7.7 %copy-start = (bf16[384,768]{1,0:T(8,128)(2,1)S(1)}, bf16[384,768]{1,0:T(8,128)(2,1)}, u32[]{:S(2)}) copy-start(bf16[384,768]{1,0:T(8,128)(2,1)} %q_ref) | copy-start | bytes 1769476
  1.3 7.7 %copy-start.1 = (bf16[384,768]{1,0:T(8,128)(2,1)S(1)}, bf16[384,768]{1,0:T(8,128)(2,1)}, u32[]{:S(2)}) copy-start(bf16[384,768]{1,0:T(8,128)(2,1)} %k_ref) | copy-start | bytes 1769476
  1.3 7.8 %copy-start.2 = (bf16[384,768]{1,0:T(8,128)(2,1)S(1)}, bf16[384,768]{1,0:T(8,128)(2,1)}, u32[]{:S(2)}) copy-start(bf16[384,768]{1,0:T(8,128)(2,1)} %v_ref) | copy-start | bytes 1769476
  4.0 12.1 %collective-permute-start = (bf16[1040,128]{1,0:T(8,128)(2,1)}, bf16[1040,128]{1,0:T(8,128)(2,1)S(1)}, u32[]{:S(2)}, u32[]{:S(2)}) collective-permute-start(bf16[1040,128]{1,0:T(8,128)(2,1)} %get-tuple-element.39.x0), channel_id=1, source_target_pairs={{4,0},{12,8},{20,16},{28,24},{5,1},{13,9},{21,17},{29,25},{6,2},{1... | collective-permute-start | bytes 798728 | tf_op jit(solution)/shard_map/ppermute | solution.py:128
  5.3 11.4 %collective-permute-start.1 = (bf16[1040,128]{1,0:T(8,128)(2,1)}, bf16[1040,128]{1,0:T(8,128)(2,1)S(1)}, u32[]{:S(2)}, u32[]{:S(2)}) collective-permute-start(bf16[1040,128]{1,0:T(8,128)(2,1)} %get-tuple-element.40), channel_id=1, source_target_pairs={{0,8},{8,0},{16,24},{24,16},{1,9},{9,1},{17,25},{25,17},{2,10},{10... | collective-permute-start | bytes 798728 | tf_op jit(solution)/shard_map/ppermute | solution.py:128
  7.7 10.1 %collective-permute-start.2 = (bf16[1040,128]{1,0:T(8,128)(2,1)}, bf16[1040,128]{1,0:T(8,128)(2,1)S(1)}, u32[]{:S(2)}, u32[]{:S(2)}) collective-permute-start(bf16[1040,128]{1,0:T(8,128)(2,1)} %get-tuple-element.40), channel_id=1, source_target_pairs={{4,8},{12,0},{20,24},{28,16},{5,9},{13,1},{21,25},{29,17},{6,10},{... | collective-permute-start | bytes 798728 | tf_op jit(solution)/shard_map/ppermute | solution.py:128
  10.8 7.8 %copy-start.3 = (s32[4]{0:T(128)S(1)}, s32[4]{0:T(128)}, u32[]{:S(2)}) copy-start(s32[4]{0:T(128)} %pad_add_fusion.place_ref) | copy-start | bytes 52
  10.8 7.8 %copy-start.4 = (bf16[1040,128]{1,0:T(8,128)(2,1)S(1)}, bf16[1040,128]{1,0:T(8,128)(2,1)}, u32[]{:S(2)}) copy-start(bf16[1040,128]{1,0:T(8,128)(2,1)} %get-tuple-element.39.x0) | copy-start | bytes 798724
  10.8 59.1 %collective-permute-start.10 = (bf16[2304,384]{1,0:T(8,128)(2,1)}, bf16[2304,384]{1,0:T(8,128)(2,1)}, u32[]{:S(2)}, u32[]{:S(2)}) collective-permute-start(bf16[2304,384]{1,0:T(8,128)(2,1)} %turn_weights.1.refs_6_), channel_id=1, source_target_pairs={{0,4},{4,0},{8,12},{12,8},{16,20},{20,16},{24,28},{28,24},{1,5},{5... | collective-permute-start | bytes 5308424 | tf_op jit(solution)/shard_map/ppermute | solution.py:128
  16.0 7.8 %collective-permute-start.3 = (bf16[1040,128]{1,0:T(8,128)(2,1)}, bf16[1040,128]{1,0:T(8,128)(2,1)S(1)}, u32[]{:S(2)}, u32[]{:S(2)}) collective-permute-start(bf16[1040,128]{1,0:T(8,128)(2,1)} %get-tuple-element.47), channel_id=1, source_target_pairs={{0,4},{4,0},{8,12},{12,8},{16,20},{20,16},{24,28},{28,24},{1,5},{5... | collective-permute-start | bytes 798728 | tf_op jit(solution)/shard_map/ppermute | solution.py:128
  16.1 9.4 %collective-permute-start.4 = (bf16[1040,128]{1,0:T(8,128)(2,1)}, bf16[1040,128]{1,0:T(8,128)(2,1)S(1)}, u32[]{:S(2)}, u32[]{:S(2)}) collective-permute-start(bf16[1040,128]{1,0:T(8,128)(2,1)} %get-tuple-element.48), channel_id=1, source_target_pairs={{0,8},{4,12},{8,0},{12,4},{16,24},{20,28},{24,16},{28,20},{1,9},{5... | collective-permute-start | bytes 798728 | tf_op jit(solution)/shard_map/ppermute | solution.py:128
  16.7 13.5 %copy-start.5 = (bf16[1040,128]{1,0:T(8,128)(2,1)S(1)}, bf16[1040,128]{1,0:T(8,128)(2,1)}, u32[]{:S(2)}) copy-start(bf16[1040,128]{1,0:T(8,128)(2,1)} %get-tuple-element.46.x0) | copy-start | bytes 798724
  16.7 13.5 %collective-permute-start.5 = (bf16[1040,128]{1,0:T(8,128)(2,1)}, bf16[1040,128]{1,0:T(8,128)(2,1)S(1)}, u32[]{:S(2)}, u32[]{:S(2)}) collective-permute-start(bf16[1040,128]{1,0:T(8,128)(2,1)} %get-tuple-element.49), channel_id=1, source_target_pairs={{0,12},{4,8},{8,4},{12,0},{16,28},{20,24},{24,20},{28,16},{1,13},{... | collective-permute-start | bytes 798728 | tf_op jit(solution)/shard_map/ppermute | solution.py:128
  17.8 0.7 copy-start.6
  18.6 1.0 copy-start.7
  34.4 20.4 %collective-permute-start.8 = (bf16[4,256,384]{2,1,0:T(8,128)(2,1)S(1)}, bf16[4,256,384]{2,1,0:T(8,128)(2,1)S(1)}, u32[]{:S(2)}, u32[]{:S(2)}) collective-permute-start(bf16[4,256,384]{2,1,0:T(8,128)(2,1)S(1)} %attention_gradients.3.refs_2_.refs_8_), channel_id=1, source_target_pairs={{0,8},{4,20},{8,0},{12,28},{16,24},{20,4},{24,16},{28,12},{1,9},{5... | collective-permute-start | bytes 2359304 | tf_op jit(solution)/shard_map/ppermute | solution.py:128
  35.0 22.0 %collective-permute-start.9 = (bf16[4,256,384]{2,1,0:T(8,128)(2,1)S(1)}, bf16[4,256,384]{2,1,0:T(8,128)(2,1)S(1)}, u32[]{:S(2)}, u32[]{:S(2)}) collective-permute-start(bf16[4,256,384]{2,1,0:T(8,128)(2,1)S(1)} %attention_gradients.3.refs_2_.refs_8_), channel_id=1, source_target_pairs={{0,20},{4,8},{8,28},{12,0},{16,4},{20,24},{24,12},{28,16},{1,21},{... | collective-permute-start | bytes 2359304 | tf_op jit(solution)/shard_map/ppermute | solution.py:128
  36.2 31.0 %collective-permute-start.6 = (bf16[4,256,384]{2,1,0:T(8,128)(2,1)S(1)}, bf16[4,256,384]{2,1,0:T(8,128)(2,1)}, u32[]{:S(2)}, u32[]{:S(2)}) collective-permute-start(bf16[4,256,384]{2,1,0:T(8,128)(2,1)S(1)} %attention_gradients.2.refs_0_.refs_6_), channel_id=1, source_target_pairs={{0,8},{8,0},{16,24},{24,16},{1,9},{9,1},{17,25},{25,17},{2,10},{10... | collective-permute-start | bytes 2359304 | tf_op jit(solution)/shard_map/ppermute | solution.py:128
  38.6 29.9 %collective-permute-start.7 = (bf16[4,256,384]{2,1,0:T(8,128)(2,1)S(1)}, bf16[4,256,384]{2,1,0:T(8,128)(2,1)}, u32[]{:S(2)}, u32[]{:S(2)}) collective-permute-start(bf16[4,256,384]{2,1,0:T(8,128)(2,1)S(1)} %attention_gradients.3.refs_2_.refs_8_), channel_id=1, source_target_pairs={{4,0},{12,8},{20,16},{28,24},{5,1},{13,9},{21,17},{29,25},{6,2},{1... | collective-permute-start | bytes 2359304 | tf_op jit(solution)/shard_map/ppermute | solution.py:128
  54.8 31.5 %collective-permute-start.16 = (bf16[4,256,384]{2,1,0:T(8,128)(2,1)S(1)}, bf16[4,256,384]{2,1,0:T(8,128)(2,1)}, u32[]{:S(2)}, u32[]{:S(2)}) collective-permute-start(bf16[4,256,384]{2,1,0:T(8,128)(2,1)S(1)} %attention_gradients.2.refs_0_.refs_6_), channel_id=1, source_target_pairs={{0,20},{8,28},{16,4},{24,12},{1,21},{9,29},{17,5},{25,13},{2,22},{... | collective-permute-start | bytes 2359304 | tf_op jit(solution)/shard_map/ppermute | solution.py:128
  57.0 33.8 %collective-permute-start.18 = (bf16[4,256,384]{2,1,0:T(8,128)(2,1)S(1)}, bf16[4,256,384]{2,1,0:T(8,128)(2,1)}, u32[]{:S(2)}, u32[]{:S(2)}) collective-permute-start(bf16[4,256,384]{2,1,0:T(8,128)(2,1)S(1)} %collective-permute-done.8.refs_4_.refs_2_.refs_10_.refs_14_), channel_id=1, source_target_pairs={{4,12},{12,4},{20,28},{28,20},{5,13},{13,5},{21,29},{29,21},{6,14}... | collective-permute-start | bytes 2359304 | tf_op jit(solution)/shard_map/ppermute | solution.py:128
  58.6 34.4 %copy-start.8 = (bf16[1,1,256,3072]{3,2,1,0:T(8,128)(2,1)S(1)}, bf16[1,1,256,3072]{3,2,1,0:T(8,128)(2,1)}, u32[]{:S(2)}) copy-start(bf16[1,1,256,3072]{3,2,1,0:T(8,128)(2,1)} %param.9) | copy-start | bytes 4718596
  67.2 26.3 %collective-permute-start.19 = (bf16[4,256,384]{2,1,0:T(8,128)(2,1)S(1)}, bf16[4,256,384]{2,1,0:T(8,128)(2,1)S(1)}, u32[]{:S(2)}, u32[]{:S(2)}) collective-permute-start(bf16[4,256,384]{2,1,0:T(8,128)(2,1)S(1)} %collective-permute-done.8.refs_4_.refs_2_.refs_10_.refs_14_), channel_id=1, source_target_pairs={{0,20},{8,28},{16,4},{24,12},{1,21},{9,29},{17,5},{25,13},{2,22},{... | collective-permute-start | bytes 2359304 | tf_op jit(solution)/shard_map/ppermute | solution.py:128
  68.5 26.3 %collective-permute-start.17 = (bf16[4,256,384]{2,1,0:T(8,128)(2,1)}, bf16[4,256,384]{2,1,0:T(8,128)(2,1)S(1)}, u32[]{:S(2)}, u32[]{:S(2)}) collective-permute-start(bf16[4,256,384]{2,1,0:T(8,128)(2,1)} %collective-permute-done.6.refs_1_.refs_7_), channel_id=1, source_target_pairs={{0,20},{8,28},{16,4},{24,12},{1,21},{9,29},{17,5},{25,13},{2,22},{... | collective-permute-start | bytes 2359304 | tf_op jit(solution)/shard_map/ppermute | solution.py:128
  82.8 12.7 %collective-permute-start.11 = (bf16[256,768]{1,0:T(8,128)(2,1)S(1)}, bf16[256,768]{1,0:T(8,128)(2,1)S(1)}, u32[]{:S(2)}, u32[]{:S(2)}) collective-permute-start(bf16[256,768]{1,0:T(8,128)(2,1)S(1)} %get-tuple-element.55), channel_id=1, source_target_pairs={{0,1},{1,0},{2,3},{3,2},{8,9},{9,8},{10,11},{11,10},{16,17},{17,16... | collective-permute-start | bytes 1179656 | tf_op jit(solution)/shard_map/ppermute | solution.py:602
  86.3 19.0 %collective-permute-start.12 = (bf16[256,768]{1,0:T(8,128)(2,1)S(1)}, bf16[256,768]{1,0:T(8,128)(2,1)S(1)}, u32[]{:S(2)}, u32[]{:S(2)}) collective-permute-start(bf16[256,768]{1,0:T(8,128)(2,1)S(1)} %get-tuple-element.56), channel_id=1, source_target_pairs={{0,2},{1,3},{2,0},{3,1},{8,10},{9,11},{10,8},{11,9},{16,18},{17,19... | collective-permute-start | bytes 1179656 | tf_op jit(solution)/shard_map/ppermute | solution.py:602
  90.8 15.1 %collective-permute-start.13 = (bf16[256,768]{1,0:T(8,128)(2,1)S(1)}, bf16[256,768]{1,0:T(8,128)(2,1)S(1)}, u32[]{:S(2)}, u32[]{:S(2)}) collective-permute-start(bf16[256,768]{1,0:T(8,128)(2,1)S(1)} %get-tuple-element.57), channel_id=1, source_target_pairs={{0,3},{1,2},{2,1},{3,0},{8,11},{9,10},{10,9},{11,8},{16,19},{17,18... | collective-permute-start | bytes 1179656 | tf_op jit(solution)/shard_map/ppermute | solution.py:602
  93.5 15.2 %collective-permute-start.24 = (bf16[2,256,384]{2,1,0:T(8,128)(2,1)S(1)}, bf16[2,256,384]{2,1,0:T(8,128)(2,1)S(1)}, u32[]{:S(2)}, u32[]{:S(2)}) collective-permute-start(bf16[2,256,384]{2,1,0:T(8,128)(2,1)S(1)} %pad_maximum_fusion.refs_0_), channel_id=1, source_target_pairs={{4,0},{12,8},{20,16},{28,24},{5,1},{13,9},{21,17},{29,25},{6,2},{1... | collective-permute-start | bytes 1179656 | tf_op jit(solution)/shard_map/ppermute | solution.py:128
  94.8 22.9 %collective-permute-start.27 = (bf16[2,256,384]{2,1,0:T(8,128)(2,1)S(1)}, bf16[2,256,384]{2,1,0:T(8,128)(2,1)S(1)}, u32[]{:S(2)}, u32[]{:S(2)}) collective-permute-start(bf16[2,256,384]{2,1,0:T(8,128)(2,1)S(1)} %pad_maximum_fusion.3), channel_id=1, source_target_pairs={{4,28},{12,20},{20,12},{28,4},{5,29},{13,21},{21,13},{29,5},{6,30}... | collective-permute-start | bytes 1179656 | tf_op jit(solution)/shard_map/ppermute | solution.py:128
  95.5 22.2 %collective-permute-start.28 = (bf16[2,256,384]{2,1,0:T(8,128)(2,1)S(1)}, bf16[2,256,384]{2,1,0:T(8,128)(2,1)S(1)}, u32[]{:S(2)}, u32[]{:S(2)}) collective-permute-start(bf16[2,256,384]{2,1,0:T(8,128)(2,1)S(1)} %pad_maximum_fusion.3), channel_id=1, source_target_pairs={{0,28},{8,20},{16,12},{24,4},{1,29},{9,21},{17,13},{25,5},{2,30},{... | collective-permute-start | bytes 1179656 | tf_op jit(solution)/shard_map/ppermute | solution.py:128
  105.3 12.4 %collective-permute-start.25 = (bf16[2,256,384]{2,1,0:T(8,128)(2,1)S(1)}, bf16[2,256,384]{2,1,0:T(8,128)(2,1)S(1)}, u32[]{:S(2)}, u32[]{:S(2)}) collective-permute-start(bf16[2,256,384]{2,1,0:T(8,128)(2,1)S(1)} %get-tuple-element.64), channel_id=1, source_target_pairs={{0,8},{4,20},{8,0},{12,28},{16,24},{20,4},{24,16},{28,12},{1,9},{5... | collective-permute-start | bytes 1179656 | tf_op jit(solution)/shard_map/ppermute | solution.py:128
  105.9 11.8 %collective-permute-start.26 = (bf16[2,256,384]{2,1,0:T(8,128)(2,1)S(1)}, bf16[2,256,384]{2,1,0:T(8,128)(2,1)S(1)}, u32[]{:S(2)}, u32[]{:S(2)}) collective-permute-start(bf16[2,256,384]{2,1,0:T(8,128)(2,1)S(1)} %get-tuple-element.65), channel_id=1, source_target_pairs={{0,20},{4,8},{8,28},{12,0},{16,4},{20,24},{24,12},{28,16},{1,21},{... | collective-permute-start | bytes 1179656 | tf_op jit(solution)/shard_map/ppermute | solution.py:128
  108.6 26.9 %collective-permute-start.20 = (bf16[256,768]{1,0:T(8,128)(2,1)S(1)}, bf16[256,768]{1,0:T(8,128)(2,1)S(1)}, u32[]{:S(2)}, u32[]{:S(2)}) collective-permute-start(bf16[256,768]{1,0:T(8,128)(2,1)S(1)} %get-tuple-element.60), channel_id=1, source_target_pairs={{4,5},{5,4},{6,7},{7,6},{12,13},{13,12},{14,15},{15,14},{20,21},{2... | collective-permute-start | bytes 1179656 | tf_op jit(solution)/shard_map/ppermute | solution.py:602
  126.1 46.6 %collective-permute-start.29 = (f32[384,768]{1,0:T(8,128)S(1)}, f32[384,768]{1,0:T(8,128)S(1)}, u32[]{:S(2)}, u32[]{:S(2)}) collective-permute-start(f32[384,768]{1,0:T(8,128)S(1)} %get-tuple-element.67), channel_id=1, source_target_pairs={{0,4},{4,0},{8,12},{12,8},{16,20},{20,16},{24,28},{28,24},{1,5},{5... | collective-permute-start | bytes 3538952 | tf_op jit(solution)/shard_map/ppermute | solution.py:128
  134.3 38.3 %collective-permute-start.30 = (f32[384,768]{1,0:T(8,128)S(1)}, f32[384,768]{1,0:T(8,128)S(1)}, u32[]{:S(2)}, u32[]{:S(2)}) collective-permute-start(f32[384,768]{1,0:T(8,128)S(1)} %get-tuple-element.68), channel_id=1, source_target_pairs={{0,4},{4,0},{8,12},{12,8},{16,20},{20,16},{24,28},{28,24},{1,5},{5... | collective-permute-start | bytes 3538952 | tf_op jit(solution)/shard_map/ppermute | solution.py:128
  134.4 38.3 %collective-permute-start.31 = (f32[384,768]{1,0:T(8,128)S(1)}, f32[384,768]{1,0:T(8,128)S(1)}, u32[]{:S(2)}, u32[]{:S(2)}) collective-permute-start(f32[384,768]{1,0:T(8,128)S(1)} %get-tuple-element.69), channel_id=1, source_target_pairs={{0,4},{4,0},{8,12},{12,8},{16,20},{20,16},{24,28},{28,24},{1,5},{5... | collective-permute-start | bytes 3538952 | tf_op jit(solution)/shard_map/ppermute | solution.py:128
  134.8 1.4 collective-permute-start.21
  135.5 2.1 %collective-permute-start.22 = (bf16[256,768]{1,0:T(8,128)(2,1)S(1)}, bf16[256,768]{1,0:T(8,128)(2,1)S(1)}, u32[]{:S(2)}, u32[]{:S(2)}) collective-permute-start(bf16[256,768]{1,0:T(8,128)(2,1)S(1)} %get-tuple-element.62), channel_id=1, source_target_pairs={{4,7},{5,6},{6,5},{7,4},{12,15},{13,14},{14,13},{15,12},{20,23},{2... | collective-permute-start | bytes 1179656 | tf_op jit(solution)/shard_map/ppermute | solution.py:602
  136.2 3.0 %collective-permute-start.14 = (bf16[256,768]{1,0:T(8,128)(2,1)S(1)}, bf16[256,768]{1,0:T(8,128)(2,1)}, u32[]{:S(2)}, u32[]{:S(2)}) collective-permute-start(bf16[256,768]{1,0:T(8,128)(2,1)S(1)} %add_convert_fusion.1), channel_id=1, source_target_pairs={{0,0},{1,5},{2,10},{3,15},{8,8},{9,13},{10,2},{11,7},{16,16},{17,2... | collective-permute-start | bytes 1179656 | tf_op jit(solution)/shard_map/ppermute | solution.py:613
  137.9 46.0 %collective-permute-start.23 = (bf16[256,768]{1,0:T(8,128)(2,1)S(1)}, bf16[256,768]{1,0:T(8,128)(2,1)}, u32[]{:S(2)}, u32[]{:S(2)}) collective-permute-start(bf16[256,768]{1,0:T(8,128)(2,1)S(1)} %add_convert_fusion), channel_id=1, source_target_pairs={{4,20},{5,17},{6,30},{7,27},{12,28},{13,25},{14,22},{15,19},{20,4}... | collective-permute-start | bytes 1179656 | tf_op jit(solution)/shard_map/ppermute | solution.py:613
  139.3 45.9 %collective-permute-start.15 = (bf16[256,768]{1,0:T(8,128)(2,1)}, bf16[256,768]{1,0:T(8,128)(2,1)S(1)}, u32[]{:S(2)}, u32[]{:S(2)}) collective-permute-start(bf16[256,768]{1,0:T(8,128)(2,1)} %collective-permute-done.14), channel_id=1, source_target_pairs={{0,0},{5,4},{10,8},{15,12},{8,9},{13,13},{2,1},{7,5},{16,18},{21,2... | collective-permute-start | bytes 1179656 | tf_op jit(solution)/shard_map/ppermute | solution.py:619
  183.9 11.7 %collective-permute-start.32 = (bf16[256,768]{1,0:T(8,128)(2,1)}, bf16[256,768]{1,0:T(8,128)(2,1)S(1)}, u32[]{:S(2)}, u32[]{:S(2)}) collective-permute-start(bf16[256,768]{1,0:T(8,128)(2,1)} %collective-permute-done.23), channel_id=1, source_target_pairs={{20,20},{17,16},{30,28},{27,24},{28,29},{25,25},{22,21},{19,17},{4... | collective-permute-start | bytes 1179656 | tf_op jit(solution)/shard_map/ppermute | solution.py:619
  185.2 10.4 %copy-start.9 = (bf16[256,768]{1,0:T(8,128)(2,1)}, bf16[256,768]{1,0:T(8,128)(2,1)S(1)}, u32[]{:S(2)}) copy-start(bf16[256,768]{1,0:T(8,128)(2,1)S(1)} %collective-permute-done.15.first_ref) | copy-start | bytes 1179652
  195.5 0.7 copy-start.10

commit v6 on v0

--- a/solution.py
+++ b/solution.py
@@ -1,9 +1,15 @@
+import functools
+
 import jax
 import jax.numpy as jnp
 from jax import lax
+from jax.experimental import pallas as pl
+from jax.experimental.pallas import tpu as pltpu
 from jax.sharding import PartitionSpec as P
 
 HD = 128
+LOG2E = 1.4426950408889634
+MIB = 1024 * 1024
 
 
 def shifted(value, axis, steps):
@@ -48,7 +54,7 @@
     return (query_grad, jnp.concatenate([key_grad, value_grad], axis=-1))
 
 
-def body(
+def halo_body(
     normed,
     queries,
     saved_keys,
@@ -111,7 +117,512 @@
     return (input_grad, grad_query, grad_key, grad_value)
 
 
+def moved(value, target):
+    prompts, views = lax.axis_size("dp"), lax.axis_size("view")
+    pairs = []
+    for y in range(prompts):
+        for v in range(views):
+            goal = target(y, v)
+            if goal is not None:
+                pairs.append((y * views + v, goal[0] * views + goal[1]))
+    return lax.ppermute(value, ("dp", "view"), pairs)
+
+
+def mate(y, v):
+    return (y, v ^ 1)
+
+
+def along_x(y, v):
+    return (y, v ^ 2)
+
+
+def across_x(y, v):
+    return (y, v ^ 3)
+
+
+def only(core, target):
+    return lambda y, v: target(y, v) if v % 2 == core else None
+
+
+def along_y(y, v):
+    return (y ^ 1, v)
+
+
+def across_y(y, v):
+    return (y ^ 1, v ^ 1)
+
+
+def straight(y, v):
+    return along_x(y, v) if v % 2 == 0 else along_y(y, v)
+
+
+def crossed(y, v):
+    return across_y(y, v) if v % 2 == 0 else across_x(y, v)
+
+
+def corner_same(y, v):
+    return None if v % 2 == 0 else (y ^ 1, v ^ 2)
+
+
+def corner_cross(y, v):
+    return (y ^ 1, v ^ 3) if v % 2 == 0 else None
+
+
+def lanes(start, size):
+    return pl.ds(pl.multiple_of(start, HD), size)
+
+
+def whole(space=pltpu.VMEM):
+    return pl.BlockSpec(memory_space=space)
+
+
+def dot_last(a, b):
+    return lax.dot_general(a, b, (((1,), (1,)), ((), ())), preferred_element_type=jnp.float32)
+
+
+def dot_first(a, b):
+    return lax.dot_general(a, b, (((0,), (0,)), ((), ())), preferred_element_type=jnp.float32)
+
+
+def dot(a, b):
+    return jnp.dot(a, b, preferred_element_type=jnp.float32)
+
+
+def after(values, *earlier):
+    return lax.optimization_barrier((tuple(values), tuple(earlier)))[0]
+
+
+CORE, PLANE, HERE, BESIDE = range(4)
+FLAG_ROWS = 16
+
+
+def pack_kernel(picks, place_ref, links_ref, q_ref, k_ref, v_ref, g_ref, *out_refs):
+    length = q_ref.shape[0]
+    row = lax.broadcasted_iota(jnp.int32, (FLAG_ROWS, HD), 0)
+    gaps = [jnp.where(links_ref[0, side] >= 0, 0.0, 1.0).astype(jnp.float32) for side in range(2)]
+    flags = jnp.where(row < FLAG_ROWS // 2, gaps[0], gaps[1])
+    for heads, out_ref in zip(picks, out_refs):
+        for at, (base, step, sign) in enumerate(heads):
+            head = place_ref[base] + step + sign * place_ref[CORE]
+            for kind, source in enumerate((q_ref, k_ref, v_ref, g_ref)):
+                out_ref[at, kind * length : (kind + 1) * length] = source[:, lanes(head * HD, HD)]
+            out_ref[at, 4 * length : 4 * length + FLAG_ROWS] = flags.astype(out_ref.dtype)
+
+
+def pack(picks, place, links, arrays):
+    length = arrays[0].shape[0]
+    height = 4 * length + FLAG_ROWS
+    return pl.pallas_call(
+        functools.partial(pack_kernel, picks),
+        out_shape=[
+            jax.ShapeDtypeStruct((len(heads), height, HD), jnp.bfloat16) for heads in picks
+        ],
+        in_specs=[whole(pltpu.SMEM)] * 2 + [whole()] * 4,
+        out_specs=[whole()] * len(picks),
+        compiler_params=pltpu.CompilerParams(vmem_limit_bytes=12 * MIB),
+        name="pack_heads",
+    )(place, links, *arrays)
+
+
+def one_head(scaling, core, xs, length, keys, values, key_sums, value_sums):
+    factor = scaling * LOG2E
+
+    def rows(e, kind):
+        return xs[e][kind * length : (kind + 1) * length]
+
+    def gap(e, side):
+        at = 4 * length + side * (FLAG_ROWS // 2)
+        flags = xs[e][at : at + FLAG_ROWS // 2].astype(jnp.float32)[0:1]
+        return jnp.concatenate([flags] * (length // HD), axis=1) * 1e30
+
+    for at in range(6):
+        keys[at * length : (at + 1) * length] = rows((at + 3) % 4, 1)
+        values[at * length : (at + 1) * length] = rows((at + 3) % 4, 2)
+    query_grads = []
+    for e in range(4):
+        blocks = slice(e * length, (e + 3) * length)
+        before, behind = gap(e, 0), gap(e, 1)
+        far_below = jnp.where(core == 0, before, behind)
+        far_above = jnp.where(core == 0, behind, before)
+        q, g = rows(e, 0), rows(e, 3)
+        near = keys[blocks]
+        scores = dot_last(near, q)
+        scores = [scores[at * length : (at + 1) * length] for at in range(3)]
+        tops = [jnp.max(part, axis=0, keepdims=True) for part in scores]
+        top = jnp.maximum(tops[1], jnp.maximum(tops[0] - far_below, tops[2] - far_above))
+        offsets = (top + far_below, top, top + far_above)
+        powers = [jnp.exp2((part - o) * factor) for part, o in zip(scores, offsets)]
+        inverse = 1.0 / sum(jnp.sum(p, axis=0, keepdims=True) for p in powers)
+        prob_grads = dot_last(values[blocks], g)
+        prob_grads = [prob_grads[at * length : (at + 1) * length] for at in range(3)]
+        delta = inverse * sum(
+            jnp.sum(p * d, axis=0, keepdims=True) for p, d in zip(powers, prob_grads)
+        )
+        probs = [p * inverse for p in powers]
+        score_grad = jnp.concatenate(
+            [
+                (p * scaling * (d - delta)).astype(jnp.bfloat16)
+                for p, d in zip(probs, prob_grads)
+            ],
+            axis=0,
+        )
+        probs_half = jnp.concatenate([p.astype(jnp.bfloat16) for p in probs], axis=0)
+        query_grads.append(dot_first(score_grad, near))
+        for sums, part in ((key_sums, dot(score_grad, q)), (value_sums, dot(probs_half, g))):
+            if e == 0:
+                sums[blocks] = part
+            else:
+                held = slice(e * length, (e + 2) * length)
+                sums[held] += part[: 2 * length]
+                sums[(e + 2) * length : (e + 3) * length] = part[2 * length :]
+
+    def by_view(sums):
+        parts = [sums[at * length : (at + 1) * length] for at in range(6)]
+        return (parts[1] + parts[5], parts[2], parts[3], parts[0] + parts[4])
+
+    return query_grads, by_view(key_sums), by_view(value_sums)
+
+
+def attention_kernel(scaling, own_heads, place_ref, *refs):
+    own, mate_in, x_in, cross_in, mate_x_in = refs[:5]
+    out_ref, keys, values, key_sums, value_sums = refs[5:]
+    length = out_ref.shape[1]
+    heads = own.shape[0]
+    for head in range(heads):
+        shared = head >= own_heads
+        far = mate_x_in if shared else cross_in
+        xs = [own.at[head], mate_in.at[head], x_in.at[head], far.at[head]]
+        grads = one_head(
+            scaling, place_ref[CORE], xs, length, keys, values, key_sums, value_sums
+        )
+        for e in range(4):
+            if shared and e % 2 == 1:
+                continue
+            at = 4 * own_heads + e // 2 if shared else 4 * head + e
+            for kind in range(3):
+                out_ref[at, :, kind * HD : (kind + 1) * HD] = grads[kind][e].astype(out_ref.dtype)
+
+
+def attention(place, own_heads, sources):
+    heads, height, _ = sources[0].shape
+    length = (height - FLAG_ROWS) // 4
+    held = 4 * own_heads + 2 * (heads - own_heads)
+    return pl.pallas_call(
+        functools.partial(attention_kernel, HD ** (-0.5), own_heads),
+        out_shape=jax.ShapeDtypeStruct((held, length, 3 * HD), jnp.bfloat16),
+        in_specs=[whole(pltpu.SMEM)] + [whole()] * 5,
+        out_specs=whole(),
+        scratch_shapes=[pltpu.VMEM((6 * length, HD), jnp.bfloat16)] * 2
+        + [pltpu.VMEM((6 * length, HD), jnp.float32)] * 2,
+        compiler_params=pltpu.CompilerParams(vmem_limit_bytes=20 * MIB),
+        cost_estimate=pl.CostEstimate(
+            flops=heads * 4 * 5 * 2 * length * 3 * length * HD * 2,
+            bytes_accessed=heads * 2 * length * 7 * HD * 4,
+            transcendentals=heads * 12 * length * length,
+        ),
+        name="attention_gradients",
+    )(place, *sources)
+
+
+def turn_kernel(q_ref, k_ref, v_ref, out_ref):
+    for head in range(q_ref.shape[1] // HD):
+        for kind, source in enumerate((q_ref, k_ref, v_ref)):
+            at = (head * 3 + kind) * HD
+            out_ref[at : at + HD] = source[:, head * HD : (head + 1) * HD].T
+
+
+def turned_weights(weights):
+    rows, cols = weights[0].shape
+    return pl.pallas_call(
+        turn_kernel,
+        out_shape=jax.ShapeDtypeStruct((3 * cols, rows), jnp.bfloat16),
+        in_specs=[whole()] * 3,
+        out_specs=whole(),
+        compiler_params=pltpu.CompilerParams(vmem_limit_bytes=8 * MIB),
+        name="turn_weights",
+    )(*weights)
+
+
+def gathered(role, own_heads, shared, refs):
+    sides = []
+    for side in range(2):
+        pieces = []
+        for head in range(own_heads):
+            for maker in range(2):
+                k = 2 * side + (maker ^ role)
+                pieces.append([refs[k][4 * head + (e ^ k)] for e in range(4)])
+        for at in range(shared):
+            rows = []
+            for e in range(4):
+                k = 2 * side + e % 2
+                rows.append(refs[k][4 * own_heads + 2 * at + (e // 2 ^ side)])
+            pieces.append(rows)
+        sides.append(
+            jnp.concatenate([jnp.concatenate(rows, axis=0) for rows in pieces], axis=1)
+        )
+    return sides
+
+
+def input_kernel(role, own_heads, shared, place_ref, *refs):
+    grad_refs, weight_refs, out_refs, total = refs[:4], refs[4:6], refs[6:-1], refs[-1]
+    core, plane = place_ref[CORE], place_ref[PLANE]
+    rows = weight_refs[0].shape[1]
+    length = out_refs[0].shape[0]
+
+    @pl.when(core == role)
+    def _():
+        lefts = gathered(role, own_heads, shared, grad_refs)
+        depth = lefts[0].shape[1]
+        for weights, at in zip(weight_refs, (core, 1 - core)):
+            parts = []
+            for base, left in zip((HERE, BESIDE), lefts):
+                start = pl.multiple_of(place_ref[base] * (3 * HD), HD)
+                parts.append(dot(left, weights[pl.ds(start, depth)]))
+            product = (parts[0] + parts[1]).astype(total.dtype)
+            for e in range(4):
+                total[e, :, lanes(at * rows, rows)] = product[e * length : (e + 1) * length]
+        for s, out_ref in enumerate(out_refs):
+            out_ref[...] = total[jnp.bitwise_xor(plane, s)]
+
+
+def input_product(place, role, own_heads, shared, grads, own_weights, mate_weights):
+    _, length, _ = grads[0].shape
+    depth, rows = own_weights.shape
+    out = jax.ShapeDtypeStruct((length, 2 * rows), jnp.bfloat16)
+    return pl.pallas_call(
+        functools.partial(input_kernel, role, own_heads, shared),
+        out_shape=[out] * 4,
+        in_specs=[whole(pltpu.SMEM)] + [whole()] * 6,
+        out_specs=[whole()] * 4,
+        scratch_shapes=[pltpu.VMEM((4, length, 2 * rows), jnp.bfloat16)],
+        compiler_params=pltpu.CompilerParams(vmem_limit_bytes=28 * MIB),
+        cost_estimate=pl.CostEstimate(
+            flops=8 * length * 2 * rows * depth,
+            bytes_accessed=8 * length * (2 * rows + depth) + 4 * rows * depth,
+            transcendentals=0,
+        ),
+        name="input_gradient",
+    )(place, *grads, own_weights, mate_weights)
+
+
+def weight_kernel(mine, mean_scale, own_heads, shared, place_ref, *refs):
+    own, mate_in, first, second, corner, corner_far = refs[:6]
+    made, inward, ahead, aside, relay_x, relay_y = refs[6:12]
+    if mine:
+        received, out_refs, turned = refs[12], refs[13:16], refs[16]
+    else:
+        received, out_refs, turned = None, [refs[12].at[kind] for kind in range(3)], refs[13]
+    core = place_ref[CORE]
+    length = own.shape[1]
+    part = core if mine else 1 - core
+    tokens = ((own, mate_in, first, second), (first, second, corner, corner_far))
+    grads = ((made, inward, ahead, aside), (ahead, aside, relay_x, relay_y))
+    for role in range(2):
+
+        @pl.when(core == role)
+        def _():
+            for e, source in enumerate(tokens[role]):
+                turned[:, e * length : (e + 1) * length] = source[part].T
+            sides = gathered(role, own_heads, shared, grads[role])
+            for base, side in zip((HERE, BESIDE), sides):
+                total = dot(turned[...], side)
+                for head in range(side.shape[1] // (3 * HD)):
+                    here = lanes((place_ref[base] + head) * HD, HD)
+                    for kind, out in enumerate(out_refs):
+                        at = (head * 3 + kind) * HD
+                        value = total[:, at : at + HD]
+                        if mine:
+                            value = (value + received[kind, :, here]) * mean_scale
+                        out[:, here] = value
+
+
+def weight_product(place, mine, mean_scale, own_heads, shared, tokens, grads, received=()):
+    _, length, triple = grads[0].shape
+    rows = tokens[0].shape[2]
+    cols = 2 * (2 * own_heads + shared) * HD
+    out = jax.ShapeDtypeStruct((rows, cols), jnp.float32)
+    both = jax.ShapeDtypeStruct((3, rows, cols), jnp.float32)
+    return pl.pallas_call(
+        functools.partial(weight_kernel, mine, mean_scale, own_heads, shared),
+        out_shape=[out] * 3 if mine else both,
+        in_specs=[whole(pltpu.SMEM)] + [whole()] * (12 + len(received)),
+        out_specs=[whole()] * 3 if mine else whole(),
+        scratch_shapes=[pltpu.VMEM((rows, 4 * length), jnp.bfloat16)],
+        compiler_params=pltpu.CompilerParams(vmem_limit_bytes=36 * MIB),
+        cost_estimate=pl.CostEstimate(
+            flops=8 * rows * 3 * cols * length,
+            bytes_accessed=8 * length * (rows + 3 * cols) + 12 * rows * cols,
+            transcendentals=0,
+        ),
+        name="weight_gradient_own" if mine else "weight_gradient_mate",
+    )(place, *tokens, *grads, *received)
+
+
+def choose_kernel(which_ref, first_ref, second_ref, out_ref):
+    for which, ref in enumerate((first_ref, second_ref)):
+
+        @pl.when(which_ref[0] == which)
+        def _():
+            out_ref[...] = ref[...]
+
+
+def chosen_of(which, first, second):
+    return pl.pallas_call(
+        choose_kernel,
+        out_shape=jax.ShapeDtypeStruct(first.shape, first.dtype),
+        in_specs=[whole(pltpu.SMEM)] + [whole()] * 2,
+        out_specs=whole(),
+        compiler_params=pltpu.CompilerParams(vmem_limit_bytes=8 * MIB),
+        name="choose_block",
+    )(which, first, second)
+
+
+def gather_body(
+    normed,
+    queries,
+    saved_keys,
+    saved_values,
+    output_grad,
+    view_links,
+    query_weight,
+    key_weight,
+    value_weight,
+):
+    length, cols = queries.shape[2:]
+    model_width = normed.shape[-1]
+    rows = query_weight.shape[0]
+    prompts, views, groups = (lax.axis_size(name) for name in ("dp", "view", "head"))
+    mean_scale = 1.0 / (prompts * views)
+    half = cols // HD // 2
+    view = lax.axis_index("view")
+    core = lax.rem(view, 2)
+    side = view // 2
+    chip = lax.axis_index("dp") * (views // 2) + side
+    place = jnp.stack([core, lax.axis_index("head"), side * half, (1 - side) * half])
+    place = place.astype(jnp.int32)
+    arrays = tuple(a.reshape(length, cols) for a in (queries, saved_keys, saved_values, output_grad))
+
+    own_heads, shared = half // 2, half % 2
+    both = [2 * own_heads + at for at in range(shared)]
+    each = [2 * step for step in range(own_heads)]
+    to_x, to_cross, to_mate, own = pack(
+        (
+            [(BESIDE, step, 1) for step in each] + [(BESIDE, step, 0) for step in both],
+            [(BESIDE, step + 1, -1) for step in each],
+            [(HERE, step + 1, -1) for step in each] + [(HERE, step, 0) for step in both],
+            [(HERE, step, 1) for step in each] + [(HERE, step, 0) for step in both],
+        ),
+        place,
+        view_links,
+        arrays,
+    )
+    x_in = moved(to_x, along_x)
+    cross_in = moved(to_cross, across_x)
+    mate_in = moved(to_mate, mate)
+    mate_x_in = moved(x_in, mate)
+
+    own_weights = turned_weights(after((query_weight, key_weight, value_weight), own))
+    mate_weights = moved(own_weights, mate)
+
+    flat = normed.reshape(length, model_width)
+
+    def columns(of_chip):
+        parts = [
+            lax.dynamic_slice_in_dim(flat, (2 * of_chip + part) * rows, rows, axis=1)
+            for part in range(2)
+        ]
+        return jnp.stack(parts)
+
+    toward_x, toward_y = jnp.bitwise_xor(chip, 1), jnp.bitwise_xor(chip, 2)
+    here = columns(chip)
+    to_straight = columns(jnp.where(core == 0, toward_x, toward_y))
+    to_crossed = columns(jnp.where(core == 0, toward_y, toward_x))
+    to_corner = columns(jnp.bitwise_xor(chip, 3))
+    (sent,) = after((here,), mate_in)
+    mate_here = moved(sent, only(1, mate))
+    to_straight, to_crossed = after((to_straight, to_crossed), cross_in)
+    normed_ahead = moved(to_straight, straight)
+    normed_aside = moved(to_crossed, crossed)
+
+    made = attention(place, own_heads, (own, mate_in, x_in, cross_in, mate_x_in))
+    (made,) = after((made,), mate_here, normed_ahead, normed_aside)
+    ahead = moved(made, straight)
+    aside = moved(made, crossed)
+    inward = moved(made, only(1, mate))
+    relay_x = moved(ahead, only(1, along_x))
+    relay_y = moved(ahead, only(0, across_y))
+    first = (made, inward, ahead, aside)
+    second = (ahead, aside, relay_x, relay_y)
+
+    def exchange(role, slots):
+        arrived = []
+        for s in range(1, groups):
+            pairs = [
+                ((y * views + v) * groups + z, (y * views + v) * groups + (z ^ s))
+                for y in range(prompts)
+                for v in range(role, views, 2)
+                for z in range(groups)
+            ]
+            arrived.append(lax.ppermute(slots[s], ("dp", "view", "head"), pairs))
+        total = sum(array.astype(jnp.float32) for array in (slots[0], *arrived))
+        return total.astype(jnp.bfloat16), arrived
+
+    def deliver(role, total, *earlier):
+        def spot(y, v, z):
+            return (y * views + v) * groups + z
+
+        corners = [
+            (y, v, z) for y in range(prompts) for v in range(role, views, 2) for z in range(groups)
+        ]
+        pairs = [(spot(y, v, z), spot(y ^ role, v ^ z, z)) for y, v, z in corners]
+        beside = lax.ppermute(total, ("dp", "view", "head"), pairs)
+        pairs = [
+            (spot(y ^ role, v ^ z, z), spot(y ^ role, v ^ z, y * (views // 2) + v // 2))
+            for y, v, z in corners
+        ]
+        (beside,) = after((beside,), *earlier)
+        return lax.ppermute(beside, ("dp", "view", "head"), pairs)
+
+    first_slots = input_product(place, 0, own_heads, shared, first, own_weights, mate_weights)
+    first_total, _ = exchange(0, first_slots)
+    (turn,) = after((place,), first_total)
+    second_slots = input_product(turn, 1, own_heads, shared, second, own_weights, mate_weights)
+    second_total, arrived = exchange(1, second_slots)
+    (to_corner,) = after((to_corner,), *second_slots)
+    tokens = (
+        here,
+        mate_here,
+        normed_ahead,
+        normed_aside,
+        moved(to_corner, corner_same),
+        moved(to_corner, corner_cross),
+    )
+    grads = (made, inward, ahead, aside, relay_x, relay_y)
+    (turn,) = after((place,), arrived[1])
+    for_mate = weight_product(turn, False, mean_scale, own_heads, shared, tokens, grads)
+    from_mate = moved(for_mate, mate)
+    weight_grads = weight_product(
+        place, True, mean_scale, own_heads, shared, tokens, grads, (from_mate,)
+    )
+    landed = (deliver(0, first_total), deliver(1, second_total, *weight_grads))
+    which = jnp.bitwise_xor(lax.axis_index("head") // (views // 2), lax.axis_index("dp"))
+    input_grad = chosen_of(which.reshape(1).astype(jnp.int32), *landed)
+    return (
+        input_grad.reshape(1, 1, length, model_width // groups),
+        *weight_grads,
+    )
+
+
 def solution(mesh):
+    prompts, views, groups = (mesh.shape[name] for name in ("dp", "view", "head"))
+    loop_of_four = prompts * 2 == views and prompts * views == 2 * groups and views == groups
+
+    def choose(*arrays):
+        batch, held, length, cols = arrays[1].shape
+        if loop_of_four and batch == held == 1 and length % HD == 0 and cols % (2 * HD) == 0:
+            return gather_body(*arrays)
+        return halo_body(*arrays)
+
     placed = (
         P("dp", "view", None, None),
         P("dp", "view", None, "head"),
@@ -124,7 +635,7 @@
         P(("dp", "view"), "head"),
     )
     return jax.shard_map(
-        body,
+        choose,
         mesh=mesh,
         in_specs=placed,
         out_specs=(

time: 400 us -> 167 us (0.42)
  waiting for transfers between devices: 288 us -> 92 us
  local copies, waits for them, and re-layouts: 46.5 us -> 7.43 us
  matrix products: 34.9 us -> 0 us
  starting transfers between devices: 2.85 us -> 34.7 us
  Pallas kernels: 0 us -> 28.5 us
  between operations: 13.9 us -> 1.09 us
  other arithmetic: 11.1 us -> 0.66 us
    reduce_scatter x2 -> x0, waiting for transfers between devices: 224 us -> none  [the longest x1 175 us: body(): lax.psum_scatter(product * mean_scale, ('dp', 'view'), scatter_dimension=...]
    ppermute x4 -> x26, starting transfers between devices: 2.73 us -> 34.7 us  [the longest x16 18.2 us: moved(): return lax.ppermute(value, ('dp', 'view'), pairs)]
    dot_general x6 -> x0, matrix products: 30.9 us -> none  [the longest x1 11.9 us: body(): lax.dot_general(flat_input, all_grads, (((0,), (0,)), ((), ())), preferre...]
    pallas_call x0 -> x8, Pallas kernels: none -> 28.5 us  [the longest x1 8.93 us: attention(): pl.pallas_call(functools.partial(attention_kernel, HD ** (-0.5), own_head...]
    ppermute x4 -> x26, waiting for transfers between devices: 64.2 us -> 92 us  [the longest x16 44.1 us: moved(): return lax.ppermute(value, ('dp', 'view'), pairs)]
    unnamed x35 -> x16, local copies, waits for them, and re-layouts: 14.5 us -> 5.79 us
    reshape x3 -> x0, local copies, waits for them, and re-layouts: 8.38 us -> none  [the longest x1 4.16 us: attend(): value_grad = value_grad.reshape(batch_size, 3, length, col_count)]
    slice x4 -> x0, local copies, waits for them, and re-layouts: 7.65 us -> none  [the longest x1 3.61 us: body(): grad_value = together[:, 2 * col_count:]]
  transfers between devices with their start and end apart: 7 -> 26, of which waited for: 5 -> 9; matrix products, arithmetic and copies ran while one was open for 17% -> 1% of each run, Pallas kernels for 0% -> 13%
where the time goes in v6:
time: 167 us; the launch traced here: 164 us
  waiting for transfers between devices  92 us (55%)
  starting transfers between devices  34.7 us (21%)
  Pallas kernels  28.5 us (17%)
  local copies, waits for them, and re-layouts  7.43 us (4%)
    ppermute x16, waiting for transfers between devices, moved(): return lax.ppermute(value, ('dp', 'view'), pairs)  44.1 us
    ppermute x6, waiting for transfers between devices, exchange(): arrived.append(lax.ppermute(slots[s], ('dp', 'view', 'head'), pairs))  24.9 us
    ppermute x16, starting transfers between devices, moved(): return lax.ppermute(value, ('dp', 'view'), pairs)  18.2 us
    ppermute x2, waiting for transfers between devices, deliver(): return lax.ppermute(beside, ('dp', 'view', 'head'), pairs)  16.3 us
    ppermute x6, starting transfers between devices, exchange(): arrived.append(lax.ppermute(slots[s], ('dp', 'view', 'head'), pairs))  11.3 us
    pallas_call x1, Pallas kernels, attention(): pl.pallas_call(functools.partial(attention_kernel, HD ** (-0.5), own_head...  8.93 us
    pallas_call x2, Pallas kernels, input_product(): pl.pallas_call(functools.partial(input_kernel, role, own_heads, shared),...  8.64 us
    pallas_call x2, Pallas kernels, weight_product(): pl.pallas_call(functools.partial(weight_kernel, mine, mean_scale, own_hea...  7.85 us
  transfers between devices with their start and end apart: 26, of which 9 were waited for; matrix products, arithmetic and copies ran while one was open for 1% of the time, Pallas kernels for 13%

profile of v6, /device:TPU:16, one launch (start us, length us, event | category | flops | bytes accessed | tf_op | source)
XLA Modules:
  0.0 164.3 jit_solution(2955483933709437947)
XLA Ops:
  0.7 0.1 pad_add_fusion.place_ref
  0.7 1.1 copy-done.3
  1.8 1.0 copy-done.4
  2.8 1.0 copy-done.5
  3.8 1.0 copy-done.6
  4.8 0.7 copy-done.7
  5.5 1.8 %pack_heads.1 = (bf16[2,1040,128]{2,1,0:T(8,128)(2,1)S(1)}, bf16[1,1040,128]{2,1,0:T(8,128)(2,1)}, bf16[2,1040,128]{2,1,0:T(8,128)(2,1)}, bf16[2,1040,128]{2,1,0:T(8,128)(2,1)S(1)}) custom-call(s32[4]{0:T(128)S(1)} %pad_add_fusion.place_ref, s32[1,2]{1,0:T(1,128)S(1)} %copy-done.7, bf16[256,768]{1,0:T(8,128)(2,1)S(1)} %bitcast.26, ...), custom_call_target="tpu_custom_call" | custom-call | tf_op jit(solution)/shard_map/pack_heads/pallas_call | solution.py:215
  7.2 1.5 collective-permute-start.1
  8.7 0.0 collective-permute-start
  8.7 12.4 %collective-permute-done.1.refs_2_ = bf16[2,1040,128]{2,1,0:T(8,128)(2,1)} collective-permute-done((bf16[2,1040,128]{2,1,0:T(8,128)(2,1)S(1)}, bf16[2,1040,128]{2,1,0:T(8,128)(2,1)}, u32[]{:S(2)}, u32[]{:S(2)}) %collective-permute-start.1) | collective-permute-done | bytes 532512 | tf_op jit(solution)/shard_map/ppermute | solution.py:128
  21.2 0.0 collective-permute-start.3
  21.2 1.6 collective-permute-start.2
  22.8 1.1 copy-done.2
  23.8 0.5 turn_weights.1.refs_4_
  24.4 0.1 collective-permute-start.10
  24.5 1.6 %dynamic-slice_bitcast_fusion.1 = (bf16[1,256,384]{2,1,0:T(8,128)(2,1)S(1)}, bf16[1,256,384]{2,1,0:T(8,128)(2,1)S(1)}, bf16[1,256,384]{2,1,0:T(8,128)(2,1)S(1)},...) fusion(bf16[1,1,256,3072]{3,2,1,0:T(8,128)(2,1)} %param.9, ...), kind=kLoop, calls=%fused_computation.7 | loop fusion | bytes 3145760 | tf_op jit(solution)/shard_map/stack | solution.py:534
  26.2 0.1 pad_maximum_fusion.1
  26.3 3.2 %collective-permute-done.2.refs_3_ = bf16[1,1040,128]{2,1,0:T(8,128)(2,1)} collective-permute-done((bf16[1,1040,128]{2,1,0:T(8,128)(2,1)}, bf16[1,1040,128]{2,1,0:T(8,128)(2,1)}, u32[]{:S(2)}, u32[]{:S(2)}) %collective-permute-start.2) | collective-permute-done | bytes 266272 | tf_op jit(solution)/shard_map/ppermute | solution.py:128
  29.5 1.5 collective-permute-start.5
  31.0 0.3 collective-permute-start.6
  31.4 0.0 collective-permute-done.refs_1_
  31.4 1.3 collective-permute-start.4
  32.7 8.9 %attention_gradients.1.refs_0_.refs_6_ = bf16[6,256,384]{2,1,0:T(8,128)(2,1)S(1)} custom-call(s32[4]{0:T(128)S(1)} %pad_add_fusion.place_ref, bf16[2,1040,128]{2,1,0:T(8,128)(2,1)S(1)} %get-tuple-element.30.refs_0_, bf16[2,1040,128]{2,1,0:T(8,128)(2,1)} %collective-permute-done.refs_1_, bf16[2,1040,128]{2,1,0:T(8,128)(2,1)} %collective-permute-done.1.refs_2_, ...), custom_call_target="tpu_custom_call" | custom-call | flops 4026531840 | bytes 3670016 | tf_op jit(solution)/shard_map/attention_gradients/pallas_call | solution.py:310
  41.6 0.0 collective-permute-done.5.refs_2_
  41.6 1.6 collective-permute-start.8
  43.2 1.0 collective-permute-start.9
  44.2 1.3 collective-permute-start.7
  45.5 23.9 %collective-permute-done.8.refs_2_.refs_0_.refs_8_ = bf16[6,256,384]{2,1,0:T(8,128)(2,1)S(1)} collective-permute-done((bf16[6,256,384]{2,1,0:T(8,128)(2,1)S(1)}, bf16[6,256,384]{2,1,0:T(8,128)(2,1)S(1)}, u32[]{:S(2)}, u32[]{:S(2)}) %collective-permute-start.8) | collective-permute-done | bytes 1179680 | tf_op jit(solution)/shard_map/ppermute | solution.py:128
  69.3 3.8 %collective-permute-start.17 = (bf16[6,256,384]{2,1,0:T(8,128)(2,1)S(1)}, bf16[6,256,384]{2,1,0:T(8,128)(2,1)S(1)}, u32[]{:S(2)}, u32[]{:S(2)}) collective-permute-start(bf16[6,256,384]{2,1,0:T(8,128)(2,1)S(1)} %collective-permute-done.8.refs_2_.refs_0_.refs_8_), channel_id=1, source_target_pairs={{0,20},{8,28},{16,4},{24,12},{1,21},{9,29},{17,5},{25,13},{2,22},{... | collective-permute-start | bytes 3538952 | tf_op jit(solution)/shard_map/ppermute | solution.py:128
  73.1 0.7 collective-permute-start.16
  73.9 0.0 collective-permute-done.10.refs_5_
  73.9 0.0 collective-permute-done.9.refs_3_.refs_1_.refs_9_
  73.9 7.1 %input_gradient.2 = (bf16[256,768]{1,0:T(8,128)(2,1)S(1)}, bf16[256,768]{1,0:T(8,128)(2,1)S(1)}, bf16[256,768]{1,0:T(8,128)(2,1)S(1)}, bf16[256,768]{1,0:T(8,128)(2,1)S(1)}) custom-call(s32[4]{0:T(128)S(1)} %pad_add_fusion.place_ref, bf16[6,256,384]{2,1,0:T(8,128)(2,1)S(1)} %attention_gradients.1.refs_0_.refs_6_, ...), custom_call_target="tpu_custom_call" | custom-call | flops 3623878656 | bytes 9830400 | tf_op jit(solution)/shard_map/input_gradient/pallas_call | solution.py:392
  81.1 3.5 %collective-permute-start.11 = (bf16[256,768]{1,0:T(8,128)(2,1)S(1)}, bf16[256,768]{1,0:T(8,128)(2,1)S(1)}, u32[]{:S(2)}, u32[]{:S(2)}) collective-permute-start(bf16[256,768]{1,0:T(8,128)(2,1)S(1)} %get-tuple-element.42), channel_id=1, source_target_pairs={{0,1},{1,0},{2,3},{3,2},{8,9},{9,8},{10,11},{11,10},{16,17},{17,16... | collective-permute-start | bytes 1179656 | tf_op jit(solution)/shard_map/ppermute | solution.py:566
  84.6 2.2 %collective-permute-start.12 = (bf16[256,768]{1,0:T(8,128)(2,1)S(1)}, bf16[256,768]{1,0:T(8,128)(2,1)S(1)}, u32[]{:S(2)}, u32[]{:S(2)}) collective-permute-start(bf16[256,768]{1,0:T(8,128)(2,1)S(1)} %get-tuple-element.43), channel_id=1, source_target_pairs={{0,2},{1,3},{2,0},{3,1},{8,10},{9,11},{10,8},{11,9},{16,18},{17,19... | collective-permute-start | bytes 1179656 | tf_op jit(solution)/shard_map/ppermute | solution.py:566
  86.8 3.5 %collective-permute-start.13 = (bf16[256,768]{1,0:T(8,128)(2,1)S(1)}, bf16[256,768]{1,0:T(8,128)(2,1)S(1)}, u32[]{:S(2)}, u32[]{:S(2)}) collective-permute-start(bf16[256,768]{1,0:T(8,128)(2,1)S(1)} %get-tuple-element.44), channel_id=1, source_target_pairs={{0,3},{1,2},{2,1},{3,0},{8,11},{9,10},{10,9},{11,8},{16,19},{17,18... | collective-permute-start | bytes 1179656 | tf_op jit(solution)/shard_map/ppermute | solution.py:566
  90.4 0.5 collective-permute-done.11
  90.9 16.0 %collective-permute-done.12 = bf16[256,768]{1,0:T(8,128)(2,1)S(1)} collective-permute-done((bf16[256,768]{1,0:T(8,128)(2,1)S(1)}, bf16[256,768]{1,0:T(8,128)(2,1)S(1)}, u32[]{:S(2)}, u32[]{:S(2)}) %collective-permute-start.12) | collective-permute-done | bytes 393248 | tf_op jit(solution)/shard_map/ppermute | solution.py:566
  106.9 8.3 %collective-permute-done.13 = bf16[256,768]{1,0:T(8,128)(2,1)S(1)} collective-permute-done((bf16[256,768]{1,0:T(8,128)(2,1)S(1)}, bf16[256,768]{1,0:T(8,128)(2,1)S(1)}, u32[]{:S(2)}, u32[]{:S(2)}) %collective-permute-start.13) | collective-permute-done | bytes 393248 | tf_op jit(solution)/shard_map/ppermute | solution.py:566
  115.2 0.2 add_convert_fusion.1
  115.4 0.0 collective-permute-done.17.refs_3_.refs_11_
  115.4 0.0 collective-permute-done.16.refs_2_.refs_10_
  115.5 1.5 input_gradient.3
  117.0 0.7 collective-permute-start.19
  117.7 1.3 collective-permute-start.23
  119.0 0.7 collective-permute-start.22
  119.7 4.5 %collective-permute-done.23.refs_5_ = bf16[2,256,384]{2,1,0:T(8,128)(2,1)S(1)} collective-permute-done((bf16[2,256,384]{2,1,0:T(8,128)(2,1)S(1)}, bf16[2,256,384]{2,1,0:T(8,128)(2,1)S(1)}, u32[]{:S(2)}, u32[]{:S(2)}) %collective-permute-start.23) | collective-permute-done | bytes 393248 | tf_op jit(solution)/shard_map/ppermute | solution.py:128
  124.2 3.1 %weight_gradient_mate.1 = f32[3,384,768]{2,1,0:T(8,128)S(1)} custom-call(s32[4]{0:T(128)S(1)} %pad_add_fusion.place_ref, bf16[2,256,384]{2,1,0:T(8,128)(2,1)S(1)} %pad_maximum_fusion.refs_0_, bf16[2,256,384]{2,1,0:T(8,128)(2,1)S(1)} %collective-permute-done.4.refs_1_, bf16[2,256,384]{2,1,0:T(8,128)(2,1)S(1)} %collective-permute-done.5.refs_2_, ...), custom_call_target="tpu_custom_call" | custom-call | flops 1811939328 | bytes 9043968 | tf_op jit(solution)/shard_map/weight_gradient_mate/pallas_call | solution.py:445
  127.4 1.5 collective-permute-start.24
  128.9 0.7 collective-permute-start.18
  129.6 0.7 collective-permute-start.20
  130.3 2.0 %collective-permute-start.14 = (bf16[256,768]{1,0:T(8,128)(2,1)S(1)}, bf16[256,768]{1,0:T(8,128)(2,1)S(1)}, u32[]{:S(2)}, u32[]{:S(2)}) collective-permute-start(bf16[256,768]{1,0:T(8,128)(2,1)S(1)} %add_convert_fusion.1), channel_id=1, source_target_pairs={{0,0},{1,5},{2,10},{3,15},{8,8},{9,13},{10,2},{11,7},{16,16},{17,2... | collective-permute-start | bytes 1179656 | tf_op jit(solution)/shard_map/ppermute | solution.py:578
  132.3 0.0 collective-permute-done.18
  132.3 0.0 collective-permute-done.20
  132.3 0.2 add_convert_fusion
  132.5 0.7 collective-permute-start.21
  133.2 6.8 %collective-permute-done.14 = bf16[256,768]{1,0:T(8,128)(2,1)S(1)} collective-permute-done((bf16[256,768]{1,0:T(8,128)(2,1)S(1)}, bf16[256,768]{1,0:T(8,128)(2,1)S(1)}, u32[]{:S(2)}, u32[]{:S(2)}) %collective-permute-start.14) | collective-permute-done | bytes 393248 | tf_op jit(solution)/shard_map/ppermute | solution.py:578
  139.9 1.3 collective-permute-start.15
  141.2 4.7 %weight_gradient_own.1 = (f32[384,768]{1,0:T(8,128)}, f32[384,768]{1,0:T(8,128)}, f32[384,768]{1,0:T(8,128)}) custom-call(s32[4]{0:T(128)S(1)} %pad_add_fusion.place_ref, bf16[2,256,384]{2,1,0:T(8,128)(2,1)S(1)} %pad_maximum_fusion.refs_0_, bf16[2,256,384]{2,1,0:T(8,128)(2,1)S(1)} %collective-permute-done.4.refs_1_, ...), custom_call_target="tpu_custom_call" | custom-call | flops 1811939328 | bytes 9043968 | tf_op jit(solution)/shard_map/weight_gradient_own/pallas_call | solution.py:445
  146.0 0.0 collective-permute-done.21
  146.0 1.3 collective-permute-start.25
  147.3 0.0 collective-permute-done.15.first_ref
  147.3 16.3 %collective-permute-done.25.second_ref = bf16[256,768]{1,0:T(8,128)(2,1)S(1)} collective-permute-done((bf16[256,768]{1,0:T(8,128)(2,1)S(1)}, bf16[256,768]{1,0:T(8,128)(2,1)S(1)}, u32[]{:S(2)}, u32[]{:S(2)}) %collective-permute-start.25) | collective-permute-done | bytes 393248 | tf_op jit(solution)/shard_map/ppermute | solution.py:584
  163.5 0.8 choose_block.1
  (19 shorter events, 0.1 us)
Async XLA Ops:
  0.6 22.1 %copy-start.1 = (bf16[384,768]{1,0:T(8,128)(2,1)S(1)}, bf16[384,768]{1,0:T(8,128)(2,1)}, u32[]{:S(2)}) copy-start(bf16[384,768]{1,0:T(8,128)(2,1)} %k_ref) | copy-start | bytes 1769476
  0.6 22.1 %copy-start = (bf16[384,768]{1,0:T(8,128)(2,1)S(1)}, bf16[384,768]{1,0:T(8,128)(2,1)}, u32[]{:S(2)}) copy-start(bf16[384,768]{1,0:T(8,128)(2,1)} %q_ref) | copy-start | bytes 1769476
  0.7 1.1 copy-start.3
  1.8 1.0 copy-start.4
  2.8 1.0 copy-start.5
  3.8 1.0 copy-start.6
  4.8 0.7 copy-start.7
  7.2 13.9 %collective-permute-start.1 = (bf16[2,1040,128]{2,1,0:T(8,128)(2,1)S(1)}, bf16[2,1040,128]{2,1,0:T(8,128)(2,1)}, u32[]{:S(2)}, u32[]{:S(2)}) collective-permute-start(bf16[2,1040,128]{2,1,0:T(8,128)(2,1)S(1)} %get-tuple-element.32), channel_id=1, source_target_pairs={{0,8},{4,12},{8,0},{12,4},{16,24},{20,28},{24,16},{28,20},{1,9},{5... | collective-permute-start | bytes 1597448 | tf_op jit(solution)/shard_map/ppermute | solution.py:128
  8.7 22.6 %collective-permute-start = (bf16[2,1040,128]{2,1,0:T(8,128)(2,1)}, bf16[2,1040,128]{2,1,0:T(8,128)(2,1)}, u32[]{:S(2)}, u32[]{:S(2)}) collective-permute-start(bf16[2,1040,128]{2,1,0:T(8,128)(2,1)} %get-tuple-element.31), channel_id=1, source_target_pairs={{0,4},{4,0},{8,12},{12,8},{16,20},{20,16},{24,28},{28,24},{1,5},{5... | collective-permute-start | bytes 1597448 | tf_op jit(solution)/shard_map/ppermute | solution.py:128
  21.2 11.5 %collective-permute-start.3 = (bf16[2,1040,128]{2,1,0:T(8,128)(2,1)}, bf16[2,1040,128]{2,1,0:T(8,128)(2,1)}, u32[]{:S(2)}, u32[]{:S(2)}) collective-permute-start(bf16[2,1040,128]{2,1,0:T(8,128)(2,1)} %collective-permute-done.1.refs_2_), channel_id=1, source_target_pairs={{0,4},{4,0},{8,12},{12,8},{16,20},{20,16},{24,28},{28,24},{1,5},{5... | collective-permute-start | bytes 1597448 | tf_op jit(solution)/shard_map/ppermute | solution.py:128
  21.2 8.4 %collective-permute-start.2 = (bf16[1,1040,128]{2,1,0:T(8,128)(2,1)}, bf16[1,1040,128]{2,1,0:T(8,128)(2,1)}, u32[]{:S(2)}, u32[]{:S(2)}) collective-permute-start(bf16[1,1040,128]{2,1,0:T(8,128)(2,1)} %get-tuple-element.33), channel_id=1, source_target_pairs={{0,12},{4,8},{8,4},{12,0},{16,28},{20,24},{24,20},{28,16},{1,13},{... | collective-permute-start | bytes 798728 | tf_op jit(solution)/shard_map/ppermute | solution.py:128
  22.8 1.1 copy-start.2
  24.4 49.5 %collective-permute-start.10 = (bf16[2304,384]{1,0:T(8,128)(2,1)S(1)}, bf16[2304,384]{1,0:T(8,128)(2,1)}, u32[]{:S(2)}, u32[]{:S(2)}) collective-permute-start(bf16[2304,384]{1,0:T(8,128)(2,1)S(1)} %turn_weights.1.refs_4_), channel_id=1, source_target_pairs={{0,4},{4,0},{8,12},{12,8},{16,20},{20,16},{24,28},{28,24},{1,5},{5... | collective-permute-start | bytes 5308424 | tf_op jit(solution)/shard_map/ppermute | solution.py:128
  29.5 12.1 %collective-permute-start.5 = (bf16[2,256,384]{2,1,0:T(8,128)(2,1)S(1)}, bf16[2,256,384]{2,1,0:T(8,128)(2,1)S(1)}, u32[]{:S(2)}, u32[]{:S(2)}) collective-permute-start(bf16[2,256,384]{2,1,0:T(8,128)(2,1)S(1)} %get-tuple-element.35), channel_id=1, source_target_pairs={{0,8},{4,20},{8,0},{12,28},{16,24},{20,4},{24,16},{28,12},{1,9},{5... | collective-permute-start | bytes 1179656 | tf_op jit(solution)/shard_map/ppermute | solution.py:128
  31.0 10.6 %collective-permute-start.6 = (bf16[2,256,384]{2,1,0:T(8,128)(2,1)S(1)}, bf16[2,256,384]{2,1,0:T(8,128)(2,1)S(1)}, u32[]{:S(2)}, u32[]{:S(2)}) collective-permute-start(bf16[2,256,384]{2,1,0:T(8,128)(2,1)S(1)} %get-tuple-element.36), channel_id=1, source_target_pairs={{0,20},{4,8},{8,28},{12,0},{16,4},{20,24},{24,12},{28,16},{1,21},{... | collective-permute-start | bytes 1179656 | tf_op jit(solution)/shard_map/ppermute | solution.py:128
  31.4 10.3 %collective-permute-start.4 = (bf16[2,256,384]{2,1,0:T(8,128)(2,1)S(1)}, bf16[2,256,384]{2,1,0:T(8,128)(2,1)S(1)}, u32[]{:S(2)}, u32[]{:S(2)}) collective-permute-start(bf16[2,256,384]{2,1,0:T(8,128)(2,1)S(1)} %pad_maximum_fusion.refs_0_), channel_id=1, source_target_pairs={{4,0},{12,8},{20,16},{28,24},{5,1},{13,9},{21,17},{29,25},{6,2},{1... | collective-permute-start | bytes 1179656 | tf_op jit(solution)/shard_map/ppermute | solution.py:128
  41.6 27.7 %collective-permute-start.8 = (bf16[6,256,384]{2,1,0:T(8,128)(2,1)S(1)}, bf16[6,256,384]{2,1,0:T(8,128)(2,1)S(1)}, u32[]{:S(2)}, u32[]{:S(2)}) collective-permute-start(bf16[6,256,384]{2,1,0:T(8,128)(2,1)S(1)} %attention_gradients.1.refs_0_.refs_6_), channel_id=1, source_target_pairs={{0,8},{4,20},{8,0},{12,28},{16,24},{20,4},{24,16},{28,12},{1,9},{5... | collective-permute-start | bytes 3538952 | tf_op jit(solution)/shard_map/ppermute | solution.py:128
  43.2 30.7 %collective-permute-start.9 = (bf16[6,256,384]{2,1,0:T(8,128)(2,1)S(1)}, bf16[6,256,384]{2,1,0:T(8,128)(2,1)S(1)}, u32[]{:S(2)}, u32[]{:S(2)}) collective-permute-start(bf16[6,256,384]{2,1,0:T(8,128)(2,1)S(1)} %attention_gradients.1.refs_0_.refs_6_), channel_id=1, source_target_pairs={{0,20},{4,8},{8,28},{12,0},{16,4},{20,24},{24,12},{28,16},{1,21},{... | collective-permute-start | bytes 3538952 | tf_op jit(solution)/shard_map/ppermute | solution.py:128
  44.2 29.7 %collective-permute-start.7 = (bf16[6,256,384]{2,1,0:T(8,128)(2,1)S(1)}, bf16[6,256,384]{2,1,0:T(8,128)(2,1)S(1)}, u32[]{:S(2)}, u32[]{:S(2)}) collective-permute-start(bf16[6,256,384]{2,1,0:T(8,128)(2,1)S(1)} %attention_gradients.1.refs_0_.refs_6_), channel_id=1, source_target_pairs={{4,0},{12,8},{20,16},{28,24},{5,1},{13,9},{21,17},{29,25},{6,2},{1... | collective-permute-start | bytes 3538952 | tf_op jit(solution)/shard_map/ppermute | solution.py:128
  69.3 46.1 %collective-permute-start.17 = (bf16[6,256,384]{2,1,0:T(8,128)(2,1)S(1)}, bf16[6,256,384]{2,1,0:T(8,128)(2,1)S(1)}, u32[]{:S(2)}, u32[]{:S(2)}) collective-permute-start(bf16[6,256,384]{2,1,0:T(8,128)(2,1)S(1)} %collective-permute-done.8.refs_2_.refs_0_.refs_8_), channel_id=1, source_target_pairs={{0,20},{8,28},{16,4},{24,12},{1,21},{9,29},{17,5},{25,13},{2,22},{... | collective-permute-start | bytes 3538952 | tf_op jit(solution)/shard_map/ppermute | solution.py:128
  73.1 42.3 %collective-permute-start.16 = (bf16[6,256,384]{2,1,0:T(8,128)(2,1)S(1)}, bf16[6,256,384]{2,1,0:T(8,128)(2,1)S(1)}, u32[]{:S(2)}, u32[]{:S(2)}) collective-permute-start(bf16[6,256,384]{2,1,0:T(8,128)(2,1)S(1)} %collective-permute-done.8.refs_2_.refs_0_.refs_8_), channel_id=1, source_target_pairs={{4,12},{12,4},{20,28},{28,20},{5,13},{13,5},{21,29},{29,21},{6,14}... | collective-permute-start | bytes 3538952 | tf_op jit(solution)/shard_map/ppermute | solution.py:128
  81.1 9.8 %collective-permute-start.11 = (bf16[256,768]{1,0:T(8,128)(2,1)S(1)}, bf16[256,768]{1,0:T(8,128)(2,1)S(1)}, u32[]{:S(2)}, u32[]{:S(2)}) collective-permute-start(bf16[256,768]{1,0:T(8,128)(2,1)S(1)} %get-tuple-element.42), channel_id=1, source_target_pairs={{0,1},{1,0},{2,3},{3,2},{8,9},{9,8},{10,11},{11,10},{16,17},{17,16... | collective-permute-start | bytes 1179656 | tf_op jit(solution)/shard_map/ppermute | solution.py:566
  84.6 22.4 %collective-permute-start.12 = (bf16[256,768]{1,0:T(8,128)(2,1)S(1)}, bf16[256,768]{1,0:T(8,128)(2,1)S(1)}, u32[]{:S(2)}, u32[]{:S(2)}) collective-permute-start(bf16[256,768]{1,0:T(8,128)(2,1)S(1)} %get-tuple-element.43), channel_id=1, source_target_pairs={{0,2},{1,3},{2,0},{3,1},{8,10},{9,11},{10,8},{11,9},{16,18},{17,19... | collective-permute-start | bytes 1179656 | tf_op jit(solution)/shard_map/ppermute | solution.py:566
  86.8 28.4 %collective-permute-start.13 = (bf16[256,768]{1,0:T(8,128)(2,1)S(1)}, bf16[256,768]{1,0:T(8,128)(2,1)S(1)}, u32[]{:S(2)}, u32[]{:S(2)}) collective-permute-start(bf16[256,768]{1,0:T(8,128)(2,1)S(1)} %get-tuple-element.44), channel_id=1, source_target_pairs={{0,3},{1,2},{2,1},{3,0},{8,11},{9,10},{10,9},{11,8},{16,19},{17,18... | collective-permute-start | bytes 1179656 | tf_op jit(solution)/shard_map/ppermute | solution.py:566
  117.0 2.7 %collective-permute-start.19 = (bf16[256,768]{1,0:T(8,128)(2,1)S(1)}, bf16[256,768]{1,0:T(8,128)(2,1)S(1)}, u32[]{:S(2)}, u32[]{:S(2)}) collective-permute-start(bf16[256,768]{1,0:T(8,128)(2,1)S(1)} %get-tuple-element.48), channel_id=1, source_target_pairs={{4,6},{5,7},{6,4},{7,5},{12,14},{13,15},{14,12},{15,13},{20,22},{2... | collective-permute-start | bytes 1179656 | tf_op jit(solution)/shard_map/ppermute | solution.py:566
  117.7 6.6 %collective-permute-start.23 = (bf16[2,256,384]{2,1,0:T(8,128)(2,1)S(1)}, bf16[2,256,384]{2,1,0:T(8,128)(2,1)S(1)}, u32[]{:S(2)}, u32[]{:S(2)}) collective-permute-start(bf16[2,256,384]{2,1,0:T(8,128)(2,1)S(1)} %pad_maximum_fusion.3), channel_id=1, source_target_pairs={{0,28},{8,20},{16,12},{24,4},{1,29},{9,21},{17,13},{25,5},{2,30},{... | collective-permute-start | bytes 1179656 | tf_op jit(solution)/shard_map/ppermute | solution.py:128
  119.0 5.3 %collective-permute-start.22 = (bf16[2,256,384]{2,1,0:T(8,128)(2,1)S(1)}, bf16[2,256,384]{2,1,0:T(8,128)(2,1)S(1)}, u32[]{:S(2)}, u32[]{:S(2)}) collective-permute-start(bf16[2,256,384]{2,1,0:T(8,128)(2,1)S(1)} %pad_maximum_fusion.3), channel_id=1, source_target_pairs={{4,28},{12,20},{20,12},{28,4},{5,29},{13,21},{21,13},{29,5},{6,30}... | collective-permute-start | bytes 1179656 | tf_op jit(solution)/shard_map/ppermute | solution.py:128
  127.4 13.9 %collective-permute-start.24 = (f32[3,384,768]{2,1,0:T(8,128)S(1)}, f32[3,384,768]{2,1,0:T(8,128)S(1)}, u32[]{:S(2)}, u32[]{:S(2)}) collective-permute-start(f32[3,384,768]{2,1,0:T(8,128)S(1)} %weight_gradient_mate.1), channel_id=1, source_target_pairs={{0,4},{4,0},{8,12},{12,8},{16,20},{20,16},{24,28},{28,24},{1,5},{5... | collective-permute-start | bytes 10616840 | tf_op jit(solution)/shard_map/ppermute | solution.py:128
  128.9 3.4 %collective-permute-start.18 = (bf16[256,768]{1,0:T(8,128)(2,1)S(1)}, bf16[256,768]{1,0:T(8,128)(2,1)S(1)}, u32[]{:S(2)}, u32[]{:S(2)}) collective-permute-start(bf16[256,768]{1,0:T(8,128)(2,1)S(1)} %get-tuple-element.47), channel_id=1, source_target_pairs={{4,5},{5,4},{6,7},{7,6},{12,13},{13,12},{14,15},{15,14},{20,21},{2... | collective-permute-start | bytes 1179656 | tf_op jit(solution)/shard_map/ppermute | solution.py:566
  129.6 2.7 %collective-permute-start.20 = (bf16[256,768]{1,0:T(8,128)(2,1)S(1)}, bf16[256,768]{1,0:T(8,128)(2,1)S(1)}, u32[]{:S(2)}, u32[]{:S(2)}) collective-permute-start(bf16[256,768]{1,0:T(8,128)(2,1)S(1)} %get-tuple-element.49), channel_id=1, source_target_pairs={{4,7},{5,6},{6,5},{7,4},{12,15},{13,14},{14,13},{15,12},{20,23},{2... | collective-permute-start | bytes 1179656 | tf_op jit(solution)/shard_map/ppermute | solution.py:566
  130.3 9.7 %collective-permute-start.14 = (bf16[256,768]{1,0:T(8,128)(2,1)S(1)}, bf16[256,768]{1,0:T(8,128)(2,1)S(1)}, u32[]{:S(2)}, u32[]{:S(2)}) collective-permute-start(bf16[256,768]{1,0:T(8,128)(2,1)S(1)} %add_convert_fusion.1), channel_id=1, source_target_pairs={{0,0},{1,5},{2,10},{3,15},{8,8},{9,13},{10,2},{11,7},{16,16},{17,2... | collective-permute-start | bytes 1179656 | tf_op jit(solution)/shard_map/ppermute | solution.py:578
  132.5 13.5 %collective-permute-start.21 = (bf16[256,768]{1,0:T(8,128)(2,1)S(1)}, bf16[256,768]{1,0:T(8,128)(2,1)S(1)}, u32[]{:S(2)}, u32[]{:S(2)}) collective-permute-start(bf16[256,768]{1,0:T(8,128)(2,1)S(1)} %add_convert_fusion), channel_id=1, source_target_pairs={{4,20},{5,17},{6,30},{7,27},{12,28},{13,25},{14,22},{15,19},{20,4}... | collective-permute-start | bytes 1179656 | tf_op jit(solution)/shard_map/ppermute | solution.py:578
  139.9 7.3 %collective-permute-start.15 = (bf16[256,768]{1,0:T(8,128)(2,1)S(1)}, bf16[256,768]{1,0:T(8,128)(2,1)S(1)}, u32[]{:S(2)}, u32[]{:S(2)}) collective-permute-start(bf16[256,768]{1,0:T(8,128)(2,1)S(1)} %collective-permute-done.14), channel_id=1, source_target_pairs={{0,0},{5,4},{10,8},{15,12},{8,9},{13,13},{2,1},{7,5},{16,18},{21,2... | collective-permute-start | bytes 1179656 | tf_op jit(solution)/shard_map/ppermute | solution.py:584
  146.0 17.6 %collective-permute-start.25 = (bf16[256,768]{1,0:T(8,128)(2,1)S(1)}, bf16[256,768]{1,0:T(8,128)(2,1)S(1)}, u32[]{:S(2)}, u32[]{:S(2)}) collective-permute-start(bf16[256,768]{1,0:T(8,128)(2,1)S(1)} %collective-permute-done.21), channel_id=1, source_target_pairs={{20,20},{17,16},{30,28},{27,24},{28,29},{25,25},{22,21},{19,17},{4... | collective-permute-start | bytes 1179656 | tf_op jit(solution)/shard_map/ppermute | solution.py:584

commit v7 on v6

--- a/solution.py
+++ b/solution.py
@@ -219,7 +219,6 @@
         ],
         in_specs=[whole(pltpu.SMEM)] * 2 + [whole()] * 4,
         out_specs=[whole()] * len(picks),
-        compiler_params=pltpu.CompilerParams(vmem_limit_bytes=12 * MIB),
         name="pack_heads",
     )(place, links, *arrays)
 
@@ -324,23 +323,44 @@
     )(place, *sources)
 
 
-def turn_kernel(q_ref, k_ref, v_ref, out_ref):
-    for head in range(q_ref.shape[1] // HD):
-        for kind, source in enumerate((q_ref, k_ref, v_ref)):
-            at = (head * 3 + kind) * HD
-            out_ref[at : at + HD] = source[:, head * HD : (head + 1) * HD].T
-
-
-def turned_weights(weights):
+def turn_kernel(place_ref, q_ref, k_ref, v_ref, out_ref):
+    half = q_ref.shape[1] // HD // 2
+    for side, base in enumerate((HERE, BESIDE)):
+        for head in range(half):
+            for kind, source in enumerate((q_ref, k_ref, v_ref)):
+                at = ((side * half + head) * 3 + kind) * HD
+                out_ref[at : at + HD] = source[:, lanes((place_ref[base] + head) * HD, HD)].T
+
+
+def turned_weights(place, weights):
     rows, cols = weights[0].shape
     return pl.pallas_call(
         turn_kernel,
         out_shape=jax.ShapeDtypeStruct((3 * cols, rows), jnp.bfloat16),
-        in_specs=[whole()] * 3,
+        in_specs=[whole(pltpu.SMEM)] + [whole()] * 3,
         out_specs=whole(),
         compiler_params=pltpu.CompilerParams(vmem_limit_bytes=8 * MIB),
         name="turn_weights",
-    )(*weights)
+    )(place, *weights)
+
+
+def join_kernel(place_ref, own_ref, mate_ref, out_ref):
+    core = place_ref[CORE]
+    rows = own_ref.shape[1]
+    out_ref[:, lanes(core * rows, rows)] = own_ref[...]
+    out_ref[:, lanes((1 - core) * rows, rows)] = mate_ref[...]
+
+
+def joined_weights(place, own_weights, mate_weights):
+    depth, rows = own_weights.shape
+    return pl.pallas_call(
+        join_kernel,
+        out_shape=jax.ShapeDtypeStruct((depth, 2 * rows), jnp.bfloat16),
+        in_specs=[whole(pltpu.SMEM)] + [whole()] * 2,
+        out_specs=whole(),
+        compiler_params=pltpu.CompilerParams(vmem_limit_bytes=12 * MIB),
+        name="join_weights",
+    )(place, own_weights, mate_weights)
 
 
 def gathered(role, own_heads, shared, refs):
@@ -364,45 +384,37 @@
 
 
 def input_kernel(role, own_heads, shared, place_ref, *refs):
-    grad_refs, weight_refs, out_refs, total = refs[:4], refs[4:6], refs[6:-1], refs[-1]
-    core, plane = place_ref[CORE], place_ref[PLANE]
-    rows = weight_refs[0].shape[1]
+    grad_refs, weights, out_refs, total = refs[:4], refs[4], refs[5:-1], refs[-1]
     length = out_refs[0].shape[0]
 
-    @pl.when(core == role)
+    @pl.when(place_ref[CORE] == role)
     def _():
-        lefts = gathered(role, own_heads, shared, grad_refs)
-        depth = lefts[0].shape[1]
-        for weights, at in zip(weight_refs, (core, 1 - core)):
-            parts = []
-            for base, left in zip((HERE, BESIDE), lefts):
-                start = pl.multiple_of(place_ref[base] * (3 * HD), HD)
-                parts.append(dot(left, weights[pl.ds(start, depth)]))
-            product = (parts[0] + parts[1]).astype(total.dtype)
-            for e in range(4):
-                total[e, :, lanes(at * rows, rows)] = product[e * length : (e + 1) * length]
+        left = jnp.concatenate(gathered(role, own_heads, shared, grad_refs), axis=1)
+        for e in range(4):
+            product = dot(left[e * length : (e + 1) * length], weights[...])
+            total[e] = product.astype(total.dtype)
         for s, out_ref in enumerate(out_refs):
-            out_ref[...] = total[jnp.bitwise_xor(plane, s)]
-
-
-def input_product(place, role, own_heads, shared, grads, own_weights, mate_weights):
+            out_ref[...] = total[jnp.bitwise_xor(place_ref[PLANE], s)]
+
+
+def input_product(place, role, own_heads, shared, grads, weights):
     _, length, _ = grads[0].shape
-    depth, rows = own_weights.shape
-    out = jax.ShapeDtypeStruct((length, 2 * rows), jnp.bfloat16)
+    depth, rows = weights.shape
+    out = jax.ShapeDtypeStruct((length, rows), jnp.bfloat16)
     return pl.pallas_call(
         functools.partial(input_kernel, role, own_heads, shared),
         out_shape=[out] * 4,
-        in_specs=[whole(pltpu.SMEM)] + [whole()] * 6,
+        in_specs=[whole(pltpu.SMEM)] + [whole()] * 5,
         out_specs=[whole()] * 4,
-        scratch_shapes=[pltpu.VMEM((4, length, 2 * rows), jnp.bfloat16)],
+        scratch_shapes=[pltpu.VMEM((4, length, rows), jnp.bfloat16)],
         compiler_params=pltpu.CompilerParams(vmem_limit_bytes=28 * MIB),
         cost_estimate=pl.CostEstimate(
-            flops=8 * length * 2 * rows * depth,
-            bytes_accessed=8 * length * (2 * rows + depth) + 4 * rows * depth,
+            flops=8 * length * rows * depth,
+            bytes_accessed=8 * length * (rows + depth) + 2 * rows * depth,
             transcendentals=0,
         ),
         name="input_gradient",
-    )(place, *grads, own_weights, mate_weights)
+    )(place, *grads, weights)
 
 
 def weight_kernel(mine, mean_scale, own_heads, shared, place_ref, *refs):
@@ -519,10 +531,9 @@
     x_in = moved(to_x, along_x)
     cross_in = moved(to_cross, across_x)
     mate_in = moved(to_mate, mate)
-    mate_x_in = moved(x_in, mate)
-
-    own_weights = turned_weights(after((query_weight, key_weight, value_weight), own))
-    mate_weights = moved(own_weights, mate)
+    (sent,) = after((x_in,), cross_in)
+    mate_x_in = moved(sent, mate)
+
 
     flat = normed.reshape(length, model_width)
 
@@ -538,19 +549,22 @@
     to_straight = columns(jnp.where(core == 0, toward_x, toward_y))
     to_crossed = columns(jnp.where(core == 0, toward_y, toward_x))
     to_corner = columns(jnp.bitwise_xor(chip, 3))
-    (sent,) = after((here,), mate_in)
-    mate_here = moved(sent, only(1, mate))
+    mate_here = moved(here, only(1, mate))
     to_straight, to_crossed = after((to_straight, to_crossed), cross_in)
     normed_ahead = moved(to_straight, straight)
     normed_aside = moved(to_crossed, crossed)
 
-    made = attention(place, own_heads, (own, mate_in, x_in, cross_in, mate_x_in))
-    (made,) = after((made,), mate_here, normed_ahead, normed_aside)
+    own_weights = turned_weights(place, after((query_weight, key_weight, value_weight), x_in))
+    (turn,) = after((place,), own_weights)
+    made = attention(turn, own_heads, (own, mate_in, x_in, cross_in, mate_x_in))
+    (made,) = after((made,), normed_ahead, normed_aside)
+    weights = joined_weights(place, own_weights, moved(own_weights, mate))
     ahead = moved(made, straight)
     aside = moved(made, crossed)
     inward = moved(made, only(1, mate))
-    relay_x = moved(ahead, only(1, along_x))
-    relay_y = moved(ahead, only(0, across_y))
+    (sent,) = after((ahead,), mate_here)
+    relay_x = moved(sent, only(1, along_x))
+    relay_y = moved(sent, only(0, across_y))
     first = (made, inward, ahead, aside)
     second = (ahead, aside, relay_x, relay_y)
 
@@ -583,10 +597,10 @@
         (beside,) = after((beside,), *earlier)
         return lax.ppermute(beside, ("dp", "view", "head"), pairs)
 
-    first_slots = input_product(place, 0, own_heads, shared, first, own_weights, mate_weights)
+    first_slots = input_product(place, 0, own_heads, shared, first, weights)
     first_total, _ = exchange(0, first_slots)
     (turn,) = after((place,), first_total)
-    second_slots = input_product(turn, 1, own_heads, shared, second, own_weights, mate_weights)
+    second_slots = input_product(turn, 1, own_heads, shared, second, weights)
     second_total, arrived = exchange(1, second_slots)
     (to_corner,) = after((to_corner,), *second_slots)
     tokens = (
@@ -598,13 +612,13 @@
         moved(to_corner, corner_cross),
     )
     grads = (made, inward, ahead, aside, relay_x, relay_y)
-    (turn,) = after((place,), arrived[1])
+    (turn,) = after((place,), second_total)
     for_mate = weight_product(turn, False, mean_scale, own_heads, shared, tokens, grads)
     from_mate = moved(for_mate, mate)
     weight_grads = weight_product(
         place, True, mean_scale, own_heads, shared, tokens, grads, (from_mate,)
     )
-    landed = (deliver(0, first_total), deliver(1, second_total, *weight_grads))
+    landed = (deliver(0, first_total), deliver(1, second_total))
     which = jnp.bitwise_xor(lax.axis_index("head") // (views // 2), lax.axis_index("dp"))
     input_grad = chosen_of(which.reshape(1).astype(jnp.int32), *landed)
     return (

time: 167 us -> 177 us (1.060)
  waiting for transfers between devices: 92 us -> 96.8 us
  local copies, waits for them, and re-layouts: 7.43 us -> 10.6 us
  Pallas kernels: 28.5 us -> 31.1 us
    ppermute x2, waiting for transfers between devices: 16.3 us -> 10.1 us  [deliver(): return lax.ppermute(beside, ('dp', 'view', 'head'), pairs)]
    ppermute x6, waiting for transfers between devices: 24.9 us -> 29.3 us  [exchange(): arrived.append(lax.ppermute(slots[s], ('dp', 'view', 'head'), pairs))]
    ppermute x2, waiting for transfers between devices: 6.76 us -> 10.5 us  [deliver(): beside = lax.ppermute(total, ('dp', 'view', 'head'), pairs)]
    pallas_call x2, Pallas kernels: 8.64 us -> 5.25 us  [input_product(): pl.pallas_call(functools.partial(input_kernel, role, own_heads, shared),...]
    pallas_call x2, Pallas kernels: 7.85 us -> 11.1 us  [weight_product(): pl.pallas_call(functools.partial(weight_kernel, mine, mean_scale, own_hea...]
    unnamed x16 -> x46, local copies, waits for them, and re-layouts: 5.79 us -> 8.8 us
    ppermute x16, waiting for transfers between devices: 44.1 us -> 46.9 us  [moved(): return lax.ppermute(value, ('dp', 'view'), pairs)]
  transfers between devices with their start and end apart: 26 -> 26, of which waited for: 9 -> 12; matrix products, arithmetic and copies ran while one was open for 1% -> 1% of each run, Pallas kernels for 13% -> 9%
where the time goes in v7:
time: 177 us; the launch traced here: 176 us
  waiting for transfers between devices  96.8 us (55%)
  starting transfers between devices  35 us (20%)
  Pallas kernels  31.1 us (18%)
  local copies, waits for them, and re-layouts  10.6 us (6%)
    ppermute x16, waiting for transfers between devices, moved(): return lax.ppermute(value, ('dp', 'view'), pairs)  46.9 us
    ppermute x6, waiting for transfers between devices, exchange(): arrived.append(lax.ppermute(slots[s], ('dp', 'view', 'head'), pairs))  29.3 us
    ppermute x16, starting transfers between devices, moved(): return lax.ppermute(value, ('dp', 'view'), pairs)  17.1 us
    ppermute x6, starting transfers between devices, exchange(): arrived.append(lax.ppermute(slots[s], ('dp', 'view', 'head'), pairs))  11.3 us
    pallas_call x2, Pallas kernels, weight_product(): pl.pallas_call(functools.partial(weight_kernel, mine, mean_scale, own_hea...  11.1 us
    ppermute x2, waiting for transfers between devices, deliver(): beside = lax.ppermute(total, ('dp', 'view', 'head'), pairs)  10.5 us
    ppermute x2, waiting for transfers between devices, deliver(): return lax.ppermute(beside, ('dp', 'view', 'head'), pairs)  10.1 us
    unnamed x46, local copies, waits for them, and re-layouts  8.8 us
  transfers between devices with their start and end apart: 26, of which 12 were waited for; matrix products, arithmetic and copies ran while one was open for 1% of the time, Pallas kernels for 9%

profile of v7, /device:TPU:16, one launch (start us, length us, event | category | flops | bytes accessed | tf_op | source)
XLA Modules:
  0.0 175.7 jit_solution(15048486552923205709)
XLA Ops:
  0.6 0.6 pad_add_fusion.place_ref
  1.3 2.9 %pack_heads.1 = (bf16[2,1040,128]{2,1,0:T(8,128)(2,1)}, bf16[1,1040,128]{2,1,0:T(8,128)(2,1)}, bf16[2,1040,128]{2,1,0:T(8,128)(2,1)}, bf16[2,1040,128]{2,1,0:T(8,128)(2,1)}) custom-call(s32[4]{0:T(128)} %pad_add_fusion.place_ref, s32[1,2]{1,0:T(1,128)} %links_ref.1, bf16[256,768]{1,0:T(8,128)(2,1)} %bitcast.26, bf16[256,768]{1,0:T(8,128)(2,1)} %bitcast.27, ...), custom_call_target="tpu_custom_call" | custom-call | tf_op jit(solution)/shard_map/pack_heads/pallas_call | solution.py:215
  4.2 1.5 collective-permute-start
  5.7 0.6 collective-permute-start.1
  6.3 16.7 %collective-permute-done.2.refs_3_ = bf16[1,1040,128]{2,1,0:T(8,128)(2,1)S(1)} collective-permute-done((bf16[1,1040,128]{2,1,0:T(8,128)(2,1)}, bf16[1,1040,128]{2,1,0:T(8,128)(2,1)S(1)}, u32[]{:S(2)}, u32[]{:S(2)}) %collective-permute-start.2) | collective-permute-done | bytes 266272 | tf_op jit(solution)/shard_map/ppermute | solution.py:128
  23.1 0.7 collective-permute-start.3
  23.8 1.8 %dynamic-slice_bitcast_fusion.1 = (bf16[1,256,384]{2,1,0:T(8,128)(2,1)S(1)}, bf16[1,256,384]{2,1,0:T(8,128)(2,1)S(1)}, bf16[1,256,384]{2,1,0:T(8,128)(2,1)S(1)},...) fusion(bf16[1,1,256,3072]{3,2,1,0:T(8,128)(2,1)} %param.9, ...), kind=kLoop, calls=%fused_computation.7 | loop fusion | bytes 3145760 | tf_op jit(solution)/shard_map/stack | solution.py:545
  25.6 0.0 copy-done.19
  25.6 0.2 copy-done.20
  25.8 1.1 turn_weights.1.own_ref
  26.9 0.0 copy-start.22
  26.9 0.1 collective-permute-start.9
  26.9 0.1 pad_maximum_fusion
  27.0 1.6 collective-permute-start.4
  28.6 0.3 collective-permute-start.5
  29.0 8.0 %attention_gradients.1.refs_0_.refs_6_ = bf16[6,256,384]{2,1,0:T(8,128)(2,1)S(1)} custom-call(s32[4]{0:T(128)S(1)} %copy-done.21, bf16[2,1040,128]{2,1,0:T(8,128)(2,1)S(1)} %copy-done.22, bf16[2,1040,128]{2,1,0:T(8,128)(2,1)S(1)} %collective-permute-done.1.refs_1_, bf16[2,1040,128]{2,1,0:T(8,128)(2,1)S(1)} %collective-permute-done.refs_2_, ...), custom_call_target="tpu_custom_call" | custom-call | flops 4026531840 | bytes 3670016 | tf_op jit(solution)/shard_map/attention_gradients/pallas_call | solution.py:309
  37.0 1.2 collective-permute-done.4.refs_2_
  38.2 0.9 collective-permute-done.5.refs_3_
  39.1 1.5 collective-permute-start.7
  40.6 1.3 collective-permute-start.6
  42.0 1.3 collective-permute-start.15
  43.3 2.6 %collective-permute-done.15.refs_1_ = bf16[2,256,384]{2,1,0:T(8,128)(2,1)S(1)} collective-permute-done((bf16[2,256,384]{2,1,0:T(8,128)(2,1)S(1)}, bf16[2,256,384]{2,1,0:T(8,128)(2,1)S(1)}, u32[]{:S(2)}, u32[]{:S(2)}) %collective-permute-start.15) | collective-permute-done | bytes 393248 | tf_op jit(solution)/shard_map/ppermute | solution.py:128
  45.9 21.1 %collective-permute-done.7.refs_2_.refs_0_.refs_8_ = bf16[6,256,384]{2,1,0:T(8,128)(2,1)S(1)} collective-permute-done((bf16[6,256,384]{2,1,0:T(8,128)(2,1)S(1)}, bf16[6,256,384]{2,1,0:T(8,128)(2,1)S(1)}, u32[]{:S(2)}, u32[]{:S(2)}) %collective-permute-start.7) | collective-permute-done | bytes 1179680 | tf_op jit(solution)/shard_map/ppermute | solution.py:128
  67.0 1.4 collective-permute-start.17
  68.4 0.7 collective-permute-start.16
  69.2 0.9 join_weights.1.refs_4_
  70.1 0.0 copy-start
  70.1 4.7 %input_gradient.2 = (bf16[256,768]{1,0:T(8,128)(2,1)S(1)}, bf16[256,768]{1,0:T(8,128)(2,1)S(1)}, bf16[256,768]{1,0:T(8,128)(2,1)S(1)}, bf16[256,768]{1,0:T(8,128)(2,1)S(1)}) custom-call(s32[4]{0:T(128)S(1)} %copy-done.21, bf16[6,256,384]{2,1,0:T(8,128)(2,1)S(1)} %attention_gradients.1.refs_0_.refs_6_, ...), custom_call_target="tpu_custom_call" | custom-call | flops 3623878656 | bytes 9830400 | tf_op jit(solution)/shard_map/input_gradient/pallas_call | solution.py:404
  74.8 3.5 %collective-permute-start.10 = (bf16[256,768]{1,0:T(8,128)(2,1)S(1)}, bf16[256,768]{1,0:T(8,128)(2,1)S(1)}, u32[]{:S(2)}, u32[]{:S(2)}) collective-permute-start(bf16[256,768]{1,0:T(8,128)(2,1)S(1)} %get-tuple-element.44), channel_id=1, source_target_pairs={{0,1},{1,0},{2,3},{3,2},{8,9},{9,8},{10,11},{11,10},{16,17},{17,16... | collective-permute-start | bytes 1179656 | tf_op jit(solution)/shard_map/ppermute | solution.py:580
  78.3 2.2 %collective-permute-start.11 = (bf16[256,768]{1,0:T(8,128)(2,1)S(1)}, bf16[256,768]{1,0:T(8,128)(2,1)S(1)}, u32[]{:S(2)}, u32[]{:S(2)}) collective-permute-start(bf16[256,768]{1,0:T(8,128)(2,1)S(1)} %get-tuple-element.45), channel_id=1, source_target_pairs={{0,2},{1,3},{2,0},{3,1},{8,10},{9,11},{10,8},{11,9},{16,18},{17,19... | collective-permute-start | bytes 1179656 | tf_op jit(solution)/shard_map/ppermute | solution.py:580
  80.5 3.5 %collective-permute-start.12 = (bf16[256,768]{1,0:T(8,128)(2,1)S(1)}, bf16[256,768]{1,0:T(8,128)(2,1)S(1)}, u32[]{:S(2)}, u32[]{:S(2)}) collective-permute-start(bf16[256,768]{1,0:T(8,128)(2,1)S(1)} %get-tuple-element.46), channel_id=1, source_target_pairs={{0,3},{1,2},{2,1},{3,0},{8,11},{9,10},{10,9},{11,8},{16,19},{17,18... | collective-permute-start | bytes 1179656 | tf_op jit(solution)/shard_map/ppermute | solution.py:580
  84.0 0.6 collective-permute-done.10
  84.6 9.7 %collective-permute-done.11 = bf16[256,768]{1,0:T(8,128)(2,1)S(1)} collective-permute-done((bf16[256,768]{1,0:T(8,128)(2,1)S(1)}, bf16[256,768]{1,0:T(8,128)(2,1)S(1)}, u32[]{:S(2)}, u32[]{:S(2)}) %collective-permute-start.11) | collective-permute-done | bytes 393248 | tf_op jit(solution)/shard_map/ppermute | solution.py:580
  94.3 19.0 %collective-permute-done.12 = bf16[256,768]{1,0:T(8,128)(2,1)S(1)} collective-permute-done((bf16[256,768]{1,0:T(8,128)(2,1)S(1)}, bf16[256,768]{1,0:T(8,128)(2,1)S(1)}, u32[]{:S(2)}, u32[]{:S(2)}) %collective-permute-start.12) | collective-permute-done | bytes 393248 | tf_op jit(solution)/shard_map/ppermute | solution.py:580
  113.3 0.2 add_convert_fusion.1
  113.5 0.0 copy-start.2
  113.5 0.0 copy-start.4
  113.6 0.6 input_gradient.3
  114.1 0.7 collective-permute-start.18
  114.8 0.7 collective-permute-start.19
  115.5 0.7 collective-permute-start.20
  116.2 1.3 collective-permute-start.24
  117.6 0.7 collective-permute-start.23
  118.3 0.2 add_convert_fusion
  118.5 4.3 %collective-permute-done.24.refs_5_ = bf16[2,256,384]{2,1,0:T(8,128)(2,1)S(1)} collective-permute-done((bf16[2,256,384]{2,1,0:T(8,128)(2,1)S(1)}, bf16[2,256,384]{2,1,0:T(8,128)(2,1)S(1)}, u32[]{:S(2)}, u32[]{:S(2)}) %collective-permute-start.24) | collective-permute-done | bytes 393248 | tf_op jit(solution)/shard_map/ppermute | solution.py:128
  122.9 4.7 %weight_gradient_mate.1 = f32[3,384,768]{2,1,0:T(8,128)} custom-call(s32[4]{0:T(128)S(1)} %copy-done.21, bf16[2,256,384]{2,1,0:T(8,128)(2,1)S(1)} %pad_maximum_fusion.2.refs_0_, bf16[2,256,384]{2,1,0:T(8,128)(2,1)S(1)} %collective-permute-done.15.refs_1_, bf16[2,256,384]{2,1,0:T(8,128)(2,1)S(1)} %collective-permute-done.4.refs_2_, ...), custom_call_target="tpu_custom_call" | custom-call | flops 1811939328 | bytes 9043968 | tf_op jit(solution)/shard_map/weight_gradient_mate/pallas_call | solution.py:457
  127.6 4.0 %collective-permute-start.25 = (f32[3,384,768]{2,1,0:T(8,128)}, f32[3,384,768]{2,1,0:T(8,128)}, u32[]{:S(2)}, u32[]{:S(2)}) collective-permute-start(f32[3,384,768]{2,1,0:T(8,128)} %weight_gradient_mate.1), channel_id=1, source_target_pairs={{0,4},{4,0},{8,12},{12,8},{16,20},{20,16},{24,28},{28,24},{1,5},{5... | collective-permute-start | bytes 10616840 | tf_op jit(solution)/shard_map/ppermute | solution.py:128
  131.6 1.9 %collective-permute-start.13 = (bf16[256,768]{1,0:T(8,128)(2,1)S(1)}, bf16[256,768]{1,0:T(8,128)(2,1)}, u32[]{:S(2)}, u32[]{:S(2)}) collective-permute-start(bf16[256,768]{1,0:T(8,128)(2,1)S(1)} %add_convert_fusion.1), channel_id=1, source_target_pairs={{0,0},{1,5},{2,10},{3,15},{8,8},{9,13},{10,2},{11,7},{16,16},{17,2... | collective-permute-start | bytes 1179656 | tf_op jit(solution)/shard_map/ppermute | solution.py:592
  133.5 1.4 collective-permute-start.21
  134.9 10.5 %collective-permute-done.13 = bf16[256,768]{1,0:T(8,128)(2,1)} collective-permute-done((bf16[256,768]{1,0:T(8,128)(2,1)S(1)}, bf16[256,768]{1,0:T(8,128)(2,1)}, u32[]{:S(2)}, u32[]{:S(2)}) %collective-permute-start.13) | collective-permute-done | bytes 393248 | tf_op jit(solution)/shard_map/ppermute | solution.py:592
  145.4 2.1 %collective-permute-start.14 = (bf16[256,768]{1,0:T(8,128)(2,1)}, bf16[256,768]{1,0:T(8,128)(2,1)}, u32[]{:S(2)}, u32[]{:S(2)}) collective-permute-start(bf16[256,768]{1,0:T(8,128)(2,1)} %collective-permute-done.13), channel_id=1, source_target_pairs={{0,0},{5,4},{10,8},{15,12},{8,9},{13,13},{2,1},{7,5},{16,18},{21,2... | collective-permute-start | bytes 1179656 | tf_op jit(solution)/shard_map/ppermute | solution.py:598
  147.5 1.3 collective-permute-start.22
  148.8 3.5 %collective-permute-done.14.first_ref = bf16[256,768]{1,0:T(8,128)(2,1)} collective-permute-done((bf16[256,768]{1,0:T(8,128)(2,1)}, bf16[256,768]{1,0:T(8,128)(2,1)}, u32[]{:S(2)}, u32[]{:S(2)}) %collective-permute-start.14) | collective-permute-done | bytes 393248 | tf_op jit(solution)/shard_map/ppermute | solution.py:598
  152.3 6.6 %collective-permute-done.22.second_ref = bf16[256,768]{1,0:T(8,128)(2,1)} collective-permute-done((bf16[256,768]{1,0:T(8,128)(2,1)}, bf16[256,768]{1,0:T(8,128)(2,1)}, u32[]{:S(2)}, u32[]{:S(2)}) %collective-permute-start.22) | collective-permute-done | bytes 393248 | tf_op jit(solution)/shard_map/ppermute | solution.py:598
  158.9 1.9 %choose_block.1 = bf16[256,768]{1,0:T(8,128)(2,1)} custom-call(s32[1]{0:T(128)} %bitcast.which_ref, bf16[256,768]{1,0:T(8,128)(2,1)} %collective-permute-done.14.first_ref, bf16[256,768]{1,0:T(8,128)(2,1)} %collective-permute-done.22.second_ref), custom_call_target="tpu_custom_call" | custom-call | tf_op jit(solution)/shard_map/choose_block/pallas_call | solution.py:482
  160.8 1.3 copy-done.3
  162.1 1.3 copy-done.5
  163.4 1.0 copy-done.7
  164.4 1.0 copy-done.9
  165.3 1.0 copy-done.11
  166.3 1.0 copy-done.13
  167.3 1.0 copy-done.15
  168.3 1.0 copy-done.17
  169.3 6.4 %weight_gradient_own.1 = (f32[384,768]{1,0:T(8,128)}, f32[384,768]{1,0:T(8,128)}, f32[384,768]{1,0:T(8,128)}) custom-call(s32[4]{0:T(128)S(1)} %copy-done.21, bf16[2,256,384]{2,1,0:T(8,128)(2,1)S(1)} %copy-done.7, bf16[2,256,384]{2,1,0:T(8,128)(2,1)S(1)} %copy-done.13, bf16[2,256,384]{2,1,0:T(8,128)(2,1)S(1)} %copy-done.9, ...), custom_call_target="tpu_custom_call" | custom-call | flops 1811939328 | bytes 9043968 | tf_op jit(solution)/shard_map/weight_gradient_own/pallas_call | solution.py:457
  (50 shorter events, 0.2 us)
Async XLA Ops:
  4.2 18.9 %collective-permute-start = (bf16[2,1040,128]{2,1,0:T(8,128)(2,1)}, bf16[2,1040,128]{2,1,0:T(8,128)(2,1)S(1)}, u32[]{:S(2)}, u32[]{:S(2)}) collective-permute-start(bf16[2,1040,128]{2,1,0:T(8,128)(2,1)} %get-tuple-element.31), channel_id=1, source_target_pairs={{0,8},{4,12},{8,0},{12,4},{16,24},{20,28},{24,16},{28,20},{1,9},{5... | collective-permute-start | bytes 1597448 | tf_op jit(solution)/shard_map/ppermute | solution.py:128
  5.7 17.4 %collective-permute-start.2 = (bf16[1,1040,128]{2,1,0:T(8,128)(2,1)}, bf16[1,1040,128]{2,1,0:T(8,128)(2,1)S(1)}, u32[]{:S(2)}, u32[]{:S(2)}) collective-permute-start(bf16[1,1040,128]{2,1,0:T(8,128)(2,1)} %get-tuple-element.38), channel_id=1, source_target_pairs={{0,12},{4,8},{8,4},{12,0},{16,28},{20,24},{24,20},{28,16},{1,13},{... | collective-permute-start | bytes 798728 | tf_op jit(solution)/shard_map/ppermute | solution.py:128
  5.7 23.3 %collective-permute-start.1 = (bf16[2,1040,128]{2,1,0:T(8,128)(2,1)}, bf16[2,1040,128]{2,1,0:T(8,128)(2,1)S(1)}, u32[]{:S(2)}, u32[]{:S(2)}) collective-permute-start(bf16[2,1040,128]{2,1,0:T(8,128)(2,1)} %get-tuple-element.37), channel_id=1, source_target_pairs={{0,4},{4,0},{8,12},{12,8},{16,20},{20,16},{24,28},{28,24},{1,5},{5... | collective-permute-start | bytes 1597448 | tf_op jit(solution)/shard_map/ppermute | solution.py:128
  23.1 5.9 %collective-permute-start.3 = (bf16[2,1040,128]{2,1,0:T(8,128)(2,1)S(1)}, bf16[2,1040,128]{2,1,0:T(8,128)(2,1)S(1)}, u32[]{:S(2)}, u32[]{:S(2)}) collective-permute-start(bf16[2,1040,128]{2,1,0:T(8,128)(2,1)S(1)} %collective-permute-done.refs_2_), channel_id=1, source_target_pairs={{0,4},{4,0},{8,12},{12,8},{16,20},{20,16},{24,28},{28,24},{1,5},{5... | collective-permute-start | bytes 1597448 | tf_op jit(solution)/shard_map/ppermute | solution.py:128
  23.8 1.8 %copy-start.18 = (bf16[384,768]{1,0:T(8,128)(2,1)S(1)}, bf16[384,768]{1,0:T(8,128)(2,1)}, u32[]{:S(2)}) copy-start(bf16[384,768]{1,0:T(8,128)(2,1)} %q_ref) | copy-start | bytes 1769476
  23.8 1.8 %copy-start.19 = (bf16[384,768]{1,0:T(8,128)(2,1)S(1)}, bf16[384,768]{1,0:T(8,128)(2,1)}, u32[]{:S(2)}) copy-start(bf16[384,768]{1,0:T(8,128)(2,1)} %k_ref) | copy-start | bytes 1769476
  23.8 2.0 %copy-start.20 = (bf16[384,768]{1,0:T(8,128)(2,1)S(1)}, bf16[384,768]{1,0:T(8,128)(2,1)}, u32[]{:S(2)}) copy-start(bf16[384,768]{1,0:T(8,128)(2,1)} %v_ref) | copy-start | bytes 1769476
  23.8 2.0 %copy-start.21 = (s32[4]{0:T(128)S(1)}, s32[4]{0:T(128)}, u32[]{:S(2)}) copy-start(s32[4]{0:T(128)} %pad_add_fusion.place_ref) | copy-start | bytes 52
  26.9 2.1 %copy-start.22 = (bf16[2,1040,128]{2,1,0:T(8,128)(2,1)S(1)}, bf16[2,1040,128]{2,1,0:T(8,128)(2,1)}, u32[]{:S(2)}) copy-start(bf16[2,1040,128]{2,1,0:T(8,128)(2,1)} %get-tuple-element.36.refs_0_) | copy-start | bytes 1597444
  26.9 42.3 %collective-permute-start.9 = (bf16[2304,384]{1,0:T(8,128)(2,1)S(1)}, bf16[2304,384]{1,0:T(8,128)(2,1)S(1)}, u32[]{:S(2)}, u32[]{:S(2)}) collective-permute-start(bf16[2304,384]{1,0:T(8,128)(2,1)S(1)} %turn_weights.1.own_ref), channel_id=1, source_target_pairs={{0,4},{4,0},{8,12},{12,8},{16,20},{20,16},{24,28},{28,24},{1,5},{5... | collective-permute-start | bytes 5308424 | tf_op jit(solution)/shard_map/ppermute | solution.py:128
  27.0 11.2 %collective-permute-start.4 = (bf16[2,256,384]{2,1,0:T(8,128)(2,1)S(1)}, bf16[2,256,384]{2,1,0:T(8,128)(2,1)S(1)}, u32[]{:S(2)}, u32[]{:S(2)}) collective-permute-start(bf16[2,256,384]{2,1,0:T(8,128)(2,1)S(1)} %get-tuple-element.40), channel_id=1, source_target_pairs={{0,8},{4,20},{8,0},{12,28},{16,24},{20,4},{24,16},{28,12},{1,9},{5... | collective-permute-start | bytes 1179656 | tf_op jit(solution)/shard_map/ppermute | solution.py:128
  28.6 10.5 %collective-permute-start.5 = (bf16[2,256,384]{2,1,0:T(8,128)(2,1)S(1)}, bf16[2,256,384]{2,1,0:T(8,128)(2,1)S(1)}, u32[]{:S(2)}, u32[]{:S(2)}) collective-permute-start(bf16[2,256,384]{2,1,0:T(8,128)(2,1)S(1)} %get-tuple-element.41), channel_id=1, source_target_pairs={{0,20},{4,8},{8,28},{12,0},{16,4},{20,24},{24,12},{28,16},{1,21},{... | collective-permute-start | bytes 1179656 | tf_op jit(solution)/shard_map/ppermute | solution.py:128
  38.2 84.6 %copy-start.8 = (bf16[2,256,384]{2,1,0:T(8,128)(2,1)}, bf16[2,256,384]{2,1,0:T(8,128)(2,1)S(1)}, u32[]{:S(2)}) copy-start(bf16[2,256,384]{2,1,0:T(8,128)(2,1)S(1)} %collective-permute-done.4.refs_2_) | copy-start | bytes 1179652
  39.1 83.7 %copy-start.10 = (bf16[2,256,384]{2,1,0:T(8,128)(2,1)}, bf16[2,256,384]{2,1,0:T(8,128)(2,1)S(1)}, u32[]{:S(2)}) copy-start(bf16[2,256,384]{2,1,0:T(8,128)(2,1)S(1)} %collective-permute-done.5.refs_3_) | copy-start | bytes 1179652
  39.1 27.9 %collective-permute-start.7 = (bf16[6,256,384]{2,1,0:T(8,128)(2,1)S(1)}, bf16[6,256,384]{2,1,0:T(8,128)(2,1)S(1)}, u32[]{:S(2)}, u32[]{:S(2)}) collective-permute-start(bf16[6,256,384]{2,1,0:T(8,128)(2,1)S(1)} %attention_gradients.1.refs_0_.refs_6_), channel_id=1, source_target_pairs={{0,8},{4,20},{8,0},{12,28},{16,24},{20,4},{24,16},{28,12},{1,9},{5... | collective-permute-start | bytes 3538952 | tf_op jit(solution)/shard_map/ppermute | solution.py:128
  40.6 29.4 %collective-permute-start.8 = (bf16[6,256,384]{2,1,0:T(8,128)(2,1)S(1)}, bf16[6,256,384]{2,1,0:T(8,128)(2,1)S(1)}, u32[]{:S(2)}, u32[]{:S(2)}) collective-permute-start(bf16[6,256,384]{2,1,0:T(8,128)(2,1)S(1)} %attention_gradients.1.refs_0_.refs_6_), channel_id=1, source_target_pairs={{0,20},{4,8},{8,28},{12,0},{16,4},{20,24},{24,12},{28,16},{1,21},{... | collective-permute-start | bytes 3538952 | tf_op jit(solution)/shard_map/ppermute | solution.py:128
  40.6 29.4 %collective-permute-start.6 = (bf16[6,256,384]{2,1,0:T(8,128)(2,1)S(1)}, bf16[6,256,384]{2,1,0:T(8,128)(2,1)S(1)}, u32[]{:S(2)}, u32[]{:S(2)}) collective-permute-start(bf16[6,256,384]{2,1,0:T(8,128)(2,1)S(1)} %attention_gradients.1.refs_0_.refs_6_), channel_id=1, source_target_pairs={{4,0},{12,8},{20,16},{28,24},{5,1},{13,9},{21,17},{29,25},{6,2},{1... | collective-permute-start | bytes 3538952 | tf_op jit(solution)/shard_map/ppermute | solution.py:128
  42.0 80.9 %copy-start.6 = (bf16[2,256,384]{2,1,0:T(8,128)(2,1)}, bf16[2,256,384]{2,1,0:T(8,128)(2,1)S(1)}, u32[]{:S(2)}) copy-start(bf16[2,256,384]{2,1,0:T(8,128)(2,1)S(1)} %pad_maximum_fusion.2.refs_0_) | copy-start | bytes 1179652
  42.0 3.9 %collective-permute-start.15 = (bf16[2,256,384]{2,1,0:T(8,128)(2,1)S(1)}, bf16[2,256,384]{2,1,0:T(8,128)(2,1)S(1)}, u32[]{:S(2)}, u32[]{:S(2)}) collective-permute-start(bf16[2,256,384]{2,1,0:T(8,128)(2,1)S(1)} %pad_maximum_fusion.2.refs_0_), channel_id=1, source_target_pairs={{4,0},{12,8},{20,16},{28,24},{5,1},{13,9},{21,17},{29,25},{6,2},{1... | collective-permute-start | bytes 1179656 | tf_op jit(solution)/shard_map/ppermute | solution.py:128
  45.9 76.9 %copy-start.12 = (bf16[2,256,384]{2,1,0:T(8,128)(2,1)}, bf16[2,256,384]{2,1,0:T(8,128)(2,1)S(1)}, u32[]{:S(2)}) copy-start(bf16[2,256,384]{2,1,0:T(8,128)(2,1)S(1)} %collective-permute-done.15.refs_1_) | copy-start | bytes 1179652
  67.0 46.5 %collective-permute-start.17 = (bf16[6,256,384]{2,1,0:T(8,128)(2,1)S(1)}, bf16[6,256,384]{2,1,0:T(8,128)(2,1)S(1)}, u32[]{:S(2)}, u32[]{:S(2)}) collective-permute-start(bf16[6,256,384]{2,1,0:T(8,128)(2,1)S(1)} %collective-permute-done.7.refs_2_.refs_0_.refs_8_), channel_id=1, source_target_pairs={{0,20},{8,28},{16,4},{24,12},{1,21},{9,29},{17,5},{25,13},{2,22},{... | collective-permute-start | bytes 3538952 | tf_op jit(solution)/shard_map/ppermute | solution.py:128
  68.4 45.1 %collective-permute-start.16 = (bf16[6,256,384]{2,1,0:T(8,128)(2,1)S(1)}, bf16[6,256,384]{2,1,0:T(8,128)(2,1)S(1)}, u32[]{:S(2)}, u32[]{:S(2)}) collective-permute-start(bf16[6,256,384]{2,1,0:T(8,128)(2,1)S(1)} %collective-permute-done.7.refs_2_.refs_0_.refs_8_), channel_id=1, source_target_pairs={{4,12},{12,4},{20,28},{28,20},{5,13},{13,5},{21,29},{29,21},{6,14}... | collective-permute-start | bytes 3538952 | tf_op jit(solution)/shard_map/ppermute | solution.py:128
  70.1 52.8 %copy-start = (bf16[6,256,384]{2,1,0:T(8,128)(2,1)}, bf16[6,256,384]{2,1,0:T(8,128)(2,1)S(1)}, u32[]{:S(2)}) copy-start(bf16[6,256,384]{2,1,0:T(8,128)(2,1)S(1)} %collective-permute-done.6.refs_1_.refs_7_) | copy-start | bytes 3538948
  74.8 9.8 %collective-permute-start.10 = (bf16[256,768]{1,0:T(8,128)(2,1)S(1)}, bf16[256,768]{1,0:T(8,128)(2,1)S(1)}, u32[]{:S(2)}, u32[]{:S(2)}) collective-permute-start(bf16[256,768]{1,0:T(8,128)(2,1)S(1)} %get-tuple-element.44), channel_id=1, source_target_pairs={{0,1},{1,0},{2,3},{3,2},{8,9},{9,8},{10,11},{11,10},{16,17},{17,16... | collective-permute-start | bytes 1179656 | tf_op jit(solution)/shard_map/ppermute | solution.py:580
  78.3 16.0 %collective-permute-start.11 = (bf16[256,768]{1,0:T(8,128)(2,1)S(1)}, bf16[256,768]{1,0:T(8,128)(2,1)S(1)}, u32[]{:S(2)}, u32[]{:S(2)}) collective-permute-start(bf16[256,768]{1,0:T(8,128)(2,1)S(1)} %get-tuple-element.45), channel_id=1, source_target_pairs={{0,2},{1,3},{2,0},{3,1},{8,10},{9,11},{10,8},{11,9},{16,18},{17,19... | collective-permute-start | bytes 1179656 | tf_op jit(solution)/shard_map/ppermute | solution.py:580
  80.5 32.8 %collective-permute-start.12 = (bf16[256,768]{1,0:T(8,128)(2,1)S(1)}, bf16[256,768]{1,0:T(8,128)(2,1)S(1)}, u32[]{:S(2)}, u32[]{:S(2)}) collective-permute-start(bf16[256,768]{1,0:T(8,128)(2,1)S(1)} %get-tuple-element.46), channel_id=1, source_target_pairs={{0,3},{1,2},{2,1},{3,0},{8,11},{9,10},{10,9},{11,8},{16,19},{17,18... | collective-permute-start | bytes 1179656 | tf_op jit(solution)/shard_map/ppermute | solution.py:580
  113.5 9.4 %copy-start.2 = (bf16[6,256,384]{2,1,0:T(8,128)(2,1)}, bf16[6,256,384]{2,1,0:T(8,128)(2,1)S(1)}, u32[]{:S(2)}) copy-start(bf16[6,256,384]{2,1,0:T(8,128)(2,1)S(1)} %collective-permute-done.17.refs_3_.refs_11_) | copy-start | bytes 3538948
  113.5 9.3 %copy-start.4 = (bf16[6,256,384]{2,1,0:T(8,128)(2,1)}, bf16[6,256,384]{2,1,0:T(8,128)(2,1)S(1)}, u32[]{:S(2)}) copy-start(bf16[6,256,384]{2,1,0:T(8,128)(2,1)S(1)} %collective-permute-done.16.refs_2_.refs_10_) | copy-start | bytes 3538948
  114.1 4.2 %collective-permute-start.18 = (bf16[256,768]{1,0:T(8,128)(2,1)S(1)}, bf16[256,768]{1,0:T(8,128)(2,1)S(1)}, u32[]{:S(2)}, u32[]{:S(2)}) collective-permute-start(bf16[256,768]{1,0:T(8,128)(2,1)S(1)} %get-tuple-element.50), channel_id=1, source_target_pairs={{4,5},{5,4},{6,7},{7,6},{12,13},{13,12},{14,15},{15,14},{20,21},{2... | collective-permute-start | bytes 1179656 | tf_op jit(solution)/shard_map/ppermute | solution.py:580
  114.8 3.5 %collective-permute-start.19 = (bf16[256,768]{1,0:T(8,128)(2,1)S(1)}, bf16[256,768]{1,0:T(8,128)(2,1)S(1)}, u32[]{:S(2)}, u32[]{:S(2)}) collective-permute-start(bf16[256,768]{1,0:T(8,128)(2,1)S(1)} %get-tuple-element.51), channel_id=1, source_target_pairs={{4,6},{5,7},{6,4},{7,5},{12,14},{13,15},{14,12},{15,13},{20,22},{2... | collective-permute-start | bytes 1179656 | tf_op jit(solution)/shard_map/ppermute | solution.py:580
  115.5 2.8 %collective-permute-start.20 = (bf16[256,768]{1,0:T(8,128)(2,1)S(1)}, bf16[256,768]{1,0:T(8,128)(2,1)S(1)}, u32[]{:S(2)}, u32[]{:S(2)}) collective-permute-start(bf16[256,768]{1,0:T(8,128)(2,1)S(1)} %get-tuple-element.52), channel_id=1, source_target_pairs={{4,7},{5,6},{6,5},{7,4},{12,15},{13,14},{14,13},{15,12},{20,23},{2... | collective-permute-start | bytes 1179656 | tf_op jit(solution)/shard_map/ppermute | solution.py:580
  116.2 6.6 %collective-permute-start.24 = (bf16[2,256,384]{2,1,0:T(8,128)(2,1)S(1)}, bf16[2,256,384]{2,1,0:T(8,128)(2,1)S(1)}, u32[]{:S(2)}, u32[]{:S(2)}) collective-permute-start(bf16[2,256,384]{2,1,0:T(8,128)(2,1)S(1)} %pad_maximum_fusion.3), channel_id=1, source_target_pairs={{0,28},{8,20},{16,12},{24,4},{1,29},{9,21},{17,13},{25,5},{2,30},{... | collective-permute-start | bytes 1179656 | tf_op jit(solution)/shard_map/ppermute | solution.py:128
  117.6 5.3 %collective-permute-start.23 = (bf16[2,256,384]{2,1,0:T(8,128)(2,1)S(1)}, bf16[2,256,384]{2,1,0:T(8,128)(2,1)S(1)}, u32[]{:S(2)}, u32[]{:S(2)}) collective-permute-start(bf16[2,256,384]{2,1,0:T(8,128)(2,1)S(1)} %pad_maximum_fusion.3), channel_id=1, source_target_pairs={{4,28},{12,20},{20,12},{28,4},{5,29},{13,21},{21,13},{29,5},{6,30}... | collective-permute-start | bytes 1179656 | tf_op jit(solution)/shard_map/ppermute | solution.py:128
  122.8 4.8 %copy-start.14 = (bf16[2,256,384]{2,1,0:T(8,128)(2,1)}, bf16[2,256,384]{2,1,0:T(8,128)(2,1)S(1)}, u32[]{:S(2)}) copy-start(bf16[2,256,384]{2,1,0:T(8,128)(2,1)S(1)} %collective-permute-done.24.refs_5_) | copy-start | bytes 1179652
  122.9 4.7 %copy-start.16 = (bf16[2,256,384]{2,1,0:T(8,128)(2,1)}, bf16[2,256,384]{2,1,0:T(8,128)(2,1)S(1)}, u32[]{:S(2)}) copy-start(bf16[2,256,384]{2,1,0:T(8,128)(2,1)S(1)} %collective-permute-done.23.refs_4_) | copy-start | bytes 1179652
  127.6 33.2 %collective-permute-start.25 = (f32[3,384,768]{2,1,0:T(8,128)}, f32[3,384,768]{2,1,0:T(8,128)}, u32[]{:S(2)}, u32[]{:S(2)}) collective-permute-start(f32[3,384,768]{2,1,0:T(8,128)} %weight_gradient_mate.1), channel_id=1, source_target_pairs={{0,4},{4,0},{8,12},{12,8},{16,20},{20,16},{24,28},{28,24},{1,5},{5... | collective-permute-start | bytes 10616840 | tf_op jit(solution)/shard_map/ppermute | solution.py:128
  131.6 13.9 %collective-permute-start.13 = (bf16[256,768]{1,0:T(8,128)(2,1)S(1)}, bf16[256,768]{1,0:T(8,128)(2,1)}, u32[]{:S(2)}, u32[]{:S(2)}) collective-permute-start(bf16[256,768]{1,0:T(8,128)(2,1)S(1)} %add_convert_fusion.1), channel_id=1, source_target_pairs={{0,0},{1,5},{2,10},{3,15},{8,8},{9,13},{10,2},{11,7},{16,16},{17,2... | collective-permute-start | bytes 1179656 | tf_op jit(solution)/shard_map/ppermute | solution.py:592
  133.5 14.0 %collective-permute-start.21 = (bf16[256,768]{1,0:T(8,128)(2,1)S(1)}, bf16[256,768]{1,0:T(8,128)(2,1)}, u32[]{:S(2)}, u32[]{:S(2)}) collective-permute-start(bf16[256,768]{1,0:T(8,128)(2,1)S(1)} %add_convert_fusion), channel_id=1, source_target_pairs={{4,20},{5,17},{6,30},{7,27},{12,28},{13,25},{14,22},{15,19},{20,4}... | collective-permute-start | bytes 1179656 | tf_op jit(solution)/shard_map/ppermute | solution.py:592
  145.4 6.9 %collective-permute-start.14 = (bf16[256,768]{1,0:T(8,128)(2,1)}, bf16[256,768]{1,0:T(8,128)(2,1)}, u32[]{:S(2)}, u32[]{:S(2)}) collective-permute-start(bf16[256,768]{1,0:T(8,128)(2,1)} %collective-permute-done.13), channel_id=1, source_target_pairs={{0,0},{5,4},{10,8},{15,12},{8,9},{13,13},{2,1},{7,5},{16,18},{21,2... | collective-permute-start | bytes 1179656 | tf_op jit(solution)/shard_map/ppermute | solution.py:598
  147.5 11.4 %collective-permute-start.22 = (bf16[256,768]{1,0:T(8,128)(2,1)}, bf16[256,768]{1,0:T(8,128)(2,1)}, u32[]{:S(2)}, u32[]{:S(2)}) collective-permute-start(bf16[256,768]{1,0:T(8,128)(2,1)} %collective-permute-done.21), channel_id=1, source_target_pairs={{20,20},{17,16},{30,28},{27,24},{28,29},{25,25},{22,21},{19,17},{4... | collective-permute-start | bytes 1179656 | tf_op jit(solution)/shard_map/ppermute | solution.py:598
  148.8 12.0 %copy-start.1 = (bf16[6,256,384]{2,1,0:T(8,128)(2,1)S(1)}, bf16[6,256,384]{2,1,0:T(8,128)(2,1)}, u32[]{:S(2)}) copy-start(bf16[6,256,384]{2,1,0:T(8,128)(2,1)} %copy-done) | copy-start | bytes 3538948
  160.8 1.3 copy-start.3
  162.1 1.3 copy-start.5
  163.4 1.0 copy-start.7
  164.3 1.0 copy-start.9
  165.3 1.0 copy-start.11
  166.3 1.0 copy-start.13
  167.3 1.0 copy-start.15
  168.3 1.0 copy-start.17

commit v8 on v7

--- a/solution.py
+++ b/solution.py
@@ -313,7 +313,7 @@
         out_specs=whole(),
         scratch_shapes=[pltpu.VMEM((6 * length, HD), jnp.bfloat16)] * 2
         + [pltpu.VMEM((6 * length, HD), jnp.float32)] * 2,
-        compiler_params=pltpu.CompilerParams(vmem_limit_bytes=20 * MIB),
+        compiler_params=pltpu.CompilerParams(vmem_limit_bytes=12 * MIB),
         cost_estimate=pl.CostEstimate(
             flops=heads * 4 * 5 * 2 * length * 3 * length * HD * 2,
             bytes_accessed=heads * 2 * length * 7 * HD * 4,
@@ -383,31 +383,35 @@
     return sides
 
 
-def input_kernel(role, own_heads, shared, place_ref, *refs):
-    grad_refs, weights, out_refs, total = refs[:4], refs[4], refs[5:-1], refs[-1]
+def input_kernel(own_heads, shared, place_ref, *refs):
+    grad_refs, weights, out_refs, total = refs[:6], refs[6], refs[7:-1], refs[-1]
+    made, inward, ahead, aside, relay_x, relay_y = grad_refs
+    grads = ((made, inward, ahead, aside), (ahead, aside, relay_x, relay_y))
     length = out_refs[0].shape[0]
-
-    @pl.when(place_ref[CORE] == role)
-    def _():
-        left = jnp.concatenate(gathered(role, own_heads, shared, grad_refs), axis=1)
-        for e in range(4):
-            product = dot(left[e * length : (e + 1) * length], weights[...])
-            total[e] = product.astype(total.dtype)
-        for s, out_ref in enumerate(out_refs):
-            out_ref[...] = total[jnp.bitwise_xor(place_ref[PLANE], s)]
-
-
-def input_product(place, role, own_heads, shared, grads, weights):
+    for role in range(2):
+
+        @pl.when(place_ref[CORE] == role)
+        def _():
+            left = jnp.concatenate(gathered(role, own_heads, shared, grads[role]), axis=1)
+            for e in range(4):
+                product = dot(left[e * length : (e + 1) * length], weights[...])
+                total[e] = product.astype(total.dtype)
+
+    for s, out_ref in enumerate(out_refs):
+        out_ref[...] = total[jnp.bitwise_xor(place_ref[PLANE], s)]
+
+
+def input_product(place, own_heads, shared, grads, weights):
     _, length, _ = grads[0].shape
     depth, rows = weights.shape
     out = jax.ShapeDtypeStruct((length, rows), jnp.bfloat16)
     return pl.pallas_call(
-        functools.partial(input_kernel, role, own_heads, shared),
+        functools.partial(input_kernel, own_heads, shared),
         out_shape=[out] * 4,
-        in_specs=[whole(pltpu.SMEM)] + [whole()] * 5,
+        in_specs=[whole(pltpu.SMEM)] + [whole()] * 7,
         out_specs=[whole()] * 4,
         scratch_shapes=[pltpu.VMEM((4, length, rows), jnp.bfloat16)],
-        compiler_params=pltpu.CompilerParams(vmem_limit_bytes=28 * MIB),
+        compiler_params=pltpu.CompilerParams(vmem_limit_bytes=24 * MIB),
         cost_estimate=pl.CostEstimate(
             flops=8 * length * rows * depth,
             bytes_accessed=8 * length * (rows + depth) + 2 * rows * depth,
@@ -460,7 +464,7 @@
         in_specs=[whole(pltpu.SMEM)] + [whole()] * (12 + len(received)),
         out_specs=[whole()] * 3 if mine else whole(),
         scratch_shapes=[pltpu.VMEM((rows, 4 * length), jnp.bfloat16)],
-        compiler_params=pltpu.CompilerParams(vmem_limit_bytes=36 * MIB),
+        compiler_params=pltpu.CompilerParams(vmem_limit_bytes=24 * MIB),
         cost_estimate=pl.CostEstimate(
             flops=8 * rows * 3 * cols * length,
             bytes_accessed=8 * length * (rows + 3 * cols) + 12 * rows * cols,
@@ -468,25 +472,6 @@
         ),
         name="weight_gradient_own" if mine else "weight_gradient_mate",
     )(place, *tokens, *grads, *received)
-
-
-def choose_kernel(which_ref, first_ref, second_ref, out_ref):
-    for which, ref in enumerate((first_ref, second_ref)):
-
-        @pl.when(which_ref[0] == which)
-        def _():
-            out_ref[...] = ref[...]
-
-
-def chosen_of(which, first, second):
-    return pl.pallas_call(
-        choose_kernel,
-        out_shape=jax.ShapeDtypeStruct(first.shape, first.dtype),
-        in_specs=[whole(pltpu.SMEM)] + [whole()] * 2,
-        out_specs=whole(),
-        compiler_params=pltpu.CompilerParams(vmem_limit_bytes=8 * MIB),
-        name="choose_block",
-    )(which, first, second)
 
 
 def gather_body(
@@ -558,51 +543,21 @@
     (turn,) = after((place,), own_weights)
     made = attention(turn, own_heads, (own, mate_in, x_in, cross_in, mate_x_in))
     (made,) = after((made,), normed_ahead, normed_aside)
+    ahead = moved(made, straight)
+    inward = moved(made, only(1, mate))
+    (sent,) = after((made,), ahead)
+    aside = moved(sent, crossed)
+    relay_x = moved(ahead, only(1, along_x))
+    relay_y = moved(ahead, only(0, across_y))
     weights = joined_weights(place, own_weights, moved(own_weights, mate))
-    ahead = moved(made, straight)
-    aside = moved(made, crossed)
-    inward = moved(made, only(1, mate))
-    (sent,) = after((ahead,), mate_here)
-    relay_x = moved(sent, only(1, along_x))
-    relay_y = moved(sent, only(0, across_y))
-    first = (made, inward, ahead, aside)
-    second = (ahead, aside, relay_x, relay_y)
-
-    def exchange(role, slots):
-        arrived = []
-        for s in range(1, groups):
-            pairs = [
-                ((y * views + v) * groups + z, (y * views + v) * groups + (z ^ s))
-                for y in range(prompts)
-                for v in range(role, views, 2)
-                for z in range(groups)
-            ]
-            arrived.append(lax.ppermute(slots[s], ("dp", "view", "head"), pairs))
-        total = sum(array.astype(jnp.float32) for array in (slots[0], *arrived))
-        return total.astype(jnp.bfloat16), arrived
-
-    def deliver(role, total, *earlier):
-        def spot(y, v, z):
-            return (y * views + v) * groups + z
-
-        corners = [
-            (y, v, z) for y in range(prompts) for v in range(role, views, 2) for z in range(groups)
-        ]
-        pairs = [(spot(y, v, z), spot(y ^ role, v ^ z, z)) for y, v, z in corners]
-        beside = lax.ppermute(total, ("dp", "view", "head"), pairs)
-        pairs = [
-            (spot(y ^ role, v ^ z, z), spot(y ^ role, v ^ z, y * (views // 2) + v // 2))
-            for y, v, z in corners
-        ]
-        (beside,) = after((beside,), *earlier)
-        return lax.ppermute(beside, ("dp", "view", "head"), pairs)
-
-    first_slots = input_product(place, 0, own_heads, shared, first, weights)
-    first_total, _ = exchange(0, first_slots)
-    (turn,) = after((place,), first_total)
-    second_slots = input_product(turn, 1, own_heads, shared, second, weights)
-    second_total, arrived = exchange(1, second_slots)
-    (to_corner,) = after((to_corner,), *second_slots)
+    grads = (made, inward, ahead, aside, relay_x, relay_y)
+
+    slots = input_product(place, own_heads, shared, grads, weights)
+    arrived = [
+        lax.ppermute(slots[s], "head", [(z, z ^ s) for z in range(groups)])
+        for s in range(1, groups)
+    ]
+    (to_corner,) = after((to_corner,), *slots)
     tokens = (
         here,
         mate_here,
@@ -611,16 +566,37 @@
         moved(to_corner, corner_same),
         moved(to_corner, corner_cross),
     )
-    grads = (made, inward, ahead, aside, relay_x, relay_y)
-    (turn,) = after((place,), second_total)
+    (turn,) = after((place,), arrived[1])
     for_mate = weight_product(turn, False, mean_scale, own_heads, shared, tokens, grads)
     from_mate = moved(for_mate, mate)
     weight_grads = weight_product(
         place, True, mean_scale, own_heads, shared, tokens, grads, (from_mate,)
     )
-    landed = (deliver(0, first_total), deliver(1, second_total))
-    which = jnp.bitwise_xor(lax.axis_index("head") // (views // 2), lax.axis_index("dp"))
-    input_grad = chosen_of(which.reshape(1).astype(jnp.int32), *landed)
+    (kept,) = after((slots[0],), weight_grads[0])
+    total = sum(array.astype(jnp.float32) for array in (kept, *arrived))
+    total = total.astype(jnp.bfloat16)
+
+    def spot(y, v, z):
+        return (y * views + v) * groups + z
+
+    corners = [(y, v, z) for y in range(prompts) for v in range(views) for z in range(groups)]
+    beside = lax.ppermute(
+        total,
+        ("dp", "view", "head"),
+        [(spot(y, v, z), spot(y ^ (v % 2), v ^ z, z)) for y, v, z in corners],
+    )
+    input_grad = lax.ppermute(
+        beside,
+        ("dp", "view", "head"),
+        [
+            (
+                spot(y ^ (v % 2), v ^ z, z),
+                spot(y ^ (v % 2), v ^ z, y * (views // 2) + v // 2),
+            )
+            for y, v, z in corners
+        ],
+    )
+
     return (
         input_grad.reshape(1, 1, length, model_width // groups),
         *weight_grads,

time: 177 us -> 157 us (0.89)
  local copies, waits for them, and re-layouts: 10.6 us -> 1.02 us
  Pallas kernels: 31.1 us -> 25.1 us
  starting transfers between devices: 35 us -> 31.6 us
    unnamed x46 -> x13, local copies, waits for them, and re-layouts: 8.8 us -> 0.78 us
    ppermute x10 -> x5, starting transfers between devices: 18 us -> 10.1 us  [the longest x3 4.86 us: gather_body(): lax.ppermute(slots[s], 'head', [(z, z ^ s) for z in range(groups)])]
    ppermute x10 -> x5, waiting for transfers between devices: 49.9 us -> 44.2 us  [the longest x3 24.2 us: gather_body(): lax.ppermute(slots[s], 'head', [(z, z ^ s) for z in range(groups)])]
    ppermute x16, waiting for transfers between devices: 46.9 us -> 51.4 us  [moved(): return lax.ppermute(value, ('dp', 'view'), pairs)]
    ppermute x16, starting transfers between devices: 17.1 us -> 21.4 us  [moved(): return lax.ppermute(value, ('dp', 'view'), pairs)]
    pallas_call x2, Pallas kernels: 11.1 us -> 7.62 us  [weight_product(): pl.pallas_call(functools.partial(weight_kernel, mine, mean_scale, own_hea...]
    pallas_call x3 -> x1, Pallas kernels: 7.13 us -> 4.65 us  [input_product(): pl.pallas_call(functools.partial(input_kernel, own_heads, shared), out_sh...]
  transfers between devices with their start and end apart: 26 -> 21, of which waited for: 12 -> 12; matrix products, arithmetic and copies ran while one was open for 1% -> 0% of each run, Pallas kernels for 9% -> 12%
where the time goes in v8:
time: 157 us; the launch traced here: 155 us
  waiting for transfers between devices  95.6 us (61%)
  starting transfers between devices  31.6 us (20%)
  Pallas kernels  25.1 us (16%)
    ppermute x16, waiting for transfers between devices, moved(): return lax.ppermute(value, ('dp', 'view'), pairs)  51.4 us
    ppermute x3, waiting for transfers between devices, gather_body(): lax.ppermute(slots[s], 'head', [(z, z ^ s) for z in range(groups)])  24.2 us
    ppermute x16, starting transfers between devices, moved(): return lax.ppermute(value, ('dp', 'view'), pairs)  21.4 us
    ppermute x1, waiting for transfers between devices, gather_body(): lax.ppermute(beside, ('dp', 'view', 'head'), [(spot(y ^ v % 2, v ^ z, z),...  10.2 us
    ppermute x1, waiting for transfers between devices, gather_body(): lax.ppermute(total, ('dp', 'view', 'head'), [(spot(y, v, z), spot(y ^ v %...  9.76 us
    pallas_call x1, Pallas kernels, attention(): pl.pallas_call(functools.partial(attention_kernel, HD ** (-0.5), own_head...  8.01 us
    pallas_call x2, Pallas kernels, weight_product(): pl.pallas_call(functools.partial(weight_kernel, mine, mean_scale, own_hea...  7.62 us
    ppermute x3, starting transfers between devices, gather_body(): lax.ppermute(slots[s], 'head', [(z, z ^ s) for z in range(groups)])  4.86 us
  transfers between devices with their start and end apart: 21, of which 12 were waited for; matrix products, arithmetic and copies ran while one was open for 0% of the time, Pallas kernels for 12%

profile of v8, /device:TPU:16, one launch (start us, length us, event | category | flops | bytes accessed | tf_op | source)
XLA Modules:
  0.0 155.1 jit_solution(5258721668617074124)
XLA Ops:
  0.6 0.0 copy-start.5
  0.7 0.6 pad_add_fusion.place_ref
  1.2 2.9 %pack_heads.1 = (bf16[2,1040,128]{2,1,0:T(8,128)(2,1)}, bf16[1,1040,128]{2,1,0:T(8,128)(2,1)}, bf16[2,1040,128]{2,1,0:T(8,128)(2,1)}, bf16[2,1040,128]{2,1,0:T(8,128)(2,1)}) custom-call(s32[4]{0:T(128)} %pad_add_fusion.place_ref, s32[1,2]{1,0:T(1,128)} %links_ref.1, bf16[256,768]{1,0:T(8,128)(2,1)} %bitcast.26, bf16[256,768]{1,0:T(8,128)(2,1)} %bitcast.27, ...), custom_call_target="tpu_custom_call" | custom-call | tf_op jit(solution)/shard_map/pack_heads/pallas_call | solution.py:215
  4.2 1.5 collective-permute-start
  5.7 0.0 collective-permute-start.2
  5.7 0.6 collective-permute-start.1
  6.3 16.7 %collective-permute-done.2.refs_3_ = bf16[1,1040,128]{2,1,0:T(8,128)(2,1)S(1)} collective-permute-done((bf16[1,1040,128]{2,1,0:T(8,128)(2,1)}, bf16[1,1040,128]{2,1,0:T(8,128)(2,1)S(1)}, u32[]{:S(2)}, u32[]{:S(2)}) %collective-permute-start.2) | collective-permute-done | bytes 266272 | tf_op jit(solution)/shard_map/ppermute | solution.py:128
  23.0 0.0 collective-permute-done.refs_2_
  23.0 0.7 collective-permute-start.3
  23.8 0.0 copy-done.5
  23.8 0.2 dynamic-slice_bitcast_fusion.1
  24.0 0.0 copy-start
  24.0 0.0 copy-start.1
  24.0 0.0 copy-start.3
  24.0 0.1 pad_maximum_fusion
  24.1 0.0 copy-start.4
  24.1 1.6 %collective-permute-start.4 = (bf16[2,256,384]{2,1,0:T(8,128)(2,1)S(1)}, bf16[2,256,384]{2,1,0:T(8,128)(2,1)S(1)}, u32[]{:S(2)}, u32[]{:S(2)}) collective-permute-start(bf16[2,256,384]{2,1,0:T(8,128)(2,1)S(1)} %get-tuple-element.36), channel_id=1, source_target_pairs={{0,8},{4,20},{8,0},{12,28},{16,24},{20,4},{24,16},{28,12},{1,9},{5... | collective-permute-start | bytes 1179656 | tf_op jit(solution)/shard_map/ppermute | solution.py:128
  25.7 0.0 collective-permute-start.5
  25.7 0.0 copy-done
  25.7 0.0 copy-done.1
  25.7 0.0 copy-done.3
  25.7 1.1 turn_weights.1.own_ref
  26.8 0.0 collective-permute-done.1.refs_1_
  26.8 0.0 collective-permute-done.3.refs_4_
  26.8 0.0 copy-done.4
  26.8 8.0 %attention_gradients.1.refs_0_.refs_6_ = bf16[6,256,384]{2,1,0:T(8,128)(2,1)S(1)} custom-call(s32[4]{0:T(128)S(1)} %copy-done.3, bf16[2,1040,128]{2,1,0:T(8,128)(2,1)S(1)} %copy-done.4, bf16[2,1040,128]{2,1,0:T(8,128)(2,1)S(1)} %collective-permute-done.1.refs_1_, bf16[2,1040,128]{2,1,0:T(8,128)(2,1)S(1)} %collective-permute-done.refs_2_, ...), custom_call_target="tpu_custom_call" | custom-call | flops 4026531840 | bytes 3670016 | tf_op jit(solution)/shard_map/attention_gradients/pallas_call | solution.py:309
  34.8 0.5 collective-permute-done.4.refs_2_
  35.3 0.9 collective-permute-done.5.refs_3_
  36.2 1.5 collective-permute-start.7
  37.7 0.0 collective-permute-start.11
  37.7 1.3 collective-permute-start.6
  39.0 13.5 %collective-permute-done.7.refs_2_.refs_8_ = bf16[6,256,384]{2,1,0:T(8,128)(2,1)S(1)} collective-permute-done((bf16[6,256,384]{2,1,0:T(8,128)(2,1)S(1)}, bf16[6,256,384]{2,1,0:T(8,128)(2,1)S(1)}, u32[]{:S(2)}, u32[]{:S(2)}) %collective-permute-start.7) | collective-permute-done | bytes 1179680 | tf_op jit(solution)/shard_map/ppermute | solution.py:128
  52.4 0.0 collective-permute-start.8
  52.4 4.7 %collective-permute-start.10 = (bf16[6,256,384]{2,1,0:T(8,128)(2,1)S(1)}, bf16[6,256,384]{2,1,0:T(8,128)(2,1)S(1)}, u32[]{:S(2)}, u32[]{:S(2)}) collective-permute-start(bf16[6,256,384]{2,1,0:T(8,128)(2,1)S(1)} %collective-permute-done.7.refs_2_.refs_8_), channel_id=1, source_target_pairs={{0,20},{8,28},{16,4},{24,12},{1,21},{9,29},{17,5},{25,13},{2,22},{... | collective-permute-start | bytes 3538952 | tf_op jit(solution)/shard_map/ppermute | solution.py:128
  57.1 0.7 collective-permute-start.9
  57.9 0.0 collective-permute-done.11.mate_ref
  57.9 1.3 collective-permute-start.12
  59.2 0.9 join_weights.1.refs_6_
  60.1 0.0 collective-permute-done.6.refs_1_.refs_7_
  60.1 7.9 %collective-permute-done.8.refs_3_.refs_9_ = bf16[6,256,384]{2,1,0:T(8,128)(2,1)S(1)} collective-permute-done((bf16[6,256,384]{2,1,0:T(8,128)(2,1)S(1)}, bf16[6,256,384]{2,1,0:T(8,128)(2,1)S(1)}, u32[]{:S(2)}, u32[]{:S(2)}) %collective-permute-start.8) | collective-permute-done | bytes 1179680 | tf_op jit(solution)/shard_map/ppermute | solution.py:128
  68.0 10.7 %collective-permute-done.10.refs_5_.refs_11_ = bf16[6,256,384]{2,1,0:T(8,128)(2,1)S(1)} collective-permute-done((bf16[6,256,384]{2,1,0:T(8,128)(2,1)S(1)}, bf16[6,256,384]{2,1,0:T(8,128)(2,1)S(1)}, u32[]{:S(2)}, u32[]{:S(2)}) %collective-permute-start.10) | collective-permute-done | bytes 1179680 | tf_op jit(solution)/shard_map/ppermute | solution.py:128
  78.8 0.0 collective-permute-done.9.refs_4_.refs_10_
  78.8 4.7 %input_gradient.1 = (bf16[256,768]{1,0:T(8,128)(2,1)S(1)}, bf16[256,768]{1,0:T(8,128)(2,1)S(1)}, bf16[256,768]{1,0:T(8,128)(2,1)S(1)}, bf16[256,768]{1,0:T(8,128)(2,1)S(1)}) custom-call(s32[4]{0:T(128)S(1)} %copy-done.3, bf16[6,256,384]{2,1,0:T(8,128)(2,1)S(1)} %attention_gradients.1.refs_0_.refs_6_, ...), custom_call_target="tpu_custom_call" | custom-call | flops 3623878656 | bytes 9830400 | tf_op jit(solution)/shard_map/input_gradient/pallas_call | solution.py:408
  83.4 0.1 collective-permute-start.15
  83.6 5.6 %collective-permute-start.14 = (bf16[2,256,384]{2,1,0:T(8,128)(2,1)S(1)}, bf16[2,256,384]{2,1,0:T(8,128)(2,1)S(1)}, u32[]{:S(2)}, u32[]{:S(2)}) collective-permute-start(bf16[2,256,384]{2,1,0:T(8,128)(2,1)S(1)} %pad_maximum_fusion.3), channel_id=1, source_target_pairs={{0,28},{8,20},{16,12},{24,4},{1,29},{9,21},{17,13},{25,5},{2,30},{... | collective-permute-start | bytes 1179656 | tf_op jit(solution)/shard_map/ppermute | solution.py:128
  89.2 0.7 collective-permute-start.13
  89.9 10.5 %collective-permute-done.15 = bf16[256,768]{1,0:T(8,128)(2,1)S(1)} collective-permute-done((bf16[256,768]{1,0:T(8,128)(2,1)S(1)}, bf16[256,768]{1,0:T(8,128)(2,1)S(1)}, u32[]{:S(2)}, u32[]{:S(2)}) %collective-permute-start.15) | collective-permute-done | bytes 393248 | tf_op jit(solution)/shard_map/ppermute | solution.py:557
  100.4 0.0 collective-permute-done.12.refs_1_
  100.4 0.0 collective-permute-done.14.refs_5_
  100.4 0.0 collective-permute-done.13.refs_4_
  100.4 2.9 %weight_gradient_mate.1 = f32[3,384,768]{2,1,0:T(8,128)S(1)} custom-call(s32[4]{0:T(128)S(1)} %copy-done.3, bf16[2,256,384]{2,1,0:T(8,128)(2,1)S(1)} %pad_maximum_fusion.2.refs_0_, bf16[2,256,384]{2,1,0:T(8,128)(2,1)S(1)} %collective-permute-done.12.refs_1_, bf16[2,256,384]{2,1,0:T(8,128)(2,1)S(1)} %collective-permute-done.4.refs_2_, ...), custom_call_target="tpu_custom_call" | custom-call | flops 1811939328 | bytes 9043968 | tf_op jit(solution)/shard_map/weight_gradient_mate/pallas_call | solution.py:461
  103.4 1.3 collective-permute-start.16
  104.7 4.7 %collective-permute-start.17 = (bf16[256,768]{1,0:T(8,128)(2,1)S(1)}, bf16[256,768]{1,0:T(8,128)(2,1)S(1)}, u32[]{:S(2)}, u32[]{:S(2)}) collective-permute-start(bf16[256,768]{1,0:T(8,128)(2,1)S(1)} %get-tuple-element.41), channel_id=1, source_target_pairs={{0,1},{1,0},{2,3},{3,2},{4,5},{5,4},{6,7},{7,6},{8,9},{9,8},{10,11... | collective-permute-start | bytes 1179656 | tf_op jit(solution)/shard_map/ppermute | solution.py:557
  109.4 0.0 collective-permute-start.18
  109.4 1.1 collective-permute-done.16.refs_12_
  110.5 4.7 %weight_gradient_own.1 = (f32[384,768]{1,0:T(8,128)}, f32[384,768]{1,0:T(8,128)}, f32[384,768]{1,0:T(8,128)}) custom-call(s32[4]{0:T(128)S(1)} %copy-done.3, bf16[2,256,384]{2,1,0:T(8,128)(2,1)S(1)} %pad_maximum_fusion.2.refs_0_, bf16[2,256,384]{2,1,0:T(8,128)(2,1)S(1)} %collective-permute-done.12.refs_1_, ...), custom_call_target="tpu_custom_call" | custom-call | flops 1811939328 | bytes 9043968 | tf_op jit(solution)/shard_map/weight_gradient_own/pallas_call | solution.py:461
  115.2 11.5 %collective-permute-done.17 = bf16[256,768]{1,0:T(8,128)(2,1)S(1)} collective-permute-done((bf16[256,768]{1,0:T(8,128)(2,1)S(1)}, bf16[256,768]{1,0:T(8,128)(2,1)S(1)}, u32[]{:S(2)}, u32[]{:S(2)}) %collective-permute-start.17) | collective-permute-done | bytes 393248 | tf_op jit(solution)/shard_map/ppermute | solution.py:557
  126.7 2.2 %collective-permute-done.18 = bf16[256,768]{1,0:T(8,128)(2,1)S(1)} collective-permute-done((bf16[256,768]{1,0:T(8,128)(2,1)S(1)}, bf16[256,768]{1,0:T(8,128)(2,1)S(1)}, u32[]{:S(2)}, u32[]{:S(2)}) %collective-permute-start.18) | collective-permute-done | bytes 393248 | tf_op jit(solution)/shard_map/ppermute | solution.py:557
  128.9 0.2 add_convert_fusion
  129.1 3.4 %collective-permute-start.19 = (bf16[256,768]{1,0:T(8,128)(2,1)S(1)}, bf16[256,768]{1,0:T(8,128)(2,1)S(1)}, u32[]{:S(2)}, u32[]{:S(2)}) collective-permute-start(bf16[256,768]{1,0:T(8,128)(2,1)S(1)} %add_convert_fusion), channel_id=1, source_target_pairs={{0,0},{1,5},{2,10},{3,15},{4,20},{5,17},{6,30},{7,27},{8,8},{9,13}... | collective-permute-start | bytes 1179656 | tf_op jit(solution)/shard_map/ppermute | solution.py:583
  132.5 9.8 %collective-permute-done.19 = bf16[256,768]{1,0:T(8,128)(2,1)S(1)} collective-permute-done((bf16[256,768]{1,0:T(8,128)(2,1)S(1)}, bf16[256,768]{1,0:T(8,128)(2,1)S(1)}, u32[]{:S(2)}, u32[]{:S(2)}) %collective-permute-start.19) | collective-permute-done | bytes 393248 | tf_op jit(solution)/shard_map/ppermute | solution.py:583
  142.2 1.9 %collective-permute-start.20 = (bf16[256,768]{1,0:T(8,128)(2,1)S(1)}, bf16[256,768]{1,0:T(8,128)(2,1)S(1)}, u32[]{:S(2)}, u32[]{:S(2)}) collective-permute-start(bf16[256,768]{1,0:T(8,128)(2,1)S(1)} %collective-permute-done.19), channel_id=1, source_target_pairs={{0,0},{5,4},{10,8},{15,12},{20,20},{17,16},{30,28},{27,24},{8,9},{... | collective-permute-start | bytes 1179656 | tf_op jit(solution)/shard_map/ppermute | solution.py:588
  144.1 10.2 %collective-permute-done.20 = bf16[256,768]{1,0:T(8,128)(2,1)S(1)} collective-permute-done((bf16[256,768]{1,0:T(8,128)(2,1)S(1)}, bf16[256,768]{1,0:T(8,128)(2,1)S(1)}, u32[]{:S(2)}, u32[]{:S(2)}) %collective-permute-start.20) | collective-permute-done | bytes 393248 | tf_op jit(solution)/shard_map/ppermute | solution.py:588
  154.4 0.7 copy.14
  (4 shorter events, 0.1 us)
Async XLA Ops:
  0.6 23.1 %copy-start.5 = (bf16[1,1,256,3072]{3,2,1,0:T(8,128)(2,1)S(1)}, bf16[1,1,256,3072]{3,2,1,0:T(8,128)(2,1)}, u32[]{:S(2)}) copy-start(bf16[1,1,256,3072]{3,2,1,0:T(8,128)(2,1)} %param.9) | copy-start | bytes 4718596
  4.2 18.9 %collective-permute-start = (bf16[2,1040,128]{2,1,0:T(8,128)(2,1)}, bf16[2,1040,128]{2,1,0:T(8,128)(2,1)S(1)}, u32[]{:S(2)}, u32[]{:S(2)}) collective-permute-start(bf16[2,1040,128]{2,1,0:T(8,128)(2,1)} %get-tuple-element.27), channel_id=1, source_target_pairs={{0,8},{4,12},{8,0},{12,4},{16,24},{20,28},{24,16},{28,20},{1,9},{5... | collective-permute-start | bytes 1597448 | tf_op jit(solution)/shard_map/ppermute | solution.py:128
  5.7 17.4 %collective-permute-start.2 = (bf16[1,1040,128]{2,1,0:T(8,128)(2,1)}, bf16[1,1040,128]{2,1,0:T(8,128)(2,1)S(1)}, u32[]{:S(2)}, u32[]{:S(2)}) collective-permute-start(bf16[1,1040,128]{2,1,0:T(8,128)(2,1)} %get-tuple-element.34), channel_id=1, source_target_pairs={{0,12},{4,8},{8,4},{12,0},{16,28},{20,24},{24,20},{28,16},{1,13},{... | collective-permute-start | bytes 798728 | tf_op jit(solution)/shard_map/ppermute | solution.py:128
  5.7 21.1 %collective-permute-start.1 = (bf16[2,1040,128]{2,1,0:T(8,128)(2,1)}, bf16[2,1040,128]{2,1,0:T(8,128)(2,1)S(1)}, u32[]{:S(2)}, u32[]{:S(2)}) collective-permute-start(bf16[2,1040,128]{2,1,0:T(8,128)(2,1)} %get-tuple-element.33), channel_id=1, source_target_pairs={{0,4},{4,0},{8,12},{12,8},{16,20},{20,16},{24,28},{28,24},{1,5},{5... | collective-permute-start | bytes 1597448 | tf_op jit(solution)/shard_map/ppermute | solution.py:128
  23.0 3.8 %collective-permute-start.3 = (bf16[2,1040,128]{2,1,0:T(8,128)(2,1)S(1)}, bf16[2,1040,128]{2,1,0:T(8,128)(2,1)S(1)}, u32[]{:S(2)}, u32[]{:S(2)}) collective-permute-start(bf16[2,1040,128]{2,1,0:T(8,128)(2,1)S(1)} %collective-permute-done.refs_2_), channel_id=1, source_target_pairs={{0,4},{4,0},{8,12},{12,8},{16,20},{20,16},{24,28},{28,24},{1,5},{5... | collective-permute-start | bytes 1597448 | tf_op jit(solution)/shard_map/ppermute | solution.py:128
  23.8 2.0 %copy-start.2 = (bf16[384,768]{1,0:T(8,128)(2,1)S(1)}, bf16[384,768]{1,0:T(8,128)(2,1)}, u32[]{:S(2)}) copy-start(bf16[384,768]{1,0:T(8,128)(2,1)} %v_ref) | copy-start | bytes 1769476
  24.0 1.7 %copy-start = (bf16[384,768]{1,0:T(8,128)(2,1)S(1)}, bf16[384,768]{1,0:T(8,128)(2,1)}, u32[]{:S(2)}) copy-start(bf16[384,768]{1,0:T(8,128)(2,1)} %q_ref) | copy-start | bytes 1769476
  24.0 1.7 %copy-start.1 = (bf16[384,768]{1,0:T(8,128)(2,1)S(1)}, bf16[384,768]{1,0:T(8,128)(2,1)}, u32[]{:S(2)}) copy-start(bf16[384,768]{1,0:T(8,128)(2,1)} %k_ref) | copy-start | bytes 1769476
  24.0 1.7 %copy-start.3 = (s32[4]{0:T(128)S(1)}, s32[4]{0:T(128)}, u32[]{:S(2)}) copy-start(s32[4]{0:T(128)} %pad_add_fusion.place_ref) | copy-start | bytes 52
  24.1 2.7 %copy-start.4 = (bf16[2,1040,128]{2,1,0:T(8,128)(2,1)S(1)}, bf16[2,1040,128]{2,1,0:T(8,128)(2,1)}, u32[]{:S(2)}) copy-start(bf16[2,1040,128]{2,1,0:T(8,128)(2,1)} %get-tuple-element.32.refs_0_) | copy-start | bytes 1597444
  24.1 11.2 %collective-permute-start.4 = (bf16[2,256,384]{2,1,0:T(8,128)(2,1)S(1)}, bf16[2,256,384]{2,1,0:T(8,128)(2,1)S(1)}, u32[]{:S(2)}, u32[]{:S(2)}) collective-permute-start(bf16[2,256,384]{2,1,0:T(8,128)(2,1)S(1)} %get-tuple-element.36), channel_id=1, source_target_pairs={{0,8},{4,20},{8,0},{12,28},{16,24},{20,4},{24,16},{28,12},{1,9},{5... | collective-permute-start | bytes 1179656 | tf_op jit(solution)/shard_map/ppermute | solution.py:128
  25.7 10.5 %collective-permute-start.5 = (bf16[2,256,384]{2,1,0:T(8,128)(2,1)S(1)}, bf16[2,256,384]{2,1,0:T(8,128)(2,1)S(1)}, u32[]{:S(2)}, u32[]{:S(2)}) collective-permute-start(bf16[2,256,384]{2,1,0:T(8,128)(2,1)S(1)} %get-tuple-element.37), channel_id=1, source_target_pairs={{0,20},{4,8},{8,28},{12,0},{16,4},{20,24},{24,12},{28,16},{1,21},{... | collective-permute-start | bytes 1179656 | tf_op jit(solution)/shard_map/ppermute | solution.py:128
  36.2 16.2 %collective-permute-start.7 = (bf16[6,256,384]{2,1,0:T(8,128)(2,1)S(1)}, bf16[6,256,384]{2,1,0:T(8,128)(2,1)S(1)}, u32[]{:S(2)}, u32[]{:S(2)}) collective-permute-start(bf16[6,256,384]{2,1,0:T(8,128)(2,1)S(1)} %attention_gradients.1.refs_0_.refs_6_), channel_id=1, source_target_pairs={{0,8},{4,20},{8,0},{12,28},{16,24},{20,4},{24,16},{28,12},{1,9},{5... | collective-permute-start | bytes 3538952 | tf_op jit(solution)/shard_map/ppermute | solution.py:128
  37.7 20.3 %collective-permute-start.11 = (bf16[2304,384]{1,0:T(8,128)(2,1)S(1)}, bf16[2304,384]{1,0:T(8,128)(2,1)S(1)}, u32[]{:S(2)}, u32[]{:S(2)}) collective-permute-start(bf16[2304,384]{1,0:T(8,128)(2,1)S(1)} %turn_weights.1.own_ref), channel_id=1, source_target_pairs={{0,4},{4,0},{8,12},{12,8},{16,20},{20,16},{24,28},{28,24},{1,5},{5... | collective-permute-start | bytes 5308424 | tf_op jit(solution)/shard_map/ppermute | solution.py:128
  37.7 22.4 %collective-permute-start.6 = (bf16[6,256,384]{2,1,0:T(8,128)(2,1)S(1)}, bf16[6,256,384]{2,1,0:T(8,128)(2,1)S(1)}, u32[]{:S(2)}, u32[]{:S(2)}) collective-permute-start(bf16[6,256,384]{2,1,0:T(8,128)(2,1)S(1)} %attention_gradients.1.refs_0_.refs_6_), channel_id=1, source_target_pairs={{4,0},{12,8},{20,16},{28,24},{5,1},{13,9},{21,17},{29,25},{6,2},{1... | collective-permute-start | bytes 3538952 | tf_op jit(solution)/shard_map/ppermute | solution.py:128
  52.4 15.6 %collective-permute-start.8 = (bf16[6,256,384]{2,1,0:T(8,128)(2,1)S(1)}, bf16[6,256,384]{2,1,0:T(8,128)(2,1)S(1)}, u32[]{:S(2)}, u32[]{:S(2)}) collective-permute-start(bf16[6,256,384]{2,1,0:T(8,128)(2,1)S(1)} %attention_gradients.1.refs_0_.refs_6_), channel_id=1, source_target_pairs={{0,20},{4,8},{8,28},{12,0},{16,4},{20,24},{24,12},{28,16},{1,21},{... | collective-permute-start | bytes 3538952 | tf_op jit(solution)/shard_map/ppermute | solution.py:128
  52.4 26.4 %collective-permute-start.10 = (bf16[6,256,384]{2,1,0:T(8,128)(2,1)S(1)}, bf16[6,256,384]{2,1,0:T(8,128)(2,1)S(1)}, u32[]{:S(2)}, u32[]{:S(2)}) collective-permute-start(bf16[6,256,384]{2,1,0:T(8,128)(2,1)S(1)} %collective-permute-done.7.refs_2_.refs_8_), channel_id=1, source_target_pairs={{0,20},{8,28},{16,4},{24,12},{1,21},{9,29},{17,5},{25,13},{2,22},{... | collective-permute-start | bytes 3538952 | tf_op jit(solution)/shard_map/ppermute | solution.py:128
  57.1 21.7 %collective-permute-start.9 = (bf16[6,256,384]{2,1,0:T(8,128)(2,1)S(1)}, bf16[6,256,384]{2,1,0:T(8,128)(2,1)S(1)}, u32[]{:S(2)}, u32[]{:S(2)}) collective-permute-start(bf16[6,256,384]{2,1,0:T(8,128)(2,1)S(1)} %collective-permute-done.7.refs_2_.refs_8_), channel_id=1, source_target_pairs={{4,12},{12,4},{20,28},{28,20},{5,13},{13,5},{21,29},{29,21},{6,14}... | collective-permute-start | bytes 3538952 | tf_op jit(solution)/shard_map/ppermute | solution.py:128
  57.9 42.5 %collective-permute-start.12 = (bf16[2,256,384]{2,1,0:T(8,128)(2,1)S(1)}, bf16[2,256,384]{2,1,0:T(8,128)(2,1)S(1)}, u32[]{:S(2)}, u32[]{:S(2)}) collective-permute-start(bf16[2,256,384]{2,1,0:T(8,128)(2,1)S(1)} %pad_maximum_fusion.2.refs_0_), channel_id=1, source_target_pairs={{4,0},{12,8},{20,16},{28,24},{5,1},{13,9},{21,17},{29,25},{6,2},{1... | collective-permute-start | bytes 1179656 | tf_op jit(solution)/shard_map/ppermute | solution.py:128
  83.4 17.0 %collective-permute-start.15 = (bf16[256,768]{1,0:T(8,128)(2,1)S(1)}, bf16[256,768]{1,0:T(8,128)(2,1)S(1)}, u32[]{:S(2)}, u32[]{:S(2)}) collective-permute-start(bf16[256,768]{1,0:T(8,128)(2,1)S(1)} %get-tuple-element.42), channel_id=1, source_target_pairs={{0,2},{1,3},{2,0},{3,1},{4,6},{5,7},{6,4},{7,5},{8,10},{9,11},{10,... | collective-permute-start | bytes 1179656 | tf_op jit(solution)/shard_map/ppermute | solution.py:557
  83.6 16.8 %collective-permute-start.14 = (bf16[2,256,384]{2,1,0:T(8,128)(2,1)S(1)}, bf16[2,256,384]{2,1,0:T(8,128)(2,1)S(1)}, u32[]{:S(2)}, u32[]{:S(2)}) collective-permute-start(bf16[2,256,384]{2,1,0:T(8,128)(2,1)S(1)} %pad_maximum_fusion.3), channel_id=1, source_target_pairs={{0,28},{8,20},{16,12},{24,4},{1,29},{9,21},{17,13},{25,5},{2,30},{... | collective-permute-start | bytes 1179656 | tf_op jit(solution)/shard_map/ppermute | solution.py:128
  89.2 11.2 %collective-permute-start.13 = (bf16[2,256,384]{2,1,0:T(8,128)(2,1)S(1)}, bf16[2,256,384]{2,1,0:T(8,128)(2,1)S(1)}, u32[]{:S(2)}, u32[]{:S(2)}) collective-permute-start(bf16[2,256,384]{2,1,0:T(8,128)(2,1)S(1)} %pad_maximum_fusion.3), channel_id=1, source_target_pairs={{4,28},{12,20},{20,12},{28,4},{5,29},{13,21},{21,13},{29,5},{6,30}... | collective-permute-start | bytes 1179656 | tf_op jit(solution)/shard_map/ppermute | solution.py:128
  103.4 7.1 %collective-permute-start.16 = (f32[3,384,768]{2,1,0:T(8,128)S(1)}, f32[3,384,768]{2,1,0:T(8,128)S(1)}, u32[]{:S(2)}, u32[]{:S(2)}) collective-permute-start(f32[3,384,768]{2,1,0:T(8,128)S(1)} %weight_gradient_mate.1), channel_id=1, source_target_pairs={{0,4},{4,0},{8,12},{12,8},{16,20},{20,16},{24,28},{28,24},{1,5},{5... | collective-permute-start | bytes 10616840 | tf_op jit(solution)/shard_map/ppermute | solution.py:128
  104.7 22.0 %collective-permute-start.17 = (bf16[256,768]{1,0:T(8,128)(2,1)S(1)}, bf16[256,768]{1,0:T(8,128)(2,1)S(1)}, u32[]{:S(2)}, u32[]{:S(2)}) collective-permute-start(bf16[256,768]{1,0:T(8,128)(2,1)S(1)} %get-tuple-element.41), channel_id=1, source_target_pairs={{0,1},{1,0},{2,3},{3,2},{4,5},{5,4},{6,7},{7,6},{8,9},{9,8},{10,11... | collective-permute-start | bytes 1179656 | tf_op jit(solution)/shard_map/ppermute | solution.py:557
  109.4 19.5 %collective-permute-start.18 = (bf16[256,768]{1,0:T(8,128)(2,1)S(1)}, bf16[256,768]{1,0:T(8,128)(2,1)S(1)}, u32[]{:S(2)}, u32[]{:S(2)}) collective-permute-start(bf16[256,768]{1,0:T(8,128)(2,1)S(1)} %get-tuple-element.43), channel_id=1, source_target_pairs={{0,3},{1,2},{2,1},{3,0},{4,7},{5,6},{6,5},{7,4},{8,11},{9,10},{10,... | collective-permute-start | bytes 1179656 | tf_op jit(solution)/shard_map/ppermute | solution.py:557
  129.1 13.1 %collective-permute-start.19 = (bf16[256,768]{1,0:T(8,128)(2,1)S(1)}, bf16[256,768]{1,0:T(8,128)(2,1)S(1)}, u32[]{:S(2)}, u32[]{:S(2)}) collective-permute-start(bf16[256,768]{1,0:T(8,128)(2,1)S(1)} %add_convert_fusion), channel_id=1, source_target_pairs={{0,0},{1,5},{2,10},{3,15},{4,20},{5,17},{6,30},{7,27},{8,8},{9,13}... | collective-permute-start | bytes 1179656 | tf_op jit(solution)/shard_map/ppermute | solution.py:583
  142.2 12.2 %collective-permute-start.20 = (bf16[256,768]{1,0:T(8,128)(2,1)S(1)}, bf16[256,768]{1,0:T(8,128)(2,1)S(1)}, u32[]{:S(2)}, u32[]{:S(2)}) collective-permute-start(bf16[256,768]{1,0:T(8,128)(2,1)S(1)} %collective-permute-done.19), channel_id=1, source_target_pairs={{0,0},{5,4},{10,8},{15,12},{20,20},{17,16},{30,28},{27,24},{8,9},{... | collective-permute-start | bytes 1179656 | tf_op jit(solution)/shard_map/ppermute | solution.py:588

commit v9 on v8

--- a/solution.py
+++ b/solution.py
@@ -282,34 +282,29 @@
     return query_grads, by_view(key_sums), by_view(value_sums)
 
 
-def attention_kernel(scaling, own_heads, place_ref, *refs):
-    own, mate_in, x_in, cross_in, mate_x_in = refs[:5]
-    out_ref, keys, values, key_sums, value_sums = refs[5:]
+def attention_kernel(scaling, kept, place_ref, own, mate_in, x_in, far_in, *refs):
+    out_ref, keys, values, key_sums, value_sums = refs
     length = out_ref.shape[1]
     heads = own.shape[0]
     for head in range(heads):
-        shared = head >= own_heads
-        far = mate_x_in if shared else cross_in
-        xs = [own.at[head], mate_in.at[head], x_in.at[head], far.at[head]]
+        xs = [own.at[head], mate_in.at[head], x_in.at[head], far_in.at[head]]
         grads = one_head(
             scaling, place_ref[CORE], xs, length, keys, values, key_sums, value_sums
         )
-        for e in range(4):
-            if shared and e % 2 == 1:
-                continue
-            at = 4 * own_heads + e // 2 if shared else 4 * head + e
+        for at, e in enumerate(kept):
             for kind in range(3):
-                out_ref[at, :, kind * HD : (kind + 1) * HD] = grads[kind][e].astype(out_ref.dtype)
-
-
-def attention(place, own_heads, sources):
+                out_ref[len(kept) * head + at, :, kind * HD : (kind + 1) * HD] = grads[kind][
+                    e
+                ].astype(out_ref.dtype)
+
+
+def attention(place, kept, sources):
     heads, height, _ = sources[0].shape
     length = (height - FLAG_ROWS) // 4
-    held = 4 * own_heads + 2 * (heads - own_heads)
     return pl.pallas_call(
-        functools.partial(attention_kernel, HD ** (-0.5), own_heads),
-        out_shape=jax.ShapeDtypeStruct((held, length, 3 * HD), jnp.bfloat16),
-        in_specs=[whole(pltpu.SMEM)] + [whole()] * 5,
+        functools.partial(attention_kernel, HD ** (-0.5), kept),
+        out_shape=jax.ShapeDtypeStruct((len(kept) * heads, length, 3 * HD), jnp.bfloat16),
+        in_specs=[whole(pltpu.SMEM)] + [whole()] * 4,
         out_specs=whole(),
         scratch_shapes=[pltpu.VMEM((6 * length, HD), jnp.bfloat16)] * 2
         + [pltpu.VMEM((6 * length, HD), jnp.float32)] * 2,
@@ -363,19 +358,19 @@
     )(place, own_weights, mate_weights)
 
 
-def gathered(role, own_heads, shared, refs):
+def gathered(role, refs):
     sides = []
     for side in range(2):
         pieces = []
-        for head in range(own_heads):
+        for head in range(refs[0][0].shape[0] // 4):
             for maker in range(2):
                 k = 2 * side + (maker ^ role)
-                pieces.append([refs[k][4 * head + (e ^ k)] for e in range(4)])
-        for at in range(shared):
+                pieces.append([refs[k][0][4 * head + (e ^ k)] for e in range(4)])
+        for at in range(refs[0][1].shape[0] // 2 if len(refs[0]) > 1 else 0):
             rows = []
             for e in range(4):
                 k = 2 * side + e % 2
-                rows.append(refs[k][4 * own_heads + 2 * at + (e // 2 ^ side)])
+                rows.append(refs[k][1][2 * at + (e // 2 ^ side)])
             pieces.append(rows)
         sides.append(
             jnp.concatenate([jnp.concatenate(rows, axis=0) for rows in pieces], axis=1)
@@ -383,16 +378,21 @@
     return sides
 
 
-def input_kernel(own_heads, shared, place_ref, *refs):
-    grad_refs, weights, out_refs, total = refs[:6], refs[6], refs[7:-1], refs[-1]
-    made, inward, ahead, aside, relay_x, relay_y = grad_refs
-    grads = ((made, inward, ahead, aside), (ahead, aside, relay_x, relay_y))
+def by_role(refs, parts):
+    made, inward, ahead, aside, relay_x, relay_y = [
+        refs[at * parts : (at + 1) * parts] for at in range(6)
+    ]
+    return ((made, inward, ahead, aside), (ahead, aside, relay_x, relay_y))
+
+
+def input_kernel(parts, place_ref, *refs):
+    weights, out_refs, total = refs[6 * parts], refs[6 * parts + 1 : -1], refs[-1]
     length = out_refs[0].shape[0]
-    for role in range(2):
+    for role, grads in enumerate(by_role(refs, parts)):
 
         @pl.when(place_ref[CORE] == role)
         def _():
-            left = jnp.concatenate(gathered(role, own_heads, shared, grads[role]), axis=1)
+            left = jnp.concatenate(gathered(role, grads), axis=1)
             for e in range(4):
                 product = dot(left[e * length : (e + 1) * length], weights[...])
                 total[e] = product.astype(total.dtype)
@@ -401,14 +401,14 @@
         out_ref[...] = total[jnp.bitwise_xor(place_ref[PLANE], s)]
 
 
-def input_product(place, own_heads, shared, grads, weights):
+def input_product(place, grads, weights):
     _, length, _ = grads[0].shape
     depth, rows = weights.shape
     out = jax.ShapeDtypeStruct((length, rows), jnp.bfloat16)
     return pl.pallas_call(
-        functools.partial(input_kernel, own_heads, shared),
+        functools.partial(input_kernel, len(grads) // 6),
         out_shape=[out] * 4,
-        in_specs=[whole(pltpu.SMEM)] + [whole()] * 7,
+        in_specs=[whole(pltpu.SMEM)] + [whole()] * (len(grads) + 1),
         out_specs=[whole()] * 4,
         scratch_shapes=[pltpu.VMEM((4, length, rows), jnp.bfloat16)],
         compiler_params=pltpu.CompilerParams(vmem_limit_bytes=24 * MIB),
@@ -421,26 +421,24 @@
     )(place, *grads, weights)
 
 
-def weight_kernel(mine, mean_scale, own_heads, shared, place_ref, *refs):
+def weight_kernel(mine, mean_scale, parts, place_ref, *refs):
     own, mate_in, first, second, corner, corner_far = refs[:6]
-    made, inward, ahead, aside, relay_x, relay_y = refs[6:12]
+    grad_refs, refs = refs[6 : 6 + 6 * parts], refs[6 + 6 * parts :]
     if mine:
-        received, out_refs, turned = refs[12], refs[13:16], refs[16]
+        received, out_refs, turned = refs[0], refs[1:4], refs[4]
     else:
-        received, out_refs, turned = None, [refs[12].at[kind] for kind in range(3)], refs[13]
+        received, out_refs, turned = None, [refs[0].at[kind] for kind in range(3)], refs[1]
     core = place_ref[CORE]
     length = own.shape[1]
     part = core if mine else 1 - core
     tokens = ((own, mate_in, first, second), (first, second, corner, corner_far))
-    grads = ((made, inward, ahead, aside), (ahead, aside, relay_x, relay_y))
-    for role in range(2):
+    for role, grads in enumerate(by_role(grad_refs, parts)):
 
         @pl.when(core == role)
         def _():
             for e, source in enumerate(tokens[role]):
                 turned[:, e * length : (e + 1) * length] = source[part].T
-            sides = gathered(role, own_heads, shared, grads[role])
-            for base, side in zip((HERE, BESIDE), sides):
+            for base, side in zip((HERE, BESIDE), gathered(role, grads)):
                 total = dot(turned[...], side)
                 for head in range(side.shape[1] // (3 * HD)):
                     here = lanes((place_ref[base] + head) * HD, HD)
@@ -452,16 +450,15 @@
                         out[:, here] = value
 
 
-def weight_product(place, mine, mean_scale, own_heads, shared, tokens, grads, received=()):
-    _, length, triple = grads[0].shape
+def weight_product(place, mine, mean_scale, cols, tokens, grads, received=()):
+    _, length, _ = grads[0].shape
     rows = tokens[0].shape[2]
-    cols = 2 * (2 * own_heads + shared) * HD
     out = jax.ShapeDtypeStruct((rows, cols), jnp.float32)
     both = jax.ShapeDtypeStruct((3, rows, cols), jnp.float32)
     return pl.pallas_call(
-        functools.partial(weight_kernel, mine, mean_scale, own_heads, shared),
+        functools.partial(weight_kernel, mine, mean_scale, len(grads) // 6),
         out_shape=[out] * 3 if mine else both,
-        in_specs=[whole(pltpu.SMEM)] + [whole()] * (12 + len(received)),
+        in_specs=[whole(pltpu.SMEM)] + [whole()] * (6 + len(grads) + len(received)),
         out_specs=[whole()] * 3 if mine else whole(),
         scratch_shapes=[pltpu.VMEM((rows, 4 * length), jnp.bfloat16)],
         compiler_params=pltpu.CompilerParams(vmem_limit_bytes=24 * MIB),
@@ -500,82 +497,79 @@
     arrays = tuple(a.reshape(length, cols) for a in (queries, saved_keys, saved_values, output_grad))
 
     own_heads, shared = half // 2, half % 2
-    both = [2 * own_heads + at for at in range(shared)]
     each = [2 * step for step in range(own_heads)]
-    to_x, to_cross, to_mate, own = pack(
-        (
-            [(BESIDE, step, 1) for step in each] + [(BESIDE, step, 0) for step in both],
-            [(BESIDE, step + 1, -1) for step in each],
-            [(HERE, step + 1, -1) for step in each] + [(HERE, step, 0) for step in both],
-            [(HERE, step, 1) for step in each] + [(HERE, step, 0) for step in both],
-        ),
-        place,
-        view_links,
-        arrays,
-    )
+    picks = [
+        [(BESIDE, step, 1) for step in each],
+        [(BESIDE, step + 1, -1) for step in each],
+        [(HERE, step + 1, -1) for step in each],
+        [(HERE, step, 1) for step in each],
+    ]
+    if shared:
+        picks += [[(BESIDE, 2 * own_heads, 0)], [(HERE, 2 * own_heads, 0)]]
+    packed = pack(picks, place, view_links, arrays)
+    to_x, to_cross, to_mate, own = packed[:4]
     x_in = moved(to_x, along_x)
     cross_in = moved(to_cross, across_x)
     mate_in = moved(to_mate, mate)
-    (sent,) = after((x_in,), cross_in)
-    mate_x_in = moved(sent, mate)
-
-
-    flat = normed.reshape(length, model_width)
+    sets = [((0, 1, 2, 3), (own, mate_in, x_in, cross_in))]
+    if shared:
+        to_x, own = packed[4:]
+        (to_x,) = after((to_x,), x_in)
+        x_in = moved(to_x, along_x)
+        sets.append(((0, 2), (own, moved(own, mate), x_in, moved(x_in, mate))))
+
+    own_weights, turn = None, place
+    parts = []
+    for kept, sources in sets:
+        made = attention(turn, kept, sources)
+        if own_weights is None:
+            ready = after((query_weight, key_weight, value_weight), made)
+            own_weights = turned_weights(place, ready)
+        (turn,) = after((place,), made, own_weights)
+        ahead = moved(made, straight)
+        aside = moved(made, crossed)
+        inward = moved(made, only(1, mate))
+        (sent,) = after((ahead,), aside, inward)
+        relay_x = moved(sent, only(1, along_x))
+        relay_y = moved(sent, only(0, across_y))
+        parts.append((made, inward, ahead, aside, relay_x, relay_y))
+    grads = [array for kind in zip(*parts) for array in kind]
+    weights = joined_weights(place, own_weights, moved(own_weights, mate))
+
+    slots = input_product(place, grads, weights)
+    arrived = [
+        lax.ppermute(slots[s], "head", [(z, z ^ s) for z in range(groups)])
+        for s in range(1, groups)
+    ]
+    total = sum(array.astype(jnp.float32) for array in (slots[0], *arrived))
+    total = total.astype(jnp.bfloat16)
+
+    (flat,) = after((normed.reshape(length, model_width),), *slots)
 
     def columns(of_chip):
-        parts = [
+        columns = [
             lax.dynamic_slice_in_dim(flat, (2 * of_chip + part) * rows, rows, axis=1)
             for part in range(2)
         ]
-        return jnp.stack(parts)
+        return jnp.stack(columns)
 
     toward_x, toward_y = jnp.bitwise_xor(chip, 1), jnp.bitwise_xor(chip, 2)
     here = columns(chip)
     to_straight = columns(jnp.where(core == 0, toward_x, toward_y))
     to_crossed = columns(jnp.where(core == 0, toward_y, toward_x))
     to_corner = columns(jnp.bitwise_xor(chip, 3))
-    mate_here = moved(here, only(1, mate))
-    to_straight, to_crossed = after((to_straight, to_crossed), cross_in)
-    normed_ahead = moved(to_straight, straight)
-    normed_aside = moved(to_crossed, crossed)
-
-    own_weights = turned_weights(place, after((query_weight, key_weight, value_weight), x_in))
-    (turn,) = after((place,), own_weights)
-    made = attention(turn, own_heads, (own, mate_in, x_in, cross_in, mate_x_in))
-    (made,) = after((made,), normed_ahead, normed_aside)
-    ahead = moved(made, straight)
-    inward = moved(made, only(1, mate))
-    (sent,) = after((made,), ahead)
-    aside = moved(sent, crossed)
-    relay_x = moved(ahead, only(1, along_x))
-    relay_y = moved(ahead, only(0, across_y))
-    weights = joined_weights(place, own_weights, moved(own_weights, mate))
-    grads = (made, inward, ahead, aside, relay_x, relay_y)
-
-    slots = input_product(place, own_heads, shared, grads, weights)
-    arrived = [
-        lax.ppermute(slots[s], "head", [(z, z ^ s) for z in range(groups)])
-        for s in range(1, groups)
-    ]
-    (to_corner,) = after((to_corner,), *slots)
     tokens = (
         here,
-        mate_here,
-        normed_ahead,
-        normed_aside,
+        moved(here, only(1, mate)),
+        moved(to_straight, straight),
+        moved(to_crossed, crossed),
         moved(to_corner, corner_same),
         moved(to_corner, corner_cross),
     )
-    (turn,) = after((place,), arrived[1])
-    for_mate = weight_product(turn, False, mean_scale, own_heads, shared, tokens, grads)
+    (turn,) = after((place,), total)
+    for_mate = weight_product(turn, False, mean_scale, cols, tokens, grads)
     from_mate = moved(for_mate, mate)
-    weight_grads = weight_product(
-        place, True, mean_scale, own_heads, shared, tokens, grads, (from_mate,)
-    )
-    (kept,) = after((slots[0],), weight_grads[0])
-    total = sum(array.astype(jnp.float32) for array in (kept, *arrived))
-    total = total.astype(jnp.bfloat16)
-
+    weight_grads = weight_product(place, True, mean_scale, cols, tokens, grads, (from_mate,))
     def spot(y, v, z):
         return (y * views + v) * groups + z
 
@@ -585,6 +579,7 @@
         ("dp", "view", "head"),
         [(spot(y, v, z), spot(y ^ (v % 2), v ^ z, z)) for y, v, z in corners],
     )
+    (beside,) = after((beside,), weight_grads[0])
     input_grad = lax.ppermute(
         beside,
         ("dp", "view", "head"),

time: 157 us -> 155 us (0.987); the launches traced: 155 us -> 155 us
  waiting for transfers between devices: 95.6 us -> 53.4 us
  starting transfers between devices: 31.6 us -> 62.4 us
  Pallas kernels: 25.1 us -> 31.3 us
  local copies, waits for them, and re-layouts: 1.02 us -> 5.73 us
    ppermute x16 -> x23, starting transfers between devices: 21.4 us -> 53.6 us  [moved(): return lax.ppermute(value, ('dp', 'view'), pairs)]
    ppermute x16 -> x23, waiting for transfers between devices: 51.4 us -> 28.6 us  [moved(): return lax.ppermute(value, ('dp', 'view'), pairs)]
    ppermute x3, waiting for transfers between devices: 24.2 us -> 12.1 us  [gather_body(): lax.ppermute(slots[s], 'head', [(z, z ^ s) for z in range(groups)])]
    ppermute x1, waiting for transfers between devices: 9.76 us -> 1.64 us  [gather_body(): lax.ppermute(total, ('dp', 'view', 'head'), [(spot(y, v, z), spot(y ^ v %...]
    pallas_call x4 -> x5, Pallas kernels: 20.3 us -> 25.5 us  [the longest x2 10.6 us: weight_product(): pl.pallas_call(functools.partial(weight_kernel, mine, mean_scale, len(gra...]
    unnamed x13 -> x33, local copies, waits for them, and re-layouts: 0.78 us -> 5.49 us
  transfers between devices with their start and end apart: 21 -> 28, of which waited for: 12 -> 12; matrix products, arithmetic and copies ran while one was open for 0% -> 0% of each run, Pallas kernels for 12% -> 12%
where the time goes in v9:
time: 155 us
  starting transfers between devices  62.4 us (40%)
  waiting for transfers between devices  53.4 us (34%)
  Pallas kernels  31.3 us (20%)
  local copies, waits for them, and re-layouts  5.73 us (4%)
    ppermute x23, starting transfers between devices, moved(): return lax.ppermute(value, ('dp', 'view'), pairs)  53.6 us
    ppermute x23, waiting for transfers between devices, moved(): return lax.ppermute(value, ('dp', 'view'), pairs)  28.6 us
    ppermute x3, waiting for transfers between devices, gather_body(): lax.ppermute(slots[s], 'head', [(z, z ^ s) for z in range(groups)])  12.1 us
    ppermute x1, waiting for transfers between devices, gather_body(): lax.ppermute(beside, ('dp', 'view', 'head'), [(spot(y ^ v % 2, v ^ z, z),...  11.1 us
    pallas_call x2, Pallas kernels, weight_product(): pl.pallas_call(functools.partial(weight_kernel, mine, mean_scale, len(gra...  10.6 us
    pallas_call x2, Pallas kernels, attention(): pl.pallas_call(functools.partial(attention_kernel, HD ** (-0.5), kept), o...  8.77 us
    pallas_call x1, Pallas kernels, input_product(): pl.pallas_call(functools.partial(input_kernel, len(grads) // 6), out_shap...  6.13 us
    unnamed x33, local copies, waits for them, and re-layouts  5.49 us
  transfers between devices with their start and end apart: 28, of which 12 were waited for; matrix products, arithmetic and copies ran while one was open for 0% of the time, Pallas kernels for 12%

profile of v9, /device:TPU:16, one launch (start us, length us, event | category | flops | bytes accessed | tf_op | source)
XLA Modules:
  0.0 154.8 jit_solution(7642783196173690831)
XLA Ops:
  0.6 0.6 pad_add_fusion.place_ref
  1.3 2.8 %pack_heads.1 = (bf16[1,1040,128]{2,1,0:T(8,128)(2,1)}, bf16[1,1040,128]{2,1,0:T(8,128)(2,1)}, bf16[1,1040,128]{2,1,0:T(8,128)(2,1)}, bf16[1,1040,128]{2,1,0:T(8...) custom-call(s32[4]{0:T(128)} %pad_add_fusion.place_ref, s32[1,2]{1,0:T(1,128)} %links_ref.1, ...), custom_call_target="tpu_custom_call" | custom-call | tf_op jit(solution)/shard_map/pack_heads/pallas_call | solution.py:215
  4.1 1.5 collective-permute-start.1
  5.6 0.6 collective-permute-start.2
  6.2 0.0 collective-permute-start.3
  6.2 7.3 %collective-permute-done.1.x_in = bf16[1,1040,128]{2,1,0:T(8,128)(2,1)S(1)} collective-permute-done((bf16[1,1040,128]{2,1,0:T(8,128)(2,1)}, bf16[1,1040,128]{2,1,0:T(8,128)(2,1)S(1)}, u32[]{:S(2)}, u32[]{:S(2)}) %collective-permute-start.1) | collective-permute-done | bytes 266272 | tf_op jit(solution)/shard_map/ppermute | solution.py:128
  13.6 1.5 collective-permute-start.4
  15.1 0.0 collective-permute-done.mate_in
  15.1 3.3 %collective-permute-done.2.far_in = bf16[1,1040,128]{2,1,0:T(8,128)(2,1)S(1)} collective-permute-done((bf16[1,1040,128]{2,1,0:T(8,128)(2,1)}, bf16[1,1040,128]{2,1,0:T(8,128)(2,1)S(1)}, u32[]{:S(2)}, u32[]{:S(2)}) %collective-permute-start.2) | collective-permute-done | bytes 266272 | tf_op jit(solution)/shard_map/ppermute | solution.py:128
  18.4 0.6 copy-done.11
  19.0 0.9 copy-done.14
  20.0 4.5 %attention_gradients.2.refs_0_.refs_6_ = bf16[4,256,384]{2,1,0:T(8,128)(2,1)S(1)} custom-call(s32[4]{0:T(128)S(1)} %copy-done.11, bf16[1,1040,128]{2,1,0:T(8,128)(2,1)S(1)} %copy-done.14, bf16[1,1040,128]{2,1,0:T(8,128)(2,1)S(1)} %collective-permute-done.mate_in, bf16[1,1040,128]{2,1,0:T(8,128)(2,1)S(1)} %collective-permute-done.1.x_in, ...), custom_call_target="tpu_custom_call" | custom-call | flops 2013265920 | bytes 1835008 | tf_op jit(solution)/shard_map/attention_gradients/pallas_call | solution.py:304
  24.5 1.1 turn_weights.1.own_ref
  25.5 0.8 collective-permute-start.16
  26.3 0.1 collective-permute-start.5
  26.4 1.5 %collective-permute-start.10 = (bf16[4,256,384]{2,1,0:T(8,128)(2,1)S(1)}, bf16[4,256,384]{2,1,0:T(8,128)(2,1)S(1)}, u32[]{:S(2)}, u32[]{:S(2)}) collective-permute-start(bf16[4,256,384]{2,1,0:T(8,128)(2,1)S(1)} %attention_gradients.2.refs_0_.refs_6_), channel_id=1, source_target_pairs={{0,20},{4,8},{8,28},{12,0},{16,4},{20,24},{24,12},{28,16},{1,21},{... | collective-permute-start | bytes 2359304 | tf_op jit(solution)/shard_map/ppermute | solution.py:128
  28.0 1.5 collective-permute-start.8
  29.4 0.0 collective-permute-done.3.mate_in
  29.5 1.3 collective-permute-start.6
  30.8 4.3 %attention_gradients.3.refs_1_.refs_7_ = bf16[2,256,384]{2,1,0:T(8,128)(2,1)S(1)} custom-call(s32[4]{0:T(128)S(1)} %copy-done.11, bf16[1,1040,128]{2,1,0:T(8,128)(2,1)S(1)} %copy-done.13, bf16[1,1040,128]{2,1,0:T(8,128)(2,1)S(1)} %collective-permute-done.3.mate_in, bf16[1,1040,128]{2,1,0:T(8,128)(2,1)S(1)} %collective-permute-done.4.x_in, ...), custom_call_target="tpu_custom_call" | custom-call | flops 2013265920 | bytes 1835008 | tf_op jit(solution)/shard_map/attention_gradients/pallas_call | solution.py:304
  35.1 1.3 collective-permute-start.11
  36.4 8.9 %collective-permute-done.10.refs_6_.refs_12_ = bf16[4,256,384]{2,1,0:T(8,128)(2,1)S(1)} collective-permute-done((bf16[4,256,384]{2,1,0:T(8,128)(2,1)S(1)}, bf16[4,256,384]{2,1,0:T(8,128)(2,1)S(1)}, u32[]{:S(2)}, u32[]{:S(2)}) %collective-permute-start.10) | collective-permute-done | bytes 786464 | tf_op jit(solution)/shard_map/ppermute | solution.py:128
  45.3 1.7 %collective-permute-start.9 = (bf16[2,256,384]{2,1,0:T(8,128)(2,1)S(1)}, bf16[2,256,384]{2,1,0:T(8,128)(2,1)}, u32[]{:S(2)}, u32[]{:S(2)}) collective-permute-start(bf16[2,256,384]{2,1,0:T(8,128)(2,1)S(1)} %attention_gradients.3.refs_1_.refs_7_), channel_id=1, source_target_pairs={{0,8},{4,20},{8,0},{12,28},{16,24},{20,4},{24,16},{28,12},{1,9},{5... | collective-permute-start | bytes 1179656 | tf_op jit(solution)/shard_map/ppermute | solution.py:128
  47.0 1.5 collective-permute-done.8.refs_4_.refs_10_
  48.5 1.3 collective-permute-start.7
  49.8 0.0 copy-start.2
  49.8 0.7 copy-done.2
  50.6 0.0 collective-permute-done.6.refs_2_.refs_8_
  50.6 0.9 copy-done
  51.5 4.0 %collective-permute-start.14 = (bf16[4,256,384]{2,1,0:T(8,128)(2,1)}, bf16[4,256,384]{2,1,0:T(8,128)(2,1)}, u32[]{:S(2)}, u32[]{:S(2)}) collective-permute-start(bf16[4,256,384]{2,1,0:T(8,128)(2,1)} %collective-permute-done.8.refs_4_.refs_10_), channel_id=1, source_target_pairs={{0,20},{8,28},{16,4},{24,12},{1,21},{9,29},{17,5},{25,13},{2,22},{... | collective-permute-start | bytes 2359304 | tf_op jit(solution)/shard_map/ppermute | solution.py:128
  55.5 0.7 copy-done.4
  56.2 1.6 %collective-permute-start.12 = (bf16[4,256,384]{2,1,0:T(8,128)(2,1)}, bf16[4,256,384]{2,1,0:T(8,128)(2,1)}, u32[]{:S(2)}, u32[]{:S(2)}) collective-permute-start(bf16[4,256,384]{2,1,0:T(8,128)(2,1)} %collective-permute-done.8.refs_4_.refs_10_), channel_id=1, source_target_pairs={{4,12},{12,4},{20,28},{28,20},{5,13},{13,5},{21,29},{29,21},{6,14}... | collective-permute-start | bytes 2359304 | tf_op jit(solution)/shard_map/ppermute | solution.py:128
  57.8 0.0 collective-permute-done.9.refs_5_.refs_11_
  57.8 0.0 collective-permute-done.7.refs_3_.refs_9_
  57.8 0.7 copy-done.6
  58.5 2.8 %collective-permute-start.15 = (bf16[2,256,384]{2,1,0:T(8,128)(2,1)}, bf16[2,256,384]{2,1,0:T(8,128)(2,1)}, u32[]{:S(2)}, u32[]{:S(2)}) collective-permute-start(bf16[2,256,384]{2,1,0:T(8,128)(2,1)} %collective-permute-done.9.refs_5_.refs_11_), channel_id=1, source_target_pairs={{0,20},{8,28},{16,4},{24,12},{1,21},{9,29},{17,5},{25,13},{2,22},{... | collective-permute-start | bytes 1179656 | tf_op jit(solution)/shard_map/ppermute | solution.py:128
  61.3 1.4 collective-permute-start.13
  62.7 1.9 %join_weights.1.refs_12_ = bf16[2304,768]{1,0:T(8,128)(2,1)S(1)} custom-call(s32[4]{0:T(128)S(1)} %copy-done.12, bf16[2304,384]{1,0:T(8,128)(2,1)S(1)} %turn_weights.1.own_ref, bf16[2304,384]{1,0:T(8,128)(2,1)} %collective-permute-done.16.mate_ref), custom_call_target="tpu_custom_call" | custom-call | tf_op jit(solution)/shard_map/join_weights/pallas_call | solution.py:351
  64.6 0.0 copy-start.15
  64.7 3.9 %collective-permute-done.15.refs_11_.refs_17_ = bf16[2,256,384]{2,1,0:T(8,128)(2,1)} collective-permute-done((bf16[2,256,384]{2,1,0:T(8,128)(2,1)}, bf16[2,256,384]{2,1,0:T(8,128)(2,1)}, u32[]{:S(2)}, u32[]{:S(2)}) %collective-permute-start.15) | collective-permute-done | bytes 393248 | tf_op jit(solution)/shard_map/ppermute | solution.py:128
  68.6 6.1 %input_gradient.1 = (bf16[256,768]{1,0:T(8,128)(2,1)S(1)}, bf16[256,768]{1,0:T(8,128)(2,1)S(1)}, bf16[256,768]{1,0:T(8,128)(2,1)S(1)}, bf16[256,768]{1,0:T(8,128)(2,1)S(1)}) custom-call(s32[4]{0:T(128)S(1)} %copy-done.12, bf16[4,256,384]{2,1,0:T(8,128)(2,1)S(1)} %attention_gradients.2.refs_0_.refs_6_, bf16[2,256,384]{2,1,0:T(8,128)(2,1)S(1)} %copy-done.3, ...), custom_call_target="tpu_custom_call" | custom-call | flops 3623878656 | bytes 9830400 | tf_op jit(solution)/shard_map/input_gradient/pallas_call | solution.py:408
  74.8 1.6 %collective-permute-start.17 = (bf16[256,768]{1,0:T(8,128)(2,1)S(1)}, bf16[256,768]{1,0:T(8,128)(2,1)S(1)}, u32[]{:S(2)}, u32[]{:S(2)}) collective-permute-start(bf16[256,768]{1,0:T(8,128)(2,1)S(1)} %get-tuple-element.41), channel_id=1, source_target_pairs={{0,1},{1,0},{2,3},{3,2},{4,5},{5,4},{6,7},{7,6},{8,9},{9,8},{10,11... | collective-permute-start | bytes 1179656 | tf_op jit(solution)/shard_map/ppermute | solution.py:541
  76.4 0.3 collective-permute-start.18
  76.8 1.6 %collective-permute-start.19 = (bf16[256,768]{1,0:T(8,128)(2,1)S(1)}, bf16[256,768]{1,0:T(8,128)(2,1)S(1)}, u32[]{:S(2)}, u32[]{:S(2)}) collective-permute-start(bf16[256,768]{1,0:T(8,128)(2,1)S(1)} %get-tuple-element.43), channel_id=1, source_target_pairs={{0,3},{1,2},{2,1},{3,0},{4,7},{5,6},{6,5},{7,4},{8,11},{9,10},{10,... | collective-permute-start | bytes 1179656 | tf_op jit(solution)/shard_map/ppermute | solution.py:541
  78.3 0.2 dynamic-slice_bitcast_fusion.1
  78.6 1.5 %collective-permute-start.22 = (bf16[2,256,384]{2,1,0:T(8,128)(2,1)S(1)}, bf16[2,256,384]{2,1,0:T(8,128)(2,1)S(1)}, u32[]{:S(2)}, u32[]{:S(2)}) collective-permute-start(bf16[2,256,384]{2,1,0:T(8,128)(2,1)S(1)} %pad_maximum_fusion.1), channel_id=1, source_target_pairs={{0,8},{4,20},{8,0},{12,28},{16,24},{20,4},{24,16},{28,12},{1,9},{5... | collective-permute-start | bytes 1179656 | tf_op jit(solution)/shard_map/ppermute | solution.py:128
  80.2 2.4 %collective-permute-start.23 = (bf16[2,256,384]{2,1,0:T(8,128)(2,1)S(1)}, bf16[2,256,384]{2,1,0:T(8,128)(2,1)S(1)}, u32[]{:S(2)}, u32[]{:S(2)}) collective-permute-start(bf16[2,256,384]{2,1,0:T(8,128)(2,1)S(1)} %pad_maximum_fusion.2), channel_id=1, source_target_pairs={{0,20},{4,8},{8,28},{12,0},{16,4},{20,24},{24,12},{28,16},{1,21},{... | collective-permute-start | bytes 1179656 | tf_op jit(solution)/shard_map/ppermute | solution.py:128
  82.7 8.3 %collective-permute-done.17 = bf16[256,768]{1,0:T(8,128)(2,1)S(1)} collective-permute-done((bf16[256,768]{1,0:T(8,128)(2,1)S(1)}, bf16[256,768]{1,0:T(8,128)(2,1)S(1)}, u32[]{:S(2)}, u32[]{:S(2)}) %collective-permute-start.17) | collective-permute-done | bytes 393248 | tf_op jit(solution)/shard_map/ppermute | solution.py:541
  91.0 1.3 collective-permute-start.21
  92.3 0.5 collective-permute-done.18
  92.8 15.4 %collective-permute-start.25 = (bf16[2,256,384]{2,1,0:T(8,128)(2,1)S(1)}, bf16[2,256,384]{2,1,0:T(8,128)(2,1)S(1)}, u32[]{:S(2)}, u32[]{:S(2)}) collective-permute-start(bf16[2,256,384]{2,1,0:T(8,128)(2,1)S(1)} %pad_maximum_fusion.3), channel_id=1, source_target_pairs={{0,28},{8,20},{16,12},{24,4},{1,29},{9,21},{17,13},{25,5},{2,30},{... | collective-permute-start | bytes 1179656 | tf_op jit(solution)/shard_map/ppermute | solution.py:128
  108.2 3.3 %collective-permute-done.19 = bf16[256,768]{1,0:T(8,128)(2,1)S(1)} collective-permute-done((bf16[256,768]{1,0:T(8,128)(2,1)S(1)}, bf16[256,768]{1,0:T(8,128)(2,1)S(1)}, u32[]{:S(2)}, u32[]{:S(2)}) %collective-permute-start.19) | collective-permute-done | bytes 393248 | tf_op jit(solution)/shard_map/ppermute | solution.py:541
  111.5 0.7 collective-permute-start.24
  112.2 0.2 add_convert_fusion
  112.5 1.0 collective-permute-done.25.refs_5_
  113.5 4.3 %weight_gradient_mate.1 = f32[3,384,768]{2,1,0:T(8,128)S(1)} custom-call(s32[4]{0:T(128)S(1)} %copy-done.12, bf16[2,256,384]{2,1,0:T(8,128)(2,1)S(1)} %pad_maximum_fusion.refs_0_, bf16[2,256,384]{2,1,0:T(8,128)(2,1)S(1)} %collective-permute-done.21.refs_1_, bf16[2,256,384]{2,1,0:T(8,128)(2,1)S(1)} %collective-permute-done.22.refs_2_, ...), custom_call_target="tpu_custom_call" | custom-call | flops 1811939328 | bytes 9043968 | tf_op jit(solution)/shard_map/weight_gradient_mate/pallas_call | solution.py:458
  117.8 9.4 %collective-permute-start.26 = (f32[3,384,768]{2,1,0:T(8,128)S(1)}, f32[3,384,768]{2,1,0:T(8,128)S(1)}, u32[]{:S(2)}, u32[]{:S(2)}) collective-permute-start(f32[3,384,768]{2,1,0:T(8,128)S(1)} %weight_gradient_mate.1), channel_id=1, source_target_pairs={{0,4},{4,0},{8,12},{12,8},{16,20},{20,16},{24,28},{28,24},{1,5},{5... | collective-permute-start | bytes 10616840 | tf_op jit(solution)/shard_map/ppermute | solution.py:128
  127.2 3.4 %collective-permute-start.20 = (bf16[256,768]{1,0:T(8,128)(2,1)S(1)}, bf16[256,768]{1,0:T(8,128)(2,1)S(1)}, u32[]{:S(2)}, u32[]{:S(2)}) collective-permute-start(bf16[256,768]{1,0:T(8,128)(2,1)S(1)} %add_convert_fusion), channel_id=1, source_target_pairs={{0,0},{1,5},{2,10},{3,15},{4,20},{5,17},{6,30},{7,27},{8,8},{9,13}... | collective-permute-start | bytes 1179656 | tf_op jit(solution)/shard_map/ppermute | solution.py:577
  130.6 2.5 %collective-permute-done.26.refs_18_ = f32[3,384,768]{2,1,0:T(8,128)S(1)} collective-permute-done((f32[3,384,768]{2,1,0:T(8,128)S(1)}, f32[3,384,768]{2,1,0:T(8,128)S(1)}, u32[]{:S(2)}, u32[]{:S(2)}) %collective-permute-start.26) | collective-permute-done | bytes 3538976 | tf_op jit(solution)/shard_map/ppermute | solution.py:128
  133.1 6.3 %weight_gradient_own.1 = (f32[384,768]{1,0:T(8,128)}, f32[384,768]{1,0:T(8,128)}, f32[384,768]{1,0:T(8,128)}) custom-call(s32[4]{0:T(128)S(1)} %copy-done.12, bf16[2,256,384]{2,1,0:T(8,128)(2,1)S(1)} %pad_maximum_fusion.refs_0_, bf16[2,256,384]{2,1,0:T(8,128)(2,1)S(1)} %collective-permute-done.21.refs_1_, ...), custom_call_target="tpu_custom_call" | custom-call | flops 1811939328 | bytes 9043968 | tf_op jit(solution)/shard_map/weight_gradient_own/pallas_call | solution.py:458
  139.4 1.6 %collective-permute-done.20 = bf16[256,768]{1,0:T(8,128)(2,1)S(1)} collective-permute-done((bf16[256,768]{1,0:T(8,128)(2,1)S(1)}, bf16[256,768]{1,0:T(8,128)(2,1)S(1)}, u32[]{:S(2)}, u32[]{:S(2)}) %collective-permute-start.20) | collective-permute-done | bytes 393248 | tf_op jit(solution)/shard_map/ppermute | solution.py:577
  141.1 1.9 %collective-permute-start.27 = (bf16[256,768]{1,0:T(8,128)(2,1)S(1)}, bf16[256,768]{1,0:T(8,128)(2,1)S(1)}, u32[]{:S(2)}, u32[]{:S(2)}) collective-permute-start(bf16[256,768]{1,0:T(8,128)(2,1)S(1)} %collective-permute-done.20), channel_id=1, source_target_pairs={{0,0},{5,4},{10,8},{15,12},{20,20},{17,16},{30,28},{27,24},{8,9},{... | collective-permute-start | bytes 1179656 | tf_op jit(solution)/shard_map/ppermute | solution.py:583
  143.0 11.1 %collective-permute-done.27 = bf16[256,768]{1,0:T(8,128)(2,1)S(1)} collective-permute-done((bf16[256,768]{1,0:T(8,128)(2,1)S(1)}, bf16[256,768]{1,0:T(8,128)(2,1)S(1)}, u32[]{:S(2)}, u32[]{:S(2)}) %collective-permute-start.27) | collective-permute-done | bytes 393248 | tf_op jit(solution)/shard_map/ppermute | solution.py:583
  154.1 0.7 copy.14
  (40 shorter events, 0.3 us)
Async XLA Ops:
  4.1 9.5 %collective-permute-start.1 = (bf16[1,1040,128]{2,1,0:T(8,128)(2,1)}, bf16[1,1040,128]{2,1,0:T(8,128)(2,1)S(1)}, u32[]{:S(2)}, u32[]{:S(2)}) collective-permute-start(bf16[1,1040,128]{2,1,0:T(8,128)(2,1)} %get-tuple-element.29), channel_id=1, source_target_pairs={{0,8},{4,12},{8,0},{12,4},{16,24},{20,28},{24,16},{28,20},{1,9},{5... | collective-permute-start | bytes 798728 | tf_op jit(solution)/shard_map/ppermute | solution.py:128
  5.6 9.5 %collective-permute-start = (bf16[1,1040,128]{2,1,0:T(8,128)(2,1)}, bf16[1,1040,128]{2,1,0:T(8,128)(2,1)S(1)}, u32[]{:S(2)}, u32[]{:S(2)}) collective-permute-start(bf16[1,1040,128]{2,1,0:T(8,128)(2,1)} %get-tuple-element.28), channel_id=1, source_target_pairs={{0,4},{4,0},{8,12},{12,8},{16,20},{20,16},{24,28},{28,24},{1,5},{5... | collective-permute-start | bytes 798728 | tf_op jit(solution)/shard_map/ppermute | solution.py:128
  5.6 12.8 %collective-permute-start.2 = (bf16[1,1040,128]{2,1,0:T(8,128)(2,1)}, bf16[1,1040,128]{2,1,0:T(8,128)(2,1)S(1)}, u32[]{:S(2)}, u32[]{:S(2)}) collective-permute-start(bf16[1,1040,128]{2,1,0:T(8,128)(2,1)} %get-tuple-element.30), channel_id=1, source_target_pairs={{0,12},{4,8},{8,4},{12,0},{16,28},{20,24},{24,20},{28,16},{1,13},{... | collective-permute-start | bytes 798728 | tf_op jit(solution)/shard_map/ppermute | solution.py:128
  6.2 23.2 %collective-permute-start.3 = (bf16[1,1040,128]{2,1,0:T(8,128)(2,1)}, bf16[1,1040,128]{2,1,0:T(8,128)(2,1)S(1)}, u32[]{:S(2)}, u32[]{:S(2)}) collective-permute-start(bf16[1,1040,128]{2,1,0:T(8,128)(2,1)} %get-tuple-element.35.own), channel_id=1, source_target_pairs={{0,4},{4,0},{8,12},{12,8},{16,20},{20,16},{24,28},{28,24},{1,5},{5... | collective-permute-start | bytes 798728 | tf_op jit(solution)/shard_map/ppermute | solution.py:128
  13.6 12.8 %collective-permute-start.4 = (bf16[1,1040,128]{2,1,0:T(8,128)(2,1)}, bf16[1,1040,128]{2,1,0:T(8,128)(2,1)S(1)}, u32[]{:S(2)}, u32[]{:S(2)}) collective-permute-start(bf16[1,1040,128]{2,1,0:T(8,128)(2,1)} %get-tuple-element.37), channel_id=1, source_target_pairs={{0,8},{4,12},{8,0},{12,4},{16,24},{20,28},{24,16},{28,20},{1,9},{5... | collective-permute-start | bytes 798728 | tf_op jit(solution)/shard_map/ppermute | solution.py:128
  18.4 0.6 copy-start.11
  19.0 1.0 copy-start.14
  20.0 4.5 %copy-start.8 = (bf16[384,768]{1,0:T(8,128)(2,1)S(1)}, bf16[384,768]{1,0:T(8,128)(2,1)}, u32[]{:S(2)}) copy-start(bf16[384,768]{1,0:T(8,128)(2,1)} %q_ref) | copy-start | bytes 1769476
  20.0 4.5 %copy-start.9 = (bf16[384,768]{1,0:T(8,128)(2,1)S(1)}, bf16[384,768]{1,0:T(8,128)(2,1)}, u32[]{:S(2)}) copy-start(bf16[384,768]{1,0:T(8,128)(2,1)} %k_ref) | copy-start | bytes 1769476
  20.0 4.5 %copy-start.10 = (bf16[384,768]{1,0:T(8,128)(2,1)S(1)}, bf16[384,768]{1,0:T(8,128)(2,1)}, u32[]{:S(2)}) copy-start(bf16[384,768]{1,0:T(8,128)(2,1)} %v_ref) | copy-start | bytes 1769476
  24.5 6.3 %copy-start.13 = (bf16[1,1040,128]{2,1,0:T(8,128)(2,1)S(1)}, bf16[1,1040,128]{2,1,0:T(8,128)(2,1)}, u32[]{:S(2)}) copy-start(bf16[1,1040,128]{2,1,0:T(8,128)(2,1)} %get-tuple-element.35.own) | copy-start | bytes 798724
  25.5 37.2 %copy-start.12 = (s32[4]{0:T(128)S(1)}, s32[4]{0:T(128)}, u32[]{:S(2)}) copy-start(s32[4]{0:T(128)} %pad_add_fusion.place_ref) | copy-start | bytes 52
  25.5 37.1 %collective-permute-start.16 = (bf16[2304,384]{1,0:T(8,128)(2,1)S(1)}, bf16[2304,384]{1,0:T(8,128)(2,1)}, u32[]{:S(2)}, u32[]{:S(2)}) collective-permute-start(bf16[2304,384]{1,0:T(8,128)(2,1)S(1)} %turn_weights.1.own_ref), channel_id=1, source_target_pairs={{0,4},{4,0},{8,12},{12,8},{16,20},{20,16},{24,28},{28,24},{1,5},{5... | collective-permute-start | bytes 5308424 | tf_op jit(solution)/shard_map/ppermute | solution.py:128
  26.3 4.4 %collective-permute-start.5 = (bf16[1,1040,128]{2,1,0:T(8,128)(2,1)S(1)}, bf16[1,1040,128]{2,1,0:T(8,128)(2,1)S(1)}, u32[]{:S(2)}, u32[]{:S(2)}) collective-permute-start(bf16[1,1040,128]{2,1,0:T(8,128)(2,1)S(1)} %collective-permute-done.4.x_in), channel_id=1, source_target_pairs={{0,4},{4,0},{8,12},{12,8},{16,20},{20,16},{24,28},{28,24},{1,5},{5... | collective-permute-start | bytes 798728 | tf_op jit(solution)/shard_map/ppermute | solution.py:128
  26.4 18.9 %collective-permute-start.10 = (bf16[4,256,384]{2,1,0:T(8,128)(2,1)S(1)}, bf16[4,256,384]{2,1,0:T(8,128)(2,1)S(1)}, u32[]{:S(2)}, u32[]{:S(2)}) collective-permute-start(bf16[4,256,384]{2,1,0:T(8,128)(2,1)S(1)} %attention_gradients.2.refs_0_.refs_6_), channel_id=1, source_target_pairs={{0,20},{4,8},{8,28},{12,0},{16,4},{20,24},{24,12},{28,16},{1,21},{... | collective-permute-start | bytes 2359304 | tf_op jit(solution)/shard_map/ppermute | solution.py:128
  28.0 20.6 %collective-permute-start.8 = (bf16[4,256,384]{2,1,0:T(8,128)(2,1)S(1)}, bf16[4,256,384]{2,1,0:T(8,128)(2,1)}, u32[]{:S(2)}, u32[]{:S(2)}) collective-permute-start(bf16[4,256,384]{2,1,0:T(8,128)(2,1)S(1)} %attention_gradients.2.refs_0_.refs_6_), channel_id=1, source_target_pairs={{0,8},{4,20},{8,0},{12,28},{16,24},{20,4},{24,16},{28,12},{1,9},{5... | collective-permute-start | bytes 2359304 | tf_op jit(solution)/shard_map/ppermute | solution.py:128
  29.5 21.1 %collective-permute-start.6 = (bf16[4,256,384]{2,1,0:T(8,128)(2,1)S(1)}, bf16[4,256,384]{2,1,0:T(8,128)(2,1)S(1)}, u32[]{:S(2)}, u32[]{:S(2)}) collective-permute-start(bf16[4,256,384]{2,1,0:T(8,128)(2,1)S(1)} %attention_gradients.2.refs_0_.refs_6_), channel_id=1, source_target_pairs={{4,0},{12,8},{20,16},{28,24},{5,1},{13,9},{21,17},{29,25},{6,2},{1... | collective-permute-start | bytes 2359304 | tf_op jit(solution)/shard_map/ppermute | solution.py:128
  35.1 20.4 %collective-permute-start.11 = (bf16[2,256,384]{2,1,0:T(8,128)(2,1)S(1)}, bf16[2,256,384]{2,1,0:T(8,128)(2,1)S(1)}, u32[]{:S(2)}, u32[]{:S(2)}) collective-permute-start(bf16[2,256,384]{2,1,0:T(8,128)(2,1)S(1)} %attention_gradients.3.refs_1_.refs_7_), channel_id=1, source_target_pairs={{0,20},{4,8},{8,28},{12,0},{16,4},{20,24},{24,12},{28,16},{1,21},{... | collective-permute-start | bytes 1179656 | tf_op jit(solution)/shard_map/ppermute | solution.py:128
  45.3 12.4 %collective-permute-start.9 = (bf16[2,256,384]{2,1,0:T(8,128)(2,1)S(1)}, bf16[2,256,384]{2,1,0:T(8,128)(2,1)}, u32[]{:S(2)}, u32[]{:S(2)}) collective-permute-start(bf16[2,256,384]{2,1,0:T(8,128)(2,1)S(1)} %attention_gradients.3.refs_1_.refs_7_), channel_id=1, source_target_pairs={{0,8},{4,20},{8,0},{12,28},{16,24},{20,4},{24,16},{28,12},{1,9},{5... | collective-permute-start | bytes 1179656 | tf_op jit(solution)/shard_map/ppermute | solution.py:128
  48.5 9.2 %collective-permute-start.7 = (bf16[2,256,384]{2,1,0:T(8,128)(2,1)S(1)}, bf16[2,256,384]{2,1,0:T(8,128)(2,1)S(1)}, u32[]{:S(2)}, u32[]{:S(2)}) collective-permute-start(bf16[2,256,384]{2,1,0:T(8,128)(2,1)S(1)} %attention_gradients.3.refs_1_.refs_7_), channel_id=1, source_target_pairs={{4,0},{12,8},{20,16},{28,24},{5,1},{13,9},{21,17},{29,25},{6,2},{1... | collective-permute-start | bytes 1179656 | tf_op jit(solution)/shard_map/ppermute | solution.py:128
  49.8 0.7 copy-start.2
  50.6 0.9 copy-start
  51.5 17.1 %collective-permute-start.14 = (bf16[4,256,384]{2,1,0:T(8,128)(2,1)}, bf16[4,256,384]{2,1,0:T(8,128)(2,1)}, u32[]{:S(2)}, u32[]{:S(2)}) collective-permute-start(bf16[4,256,384]{2,1,0:T(8,128)(2,1)} %collective-permute-done.8.refs_4_.refs_10_), channel_id=1, source_target_pairs={{0,20},{8,28},{16,4},{24,12},{1,21},{9,29},{17,5},{25,13},{2,22},{... | collective-permute-start | bytes 2359304 | tf_op jit(solution)/shard_map/ppermute | solution.py:128
  55.5 0.7 copy-start.4
  56.2 12.4 %collective-permute-start.12 = (bf16[4,256,384]{2,1,0:T(8,128)(2,1)}, bf16[4,256,384]{2,1,0:T(8,128)(2,1)}, u32[]{:S(2)}, u32[]{:S(2)}) collective-permute-start(bf16[4,256,384]{2,1,0:T(8,128)(2,1)} %collective-permute-done.8.refs_4_.refs_10_), channel_id=1, source_target_pairs={{4,12},{12,4},{20,28},{28,20},{5,13},{13,5},{21,29},{29,21},{6,14}... | collective-permute-start | bytes 2359304 | tf_op jit(solution)/shard_map/ppermute | solution.py:128
  57.8 0.7 copy-start.6
  58.5 10.1 %collective-permute-start.15 = (bf16[2,256,384]{2,1,0:T(8,128)(2,1)}, bf16[2,256,384]{2,1,0:T(8,128)(2,1)}, u32[]{:S(2)}, u32[]{:S(2)}) collective-permute-start(bf16[2,256,384]{2,1,0:T(8,128)(2,1)} %collective-permute-done.9.refs_5_.refs_11_), channel_id=1, source_target_pairs={{0,20},{8,28},{16,4},{24,12},{1,21},{9,29},{17,5},{25,13},{2,22},{... | collective-permute-start | bytes 1179656 | tf_op jit(solution)/shard_map/ppermute | solution.py:128
  61.3 7.3 %collective-permute-start.13 = (bf16[2,256,384]{2,1,0:T(8,128)(2,1)}, bf16[2,256,384]{2,1,0:T(8,128)(2,1)}, u32[]{:S(2)}, u32[]{:S(2)}) collective-permute-start(bf16[2,256,384]{2,1,0:T(8,128)(2,1)} %collective-permute-done.9.refs_5_.refs_11_), channel_id=1, source_target_pairs={{4,12},{12,4},{20,28},{28,20},{5,13},{13,5},{21,29},{29,21},{6,14}... | collective-permute-start | bytes 1179656 | tf_op jit(solution)/shard_map/ppermute | solution.py:128
  62.7 5.9 %copy-start.1 = (bf16[4,256,384]{2,1,0:T(8,128)(2,1)S(1)}, bf16[4,256,384]{2,1,0:T(8,128)(2,1)}, u32[]{:S(2)}) copy-start(bf16[4,256,384]{2,1,0:T(8,128)(2,1)} %copy-done) | copy-start | bytes 2359300
  62.7 5.9 %copy-start.3 = (bf16[2,256,384]{2,1,0:T(8,128)(2,1)S(1)}, bf16[2,256,384]{2,1,0:T(8,128)(2,1)}, u32[]{:S(2)}) copy-start(bf16[2,256,384]{2,1,0:T(8,128)(2,1)} %copy-done.2) | copy-start | bytes 1179652
  62.7 5.9 %copy-start.5 = (bf16[2,256,384]{2,1,0:T(8,128)(2,1)S(1)}, bf16[2,256,384]{2,1,0:T(8,128)(2,1)}, u32[]{:S(2)}) copy-start(bf16[2,256,384]{2,1,0:T(8,128)(2,1)} %copy-done.4) | copy-start | bytes 1179652
  62.7 6.0 %copy-start.7 = (bf16[2,256,384]{2,1,0:T(8,128)(2,1)S(1)}, bf16[2,256,384]{2,1,0:T(8,128)(2,1)}, u32[]{:S(2)}) copy-start(bf16[2,256,384]{2,1,0:T(8,128)(2,1)} %copy-done.6) | copy-start | bytes 1179652
  64.6 13.7 %copy-start.15 = (bf16[1,1,256,3072]{3,2,1,0:T(8,128)(2,1)S(1)}, bf16[1,1,256,3072]{3,2,1,0:T(8,128)(2,1)}, u32[]{:S(2)}) copy-start(bf16[1,1,256,3072]{3,2,1,0:T(8,128)(2,1)} %param.9) | copy-start | bytes 4718596
  74.8 16.2 %collective-permute-start.17 = (bf16[256,768]{1,0:T(8,128)(2,1)S(1)}, bf16[256,768]{1,0:T(8,128)(2,1)S(1)}, u32[]{:S(2)}, u32[]{:S(2)}) collective-permute-start(bf16[256,768]{1,0:T(8,128)(2,1)S(1)} %get-tuple-element.41), channel_id=1, source_target_pairs={{0,1},{1,0},{2,3},{3,2},{4,5},{5,4},{6,7},{7,6},{8,9},{9,8},{10,11... | collective-permute-start | bytes 1179656 | tf_op jit(solution)/shard_map/ppermute | solution.py:541
  76.4 16.4 %collective-permute-start.18 = (bf16[256,768]{1,0:T(8,128)(2,1)S(1)}, bf16[256,768]{1,0:T(8,128)(2,1)S(1)}, u32[]{:S(2)}, u32[]{:S(2)}) collective-permute-start(bf16[256,768]{1,0:T(8,128)(2,1)S(1)} %get-tuple-element.42), channel_id=1, source_target_pairs={{0,2},{1,3},{2,0},{3,1},{4,6},{5,7},{6,4},{7,5},{8,10},{9,11},{10,... | collective-permute-start | bytes 1179656 | tf_op jit(solution)/shard_map/ppermute | solution.py:541
  76.8 34.8 %collective-permute-start.19 = (bf16[256,768]{1,0:T(8,128)(2,1)S(1)}, bf16[256,768]{1,0:T(8,128)(2,1)S(1)}, u32[]{:S(2)}, u32[]{:S(2)}) collective-permute-start(bf16[256,768]{1,0:T(8,128)(2,1)S(1)} %get-tuple-element.43), channel_id=1, source_target_pairs={{0,3},{1,2},{2,1},{3,0},{4,7},{5,6},{6,5},{7,4},{8,11},{9,10},{10,... | collective-permute-start | bytes 1179656 | tf_op jit(solution)/shard_map/ppermute | solution.py:541
  78.6 33.8 %collective-permute-start.22 = (bf16[2,256,384]{2,1,0:T(8,128)(2,1)S(1)}, bf16[2,256,384]{2,1,0:T(8,128)(2,1)S(1)}, u32[]{:S(2)}, u32[]{:S(2)}) collective-permute-start(bf16[2,256,384]{2,1,0:T(8,128)(2,1)S(1)} %pad_maximum_fusion.1), channel_id=1, source_target_pairs={{0,8},{4,20},{8,0},{12,28},{16,24},{20,4},{24,16},{28,12},{1,9},{5... | collective-permute-start | bytes 1179656 | tf_op jit(solution)/shard_map/ppermute | solution.py:128
  80.2 32.2 %collective-permute-start.23 = (bf16[2,256,384]{2,1,0:T(8,128)(2,1)S(1)}, bf16[2,256,384]{2,1,0:T(8,128)(2,1)S(1)}, u32[]{:S(2)}, u32[]{:S(2)}) collective-permute-start(bf16[2,256,384]{2,1,0:T(8,128)(2,1)S(1)} %pad_maximum_fusion.2), channel_id=1, source_target_pairs={{0,20},{4,8},{8,28},{12,0},{16,4},{20,24},{24,12},{28,16},{1,21},{... | collective-permute-start | bytes 1179656 | tf_op jit(solution)/shard_map/ppermute | solution.py:128
  91.0 21.4 %collective-permute-start.21 = (bf16[2,256,384]{2,1,0:T(8,128)(2,1)S(1)}, bf16[2,256,384]{2,1,0:T(8,128)(2,1)S(1)}, u32[]{:S(2)}, u32[]{:S(2)}) collective-permute-start(bf16[2,256,384]{2,1,0:T(8,128)(2,1)S(1)} %pad_maximum_fusion.refs_0_), channel_id=1, source_target_pairs={{4,0},{12,8},{20,16},{28,24},{5,1},{13,9},{21,17},{29,25},{6,2},{1... | collective-permute-start | bytes 1179656 | tf_op jit(solution)/shard_map/ppermute | solution.py:128
  92.8 20.7 %collective-permute-start.25 = (bf16[2,256,384]{2,1,0:T(8,128)(2,1)S(1)}, bf16[2,256,384]{2,1,0:T(8,128)(2,1)S(1)}, u32[]{:S(2)}, u32[]{:S(2)}) collective-permute-start(bf16[2,256,384]{2,1,0:T(8,128)(2,1)S(1)} %pad_maximum_fusion.3), channel_id=1, source_target_pairs={{0,28},{8,20},{16,12},{24,4},{1,29},{9,21},{17,13},{25,5},{2,30},{... | collective-permute-start | bytes 1179656 | tf_op jit(solution)/shard_map/ppermute | solution.py:128
  111.5 2.0 %collective-permute-start.24 = (bf16[2,256,384]{2,1,0:T(8,128)(2,1)S(1)}, bf16[2,256,384]{2,1,0:T(8,128)(2,1)S(1)}, u32[]{:S(2)}, u32[]{:S(2)}) collective-permute-start(bf16[2,256,384]{2,1,0:T(8,128)(2,1)S(1)} %pad_maximum_fusion.3), channel_id=1, source_target_pairs={{4,28},{12,20},{20,12},{28,4},{5,29},{13,21},{21,13},{29,5},{6,30}... | collective-permute-start | bytes 1179656 | tf_op jit(solution)/shard_map/ppermute | solution.py:128
  117.8 15.3 %collective-permute-start.26 = (f32[3,384,768]{2,1,0:T(8,128)S(1)}, f32[3,384,768]{2,1,0:T(8,128)S(1)}, u32[]{:S(2)}, u32[]{:S(2)}) collective-permute-start(f32[3,384,768]{2,1,0:T(8,128)S(1)} %weight_gradient_mate.1), channel_id=1, source_target_pairs={{0,4},{4,0},{8,12},{12,8},{16,20},{20,16},{24,28},{28,24},{1,5},{5... | collective-permute-start | bytes 10616840 | tf_op jit(solution)/shard_map/ppermute | solution.py:128
  127.2 13.8 %collective-permute-start.20 = (bf16[256,768]{1,0:T(8,128)(2,1)S(1)}, bf16[256,768]{1,0:T(8,128)(2,1)S(1)}, u32[]{:S(2)}, u32[]{:S(2)}) collective-permute-start(bf16[256,768]{1,0:T(8,128)(2,1)S(1)} %add_convert_fusion), channel_id=1, source_target_pairs={{0,0},{1,5},{2,10},{3,15},{4,20},{5,17},{6,30},{7,27},{8,8},{9,13}... | collective-permute-start | bytes 1179656 | tf_op jit(solution)/shard_map/ppermute | solution.py:577
  141.1 13.0 %collective-permute-start.27 = (bf16[256,768]{1,0:T(8,128)(2,1)S(1)}, bf16[256,768]{1,0:T(8,128)(2,1)S(1)}, u32[]{:S(2)}, u32[]{:S(2)}) collective-permute-start(bf16[256,768]{1,0:T(8,128)(2,1)S(1)} %collective-permute-done.20), channel_id=1, source_target_pairs={{0,0},{5,4},{10,8},{15,12},{20,20},{17,16},{30,28},{27,24},{8,9},{... | collective-permute-start | bytes 1179656 | tf_op jit(solution)/shard_map/ppermute | solution.py:583

commit v10 on v9

--- a/solution.py
+++ b/solution.py
@@ -411,7 +411,7 @@
         in_specs=[whole(pltpu.SMEM)] + [whole()] * (len(grads) + 1),
         out_specs=[whole()] * 4,
         scratch_shapes=[pltpu.VMEM((4, length, rows), jnp.bfloat16)],
-        compiler_params=pltpu.CompilerParams(vmem_limit_bytes=24 * MIB),
+        compiler_params=pltpu.CompilerParams(vmem_limit_bytes=16 * MIB),
         cost_estimate=pl.CostEstimate(
             flops=8 * length * rows * depth,
             bytes_accessed=8 * length * (rows + depth) + 2 * rows * depth,
@@ -461,7 +461,7 @@
         in_specs=[whole(pltpu.SMEM)] + [whole()] * (6 + len(grads) + len(received)),
         out_specs=[whole()] * 3 if mine else whole(),
         scratch_shapes=[pltpu.VMEM((rows, 4 * length), jnp.bfloat16)],
-        compiler_params=pltpu.CompilerParams(vmem_limit_bytes=24 * MIB),
+        compiler_params=pltpu.CompilerParams(vmem_limit_bytes=16 * MIB),
         cost_estimate=pl.CostEstimate(
             flops=8 * rows * 3 * cols * length,
             bytes_accessed=8 * length * (rows + 3 * cols) + 12 * rows * cols,
@@ -518,6 +518,22 @@
         x_in = moved(to_x, along_x)
         sets.append(((0, 2), (own, moved(own, mate), x_in, moved(x_in, mate))))
 
+    flat = normed.reshape(length, model_width)
+
+    def columns(of_chip):
+        columns = [
+            lax.dynamic_slice_in_dim(flat, (2 * of_chip + part) * rows, rows, axis=1)
+            for part in range(2)
+        ]
+        return jnp.stack(columns)
+
+    toward_x, toward_y = jnp.bitwise_xor(chip, 1), jnp.bitwise_xor(chip, 2)
+    here = columns(chip)
+    to_straight = columns(jnp.where(core == 0, toward_x, toward_y))
+    to_crossed = columns(jnp.where(core == 0, toward_y, toward_x))
+    to_corner = columns(jnp.bitwise_xor(chip, 3))
+    mate_here = moved(here, only(1, mate))
+
     own_weights, turn = None, place
     parts = []
     for kept, sources in sets:
@@ -529,7 +545,7 @@
         ahead = moved(made, straight)
         aside = moved(made, crossed)
         inward = moved(made, only(1, mate))
-        (sent,) = after((ahead,), aside, inward)
+        (sent,) = after((ahead,), aside, inward, mate_here, to_straight, to_crossed, to_corner)
         relay_x = moved(sent, only(1, along_x))
         relay_y = moved(sent, only(0, across_y))
         parts.append((made, inward, ahead, aside, relay_x, relay_y))
@@ -544,25 +560,15 @@
     total = sum(array.astype(jnp.float32) for array in (slots[0], *arrived))
     total = total.astype(jnp.bfloat16)
 
-    (flat,) = after((normed.reshape(length, model_width),), *slots)
-
-    def columns(of_chip):
-        columns = [
-            lax.dynamic_slice_in_dim(flat, (2 * of_chip + part) * rows, rows, axis=1)
-            for part in range(2)
-        ]
-        return jnp.stack(columns)
-
-    toward_x, toward_y = jnp.bitwise_xor(chip, 1), jnp.bitwise_xor(chip, 2)
-    here = columns(chip)
-    to_straight = columns(jnp.where(core == 0, toward_x, toward_y))
-    to_crossed = columns(jnp.where(core == 0, toward_y, toward_x))
-    to_corner = columns(jnp.bitwise_xor(chip, 3))
+    to_straight, to_crossed = after((to_straight, to_crossed), *slots)
+    normed_ahead = moved(to_straight, straight)
+    normed_aside = moved(to_crossed, crossed)
+    (to_corner,) = after((to_corner,), normed_ahead, normed_aside)
     tokens = (
         here,
-        moved(here, only(1, mate)),
-        moved(to_straight, straight),
-        moved(to_crossed, crossed),
+        mate_here,
+        normed_ahead,
+        normed_aside,
         moved(to_corner, corner_same),
         moved(to_corner, corner_cross),
     )
@@ -579,7 +585,7 @@
         ("dp", "view", "head"),
         [(spot(y, v, z), spot(y ^ (v % 2), v ^ z, z)) for y, v, z in corners],
     )
-    (beside,) = after((beside,), weight_grads[0])
+    (beside,) = after((beside,), for_mate)
     input_grad = lax.ppermute(
         beside,
         ("dp", "view", "head"),
@@ -592,6 +598,7 @@
         ],
     )
 
+    (input_grad,) = after((input_grad,), *weight_grads)
     return (
         input_grad.reshape(1, 1, length, model_width // groups),
         *weight_grads,

time: 155 us -> 146 us (0.942)
  starting transfers between devices: 62.4 us -> 40.2 us
  waiting for transfers between devices: 53.4 us -> 74.6 us
  Pallas kernels: 31.3 us -> 25.8 us
  local copies, waits for them, and re-layouts: 5.73 us -> 2.58 us
    ppermute x23, starting transfers between devices: 53.6 us -> 32.3 us  [moved(): return lax.ppermute(value, ('dp', 'view'), pairs)]
    ppermute x3, waiting for transfers between devices: 12.1 us -> 23.9 us  [gather_body(): lax.ppermute(slots[s], 'head', [(z, z ^ s) for z in range(groups)])]
    ppermute x1, waiting for transfers between devices: 1.64 us -> 10.9 us  [gather_body(): lax.ppermute(total, ('dp', 'view', 'head'), [(spot(y, v, z), spot(y ^ v %...]
    ppermute x23, waiting for transfers between devices: 28.6 us -> 32.6 us  [moved(): return lax.ppermute(value, ('dp', 'view'), pairs)]
    ppermute x1, waiting for transfers between devices: 11.1 us -> 7.23 us  [gather_body(): lax.ppermute(beside, ('dp', 'view', 'head'), [(spot(y ^ v % 2, v ^ z, z),...]
    unnamed x33 -> x17, local copies, waits for them, and re-layouts: 5.49 us -> 2.35 us
    pallas_call x2, Pallas kernels: 10.6 us -> 7.66 us  [weight_product(): pl.pallas_call(functools.partial(weight_kernel, mine, mean_scale, len(gra...]
  transfers between devices with their start and end apart: 28 -> 28, of which waited for: 12 -> 13; matrix products, arithmetic and copies ran while one was open for 0% -> 0% of each run, Pallas kernels for 12% -> 11%
where the time goes in v10:
time: 146 us; the launch traced here: 145 us
  waiting for transfers between devices  74.6 us (51%)
  starting transfers between devices  40.2 us (28%)
  Pallas kernels  25.8 us (18%)
  local copies, waits for them, and re-layouts  2.58 us (2%)
    ppermute x23, waiting for transfers between devices, moved(): return lax.ppermute(value, ('dp', 'view'), pairs)  32.6 us
    ppermute x23, starting transfers between devices, moved(): return lax.ppermute(value, ('dp', 'view'), pairs)  32.3 us
    ppermute x3, waiting for transfers between devices, gather_body(): lax.ppermute(slots[s], 'head', [(z, z ^ s) for z in range(groups)])  23.9 us
    ppermute x1, waiting for transfers between devices, gather_body(): lax.ppermute(total, ('dp', 'view', 'head'), [(spot(y, v, z), spot(y ^ v %...  10.9 us
    pallas_call x2, Pallas kernels, attention(): pl.pallas_call(functools.partial(attention_kernel, HD ** (-0.5), kept), o...  8.76 us
    pallas_call x2, Pallas kernels, weight_product(): pl.pallas_call(functools.partial(weight_kernel, mine, mean_scale, len(gra...  7.66 us
    ppermute x1, waiting for transfers between devices, gather_body(): lax.ppermute(beside, ('dp', 'view', 'head'), [(spot(y ^ v % 2, v ^ z, z),...  7.23 us
    pallas_call x1, Pallas kernels, input_product(): pl.pallas_call(functools.partial(input_kernel, len(grads) // 6), out_shap...  4.66 us
  transfers between devices with their start and end apart: 28, of which 13 were waited for; matrix products, arithmetic and copies ran while one was open for 0% of the time, Pallas kernels for 11%

profile of v10, /device:TPU:16, one launch (start us, length us, event | category | flops | bytes accessed | tf_op | source)
XLA Modules:
  0.0 145.1 jit_solution(7186060231060076479)
XLA Ops:
  0.7 0.6 pad_add_fusion.place_ref
  1.3 2.8 %pack_heads.1 = (bf16[1,1040,128]{2,1,0:T(8,128)(2,1)}, bf16[1,1040,128]{2,1,0:T(8,128)(2,1)}, bf16[1,1040,128]{2,1,0:T(8,128)(2,1)}, bf16[1,1040,128]{2,1,0:T(8...) custom-call(s32[4]{0:T(128)} %pad_add_fusion.place_ref, s32[1,2]{1,0:T(1,128)} %links_ref.1, ...), custom_call_target="tpu_custom_call" | custom-call | tf_op jit(solution)/shard_map/pack_heads/pallas_call | solution.py:215
  4.1 1.5 %collective-permute-start.1 = (bf16[1,1040,128]{2,1,0:T(8,128)(2,1)}, bf16[1,1040,128]{2,1,0:T(8,128)(2,1)S(1)}, u32[]{:S(2)}, u32[]{:S(2)}) collective-permute-start(bf16[1,1040,128]{2,1,0:T(8,128)(2,1)} %get-tuple-element.32), channel_id=1, source_target_pairs={{0,8},{4,12},{8,0},{12,4},{16,24},{20,28},{24,16},{28,20},{1,9},{5... | collective-permute-start | bytes 798728 | tf_op jit(solution)/shard_map/ppermute | solution.py:128
  5.6 0.0 collective-permute-start
  5.6 0.6 collective-permute-start.2
  6.2 7.3 %collective-permute-done.1.x_in = bf16[1,1040,128]{2,1,0:T(8,128)(2,1)S(1)} collective-permute-done((bf16[1,1040,128]{2,1,0:T(8,128)(2,1)}, bf16[1,1040,128]{2,1,0:T(8,128)(2,1)S(1)}, u32[]{:S(2)}, u32[]{:S(2)}) %collective-permute-start.1) | collective-permute-done | bytes 266272 | tf_op jit(solution)/shard_map/ppermute | solution.py:128
  13.6 1.5 %collective-permute-start.4 = (bf16[1,1040,128]{2,1,0:T(8,128)(2,1)}, bf16[1,1040,128]{2,1,0:T(8,128)(2,1)S(1)}, u32[]{:S(2)}, u32[]{:S(2)}) collective-permute-start(bf16[1,1040,128]{2,1,0:T(8,128)(2,1)} %get-tuple-element.40), channel_id=1, source_target_pairs={{0,8},{4,12},{8,0},{12,4},{16,24},{20,28},{24,16},{28,20},{1,9},{5... | collective-permute-start | bytes 798728 | tf_op jit(solution)/shard_map/ppermute | solution.py:128
  15.0 0.0 collective-permute-start.3
  15.0 0.0 collective-permute-done.mate_in
  15.1 3.3 %collective-permute-done.2.far_in = bf16[1,1040,128]{2,1,0:T(8,128)(2,1)S(1)} collective-permute-done((bf16[1,1040,128]{2,1,0:T(8,128)(2,1)}, bf16[1,1040,128]{2,1,0:T(8,128)(2,1)S(1)}, u32[]{:S(2)}, u32[]{:S(2)}) %collective-permute-start.2) | collective-permute-done | bytes 266272 | tf_op jit(solution)/shard_map/ppermute | solution.py:128
  18.4 0.6 copy-done.3
  19.0 0.9 copy-done.6
  20.0 4.4 %attention_gradients.2.refs_0_.refs_6_ = bf16[4,256,384]{2,1,0:T(8,128)(2,1)S(1)} custom-call(s32[4]{0:T(128)S(1)} %copy-done.3, bf16[1,1040,128]{2,1,0:T(8,128)(2,1)S(1)} %copy-done.6, bf16[1,1040,128]{2,1,0:T(8,128)(2,1)S(1)} %collective-permute-done.mate_in, bf16[1,1040,128]{2,1,0:T(8,128)(2,1)S(1)} %collective-permute-done.1.x_in, ...), custom_call_target="tpu_custom_call" | custom-call | flops 2013265920 | bytes 1835008 | tf_op jit(solution)/shard_map/attention_gradients/pallas_call | solution.py:304
  24.4 0.0 copy-start.7
  24.5 1.1 turn_weights.1.own_ref
  25.5 0.8 collective-permute-start.17
  26.3 0.0 collective-permute-done.4.x_in
  26.3 0.1 collective-permute-start.5
  26.4 0.2 dynamic-slice_bitcast_fusion.1
  26.6 1.6 %collective-permute-start.10 = (bf16[4,256,384]{2,1,0:T(8,128)(2,1)S(1)}, bf16[4,256,384]{2,1,0:T(8,128)(2,1)S(1)}, u32[]{:S(2)}, u32[]{:S(2)}) collective-permute-start(bf16[4,256,384]{2,1,0:T(8,128)(2,1)S(1)} %attention_gradients.2.refs_0_.refs_6_), channel_id=1, source_target_pairs={{0,20},{4,8},{8,28},{12,0},{16,4},{20,24},{24,12},{28,16},{1,21},{... | collective-permute-start | bytes 2359304 | tf_op jit(solution)/shard_map/ppermute | solution.py:128
  28.2 1.5 %collective-permute-start.8 = (bf16[4,256,384]{2,1,0:T(8,128)(2,1)S(1)}, bf16[4,256,384]{2,1,0:T(8,128)(2,1)S(1)}, u32[]{:S(2)}, u32[]{:S(2)}) collective-permute-start(bf16[4,256,384]{2,1,0:T(8,128)(2,1)S(1)} %attention_gradients.2.refs_0_.refs_6_), channel_id=1, source_target_pairs={{0,8},{4,20},{8,0},{12,28},{16,24},{20,4},{24,16},{28,12},{1,9},{5... | collective-permute-start | bytes 2359304 | tf_op jit(solution)/shard_map/ppermute | solution.py:128
  29.7 0.0 collective-permute-done.3.mate_in
  29.7 1.3 collective-permute-start.6
  31.1 0.0 collective-permute-done.5.far_in
  31.1 1.3 collective-permute-start.12
  32.4 4.3 %attention_gradients.3.refs_1_.refs_7_ = bf16[2,256,384]{2,1,0:T(8,128)(2,1)S(1)} custom-call(s32[4]{0:T(128)S(1)} %copy-done.4, bf16[1,1040,128]{2,1,0:T(8,128)(2,1)S(1)} %copy-done.5, bf16[1,1040,128]{2,1,0:T(8,128)(2,1)S(1)} %collective-permute-done.3.mate_in, bf16[1,1040,128]{2,1,0:T(8,128)(2,1)S(1)} %collective-permute-done.4.x_in, ...), custom_call_target="tpu_custom_call" | custom-call | flops 2013265920 | bytes 1835008 | tf_op jit(solution)/shard_map/attention_gradients/pallas_call | solution.py:304
  36.7 1.4 collective-permute-start.11
  38.2 0.1 pad_maximum_fusion.1
  38.3 7.3 %collective-permute-done.10.refs_6_.refs_12_ = bf16[4,256,384]{2,1,0:T(8,128)(2,1)S(1)} collective-permute-done((bf16[4,256,384]{2,1,0:T(8,128)(2,1)S(1)}, bf16[4,256,384]{2,1,0:T(8,128)(2,1)S(1)}, u32[]{:S(2)}, u32[]{:S(2)}) %collective-permute-start.10) | collective-permute-done | bytes 786464 | tf_op jit(solution)/shard_map/ppermute | solution.py:128
  45.6 1.7 %collective-permute-start.9 = (bf16[2,256,384]{2,1,0:T(8,128)(2,1)S(1)}, bf16[2,256,384]{2,1,0:T(8,128)(2,1)S(1)}, u32[]{:S(2)}, u32[]{:S(2)}) collective-permute-start(bf16[2,256,384]{2,1,0:T(8,128)(2,1)S(1)} %attention_gradients.3.refs_1_.refs_7_), channel_id=1, source_target_pairs={{0,8},{4,20},{8,0},{12,28},{16,24},{20,4},{24,16},{28,12},{1,9},{5... | collective-permute-start | bytes 1179656 | tf_op jit(solution)/shard_map/ppermute | solution.py:128
  47.3 1.4 collective-permute-done.8.refs_4_.refs_10_
  48.7 1.3 collective-permute-start.7
  50.0 0.0 collective-permute-done.6.refs_2_.refs_8_
  50.0 3.2 %collective-permute-start.15 = (bf16[4,256,384]{2,1,0:T(8,128)(2,1)S(1)}, bf16[4,256,384]{2,1,0:T(8,128)(2,1)S(1)}, u32[]{:S(2)}, u32[]{:S(2)}) collective-permute-start(bf16[4,256,384]{2,1,0:T(8,128)(2,1)S(1)} %collective-permute-done.8.refs_4_.refs_10_), channel_id=1, source_target_pairs={{0,20},{8,28},{16,4},{24,12},{1,21},{9,29},{17,5},{25,13},{2,22},{... | collective-permute-start | bytes 2359304 | tf_op jit(solution)/shard_map/ppermute | solution.py:128
  53.2 0.0 collective-permute-done.11.refs_7_.refs_13_
  53.2 0.7 collective-permute-start.13
  53.9 1.0 collective-permute-done.9.refs_5_.refs_11_
  55.0 0.0 collective-permute-done.7.refs_3_.refs_9_
  55.0 3.8 %collective-permute-start.16 = (bf16[2,256,384]{2,1,0:T(8,128)(2,1)S(1)}, bf16[2,256,384]{2,1,0:T(8,128)(2,1)S(1)}, u32[]{:S(2)}, u32[]{:S(2)}) collective-permute-start(bf16[2,256,384]{2,1,0:T(8,128)(2,1)S(1)} %collective-permute-done.9.refs_5_.refs_11_), channel_id=1, source_target_pairs={{0,20},{8,28},{16,4},{24,12},{1,21},{9,29},{17,5},{25,13},{2,22},{... | collective-permute-start | bytes 1179656 | tf_op jit(solution)/shard_map/ppermute | solution.py:128
  58.8 0.7 collective-permute-start.14
  59.5 0.9 join_weights.1.refs_12_
  60.3 6.9 %collective-permute-done.16.refs_11_.refs_17_ = bf16[2,256,384]{2,1,0:T(8,128)(2,1)S(1)} collective-permute-done((bf16[2,256,384]{2,1,0:T(8,128)(2,1)S(1)}, bf16[2,256,384]{2,1,0:T(8,128)(2,1)S(1)}, u32[]{:S(2)}, u32[]{:S(2)}) %collective-permute-start.16) | collective-permute-done | bytes 393248 | tf_op jit(solution)/shard_map/ppermute | solution.py:128
  67.3 4.7 %input_gradient.1 = (bf16[256,768]{1,0:T(8,128)(2,1)S(1)}, bf16[256,768]{1,0:T(8,128)(2,1)S(1)}, bf16[256,768]{1,0:T(8,128)(2,1)S(1)}, bf16[256,768]{1,0:T(8,128)(2,1)S(1)}) custom-call(s32[4]{0:T(128)S(1)} %copy-done.4, bf16[4,256,384]{2,1,0:T(8,128)(2,1)S(1)} %attention_gradients.2.refs_0_.refs_6_, ...), custom_call_target="tpu_custom_call" | custom-call | flops 3623878656 | bytes 9830400 | tf_op jit(solution)/shard_map/input_gradient/pallas_call | solution.py:408
  71.9 1.2 collective-permute-start.22
  73.1 3.4 %collective-permute-start.23 = (bf16[2,256,384]{2,1,0:T(8,128)(2,1)S(1)}, bf16[2,256,384]{2,1,0:T(8,128)(2,1)S(1)}, u32[]{:S(2)}, u32[]{:S(2)}) collective-permute-start(bf16[2,256,384]{2,1,0:T(8,128)(2,1)S(1)} %get-tuple-element.49), channel_id=1, source_target_pairs={{0,20},{4,8},{8,28},{12,0},{16,4},{20,24},{24,12},{28,16},{1,21},{... | collective-permute-start | bytes 1179656 | tf_op jit(solution)/shard_map/ppermute | solution.py:128
  76.5 1.6 %collective-permute-start.18 = (bf16[256,768]{1,0:T(8,128)(2,1)S(1)}, bf16[256,768]{1,0:T(8,128)(2,1)S(1)}, u32[]{:S(2)}, u32[]{:S(2)}) collective-permute-start(bf16[256,768]{1,0:T(8,128)(2,1)S(1)} %get-tuple-element.44), channel_id=1, source_target_pairs={{0,1},{1,0},{2,3},{3,2},{4,5},{5,4},{6,7},{7,6},{8,9},{9,8},{10,11... | collective-permute-start | bytes 1179656 | tf_op jit(solution)/shard_map/ppermute | solution.py:557
  78.1 0.3 collective-permute-start.19
  78.4 1.6 %collective-permute-start.20 = (bf16[256,768]{1,0:T(8,128)(2,1)S(1)}, bf16[256,768]{1,0:T(8,128)(2,1)S(1)}, u32[]{:S(2)}, u32[]{:S(2)}) collective-permute-start(bf16[256,768]{1,0:T(8,128)(2,1)S(1)} %get-tuple-element.46), channel_id=1, source_target_pairs={{0,3},{1,2},{2,1},{3,0},{4,7},{5,6},{6,5},{7,4},{8,11},{9,10},{10,... | collective-permute-start | bytes 1179656 | tf_op jit(solution)/shard_map/ppermute | solution.py:557
  80.0 1.7 %collective-permute-done.22.refs_2_ = bf16[2,256,384]{2,1,0:T(8,128)(2,1)S(1)} collective-permute-done((bf16[2,256,384]{2,1,0:T(8,128)(2,1)S(1)}, bf16[2,256,384]{2,1,0:T(8,128)(2,1)S(1)}, u32[]{:S(2)}, u32[]{:S(2)}) %collective-permute-start.22) | collective-permute-done | bytes 393248 | tf_op jit(solution)/shard_map/ppermute | solution.py:128
  81.7 3.5 %collective-permute-done.23.refs_3_ = bf16[2,256,384]{2,1,0:T(8,128)(2,1)S(1)} collective-permute-done((bf16[2,256,384]{2,1,0:T(8,128)(2,1)S(1)}, bf16[2,256,384]{2,1,0:T(8,128)(2,1)S(1)}, u32[]{:S(2)}, u32[]{:S(2)}) %collective-permute-start.23) | collective-permute-done | bytes 393248 | tf_op jit(solution)/shard_map/ppermute | solution.py:128
  85.2 4.1 %collective-permute-start.25 = (bf16[2,256,384]{2,1,0:T(8,128)(2,1)S(1)}, bf16[2,256,384]{2,1,0:T(8,128)(2,1)S(1)}, u32[]{:S(2)}, u32[]{:S(2)}) collective-permute-start(bf16[2,256,384]{2,1,0:T(8,128)(2,1)S(1)} %pad_maximum_fusion.3), channel_id=1, source_target_pairs={{0,28},{8,20},{16,12},{24,4},{1,29},{9,21},{17,13},{25,5},{2,30},{... | collective-permute-start | bytes 1179656 | tf_op jit(solution)/shard_map/ppermute | solution.py:128
  89.3 0.7 collective-permute-start.24
  90.0 3.6 %collective-permute-done.18 = bf16[256,768]{1,0:T(8,128)(2,1)S(1)} collective-permute-done((bf16[256,768]{1,0:T(8,128)(2,1)S(1)}, bf16[256,768]{1,0:T(8,128)(2,1)S(1)}, u32[]{:S(2)}, u32[]{:S(2)}) %collective-permute-start.18) | collective-permute-done | bytes 393248 | tf_op jit(solution)/shard_map/ppermute | solution.py:557
  93.6 11.2 %collective-permute-done.19 = bf16[256,768]{1,0:T(8,128)(2,1)S(1)} collective-permute-done((bf16[256,768]{1,0:T(8,128)(2,1)S(1)}, bf16[256,768]{1,0:T(8,128)(2,1)S(1)}, u32[]{:S(2)}, u32[]{:S(2)}) %collective-permute-start.19) | collective-permute-done | bytes 393248 | tf_op jit(solution)/shard_map/ppermute | solution.py:557
  104.8 9.1 %collective-permute-done.20 = bf16[256,768]{1,0:T(8,128)(2,1)S(1)} collective-permute-done((bf16[256,768]{1,0:T(8,128)(2,1)S(1)}, bf16[256,768]{1,0:T(8,128)(2,1)S(1)}, u32[]{:S(2)}, u32[]{:S(2)}) %collective-permute-start.20) | collective-permute-done | bytes 393248 | tf_op jit(solution)/shard_map/ppermute | solution.py:557
  113.9 0.2 add_convert_fusion
  114.1 2.9 %weight_gradient_mate.1 = f32[3,384,768]{2,1,0:T(8,128)S(1)} custom-call(s32[4]{0:T(128)S(1)} %copy-done.4, bf16[2,256,384]{2,1,0:T(8,128)(2,1)S(1)} %pad_maximum_fusion.refs_0_, bf16[2,256,384]{2,1,0:T(8,128)(2,1)S(1)} %collective-permute-done.12.refs_1_, bf16[2,256,384]{2,1,0:T(8,128)(2,1)S(1)} %collective-permute-done.22.refs_2_, ...), custom_call_target="tpu_custom_call" | custom-call | flops 1811939328 | bytes 9043968 | tf_op jit(solution)/shard_map/weight_gradient_mate/pallas_call | solution.py:458
  117.1 0.1 collective-permute-start.27
  117.2 2.5 %collective-permute-start.21 = (bf16[256,768]{1,0:T(8,128)(2,1)S(1)}, bf16[256,768]{1,0:T(8,128)(2,1)S(1)}, u32[]{:S(2)}, u32[]{:S(2)}) collective-permute-start(bf16[256,768]{1,0:T(8,128)(2,1)S(1)} %add_convert_fusion), channel_id=1, source_target_pairs={{0,0},{1,5},{2,10},{3,15},{4,20},{5,17},{6,30},{7,27},{8,8},{9,13}... | collective-permute-start | bytes 1179656 | tf_op jit(solution)/shard_map/ppermute | solution.py:583
  119.6 10.9 %collective-permute-done.21 = bf16[256,768]{1,0:T(8,128)(2,1)S(1)} collective-permute-done((bf16[256,768]{1,0:T(8,128)(2,1)S(1)}, bf16[256,768]{1,0:T(8,128)(2,1)S(1)}, u32[]{:S(2)}, u32[]{:S(2)}) %collective-permute-start.21) | collective-permute-done | bytes 393248 | tf_op jit(solution)/shard_map/ppermute | solution.py:583
  130.5 1.9 %collective-permute-start.26 = (bf16[256,768]{1,0:T(8,128)(2,1)S(1)}, bf16[256,768]{1,0:T(8,128)(2,1)S(1)}, u32[]{:S(2)}, u32[]{:S(2)}) collective-permute-start(bf16[256,768]{1,0:T(8,128)(2,1)S(1)} %collective-permute-done.21), channel_id=1, source_target_pairs={{0,0},{5,4},{10,8},{15,12},{20,20},{17,16},{30,28},{27,24},{8,9},{... | collective-permute-start | bytes 1179656 | tf_op jit(solution)/shard_map/ppermute | solution.py:589
  132.4 4.7 %weight_gradient_own.1 = (f32[384,768]{1,0:T(8,128)}, f32[384,768]{1,0:T(8,128)}, f32[384,768]{1,0:T(8,128)}) custom-call(s32[4]{0:T(128)S(1)} %copy-done.4, bf16[2,256,384]{2,1,0:T(8,128)(2,1)S(1)} %pad_maximum_fusion.refs_0_, bf16[2,256,384]{2,1,0:T(8,128)(2,1)S(1)} %collective-permute-done.12.refs_1_, ...), custom_call_target="tpu_custom_call" | custom-call | flops 1811939328 | bytes 9043968 | tf_op jit(solution)/shard_map/weight_gradient_own/pallas_call | solution.py:458
  137.1 7.2 %collective-permute-done.26 = bf16[256,768]{1,0:T(8,128)(2,1)S(1)} collective-permute-done((bf16[256,768]{1,0:T(8,128)(2,1)S(1)}, bf16[256,768]{1,0:T(8,128)(2,1)S(1)}, u32[]{:S(2)}, u32[]{:S(2)}) %collective-permute-start.26) | collective-permute-done | bytes 393248 | tf_op jit(solution)/shard_map/ppermute | solution.py:589
  144.4 0.7 copy.14
  (23 shorter events, 0.1 us)
Async XLA Ops:
  4.1 9.5 %collective-permute-start.1 = (bf16[1,1040,128]{2,1,0:T(8,128)(2,1)}, bf16[1,1040,128]{2,1,0:T(8,128)(2,1)S(1)}, u32[]{:S(2)}, u32[]{:S(2)}) collective-permute-start(bf16[1,1040,128]{2,1,0:T(8,128)(2,1)} %get-tuple-element.32), channel_id=1, source_target_pairs={{0,8},{4,12},{8,0},{12,4},{16,24},{20,28},{24,16},{28,20},{1,9},{5... | collective-permute-start | bytes 798728 | tf_op jit(solution)/shard_map/ppermute | solution.py:128
  5.6 9.5 %collective-permute-start = (bf16[1,1040,128]{2,1,0:T(8,128)(2,1)}, bf16[1,1040,128]{2,1,0:T(8,128)(2,1)S(1)}, u32[]{:S(2)}, u32[]{:S(2)}) collective-permute-start(bf16[1,1040,128]{2,1,0:T(8,128)(2,1)} %get-tuple-element.31), channel_id=1, source_target_pairs={{0,4},{4,0},{8,12},{12,8},{16,20},{20,16},{24,28},{28,24},{1,5},{5... | collective-permute-start | bytes 798728 | tf_op jit(solution)/shard_map/ppermute | solution.py:128
  5.6 12.8 %collective-permute-start.2 = (bf16[1,1040,128]{2,1,0:T(8,128)(2,1)}, bf16[1,1040,128]{2,1,0:T(8,128)(2,1)S(1)}, u32[]{:S(2)}, u32[]{:S(2)}) collective-permute-start(bf16[1,1040,128]{2,1,0:T(8,128)(2,1)} %get-tuple-element.33), channel_id=1, source_target_pairs={{0,12},{4,8},{8,4},{12,0},{16,28},{20,24},{24,20},{28,16},{1,13},{... | collective-permute-start | bytes 798728 | tf_op jit(solution)/shard_map/ppermute | solution.py:128
  13.6 12.8 %collective-permute-start.4 = (bf16[1,1040,128]{2,1,0:T(8,128)(2,1)}, bf16[1,1040,128]{2,1,0:T(8,128)(2,1)S(1)}, u32[]{:S(2)}, u32[]{:S(2)}) collective-permute-start(bf16[1,1040,128]{2,1,0:T(8,128)(2,1)} %get-tuple-element.40), channel_id=1, source_target_pairs={{0,8},{4,12},{8,0},{12,4},{16,24},{20,28},{24,16},{28,20},{1,9},{5... | collective-permute-start | bytes 798728 | tf_op jit(solution)/shard_map/ppermute | solution.py:128
  15.0 14.7 %collective-permute-start.3 = (bf16[1,1040,128]{2,1,0:T(8,128)(2,1)}, bf16[1,1040,128]{2,1,0:T(8,128)(2,1)S(1)}, u32[]{:S(2)}, u32[]{:S(2)}) collective-permute-start(bf16[1,1040,128]{2,1,0:T(8,128)(2,1)} %get-tuple-element.38.own), channel_id=1, source_target_pairs={{0,4},{4,0},{8,12},{12,8},{16,20},{20,16},{24,28},{28,24},{1,5},{5... | collective-permute-start | bytes 798728 | tf_op jit(solution)/shard_map/ppermute | solution.py:128
  18.4 0.6 copy-start.3
  19.0 1.0 copy-start.6
  20.0 4.5 %copy-start = (bf16[384,768]{1,0:T(8,128)(2,1)S(1)}, bf16[384,768]{1,0:T(8,128)(2,1)}, u32[]{:S(2)}) copy-start(bf16[384,768]{1,0:T(8,128)(2,1)} %q_ref) | copy-start | bytes 1769476
  20.0 4.5 %copy-start.1 = (bf16[384,768]{1,0:T(8,128)(2,1)S(1)}, bf16[384,768]{1,0:T(8,128)(2,1)}, u32[]{:S(2)}) copy-start(bf16[384,768]{1,0:T(8,128)(2,1)} %k_ref) | copy-start | bytes 1769476
  20.0 4.5 %copy-start.2 = (bf16[384,768]{1,0:T(8,128)(2,1)S(1)}, bf16[384,768]{1,0:T(8,128)(2,1)}, u32[]{:S(2)}) copy-start(bf16[384,768]{1,0:T(8,128)(2,1)} %v_ref) | copy-start | bytes 1769476
  24.4 2.0 %copy-start.7 = (bf16[1,1,256,3072]{3,2,1,0:T(8,128)(2,1)S(1)}, bf16[1,1,256,3072]{3,2,1,0:T(8,128)(2,1)}, u32[]{:S(2)}) copy-start(bf16[1,1,256,3072]{3,2,1,0:T(8,128)(2,1)} %param.9) | copy-start | bytes 4718596
  25.5 6.9 %copy-start.4 = (s32[4]{0:T(128)S(1)}, s32[4]{0:T(128)}, u32[]{:S(2)}) copy-start(s32[4]{0:T(128)} %pad_add_fusion.place_ref) | copy-start | bytes 52
  25.5 6.9 %copy-start.5 = (bf16[1,1040,128]{2,1,0:T(8,128)(2,1)S(1)}, bf16[1,1040,128]{2,1,0:T(8,128)(2,1)}, u32[]{:S(2)}) copy-start(bf16[1,1040,128]{2,1,0:T(8,128)(2,1)} %get-tuple-element.38.own) | copy-start | bytes 798724
  25.5 33.9 %collective-permute-start.17 = (bf16[2304,384]{1,0:T(8,128)(2,1)S(1)}, bf16[2304,384]{1,0:T(8,128)(2,1)S(1)}, u32[]{:S(2)}, u32[]{:S(2)}) collective-permute-start(bf16[2304,384]{1,0:T(8,128)(2,1)S(1)} %turn_weights.1.own_ref), channel_id=1, source_target_pairs={{0,4},{4,0},{8,12},{12,8},{16,20},{20,16},{24,28},{28,24},{1,5},{5... | collective-permute-start | bytes 5308424 | tf_op jit(solution)/shard_map/ppermute | solution.py:128
  26.3 4.8 %collective-permute-start.5 = (bf16[1,1040,128]{2,1,0:T(8,128)(2,1)S(1)}, bf16[1,1040,128]{2,1,0:T(8,128)(2,1)S(1)}, u32[]{:S(2)}, u32[]{:S(2)}) collective-permute-start(bf16[1,1040,128]{2,1,0:T(8,128)(2,1)S(1)} %collective-permute-done.4.x_in), channel_id=1, source_target_pairs={{0,4},{4,0},{8,12},{12,8},{16,20},{20,16},{24,28},{28,24},{1,5},{5... | collective-permute-start | bytes 798728 | tf_op jit(solution)/shard_map/ppermute | solution.py:128
  26.6 19.0 %collective-permute-start.10 = (bf16[4,256,384]{2,1,0:T(8,128)(2,1)S(1)}, bf16[4,256,384]{2,1,0:T(8,128)(2,1)S(1)}, u32[]{:S(2)}, u32[]{:S(2)}) collective-permute-start(bf16[4,256,384]{2,1,0:T(8,128)(2,1)S(1)} %attention_gradients.2.refs_0_.refs_6_), channel_id=1, source_target_pairs={{0,20},{4,8},{8,28},{12,0},{16,4},{20,24},{24,12},{28,16},{1,21},{... | collective-permute-start | bytes 2359304 | tf_op jit(solution)/shard_map/ppermute | solution.py:128
  28.2 20.5 %collective-permute-start.8 = (bf16[4,256,384]{2,1,0:T(8,128)(2,1)S(1)}, bf16[4,256,384]{2,1,0:T(8,128)(2,1)S(1)}, u32[]{:S(2)}, u32[]{:S(2)}) collective-permute-start(bf16[4,256,384]{2,1,0:T(8,128)(2,1)S(1)} %attention_gradients.2.refs_0_.refs_6_), channel_id=1, source_target_pairs={{0,8},{4,20},{8,0},{12,28},{16,24},{20,4},{24,16},{28,12},{1,9},{5... | collective-permute-start | bytes 2359304 | tf_op jit(solution)/shard_map/ppermute | solution.py:128
  29.7 20.3 %collective-permute-start.6 = (bf16[4,256,384]{2,1,0:T(8,128)(2,1)S(1)}, bf16[4,256,384]{2,1,0:T(8,128)(2,1)S(1)}, u32[]{:S(2)}, u32[]{:S(2)}) collective-permute-start(bf16[4,256,384]{2,1,0:T(8,128)(2,1)S(1)} %attention_gradients.2.refs_0_.refs_6_), channel_id=1, source_target_pairs={{4,0},{12,8},{20,16},{28,24},{5,1},{13,9},{21,17},{29,25},{6,2},{1... | collective-permute-start | bytes 2359304 | tf_op jit(solution)/shard_map/ppermute | solution.py:128
  31.1 5.6 %collective-permute-start.12 = (bf16[2,256,384]{2,1,0:T(8,128)(2,1)S(1)}, bf16[2,256,384]{2,1,0:T(8,128)(2,1)S(1)}, u32[]{:S(2)}, u32[]{:S(2)}) collective-permute-start(bf16[2,256,384]{2,1,0:T(8,128)(2,1)S(1)} %pad_maximum_fusion.refs_0_), channel_id=1, source_target_pairs={{4,0},{12,8},{20,16},{28,24},{5,1},{13,9},{21,17},{29,25},{6,2},{1... | collective-permute-start | bytes 1179656 | tf_op jit(solution)/shard_map/ppermute | solution.py:128
  36.7 16.4 %collective-permute-start.11 = (bf16[2,256,384]{2,1,0:T(8,128)(2,1)S(1)}, bf16[2,256,384]{2,1,0:T(8,128)(2,1)S(1)}, u32[]{:S(2)}, u32[]{:S(2)}) collective-permute-start(bf16[2,256,384]{2,1,0:T(8,128)(2,1)S(1)} %attention_gradients.3.refs_1_.refs_7_), channel_id=1, source_target_pairs={{0,20},{4,8},{8,28},{12,0},{16,4},{20,24},{24,12},{28,16},{1,21},{... | collective-permute-start | bytes 1179656 | tf_op jit(solution)/shard_map/ppermute | solution.py:128
  45.6 9.4 %collective-permute-start.9 = (bf16[2,256,384]{2,1,0:T(8,128)(2,1)S(1)}, bf16[2,256,384]{2,1,0:T(8,128)(2,1)S(1)}, u32[]{:S(2)}, u32[]{:S(2)}) collective-permute-start(bf16[2,256,384]{2,1,0:T(8,128)(2,1)S(1)} %attention_gradients.3.refs_1_.refs_7_), channel_id=1, source_target_pairs={{0,8},{4,20},{8,0},{12,28},{16,24},{20,4},{24,16},{28,12},{1,9},{5... | collective-permute-start | bytes 1179656 | tf_op jit(solution)/shard_map/ppermute | solution.py:128
  48.7 6.2 %collective-permute-start.7 = (bf16[2,256,384]{2,1,0:T(8,128)(2,1)S(1)}, bf16[2,256,384]{2,1,0:T(8,128)(2,1)S(1)}, u32[]{:S(2)}, u32[]{:S(2)}) collective-permute-start(bf16[2,256,384]{2,1,0:T(8,128)(2,1)S(1)} %attention_gradients.3.refs_1_.refs_7_), channel_id=1, source_target_pairs={{4,0},{12,8},{20,16},{28,24},{5,1},{13,9},{21,17},{29,25},{6,2},{1... | collective-permute-start | bytes 1179656 | tf_op jit(solution)/shard_map/ppermute | solution.py:128
  50.0 17.2 %collective-permute-start.15 = (bf16[4,256,384]{2,1,0:T(8,128)(2,1)S(1)}, bf16[4,256,384]{2,1,0:T(8,128)(2,1)S(1)}, u32[]{:S(2)}, u32[]{:S(2)}) collective-permute-start(bf16[4,256,384]{2,1,0:T(8,128)(2,1)S(1)} %collective-permute-done.8.refs_4_.refs_10_), channel_id=1, source_target_pairs={{0,20},{8,28},{16,4},{24,12},{1,21},{9,29},{17,5},{25,13},{2,22},{... | collective-permute-start | bytes 2359304 | tf_op jit(solution)/shard_map/ppermute | solution.py:128
  53.2 14.1 %collective-permute-start.13 = (bf16[4,256,384]{2,1,0:T(8,128)(2,1)S(1)}, bf16[4,256,384]{2,1,0:T(8,128)(2,1)S(1)}, u32[]{:S(2)}, u32[]{:S(2)}) collective-permute-start(bf16[4,256,384]{2,1,0:T(8,128)(2,1)S(1)} %collective-permute-done.8.refs_4_.refs_10_), channel_id=1, source_target_pairs={{4,12},{12,4},{20,28},{28,20},{5,13},{13,5},{21,29},{29,21},{6,14}... | collective-permute-start | bytes 2359304 | tf_op jit(solution)/shard_map/ppermute | solution.py:128
  55.0 12.3 %collective-permute-start.16 = (bf16[2,256,384]{2,1,0:T(8,128)(2,1)S(1)}, bf16[2,256,384]{2,1,0:T(8,128)(2,1)S(1)}, u32[]{:S(2)}, u32[]{:S(2)}) collective-permute-start(bf16[2,256,384]{2,1,0:T(8,128)(2,1)S(1)} %collective-permute-done.9.refs_5_.refs_11_), channel_id=1, source_target_pairs={{0,20},{8,28},{16,4},{24,12},{1,21},{9,29},{17,5},{25,13},{2,22},{... | collective-permute-start | bytes 1179656 | tf_op jit(solution)/shard_map/ppermute | solution.py:128
  58.8 8.5 %collective-permute-start.14 = (bf16[2,256,384]{2,1,0:T(8,128)(2,1)S(1)}, bf16[2,256,384]{2,1,0:T(8,128)(2,1)S(1)}, u32[]{:S(2)}, u32[]{:S(2)}) collective-permute-start(bf16[2,256,384]{2,1,0:T(8,128)(2,1)S(1)} %collective-permute-done.9.refs_5_.refs_11_), channel_id=1, source_target_pairs={{4,12},{12,4},{20,28},{28,20},{5,13},{13,5},{21,29},{29,21},{6,14}... | collective-permute-start | bytes 1179656 | tf_op jit(solution)/shard_map/ppermute | solution.py:128
  71.9 9.7 %collective-permute-start.22 = (bf16[2,256,384]{2,1,0:T(8,128)(2,1)S(1)}, bf16[2,256,384]{2,1,0:T(8,128)(2,1)S(1)}, u32[]{:S(2)}, u32[]{:S(2)}) collective-permute-start(bf16[2,256,384]{2,1,0:T(8,128)(2,1)S(1)} %get-tuple-element.48), channel_id=1, source_target_pairs={{0,8},{4,20},{8,0},{12,28},{16,24},{20,4},{24,16},{28,12},{1,9},{5... | collective-permute-start | bytes 1179656 | tf_op jit(solution)/shard_map/ppermute | solution.py:128
  73.1 12.1 %collective-permute-start.23 = (bf16[2,256,384]{2,1,0:T(8,128)(2,1)S(1)}, bf16[2,256,384]{2,1,0:T(8,128)(2,1)S(1)}, u32[]{:S(2)}, u32[]{:S(2)}) collective-permute-start(bf16[2,256,384]{2,1,0:T(8,128)(2,1)S(1)} %get-tuple-element.49), channel_id=1, source_target_pairs={{0,20},{4,8},{8,28},{12,0},{16,4},{20,24},{24,12},{28,16},{1,21},{... | collective-permute-start | bytes 1179656 | tf_op jit(solution)/shard_map/ppermute | solution.py:128
  76.5 17.1 %collective-permute-start.18 = (bf16[256,768]{1,0:T(8,128)(2,1)S(1)}, bf16[256,768]{1,0:T(8,128)(2,1)S(1)}, u32[]{:S(2)}, u32[]{:S(2)}) collective-permute-start(bf16[256,768]{1,0:T(8,128)(2,1)S(1)} %get-tuple-element.44), channel_id=1, source_target_pairs={{0,1},{1,0},{2,3},{3,2},{4,5},{5,4},{6,7},{7,6},{8,9},{9,8},{10,11... | collective-permute-start | bytes 1179656 | tf_op jit(solution)/shard_map/ppermute | solution.py:557
  78.1 26.7 %collective-permute-start.19 = (bf16[256,768]{1,0:T(8,128)(2,1)S(1)}, bf16[256,768]{1,0:T(8,128)(2,1)S(1)}, u32[]{:S(2)}, u32[]{:S(2)}) collective-permute-start(bf16[256,768]{1,0:T(8,128)(2,1)S(1)} %get-tuple-element.45), channel_id=1, source_target_pairs={{0,2},{1,3},{2,0},{3,1},{4,6},{5,7},{6,4},{7,5},{8,10},{9,11},{10,... | collective-permute-start | bytes 1179656 | tf_op jit(solution)/shard_map/ppermute | solution.py:557
  78.4 35.5 %collective-permute-start.20 = (bf16[256,768]{1,0:T(8,128)(2,1)S(1)}, bf16[256,768]{1,0:T(8,128)(2,1)S(1)}, u32[]{:S(2)}, u32[]{:S(2)}) collective-permute-start(bf16[256,768]{1,0:T(8,128)(2,1)S(1)} %get-tuple-element.46), channel_id=1, source_target_pairs={{0,3},{1,2},{2,1},{3,0},{4,7},{5,6},{6,5},{7,4},{8,11},{9,10},{10,... | collective-permute-start | bytes 1179656 | tf_op jit(solution)/shard_map/ppermute | solution.py:557
  85.2 28.9 %collective-permute-start.25 = (bf16[2,256,384]{2,1,0:T(8,128)(2,1)S(1)}, bf16[2,256,384]{2,1,0:T(8,128)(2,1)S(1)}, u32[]{:S(2)}, u32[]{:S(2)}) collective-permute-start(bf16[2,256,384]{2,1,0:T(8,128)(2,1)S(1)} %pad_maximum_fusion.3), channel_id=1, source_target_pairs={{0,28},{8,20},{16,12},{24,4},{1,29},{9,21},{17,13},{25,5},{2,30},{... | collective-permute-start | bytes 1179656 | tf_op jit(solution)/shard_map/ppermute | solution.py:128
  89.3 24.8 %collective-permute-start.24 = (bf16[2,256,384]{2,1,0:T(8,128)(2,1)S(1)}, bf16[2,256,384]{2,1,0:T(8,128)(2,1)S(1)}, u32[]{:S(2)}, u32[]{:S(2)}) collective-permute-start(bf16[2,256,384]{2,1,0:T(8,128)(2,1)S(1)} %pad_maximum_fusion.3), channel_id=1, source_target_pairs={{4,28},{12,20},{20,12},{28,4},{5,29},{13,21},{21,13},{29,5},{6,30}... | collective-permute-start | bytes 1179656 | tf_op jit(solution)/shard_map/ppermute | solution.py:128
  117.1 15.3 %collective-permute-start.27 = (f32[3,384,768]{2,1,0:T(8,128)S(1)}, f32[3,384,768]{2,1,0:T(8,128)S(1)}, u32[]{:S(2)}, u32[]{:S(2)}) collective-permute-start(f32[3,384,768]{2,1,0:T(8,128)S(1)} %weight_gradient_mate.1), channel_id=1, source_target_pairs={{0,4},{4,0},{8,12},{12,8},{16,20},{20,16},{24,28},{28,24},{1,5},{5... | collective-permute-start | bytes 10616840 | tf_op jit(solution)/shard_map/ppermute | solution.py:128
  117.2 13.3 %collective-permute-start.21 = (bf16[256,768]{1,0:T(8,128)(2,1)S(1)}, bf16[256,768]{1,0:T(8,128)(2,1)S(1)}, u32[]{:S(2)}, u32[]{:S(2)}) collective-permute-start(bf16[256,768]{1,0:T(8,128)(2,1)S(1)} %add_convert_fusion), channel_id=1, source_target_pairs={{0,0},{1,5},{2,10},{3,15},{4,20},{5,17},{6,30},{7,27},{8,8},{9,13}... | collective-permute-start | bytes 1179656 | tf_op jit(solution)/shard_map/ppermute | solution.py:583
  130.5 13.9 %collective-permute-start.26 = (bf16[256,768]{1,0:T(8,128)(2,1)S(1)}, bf16[256,768]{1,0:T(8,128)(2,1)S(1)}, u32[]{:S(2)}, u32[]{:S(2)}) collective-permute-start(bf16[256,768]{1,0:T(8,128)(2,1)S(1)} %collective-permute-done.21), channel_id=1, source_target_pairs={{0,0},{5,4},{10,8},{15,12},{20,20},{17,16},{30,28},{27,24},{8,9},{... | collective-permute-start | bytes 1179656 | tf_op jit(solution)/shard_map/ppermute | solution.py:589

commit v11 on v10

--- a/solution.py
+++ b/solution.py
@@ -447,14 +447,14 @@
                         value = total[:, at : at + HD]
                         if mine:
                             value = (value + received[kind, :, here]) * mean_scale
-                        out[:, here] = value
+                        out[:, here] = value.astype(out.dtype)
 
 
 def weight_product(place, mine, mean_scale, cols, tokens, grads, received=()):
     _, length, _ = grads[0].shape
     rows = tokens[0].shape[2]
     out = jax.ShapeDtypeStruct((rows, cols), jnp.float32)
-    both = jax.ShapeDtypeStruct((3, rows, cols), jnp.float32)
+    both = jax.ShapeDtypeStruct((3, rows, cols), jnp.bfloat16)
     return pl.pallas_call(
         functools.partial(weight_kernel, mine, mean_scale, len(grads) // 6),
         out_shape=[out] * 3 if mine else both,
@@ -572,10 +572,8 @@
         moved(to_corner, corner_same),
         moved(to_corner, corner_cross),
     )
-    (turn,) = after((place,), total)
-    for_mate = weight_product(turn, False, mean_scale, cols, tokens, grads)
-    from_mate = moved(for_mate, mate)
-    weight_grads = weight_product(place, True, mean_scale, cols, tokens, grads, (from_mate,))
+    (total,) = after((total,), tokens[4], tokens[5])
+
     def spot(y, v, z):
         return (y * views + v) * groups + z
 
@@ -585,6 +583,10 @@
         ("dp", "view", "head"),
         [(spot(y, v, z), spot(y ^ (v % 2), v ^ z, z)) for y, v, z in corners],
     )
+    (turn,) = after((place,), beside)
+    for_mate = weight_product(turn, False, mean_scale, cols, tokens, grads)
+    from_mate = moved(for_mate, mate)
+    weight_grads = weight_product(place, True, mean_scale, cols, tokens, grads, (from_mate,))
     (beside,) = after((beside,), for_mate)
     input_grad = lax.ppermute(
         beside,

time: 146 us -> 143 us (0.979)
  waiting for transfers between devices: 74.6 us -> 71.8 us
    ppermute x1, waiting for transfers between devices: 10.9 us -> 8.1 us  [gather_body(): lax.ppermute(total, ('dp', 'view', 'head'), [(spot(y, v, z), spot(y ^ v %...]
  transfers between devices with their start and end apart: 28 -> 28, of which waited for: 13 -> 14; matrix products, arithmetic and copies ran while one was open for 0% -> 0% of each run, Pallas kernels for 11% -> 11%
where the time goes in v11:
time: 143 us
  waiting for transfers between devices  71.8 us (50%)
  starting transfers between devices  40.7 us (28%)
  Pallas kernels  25.8 us (18%)
  local copies, waits for them, and re-layouts  2.58 us (2%)
    ppermute x23, waiting for transfers between devices, moved(): return lax.ppermute(value, ('dp', 'view'), pairs)  34 us
    ppermute x23, starting transfers between devices, moved(): return lax.ppermute(value, ('dp', 'view'), pairs)  32.8 us
    ppermute x3, waiting for transfers between devices, gather_body(): lax.ppermute(slots[s], 'head', [(z, z ^ s) for z in range(groups)])  23.9 us
    pallas_call x2, Pallas kernels, attention(): pl.pallas_call(functools.partial(attention_kernel, HD ** (-0.5), kept), o...  8.76 us
    ppermute x1, waiting for transfers between devices, gather_body(): lax.ppermute(total, ('dp', 'view', 'head'), [(spot(y, v, z), spot(y ^ v %...  8.1 us
    pallas_call x2, Pallas kernels, weight_product(): pl.pallas_call(functools.partial(weight_kernel, mine, mean_scale, len(gra...  7.63 us
    ppermute x1, waiting for transfers between devices, gather_body(): lax.ppermute(beside, ('dp', 'view', 'head'), [(spot(y ^ v % 2, v ^ z, z),...  5.82 us
    pallas_call x1, Pallas kernels, input_product(): pl.pallas_call(functools.partial(input_kernel, len(grads) // 6), out_shap...  4.66 us
  transfers between devices with their start and end apart: 28, of which 14 were waited for; matrix products, arithmetic and copies ran while one was open for 0% of the time, Pallas kernels for 11%

profile of v11, /device:TPU:16, one launch (start us, length us, event | category | flops | bytes accessed | tf_op | source)
XLA Modules:
  0.0 142.8 jit_solution(10379512985249749602)
XLA Ops:
  0.7 0.6 pad_add_fusion.place_ref
  1.3 2.8 %pack_heads.1 = (bf16[1,1040,128]{2,1,0:T(8,128)(2,1)}, bf16[1,1040,128]{2,1,0:T(8,128)(2,1)}, bf16[1,1040,128]{2,1,0:T(8,128)(2,1)}, bf16[1,1040,128]{2,1,0:T(8...) custom-call(s32[4]{0:T(128)} %pad_add_fusion.place_ref, s32[1,2]{1,0:T(1,128)} %links_ref.1, ...), custom_call_target="tpu_custom_call" | custom-call | tf_op jit(solution)/shard_map/pack_heads/pallas_call | solution.py:215
  4.1 1.5 %collective-permute-start.1 = (bf16[1,1040,128]{2,1,0:T(8,128)(2,1)}, bf16[1,1040,128]{2,1,0:T(8,128)(2,1)S(1)}, u32[]{:S(2)}, u32[]{:S(2)}) collective-permute-start(bf16[1,1040,128]{2,1,0:T(8,128)(2,1)} %get-tuple-element.33), channel_id=1, source_target_pairs={{0,8},{4,12},{8,0},{12,4},{16,24},{20,28},{24,16},{28,20},{1,9},{5... | collective-permute-start | bytes 798728 | tf_op jit(solution)/shard_map/ppermute | solution.py:128
  5.6 0.6 collective-permute-start.2
  6.2 7.3 %collective-permute-done.1.x_in = bf16[1,1040,128]{2,1,0:T(8,128)(2,1)S(1)} collective-permute-done((bf16[1,1040,128]{2,1,0:T(8,128)(2,1)}, bf16[1,1040,128]{2,1,0:T(8,128)(2,1)S(1)}, u32[]{:S(2)}, u32[]{:S(2)}) %collective-permute-start.1) | collective-permute-done | bytes 266272 | tf_op jit(solution)/shard_map/ppermute | solution.py:128
  13.6 1.5 %collective-permute-start.4 = (bf16[1,1040,128]{2,1,0:T(8,128)(2,1)}, bf16[1,1040,128]{2,1,0:T(8,128)(2,1)S(1)}, u32[]{:S(2)}, u32[]{:S(2)}) collective-permute-start(bf16[1,1040,128]{2,1,0:T(8,128)(2,1)} %get-tuple-element.41), channel_id=1, source_target_pairs={{0,8},{4,12},{8,0},{12,4},{16,24},{20,28},{24,16},{28,20},{1,9},{5... | collective-permute-start | bytes 798728 | tf_op jit(solution)/shard_map/ppermute | solution.py:128
  15.0 0.0 collective-permute-start.3
  15.0 0.0 collective-permute-done.mate_in
  15.1 3.3 %collective-permute-done.2.far_in = bf16[1,1040,128]{2,1,0:T(8,128)(2,1)S(1)} collective-permute-done((bf16[1,1040,128]{2,1,0:T(8,128)(2,1)}, bf16[1,1040,128]{2,1,0:T(8,128)(2,1)S(1)}, u32[]{:S(2)}, u32[]{:S(2)}) %collective-permute-start.2) | collective-permute-done | bytes 266272 | tf_op jit(solution)/shard_map/ppermute | solution.py:128
  18.4 0.6 copy-done.3
  19.0 0.9 copy-done.6
  20.0 4.4 %attention_gradients.2.refs_0_.refs_6_ = bf16[4,256,384]{2,1,0:T(8,128)(2,1)S(1)} custom-call(s32[4]{0:T(128)S(1)} %copy-done.3, bf16[1,1040,128]{2,1,0:T(8,128)(2,1)S(1)} %copy-done.6, bf16[1,1040,128]{2,1,0:T(8,128)(2,1)S(1)} %collective-permute-done.mate_in, bf16[1,1040,128]{2,1,0:T(8,128)(2,1)S(1)} %collective-permute-done.1.x_in, ...), custom_call_target="tpu_custom_call" | custom-call | flops 2013265920 | bytes 1835008 | tf_op jit(solution)/shard_map/attention_gradients/pallas_call | solution.py:304
  24.4 0.0 copy-start.7
  24.5 1.1 turn_weights.1.own_ref
  25.5 0.8 collective-permute-start.17
  26.3 0.0 collective-permute-done.4.x_in
  26.3 0.1 collective-permute-start.5
  26.4 0.2 dynamic-slice_bitcast_fusion.1
  26.6 1.6 %collective-permute-start.10 = (bf16[4,256,384]{2,1,0:T(8,128)(2,1)S(1)}, bf16[4,256,384]{2,1,0:T(8,128)(2,1)S(1)}, u32[]{:S(2)}, u32[]{:S(2)}) collective-permute-start(bf16[4,256,384]{2,1,0:T(8,128)(2,1)S(1)} %attention_gradients.2.refs_0_.refs_6_), channel_id=1, source_target_pairs={{0,20},{4,8},{8,28},{12,0},{16,4},{20,24},{24,12},{28,16},{1,21},{... | collective-permute-start | bytes 2359304 | tf_op jit(solution)/shard_map/ppermute | solution.py:128
  28.2 1.5 %collective-permute-start.8 = (bf16[4,256,384]{2,1,0:T(8,128)(2,1)S(1)}, bf16[4,256,384]{2,1,0:T(8,128)(2,1)S(1)}, u32[]{:S(2)}, u32[]{:S(2)}) collective-permute-start(bf16[4,256,384]{2,1,0:T(8,128)(2,1)S(1)} %attention_gradients.2.refs_0_.refs_6_), channel_id=1, source_target_pairs={{0,8},{4,20},{8,0},{12,28},{16,24},{20,4},{24,16},{28,12},{1,9},{5... | collective-permute-start | bytes 2359304 | tf_op jit(solution)/shard_map/ppermute | solution.py:128
  29.7 0.0 collective-permute-done.3.mate_in
  29.7 1.3 collective-permute-start.6
  31.1 0.0 collective-permute-done.5.far_in
  31.1 1.3 collective-permute-start.12
  32.4 4.3 %attention_gradients.3.refs_1_.refs_7_ = bf16[2,256,384]{2,1,0:T(8,128)(2,1)S(1)} custom-call(s32[4]{0:T(128)S(1)} %copy-done.4, bf16[1,1040,128]{2,1,0:T(8,128)(2,1)S(1)} %copy-done.5, bf16[1,1040,128]{2,1,0:T(8,128)(2,1)S(1)} %collective-permute-done.3.mate_in, bf16[1,1040,128]{2,1,0:T(8,128)(2,1)S(1)} %collective-permute-done.4.x_in, ...), custom_call_target="tpu_custom_call" | custom-call | flops 2013265920 | bytes 1835008 | tf_op jit(solution)/shard_map/attention_gradients/pallas_call | solution.py:304
  36.7 0.0 collective-permute-done.12.refs_1_
  36.7 1.4 collective-permute-start.11
  38.2 0.1 pad_maximum_fusion.1
  38.3 7.3 %collective-permute-done.10.refs_6_.refs_12_ = bf16[4,256,384]{2,1,0:T(8,128)(2,1)S(1)} collective-permute-done((bf16[4,256,384]{2,1,0:T(8,128)(2,1)S(1)}, bf16[4,256,384]{2,1,0:T(8,128)(2,1)S(1)}, u32[]{:S(2)}, u32[]{:S(2)}) %collective-permute-start.10) | collective-permute-done | bytes 786464 | tf_op jit(solution)/shard_map/ppermute | solution.py:128
  45.6 1.7 %collective-permute-start.9 = (bf16[2,256,384]{2,1,0:T(8,128)(2,1)S(1)}, bf16[2,256,384]{2,1,0:T(8,128)(2,1)S(1)}, u32[]{:S(2)}, u32[]{:S(2)}) collective-permute-start(bf16[2,256,384]{2,1,0:T(8,128)(2,1)S(1)} %attention_gradients.3.refs_1_.refs_7_), channel_id=1, source_target_pairs={{0,8},{4,20},{8,0},{12,28},{16,24},{20,4},{24,16},{28,12},{1,9},{5... | collective-permute-start | bytes 1179656 | tf_op jit(solution)/shard_map/ppermute | solution.py:128
  47.3 1.4 collective-permute-done.8.refs_4_.refs_10_
  48.7 1.3 collective-permute-start.7
  50.0 3.2 %collective-permute-start.15 = (bf16[4,256,384]{2,1,0:T(8,128)(2,1)S(1)}, bf16[4,256,384]{2,1,0:T(8,128)(2,1)S(1)}, u32[]{:S(2)}, u32[]{:S(2)}) collective-permute-start(bf16[4,256,384]{2,1,0:T(8,128)(2,1)S(1)} %collective-permute-done.8.refs_4_.refs_10_), channel_id=1, source_target_pairs={{0,20},{8,28},{16,4},{24,12},{1,21},{9,29},{17,5},{25,13},{2,22},{... | collective-permute-start | bytes 2359304 | tf_op jit(solution)/shard_map/ppermute | solution.py:128
  53.2 0.0 collective-permute-done.11.refs_7_.refs_13_
  53.2 0.7 collective-permute-start.13
  53.9 1.0 collective-permute-done.9.refs_5_.refs_11_
  55.0 0.0 collective-permute-done.7.refs_3_.refs_9_
  55.0 3.8 %collective-permute-start.16 = (bf16[2,256,384]{2,1,0:T(8,128)(2,1)S(1)}, bf16[2,256,384]{2,1,0:T(8,128)(2,1)S(1)}, u32[]{:S(2)}, u32[]{:S(2)}) collective-permute-start(bf16[2,256,384]{2,1,0:T(8,128)(2,1)S(1)} %collective-permute-done.9.refs_5_.refs_11_), channel_id=1, source_target_pairs={{0,20},{8,28},{16,4},{24,12},{1,21},{9,29},{17,5},{25,13},{2,22},{... | collective-permute-start | bytes 1179656 | tf_op jit(solution)/shard_map/ppermute | solution.py:128
  58.8 0.7 collective-permute-start.14
  59.5 0.9 join_weights.1.refs_12_
  60.3 6.9 %collective-permute-done.16.refs_11_.refs_17_ = bf16[2,256,384]{2,1,0:T(8,128)(2,1)S(1)} collective-permute-done((bf16[2,256,384]{2,1,0:T(8,128)(2,1)S(1)}, bf16[2,256,384]{2,1,0:T(8,128)(2,1)S(1)}, u32[]{:S(2)}, u32[]{:S(2)}) %collective-permute-start.16) | collective-permute-done | bytes 393248 | tf_op jit(solution)/shard_map/ppermute | solution.py:128
  67.3 4.7 %input_gradient.1 = (bf16[256,768]{1,0:T(8,128)(2,1)S(1)}, bf16[256,768]{1,0:T(8,128)(2,1)S(1)}, bf16[256,768]{1,0:T(8,128)(2,1)S(1)}, bf16[256,768]{1,0:T(8,128)(2,1)S(1)}) custom-call(s32[4]{0:T(128)S(1)} %copy-done.4, bf16[4,256,384]{2,1,0:T(8,128)(2,1)S(1)} %attention_gradients.2.refs_0_.refs_6_, ...), custom_call_target="tpu_custom_call" | custom-call | flops 3623878656 | bytes 9830400 | tf_op jit(solution)/shard_map/input_gradient/pallas_call | solution.py:408
  71.9 1.2 collective-permute-start.21
  73.1 3.4 %collective-permute-start.22 = (bf16[2,256,384]{2,1,0:T(8,128)(2,1)S(1)}, bf16[2,256,384]{2,1,0:T(8,128)(2,1)S(1)}, u32[]{:S(2)}, u32[]{:S(2)}) collective-permute-start(bf16[2,256,384]{2,1,0:T(8,128)(2,1)S(1)} %get-tuple-element.49), channel_id=1, source_target_pairs={{0,20},{4,8},{8,28},{12,0},{16,4},{20,24},{24,12},{28,16},{1,21},{... | collective-permute-start | bytes 1179656 | tf_op jit(solution)/shard_map/ppermute | solution.py:128
  76.5 1.6 %collective-permute-start.18 = (bf16[256,768]{1,0:T(8,128)(2,1)S(1)}, bf16[256,768]{1,0:T(8,128)(2,1)S(1)}, u32[]{:S(2)}, u32[]{:S(2)}) collective-permute-start(bf16[256,768]{1,0:T(8,128)(2,1)S(1)} %get-tuple-element.45), channel_id=1, source_target_pairs={{0,1},{1,0},{2,3},{3,2},{4,5},{5,4},{6,7},{7,6},{8,9},{9,8},{10,11... | collective-permute-start | bytes 1179656 | tf_op jit(solution)/shard_map/ppermute | solution.py:557
  78.1 0.3 collective-permute-start.19
  78.4 1.6 %collective-permute-start.20 = (bf16[256,768]{1,0:T(8,128)(2,1)S(1)}, bf16[256,768]{1,0:T(8,128)(2,1)S(1)}, u32[]{:S(2)}, u32[]{:S(2)}) collective-permute-start(bf16[256,768]{1,0:T(8,128)(2,1)S(1)} %get-tuple-element.47), channel_id=1, source_target_pairs={{0,3},{1,2},{2,1},{3,0},{4,7},{5,6},{6,5},{7,4},{8,11},{9,10},{10,... | collective-permute-start | bytes 1179656 | tf_op jit(solution)/shard_map/ppermute | solution.py:557
  80.0 1.7 %collective-permute-done.21.refs_2_ = bf16[2,256,384]{2,1,0:T(8,128)(2,1)S(1)} collective-permute-done((bf16[2,256,384]{2,1,0:T(8,128)(2,1)S(1)}, bf16[2,256,384]{2,1,0:T(8,128)(2,1)S(1)}, u32[]{:S(2)}, u32[]{:S(2)}) %collective-permute-start.21) | collective-permute-done | bytes 393248 | tf_op jit(solution)/shard_map/ppermute | solution.py:128
  81.7 3.5 %collective-permute-done.22.refs_3_ = bf16[2,256,384]{2,1,0:T(8,128)(2,1)S(1)} collective-permute-done((bf16[2,256,384]{2,1,0:T(8,128)(2,1)S(1)}, bf16[2,256,384]{2,1,0:T(8,128)(2,1)S(1)}, u32[]{:S(2)}, u32[]{:S(2)}) %collective-permute-start.22) | collective-permute-done | bytes 393248 | tf_op jit(solution)/shard_map/ppermute | solution.py:128
  85.2 4.1 %collective-permute-start.24 = (bf16[2,256,384]{2,1,0:T(8,128)(2,1)S(1)}, bf16[2,256,384]{2,1,0:T(8,128)(2,1)S(1)}, u32[]{:S(2)}, u32[]{:S(2)}) collective-permute-start(bf16[2,256,384]{2,1,0:T(8,128)(2,1)S(1)} %pad_maximum_fusion.3), channel_id=1, source_target_pairs={{0,28},{8,20},{16,12},{24,4},{1,29},{9,21},{17,13},{25,5},{2,30},{... | collective-permute-start | bytes 1179656 | tf_op jit(solution)/shard_map/ppermute | solution.py:128
  89.3 0.7 collective-permute-start.23
  90.0 3.6 %collective-permute-done.18 = bf16[256,768]{1,0:T(8,128)(2,1)S(1)} collective-permute-done((bf16[256,768]{1,0:T(8,128)(2,1)S(1)}, bf16[256,768]{1,0:T(8,128)(2,1)S(1)}, u32[]{:S(2)}, u32[]{:S(2)}) %collective-permute-start.18) | collective-permute-done | bytes 393248 | tf_op jit(solution)/shard_map/ppermute | solution.py:557
  93.6 11.2 %collective-permute-done.19 = bf16[256,768]{1,0:T(8,128)(2,1)S(1)} collective-permute-done((bf16[256,768]{1,0:T(8,128)(2,1)S(1)}, bf16[256,768]{1,0:T(8,128)(2,1)S(1)}, u32[]{:S(2)}, u32[]{:S(2)}) %collective-permute-start.19) | collective-permute-done | bytes 393248 | tf_op jit(solution)/shard_map/ppermute | solution.py:557
  104.8 9.1 %collective-permute-done.20 = bf16[256,768]{1,0:T(8,128)(2,1)S(1)} collective-permute-done((bf16[256,768]{1,0:T(8,128)(2,1)S(1)}, bf16[256,768]{1,0:T(8,128)(2,1)S(1)}, u32[]{:S(2)}, u32[]{:S(2)}) %collective-permute-start.20) | collective-permute-done | bytes 393248 | tf_op jit(solution)/shard_map/ppermute | solution.py:557
  113.9 0.2 add_convert_fusion
  114.1 2.5 %collective-permute-start.25 = (bf16[256,768]{1,0:T(8,128)(2,1)S(1)}, bf16[256,768]{1,0:T(8,128)(2,1)S(1)}, u32[]{:S(2)}, u32[]{:S(2)}) collective-permute-start(bf16[256,768]{1,0:T(8,128)(2,1)S(1)} %add_convert_fusion), channel_id=1, source_target_pairs={{0,0},{1,5},{2,10},{3,15},{4,20},{5,17},{6,30},{7,27},{8,8},{9,13}... | collective-permute-start | bytes 1179656 | tf_op jit(solution)/shard_map/ppermute | solution.py:581
  116.6 8.1 %collective-permute-done.25 = bf16[256,768]{1,0:T(8,128)(2,1)S(1)} collective-permute-done((bf16[256,768]{1,0:T(8,128)(2,1)S(1)}, bf16[256,768]{1,0:T(8,128)(2,1)S(1)}, u32[]{:S(2)}, u32[]{:S(2)}) %collective-permute-start.25) | collective-permute-done | bytes 393248 | tf_op jit(solution)/shard_map/ppermute | solution.py:581
  124.7 2.9 %weight_gradient_mate.1 = bf16[3,384,768]{2,1,0:T(8,128)(2,1)S(1)} custom-call(s32[4]{0:T(128)S(1)} %copy-done.4, bf16[2,256,384]{2,1,0:T(8,128)(2,1)S(1)} %pad_maximum_fusion.refs_0_, bf16[2,256,384]{2,1,0:T(8,128)(2,1)S(1)} %collective-permute-done.12.refs_1_, bf16[2,256,384]{2,1,0:T(8,128)(2,1)S(1)} %collective-permute-done.21.refs_2_, ...), custom_call_target="tpu_custom_call" | custom-call | flops 1811939328 | bytes 9043968 | tf_op jit(solution)/shard_map/weight_gradient_mate/pallas_call | solution.py:458
  127.7 0.6 collective-permute-start.27
  128.2 1.9 %collective-permute-start.26 = (bf16[256,768]{1,0:T(8,128)(2,1)S(1)}, bf16[256,768]{1,0:T(8,128)(2,1)S(1)}, u32[]{:S(2)}, u32[]{:S(2)}) collective-permute-start(bf16[256,768]{1,0:T(8,128)(2,1)S(1)} %collective-permute-done.25), channel_id=1, source_target_pairs={{0,0},{5,4},{10,8},{15,12},{20,20},{17,16},{30,28},{27,24},{8,9},{... | collective-permute-start | bytes 1179656 | tf_op jit(solution)/shard_map/ppermute | solution.py:591
  130.2 1.4 collective-permute-done.27.refs_18_
  131.6 4.7 %weight_gradient_own.1 = (f32[384,768]{1,0:T(8,128)}, f32[384,768]{1,0:T(8,128)}, f32[384,768]{1,0:T(8,128)}) custom-call(s32[4]{0:T(128)S(1)} %copy-done.4, bf16[2,256,384]{2,1,0:T(8,128)(2,1)S(1)} %pad_maximum_fusion.refs_0_, bf16[2,256,384]{2,1,0:T(8,128)(2,1)S(1)} %collective-permute-done.12.refs_1_, ...), custom_call_target="tpu_custom_call" | custom-call | flops 1811939328 | bytes 9043968 | tf_op jit(solution)/shard_map/weight_gradient_own/pallas_call | solution.py:458
  136.2 5.8 %collective-permute-done.26 = bf16[256,768]{1,0:T(8,128)(2,1)S(1)} collective-permute-done((bf16[256,768]{1,0:T(8,128)(2,1)S(1)}, bf16[256,768]{1,0:T(8,128)(2,1)S(1)}, u32[]{:S(2)}, u32[]{:S(2)}) %collective-permute-start.26) | collective-permute-done | bytes 393248 | tf_op jit(solution)/shard_map/ppermute | solution.py:591
  142.1 0.7 copy.14
  (23 shorter events, 0.1 us)
Async XLA Ops:
  4.1 9.5 %collective-permute-start.1 = (bf16[1,1040,128]{2,1,0:T(8,128)(2,1)}, bf16[1,1040,128]{2,1,0:T(8,128)(2,1)S(1)}, u32[]{:S(2)}, u32[]{:S(2)}) collective-permute-start(bf16[1,1040,128]{2,1,0:T(8,128)(2,1)} %get-tuple-element.33), channel_id=1, source_target_pairs={{0,8},{4,12},{8,0},{12,4},{16,24},{20,28},{24,16},{28,20},{1,9},{5... | collective-permute-start | bytes 798728 | tf_op jit(solution)/shard_map/ppermute | solution.py:128
  5.6 9.5 %collective-permute-start = (bf16[1,1040,128]{2,1,0:T(8,128)(2,1)}, bf16[1,1040,128]{2,1,0:T(8,128)(2,1)S(1)}, u32[]{:S(2)}, u32[]{:S(2)}) collective-permute-start(bf16[1,1040,128]{2,1,0:T(8,128)(2,1)} %get-tuple-element.32), channel_id=1, source_target_pairs={{0,4},{4,0},{8,12},{12,8},{16,20},{20,16},{24,28},{28,24},{1,5},{5... | collective-permute-start | bytes 798728 | tf_op jit(solution)/shard_map/ppermute | solution.py:128
  5.6 12.8 %collective-permute-start.2 = (bf16[1,1040,128]{2,1,0:T(8,128)(2,1)}, bf16[1,1040,128]{2,1,0:T(8,128)(2,1)S(1)}, u32[]{:S(2)}, u32[]{:S(2)}) collective-permute-start(bf16[1,1040,128]{2,1,0:T(8,128)(2,1)} %get-tuple-element.34), channel_id=1, source_target_pairs={{0,12},{4,8},{8,4},{12,0},{16,28},{20,24},{24,20},{28,16},{1,13},{... | collective-permute-start | bytes 798728 | tf_op jit(solution)/shard_map/ppermute | solution.py:128
  13.6 12.8 %collective-permute-start.4 = (bf16[1,1040,128]{2,1,0:T(8,128)(2,1)}, bf16[1,1040,128]{2,1,0:T(8,128)(2,1)S(1)}, u32[]{:S(2)}, u32[]{:S(2)}) collective-permute-start(bf16[1,1040,128]{2,1,0:T(8,128)(2,1)} %get-tuple-element.41), channel_id=1, source_target_pairs={{0,8},{4,12},{8,0},{12,4},{16,24},{20,28},{24,16},{28,20},{1,9},{5... | collective-permute-start | bytes 798728 | tf_op jit(solution)/shard_map/ppermute | solution.py:128
  15.0 14.7 %collective-permute-start.3 = (bf16[1,1040,128]{2,1,0:T(8,128)(2,1)}, bf16[1,1040,128]{2,1,0:T(8,128)(2,1)S(1)}, u32[]{:S(2)}, u32[]{:S(2)}) collective-permute-start(bf16[1,1040,128]{2,1,0:T(8,128)(2,1)} %get-tuple-element.39.own), channel_id=1, source_target_pairs={{0,4},{4,0},{8,12},{12,8},{16,20},{20,16},{24,28},{28,24},{1,5},{5... | collective-permute-start | bytes 798728 | tf_op jit(solution)/shard_map/ppermute | solution.py:128
  18.4 0.6 copy-start.3
  19.0 1.0 copy-start.6
  20.0 4.5 %copy-start = (bf16[384,768]{1,0:T(8,128)(2,1)S(1)}, bf16[384,768]{1,0:T(8,128)(2,1)}, u32[]{:S(2)}) copy-start(bf16[384,768]{1,0:T(8,128)(2,1)} %q_ref) | copy-start | bytes 1769476
  20.0 4.5 %copy-start.1 = (bf16[384,768]{1,0:T(8,128)(2,1)S(1)}, bf16[384,768]{1,0:T(8,128)(2,1)}, u32[]{:S(2)}) copy-start(bf16[384,768]{1,0:T(8,128)(2,1)} %k_ref) | copy-start | bytes 1769476
  20.0 4.5 %copy-start.2 = (bf16[384,768]{1,0:T(8,128)(2,1)S(1)}, bf16[384,768]{1,0:T(8,128)(2,1)}, u32[]{:S(2)}) copy-start(bf16[384,768]{1,0:T(8,128)(2,1)} %v_ref) | copy-start | bytes 1769476
  24.4 2.0 %copy-start.7 = (bf16[1,1,256,3072]{3,2,1,0:T(8,128)(2,1)S(1)}, bf16[1,1,256,3072]{3,2,1,0:T(8,128)(2,1)}, u32[]{:S(2)}) copy-start(bf16[1,1,256,3072]{3,2,1,0:T(8,128)(2,1)} %param.9) | copy-start | bytes 4718596
  25.5 6.9 %copy-start.4 = (s32[4]{0:T(128)S(1)}, s32[4]{0:T(128)}, u32[]{:S(2)}) copy-start(s32[4]{0:T(128)} %pad_add_fusion.place_ref) | copy-start | bytes 52
  25.5 6.9 %copy-start.5 = (bf16[1,1040,128]{2,1,0:T(8,128)(2,1)S(1)}, bf16[1,1040,128]{2,1,0:T(8,128)(2,1)}, u32[]{:S(2)}) copy-start(bf16[1,1040,128]{2,1,0:T(8,128)(2,1)} %get-tuple-element.39.own) | copy-start | bytes 798724
  25.5 33.9 %collective-permute-start.17 = (bf16[2304,384]{1,0:T(8,128)(2,1)S(1)}, bf16[2304,384]{1,0:T(8,128)(2,1)S(1)}, u32[]{:S(2)}, u32[]{:S(2)}) collective-permute-start(bf16[2304,384]{1,0:T(8,128)(2,1)S(1)} %turn_weights.1.own_ref), channel_id=1, source_target_pairs={{0,4},{4,0},{8,12},{12,8},{16,20},{20,16},{24,28},{28,24},{1,5},{5... | collective-permute-start | bytes 5308424 | tf_op jit(solution)/shard_map/ppermute | solution.py:128
  26.3 4.8 %collective-permute-start.5 = (bf16[1,1040,128]{2,1,0:T(8,128)(2,1)S(1)}, bf16[1,1040,128]{2,1,0:T(8,128)(2,1)S(1)}, u32[]{:S(2)}, u32[]{:S(2)}) collective-permute-start(bf16[1,1040,128]{2,1,0:T(8,128)(2,1)S(1)} %collective-permute-done.4.x_in), channel_id=1, source_target_pairs={{0,4},{4,0},{8,12},{12,8},{16,20},{20,16},{24,28},{28,24},{1,5},{5... | collective-permute-start | bytes 798728 | tf_op jit(solution)/shard_map/ppermute | solution.py:128
  26.6 19.0 %collective-permute-start.10 = (bf16[4,256,384]{2,1,0:T(8,128)(2,1)S(1)}, bf16[4,256,384]{2,1,0:T(8,128)(2,1)S(1)}, u32[]{:S(2)}, u32[]{:S(2)}) collective-permute-start(bf16[4,256,384]{2,1,0:T(8,128)(2,1)S(1)} %attention_gradients.2.refs_0_.refs_6_), channel_id=1, source_target_pairs={{0,20},{4,8},{8,28},{12,0},{16,4},{20,24},{24,12},{28,16},{1,21},{... | collective-permute-start | bytes 2359304 | tf_op jit(solution)/shard_map/ppermute | solution.py:128
  28.2 20.5 %collective-permute-start.8 = (bf16[4,256,384]{2,1,0:T(8,128)(2,1)S(1)}, bf16[4,256,384]{2,1,0:T(8,128)(2,1)S(1)}, u32[]{:S(2)}, u32[]{:S(2)}) collective-permute-start(bf16[4,256,384]{2,1,0:T(8,128)(2,1)S(1)} %attention_gradients.2.refs_0_.refs_6_), channel_id=1, source_target_pairs={{0,8},{4,20},{8,0},{12,28},{16,24},{20,4},{24,16},{28,12},{1,9},{5... | collective-permute-start | bytes 2359304 | tf_op jit(solution)/shard_map/ppermute | solution.py:128
  29.7 20.3 %collective-permute-start.6 = (bf16[4,256,384]{2,1,0:T(8,128)(2,1)S(1)}, bf16[4,256,384]{2,1,0:T(8,128)(2,1)S(1)}, u32[]{:S(2)}, u32[]{:S(2)}) collective-permute-start(bf16[4,256,384]{2,1,0:T(8,128)(2,1)S(1)} %attention_gradients.2.refs_0_.refs_6_), channel_id=1, source_target_pairs={{4,0},{12,8},{20,16},{28,24},{5,1},{13,9},{21,17},{29,25},{6,2},{1... | collective-permute-start | bytes 2359304 | tf_op jit(solution)/shard_map/ppermute | solution.py:128
  31.1 5.6 %collective-permute-start.12 = (bf16[2,256,384]{2,1,0:T(8,128)(2,1)S(1)}, bf16[2,256,384]{2,1,0:T(8,128)(2,1)S(1)}, u32[]{:S(2)}, u32[]{:S(2)}) collective-permute-start(bf16[2,256,384]{2,1,0:T(8,128)(2,1)S(1)} %pad_maximum_fusion.refs_0_), channel_id=1, source_target_pairs={{4,0},{12,8},{20,16},{28,24},{5,1},{13,9},{21,17},{29,25},{6,2},{1... | collective-permute-start | bytes 1179656 | tf_op jit(solution)/shard_map/ppermute | solution.py:128
  36.7 16.4 %collective-permute-start.11 = (bf16[2,256,384]{2,1,0:T(8,128)(2,1)S(1)}, bf16[2,256,384]{2,1,0:T(8,128)(2,1)S(1)}, u32[]{:S(2)}, u32[]{:S(2)}) collective-permute-start(bf16[2,256,384]{2,1,0:T(8,128)(2,1)S(1)} %attention_gradients.3.refs_1_.refs_7_), channel_id=1, source_target_pairs={{0,20},{4,8},{8,28},{12,0},{16,4},{20,24},{24,12},{28,16},{1,21},{... | collective-permute-start | bytes 1179656 | tf_op jit(solution)/shard_map/ppermute | solution.py:128
  45.6 9.4 %collective-permute-start.9 = (bf16[2,256,384]{2,1,0:T(8,128)(2,1)S(1)}, bf16[2,256,384]{2,1,0:T(8,128)(2,1)S(1)}, u32[]{:S(2)}, u32[]{:S(2)}) collective-permute-start(bf16[2,256,384]{2,1,0:T(8,128)(2,1)S(1)} %attention_gradients.3.refs_1_.refs_7_), channel_id=1, source_target_pairs={{0,8},{4,20},{8,0},{12,28},{16,24},{20,4},{24,16},{28,12},{1,9},{5... | collective-permute-start | bytes 1179656 | tf_op jit(solution)/shard_map/ppermute | solution.py:128
  48.7 6.2 %collective-permute-start.7 = (bf16[2,256,384]{2,1,0:T(8,128)(2,1)S(1)}, bf16[2,256,384]{2,1,0:T(8,128)(2,1)S(1)}, u32[]{:S(2)}, u32[]{:S(2)}) collective-permute-start(bf16[2,256,384]{2,1,0:T(8,128)(2,1)S(1)} %attention_gradients.3.refs_1_.refs_7_), channel_id=1, source_target_pairs={{4,0},{12,8},{20,16},{28,24},{5,1},{13,9},{21,17},{29,25},{6,2},{1... | collective-permute-start | bytes 1179656 | tf_op jit(solution)/shard_map/ppermute | solution.py:128
  50.0 17.2 %collective-permute-start.15 = (bf16[4,256,384]{2,1,0:T(8,128)(2,1)S(1)}, bf16[4,256,384]{2,1,0:T(8,128)(2,1)S(1)}, u32[]{:S(2)}, u32[]{:S(2)}) collective-permute-start(bf16[4,256,384]{2,1,0:T(8,128)(2,1)S(1)} %collective-permute-done.8.refs_4_.refs_10_), channel_id=1, source_target_pairs={{0,20},{8,28},{16,4},{24,12},{1,21},{9,29},{17,5},{25,13},{2,22},{... | collective-permute-start | bytes 2359304 | tf_op jit(solution)/shard_map/ppermute | solution.py:128
  53.2 14.1 %collective-permute-start.13 = (bf16[4,256,384]{2,1,0:T(8,128)(2,1)S(1)}, bf16[4,256,384]{2,1,0:T(8,128)(2,1)S(1)}, u32[]{:S(2)}, u32[]{:S(2)}) collective-permute-start(bf16[4,256,384]{2,1,0:T(8,128)(2,1)S(1)} %collective-permute-done.8.refs_4_.refs_10_), channel_id=1, source_target_pairs={{4,12},{12,4},{20,28},{28,20},{5,13},{13,5},{21,29},{29,21},{6,14}... | collective-permute-start | bytes 2359304 | tf_op jit(solution)/shard_map/ppermute | solution.py:128
  55.0 12.3 %collective-permute-start.16 = (bf16[2,256,384]{2,1,0:T(8,128)(2,1)S(1)}, bf16[2,256,384]{2,1,0:T(8,128)(2,1)S(1)}, u32[]{:S(2)}, u32[]{:S(2)}) collective-permute-start(bf16[2,256,384]{2,1,0:T(8,128)(2,1)S(1)} %collective-permute-done.9.refs_5_.refs_11_), channel_id=1, source_target_pairs={{0,20},{8,28},{16,4},{24,12},{1,21},{9,29},{17,5},{25,13},{2,22},{... | collective-permute-start | bytes 1179656 | tf_op jit(solution)/shard_map/ppermute | solution.py:128
  58.8 8.5 %collective-permute-start.14 = (bf16[2,256,384]{2,1,0:T(8,128)(2,1)S(1)}, bf16[2,256,384]{2,1,0:T(8,128)(2,1)S(1)}, u32[]{:S(2)}, u32[]{:S(2)}) collective-permute-start(bf16[2,256,384]{2,1,0:T(8,128)(2,1)S(1)} %collective-permute-done.9.refs_5_.refs_11_), channel_id=1, source_target_pairs={{4,12},{12,4},{20,28},{28,20},{5,13},{13,5},{21,29},{29,21},{6,14}... | collective-permute-start | bytes 1179656 | tf_op jit(solution)/shard_map/ppermute | solution.py:128
  71.9 9.7 %collective-permute-start.21 = (bf16[2,256,384]{2,1,0:T(8,128)(2,1)S(1)}, bf16[2,256,384]{2,1,0:T(8,128)(2,1)S(1)}, u32[]{:S(2)}, u32[]{:S(2)}) collective-permute-start(bf16[2,256,384]{2,1,0:T(8,128)(2,1)S(1)} %get-tuple-element.48), channel_id=1, source_target_pairs={{0,8},{4,20},{8,0},{12,28},{16,24},{20,4},{24,16},{28,12},{1,9},{5... | collective-permute-start | bytes 1179656 | tf_op jit(solution)/shard_map/ppermute | solution.py:128
  73.1 12.1 %collective-permute-start.22 = (bf16[2,256,384]{2,1,0:T(8,128)(2,1)S(1)}, bf16[2,256,384]{2,1,0:T(8,128)(2,1)S(1)}, u32[]{:S(2)}, u32[]{:S(2)}) collective-permute-start(bf16[2,256,384]{2,1,0:T(8,128)(2,1)S(1)} %get-tuple-element.49), channel_id=1, source_target_pairs={{0,20},{4,8},{8,28},{12,0},{16,4},{20,24},{24,12},{28,16},{1,21},{... | collective-permute-start | bytes 1179656 | tf_op jit(solution)/shard_map/ppermute | solution.py:128
  76.5 17.1 %collective-permute-start.18 = (bf16[256,768]{1,0:T(8,128)(2,1)S(1)}, bf16[256,768]{1,0:T(8,128)(2,1)S(1)}, u32[]{:S(2)}, u32[]{:S(2)}) collective-permute-start(bf16[256,768]{1,0:T(8,128)(2,1)S(1)} %get-tuple-element.45), channel_id=1, source_target_pairs={{0,1},{1,0},{2,3},{3,2},{4,5},{5,4},{6,7},{7,6},{8,9},{9,8},{10,11... | collective-permute-start | bytes 1179656 | tf_op jit(solution)/shard_map/ppermute | solution.py:557
  78.1 26.7 %collective-permute-start.19 = (bf16[256,768]{1,0:T(8,128)(2,1)S(1)}, bf16[256,768]{1,0:T(8,128)(2,1)S(1)}, u32[]{:S(2)}, u32[]{:S(2)}) collective-permute-start(bf16[256,768]{1,0:T(8,128)(2,1)S(1)} %get-tuple-element.46), channel_id=1, source_target_pairs={{0,2},{1,3},{2,0},{3,1},{4,6},{5,7},{6,4},{7,5},{8,10},{9,11},{10,... | collective-permute-start | bytes 1179656 | tf_op jit(solution)/shard_map/ppermute | solution.py:557
  78.4 35.5 %collective-permute-start.20 = (bf16[256,768]{1,0:T(8,128)(2,1)S(1)}, bf16[256,768]{1,0:T(8,128)(2,1)S(1)}, u32[]{:S(2)}, u32[]{:S(2)}) collective-permute-start(bf16[256,768]{1,0:T(8,128)(2,1)S(1)} %get-tuple-element.47), channel_id=1, source_target_pairs={{0,3},{1,2},{2,1},{3,0},{4,7},{5,6},{6,5},{7,4},{8,11},{9,10},{10,... | collective-permute-start | bytes 1179656 | tf_op jit(solution)/shard_map/ppermute | solution.py:557
  85.2 28.9 %collective-permute-start.24 = (bf16[2,256,384]{2,1,0:T(8,128)(2,1)S(1)}, bf16[2,256,384]{2,1,0:T(8,128)(2,1)S(1)}, u32[]{:S(2)}, u32[]{:S(2)}) collective-permute-start(bf16[2,256,384]{2,1,0:T(8,128)(2,1)S(1)} %pad_maximum_fusion.3), channel_id=1, source_target_pairs={{0,28},{8,20},{16,12},{24,4},{1,29},{9,21},{17,13},{25,5},{2,30},{... | collective-permute-start | bytes 1179656 | tf_op jit(solution)/shard_map/ppermute | solution.py:128
  89.3 24.8 %collective-permute-start.23 = (bf16[2,256,384]{2,1,0:T(8,128)(2,1)S(1)}, bf16[2,256,384]{2,1,0:T(8,128)(2,1)S(1)}, u32[]{:S(2)}, u32[]{:S(2)}) collective-permute-start(bf16[2,256,384]{2,1,0:T(8,128)(2,1)S(1)} %pad_maximum_fusion.3), channel_id=1, source_target_pairs={{4,28},{12,20},{20,12},{28,4},{5,29},{13,21},{21,13},{29,5},{6,30}... | collective-permute-start | bytes 1179656 | tf_op jit(solution)/shard_map/ppermute | solution.py:128
  114.1 10.6 %collective-permute-start.25 = (bf16[256,768]{1,0:T(8,128)(2,1)S(1)}, bf16[256,768]{1,0:T(8,128)(2,1)S(1)}, u32[]{:S(2)}, u32[]{:S(2)}) collective-permute-start(bf16[256,768]{1,0:T(8,128)(2,1)S(1)} %add_convert_fusion), channel_id=1, source_target_pairs={{0,0},{1,5},{2,10},{3,15},{4,20},{5,17},{6,30},{7,27},{8,8},{9,13}... | collective-permute-start | bytes 1179656 | tf_op jit(solution)/shard_map/ppermute | solution.py:581
  127.7 3.9 %collective-permute-start.27 = (bf16[3,384,768]{2,1,0:T(8,128)(2,1)S(1)}, bf16[3,384,768]{2,1,0:T(8,128)(2,1)S(1)}, u32[]{:S(2)}, u32[]{:S(2)}) collective-permute-start(bf16[3,384,768]{2,1,0:T(8,128)(2,1)S(1)} %weight_gradient_mate.1), channel_id=1, source_target_pairs={{0,4},{4,0},{8,12},{12,8},{16,20},{20,16},{24,28},{28,24},{1,5},{5... | collective-permute-start | bytes 5308424 | tf_op jit(solution)/shard_map/ppermute | solution.py:128
  128.2 13.8 %collective-permute-start.26 = (bf16[256,768]{1,0:T(8,128)(2,1)S(1)}, bf16[256,768]{1,0:T(8,128)(2,1)S(1)}, u32[]{:S(2)}, u32[]{:S(2)}) collective-permute-start(bf16[256,768]{1,0:T(8,128)(2,1)S(1)} %collective-permute-done.25), channel_id=1, source_target_pairs={{0,0},{5,4},{10,8},{15,12},{20,20},{17,16},{30,28},{27,24},{8,9},{... | collective-permute-start | bytes 1179656 | tf_op jit(solution)/shard_map/ppermute | solution.py:591

commit v12 on v11

--- a/solution.py
+++ b/solution.py
@@ -308,7 +308,7 @@
         out_specs=whole(),
         scratch_shapes=[pltpu.VMEM((6 * length, HD), jnp.bfloat16)] * 2
         + [pltpu.VMEM((6 * length, HD), jnp.float32)] * 2,
-        compiler_params=pltpu.CompilerParams(vmem_limit_bytes=12 * MIB),
+        compiler_params=pltpu.CompilerParams(vmem_limit_bytes=40 * MIB),
         cost_estimate=pl.CostEstimate(
             flops=heads * 4 * 5 * 2 * length * 3 * length * HD * 2,
             bytes_accessed=heads * 2 * length * 7 * HD * 4,
@@ -532,8 +532,6 @@
     to_straight = columns(jnp.where(core == 0, toward_x, toward_y))
     to_crossed = columns(jnp.where(core == 0, toward_y, toward_x))
     to_corner = columns(jnp.bitwise_xor(chip, 3))
-    mate_here = moved(here, only(1, mate))
-
     own_weights, turn = None, place
     parts = []
     for kept, sources in sets:
@@ -541,11 +539,11 @@
         if own_weights is None:
             ready = after((query_weight, key_weight, value_weight), made)
             own_weights = turned_weights(place, ready)
-        (turn,) = after((place,), made, own_weights)
         ahead = moved(made, straight)
         aside = moved(made, crossed)
         inward = moved(made, only(1, mate))
-        (sent,) = after((ahead,), aside, inward, mate_here, to_straight, to_crossed, to_corner)
+        (turn,) = after((place,), made, own_weights)
+        (sent,) = after((ahead,), aside, inward, here, to_straight, to_crossed, to_corner)
         relay_x = moved(sent, only(1, along_x))
         relay_y = moved(sent, only(0, across_y))
         parts.append((made, inward, ahead, aside, relay_x, relay_y))
@@ -563,7 +561,8 @@
     to_straight, to_crossed = after((to_straight, to_crossed), *slots)
     normed_ahead = moved(to_straight, straight)
     normed_aside = moved(to_crossed, crossed)
-    (to_corner,) = after((to_corner,), normed_ahead, normed_aside)
+    to_corner, sent = after((to_corner, here), normed_ahead, normed_aside)
+    mate_here = moved(sent, only(1, mate))
     tokens = (
         here,
         mate_here,

time: 143 us -> 145 us (1.014)
  waiting for transfers between devices: 71.8 us -> 65.7 us
  Pallas kernels: 25.8 us -> 30.1 us
  local copies, waits for them, and re-layouts: 2.58 us -> 5.12 us
    ppermute x23, waiting for transfers between devices: 34 us -> 30.3 us  [moved(): return lax.ppermute(value, ('dp', 'view'), pairs)]
    unnamed x17 -> x21, local copies, waits for them, and re-layouts: 2.35 us -> 4.88 us
    pallas_call x2, Pallas kernels: 7.63 us -> 9.5 us  [weight_product(): pl.pallas_call(functools.partial(weight_kernel, mine, mean_scale, len(gra...]
  transfers between devices with their start and end apart: 28 -> 28, of which waited for: 14 -> 14; matrix products, arithmetic and copies ran while one was open for 0% -> 0% of each run, Pallas kernels for 11% -> 12%
where the time goes in v12:
time: 145 us; the launch traced here: 144 us
  waiting for transfers between devices  65.7 us (45%)
  starting transfers between devices  41.3 us (28%)
  Pallas kernels  30.1 us (21%)
  local copies, waits for them, and re-layouts  5.12 us (4%)
    ppermute x23, starting transfers between devices, moved(): return lax.ppermute(value, ('dp', 'view'), pairs)  33.4 us
    ppermute x23, waiting for transfers between devices, moved(): return lax.ppermute(value, ('dp', 'view'), pairs)  30.3 us
    ppermute x3, waiting for transfers between devices, gather_body(): lax.ppermute(slots[s], 'head', [(z, z ^ s) for z in range(groups)])  23.9 us
    pallas_call x2, Pallas kernels, weight_product(): pl.pallas_call(functools.partial(weight_kernel, mine, mean_scale, len(gra...  9.5 us
    pallas_call x2, Pallas kernels, attention(): pl.pallas_call(functools.partial(attention_kernel, HD ** (-0.5), kept), o...  9.36 us
    ppermute x1, waiting for transfers between devices, gather_body(): lax.ppermute(total, ('dp', 'view', 'head'), [(spot(y, v, z), spot(y ^ v %...  6.76 us
    pallas_call x1, Pallas kernels, input_product(): pl.pallas_call(functools.partial(input_kernel, len(grads) // 6), out_shap...  5.56 us
    unnamed x21, local copies, waits for them, and re-layouts  4.88 us
  transfers between devices with their start and end apart: 28, of which 14 were waited for; matrix products, arithmetic and copies ran while one was open for 0% of the time, Pallas kernels for 12%

profile of v12, /device:TPU:16, one launch (start us, length us, event | category | flops | bytes accessed | tf_op | source)
XLA Modules:
  0.0 144.2 jit_solution(922237541141236517)
XLA Ops:
  0.6 0.6 pad_add_fusion.place_ref
  1.2 2.8 %pack_heads.1 = (bf16[1,1040,128]{2,1,0:T(8,128)(2,1)}, bf16[1,1040,128]{2,1,0:T(8,128)(2,1)}, bf16[1,1040,128]{2,1,0:T(8,128)(2,1)}, bf16[1,1040,128]{2,1,0:T(8...) custom-call(s32[4]{0:T(128)} %pad_add_fusion.place_ref, s32[1,2]{1,0:T(1,128)} %links_ref.1, ...), custom_call_target="tpu_custom_call" | custom-call | tf_op jit(solution)/shard_map/pack_heads/pallas_call | solution.py:215
  4.0 1.5 %collective-permute-start.1 = (bf16[1,1040,128]{2,1,0:T(8,128)(2,1)}, bf16[1,1040,128]{2,1,0:T(8,128)(2,1)S(1)}, u32[]{:S(2)}, u32[]{:S(2)}) collective-permute-start(bf16[1,1040,128]{2,1,0:T(8,128)(2,1)} %get-tuple-element.34), channel_id=1, source_target_pairs={{0,8},{4,12},{8,0},{12,4},{16,24},{20,28},{24,16},{28,20},{1,9},{5... | collective-permute-start | bytes 798728 | tf_op jit(solution)/shard_map/ppermute | solution.py:128
  5.5 0.0 collective-permute-start
  5.5 0.6 collective-permute-start.2
  6.1 0.0 collective-permute-start.3
  6.1 7.3 %collective-permute-done.1.x_in = bf16[1,1040,128]{2,1,0:T(8,128)(2,1)S(1)} collective-permute-done((bf16[1,1040,128]{2,1,0:T(8,128)(2,1)}, bf16[1,1040,128]{2,1,0:T(8,128)(2,1)S(1)}, u32[]{:S(2)}, u32[]{:S(2)}) %collective-permute-start.1) | collective-permute-done | bytes 266272 | tf_op jit(solution)/shard_map/ppermute | solution.py:128
  13.5 1.5 %collective-permute-start.4 = (bf16[1,1040,128]{2,1,0:T(8,128)(2,1)}, bf16[1,1040,128]{2,1,0:T(8,128)(2,1)}, u32[]{:S(2)}, u32[]{:S(2)}) collective-permute-start(bf16[1,1040,128]{2,1,0:T(8,128)(2,1)} %get-tuple-element.42), channel_id=1, source_target_pairs={{0,8},{4,12},{8,0},{12,4},{16,24},{20,28},{24,16},{28,20},{1,9},{5... | collective-permute-start | bytes 798728 | tf_op jit(solution)/shard_map/ppermute | solution.py:128
  15.0 3.3 %collective-permute-done.2.far_in = bf16[1,1040,128]{2,1,0:T(8,128)(2,1)S(1)} collective-permute-done((bf16[1,1040,128]{2,1,0:T(8,128)(2,1)}, bf16[1,1040,128]{2,1,0:T(8,128)(2,1)S(1)}, u32[]{:S(2)}, u32[]{:S(2)}) %collective-permute-start.2) | collective-permute-done | bytes 266272 | tf_op jit(solution)/shard_map/ppermute | solution.py:128
  18.3 0.6 copy-done.3
  18.9 0.9 copy-done.8
  19.8 4.5 %attention_gradients.2.refs_0_.refs_6_ = bf16[4,256,384]{2,1,0:T(8,128)(2,1)S(1)} custom-call(s32[4]{0:T(128)S(1)} %copy-done.3, bf16[1,1040,128]{2,1,0:T(8,128)(2,1)S(1)} %copy-done.8, bf16[1,1040,128]{2,1,0:T(8,128)(2,1)S(1)} %collective-permute-done.mate_in, bf16[1,1040,128]{2,1,0:T(8,128)(2,1)S(1)} %collective-permute-done.1.x_in, ...), custom_call_target="tpu_custom_call" | custom-call | flops 2013265920 | bytes 1835008 | tf_op jit(solution)/shard_map/attention_gradients/pallas_call | solution.py:304
  24.3 1.1 turn_weights.1.own_ref
  25.4 0.8 collective-permute-start.16
  26.2 0.0 collective-permute-done.4.x_in
  26.2 0.1 collective-permute-start.5
  26.3 1.5 %collective-permute-start.10 = (bf16[4,256,384]{2,1,0:T(8,128)(2,1)S(1)}, bf16[4,256,384]{2,1,0:T(8,128)(2,1)S(1)}, u32[]{:S(2)}, u32[]{:S(2)}) collective-permute-start(bf16[4,256,384]{2,1,0:T(8,128)(2,1)S(1)} %attention_gradients.2.refs_0_.refs_6_), channel_id=1, source_target_pairs={{0,20},{4,8},{8,28},{12,0},{16,4},{20,24},{24,12},{28,16},{1,21},{... | collective-permute-start | bytes 2359304 | tf_op jit(solution)/shard_map/ppermute | solution.py:128
  27.8 1.5 %collective-permute-start.8 = (bf16[4,256,384]{2,1,0:T(8,128)(2,1)S(1)}, bf16[4,256,384]{2,1,0:T(8,128)(2,1)}, u32[]{:S(2)}, u32[]{:S(2)}) collective-permute-start(bf16[4,256,384]{2,1,0:T(8,128)(2,1)S(1)} %attention_gradients.2.refs_0_.refs_6_), channel_id=1, source_target_pairs={{0,8},{4,20},{8,0},{12,28},{16,24},{20,4},{24,16},{28,12},{1,9},{5... | collective-permute-start | bytes 2359304 | tf_op jit(solution)/shard_map/ppermute | solution.py:128
  29.3 0.0 collective-permute-done.3.mate_in
  29.3 0.7 copy-done.6
  30.0 1.3 collective-permute-start.6
  31.4 0.9 copy-done.5
  32.3 0.9 copy-done.7
  33.3 4.9 %attention_gradients.3.refs_1_.refs_7_ = bf16[2,256,384]{2,1,0:T(8,128)(2,1)S(1)} custom-call(s32[4]{0:T(128)S(1)} %copy-done.4, bf16[1,1040,128]{2,1,0:T(8,128)(2,1)S(1)} %copy-done.5, bf16[1,1040,128]{2,1,0:T(8,128)(2,1)S(1)} %copy-done.7, bf16[1,1040,128]{2,1,0:T(8,128)(2,1)} %collective-permute-done.4.x_in, ...), custom_call_target="tpu_custom_call" | custom-call | flops 2013265920 | bytes 1835008 | tf_op jit(solution)/shard_map/attention_gradients/pallas_call | solution.py:304
  38.2 2.1 %collective-permute-start.11 = (bf16[2,256,384]{2,1,0:T(8,128)(2,1)S(1)}, bf16[2,256,384]{2,1,0:T(8,128)(2,1)S(1)}, u32[]{:S(2)}, u32[]{:S(2)}) collective-permute-start(bf16[2,256,384]{2,1,0:T(8,128)(2,1)S(1)} %attention_gradients.3.refs_1_.refs_7_), channel_id=1, source_target_pairs={{0,20},{4,8},{8,28},{12,0},{16,4},{20,24},{24,12},{28,16},{1,21},{... | collective-permute-start | bytes 1179656 | tf_op jit(solution)/shard_map/ppermute | solution.py:128
  40.3 0.2 dynamic-slice_bitcast_fusion.1
  40.5 0.1 pad_maximum_fusion.2
  40.6 0.1 pad_maximum_fusion
  40.7 4.5 %collective-permute-done.10.refs_6_.refs_12_ = bf16[4,256,384]{2,1,0:T(8,128)(2,1)S(1)} collective-permute-done((bf16[4,256,384]{2,1,0:T(8,128)(2,1)S(1)}, bf16[4,256,384]{2,1,0:T(8,128)(2,1)S(1)}, u32[]{:S(2)}, u32[]{:S(2)}) %collective-permute-start.10) | collective-permute-done | bytes 786464 | tf_op jit(solution)/shard_map/ppermute | solution.py:128
  45.2 1.7 %collective-permute-start.9 = (bf16[2,256,384]{2,1,0:T(8,128)(2,1)S(1)}, bf16[2,256,384]{2,1,0:T(8,128)(2,1)S(1)}, u32[]{:S(2)}, u32[]{:S(2)}) collective-permute-start(bf16[2,256,384]{2,1,0:T(8,128)(2,1)S(1)} %attention_gradients.3.refs_1_.refs_7_), channel_id=1, source_target_pairs={{0,8},{4,20},{8,0},{12,28},{16,24},{20,4},{24,16},{28,12},{1,9},{5... | collective-permute-start | bytes 1179656 | tf_op jit(solution)/shard_map/ppermute | solution.py:128
  46.9 1.5 %collective-permute-done.8.refs_4_.refs_10_ = bf16[4,256,384]{2,1,0:T(8,128)(2,1)} collective-permute-done((bf16[4,256,384]{2,1,0:T(8,128)(2,1)S(1)}, bf16[4,256,384]{2,1,0:T(8,128)(2,1)}, u32[]{:S(2)}, u32[]{:S(2)}) %collective-permute-start.8) | collective-permute-done | bytes 786464 | tf_op jit(solution)/shard_map/ppermute | solution.py:128
  48.4 1.3 collective-permute-start.7
  49.7 0.0 collective-permute-done.6.refs_2_.refs_8_
  49.7 3.2 %collective-permute-start.14 = (bf16[4,256,384]{2,1,0:T(8,128)(2,1)}, bf16[4,256,384]{2,1,0:T(8,128)(2,1)S(1)}, u32[]{:S(2)}, u32[]{:S(2)}) collective-permute-start(bf16[4,256,384]{2,1,0:T(8,128)(2,1)} %collective-permute-done.8.refs_4_.refs_10_), channel_id=1, source_target_pairs={{0,20},{8,28},{16,4},{24,12},{1,21},{9,29},{17,5},{25,13},{2,22},{... | collective-permute-start | bytes 2359304 | tf_op jit(solution)/shard_map/ppermute | solution.py:128
  52.9 0.7 collective-permute-start.12
  53.6 0.9 collective-permute-done.9.refs_5_.refs_11_
  54.5 3.7 %collective-permute-start.15 = (bf16[2,256,384]{2,1,0:T(8,128)(2,1)S(1)}, bf16[2,256,384]{2,1,0:T(8,128)(2,1)S(1)}, u32[]{:S(2)}, u32[]{:S(2)}) collective-permute-start(bf16[2,256,384]{2,1,0:T(8,128)(2,1)S(1)} %collective-permute-done.9.refs_5_.refs_11_), channel_id=1, source_target_pairs={{0,20},{8,28},{16,4},{24,12},{1,21},{9,29},{17,5},{25,13},{2,22},{... | collective-permute-start | bytes 1179656 | tf_op jit(solution)/shard_map/ppermute | solution.py:128
  58.2 0.7 collective-permute-start.13
  58.9 1.8 %join_weights.1.refs_12_ = bf16[2304,768]{1,0:T(8,128)(2,1)S(1)} custom-call(s32[4]{0:T(128)S(1)} %copy-done.4, bf16[2304,384]{1,0:T(8,128)(2,1)S(1)} %turn_weights.1.own_ref, bf16[2304,384]{1,0:T(8,128)(2,1)} %collective-permute-done.16.mate_ref), custom_call_target="tpu_custom_call" | custom-call | tf_op jit(solution)/shard_map/join_weights/pallas_call | solution.py:351
  60.7 6.1 %collective-permute-done.15.refs_11_.refs_17_ = bf16[2,256,384]{2,1,0:T(8,128)(2,1)S(1)} collective-permute-done((bf16[2,256,384]{2,1,0:T(8,128)(2,1)S(1)}, bf16[2,256,384]{2,1,0:T(8,128)(2,1)S(1)}, u32[]{:S(2)}, u32[]{:S(2)}) %collective-permute-start.15) | collective-permute-done | bytes 393248 | tf_op jit(solution)/shard_map/ppermute | solution.py:128
  66.8 5.6 %input_gradient.1 = (bf16[256,768]{1,0:T(8,128)(2,1)S(1)}, bf16[256,768]{1,0:T(8,128)(2,1)S(1)}, bf16[256,768]{1,0:T(8,128)(2,1)S(1)}, bf16[256,768]{1,0:T(8,128)(2,1)S(1)}) custom-call(s32[4]{0:T(128)S(1)} %copy-done.4, bf16[4,256,384]{2,1,0:T(8,128)(2,1)S(1)} %attention_gradients.2.refs_0_.refs_6_, ...), custom_call_target="tpu_custom_call" | custom-call | flops 3623878656 | bytes 9830400 | tf_op jit(solution)/shard_map/input_gradient/pallas_call | solution.py:408
  72.4 1.5 %collective-permute-start.20 = (bf16[2,256,384]{2,1,0:T(8,128)(2,1)S(1)}, bf16[2,256,384]{2,1,0:T(8,128)(2,1)S(1)}, u32[]{:S(2)}, u32[]{:S(2)}) collective-permute-start(bf16[2,256,384]{2,1,0:T(8,128)(2,1)S(1)} %get-tuple-element.49), channel_id=1, source_target_pairs={{0,8},{4,20},{8,0},{12,28},{16,24},{20,4},{24,16},{28,12},{1,9},{5... | collective-permute-start | bytes 1179656 | tf_op jit(solution)/shard_map/ppermute | solution.py:128
  73.9 3.2 %collective-permute-start.21 = (bf16[2,256,384]{2,1,0:T(8,128)(2,1)S(1)}, bf16[2,256,384]{2,1,0:T(8,128)(2,1)S(1)}, u32[]{:S(2)}, u32[]{:S(2)}) collective-permute-start(bf16[2,256,384]{2,1,0:T(8,128)(2,1)S(1)} %get-tuple-element.50), channel_id=1, source_target_pairs={{0,20},{4,8},{8,28},{12,0},{16,4},{20,24},{24,12},{28,16},{1,21},{... | collective-permute-start | bytes 1179656 | tf_op jit(solution)/shard_map/ppermute | solution.py:128
  77.0 1.6 %collective-permute-start.17 = (bf16[256,768]{1,0:T(8,128)(2,1)S(1)}, bf16[256,768]{1,0:T(8,128)(2,1)S(1)}, u32[]{:S(2)}, u32[]{:S(2)}) collective-permute-start(bf16[256,768]{1,0:T(8,128)(2,1)S(1)} %get-tuple-element.46), channel_id=1, source_target_pairs={{0,1},{1,0},{2,3},{3,2},{4,5},{5,4},{6,7},{7,6},{8,9},{9,8},{10,11... | collective-permute-start | bytes 1179656 | tf_op jit(solution)/shard_map/ppermute | solution.py:555
  78.6 0.3 collective-permute-start.18
  78.9 1.6 %collective-permute-start.19 = (bf16[256,768]{1,0:T(8,128)(2,1)S(1)}, bf16[256,768]{1,0:T(8,128)(2,1)S(1)}, u32[]{:S(2)}, u32[]{:S(2)}) collective-permute-start(bf16[256,768]{1,0:T(8,128)(2,1)S(1)} %get-tuple-element.48), channel_id=1, source_target_pairs={{0,3},{1,2},{2,1},{3,0},{4,7},{5,6},{6,5},{7,4},{8,11},{9,10},{10,... | collective-permute-start | bytes 1179656 | tf_op jit(solution)/shard_map/ppermute | solution.py:555
  80.5 1.5 %collective-permute-done.20.refs_2_ = bf16[2,256,384]{2,1,0:T(8,128)(2,1)S(1)} collective-permute-done((bf16[2,256,384]{2,1,0:T(8,128)(2,1)S(1)}, bf16[2,256,384]{2,1,0:T(8,128)(2,1)S(1)}, u32[]{:S(2)}, u32[]{:S(2)}) %collective-permute-start.20) | collective-permute-done | bytes 393248 | tf_op jit(solution)/shard_map/ppermute | solution.py:128
  82.0 3.7 %collective-permute-done.21.refs_3_ = bf16[2,256,384]{2,1,0:T(8,128)(2,1)S(1)} collective-permute-done((bf16[2,256,384]{2,1,0:T(8,128)(2,1)S(1)}, bf16[2,256,384]{2,1,0:T(8,128)(2,1)S(1)}, u32[]{:S(2)}, u32[]{:S(2)}) %collective-permute-start.21) | collective-permute-done | bytes 393248 | tf_op jit(solution)/shard_map/ppermute | solution.py:128
  85.7 4.2 %collective-permute-start.23 = (bf16[2,256,384]{2,1,0:T(8,128)(2,1)S(1)}, bf16[2,256,384]{2,1,0:T(8,128)(2,1)S(1)}, u32[]{:S(2)}, u32[]{:S(2)}) collective-permute-start(bf16[2,256,384]{2,1,0:T(8,128)(2,1)S(1)} %get-tuple-element.51), channel_id=1, source_target_pairs={{0,28},{8,20},{16,12},{24,4},{1,29},{9,21},{17,13},{25,5},{2,30},{... | collective-permute-start | bytes 1179656 | tf_op jit(solution)/shard_map/ppermute | solution.py:128
  89.9 0.7 collective-permute-start.22
  90.6 3.6 %collective-permute-done.17 = bf16[256,768]{1,0:T(8,128)(2,1)S(1)} collective-permute-done((bf16[256,768]{1,0:T(8,128)(2,1)S(1)}, bf16[256,768]{1,0:T(8,128)(2,1)S(1)}, u32[]{:S(2)}, u32[]{:S(2)}) %collective-permute-start.17) | collective-permute-done | bytes 393248 | tf_op jit(solution)/shard_map/ppermute | solution.py:555
  94.1 11.2 %collective-permute-done.18 = bf16[256,768]{1,0:T(8,128)(2,1)S(1)} collective-permute-done((bf16[256,768]{1,0:T(8,128)(2,1)S(1)}, bf16[256,768]{1,0:T(8,128)(2,1)S(1)}, u32[]{:S(2)}, u32[]{:S(2)}) %collective-permute-start.18) | collective-permute-done | bytes 393248 | tf_op jit(solution)/shard_map/ppermute | solution.py:555
  105.3 9.1 %collective-permute-done.19 = bf16[256,768]{1,0:T(8,128)(2,1)S(1)} collective-permute-done((bf16[256,768]{1,0:T(8,128)(2,1)S(1)}, bf16[256,768]{1,0:T(8,128)(2,1)S(1)}, u32[]{:S(2)}, u32[]{:S(2)}) %collective-permute-start.19) | collective-permute-done | bytes 393248 | tf_op jit(solution)/shard_map/ppermute | solution.py:555
  114.4 0.2 add_convert_fusion
  114.6 2.5 %collective-permute-start.24 = (bf16[256,768]{1,0:T(8,128)(2,1)S(1)}, bf16[256,768]{1,0:T(8,128)(2,1)S(1)}, u32[]{:S(2)}, u32[]{:S(2)}) collective-permute-start(bf16[256,768]{1,0:T(8,128)(2,1)S(1)} %add_convert_fusion), channel_id=1, source_target_pairs={{0,0},{1,5},{2,10},{3,15},{4,20},{5,17},{6,30},{7,27},{8,8},{9,13}... | collective-permute-start | bytes 1179656 | tf_op jit(solution)/shard_map/ppermute | solution.py:580
  117.2 1.3 collective-permute-start.25
  118.5 6.8 %collective-permute-done.24 = bf16[256,768]{1,0:T(8,128)(2,1)S(1)} collective-permute-done((bf16[256,768]{1,0:T(8,128)(2,1)S(1)}, bf16[256,768]{1,0:T(8,128)(2,1)S(1)}, u32[]{:S(2)}, u32[]{:S(2)}) %collective-permute-start.24) | collective-permute-done | bytes 393248 | tf_op jit(solution)/shard_map/ppermute | solution.py:580
  125.2 3.8 %weight_gradient_mate.1 = bf16[3,384,768]{2,1,0:T(8,128)(2,1)S(1)} custom-call(s32[4]{0:T(128)S(1)} %copy-done.4, bf16[2,256,384]{2,1,0:T(8,128)(2,1)S(1)} %get-tuple-element.54.refs_0_, bf16[2,256,384]{2,1,0:T(8,128)(2,1)S(1)} %collective-permute-done.25.refs_1_, bf16[2,256,384]{2,1,0:T(8,128)(2,1)S(1)} %collective-permute-done.20.refs_2_, ...), custom_call_target="tpu_custom_call" | custom-call | flops 1811939328 | bytes 9043968 | tf_op jit(solution)/shard_map/weight_gradient_mate/pallas_call | solution.py:458
  129.0 0.6 collective-permute-start.27
  129.6 1.9 %collective-permute-start.26 = (bf16[256,768]{1,0:T(8,128)(2,1)S(1)}, bf16[256,768]{1,0:T(8,128)(2,1)S(1)}, u32[]{:S(2)}, u32[]{:S(2)}) collective-permute-start(bf16[256,768]{1,0:T(8,128)(2,1)S(1)} %collective-permute-done.24), channel_id=1, source_target_pairs={{0,0},{5,4},{10,8},{15,12},{20,20},{17,16},{30,28},{27,24},{8,9},{... | collective-permute-start | bytes 1179656 | tf_op jit(solution)/shard_map/ppermute | solution.py:590
  131.5 1.4 collective-permute-done.27.refs_18_
  132.9 5.7 %weight_gradient_own.1 = (f32[384,768]{1,0:T(8,128)}, f32[384,768]{1,0:T(8,128)}, f32[384,768]{1,0:T(8,128)}) custom-call(s32[4]{0:T(128)S(1)} %copy-done.4, bf16[2,256,384]{2,1,0:T(8,128)(2,1)S(1)} %get-tuple-element.54.refs_0_, bf16[2,256,384]{2,1,0:T(8,128)(2,1)S(1)} %collective-permute-done.25.refs_1_, ...), custom_call_target="tpu_custom_call" | custom-call | flops 1811939328 | bytes 9043968 | tf_op jit(solution)/shard_map/weight_gradient_own/pallas_call | solution.py:458
  138.6 4.8 %collective-permute-done.26 = bf16[256,768]{1,0:T(8,128)(2,1)S(1)} collective-permute-done((bf16[256,768]{1,0:T(8,128)(2,1)S(1)}, bf16[256,768]{1,0:T(8,128)(2,1)S(1)}, u32[]{:S(2)}, u32[]{:S(2)}) %collective-permute-start.26) | collective-permute-done | bytes 393248 | tf_op jit(solution)/shard_map/ppermute | solution.py:590
  143.4 0.7 copy.14
  (26 shorter events, 0.1 us)
Async XLA Ops:
  4.0 9.5 %collective-permute-start.1 = (bf16[1,1040,128]{2,1,0:T(8,128)(2,1)}, bf16[1,1040,128]{2,1,0:T(8,128)(2,1)S(1)}, u32[]{:S(2)}, u32[]{:S(2)}) collective-permute-start(bf16[1,1040,128]{2,1,0:T(8,128)(2,1)} %get-tuple-element.34), channel_id=1, source_target_pairs={{0,8},{4,12},{8,0},{12,4},{16,24},{20,28},{24,16},{28,20},{1,9},{5... | collective-permute-start | bytes 798728 | tf_op jit(solution)/shard_map/ppermute | solution.py:128
  5.5 9.5 %collective-permute-start = (bf16[1,1040,128]{2,1,0:T(8,128)(2,1)}, bf16[1,1040,128]{2,1,0:T(8,128)(2,1)S(1)}, u32[]{:S(2)}, u32[]{:S(2)}) collective-permute-start(bf16[1,1040,128]{2,1,0:T(8,128)(2,1)} %get-tuple-element.33), channel_id=1, source_target_pairs={{0,4},{4,0},{8,12},{12,8},{16,20},{20,16},{24,28},{28,24},{1,5},{5... | collective-permute-start | bytes 798728 | tf_op jit(solution)/shard_map/ppermute | solution.py:128
  5.5 12.8 %collective-permute-start.2 = (bf16[1,1040,128]{2,1,0:T(8,128)(2,1)}, bf16[1,1040,128]{2,1,0:T(8,128)(2,1)S(1)}, u32[]{:S(2)}, u32[]{:S(2)}) collective-permute-start(bf16[1,1040,128]{2,1,0:T(8,128)(2,1)} %get-tuple-element.35), channel_id=1, source_target_pairs={{0,12},{4,8},{8,4},{12,0},{16,28},{20,24},{24,20},{28,16},{1,13},{... | collective-permute-start | bytes 798728 | tf_op jit(solution)/shard_map/ppermute | solution.py:128
  6.1 23.2 %collective-permute-start.3 = (bf16[1,1040,128]{2,1,0:T(8,128)(2,1)}, bf16[1,1040,128]{2,1,0:T(8,128)(2,1)S(1)}, u32[]{:S(2)}, u32[]{:S(2)}) collective-permute-start(bf16[1,1040,128]{2,1,0:T(8,128)(2,1)} %get-tuple-element.40.own), channel_id=1, source_target_pairs={{0,4},{4,0},{8,12},{12,8},{16,20},{20,16},{24,28},{28,24},{1,5},{5... | collective-permute-start | bytes 798728 | tf_op jit(solution)/shard_map/ppermute | solution.py:128
  13.5 12.7 %collective-permute-start.4 = (bf16[1,1040,128]{2,1,0:T(8,128)(2,1)}, bf16[1,1040,128]{2,1,0:T(8,128)(2,1)}, u32[]{:S(2)}, u32[]{:S(2)}) collective-permute-start(bf16[1,1040,128]{2,1,0:T(8,128)(2,1)} %get-tuple-element.42), channel_id=1, source_target_pairs={{0,8},{4,12},{8,0},{12,4},{16,24},{20,28},{24,16},{28,20},{1,9},{5... | collective-permute-start | bytes 798728 | tf_op jit(solution)/shard_map/ppermute | solution.py:128
  18.3 0.6 copy-start.3
  18.9 1.0 copy-start.8
  19.8 4.5 %copy-start = (bf16[384,768]{1,0:T(8,128)(2,1)S(1)}, bf16[384,768]{1,0:T(8,128)(2,1)}, u32[]{:S(2)}) copy-start(bf16[384,768]{1,0:T(8,128)(2,1)} %q_ref) | copy-start | bytes 1769476
  19.8 4.5 %copy-start.1 = (bf16[384,768]{1,0:T(8,128)(2,1)S(1)}, bf16[384,768]{1,0:T(8,128)(2,1)}, u32[]{:S(2)}) copy-start(bf16[384,768]{1,0:T(8,128)(2,1)} %k_ref) | copy-start | bytes 1769476
  19.8 4.5 %copy-start.2 = (bf16[384,768]{1,0:T(8,128)(2,1)S(1)}, bf16[384,768]{1,0:T(8,128)(2,1)}, u32[]{:S(2)}) copy-start(bf16[384,768]{1,0:T(8,128)(2,1)} %v_ref) | copy-start | bytes 1769476
  24.3 7.0 %copy-start.4 = (s32[4]{0:T(128)S(1)}, s32[4]{0:T(128)}, u32[]{:S(2)}) copy-start(s32[4]{0:T(128)} %pad_add_fusion.place_ref) | copy-start | bytes 52
  25.4 33.5 %collective-permute-start.16 = (bf16[2304,384]{1,0:T(8,128)(2,1)S(1)}, bf16[2304,384]{1,0:T(8,128)(2,1)}, u32[]{:S(2)}, u32[]{:S(2)}) collective-permute-start(bf16[2304,384]{1,0:T(8,128)(2,1)S(1)} %turn_weights.1.own_ref), channel_id=1, source_target_pairs={{0,4},{4,0},{8,12},{12,8},{16,20},{20,16},{24,28},{28,24},{1,5},{5... | collective-permute-start | bytes 5308424 | tf_op jit(solution)/shard_map/ppermute | solution.py:128
  26.2 5.2 %collective-permute-start.5 = (bf16[1,1040,128]{2,1,0:T(8,128)(2,1)}, bf16[1,1040,128]{2,1,0:T(8,128)(2,1)}, u32[]{:S(2)}, u32[]{:S(2)}) collective-permute-start(bf16[1,1040,128]{2,1,0:T(8,128)(2,1)} %collective-permute-done.4.x_in), channel_id=1, source_target_pairs={{0,4},{4,0},{8,12},{12,8},{16,20},{20,16},{24,28},{28,24},{1,5},{5... | collective-permute-start | bytes 798728 | tf_op jit(solution)/shard_map/ppermute | solution.py:128
  26.3 18.9 %collective-permute-start.10 = (bf16[4,256,384]{2,1,0:T(8,128)(2,1)S(1)}, bf16[4,256,384]{2,1,0:T(8,128)(2,1)S(1)}, u32[]{:S(2)}, u32[]{:S(2)}) collective-permute-start(bf16[4,256,384]{2,1,0:T(8,128)(2,1)S(1)} %attention_gradients.2.refs_0_.refs_6_), channel_id=1, source_target_pairs={{0,20},{4,8},{8,28},{12,0},{16,4},{20,24},{24,12},{28,16},{1,21},{... | collective-permute-start | bytes 2359304 | tf_op jit(solution)/shard_map/ppermute | solution.py:128
  27.8 20.6 %collective-permute-start.8 = (bf16[4,256,384]{2,1,0:T(8,128)(2,1)S(1)}, bf16[4,256,384]{2,1,0:T(8,128)(2,1)}, u32[]{:S(2)}, u32[]{:S(2)}) collective-permute-start(bf16[4,256,384]{2,1,0:T(8,128)(2,1)S(1)} %attention_gradients.2.refs_0_.refs_6_), channel_id=1, source_target_pairs={{0,8},{4,20},{8,0},{12,28},{16,24},{20,4},{24,16},{28,12},{1,9},{5... | collective-permute-start | bytes 2359304 | tf_op jit(solution)/shard_map/ppermute | solution.py:128
  29.3 0.7 copy-start.6
  30.0 19.7 %collective-permute-start.6 = (bf16[4,256,384]{2,1,0:T(8,128)(2,1)S(1)}, bf16[4,256,384]{2,1,0:T(8,128)(2,1)}, u32[]{:S(2)}, u32[]{:S(2)}) collective-permute-start(bf16[4,256,384]{2,1,0:T(8,128)(2,1)S(1)} %attention_gradients.2.refs_0_.refs_6_), channel_id=1, source_target_pairs={{4,0},{12,8},{20,16},{28,24},{5,1},{13,9},{21,17},{29,25},{6,2},{1... | collective-permute-start | bytes 2359304 | tf_op jit(solution)/shard_map/ppermute | solution.py:128
  31.4 1.0 copy-start.5
  32.3 1.0 copy-start.7
  33.3 7.0 %copy-start.9 = (bf16[1,1,256,3072]{3,2,1,0:T(8,128)(2,1)S(1)}, bf16[1,1,256,3072]{3,2,1,0:T(8,128)(2,1)}, u32[]{:S(2)}) copy-start(bf16[1,1,256,3072]{3,2,1,0:T(8,128)(2,1)} %param.9) | copy-start | bytes 4718596
  38.2 14.7 %collective-permute-start.11 = (bf16[2,256,384]{2,1,0:T(8,128)(2,1)S(1)}, bf16[2,256,384]{2,1,0:T(8,128)(2,1)S(1)}, u32[]{:S(2)}, u32[]{:S(2)}) collective-permute-start(bf16[2,256,384]{2,1,0:T(8,128)(2,1)S(1)} %attention_gradients.3.refs_1_.refs_7_), channel_id=1, source_target_pairs={{0,20},{4,8},{8,28},{12,0},{16,4},{20,24},{24,12},{28,16},{1,21},{... | collective-permute-start | bytes 1179656 | tf_op jit(solution)/shard_map/ppermute | solution.py:128
  45.2 9.3 %collective-permute-start.9 = (bf16[2,256,384]{2,1,0:T(8,128)(2,1)S(1)}, bf16[2,256,384]{2,1,0:T(8,128)(2,1)S(1)}, u32[]{:S(2)}, u32[]{:S(2)}) collective-permute-start(bf16[2,256,384]{2,1,0:T(8,128)(2,1)S(1)} %attention_gradients.3.refs_1_.refs_7_), channel_id=1, source_target_pairs={{0,8},{4,20},{8,0},{12,28},{16,24},{20,4},{24,16},{28,12},{1,9},{5... | collective-permute-start | bytes 1179656 | tf_op jit(solution)/shard_map/ppermute | solution.py:128
  48.4 6.1 %collective-permute-start.7 = (bf16[2,256,384]{2,1,0:T(8,128)(2,1)S(1)}, bf16[2,256,384]{2,1,0:T(8,128)(2,1)S(1)}, u32[]{:S(2)}, u32[]{:S(2)}) collective-permute-start(bf16[2,256,384]{2,1,0:T(8,128)(2,1)S(1)} %attention_gradients.3.refs_1_.refs_7_), channel_id=1, source_target_pairs={{4,0},{12,8},{20,16},{28,24},{5,1},{13,9},{21,17},{29,25},{6,2},{1... | collective-permute-start | bytes 1179656 | tf_op jit(solution)/shard_map/ppermute | solution.py:128
  49.7 17.1 %collective-permute-start.14 = (bf16[4,256,384]{2,1,0:T(8,128)(2,1)}, bf16[4,256,384]{2,1,0:T(8,128)(2,1)S(1)}, u32[]{:S(2)}, u32[]{:S(2)}) collective-permute-start(bf16[4,256,384]{2,1,0:T(8,128)(2,1)} %collective-permute-done.8.refs_4_.refs_10_), channel_id=1, source_target_pairs={{0,20},{8,28},{16,4},{24,12},{1,21},{9,29},{17,5},{25,13},{2,22},{... | collective-permute-start | bytes 2359304 | tf_op jit(solution)/shard_map/ppermute | solution.py:128
  52.9 14.0 %collective-permute-start.12 = (bf16[4,256,384]{2,1,0:T(8,128)(2,1)}, bf16[4,256,384]{2,1,0:T(8,128)(2,1)S(1)}, u32[]{:S(2)}, u32[]{:S(2)}) collective-permute-start(bf16[4,256,384]{2,1,0:T(8,128)(2,1)} %collective-permute-done.8.refs_4_.refs_10_), channel_id=1, source_target_pairs={{4,12},{12,4},{20,28},{28,20},{5,13},{13,5},{21,29},{29,21},{6,14}... | collective-permute-start | bytes 2359304 | tf_op jit(solution)/shard_map/ppermute | solution.py:128
  54.5 12.3 %collective-permute-start.15 = (bf16[2,256,384]{2,1,0:T(8,128)(2,1)S(1)}, bf16[2,256,384]{2,1,0:T(8,128)(2,1)S(1)}, u32[]{:S(2)}, u32[]{:S(2)}) collective-permute-start(bf16[2,256,384]{2,1,0:T(8,128)(2,1)S(1)} %collective-permute-done.9.refs_5_.refs_11_), channel_id=1, source_target_pairs={{0,20},{8,28},{16,4},{24,12},{1,21},{9,29},{17,5},{25,13},{2,22},{... | collective-permute-start | bytes 1179656 | tf_op jit(solution)/shard_map/ppermute | solution.py:128
  58.2 8.6 %collective-permute-start.13 = (bf16[2,256,384]{2,1,0:T(8,128)(2,1)S(1)}, bf16[2,256,384]{2,1,0:T(8,128)(2,1)S(1)}, u32[]{:S(2)}, u32[]{:S(2)}) collective-permute-start(bf16[2,256,384]{2,1,0:T(8,128)(2,1)S(1)} %collective-permute-done.9.refs_5_.refs_11_), channel_id=1, source_target_pairs={{4,12},{12,4},{20,28},{28,20},{5,13},{13,5},{21,29},{29,21},{6,14}... | collective-permute-start | bytes 1179656 | tf_op jit(solution)/shard_map/ppermute | solution.py:128
  72.4 9.7 %collective-permute-start.20 = (bf16[2,256,384]{2,1,0:T(8,128)(2,1)S(1)}, bf16[2,256,384]{2,1,0:T(8,128)(2,1)S(1)}, u32[]{:S(2)}, u32[]{:S(2)}) collective-permute-start(bf16[2,256,384]{2,1,0:T(8,128)(2,1)S(1)} %get-tuple-element.49), channel_id=1, source_target_pairs={{0,8},{4,20},{8,0},{12,28},{16,24},{20,4},{24,16},{28,12},{1,9},{5... | collective-permute-start | bytes 1179656 | tf_op jit(solution)/shard_map/ppermute | solution.py:128
  73.9 11.9 %collective-permute-start.21 = (bf16[2,256,384]{2,1,0:T(8,128)(2,1)S(1)}, bf16[2,256,384]{2,1,0:T(8,128)(2,1)S(1)}, u32[]{:S(2)}, u32[]{:S(2)}) collective-permute-start(bf16[2,256,384]{2,1,0:T(8,128)(2,1)S(1)} %get-tuple-element.50), channel_id=1, source_target_pairs={{0,20},{4,8},{8,28},{12,0},{16,4},{20,24},{24,12},{28,16},{1,21},{... | collective-permute-start | bytes 1179656 | tf_op jit(solution)/shard_map/ppermute | solution.py:128
  77.0 17.1 %collective-permute-start.17 = (bf16[256,768]{1,0:T(8,128)(2,1)S(1)}, bf16[256,768]{1,0:T(8,128)(2,1)S(1)}, u32[]{:S(2)}, u32[]{:S(2)}) collective-permute-start(bf16[256,768]{1,0:T(8,128)(2,1)S(1)} %get-tuple-element.46), channel_id=1, source_target_pairs={{0,1},{1,0},{2,3},{3,2},{4,5},{5,4},{6,7},{7,6},{8,9},{9,8},{10,11... | collective-permute-start | bytes 1179656 | tf_op jit(solution)/shard_map/ppermute | solution.py:555
  78.6 26.7 %collective-permute-start.18 = (bf16[256,768]{1,0:T(8,128)(2,1)S(1)}, bf16[256,768]{1,0:T(8,128)(2,1)S(1)}, u32[]{:S(2)}, u32[]{:S(2)}) collective-permute-start(bf16[256,768]{1,0:T(8,128)(2,1)S(1)} %get-tuple-element.47), channel_id=1, source_target_pairs={{0,2},{1,3},{2,0},{3,1},{4,6},{5,7},{6,4},{7,5},{8,10},{9,11},{10,... | collective-permute-start | bytes 1179656 | tf_op jit(solution)/shard_map/ppermute | solution.py:555
  78.9 35.5 %collective-permute-start.19 = (bf16[256,768]{1,0:T(8,128)(2,1)S(1)}, bf16[256,768]{1,0:T(8,128)(2,1)S(1)}, u32[]{:S(2)}, u32[]{:S(2)}) collective-permute-start(bf16[256,768]{1,0:T(8,128)(2,1)S(1)} %get-tuple-element.48), channel_id=1, source_target_pairs={{0,3},{1,2},{2,1},{3,0},{4,7},{5,6},{6,5},{7,4},{8,11},{9,10},{10,... | collective-permute-start | bytes 1179656 | tf_op jit(solution)/shard_map/ppermute | solution.py:555
  85.7 28.9 %collective-permute-start.23 = (bf16[2,256,384]{2,1,0:T(8,128)(2,1)S(1)}, bf16[2,256,384]{2,1,0:T(8,128)(2,1)S(1)}, u32[]{:S(2)}, u32[]{:S(2)}) collective-permute-start(bf16[2,256,384]{2,1,0:T(8,128)(2,1)S(1)} %get-tuple-element.51), channel_id=1, source_target_pairs={{0,28},{8,20},{16,12},{24,4},{1,29},{9,21},{17,13},{25,5},{2,30},{... | collective-permute-start | bytes 1179656 | tf_op jit(solution)/shard_map/ppermute | solution.py:128
  89.9 24.8 %collective-permute-start.22 = (bf16[2,256,384]{2,1,0:T(8,128)(2,1)S(1)}, bf16[2,256,384]{2,1,0:T(8,128)(2,1)S(1)}, u32[]{:S(2)}, u32[]{:S(2)}) collective-permute-start(bf16[2,256,384]{2,1,0:T(8,128)(2,1)S(1)} %get-tuple-element.51), channel_id=1, source_target_pairs={{4,28},{12,20},{20,12},{28,4},{5,29},{13,21},{21,13},{29,5},{6,30}... | collective-permute-start | bytes 1179656 | tf_op jit(solution)/shard_map/ppermute | solution.py:128
  114.6 10.6 %collective-permute-start.24 = (bf16[256,768]{1,0:T(8,128)(2,1)S(1)}, bf16[256,768]{1,0:T(8,128)(2,1)S(1)}, u32[]{:S(2)}, u32[]{:S(2)}) collective-permute-start(bf16[256,768]{1,0:T(8,128)(2,1)S(1)} %add_convert_fusion), channel_id=1, source_target_pairs={{0,0},{1,5},{2,10},{3,15},{4,20},{5,17},{6,30},{7,27},{8,8},{9,13}... | collective-permute-start | bytes 1179656 | tf_op jit(solution)/shard_map/ppermute | solution.py:580
  117.2 8.1 %collective-permute-start.25 = (bf16[2,256,384]{2,1,0:T(8,128)(2,1)S(1)}, bf16[2,256,384]{2,1,0:T(8,128)(2,1)S(1)}, u32[]{:S(2)}, u32[]{:S(2)}) collective-permute-start(bf16[2,256,384]{2,1,0:T(8,128)(2,1)S(1)} %get-tuple-element.54.refs_0_), channel_id=1, source_target_pairs={{4,0},{12,8},{20,16},{28,24},{5,1},{13,9},{21,17},{29,25},{6,2},{1... | collective-permute-start | bytes 1179656 | tf_op jit(solution)/shard_map/ppermute | solution.py:128
  129.0 3.9 %collective-permute-start.27 = (bf16[3,384,768]{2,1,0:T(8,128)(2,1)S(1)}, bf16[3,384,768]{2,1,0:T(8,128)(2,1)S(1)}, u32[]{:S(2)}, u32[]{:S(2)}) collective-permute-start(bf16[3,384,768]{2,1,0:T(8,128)(2,1)S(1)} %weight_gradient_mate.1), channel_id=1, source_target_pairs={{0,4},{4,0},{8,12},{12,8},{16,20},{20,16},{24,28},{28,24},{1,5},{5... | collective-permute-start | bytes 5308424 | tf_op jit(solution)/shard_map/ppermute | solution.py:128
  129.6 13.8 %collective-permute-start.26 = (bf16[256,768]{1,0:T(8,128)(2,1)S(1)}, bf16[256,768]{1,0:T(8,128)(2,1)S(1)}, u32[]{:S(2)}, u32[]{:S(2)}) collective-permute-start(bf16[256,768]{1,0:T(8,128)(2,1)S(1)} %collective-permute-done.24), channel_id=1, source_target_pairs={{0,0},{5,4},{10,8},{15,12},{20,20},{17,16},{30,28},{27,24},{8,9},{... | collective-permute-start | bytes 1179656 | tf_op jit(solution)/shard_map/ppermute | solution.py:590

commit v13 on v11

--- a/solution.py
+++ b/solution.py
@@ -425,9 +425,9 @@
     own, mate_in, first, second, corner, corner_far = refs[:6]
     grad_refs, refs = refs[6 : 6 + 6 * parts], refs[6 + 6 * parts :]
     if mine:
-        received, out_refs, turned = refs[0], refs[1:4], refs[4]
+        received, out_refs, turned = refs[:3], refs[3:6], refs[6]
     else:
-        received, out_refs, turned = None, [refs[0].at[kind] for kind in range(3)], refs[1]
+        received, out_refs, turned = None, refs[:3], refs[3]
     core = place_ref[CORE]
     length = own.shape[1]
     part = core if mine else 1 - core
@@ -446,20 +446,19 @@
                         at = (head * 3 + kind) * HD
                         value = total[:, at : at + HD]
                         if mine:
-                            value = (value + received[kind, :, here]) * mean_scale
+                            value = (value + received[kind][:, here]) * mean_scale
                         out[:, here] = value.astype(out.dtype)
 
 
 def weight_product(place, mine, mean_scale, cols, tokens, grads, received=()):
     _, length, _ = grads[0].shape
     rows = tokens[0].shape[2]
-    out = jax.ShapeDtypeStruct((rows, cols), jnp.float32)
-    both = jax.ShapeDtypeStruct((3, rows, cols), jnp.bfloat16)
+    out = jax.ShapeDtypeStruct((rows, cols), jnp.float32 if mine else jnp.bfloat16)
     return pl.pallas_call(
         functools.partial(weight_kernel, mine, mean_scale, len(grads) // 6),
-        out_shape=[out] * 3 if mine else both,
+        out_shape=[out] * 3,
         in_specs=[whole(pltpu.SMEM)] + [whole()] * (6 + len(grads) + len(received)),
-        out_specs=[whole()] * 3 if mine else whole(),
+        out_specs=[whole()] * 3,
         scratch_shapes=[pltpu.VMEM((rows, 4 * length), jnp.bfloat16)],
         compiler_params=pltpu.CompilerParams(vmem_limit_bytes=16 * MIB),
         cost_estimate=pl.CostEstimate(
@@ -553,10 +552,13 @@
     weights = joined_weights(place, own_weights, moved(own_weights, mate))
 
     slots = input_product(place, grads, weights)
-    arrived = [
-        lax.ppermute(slots[s], "head", [(z, z ^ s) for z in range(groups)])
-        for s in range(1, groups)
-    ]
+    last = groups - 1
+    far = lax.ppermute(slots[3], "head", [(0, 1), (last, last - 1)])
+    nearest = lax.ppermute(slots[1], "head", [(z, z ^ 1) for z in range(groups)])
+    inner = lax.ppermute(slots[3], "head", [(1, last - 1), (last - 1, 1)])
+    joint = (slots[2].astype(jnp.float32) + far.astype(jnp.float32)).astype(jnp.bfloat16)
+    across = lax.ppermute(joint, "head", [(z, z ^ 2) for z in range(groups)])
+    arrived = [nearest, inner, across]
     total = sum(array.astype(jnp.float32) for array in (slots[0], *arrived))
     total = total.astype(jnp.bfloat16)
 
@@ -583,11 +585,10 @@
         ("dp", "view", "head"),
         [(spot(y, v, z), spot(y ^ (v % 2), v ^ z, z)) for y, v, z in corners],
     )
-    (turn,) = after((place,), beside)
+    (turn,) = after((place,), arrived[0])
     for_mate = weight_product(turn, False, mean_scale, cols, tokens, grads)
-    from_mate = moved(for_mate, mate)
-    weight_grads = weight_product(place, True, mean_scale, cols, tokens, grads, (from_mate,))
-    (beside,) = after((beside,), for_mate)
+    from_mate = [moved(part, mate) for part in for_mate]
+    weight_grads = weight_product(place, True, mean_scale, cols, tokens, grads, from_mate)
     input_grad = lax.ppermute(
         beside,
         ("dp", "view", "head"),

time: 143 us -> 131 us (0.916)
  the two profiles are of different devices: /device:TPU:16 before, /device:TPU:26 now
where the time goes in v13:
time: 131 us; the launch traced here: 130 us
  waiting for transfers between devices  56.6 us (43%)
  starting transfers between devices  43.9 us (34%)
  Pallas kernels  25.7 us (20%)
  local copies, waits for them, and re-layouts  1.98 us (2%)
    ppermute x25, waiting for transfers between devices, moved(): return lax.ppermute(value, ('dp', 'view'), pairs)  35 us
    ppermute x25, starting transfers between devices, moved(): return lax.ppermute(value, ('dp', 'view'), pairs)  31 us
    pallas_call x2, Pallas kernels, attention(): pl.pallas_call(functools.partial(attention_kernel, HD ** (-0.5), kept), o...  8.76 us
    ppermute x1, waiting for transfers between devices, gather_body(): lax.ppermute(beside, ('dp', 'view', 'head'), [(spot(y ^ v % 2, v ^ z, z),...  8.12 us
    pallas_call x2, Pallas kernels, weight_product(): pl.pallas_call(functools.partial(weight_kernel, mine, mean_scale, len(gra...  7.54 us
    ppermute x1, waiting for transfers between devices, gather_body(): lax.ppermute(total, ('dp', 'view', 'head'), [(spot(y, v, z), spot(y ^ v %...  5.76 us
    ppermute x1, waiting for transfers between devices, gather_body(): across = lax.ppermute(joint, 'head', [(z, z ^ 2) for z in range(groups)])  5.07 us
    pallas_call x1, Pallas kernels, input_product(): pl.pallas_call(functools.partial(input_kernel, len(grads) // 6), out_shap...  4.66 us
  transfers between devices with their start and end apart: 31, of which 13 were waited for; matrix products, arithmetic and copies ran while one was open for 1% of the time, Pallas kernels for 14%

profile of v13, /device:TPU:26, one launch (start us, length us, event | category | flops | bytes accessed | tf_op | source)
XLA Modules:
  0.0 130.3 jit_solution(7100537968350983877)
XLA Ops:
  0.7 0.7 pad_add_fusion.place_ref
  1.3 2.8 %pack_heads.1 = (bf16[1,1040,128]{2,1,0:T(8,128)(2,1)}, bf16[1,1040,128]{2,1,0:T(8,128)(2,1)}, bf16[1,1040,128]{2,1,0:T(8,128)(2,1)}, bf16[1,1040,128]{2,1,0:T(8...) custom-call(s32[4]{0:T(128)} %pad_add_fusion.place_ref, s32[1,2]{1,0:T(1,128)} %links_ref.1, ...), custom_call_target="tpu_custom_call" | custom-call | tf_op jit(solution)/shard_map/pack_heads/pallas_call | solution.py:215
  4.1 0.5 collective-permute-start.1
  4.7 0.0 collective-permute-start
  4.7 1.6 %collective-permute-start.2 = (bf16[1,1040,128]{2,1,0:T(8,128)(2,1)}, bf16[1,1040,128]{2,1,0:T(8,128)(2,1)S(1)}, u32[]{:S(2)}, u32[]{:S(2)}) collective-permute-start(bf16[1,1040,128]{2,1,0:T(8,128)(2,1)} %get-tuple-element.36), channel_id=1, source_target_pairs={{0,12},{4,8},{8,4},{12,0},{16,28},{20,24},{24,20},{28,16},{1,13},{... | collective-permute-start | bytes 798728 | tf_op jit(solution)/shard_map/ppermute | solution.py:128
  6.3 7.3 %collective-permute-done.1.x_in = bf16[1,1040,128]{2,1,0:T(8,128)(2,1)S(1)} collective-permute-done((bf16[1,1040,128]{2,1,0:T(8,128)(2,1)}, bf16[1,1040,128]{2,1,0:T(8,128)(2,1)S(1)}, u32[]{:S(2)}, u32[]{:S(2)}) %collective-permute-start.1) | collective-permute-done | bytes 266272 | tf_op jit(solution)/shard_map/ppermute | solution.py:128
  13.6 0.5 collective-permute-start.4
  14.2 3.3 %collective-permute-done.2.far_in = bf16[1,1040,128]{2,1,0:T(8,128)(2,1)S(1)} collective-permute-done((bf16[1,1040,128]{2,1,0:T(8,128)(2,1)}, bf16[1,1040,128]{2,1,0:T(8,128)(2,1)S(1)}, u32[]{:S(2)}, u32[]{:S(2)}) %collective-permute-start.2) | collective-permute-done | bytes 266272 | tf_op jit(solution)/shard_map/ppermute | solution.py:128
  17.5 0.9 copy-done.5
  18.4 4.4 %attention_gradients.2.refs_0_.refs_6_ = bf16[4,256,384]{2,1,0:T(8,128)(2,1)S(1)} custom-call(s32[4]{0:T(128)S(1)} %copy-done.3, bf16[1,1040,128]{2,1,0:T(8,128)(2,1)S(1)} %copy-done.5, bf16[1,1040,128]{2,1,0:T(8,128)(2,1)S(1)} %collective-permute-done.mate_in, bf16[1,1040,128]{2,1,0:T(8,128)(2,1)S(1)} %collective-permute-done.1.x_in, ...), custom_call_target="tpu_custom_call" | custom-call | flops 2013265920 | bytes 1835008 | tf_op jit(solution)/shard_map/attention_gradients/pallas_call | solution.py:304
  22.9 0.0 copy-start.6
  22.9 1.1 turn_weights.1.own_ref
  24.0 1.7 %collective-permute-start.17 = (bf16[2304,384]{1,0:T(8,128)(2,1)S(1)}, bf16[2304,384]{1,0:T(8,128)(2,1)S(1)}, u32[]{:S(2)}, u32[]{:S(2)}) collective-permute-start(bf16[2304,384]{1,0:T(8,128)(2,1)S(1)} %turn_weights.1.own_ref), channel_id=1, source_target_pairs={{0,4},{4,0},{8,12},{12,8},{16,20},{20,16},{24,28},{28,24},{1,5},{5... | collective-permute-start | bytes 5308424 | tf_op jit(solution)/shard_map/ppermute | solution.py:128
  25.7 0.0 collective-permute-done.4.x_in
  25.7 0.1 collective-permute-start.5
  25.8 0.3 dynamic-slice_bitcast_fusion.1
  26.1 1.6 %collective-permute-start.10 = (bf16[4,256,384]{2,1,0:T(8,128)(2,1)S(1)}, bf16[4,256,384]{2,1,0:T(8,128)(2,1)S(1)}, u32[]{:S(2)}, u32[]{:S(2)}) collective-permute-start(bf16[4,256,384]{2,1,0:T(8,128)(2,1)S(1)} %attention_gradients.2.refs_0_.refs_6_), channel_id=1, source_target_pairs={{0,20},{4,8},{8,28},{12,0},{16,4},{20,24},{24,12},{28,16},{1,21},{... | collective-permute-start | bytes 2359304 | tf_op jit(solution)/shard_map/ppermute | solution.py:128
  27.7 0.5 collective-permute-start.8
  28.2 1.3 collective-permute-start.6
  29.6 0.0 collective-permute-done.5.far_in
  29.6 1.3 collective-permute-start.12
  30.9 4.3 %attention_gradients.3.refs_1_.refs_7_ = bf16[2,256,384]{2,1,0:T(8,128)(2,1)S(1)} custom-call(s32[4]{0:T(128)S(1)} %copy-done.3, bf16[1,1040,128]{2,1,0:T(8,128)(2,1)S(1)} %copy-done.4, bf16[1,1040,128]{2,1,0:T(8,128)(2,1)S(1)} %collective-permute-done.3.mate_in, bf16[1,1040,128]{2,1,0:T(8,128)(2,1)S(1)} %collective-permute-done.4.x_in, ...), custom_call_target="tpu_custom_call" | custom-call | flops 2013265920 | bytes 1835008 | tf_op jit(solution)/shard_map/attention_gradients/pallas_call | solution.py:304
  35.2 0.0 collective-permute-done.12.refs_1_
  35.2 2.2 %collective-permute-start.11 = (bf16[2,256,384]{2,1,0:T(8,128)(2,1)S(1)}, bf16[2,256,384]{2,1,0:T(8,128)(2,1)S(1)}, u32[]{:S(2)}, u32[]{:S(2)}) collective-permute-start(bf16[2,256,384]{2,1,0:T(8,128)(2,1)S(1)} %attention_gradients.3.refs_1_.refs_7_), channel_id=1, source_target_pairs={{0,20},{4,8},{8,28},{12,0},{16,4},{20,24},{24,12},{28,16},{1,21},{... | collective-permute-start | bytes 1179656 | tf_op jit(solution)/shard_map/ppermute | solution.py:128
  37.4 0.1 pad_maximum_fusion.1
  37.5 7.7 %collective-permute-done.10.refs_6_.refs_12_ = bf16[4,256,384]{2,1,0:T(8,128)(2,1)S(1)} collective-permute-done((bf16[4,256,384]{2,1,0:T(8,128)(2,1)S(1)}, bf16[4,256,384]{2,1,0:T(8,128)(2,1)S(1)}, u32[]{:S(2)}, u32[]{:S(2)}) %collective-permute-start.10) | collective-permute-done | bytes 786464 | tf_op jit(solution)/shard_map/ppermute | solution.py:128
  45.2 0.3 collective-permute-start.9
  45.6 2.6 %collective-permute-done.8.refs_4_.refs_10_ = bf16[4,256,384]{2,1,0:T(8,128)(2,1)S(1)} collective-permute-done((bf16[4,256,384]{2,1,0:T(8,128)(2,1)S(1)}, bf16[4,256,384]{2,1,0:T(8,128)(2,1)S(1)}, u32[]{:S(2)}, u32[]{:S(2)}) %collective-permute-start.8) | collective-permute-done | bytes 786464 | tf_op jit(solution)/shard_map/ppermute | solution.py:128
  48.1 1.3 collective-permute-start.7
  49.4 3.2 %collective-permute-start.15 = (bf16[4,256,384]{2,1,0:T(8,128)(2,1)S(1)}, bf16[4,256,384]{2,1,0:T(8,128)(2,1)S(1)}, u32[]{:S(2)}, u32[]{:S(2)}) collective-permute-start(bf16[4,256,384]{2,1,0:T(8,128)(2,1)S(1)} %collective-permute-done.8.refs_4_.refs_10_), channel_id=1, source_target_pairs={{0,20},{8,28},{16,4},{24,12},{1,21},{9,29},{17,5},{25,13},{2,22},{... | collective-permute-start | bytes 2359304 | tf_op jit(solution)/shard_map/ppermute | solution.py:128
  52.6 0.0 collective-permute-done.11.refs_7_.refs_13_
  52.6 0.7 collective-permute-start.13
  53.3 1.1 collective-permute-done.9.refs_5_.refs_11_
  54.4 0.0 collective-permute-done.7.refs_3_.refs_9_
  54.4 3.7 %collective-permute-start.16 = (bf16[2,256,384]{2,1,0:T(8,128)(2,1)S(1)}, bf16[2,256,384]{2,1,0:T(8,128)(2,1)S(1)}, u32[]{:S(2)}, u32[]{:S(2)}) collective-permute-start(bf16[2,256,384]{2,1,0:T(8,128)(2,1)S(1)} %collective-permute-done.9.refs_5_.refs_11_), channel_id=1, source_target_pairs={{0,20},{8,28},{16,4},{24,12},{1,21},{9,29},{17,5},{25,13},{2,22},{... | collective-permute-start | bytes 1179656 | tf_op jit(solution)/shard_map/ppermute | solution.py:128
  58.1 0.7 collective-permute-start.14
  58.8 0.9 join_weights.1.refs_12_
  59.7 6.6 %collective-permute-done.16.refs_11_.refs_17_ = bf16[2,256,384]{2,1,0:T(8,128)(2,1)S(1)} collective-permute-done((bf16[2,256,384]{2,1,0:T(8,128)(2,1)S(1)}, bf16[2,256,384]{2,1,0:T(8,128)(2,1)S(1)}, u32[]{:S(2)}, u32[]{:S(2)}) %collective-permute-start.16) | collective-permute-done | bytes 393248 | tf_op jit(solution)/shard_map/ppermute | solution.py:128
  66.3 4.7 %input_gradient.1 = (bf16[256,768]{1,0:T(8,128)(2,1)S(1)}, bf16[256,768]{1,0:T(8,128)(2,1)S(1)}, bf16[256,768]{1,0:T(8,128)(2,1)S(1)}, bf16[256,768]{1,0:T(8,128)(2,1)S(1)}) custom-call(s32[4]{0:T(128)S(1)} %copy-done.3, bf16[4,256,384]{2,1,0:T(8,128)(2,1)S(1)} %attention_gradients.2.refs_0_.refs_6_, ...), custom_call_target="tpu_custom_call" | custom-call | flops 3623878656 | bytes 9830400 | tf_op jit(solution)/shard_map/input_gradient/pallas_call | solution.py:408
  71.0 2.4 %collective-permute-start.20 = (bf16[256,768]{1,0:T(8,128)(2,1)S(1)}, bf16[256,768]{1,0:T(8,128)(2,1)S(1)}, u32[]{:S(2)}, u32[]{:S(2)}) collective-permute-start(bf16[256,768]{1,0:T(8,128)(2,1)S(1)} %get-tuple-element.48), channel_id=1, source_target_pairs={{0,1},{3,2},{4,5},{7,6},{8,9},{11,10},{12,13},{15,14},{16,17},{19,... | collective-permute-start | bytes 1179656 | tf_op jit(solution)/shard_map/ppermute | solution.py:556
  73.4 0.7 collective-permute-start.19
  74.1 1.1 collective-permute-start.18
  75.2 0.9 collective-permute-start.22
  76.1 2.5 %collective-permute-start.23 = (bf16[2,256,384]{2,1,0:T(8,128)(2,1)S(1)}, bf16[2,256,384]{2,1,0:T(8,128)(2,1)S(1)}, u32[]{:S(2)}, u32[]{:S(2)}) collective-permute-start(bf16[2,256,384]{2,1,0:T(8,128)(2,1)S(1)} %get-tuple-element.51), channel_id=1, source_target_pairs={{0,20},{4,8},{8,28},{12,0},{16,4},{20,24},{24,12},{28,16},{1,21},{... | collective-permute-start | bytes 1179656 | tf_op jit(solution)/shard_map/ppermute | solution.py:128
  78.6 2.6 %collective-permute-done.20 = bf16[256,768]{1,0:T(8,128)(2,1)S(1)} collective-permute-done((bf16[256,768]{1,0:T(8,128)(2,1)S(1)}, bf16[256,768]{1,0:T(8,128)(2,1)S(1)}, u32[]{:S(2)}, u32[]{:S(2)}) %collective-permute-start.20) | collective-permute-done | bytes 393248 | tf_op jit(solution)/shard_map/ppermute | solution.py:556
  81.2 0.1 add_convert_fusion.1
  81.3 2.4 %collective-permute-start.21 = (bf16[256,768]{1,0:T(8,128)(2,1)S(1)}, bf16[256,768]{1,0:T(8,128)(2,1)S(1)}, u32[]{:S(2)}, u32[]{:S(2)}) collective-permute-start(bf16[256,768]{1,0:T(8,128)(2,1)S(1)} %add_convert_fusion.1), channel_id=1, source_target_pairs={{0,2},{1,3},{2,0},{3,1},{4,6},{5,7},{6,4},{7,5},{8,10},{9,11},{10,... | collective-permute-start | bytes 1179656 | tf_op jit(solution)/shard_map/ppermute | solution.py:560
  83.7 1.4 %collective-permute-done.22.refs_2_ = bf16[2,256,384]{2,1,0:T(8,128)(2,1)S(1)} collective-permute-done((bf16[2,256,384]{2,1,0:T(8,128)(2,1)S(1)}, bf16[2,256,384]{2,1,0:T(8,128)(2,1)S(1)}, u32[]{:S(2)}, u32[]{:S(2)}) %collective-permute-start.22) | collective-permute-done | bytes 393248 | tf_op jit(solution)/shard_map/ppermute | solution.py:128
  85.1 2.2 %collective-permute-done.23.refs_3_ = bf16[2,256,384]{2,1,0:T(8,128)(2,1)S(1)} collective-permute-done((bf16[2,256,384]{2,1,0:T(8,128)(2,1)S(1)}, bf16[2,256,384]{2,1,0:T(8,128)(2,1)S(1)}, u32[]{:S(2)}, u32[]{:S(2)}) %collective-permute-start.23) | collective-permute-done | bytes 393248 | tf_op jit(solution)/shard_map/ppermute | solution.py:128
  87.3 5.0 %collective-permute-start.25 = (bf16[2,256,384]{2,1,0:T(8,128)(2,1)S(1)}, bf16[2,256,384]{2,1,0:T(8,128)(2,1)S(1)}, u32[]{:S(2)}, u32[]{:S(2)}) collective-permute-start(bf16[2,256,384]{2,1,0:T(8,128)(2,1)S(1)} %pad_maximum_fusion.3), channel_id=1, source_target_pairs={{0,28},{8,20},{16,12},{24,4},{1,29},{9,21},{17,13},{25,5},{2,30},{... | collective-permute-start | bytes 1179656 | tf_op jit(solution)/shard_map/ppermute | solution.py:128
  92.3 0.7 collective-permute-start.24
  93.0 5.1 %collective-permute-done.21 = bf16[256,768]{1,0:T(8,128)(2,1)S(1)} collective-permute-done((bf16[256,768]{1,0:T(8,128)(2,1)S(1)}, bf16[256,768]{1,0:T(8,128)(2,1)S(1)}, u32[]{:S(2)}, u32[]{:S(2)}) %collective-permute-start.21) | collective-permute-done | bytes 393248 | tf_op jit(solution)/shard_map/ppermute | solution.py:560
  98.1 0.2 add_convert_fusion
  98.3 2.8 %collective-permute-done.25.refs_5_ = bf16[2,256,384]{2,1,0:T(8,128)(2,1)S(1)} collective-permute-done((bf16[2,256,384]{2,1,0:T(8,128)(2,1)S(1)}, bf16[2,256,384]{2,1,0:T(8,128)(2,1)S(1)}, u32[]{:S(2)}, u32[]{:S(2)}) %collective-permute-start.25) | collective-permute-done | bytes 393248 | tf_op jit(solution)/shard_map/ppermute | solution.py:128
  101.1 4.4 %collective-permute-start.26 = (bf16[256,768]{1,0:T(8,128)(2,1)S(1)}, bf16[256,768]{1,0:T(8,128)(2,1)S(1)}, u32[]{:S(2)}, u32[]{:S(2)}) collective-permute-start(bf16[256,768]{1,0:T(8,128)(2,1)S(1)} %add_convert_fusion), channel_id=1, source_target_pairs={{0,0},{1,5},{2,10},{3,15},{4,20},{5,17},{6,30},{7,27},{8,8},{9,13}... | collective-permute-start | bytes 1179656 | tf_op jit(solution)/shard_map/ppermute | solution.py:583
  105.5 2.8 %weight_gradient_mate.1 = (bf16[384,768]{1,0:T(8,128)(2,1)S(1)}, bf16[384,768]{1,0:T(8,128)(2,1)S(1)}, bf16[384,768]{1,0:T(8,128)(2,1)S(1)}) custom-call(s32[4]{0:T(128)S(1)} %copy-done.3, bf16[2,256,384]{2,1,0:T(8,128)(2,1)S(1)} %pad_maximum_fusion.refs_0_, bf16[2,256,384]{2,1,0:T(8,128)(2,1)S(1)} %collective-permute-done.12.refs_1_, ...), custom_call_target="tpu_custom_call" | custom-call | flops 1811939328 | bytes 9043968 | tf_op jit(solution)/shard_map/weight_gradient_mate/pallas_call | solution.py:457
  108.4 0.1 collective-permute-start.28
  108.4 0.5 collective-permute-start.29
  108.9 0.1 collective-permute-start.30
  109.0 5.8 %collective-permute-done.26 = bf16[256,768]{1,0:T(8,128)(2,1)S(1)} collective-permute-done((bf16[256,768]{1,0:T(8,128)(2,1)S(1)}, bf16[256,768]{1,0:T(8,128)(2,1)S(1)}, u32[]{:S(2)}, u32[]{:S(2)}) %collective-permute-start.26) | collective-permute-done | bytes 393248 | tf_op jit(solution)/shard_map/ppermute | solution.py:583
  114.8 1.9 %collective-permute-start.27 = (bf16[256,768]{1,0:T(8,128)(2,1)S(1)}, bf16[256,768]{1,0:T(8,128)(2,1)S(1)}, u32[]{:S(2)}, u32[]{:S(2)}) collective-permute-start(bf16[256,768]{1,0:T(8,128)(2,1)S(1)} %collective-permute-done.26), channel_id=1, source_target_pairs={{0,0},{5,4},{10,8},{15,12},{20,20},{17,16},{30,28},{27,24},{8,9},{... | collective-permute-start | bytes 1179656 | tf_op jit(solution)/shard_map/ppermute | solution.py:592
  116.7 4.7 %weight_gradient_own.1 = (f32[384,768]{1,0:T(8,128)}, f32[384,768]{1,0:T(8,128)}, f32[384,768]{1,0:T(8,128)}) custom-call(s32[4]{0:T(128)S(1)} %copy-done.3, bf16[2,256,384]{2,1,0:T(8,128)(2,1)S(1)} %pad_maximum_fusion.refs_0_, bf16[2,256,384]{2,1,0:T(8,128)(2,1)S(1)} %collective-permute-done.12.refs_1_, ...), custom_call_target="tpu_custom_call" | custom-call | flops 1811939328 | bytes 9043968 | tf_op jit(solution)/shard_map/weight_gradient_own/pallas_call | solution.py:457
  121.4 8.1 %collective-permute-done.27 = bf16[256,768]{1,0:T(8,128)(2,1)S(1)} collective-permute-done((bf16[256,768]{1,0:T(8,128)(2,1)S(1)}, bf16[256,768]{1,0:T(8,128)(2,1)S(1)}, u32[]{:S(2)}, u32[]{:S(2)}) %collective-permute-start.27) | collective-permute-done | bytes 393248 | tf_op jit(solution)/shard_map/ppermute | solution.py:592
  129.5 0.7 copy.14
  (28 shorter events, 0.2 us)
Async XLA Ops:
  1.3 16.2 %copy-start.3 = (s32[4]{0:T(128)S(1)}, s32[4]{0:T(128)}, u32[]{:S(2)}) copy-start(s32[4]{0:T(128)} %pad_add_fusion.place_ref) | copy-start | bytes 52
  4.1 9.5 %collective-permute-start.1 = (bf16[1,1040,128]{2,1,0:T(8,128)(2,1)}, bf16[1,1040,128]{2,1,0:T(8,128)(2,1)S(1)}, u32[]{:S(2)}, u32[]{:S(2)}) collective-permute-start(bf16[1,1040,128]{2,1,0:T(8,128)(2,1)} %get-tuple-element.35), channel_id=1, source_target_pairs={{0,8},{4,12},{8,0},{12,4},{16,24},{20,28},{24,16},{28,20},{1,9},{5... | collective-permute-start | bytes 798728 | tf_op jit(solution)/shard_map/ppermute | solution.py:128
  4.7 9.5 %collective-permute-start = (bf16[1,1040,128]{2,1,0:T(8,128)(2,1)}, bf16[1,1040,128]{2,1,0:T(8,128)(2,1)S(1)}, u32[]{:S(2)}, u32[]{:S(2)}) collective-permute-start(bf16[1,1040,128]{2,1,0:T(8,128)(2,1)} %get-tuple-element.34), channel_id=1, source_target_pairs={{0,4},{4,0},{8,12},{12,8},{16,20},{20,16},{24,28},{28,24},{1,5},{5... | collective-permute-start | bytes 798728 | tf_op jit(solution)/shard_map/ppermute | solution.py:128
  4.7 12.8 %collective-permute-start.2 = (bf16[1,1040,128]{2,1,0:T(8,128)(2,1)}, bf16[1,1040,128]{2,1,0:T(8,128)(2,1)S(1)}, u32[]{:S(2)}, u32[]{:S(2)}) collective-permute-start(bf16[1,1040,128]{2,1,0:T(8,128)(2,1)} %get-tuple-element.36), channel_id=1, source_target_pairs={{0,12},{4,8},{8,4},{12,0},{16,28},{20,24},{24,20},{28,16},{1,13},{... | collective-permute-start | bytes 798728 | tf_op jit(solution)/shard_map/ppermute | solution.py:128
  13.6 12.1 %collective-permute-start.4 = (bf16[1,1040,128]{2,1,0:T(8,128)(2,1)}, bf16[1,1040,128]{2,1,0:T(8,128)(2,1)S(1)}, u32[]{:S(2)}, u32[]{:S(2)}) collective-permute-start(bf16[1,1040,128]{2,1,0:T(8,128)(2,1)} %get-tuple-element.43), channel_id=1, source_target_pairs={{0,8},{4,12},{8,0},{12,4},{16,24},{20,28},{24,16},{28,20},{1,9},{5... | collective-permute-start | bytes 798728 | tf_op jit(solution)/shard_map/ppermute | solution.py:128
  14.2 14.1 %collective-permute-start.3 = (bf16[1,1040,128]{2,1,0:T(8,128)(2,1)}, bf16[1,1040,128]{2,1,0:T(8,128)(2,1)S(1)}, u32[]{:S(2)}, u32[]{:S(2)}) collective-permute-start(bf16[1,1040,128]{2,1,0:T(8,128)(2,1)} %get-tuple-element.41.own), channel_id=1, source_target_pairs={{0,4},{4,0},{8,12},{12,8},{16,20},{20,16},{24,28},{28,24},{1,5},{5... | collective-permute-start | bytes 798728 | tf_op jit(solution)/shard_map/ppermute | solution.py:128
  17.5 1.0 copy-start.5
  18.4 4.5 %copy-start = (bf16[384,768]{1,0:T(8,128)(2,1)S(1)}, bf16[384,768]{1,0:T(8,128)(2,1)}, u32[]{:S(2)}) copy-start(bf16[384,768]{1,0:T(8,128)(2,1)} %q_ref) | copy-start | bytes 1769476
  18.4 4.5 %copy-start.1 = (bf16[384,768]{1,0:T(8,128)(2,1)S(1)}, bf16[384,768]{1,0:T(8,128)(2,1)}, u32[]{:S(2)}) copy-start(bf16[384,768]{1,0:T(8,128)(2,1)} %k_ref) | copy-start | bytes 1769476
  18.4 4.5 %copy-start.2 = (bf16[384,768]{1,0:T(8,128)(2,1)S(1)}, bf16[384,768]{1,0:T(8,128)(2,1)}, u32[]{:S(2)}) copy-start(bf16[384,768]{1,0:T(8,128)(2,1)} %v_ref) | copy-start | bytes 1769476
  22.9 2.9 %copy-start.6 = (bf16[1,1,256,3072]{3,2,1,0:T(8,128)(2,1)S(1)}, bf16[1,1,256,3072]{3,2,1,0:T(8,128)(2,1)}, u32[]{:S(2)}) copy-start(bf16[1,1,256,3072]{3,2,1,0:T(8,128)(2,1)} %param.9) | copy-start | bytes 4718596
  24.0 6.9 %copy-start.4 = (bf16[1,1040,128]{2,1,0:T(8,128)(2,1)S(1)}, bf16[1,1040,128]{2,1,0:T(8,128)(2,1)}, u32[]{:S(2)}) copy-start(bf16[1,1040,128]{2,1,0:T(8,128)(2,1)} %get-tuple-element.41.own) | copy-start | bytes 798724
  24.0 34.8 %collective-permute-start.17 = (bf16[2304,384]{1,0:T(8,128)(2,1)S(1)}, bf16[2304,384]{1,0:T(8,128)(2,1)S(1)}, u32[]{:S(2)}, u32[]{:S(2)}) collective-permute-start(bf16[2304,384]{1,0:T(8,128)(2,1)S(1)} %turn_weights.1.own_ref), channel_id=1, source_target_pairs={{0,4},{4,0},{8,12},{12,8},{16,20},{20,16},{24,28},{28,24},{1,5},{5... | collective-permute-start | bytes 5308424 | tf_op jit(solution)/shard_map/ppermute | solution.py:128
  25.7 3.8 %collective-permute-start.5 = (bf16[1,1040,128]{2,1,0:T(8,128)(2,1)S(1)}, bf16[1,1040,128]{2,1,0:T(8,128)(2,1)S(1)}, u32[]{:S(2)}, u32[]{:S(2)}) collective-permute-start(bf16[1,1040,128]{2,1,0:T(8,128)(2,1)S(1)} %collective-permute-done.4.x_in), channel_id=1, source_target_pairs={{0,4},{4,0},{8,12},{12,8},{16,20},{20,16},{24,28},{28,24},{1,5},{5... | collective-permute-start | bytes 798728 | tf_op jit(solution)/shard_map/ppermute | solution.py:128
  26.1 19.2 %collective-permute-start.10 = (bf16[4,256,384]{2,1,0:T(8,128)(2,1)S(1)}, bf16[4,256,384]{2,1,0:T(8,128)(2,1)S(1)}, u32[]{:S(2)}, u32[]{:S(2)}) collective-permute-start(bf16[4,256,384]{2,1,0:T(8,128)(2,1)S(1)} %attention_gradients.2.refs_0_.refs_6_), channel_id=1, source_target_pairs={{0,20},{4,8},{8,28},{12,0},{16,4},{20,24},{24,12},{28,16},{1,21},{... | collective-permute-start | bytes 2359304 | tf_op jit(solution)/shard_map/ppermute | solution.py:128
  27.7 20.5 %collective-permute-start.8 = (bf16[4,256,384]{2,1,0:T(8,128)(2,1)S(1)}, bf16[4,256,384]{2,1,0:T(8,128)(2,1)S(1)}, u32[]{:S(2)}, u32[]{:S(2)}) collective-permute-start(bf16[4,256,384]{2,1,0:T(8,128)(2,1)S(1)} %attention_gradients.2.refs_0_.refs_6_), channel_id=1, source_target_pairs={{0,8},{4,20},{8,0},{12,28},{16,24},{20,4},{24,16},{28,12},{1,9},{5... | collective-permute-start | bytes 2359304 | tf_op jit(solution)/shard_map/ppermute | solution.py:128
  28.2 21.2 %collective-permute-start.6 = (bf16[4,256,384]{2,1,0:T(8,128)(2,1)S(1)}, bf16[4,256,384]{2,1,0:T(8,128)(2,1)S(1)}, u32[]{:S(2)}, u32[]{:S(2)}) collective-permute-start(bf16[4,256,384]{2,1,0:T(8,128)(2,1)S(1)} %attention_gradients.2.refs_0_.refs_6_), channel_id=1, source_target_pairs={{4,0},{12,8},{20,16},{28,24},{5,1},{13,9},{21,17},{29,25},{6,2},{1... | collective-permute-start | bytes 2359304 | tf_op jit(solution)/shard_map/ppermute | solution.py:128
  29.6 5.6 %collective-permute-start.12 = (bf16[2,256,384]{2,1,0:T(8,128)(2,1)S(1)}, bf16[2,256,384]{2,1,0:T(8,128)(2,1)S(1)}, u32[]{:S(2)}, u32[]{:S(2)}) collective-permute-start(bf16[2,256,384]{2,1,0:T(8,128)(2,1)S(1)} %pad_maximum_fusion.refs_0_), channel_id=1, source_target_pairs={{4,0},{12,8},{20,16},{28,24},{5,1},{13,9},{21,17},{29,25},{6,2},{1... | collective-permute-start | bytes 1179656 | tf_op jit(solution)/shard_map/ppermute | solution.py:128
  35.2 17.4 %collective-permute-start.11 = (bf16[2,256,384]{2,1,0:T(8,128)(2,1)S(1)}, bf16[2,256,384]{2,1,0:T(8,128)(2,1)S(1)}, u32[]{:S(2)}, u32[]{:S(2)}) collective-permute-start(bf16[2,256,384]{2,1,0:T(8,128)(2,1)S(1)} %attention_gradients.3.refs_1_.refs_7_), channel_id=1, source_target_pairs={{0,20},{4,8},{8,28},{12,0},{16,4},{20,24},{24,12},{28,16},{1,21},{... | collective-permute-start | bytes 1179656 | tf_op jit(solution)/shard_map/ppermute | solution.py:128
  45.2 9.2 %collective-permute-start.9 = (bf16[2,256,384]{2,1,0:T(8,128)(2,1)S(1)}, bf16[2,256,384]{2,1,0:T(8,128)(2,1)S(1)}, u32[]{:S(2)}, u32[]{:S(2)}) collective-permute-start(bf16[2,256,384]{2,1,0:T(8,128)(2,1)S(1)} %attention_gradients.3.refs_1_.refs_7_), channel_id=1, source_target_pairs={{0,8},{4,20},{8,0},{12,28},{16,24},{20,4},{24,16},{28,12},{1,9},{5... | collective-permute-start | bytes 1179656 | tf_op jit(solution)/shard_map/ppermute | solution.py:128
  48.1 6.3 %collective-permute-start.7 = (bf16[2,256,384]{2,1,0:T(8,128)(2,1)S(1)}, bf16[2,256,384]{2,1,0:T(8,128)(2,1)S(1)}, u32[]{:S(2)}, u32[]{:S(2)}) collective-permute-start(bf16[2,256,384]{2,1,0:T(8,128)(2,1)S(1)} %attention_gradients.3.refs_1_.refs_7_), channel_id=1, source_target_pairs={{4,0},{12,8},{20,16},{28,24},{5,1},{13,9},{21,17},{29,25},{6,2},{1... | collective-permute-start | bytes 1179656 | tf_op jit(solution)/shard_map/ppermute | solution.py:128
  49.4 16.9 %collective-permute-start.15 = (bf16[4,256,384]{2,1,0:T(8,128)(2,1)S(1)}, bf16[4,256,384]{2,1,0:T(8,128)(2,1)S(1)}, u32[]{:S(2)}, u32[]{:S(2)}) collective-permute-start(bf16[4,256,384]{2,1,0:T(8,128)(2,1)S(1)} %collective-permute-done.8.refs_4_.refs_10_), channel_id=1, source_target_pairs={{0,20},{8,28},{16,4},{24,12},{1,21},{9,29},{17,5},{25,13},{2,22},{... | collective-permute-start | bytes 2359304 | tf_op jit(solution)/shard_map/ppermute | solution.py:128
  52.6 13.7 %collective-permute-start.13 = (bf16[4,256,384]{2,1,0:T(8,128)(2,1)S(1)}, bf16[4,256,384]{2,1,0:T(8,128)(2,1)S(1)}, u32[]{:S(2)}, u32[]{:S(2)}) collective-permute-start(bf16[4,256,384]{2,1,0:T(8,128)(2,1)S(1)} %collective-permute-done.8.refs_4_.refs_10_), channel_id=1, source_target_pairs={{4,12},{12,4},{20,28},{28,20},{5,13},{13,5},{21,29},{29,21},{6,14}... | collective-permute-start | bytes 2359304 | tf_op jit(solution)/shard_map/ppermute | solution.py:128
  54.4 11.9 %collective-permute-start.16 = (bf16[2,256,384]{2,1,0:T(8,128)(2,1)S(1)}, bf16[2,256,384]{2,1,0:T(8,128)(2,1)S(1)}, u32[]{:S(2)}, u32[]{:S(2)}) collective-permute-start(bf16[2,256,384]{2,1,0:T(8,128)(2,1)S(1)} %collective-permute-done.9.refs_5_.refs_11_), channel_id=1, source_target_pairs={{0,20},{8,28},{16,4},{24,12},{1,21},{9,29},{17,5},{25,13},{2,22},{... | collective-permute-start | bytes 1179656 | tf_op jit(solution)/shard_map/ppermute | solution.py:128
  58.1 8.2 %collective-permute-start.14 = (bf16[2,256,384]{2,1,0:T(8,128)(2,1)S(1)}, bf16[2,256,384]{2,1,0:T(8,128)(2,1)S(1)}, u32[]{:S(2)}, u32[]{:S(2)}) collective-permute-start(bf16[2,256,384]{2,1,0:T(8,128)(2,1)S(1)} %collective-permute-done.9.refs_5_.refs_11_), channel_id=1, source_target_pairs={{4,12},{12,4},{20,28},{28,20},{5,13},{13,5},{21,29},{29,21},{6,14}... | collective-permute-start | bytes 1179656 | tf_op jit(solution)/shard_map/ppermute | solution.py:128
  71.0 10.2 %collective-permute-start.20 = (bf16[256,768]{1,0:T(8,128)(2,1)S(1)}, bf16[256,768]{1,0:T(8,128)(2,1)S(1)}, u32[]{:S(2)}, u32[]{:S(2)}) collective-permute-start(bf16[256,768]{1,0:T(8,128)(2,1)S(1)} %get-tuple-element.48), channel_id=1, source_target_pairs={{0,1},{3,2},{4,5},{7,6},{8,9},{11,10},{12,13},{15,14},{16,17},{19,... | collective-permute-start | bytes 1179656 | tf_op jit(solution)/shard_map/ppermute | solution.py:556
  73.4 19.6 %collective-permute-start.19 = (bf16[256,768]{1,0:T(8,128)(2,1)S(1)}, bf16[256,768]{1,0:T(8,128)(2,1)S(1)}, u32[]{:S(2)}, u32[]{:S(2)}) collective-permute-start(bf16[256,768]{1,0:T(8,128)(2,1)S(1)} %get-tuple-element.48), channel_id=1, source_target_pairs={{1,2},{2,1},{5,6},{6,5},{9,10},{10,9},{13,14},{14,13},{17,18},{18,... | collective-permute-start | bytes 1179656 | tf_op jit(solution)/shard_map/ppermute | solution.py:558
  74.1 18.9 %collective-permute-start.18 = (bf16[256,768]{1,0:T(8,128)(2,1)S(1)}, bf16[256,768]{1,0:T(8,128)(2,1)S(1)}, u32[]{:S(2)}, u32[]{:S(2)}) collective-permute-start(bf16[256,768]{1,0:T(8,128)(2,1)S(1)} %get-tuple-element.47), channel_id=1, source_target_pairs={{0,1},{1,0},{2,3},{3,2},{4,5},{5,4},{6,7},{7,6},{8,9},{9,8},{10,11... | collective-permute-start | bytes 1179656 | tf_op jit(solution)/shard_map/ppermute | solution.py:557
  75.2 9.9 %collective-permute-start.22 = (bf16[2,256,384]{2,1,0:T(8,128)(2,1)S(1)}, bf16[2,256,384]{2,1,0:T(8,128)(2,1)S(1)}, u32[]{:S(2)}, u32[]{:S(2)}) collective-permute-start(bf16[2,256,384]{2,1,0:T(8,128)(2,1)S(1)} %get-tuple-element.50), channel_id=1, source_target_pairs={{0,8},{4,20},{8,0},{12,28},{16,24},{20,4},{24,16},{28,12},{1,9},{5... | collective-permute-start | bytes 1179656 | tf_op jit(solution)/shard_map/ppermute | solution.py:128
  76.1 11.2 %collective-permute-start.23 = (bf16[2,256,384]{2,1,0:T(8,128)(2,1)S(1)}, bf16[2,256,384]{2,1,0:T(8,128)(2,1)S(1)}, u32[]{:S(2)}, u32[]{:S(2)}) collective-permute-start(bf16[2,256,384]{2,1,0:T(8,128)(2,1)S(1)} %get-tuple-element.51), channel_id=1, source_target_pairs={{0,20},{4,8},{8,28},{12,0},{16,4},{20,24},{24,12},{28,16},{1,21},{... | collective-permute-start | bytes 1179656 | tf_op jit(solution)/shard_map/ppermute | solution.py:128
  81.3 16.8 %collective-permute-start.21 = (bf16[256,768]{1,0:T(8,128)(2,1)S(1)}, bf16[256,768]{1,0:T(8,128)(2,1)S(1)}, u32[]{:S(2)}, u32[]{:S(2)}) collective-permute-start(bf16[256,768]{1,0:T(8,128)(2,1)S(1)} %add_convert_fusion.1), channel_id=1, source_target_pairs={{0,2},{1,3},{2,0},{3,1},{4,6},{5,7},{6,4},{7,5},{8,10},{9,11},{10,... | collective-permute-start | bytes 1179656 | tf_op jit(solution)/shard_map/ppermute | solution.py:560
  87.3 13.8 %collective-permute-start.25 = (bf16[2,256,384]{2,1,0:T(8,128)(2,1)S(1)}, bf16[2,256,384]{2,1,0:T(8,128)(2,1)S(1)}, u32[]{:S(2)}, u32[]{:S(2)}) collective-permute-start(bf16[2,256,384]{2,1,0:T(8,128)(2,1)S(1)} %pad_maximum_fusion.3), channel_id=1, source_target_pairs={{0,28},{8,20},{16,12},{24,4},{1,29},{9,21},{17,13},{25,5},{2,30},{... | collective-permute-start | bytes 1179656 | tf_op jit(solution)/shard_map/ppermute | solution.py:128
  92.3 8.8 %collective-permute-start.24 = (bf16[2,256,384]{2,1,0:T(8,128)(2,1)S(1)}, bf16[2,256,384]{2,1,0:T(8,128)(2,1)S(1)}, u32[]{:S(2)}, u32[]{:S(2)}) collective-permute-start(bf16[2,256,384]{2,1,0:T(8,128)(2,1)S(1)} %pad_maximum_fusion.3), channel_id=1, source_target_pairs={{4,28},{12,20},{20,12},{28,4},{5,29},{13,21},{21,13},{29,5},{6,30}... | collective-permute-start | bytes 1179656 | tf_op jit(solution)/shard_map/ppermute | solution.py:128
  101.1 13.7 %collective-permute-start.26 = (bf16[256,768]{1,0:T(8,128)(2,1)S(1)}, bf16[256,768]{1,0:T(8,128)(2,1)S(1)}, u32[]{:S(2)}, u32[]{:S(2)}) collective-permute-start(bf16[256,768]{1,0:T(8,128)(2,1)S(1)} %add_convert_fusion), channel_id=1, source_target_pairs={{0,0},{1,5},{2,10},{3,15},{4,20},{5,17},{6,30},{7,27},{8,8},{9,13}... | collective-permute-start | bytes 1179656 | tf_op jit(solution)/shard_map/ppermute | solution.py:583
  108.4 8.3 %collective-permute-start.28 = (bf16[384,768]{1,0:T(8,128)(2,1)S(1)}, bf16[384,768]{1,0:T(8,128)(2,1)S(1)}, u32[]{:S(2)}, u32[]{:S(2)}) collective-permute-start(bf16[384,768]{1,0:T(8,128)(2,1)S(1)} %get-tuple-element.55), channel_id=1, source_target_pairs={{0,4},{4,0},{8,12},{12,8},{16,20},{20,16},{24,28},{28,24},{1,5},{5... | collective-permute-start | bytes 1769480 | tf_op jit(solution)/shard_map/ppermute | solution.py:128
  108.4 8.3 %collective-permute-start.29 = (bf16[384,768]{1,0:T(8,128)(2,1)S(1)}, bf16[384,768]{1,0:T(8,128)(2,1)S(1)}, u32[]{:S(2)}, u32[]{:S(2)}) collective-permute-start(bf16[384,768]{1,0:T(8,128)(2,1)S(1)} %get-tuple-element.56), channel_id=1, source_target_pairs={{0,4},{4,0},{8,12},{12,8},{16,20},{20,16},{24,28},{28,24},{1,5},{5... | collective-permute-start | bytes 1769480 | tf_op jit(solution)/shard_map/ppermute | solution.py:128
  108.9 7.8 %collective-permute-start.30 = (bf16[384,768]{1,0:T(8,128)(2,1)S(1)}, bf16[384,768]{1,0:T(8,128)(2,1)S(1)}, u32[]{:S(2)}, u32[]{:S(2)}) collective-permute-start(bf16[384,768]{1,0:T(8,128)(2,1)S(1)} %get-tuple-element.57), channel_id=1, source_target_pairs={{0,4},{4,0},{8,12},{12,8},{16,20},{20,16},{24,28},{28,24},{1,5},{5... | collective-permute-start | bytes 1769480 | tf_op jit(solution)/shard_map/ppermute | solution.py:128
  114.8 14.8 %collective-permute-start.27 = (bf16[256,768]{1,0:T(8,128)(2,1)S(1)}, bf16[256,768]{1,0:T(8,128)(2,1)S(1)}, u32[]{:S(2)}, u32[]{:S(2)}) collective-permute-start(bf16[256,768]{1,0:T(8,128)(2,1)S(1)} %collective-permute-done.26), channel_id=1, source_target_pairs={{0,0},{5,4},{10,8},{15,12},{20,20},{17,16},{30,28},{27,24},{8,9},{... | collective-permute-start | bytes 1179656 | tf_op jit(solution)/shard_map/ppermute | solution.py:592

commit v14 on v13

--- a/solution.py
+++ b/solution.py
@@ -196,31 +196,34 @@
 FLAG_ROWS = 16
 
 
-def pack_kernel(picks, place_ref, links_ref, q_ref, k_ref, v_ref, g_ref, *out_refs):
+def pack_kernel(picks, half, links_ref, q_ref, k_ref, v_ref, g_ref, *out_refs):
     length = q_ref.shape[0]
     row = lax.broadcasted_iota(jnp.int32, (FLAG_ROWS, HD), 0)
     gaps = [jnp.where(links_ref[0, side] >= 0, 0.0, 1.0).astype(jnp.float32) for side in range(2)]
     flags = jnp.where(row < FLAG_ROWS // 2, gaps[0], gaps[1])
+    view = lax.axis_index("view")
+    side = view // 2
+    first = {HERE: side * half, BESIDE: (1 - side) * half}
     for heads, out_ref in zip(picks, out_refs):
         for at, (base, step, sign) in enumerate(heads):
-            head = place_ref[base] + step + sign * place_ref[CORE]
+            head = first[base] + step + sign * lax.rem(view, 2)
             for kind, source in enumerate((q_ref, k_ref, v_ref, g_ref)):
                 out_ref[at, kind * length : (kind + 1) * length] = source[:, lanes(head * HD, HD)]
             out_ref[at, 4 * length : 4 * length + FLAG_ROWS] = flags.astype(out_ref.dtype)
 
 
-def pack(picks, place, links, arrays):
+def pack(picks, half, links, arrays):
     length = arrays[0].shape[0]
     height = 4 * length + FLAG_ROWS
     return pl.pallas_call(
-        functools.partial(pack_kernel, picks),
+        functools.partial(pack_kernel, picks, half),
         out_shape=[
             jax.ShapeDtypeStruct((len(heads), height, HD), jnp.bfloat16) for heads in picks
         ],
-        in_specs=[whole(pltpu.SMEM)] * 2 + [whole()] * 4,
+        in_specs=[whole(pltpu.SMEM)] + [whole()] * 4,
         out_specs=[whole()] * len(picks),
         name="pack_heads",
-    )(place, links, *arrays)
+    )(links, *arrays)
 
 
 def one_head(scaling, core, xs, length, keys, values, key_sums, value_sums):
@@ -358,67 +361,71 @@
     )(place, own_weights, mate_weights)
 
 
-def gathered(role, refs):
-    sides = []
-    for side in range(2):
-        pieces = []
-        for head in range(refs[0][0].shape[0] // 4):
-            for maker in range(2):
-                k = 2 * side + (maker ^ role)
-                pieces.append([refs[k][0][4 * head + (e ^ k)] for e in range(4)])
-        for at in range(refs[0][1].shape[0] // 2 if len(refs[0]) > 1 else 0):
-            rows = []
-            for e in range(4):
-                k = 2 * side + e % 2
-                rows.append(refs[k][1][2 * at + (e // 2 ^ side)])
-            pieces.append(rows)
-        sides.append(
-            jnp.concatenate([jnp.concatenate(rows, axis=0) for rows in pieces], axis=1)
-        )
-    return sides
+def gathered(role, side, refs):
+    pieces = []
+    for head in range(refs[0][0].shape[0] // 4):
+        for maker in range(2):
+            k = maker ^ role
+            pieces.append([refs[k][0][4 * head + (e ^ (2 * side + k))] for e in range(4)])
+    for at in range(refs[0][1].shape[0] // 2 if len(refs[0]) > 1 else 0):
+        pieces.append([refs[e % 2][1][2 * at + (e // 2 ^ side)] for e in range(4)])
+    return jnp.concatenate([jnp.concatenate(rows, axis=0) for rows in pieces], axis=1)
 
 
 def by_role(refs, parts):
     made, inward, ahead, aside, relay_x, relay_y = [
         refs[at * parts : (at + 1) * parts] for at in range(6)
     ]
-    return ((made, inward, ahead, aside), (ahead, aside, relay_x, relay_y))
-
-
-def input_kernel(parts, place_ref, *refs):
-    weights, out_refs, total = refs[6 * parts], refs[6 * parts + 1 : -1], refs[-1]
-    length = out_refs[0].shape[0]
-    for role, grads in enumerate(by_role(refs, parts)):
+    return (((made, inward), (ahead, aside)), ((ahead, aside), (relay_x, relay_y)))
+
+
+def input_kernel(side, parts, place_ref, *refs):
+    pairs = [refs[at * parts : (at + 1) * parts] for at in range(4)]
+    weights, refs = refs[4 * parts], refs[4 * parts + 1 :]
+    if side == 0:
+        total, before = refs[0], None
+    else:
+        before, out_refs, total = refs[0], refs[1:-1], refs[-1]
+    length = total.shape[1]
+    for role in range(2):
 
         @pl.when(place_ref[CORE] == role)
         def _():
-            left = jnp.concatenate(gathered(role, grads), axis=1)
+            left = gathered(role, side, pairs[2 * role : 2 * role + 2])
+            depth = left.shape[1]
+            rows = weights[side * depth : (side + 1) * depth]
             for e in range(4):
-                product = dot(left[e * length : (e + 1) * length], weights[...])
+                product = dot(left[e * length : (e + 1) * length], rows)
+                if before is not None:
+                    product += before[e]
                 total[e] = product.astype(total.dtype)
 
-    for s, out_ref in enumerate(out_refs):
-        out_ref[...] = total[jnp.bitwise_xor(place_ref[PLANE], s)]
-
-
-def input_product(place, grads, weights):
+    if before is not None:
+        for s, out_ref in enumerate(out_refs):
+            out_ref[...] = total[jnp.bitwise_xor(place_ref[PLANE], s)]
+
+
+def input_product(place, side, grads, weights, before=()):
     _, length, _ = grads[0].shape
     depth, rows = weights.shape
-    out = jax.ShapeDtypeStruct((length, rows), jnp.bfloat16)
+    if side == 0:
+        out = jax.ShapeDtypeStruct((4, length, rows), jnp.float32)
+    else:
+        out = [jax.ShapeDtypeStruct((length, rows), jnp.bfloat16)] * 4
     return pl.pallas_call(
-        functools.partial(input_kernel, len(grads) // 6),
-        out_shape=[out] * 4,
-        in_specs=[whole(pltpu.SMEM)] + [whole()] * (len(grads) + 1),
-        out_specs=[whole()] * 4,
-        scratch_shapes=[pltpu.VMEM((4, length, rows), jnp.bfloat16)],
+        functools.partial(input_kernel, side, len(grads) // 4),
+        out_shape=out,
+        in_specs=[whole(pltpu.SMEM)] + [whole()] * (len(grads) + 1 + len(before)),
+        out_specs=whole() if side == 0 else [whole()] * 4,
+        scratch_shapes=[pltpu.VMEM((4, length, rows), jnp.bfloat16)] if side else [],
         compiler_params=pltpu.CompilerParams(vmem_limit_bytes=16 * MIB),
         cost_estimate=pl.CostEstimate(
-            flops=8 * length * rows * depth,
-            bytes_accessed=8 * length * (rows + depth) + 2 * rows * depth,
+            flops=4 * length * rows * depth,
+            bytes_accessed=8 * length * (rows + depth) + rows * depth,
             transcendentals=0,
         ),
-        name="input_gradient",
-    )(place, *grads, weights)
+        name="input_gradient_next" if side else "input_gradient_here",
+    )(place, *grads, weights, *before)
 
 
 def weight_kernel(mine, mean_scale, parts, place_ref, *refs):
@@ -438,9 +445,9 @@
         def _():
             for e, source in enumerate(tokens[role]):
                 turned[:, e * length : (e + 1) * length] = source[part].T
-            for base, side in zip((HERE, BESIDE), gathered(role, grads)):
-                total = dot(turned[...], side)
-                for head in range(side.shape[1] // (3 * HD)):
+            for side, base in enumerate((HERE, BESIDE)):
+                total = dot(turned[...], gathered(role, side, grads[side]))
+                for head in range(total.shape[1] // (3 * HD)):
                     here = lanes((place_ref[base] + head) * HD, HD)
                     for kind, out in enumerate(out_refs):
                         at = (head * 3 + kind) * HD
@@ -505,7 +512,7 @@
     ]
     if shared:
         picks += [[(BESIDE, 2 * own_heads, 0)], [(HERE, 2 * own_heads, 0)]]
-    packed = pack(picks, place, view_links, arrays)
+    packed = pack(picks, half, view_links, arrays)
     to_x, to_cross, to_mate, own = packed[:4]
     x_in = moved(to_x, along_x)
     cross_in = moved(to_cross, across_x)
@@ -534,7 +541,7 @@
     mate_here = moved(here, only(1, mate))
 
     own_weights, turn = None, place
-    parts = []
+    parts, sents = [], []
     for kept, sources in sets:
         made = attention(turn, kept, sources)
         if own_weights is None:
@@ -547,11 +554,14 @@
         (sent,) = after((ahead,), aside, inward, mate_here, to_straight, to_crossed, to_corner)
         relay_x = moved(sent, only(1, along_x))
         relay_y = moved(sent, only(0, across_y))
+        sents.append(sent)
         parts.append((made, inward, ahead, aside, relay_x, relay_y))
     grads = [array for kind in zip(*parts) for array in kind]
     weights = joined_weights(place, own_weights, moved(own_weights, mate))
 
-    slots = input_product(place, grads, weights)
+    count = 2 * len(parts)
+    here_sum = input_product(place, 0, [*grads[:count], *sents, *grads[3 * len(parts) : 4 * len(parts)]], weights)
+    slots = input_product(place, 1, grads[count:], weights, (here_sum,))
     last = groups - 1
     far = lax.ppermute(slots[3], "head", [(0, 1), (last, last - 1)])
     nearest = lax.ppermute(slots[1], "head", [(z, z ^ 1) for z in range(groups)])

time: 131 us -> 133 us (1.015)
  the two profiles are of different devices: /device:TPU:26 before, /device:TPU:16 now
where the time goes in v14:
time: 133 us; the launch traced here: 131 us
  waiting for transfers between devices  58.4 us (44%)
  starting transfers between devices  39.3 us (30%)
  Pallas kernels  28 us (21%)
  local copies, waits for them, and re-layouts  3.34 us (3%)
    ppermute x25, starting transfers between devices, moved(): return lax.ppermute(value, ('dp', 'view'), pairs)  29.5 us
    ppermute x25, waiting for transfers between devices, moved(): return lax.ppermute(value, ('dp', 'view'), pairs)  27.3 us
    pallas_call x2, Pallas kernels, attention(): pl.pallas_call(functools.partial(attention_kernel, HD ** (-0.5), kept), o...  8.77 us
    ppermute x1, waiting for transfers between devices, gather_body(): across = lax.ppermute(joint, 'head', [(z, z ^ 2) for z in range(groups)])  8.72 us
    pallas_call x2, Pallas kernels, weight_product(): pl.pallas_call(functools.partial(weight_kernel, mine, mean_scale, len(gra...  7.78 us
    ppermute x1, waiting for transfers between devices, gather_body(): far = lax.ppermute(slots[3], 'head', [(0, 1), (last, last - 1)])  7.59 us
    ppermute x1, waiting for transfers between devices, gather_body(): lax.ppermute(total, ('dp', 'view', 'head'), [(spot(y, v, z), spot(y ^ v %...  6.55 us
    ppermute x1, waiting for transfers between devices, gather_body(): lax.ppermute(beside, ('dp', 'view', 'head'), [(spot(y ^ v % 2, v ^ z, z),...  6.33 us
  transfers between devices with their start and end apart: 31, of which 14 were waited for; matrix products, arithmetic and copies ran while one was open for 2% of the time, Pallas kernels for 17%

profile of v14, /device:TPU:16, one launch (start us, length us, event | category | flops | bytes accessed | tf_op | source)
XLA Modules:
  0.0 130.5 jit_solution(7421012632763889005)
XLA Ops:
  0.6 2.8 %pack_heads.1 = (bf16[1,1040,128]{2,1,0:T(8,128)(2,1)}, bf16[1,1040,128]{2,1,0:T(8,128)(2,1)}, bf16[1,1040,128]{2,1,0:T(8,128)(2,1)}, bf16[1,1040,128]{2,1,0:T(8...) custom-call(s32[1,2]{1,0:T(1,128)} %links_ref.1, bf16[256,768]{1,0:T(8,128)(2,1)} %bitcast.26, ...), custom_call_target="tpu_custom_call" | custom-call | tf_op jit(solution)/shard_map/pack_heads/pallas_call | solution.py:218
  3.4 1.5 %collective-permute-start.1 = (bf16[1,1040,128]{2,1,0:T(8,128)(2,1)}, bf16[1,1040,128]{2,1,0:T(8,128)(2,1)S(1)}, u32[]{:S(2)}, u32[]{:S(2)}) collective-permute-start(bf16[1,1040,128]{2,1,0:T(8,128)(2,1)} %get-tuple-element.35), channel_id=1, source_target_pairs={{0,8},{4,12},{8,0},{12,4},{16,24},{20,28},{24,16},{28,20},{1,9},{5... | collective-permute-start | bytes 798728 | tf_op jit(solution)/shard_map/ppermute | solution.py:128
  4.9 0.0 collective-permute-start
  4.9 0.6 collective-permute-start.2
  5.6 0.0 collective-permute-start.4
  5.6 0.1 pad_add_fusion.place_ref
  5.7 7.3 %collective-permute-done.1.x_in = bf16[1,1040,128]{2,1,0:T(8,128)(2,1)S(1)} collective-permute-done((bf16[1,1040,128]{2,1,0:T(8,128)(2,1)}, bf16[1,1040,128]{2,1,0:T(8,128)(2,1)S(1)}, u32[]{:S(2)}, u32[]{:S(2)}) %collective-permute-start.1) | collective-permute-done | bytes 266272 | tf_op jit(solution)/shard_map/ppermute | solution.py:128
  12.9 1.5 %collective-permute-start.5 = (bf16[1,1040,128]{2,1,0:T(8,128)(2,1)}, bf16[1,1040,128]{2,1,0:T(8,128)(2,1)S(1)}, u32[]{:S(2)}, u32[]{:S(2)}) collective-permute-start(bf16[1,1040,128]{2,1,0:T(8,128)(2,1)} %get-tuple-element.43), channel_id=1, source_target_pairs={{0,8},{4,12},{8,0},{12,4},{16,24},{20,28},{24,16},{28,20},{1,9},{5... | collective-permute-start | bytes 798728 | tf_op jit(solution)/shard_map/ppermute | solution.py:128
  14.4 0.0 collective-permute-done.mate_in
  14.4 3.3 %collective-permute-done.2.far_in = bf16[1,1040,128]{2,1,0:T(8,128)(2,1)S(1)} collective-permute-done((bf16[1,1040,128]{2,1,0:T(8,128)(2,1)}, bf16[1,1040,128]{2,1,0:T(8,128)(2,1)S(1)}, u32[]{:S(2)}, u32[]{:S(2)}) %collective-permute-start.2) | collective-permute-done | bytes 266272 | tf_op jit(solution)/shard_map/ppermute | solution.py:128
  17.7 0.9 copy-done.4
  18.7 4.5 %attention_gradients.2.refs_0_.refs_6_ = bf16[4,256,384]{2,1,0:T(8,128)(2,1)S(1)} custom-call(s32[4]{0:T(128)S(1)} %pad_add_fusion.place_ref, bf16[1,1040,128]{2,1,0:T(8,128)(2,1)S(1)} %copy-done.4, bf16[1,1040,128]{2,1,0:T(8,128)(2,1)S(1)} %collective-permute-done.mate_in, bf16[1,1040,128]{2,1,0:T(8,128)(2,1)S(1)} %collective-permute-done.1.x_in, ...), custom_call_target="tpu_custom_call" | custom-call | flops 2013265920 | bytes 1835008 | tf_op jit(solution)/shard_map/attention_gradients/pallas_call | solution.py:307
  23.2 1.1 turn_weights.1.own_ref
  24.2 0.8 collective-permute-start.17
  25.0 0.2 collective-permute-start.6
  25.2 1.6 %dynamic-slice_bitcast_fusion.1 = (bf16[1,256,384]{2,1,0:T(8,128)(2,1)S(1)}, bf16[1,256,384]{2,1,0:T(8,128)(2,1)S(1)}, bf16[1,256,384]{2,1,0:T(8,128)(2,1)S(1)},...) fusion(bf16[1,1,256,3072]{3,2,1,0:T(8,128)(2,1)} %param.9, ...), kind=kLoop, calls=%fused_computation.7 | loop fusion | bytes 3145760 | tf_op jit(solution)/shard_map/stack | solution.py:534
  26.8 1.3 collective-permute-start.10
  28.1 2.3 %collective-permute-start.8 = (bf16[4,256,384]{2,1,0:T(8,128)(2,1)S(1)}, bf16[4,256,384]{2,1,0:T(8,128)(2,1)S(1)}, u32[]{:S(2)}, u32[]{:S(2)}) collective-permute-start(bf16[4,256,384]{2,1,0:T(8,128)(2,1)S(1)} %attention_gradients.2.refs_0_.refs_6_), channel_id=1, source_target_pairs={{0,20},{4,8},{8,28},{12,0},{16,4},{20,24},{24,12},{28,16},{1,21},{... | collective-permute-start | bytes 2359304 | tf_op jit(solution)/shard_map/ppermute | solution.py:128
  30.5 0.0 collective-permute-done.4.mate_in
  30.5 1.5 %collective-permute-start.3 = (bf16[4,256,384]{2,1,0:T(8,128)(2,1)S(1)}, bf16[4,256,384]{2,1,0:T(8,128)(2,1)S(1)}, u32[]{:S(2)}, u32[]{:S(2)}) collective-permute-start(bf16[4,256,384]{2,1,0:T(8,128)(2,1)S(1)} %attention_gradients.2.refs_0_.refs_6_), channel_id=1, source_target_pairs={{0,8},{4,20},{8,0},{12,28},{16,24},{20,4},{24,16},{28,12},{1,9},{5... | collective-permute-start | bytes 2359304 | tf_op jit(solution)/shard_map/ppermute | solution.py:128
  32.0 0.0 collective-permute-done.6.far_in
  32.0 1.3 collective-permute-start.11
  33.3 4.3 %attention_gradients.3.refs_1_.refs_7_ = bf16[2,256,384]{2,1,0:T(8,128)(2,1)S(1)} custom-call(s32[4]{0:T(128)S(1)} %pad_add_fusion.place_ref, bf16[1,1040,128]{2,1,0:T(8,128)(2,1)S(1)} %copy-done.3, bf16[1,1040,128]{2,1,0:T(8,128)(2,1)S(1)} %collective-permute-done.4.mate_in, bf16[1,1040,128]{2,1,0:T(8,128)(2,1)S(1)} %collective-permute-done.5.x_in, ...), custom_call_target="tpu_custom_call" | custom-call | flops 2013265920 | bytes 1835008 | tf_op jit(solution)/shard_map/attention_gradients/pallas_call | solution.py:307
  37.7 1.3 collective-permute-start.13
  39.0 0.1 pad_maximum_fusion.1
  39.1 1.3 %collective-permute-start.9 = (bf16[2,256,384]{2,1,0:T(8,128)(2,1)S(1)}, bf16[2,256,384]{2,1,0:T(8,128)(2,1)S(1)}, u32[]{:S(2)}, u32[]{:S(2)}) collective-permute-start(bf16[2,256,384]{2,1,0:T(8,128)(2,1)S(1)} %attention_gradients.3.refs_1_.refs_7_), channel_id=1, source_target_pairs={{0,20},{4,8},{8,28},{12,0},{16,4},{20,24},{24,12},{28,16},{1,21},{... | collective-permute-start | bytes 1179656 | tf_op jit(solution)/shard_map/ppermute | solution.py:128
  40.5 7.8 %collective-permute-done.8.refs_6_.refs_2_.refs_12_ = bf16[4,256,384]{2,1,0:T(8,128)(2,1)S(1)} collective-permute-done((bf16[4,256,384]{2,1,0:T(8,128)(2,1)S(1)}, bf16[4,256,384]{2,1,0:T(8,128)(2,1)S(1)}, u32[]{:S(2)}, u32[]{:S(2)}) %collective-permute-start.8) | collective-permute-done | bytes 786464 | tf_op jit(solution)/shard_map/ppermute | solution.py:128
  48.3 1.1 collective-permute-start.7
  49.4 1.5 %collective-permute-done.3.refs_4_.refs_0_.refs_10_ = bf16[4,256,384]{2,1,0:T(8,128)(2,1)S(1)} collective-permute-done((bf16[4,256,384]{2,1,0:T(8,128)(2,1)S(1)}, bf16[4,256,384]{2,1,0:T(8,128)(2,1)S(1)}, u32[]{:S(2)}, u32[]{:S(2)}) %collective-permute-start.3) | collective-permute-done | bytes 786464 | tf_op jit(solution)/shard_map/ppermute | solution.py:128
  50.9 1.7 %collective-permute-start.15 = (bf16[4,256,384]{2,1,0:T(8,128)(2,1)S(1)}, bf16[4,256,384]{2,1,0:T(8,128)(2,1)S(1)}, u32[]{:S(2)}, u32[]{:S(2)}) collective-permute-start(bf16[4,256,384]{2,1,0:T(8,128)(2,1)S(1)} %collective-permute-done.3.refs_4_.refs_0_.refs_10_), channel_id=1, source_target_pairs={{0,20},{8,28},{16,4},{24,12},{1,21},{9,29},{17,5},{25,13},{2,22},{... | collective-permute-start | bytes 2359304 | tf_op jit(solution)/shard_map/ppermute | solution.py:128
  52.7 0.7 collective-permute-start.12
  53.4 0.5 collective-permute-done.9.refs_7_.refs_3_.refs_13_
  53.9 3.6 %collective-permute-done.7.refs_5_.refs_1_.refs_11_ = bf16[2,256,384]{2,1,0:T(8,128)(2,1)S(1)} collective-permute-done((bf16[2,256,384]{2,1,0:T(8,128)(2,1)S(1)}, bf16[2,256,384]{2,1,0:T(8,128)(2,1)S(1)}, u32[]{:S(2)}, u32[]{:S(2)}) %collective-permute-start.7) | collective-permute-done | bytes 393248 | tf_op jit(solution)/shard_map/ppermute | solution.py:128
  57.5 5.8 %collective-permute-start.16 = (bf16[2,256,384]{2,1,0:T(8,128)(2,1)S(1)}, bf16[2,256,384]{2,1,0:T(8,128)(2,1)S(1)}, u32[]{:S(2)}, u32[]{:S(2)}) collective-permute-start(bf16[2,256,384]{2,1,0:T(8,128)(2,1)S(1)} %collective-permute-done.7.refs_5_.refs_1_.refs_11_), channel_id=1, source_target_pairs={{0,20},{8,28},{16,4},{24,12},{1,21},{9,29},{17,5},{25,13},{2,22},{... | collective-permute-start | bytes 1179656 | tf_op jit(solution)/shard_map/ppermute | solution.py:128
  63.3 0.7 collective-permute-start.14
  64.0 1.8 %join_weights.1.refs_8_ = bf16[2304,768]{1,0:T(8,128)(2,1)S(1)} custom-call(s32[4]{0:T(128)S(1)} %pad_add_fusion.place_ref, bf16[2304,384]{1,0:T(8,128)(2,1)S(1)} %turn_weights.1.own_ref, bf16[2304,384]{1,0:T(8,128)(2,1)} %collective-permute-done.17.mate_ref), custom_call_target="tpu_custom_call" | custom-call | tf_op jit(solution)/shard_map/join_weights/pallas_call | solution.py:354
  65.8 2.9 %input_gradient_here.1.refs_9_ = f32[4,256,768]{2,1,0:T(8,128)S(1)} custom-call(s32[4]{0:T(128)S(1)} %pad_add_fusion.place_ref, bf16[4,256,384]{2,1,0:T(8,128)(2,1)S(1)} %attention_gradients.2.refs_0_.refs_6_, bf16[2,256,384]{2,1,0:T(8,128)(2,1)S(1)} %attention_gradients.3.refs_1_.refs_7_, bf16[4,256,384]{2,1,0:T(8,128)(2,1)S(1)} %collective-permute-done.10.refs_2_.refs_8_, ...), custom_call_target="tpu_custom_call" | custom-call | flops 1811939328 | bytes 8060928 | tf_op jit(solution)/shard_map/input_gradient_here/pallas_call | solution.py:415
  68.7 0.6 collective-permute-done.16.refs_7_.refs_17_
  69.3 2.9 %input_gradient_next.1 = (bf16[256,768]{1,0:T(8,128)(2,1)S(1)}, bf16[256,768]{1,0:T(8,128)(2,1)S(1)}, bf16[256,768]{1,0:T(8,128)(2,1)S(1)}, bf16[256,768]{1,0:T(8,128)(2,1)S(1)}) custom-call(s32[4]{0:T(128)S(1)} %pad_add_fusion.place_ref, bf16[4,256,384]{2,1,0:T(8,128)(2,1)S(1)} %collective-permute-done.3.refs_4_.refs_0_.refs_10_, ...), custom_call_target="tpu_custom_call" | custom-call | flops 1811939328 | bytes 8060928 | tf_op jit(solution)/shard_map/input_gradient_next/pallas_call | solution.py:415
  72.2 1.3 collective-permute-start.20
  73.5 2.4 %collective-permute-start.19 = (bf16[256,768]{1,0:T(8,128)(2,1)S(1)}, bf16[256,768]{1,0:T(8,128)(2,1)S(1)}, u32[]{:S(2)}, u32[]{:S(2)}) collective-permute-start(bf16[256,768]{1,0:T(8,128)(2,1)S(1)} %get-tuple-element.48), channel_id=1, source_target_pairs={{1,2},{2,1},{5,6},{6,5},{9,10},{10,9},{13,14},{14,13},{17,18},{18,... | collective-permute-start | bytes 1179656 | tf_op jit(solution)/shard_map/ppermute | solution.py:568
  75.9 1.1 collective-permute-start.18
  76.9 1.1 collective-permute-start.22
  78.1 0.4 collective-permute-start.23
  78.5 7.6 %collective-permute-done.20 = bf16[256,768]{1,0:T(8,128)(2,1)S(1)} collective-permute-done((bf16[256,768]{1,0:T(8,128)(2,1)S(1)}, bf16[256,768]{1,0:T(8,128)(2,1)S(1)}, u32[]{:S(2)}, u32[]{:S(2)}) %collective-permute-start.20) | collective-permute-done | bytes 393248 | tf_op jit(solution)/shard_map/ppermute | solution.py:566
  86.1 0.1 add_convert_fusion.1
  86.2 0.1 collective-permute-start.21
  86.3 2.1 %collective-permute-done.22.refs_2_ = bf16[2,256,384]{2,1,0:T(8,128)(2,1)S(1)} collective-permute-done((bf16[2,256,384]{2,1,0:T(8,128)(2,1)S(1)}, bf16[2,256,384]{2,1,0:T(8,128)(2,1)S(1)}, u32[]{:S(2)}, u32[]{:S(2)}) %collective-permute-start.22) | collective-permute-done | bytes 393248 | tf_op jit(solution)/shard_map/ppermute | solution.py:128
  88.4 0.5 collective-permute-done.23.refs_3_
  88.9 3.0 %collective-permute-start.25 = (bf16[2,256,384]{2,1,0:T(8,128)(2,1)S(1)}, bf16[2,256,384]{2,1,0:T(8,128)(2,1)S(1)}, u32[]{:S(2)}, u32[]{:S(2)}) collective-permute-start(bf16[2,256,384]{2,1,0:T(8,128)(2,1)S(1)} %pad_maximum_fusion.3), channel_id=1, source_target_pairs={{0,28},{8,20},{16,12},{24,4},{1,29},{9,21},{17,13},{25,5},{2,30},{... | collective-permute-start | bytes 1179656 | tf_op jit(solution)/shard_map/ppermute | solution.py:128
  91.9 0.7 collective-permute-start.24
  92.6 1.9 %collective-permute-done.18 = bf16[256,768]{1,0:T(8,128)(2,1)S(1)} collective-permute-done((bf16[256,768]{1,0:T(8,128)(2,1)S(1)}, bf16[256,768]{1,0:T(8,128)(2,1)S(1)}, u32[]{:S(2)}, u32[]{:S(2)}) %collective-permute-start.18) | collective-permute-done | bytes 393248 | tf_op jit(solution)/shard_map/ppermute | solution.py:567
  94.5 8.7 %collective-permute-done.21 = bf16[256,768]{1,0:T(8,128)(2,1)S(1)} collective-permute-done((bf16[256,768]{1,0:T(8,128)(2,1)S(1)}, bf16[256,768]{1,0:T(8,128)(2,1)S(1)}, u32[]{:S(2)}, u32[]{:S(2)}) %collective-permute-start.21) | collective-permute-done | bytes 393248 | tf_op jit(solution)/shard_map/ppermute | solution.py:570
  103.2 0.2 add_convert_fusion
  103.5 3.1 %collective-permute-start.26 = (bf16[256,768]{1,0:T(8,128)(2,1)S(1)}, bf16[256,768]{1,0:T(8,128)(2,1)S(1)}, u32[]{:S(2)}, u32[]{:S(2)}) collective-permute-start(bf16[256,768]{1,0:T(8,128)(2,1)S(1)} %add_convert_fusion), channel_id=1, source_target_pairs={{0,0},{1,5},{2,10},{3,15},{4,20},{5,17},{6,30},{7,27},{8,8},{9,13}... | collective-permute-start | bytes 1179656 | tf_op jit(solution)/shard_map/ppermute | solution.py:593
  106.5 2.9 %weight_gradient_mate.1 = (bf16[384,768]{1,0:T(8,128)(2,1)S(1)}, bf16[384,768]{1,0:T(8,128)(2,1)S(1)}, bf16[384,768]{1,0:T(8,128)(2,1)S(1)}) custom-call(s32[4]{0:T(128)S(1)} %pad_add_fusion.place_ref, bf16[2,256,384]{2,1,0:T(8,128)(2,1)S(1)} %pad_maximum_fusion.refs_0_, bf16[2,256,384]{2,1,0:T(8,128)(2,1)S(1)} %collective-permute-done.11.refs_1_, ...), custom_call_target="tpu_custom_call" | custom-call | flops 1811939328 | bytes 9043968 | tf_op jit(solution)/shard_map/weight_gradient_mate/pallas_call | solution.py:464
  109.4 0.1 collective-permute-start.28
  109.5 0.5 collective-permute-start.29
  110.0 0.1 collective-permute-start.30
  110.0 6.5 %collective-permute-done.26 = bf16[256,768]{1,0:T(8,128)(2,1)S(1)} collective-permute-done((bf16[256,768]{1,0:T(8,128)(2,1)S(1)}, bf16[256,768]{1,0:T(8,128)(2,1)S(1)}, u32[]{:S(2)}, u32[]{:S(2)}) %collective-permute-start.26) | collective-permute-done | bytes 393248 | tf_op jit(solution)/shard_map/ppermute | solution.py:593
  116.6 1.9 %collective-permute-start.27 = (bf16[256,768]{1,0:T(8,128)(2,1)S(1)}, bf16[256,768]{1,0:T(8,128)(2,1)S(1)}, u32[]{:S(2)}, u32[]{:S(2)}) collective-permute-start(bf16[256,768]{1,0:T(8,128)(2,1)S(1)} %collective-permute-done.26), channel_id=1, source_target_pairs={{0,0},{5,4},{10,8},{15,12},{20,20},{17,16},{30,28},{27,24},{8,9},{... | collective-permute-start | bytes 1179656 | tf_op jit(solution)/shard_map/ppermute | solution.py:602
  118.5 4.9 %weight_gradient_own.1 = (f32[384,768]{1,0:T(8,128)}, f32[384,768]{1,0:T(8,128)}, f32[384,768]{1,0:T(8,128)}) custom-call(s32[4]{0:T(128)S(1)} %pad_add_fusion.place_ref, bf16[2,256,384]{2,1,0:T(8,128)(2,1)S(1)} %pad_maximum_fusion.refs_0_, bf16[2,256,384]{2,1,0:T(8,128)(2,1)S(1)} %collective-permute-done.11.refs_1_, ...), custom_call_target="tpu_custom_call" | custom-call | flops 1811939328 | bytes 9043968 | tf_op jit(solution)/shard_map/weight_gradient_own/pallas_call | solution.py:464
  123.5 6.3 %collective-permute-done.27 = bf16[256,768]{1,0:T(8,128)(2,1)S(1)} collective-permute-done((bf16[256,768]{1,0:T(8,128)(2,1)S(1)}, bf16[256,768]{1,0:T(8,128)(2,1)S(1)}, u32[]{:S(2)}, u32[]{:S(2)}) %collective-permute-start.27) | collective-permute-done | bytes 393248 | tf_op jit(solution)/shard_map/ppermute | solution.py:602
  129.8 0.7 copy.14
  (25 shorter events, 0.1 us)
Async XLA Ops:
  3.4 9.5 %collective-permute-start.1 = (bf16[1,1040,128]{2,1,0:T(8,128)(2,1)}, bf16[1,1040,128]{2,1,0:T(8,128)(2,1)S(1)}, u32[]{:S(2)}, u32[]{:S(2)}) collective-permute-start(bf16[1,1040,128]{2,1,0:T(8,128)(2,1)} %get-tuple-element.35), channel_id=1, source_target_pairs={{0,8},{4,12},{8,0},{12,4},{16,24},{20,28},{24,16},{28,20},{1,9},{5... | collective-permute-start | bytes 798728 | tf_op jit(solution)/shard_map/ppermute | solution.py:128
  4.9 9.5 %collective-permute-start = (bf16[1,1040,128]{2,1,0:T(8,128)(2,1)}, bf16[1,1040,128]{2,1,0:T(8,128)(2,1)S(1)}, u32[]{:S(2)}, u32[]{:S(2)}) collective-permute-start(bf16[1,1040,128]{2,1,0:T(8,128)(2,1)} %get-tuple-element.34), channel_id=1, source_target_pairs={{0,4},{4,0},{8,12},{12,8},{16,20},{20,16},{24,28},{28,24},{1,5},{5... | collective-permute-start | bytes 798728 | tf_op jit(solution)/shard_map/ppermute | solution.py:128
  4.9 12.8 %collective-permute-start.2 = (bf16[1,1040,128]{2,1,0:T(8,128)(2,1)}, bf16[1,1040,128]{2,1,0:T(8,128)(2,1)S(1)}, u32[]{:S(2)}, u32[]{:S(2)}) collective-permute-start(bf16[1,1040,128]{2,1,0:T(8,128)(2,1)} %get-tuple-element.36), channel_id=1, source_target_pairs={{0,12},{4,8},{8,4},{12,0},{16,28},{20,24},{24,20},{28,16},{1,13},{... | collective-permute-start | bytes 798728 | tf_op jit(solution)/shard_map/ppermute | solution.py:128
  5.6 24.9 %collective-permute-start.4 = (bf16[1,1040,128]{2,1,0:T(8,128)(2,1)}, bf16[1,1040,128]{2,1,0:T(8,128)(2,1)S(1)}, u32[]{:S(2)}, u32[]{:S(2)}) collective-permute-start(bf16[1,1040,128]{2,1,0:T(8,128)(2,1)} %get-tuple-element.41.own), channel_id=1, source_target_pairs={{0,4},{4,0},{8,12},{12,8},{16,20},{20,16},{24,28},{28,24},{1,5},{5... | collective-permute-start | bytes 798728 | tf_op jit(solution)/shard_map/ppermute | solution.py:128
  12.9 12.1 %collective-permute-start.5 = (bf16[1,1040,128]{2,1,0:T(8,128)(2,1)}, bf16[1,1040,128]{2,1,0:T(8,128)(2,1)S(1)}, u32[]{:S(2)}, u32[]{:S(2)}) collective-permute-start(bf16[1,1040,128]{2,1,0:T(8,128)(2,1)} %get-tuple-element.43), channel_id=1, source_target_pairs={{0,8},{4,12},{8,0},{12,4},{16,24},{20,28},{24,16},{28,20},{1,9},{5... | collective-permute-start | bytes 798728 | tf_op jit(solution)/shard_map/ppermute | solution.py:128
  17.7 1.0 copy-start.4
  18.7 4.5 %copy-start = (bf16[384,768]{1,0:T(8,128)(2,1)S(1)}, bf16[384,768]{1,0:T(8,128)(2,1)}, u32[]{:S(2)}) copy-start(bf16[384,768]{1,0:T(8,128)(2,1)} %q_ref) | copy-start | bytes 1769476
  18.7 4.5 %copy-start.1 = (bf16[384,768]{1,0:T(8,128)(2,1)S(1)}, bf16[384,768]{1,0:T(8,128)(2,1)}, u32[]{:S(2)}) copy-start(bf16[384,768]{1,0:T(8,128)(2,1)} %k_ref) | copy-start | bytes 1769476
  18.7 4.5 %copy-start.2 = (bf16[384,768]{1,0:T(8,128)(2,1)S(1)}, bf16[384,768]{1,0:T(8,128)(2,1)}, u32[]{:S(2)}) copy-start(bf16[384,768]{1,0:T(8,128)(2,1)} %v_ref) | copy-start | bytes 1769476
  24.2 39.7 %collective-permute-start.17 = (bf16[2304,384]{1,0:T(8,128)(2,1)S(1)}, bf16[2304,384]{1,0:T(8,128)(2,1)}, u32[]{:S(2)}, u32[]{:S(2)}) collective-permute-start(bf16[2304,384]{1,0:T(8,128)(2,1)S(1)} %turn_weights.1.own_ref), channel_id=1, source_target_pairs={{0,4},{4,0},{8,12},{12,8},{16,20},{20,16},{24,28},{28,24},{1,5},{5... | collective-permute-start | bytes 5308424 | tf_op jit(solution)/shard_map/ppermute | solution.py:128
  25.0 8.3 %copy-start.3 = (bf16[1,1040,128]{2,1,0:T(8,128)(2,1)S(1)}, bf16[1,1040,128]{2,1,0:T(8,128)(2,1)}, u32[]{:S(2)}) copy-start(bf16[1,1040,128]{2,1,0:T(8,128)(2,1)} %get-tuple-element.41.own) | copy-start | bytes 798724
  25.0 7.0 %collective-permute-start.6 = (bf16[1,1040,128]{2,1,0:T(8,128)(2,1)S(1)}, bf16[1,1040,128]{2,1,0:T(8,128)(2,1)S(1)}, u32[]{:S(2)}, u32[]{:S(2)}) collective-permute-start(bf16[1,1040,128]{2,1,0:T(8,128)(2,1)S(1)} %collective-permute-done.5.x_in), channel_id=1, source_target_pairs={{0,4},{4,0},{8,12},{12,8},{16,20},{20,16},{24,28},{28,24},{1,5},{5... | collective-permute-start | bytes 798728 | tf_op jit(solution)/shard_map/ppermute | solution.py:128
  26.8 12.3 %collective-permute-start.10 = (bf16[4,256,384]{2,1,0:T(8,128)(2,1)S(1)}, bf16[4,256,384]{2,1,0:T(8,128)(2,1)S(1)}, u32[]{:S(2)}, u32[]{:S(2)}) collective-permute-start(bf16[4,256,384]{2,1,0:T(8,128)(2,1)S(1)} %attention_gradients.2.refs_0_.refs_6_), channel_id=1, source_target_pairs={{4,0},{12,8},{20,16},{28,24},{5,1},{13,9},{21,17},{29,25},{6,2},{1... | collective-permute-start | bytes 2359304 | tf_op jit(solution)/shard_map/ppermute | solution.py:128
  28.1 20.1 %collective-permute-start.8 = (bf16[4,256,384]{2,1,0:T(8,128)(2,1)S(1)}, bf16[4,256,384]{2,1,0:T(8,128)(2,1)S(1)}, u32[]{:S(2)}, u32[]{:S(2)}) collective-permute-start(bf16[4,256,384]{2,1,0:T(8,128)(2,1)S(1)} %attention_gradients.2.refs_0_.refs_6_), channel_id=1, source_target_pairs={{0,20},{4,8},{8,28},{12,0},{16,4},{20,24},{24,12},{28,16},{1,21},{... | collective-permute-start | bytes 2359304 | tf_op jit(solution)/shard_map/ppermute | solution.py:128
  30.5 20.5 %collective-permute-start.3 = (bf16[4,256,384]{2,1,0:T(8,128)(2,1)S(1)}, bf16[4,256,384]{2,1,0:T(8,128)(2,1)S(1)}, u32[]{:S(2)}, u32[]{:S(2)}) collective-permute-start(bf16[4,256,384]{2,1,0:T(8,128)(2,1)S(1)} %attention_gradients.2.refs_0_.refs_6_), channel_id=1, source_target_pairs={{0,8},{4,20},{8,0},{12,28},{16,24},{20,4},{24,16},{28,12},{1,9},{5... | collective-permute-start | bytes 2359304 | tf_op jit(solution)/shard_map/ppermute | solution.py:128
  32.0 5.6 %collective-permute-start.11 = (bf16[2,256,384]{2,1,0:T(8,128)(2,1)S(1)}, bf16[2,256,384]{2,1,0:T(8,128)(2,1)S(1)}, u32[]{:S(2)}, u32[]{:S(2)}) collective-permute-start(bf16[2,256,384]{2,1,0:T(8,128)(2,1)S(1)} %pad_maximum_fusion.refs_0_), channel_id=1, source_target_pairs={{4,0},{12,8},{20,16},{28,24},{5,1},{13,9},{21,17},{29,25},{6,2},{1... | collective-permute-start | bytes 1179656 | tf_op jit(solution)/shard_map/ppermute | solution.py:128
  37.7 15.0 %collective-permute-start.13 = (bf16[2,256,384]{2,1,0:T(8,128)(2,1)S(1)}, bf16[2,256,384]{2,1,0:T(8,128)(2,1)S(1)}, u32[]{:S(2)}, u32[]{:S(2)}) collective-permute-start(bf16[2,256,384]{2,1,0:T(8,128)(2,1)S(1)} %attention_gradients.3.refs_1_.refs_7_), channel_id=1, source_target_pairs={{4,0},{12,8},{20,16},{28,24},{5,1},{13,9},{21,17},{29,25},{6,2},{1... | collective-permute-start | bytes 1179656 | tf_op jit(solution)/shard_map/ppermute | solution.py:128
  39.1 14.8 %collective-permute-start.9 = (bf16[2,256,384]{2,1,0:T(8,128)(2,1)S(1)}, bf16[2,256,384]{2,1,0:T(8,128)(2,1)S(1)}, u32[]{:S(2)}, u32[]{:S(2)}) collective-permute-start(bf16[2,256,384]{2,1,0:T(8,128)(2,1)S(1)} %attention_gradients.3.refs_1_.refs_7_), channel_id=1, source_target_pairs={{0,20},{4,8},{8,28},{12,0},{16,4},{20,24},{24,12},{28,16},{1,21},{... | collective-permute-start | bytes 1179656 | tf_op jit(solution)/shard_map/ppermute | solution.py:128
  48.3 9.2 %collective-permute-start.7 = (bf16[2,256,384]{2,1,0:T(8,128)(2,1)S(1)}, bf16[2,256,384]{2,1,0:T(8,128)(2,1)S(1)}, u32[]{:S(2)}, u32[]{:S(2)}) collective-permute-start(bf16[2,256,384]{2,1,0:T(8,128)(2,1)S(1)} %attention_gradients.3.refs_1_.refs_7_), channel_id=1, source_target_pairs={{0,8},{4,20},{8,0},{12,28},{16,24},{20,4},{24,16},{28,12},{1,9},{5... | collective-permute-start | bytes 1179656 | tf_op jit(solution)/shard_map/ppermute | solution.py:128
  50.9 18.4 %collective-permute-start.15 = (bf16[4,256,384]{2,1,0:T(8,128)(2,1)S(1)}, bf16[4,256,384]{2,1,0:T(8,128)(2,1)S(1)}, u32[]{:S(2)}, u32[]{:S(2)}) collective-permute-start(bf16[4,256,384]{2,1,0:T(8,128)(2,1)S(1)} %collective-permute-done.3.refs_4_.refs_0_.refs_10_), channel_id=1, source_target_pairs={{0,20},{8,28},{16,4},{24,12},{1,21},{9,29},{17,5},{25,13},{2,22},{... | collective-permute-start | bytes 2359304 | tf_op jit(solution)/shard_map/ppermute | solution.py:128
  52.7 16.7 %collective-permute-start.12 = (bf16[4,256,384]{2,1,0:T(8,128)(2,1)S(1)}, bf16[4,256,384]{2,1,0:T(8,128)(2,1)S(1)}, u32[]{:S(2)}, u32[]{:S(2)}) collective-permute-start(bf16[4,256,384]{2,1,0:T(8,128)(2,1)S(1)} %collective-permute-done.3.refs_4_.refs_0_.refs_10_), channel_id=1, source_target_pairs={{4,12},{12,4},{20,28},{28,20},{5,13},{13,5},{21,29},{29,21},{6,14}... | collective-permute-start | bytes 2359304 | tf_op jit(solution)/shard_map/ppermute | solution.py:128
  57.5 11.8 %collective-permute-start.16 = (bf16[2,256,384]{2,1,0:T(8,128)(2,1)S(1)}, bf16[2,256,384]{2,1,0:T(8,128)(2,1)S(1)}, u32[]{:S(2)}, u32[]{:S(2)}) collective-permute-start(bf16[2,256,384]{2,1,0:T(8,128)(2,1)S(1)} %collective-permute-done.7.refs_5_.refs_1_.refs_11_), channel_id=1, source_target_pairs={{0,20},{8,28},{16,4},{24,12},{1,21},{9,29},{17,5},{25,13},{2,22},{... | collective-permute-start | bytes 1179656 | tf_op jit(solution)/shard_map/ppermute | solution.py:128
  63.3 6.0 %collective-permute-start.14 = (bf16[2,256,384]{2,1,0:T(8,128)(2,1)S(1)}, bf16[2,256,384]{2,1,0:T(8,128)(2,1)S(1)}, u32[]{:S(2)}, u32[]{:S(2)}) collective-permute-start(bf16[2,256,384]{2,1,0:T(8,128)(2,1)S(1)} %collective-permute-done.7.refs_5_.refs_1_.refs_11_), channel_id=1, source_target_pairs={{4,12},{12,4},{20,28},{28,20},{5,13},{13,5},{21,29},{29,21},{6,14}... | collective-permute-start | bytes 1179656 | tf_op jit(solution)/shard_map/ppermute | solution.py:128
  72.2 13.9 %collective-permute-start.20 = (bf16[256,768]{1,0:T(8,128)(2,1)S(1)}, bf16[256,768]{1,0:T(8,128)(2,1)S(1)}, u32[]{:S(2)}, u32[]{:S(2)}) collective-permute-start(bf16[256,768]{1,0:T(8,128)(2,1)S(1)} %get-tuple-element.48), channel_id=1, source_target_pairs={{0,1},{3,2},{4,5},{7,6},{8,9},{11,10},{12,13},{15,14},{16,17},{19,... | collective-permute-start | bytes 1179656 | tf_op jit(solution)/shard_map/ppermute | solution.py:566
  73.5 21.0 %collective-permute-start.19 = (bf16[256,768]{1,0:T(8,128)(2,1)S(1)}, bf16[256,768]{1,0:T(8,128)(2,1)S(1)}, u32[]{:S(2)}, u32[]{:S(2)}) collective-permute-start(bf16[256,768]{1,0:T(8,128)(2,1)S(1)} %get-tuple-element.48), channel_id=1, source_target_pairs={{1,2},{2,1},{5,6},{6,5},{9,10},{10,9},{13,14},{14,13},{17,18},{18,... | collective-permute-start | bytes 1179656 | tf_op jit(solution)/shard_map/ppermute | solution.py:568
  75.9 18.6 %collective-permute-start.18 = (bf16[256,768]{1,0:T(8,128)(2,1)S(1)}, bf16[256,768]{1,0:T(8,128)(2,1)S(1)}, u32[]{:S(2)}, u32[]{:S(2)}) collective-permute-start(bf16[256,768]{1,0:T(8,128)(2,1)S(1)} %get-tuple-element.47), channel_id=1, source_target_pairs={{0,1},{1,0},{2,3},{3,2},{4,5},{5,4},{6,7},{7,6},{8,9},{9,8},{10,11... | collective-permute-start | bytes 1179656 | tf_op jit(solution)/shard_map/ppermute | solution.py:567
  76.9 11.5 %collective-permute-start.22 = (bf16[2,256,384]{2,1,0:T(8,128)(2,1)S(1)}, bf16[2,256,384]{2,1,0:T(8,128)(2,1)S(1)}, u32[]{:S(2)}, u32[]{:S(2)}) collective-permute-start(bf16[2,256,384]{2,1,0:T(8,128)(2,1)S(1)} %get-tuple-element.50), channel_id=1, source_target_pairs={{0,8},{4,20},{8,0},{12,28},{16,24},{20,4},{24,16},{28,12},{1,9},{5... | collective-permute-start | bytes 1179656 | tf_op jit(solution)/shard_map/ppermute | solution.py:128
  78.1 10.8 %collective-permute-start.23 = (bf16[2,256,384]{2,1,0:T(8,128)(2,1)S(1)}, bf16[2,256,384]{2,1,0:T(8,128)(2,1)S(1)}, u32[]{:S(2)}, u32[]{:S(2)}) collective-permute-start(bf16[2,256,384]{2,1,0:T(8,128)(2,1)S(1)} %get-tuple-element.51), channel_id=1, source_target_pairs={{0,20},{4,8},{8,28},{12,0},{16,4},{20,24},{24,12},{28,16},{1,21},{... | collective-permute-start | bytes 1179656 | tf_op jit(solution)/shard_map/ppermute | solution.py:128
  86.2 17.1 %collective-permute-start.21 = (bf16[256,768]{1,0:T(8,128)(2,1)S(1)}, bf16[256,768]{1,0:T(8,128)(2,1)S(1)}, u32[]{:S(2)}, u32[]{:S(2)}) collective-permute-start(bf16[256,768]{1,0:T(8,128)(2,1)S(1)} %add_convert_fusion.1), channel_id=1, source_target_pairs={{0,2},{1,3},{2,0},{3,1},{4,6},{5,7},{6,4},{7,5},{8,10},{9,11},{10,... | collective-permute-start | bytes 1179656 | tf_op jit(solution)/shard_map/ppermute | solution.py:570
  88.9 14.5 %collective-permute-start.25 = (bf16[2,256,384]{2,1,0:T(8,128)(2,1)S(1)}, bf16[2,256,384]{2,1,0:T(8,128)(2,1)S(1)}, u32[]{:S(2)}, u32[]{:S(2)}) collective-permute-start(bf16[2,256,384]{2,1,0:T(8,128)(2,1)S(1)} %pad_maximum_fusion.3), channel_id=1, source_target_pairs={{0,28},{8,20},{16,12},{24,4},{1,29},{9,21},{17,13},{25,5},{2,30},{... | collective-permute-start | bytes 1179656 | tf_op jit(solution)/shard_map/ppermute | solution.py:128
  91.9 11.5 %collective-permute-start.24 = (bf16[2,256,384]{2,1,0:T(8,128)(2,1)S(1)}, bf16[2,256,384]{2,1,0:T(8,128)(2,1)S(1)}, u32[]{:S(2)}, u32[]{:S(2)}) collective-permute-start(bf16[2,256,384]{2,1,0:T(8,128)(2,1)S(1)} %pad_maximum_fusion.3), channel_id=1, source_target_pairs={{4,28},{12,20},{20,12},{28,4},{5,29},{13,21},{21,13},{29,5},{6,30}... | collective-permute-start | bytes 1179656 | tf_op jit(solution)/shard_map/ppermute | solution.py:128
  103.5 13.1 %collective-permute-start.26 = (bf16[256,768]{1,0:T(8,128)(2,1)S(1)}, bf16[256,768]{1,0:T(8,128)(2,1)S(1)}, u32[]{:S(2)}, u32[]{:S(2)}) collective-permute-start(bf16[256,768]{1,0:T(8,128)(2,1)S(1)} %add_convert_fusion), channel_id=1, source_target_pairs={{0,0},{1,5},{2,10},{3,15},{4,20},{5,17},{6,30},{7,27},{8,8},{9,13}... | collective-permute-start | bytes 1179656 | tf_op jit(solution)/shard_map/ppermute | solution.py:593
  109.4 9.1 %collective-permute-start.28 = (bf16[384,768]{1,0:T(8,128)(2,1)S(1)}, bf16[384,768]{1,0:T(8,128)(2,1)S(1)}, u32[]{:S(2)}, u32[]{:S(2)}) collective-permute-start(bf16[384,768]{1,0:T(8,128)(2,1)S(1)} %get-tuple-element.55), channel_id=1, source_target_pairs={{0,4},{4,0},{8,12},{12,8},{16,20},{20,16},{24,28},{28,24},{1,5},{5... | collective-permute-start | bytes 1769480 | tf_op jit(solution)/shard_map/ppermute | solution.py:128
  109.5 9.1 %collective-permute-start.29 = (bf16[384,768]{1,0:T(8,128)(2,1)S(1)}, bf16[384,768]{1,0:T(8,128)(2,1)S(1)}, u32[]{:S(2)}, u32[]{:S(2)}) collective-permute-start(bf16[384,768]{1,0:T(8,128)(2,1)S(1)} %get-tuple-element.56), channel_id=1, source_target_pairs={{0,4},{4,0},{8,12},{12,8},{16,20},{20,16},{24,28},{28,24},{1,5},{5... | collective-permute-start | bytes 1769480 | tf_op jit(solution)/shard_map/ppermute | solution.py:128
  110.0 8.6 %collective-permute-start.30 = (bf16[384,768]{1,0:T(8,128)(2,1)S(1)}, bf16[384,768]{1,0:T(8,128)(2,1)S(1)}, u32[]{:S(2)}, u32[]{:S(2)}) collective-permute-start(bf16[384,768]{1,0:T(8,128)(2,1)S(1)} %get-tuple-element.57), channel_id=1, source_target_pairs={{0,4},{4,0},{8,12},{12,8},{16,20},{20,16},{24,28},{28,24},{1,5},{5... | collective-permute-start | bytes 1769480 | tf_op jit(solution)/shard_map/ppermute | solution.py:128
  116.6 13.2 %collective-permute-start.27 = (bf16[256,768]{1,0:T(8,128)(2,1)S(1)}, bf16[256,768]{1,0:T(8,128)(2,1)S(1)}, u32[]{:S(2)}, u32[]{:S(2)}) collective-permute-start(bf16[256,768]{1,0:T(8,128)(2,1)S(1)} %collective-permute-done.26), channel_id=1, source_target_pairs={{0,0},{5,4},{10,8},{15,12},{20,20},{17,16},{30,28},{27,24},{8,9},{... | collective-permute-start | bytes 1179656 | tf_op jit(solution)/shard_map/ppermute | solution.py:602

commit v15 on v13

--- a/solution.py
+++ b/solution.py
@@ -513,7 +513,7 @@
     sets = [((0, 1, 2, 3), (own, mate_in, x_in, cross_in))]
     if shared:
         to_x, own = packed[4:]
-        (to_x,) = after((to_x,), x_in)
+        (to_x,) = after((to_x,), cross_in)
         x_in = moved(to_x, along_x)
         sets.append(((0, 2), (own, moved(own, mate), x_in, moved(x_in, mate))))
 
@@ -538,7 +538,7 @@
     for kept, sources in sets:
         made = attention(turn, kept, sources)
         if own_weights is None:
-            ready = after((query_weight, key_weight, value_weight), made)
+            ready = after((query_weight, key_weight, value_weight), sets[0][1][2])
             own_weights = turned_weights(place, ready)
         (turn,) = after((place,), made, own_weights)
         ahead = moved(made, straight)

time: 131 us -> 134 us (1.023)
  waiting for transfers between devices: 56.6 us -> 63 us
  starting transfers between devices: 43.9 us -> 41.3 us
    ppermute x25, waiting for transfers between devices: 35 us -> 41.5 us  [moved(): return lax.ppermute(value, ('dp', 'view'), pairs)]
    ppermute x25, starting transfers between devices: 31 us -> 28.4 us  [moved(): return lax.ppermute(value, ('dp', 'view'), pairs)]
  transfers between devices with their start and end apart: 31 -> 31, of which waited for: 13 -> 14; matrix products, arithmetic and copies ran while one was open for 1% -> 1% of each run, Pallas kernels for 14% -> 14%
where the time goes in v15:
time: 134 us; the launch traced here: 133 us
  waiting for transfers between devices  63 us (47%)
  starting transfers between devices  41.3 us (31%)
  Pallas kernels  25.7 us (19%)
    ppermute x25, waiting for transfers between devices, moved(): return lax.ppermute(value, ('dp', 'view'), pairs)  41.5 us
    ppermute x25, starting transfers between devices, moved(): return lax.ppermute(value, ('dp', 'view'), pairs)  28.4 us
    pallas_call x2, Pallas kernels, attention(): pl.pallas_call(functools.partial(attention_kernel, HD ** (-0.5), kept), o...  8.76 us
    ppermute x1, waiting for transfers between devices, gather_body(): lax.ppermute(beside, ('dp', 'view', 'head'), [(spot(y ^ v % 2, v ^ z, z),...  8.13 us
    pallas_call x2, Pallas kernels, weight_product(): pl.pallas_call(functools.partial(weight_kernel, mine, mean_scale, len(gra...  7.55 us
    ppermute x1, waiting for transfers between devices, gather_body(): lax.ppermute(total, ('dp', 'view', 'head'), [(spot(y, v, z), spot(y ^ v %...  5.77 us
    ppermute x1, waiting for transfers between devices, gather_body(): across = lax.ppermute(joint, 'head', [(z, z ^ 2) for z in range(groups)])  5.06 us
    pallas_call x1, Pallas kernels, input_product(): pl.pallas_call(functools.partial(input_kernel, len(grads) // 6), out_shap...  4.66 us
  transfers between devices with their start and end apart: 31, of which 14 were waited for; matrix products, arithmetic and copies ran while one was open for 1% of the time, Pallas kernels for 14%

profile of v15, /device:TPU:26, one launch (start us, length us, event | category | flops | bytes accessed | tf_op | source)
XLA Modules:
  0.0 133.2 jit_solution(14891342592899675378)
XLA Ops:
  0.7 0.7 pad_add_fusion.place_ref
  1.3 2.8 %pack_heads.1 = (bf16[1,1040,128]{2,1,0:T(8,128)(2,1)}, bf16[1,1040,128]{2,1,0:T(8,128)(2,1)}, bf16[1,1040,128]{2,1,0:T(8,128)(2,1)}, bf16[1,1040,128]{2,1,0:T(8...) custom-call(s32[4]{0:T(128)} %pad_add_fusion.place_ref, s32[1,2]{1,0:T(1,128)} %links_ref.1, ...), custom_call_target="tpu_custom_call" | custom-call | tf_op jit(solution)/shard_map/pack_heads/pallas_call | solution.py:215
  4.1 1.5 %collective-permute-start.1 = (bf16[1,1040,128]{2,1,0:T(8,128)(2,1)}, bf16[1,1040,128]{2,1,0:T(8,128)(2,1)S(1)}, u32[]{:S(2)}, u32[]{:S(2)}) collective-permute-start(bf16[1,1040,128]{2,1,0:T(8,128)(2,1)} %get-tuple-element.35), channel_id=1, source_target_pairs={{0,8},{4,12},{8,0},{12,4},{16,24},{20,28},{24,16},{28,20},{1,9},{5... | collective-permute-start | bytes 798728 | tf_op jit(solution)/shard_map/ppermute | solution.py:128
  5.6 7.4 %collective-permute-done.2.far_in = bf16[1,1040,128]{2,1,0:T(8,128)(2,1)S(1)} collective-permute-done((bf16[1,1040,128]{2,1,0:T(8,128)(2,1)}, bf16[1,1040,128]{2,1,0:T(8,128)(2,1)S(1)}, u32[]{:S(2)}, u32[]{:S(2)}) %collective-permute-start.2) | collective-permute-done | bytes 266272 | tf_op jit(solution)/shard_map/ppermute | solution.py:128
  13.0 0.5 collective-permute-start.4
  13.5 0.5 collective-permute-start.3
  14.1 0.3 dynamic-slice_bitcast_fusion.1
  14.3 0.0 copy-start.5
  14.4 4.4 %collective-permute-done.1.x_in = bf16[1,1040,128]{2,1,0:T(8,128)(2,1)S(1)} collective-permute-done((bf16[1,1040,128]{2,1,0:T(8,128)(2,1)}, bf16[1,1040,128]{2,1,0:T(8,128)(2,1)S(1)}, u32[]{:S(2)}, u32[]{:S(2)}) %collective-permute-start.1) | collective-permute-done | bytes 266272 | tf_op jit(solution)/shard_map/ppermute | solution.py:128
  18.8 1.1 turn_weights.1.own_ref
  19.8 0.2 collective-permute-start.17
  20.0 4.5 %collective-permute-done.4.x_in = bf16[1,1040,128]{2,1,0:T(8,128)(2,1)S(1)} collective-permute-done((bf16[1,1040,128]{2,1,0:T(8,128)(2,1)}, bf16[1,1040,128]{2,1,0:T(8,128)(2,1)S(1)}, u32[]{:S(2)}, u32[]{:S(2)}) %collective-permute-start.4) | collective-permute-done | bytes 266272 | tf_op jit(solution)/shard_map/ppermute | solution.py:128
  24.4 0.1 collective-permute-start.5
  24.6 4.4 %attention_gradients.2.refs_0_.refs_6_ = bf16[4,256,384]{2,1,0:T(8,128)(2,1)S(1)} custom-call(s32[4]{0:T(128)S(1)} %copy-done.3, bf16[1,1040,128]{2,1,0:T(8,128)(2,1)S(1)} %copy-done.5, bf16[1,1040,128]{2,1,0:T(8,128)(2,1)S(1)} %collective-permute-done.mate_in, bf16[1,1040,128]{2,1,0:T(8,128)(2,1)S(1)} %collective-permute-done.1.x_in, ...), custom_call_target="tpu_custom_call" | custom-call | flops 2013265920 | bytes 1835008 | tf_op jit(solution)/shard_map/attention_gradients/pallas_call | solution.py:304
  29.0 1.6 %collective-permute-start.10 = (bf16[4,256,384]{2,1,0:T(8,128)(2,1)S(1)}, bf16[4,256,384]{2,1,0:T(8,128)(2,1)S(1)}, u32[]{:S(2)}, u32[]{:S(2)}) collective-permute-start(bf16[4,256,384]{2,1,0:T(8,128)(2,1)S(1)} %attention_gradients.2.refs_0_.refs_6_), channel_id=1, source_target_pairs={{0,20},{4,8},{8,28},{12,0},{16,4},{20,24},{24,12},{28,16},{1,21},{... | collective-permute-start | bytes 2359304 | tf_op jit(solution)/shard_map/ppermute | solution.py:128
  30.6 0.5 collective-permute-start.8
  31.1 1.3 collective-permute-start.6
  32.5 1.3 collective-permute-start.12
  33.8 4.3 %attention_gradients.3.refs_1_.refs_7_ = bf16[2,256,384]{2,1,0:T(8,128)(2,1)S(1)} custom-call(s32[4]{0:T(128)S(1)} %copy-done.3, bf16[1,1040,128]{2,1,0:T(8,128)(2,1)S(1)} %copy-done.4, bf16[1,1040,128]{2,1,0:T(8,128)(2,1)S(1)} %collective-permute-done.3.mate_in, bf16[1,1040,128]{2,1,0:T(8,128)(2,1)S(1)} %collective-permute-done.4.x_in, ...), custom_call_target="tpu_custom_call" | custom-call | flops 2013265920 | bytes 1835008 | tf_op jit(solution)/shard_map/attention_gradients/pallas_call | solution.py:304
  38.1 0.0 collective-permute-done.12.refs_1_
  38.1 1.4 %collective-permute-start.11 = (bf16[2,256,384]{2,1,0:T(8,128)(2,1)S(1)}, bf16[2,256,384]{2,1,0:T(8,128)(2,1)S(1)}, u32[]{:S(2)}, u32[]{:S(2)}) collective-permute-start(bf16[2,256,384]{2,1,0:T(8,128)(2,1)S(1)} %attention_gradients.3.refs_1_.refs_7_), channel_id=1, source_target_pairs={{0,20},{4,8},{8,28},{12,0},{16,4},{20,24},{24,12},{28,16},{1,21},{... | collective-permute-start | bytes 1179656 | tf_op jit(solution)/shard_map/ppermute | solution.py:128
  39.5 0.1 pad_maximum_fusion.1
  39.6 8.5 %collective-permute-done.10.refs_6_.refs_12_ = bf16[4,256,384]{2,1,0:T(8,128)(2,1)S(1)} collective-permute-done((bf16[4,256,384]{2,1,0:T(8,128)(2,1)S(1)}, bf16[4,256,384]{2,1,0:T(8,128)(2,1)S(1)}, u32[]{:S(2)}, u32[]{:S(2)}) %collective-permute-start.10) | collective-permute-done | bytes 786464 | tf_op jit(solution)/shard_map/ppermute | solution.py:128
  48.2 0.3 collective-permute-start.9
  48.5 2.6 %collective-permute-done.8.refs_4_.refs_10_ = bf16[4,256,384]{2,1,0:T(8,128)(2,1)S(1)} collective-permute-done((bf16[4,256,384]{2,1,0:T(8,128)(2,1)S(1)}, bf16[4,256,384]{2,1,0:T(8,128)(2,1)S(1)}, u32[]{:S(2)}, u32[]{:S(2)}) %collective-permute-start.8) | collective-permute-done | bytes 786464 | tf_op jit(solution)/shard_map/ppermute | solution.py:128
  51.1 1.3 collective-permute-start.7
  52.4 3.2 %collective-permute-start.15 = (bf16[4,256,384]{2,1,0:T(8,128)(2,1)S(1)}, bf16[4,256,384]{2,1,0:T(8,128)(2,1)S(1)}, u32[]{:S(2)}, u32[]{:S(2)}) collective-permute-start(bf16[4,256,384]{2,1,0:T(8,128)(2,1)S(1)} %collective-permute-done.8.refs_4_.refs_10_), channel_id=1, source_target_pairs={{0,20},{8,28},{16,4},{24,12},{1,21},{9,29},{17,5},{25,13},{2,22},{... | collective-permute-start | bytes 2359304 | tf_op jit(solution)/shard_map/ppermute | solution.py:128
  55.5 0.0 collective-permute-done.11.refs_7_.refs_13_
  55.5 0.7 collective-permute-start.13
  56.3 1.1 collective-permute-done.9.refs_5_.refs_11_
  57.3 0.0 collective-permute-done.7.refs_3_.refs_9_
  57.3 3.7 %collective-permute-start.16 = (bf16[2,256,384]{2,1,0:T(8,128)(2,1)S(1)}, bf16[2,256,384]{2,1,0:T(8,128)(2,1)S(1)}, u32[]{:S(2)}, u32[]{:S(2)}) collective-permute-start(bf16[2,256,384]{2,1,0:T(8,128)(2,1)S(1)} %collective-permute-done.9.refs_5_.refs_11_), channel_id=1, source_target_pairs={{0,20},{8,28},{16,4},{24,12},{1,21},{9,29},{17,5},{25,13},{2,22},{... | collective-permute-start | bytes 1179656 | tf_op jit(solution)/shard_map/ppermute | solution.py:128
  61.1 0.7 collective-permute-start.14
  61.8 0.9 join_weights.1.refs_12_
  62.6 6.6 %collective-permute-done.16.refs_11_.refs_17_ = bf16[2,256,384]{2,1,0:T(8,128)(2,1)S(1)} collective-permute-done((bf16[2,256,384]{2,1,0:T(8,128)(2,1)S(1)}, bf16[2,256,384]{2,1,0:T(8,128)(2,1)S(1)}, u32[]{:S(2)}, u32[]{:S(2)}) %collective-permute-start.16) | collective-permute-done | bytes 393248 | tf_op jit(solution)/shard_map/ppermute | solution.py:128
  69.2 0.0 collective-permute-done.15.refs_10_.refs_16_
  69.2 0.0 collective-permute-done.13.refs_8_.refs_14_
  69.2 4.7 %input_gradient.1 = (bf16[256,768]{1,0:T(8,128)(2,1)S(1)}, bf16[256,768]{1,0:T(8,128)(2,1)S(1)}, bf16[256,768]{1,0:T(8,128)(2,1)S(1)}, bf16[256,768]{1,0:T(8,128)(2,1)S(1)}) custom-call(s32[4]{0:T(128)S(1)} %copy-done.3, bf16[4,256,384]{2,1,0:T(8,128)(2,1)S(1)} %attention_gradients.2.refs_0_.refs_6_, ...), custom_call_target="tpu_custom_call" | custom-call | flops 3623878656 | bytes 9830400 | tf_op jit(solution)/shard_map/input_gradient/pallas_call | solution.py:408
  73.9 2.4 %collective-permute-start.20 = (bf16[256,768]{1,0:T(8,128)(2,1)S(1)}, bf16[256,768]{1,0:T(8,128)(2,1)S(1)}, u32[]{:S(2)}, u32[]{:S(2)}) collective-permute-start(bf16[256,768]{1,0:T(8,128)(2,1)S(1)} %get-tuple-element.48), channel_id=1, source_target_pairs={{0,1},{3,2},{4,5},{7,6},{8,9},{11,10},{12,13},{15,14},{16,17},{19,... | collective-permute-start | bytes 1179656 | tf_op jit(solution)/shard_map/ppermute | solution.py:556
  76.3 0.7 collective-permute-start.19
  77.0 1.1 collective-permute-start.18
  78.1 0.9 collective-permute-start.22
  79.0 2.5 %collective-permute-start.23 = (bf16[2,256,384]{2,1,0:T(8,128)(2,1)S(1)}, bf16[2,256,384]{2,1,0:T(8,128)(2,1)S(1)}, u32[]{:S(2)}, u32[]{:S(2)}) collective-permute-start(bf16[2,256,384]{2,1,0:T(8,128)(2,1)S(1)} %get-tuple-element.51), channel_id=1, source_target_pairs={{0,20},{4,8},{8,28},{12,0},{16,4},{20,24},{24,12},{28,16},{1,21},{... | collective-permute-start | bytes 1179656 | tf_op jit(solution)/shard_map/ppermute | solution.py:128
  81.5 2.6 %collective-permute-done.20 = bf16[256,768]{1,0:T(8,128)(2,1)S(1)} collective-permute-done((bf16[256,768]{1,0:T(8,128)(2,1)S(1)}, bf16[256,768]{1,0:T(8,128)(2,1)S(1)}, u32[]{:S(2)}, u32[]{:S(2)}) %collective-permute-start.20) | collective-permute-done | bytes 393248 | tf_op jit(solution)/shard_map/ppermute | solution.py:556
  84.1 0.1 add_convert_fusion.1
  84.2 2.4 %collective-permute-start.21 = (bf16[256,768]{1,0:T(8,128)(2,1)S(1)}, bf16[256,768]{1,0:T(8,128)(2,1)S(1)}, u32[]{:S(2)}, u32[]{:S(2)}) collective-permute-start(bf16[256,768]{1,0:T(8,128)(2,1)S(1)} %add_convert_fusion.1), channel_id=1, source_target_pairs={{0,2},{1,3},{2,0},{3,1},{4,6},{5,7},{6,4},{7,5},{8,10},{9,11},{10,... | collective-permute-start | bytes 1179656 | tf_op jit(solution)/shard_map/ppermute | solution.py:560
  86.6 1.4 %collective-permute-done.22.refs_2_ = bf16[2,256,384]{2,1,0:T(8,128)(2,1)S(1)} collective-permute-done((bf16[2,256,384]{2,1,0:T(8,128)(2,1)S(1)}, bf16[2,256,384]{2,1,0:T(8,128)(2,1)S(1)}, u32[]{:S(2)}, u32[]{:S(2)}) %collective-permute-start.22) | collective-permute-done | bytes 393248 | tf_op jit(solution)/shard_map/ppermute | solution.py:128
  88.0 2.2 %collective-permute-done.23.refs_3_ = bf16[2,256,384]{2,1,0:T(8,128)(2,1)S(1)} collective-permute-done((bf16[2,256,384]{2,1,0:T(8,128)(2,1)S(1)}, bf16[2,256,384]{2,1,0:T(8,128)(2,1)S(1)}, u32[]{:S(2)}, u32[]{:S(2)}) %collective-permute-start.23) | collective-permute-done | bytes 393248 | tf_op jit(solution)/shard_map/ppermute | solution.py:128
  90.2 5.0 %collective-permute-start.25 = (bf16[2,256,384]{2,1,0:T(8,128)(2,1)S(1)}, bf16[2,256,384]{2,1,0:T(8,128)(2,1)S(1)}, u32[]{:S(2)}, u32[]{:S(2)}) collective-permute-start(bf16[2,256,384]{2,1,0:T(8,128)(2,1)S(1)} %pad_maximum_fusion.3), channel_id=1, source_target_pairs={{0,28},{8,20},{16,12},{24,4},{1,29},{9,21},{17,13},{25,5},{2,30},{... | collective-permute-start | bytes 1179656 | tf_op jit(solution)/shard_map/ppermute | solution.py:128
  95.2 0.7 collective-permute-start.24
  95.9 0.0 collective-permute-done.19
  95.9 5.1 %collective-permute-done.21 = bf16[256,768]{1,0:T(8,128)(2,1)S(1)} collective-permute-done((bf16[256,768]{1,0:T(8,128)(2,1)S(1)}, bf16[256,768]{1,0:T(8,128)(2,1)S(1)}, u32[]{:S(2)}, u32[]{:S(2)}) %collective-permute-start.21) | collective-permute-done | bytes 393248 | tf_op jit(solution)/shard_map/ppermute | solution.py:560
  101.0 0.2 add_convert_fusion
  101.2 2.8 %collective-permute-done.25.refs_5_ = bf16[2,256,384]{2,1,0:T(8,128)(2,1)S(1)} collective-permute-done((bf16[2,256,384]{2,1,0:T(8,128)(2,1)S(1)}, bf16[2,256,384]{2,1,0:T(8,128)(2,1)S(1)}, u32[]{:S(2)}, u32[]{:S(2)}) %collective-permute-start.25) | collective-permute-done | bytes 393248 | tf_op jit(solution)/shard_map/ppermute | solution.py:128
  104.0 4.4 %collective-permute-start.26 = (bf16[256,768]{1,0:T(8,128)(2,1)S(1)}, bf16[256,768]{1,0:T(8,128)(2,1)S(1)}, u32[]{:S(2)}, u32[]{:S(2)}) collective-permute-start(bf16[256,768]{1,0:T(8,128)(2,1)S(1)} %add_convert_fusion), channel_id=1, source_target_pairs={{0,0},{1,5},{2,10},{3,15},{4,20},{5,17},{6,30},{7,27},{8,8},{9,13}... | collective-permute-start | bytes 1179656 | tf_op jit(solution)/shard_map/ppermute | solution.py:583
  108.4 2.8 %weight_gradient_mate.1 = (bf16[384,768]{1,0:T(8,128)(2,1)S(1)}, bf16[384,768]{1,0:T(8,128)(2,1)S(1)}, bf16[384,768]{1,0:T(8,128)(2,1)S(1)}) custom-call(s32[4]{0:T(128)S(1)} %copy-done.3, bf16[2,256,384]{2,1,0:T(8,128)(2,1)S(1)} %pad_maximum_fusion.refs_0_, bf16[2,256,384]{2,1,0:T(8,128)(2,1)S(1)} %collective-permute-done.12.refs_1_, ...), custom_call_target="tpu_custom_call" | custom-call | flops 1811939328 | bytes 9043968 | tf_op jit(solution)/shard_map/weight_gradient_mate/pallas_call | solution.py:457
  111.3 0.1 collective-permute-start.28
  111.4 0.5 collective-permute-start.29
  111.9 0.1 collective-permute-start.30
  111.9 5.8 %collective-permute-done.26 = bf16[256,768]{1,0:T(8,128)(2,1)S(1)} collective-permute-done((bf16[256,768]{1,0:T(8,128)(2,1)S(1)}, bf16[256,768]{1,0:T(8,128)(2,1)S(1)}, u32[]{:S(2)}, u32[]{:S(2)}) %collective-permute-start.26) | collective-permute-done | bytes 393248 | tf_op jit(solution)/shard_map/ppermute | solution.py:583
  117.7 1.9 %collective-permute-start.27 = (bf16[256,768]{1,0:T(8,128)(2,1)S(1)}, bf16[256,768]{1,0:T(8,128)(2,1)S(1)}, u32[]{:S(2)}, u32[]{:S(2)}) collective-permute-start(bf16[256,768]{1,0:T(8,128)(2,1)S(1)} %collective-permute-done.26), channel_id=1, source_target_pairs={{0,0},{5,4},{10,8},{15,12},{20,20},{17,16},{30,28},{27,24},{8,9},{... | collective-permute-start | bytes 1179656 | tf_op jit(solution)/shard_map/ppermute | solution.py:592
  119.7 4.7 %weight_gradient_own.1 = (f32[384,768]{1,0:T(8,128)}, f32[384,768]{1,0:T(8,128)}, f32[384,768]{1,0:T(8,128)}) custom-call(s32[4]{0:T(128)S(1)} %copy-done.3, bf16[2,256,384]{2,1,0:T(8,128)(2,1)S(1)} %pad_maximum_fusion.refs_0_, bf16[2,256,384]{2,1,0:T(8,128)(2,1)S(1)} %collective-permute-done.12.refs_1_, ...), custom_call_target="tpu_custom_call" | custom-call | flops 1811939328 | bytes 9043968 | tf_op jit(solution)/shard_map/weight_gradient_own/pallas_call | solution.py:457
  124.3 8.1 %collective-permute-done.27 = bf16[256,768]{1,0:T(8,128)(2,1)S(1)} collective-permute-done((bf16[256,768]{1,0:T(8,128)(2,1)S(1)}, bf16[256,768]{1,0:T(8,128)(2,1)S(1)}, u32[]{:S(2)}, u32[]{:S(2)}) %collective-permute-start.27) | collective-permute-done | bytes 393248 | tf_op jit(solution)/shard_map/ppermute | solution.py:592
  132.5 0.7 copy.14
  (28 shorter events, 0.2 us)
Async XLA Ops:
  0.6 13.4 %copy-start.6 = (bf16[1,1,256,3072]{3,2,1,0:T(8,128)(2,1)S(1)}, bf16[1,1,256,3072]{3,2,1,0:T(8,128)(2,1)}, u32[]{:S(2)}) copy-start(bf16[1,1,256,3072]{3,2,1,0:T(8,128)(2,1)} %param.9) | copy-start | bytes 4718596
  4.1 8.9 %collective-permute-start.2 = (bf16[1,1040,128]{2,1,0:T(8,128)(2,1)}, bf16[1,1040,128]{2,1,0:T(8,128)(2,1)S(1)}, u32[]{:S(2)}, u32[]{:S(2)}) collective-permute-start(bf16[1,1040,128]{2,1,0:T(8,128)(2,1)} %get-tuple-element.36), channel_id=1, source_target_pairs={{0,12},{4,8},{8,4},{12,0},{16,28},{20,24},{24,20},{28,16},{1,13},{... | collective-permute-start | bytes 798728 | tf_op jit(solution)/shard_map/ppermute | solution.py:128
  4.1 14.6 %collective-permute-start.1 = (bf16[1,1040,128]{2,1,0:T(8,128)(2,1)}, bf16[1,1040,128]{2,1,0:T(8,128)(2,1)S(1)}, u32[]{:S(2)}, u32[]{:S(2)}) collective-permute-start(bf16[1,1040,128]{2,1,0:T(8,128)(2,1)} %get-tuple-element.35), channel_id=1, source_target_pairs={{0,8},{4,12},{8,0},{12,4},{16,24},{20,28},{24,16},{28,20},{1,9},{5... | collective-permute-start | bytes 798728 | tf_op jit(solution)/shard_map/ppermute | solution.py:128
  13.0 11.4 %collective-permute-start.4 = (bf16[1,1040,128]{2,1,0:T(8,128)(2,1)}, bf16[1,1040,128]{2,1,0:T(8,128)(2,1)S(1)}, u32[]{:S(2)}, u32[]{:S(2)}) collective-permute-start(bf16[1,1040,128]{2,1,0:T(8,128)(2,1)} %get-tuple-element.43), channel_id=1, source_target_pairs={{0,8},{4,12},{8,0},{12,4},{16,24},{20,28},{24,16},{28,20},{1,9},{5... | collective-permute-start | bytes 798728 | tf_op jit(solution)/shard_map/ppermute | solution.py:128
  13.5 11.0 %collective-permute-start = (bf16[1,1040,128]{2,1,0:T(8,128)(2,1)}, bf16[1,1040,128]{2,1,0:T(8,128)(2,1)S(1)}, u32[]{:S(2)}, u32[]{:S(2)}) collective-permute-start(bf16[1,1040,128]{2,1,0:T(8,128)(2,1)} %get-tuple-element.34), channel_id=1, source_target_pairs={{0,4},{4,0},{8,12},{12,8},{16,20},{20,16},{24,28},{28,24},{1,5},{5... | collective-permute-start | bytes 798728 | tf_op jit(solution)/shard_map/ppermute | solution.py:128
  13.5 17.6 %collective-permute-start.3 = (bf16[1,1040,128]{2,1,0:T(8,128)(2,1)}, bf16[1,1040,128]{2,1,0:T(8,128)(2,1)S(1)}, u32[]{:S(2)}, u32[]{:S(2)}) collective-permute-start(bf16[1,1040,128]{2,1,0:T(8,128)(2,1)} %get-tuple-element.41.own), channel_id=1, source_target_pairs={{0,4},{4,0},{8,12},{12,8},{16,20},{20,16},{24,28},{28,24},{1,5},{5... | collective-permute-start | bytes 798728 | tf_op jit(solution)/shard_map/ppermute | solution.py:128
  14.0 4.7 %copy-start = (bf16[384,768]{1,0:T(8,128)(2,1)S(1)}, bf16[384,768]{1,0:T(8,128)(2,1)}, u32[]{:S(2)}) copy-start(bf16[384,768]{1,0:T(8,128)(2,1)} %q_ref) | copy-start | bytes 1769476
  14.0 4.7 %copy-start.1 = (bf16[384,768]{1,0:T(8,128)(2,1)S(1)}, bf16[384,768]{1,0:T(8,128)(2,1)}, u32[]{:S(2)}) copy-start(bf16[384,768]{1,0:T(8,128)(2,1)} %k_ref) | copy-start | bytes 1769476
  14.0 4.7 %copy-start.2 = (bf16[384,768]{1,0:T(8,128)(2,1)S(1)}, bf16[384,768]{1,0:T(8,128)(2,1)}, u32[]{:S(2)}) copy-start(bf16[384,768]{1,0:T(8,128)(2,1)} %v_ref) | copy-start | bytes 1769476
  14.1 4.7 %copy-start.3 = (s32[4]{0:T(128)S(1)}, s32[4]{0:T(128)}, u32[]{:S(2)}) copy-start(s32[4]{0:T(128)} %pad_add_fusion.place_ref) | copy-start | bytes 52
  14.3 10.2 %copy-start.5 = (bf16[1,1040,128]{2,1,0:T(8,128)(2,1)S(1)}, bf16[1,1040,128]{2,1,0:T(8,128)(2,1)}, u32[]{:S(2)}) copy-start(bf16[1,1040,128]{2,1,0:T(8,128)(2,1)} %get-tuple-element.33.own) | copy-start | bytes 798724
  19.8 41.9 %collective-permute-start.17 = (bf16[2304,384]{1,0:T(8,128)(2,1)S(1)}, bf16[2304,384]{1,0:T(8,128)(2,1)S(1)}, u32[]{:S(2)}, u32[]{:S(2)}) collective-permute-start(bf16[2304,384]{1,0:T(8,128)(2,1)S(1)} %turn_weights.1.own_ref), channel_id=1, source_target_pairs={{0,4},{4,0},{8,12},{12,8},{16,20},{20,16},{24,28},{28,24},{1,5},{5... | collective-permute-start | bytes 5308424 | tf_op jit(solution)/shard_map/ppermute | solution.py:128
  24.4 8.0 %collective-permute-start.5 = (bf16[1,1040,128]{2,1,0:T(8,128)(2,1)S(1)}, bf16[1,1040,128]{2,1,0:T(8,128)(2,1)S(1)}, u32[]{:S(2)}, u32[]{:S(2)}) collective-permute-start(bf16[1,1040,128]{2,1,0:T(8,128)(2,1)S(1)} %collective-permute-done.4.x_in), channel_id=1, source_target_pairs={{0,4},{4,0},{8,12},{12,8},{16,20},{20,16},{24,28},{28,24},{1,5},{5... | collective-permute-start | bytes 798728 | tf_op jit(solution)/shard_map/ppermute | solution.py:128
  24.6 9.2 %copy-start.4 = (bf16[1,1040,128]{2,1,0:T(8,128)(2,1)S(1)}, bf16[1,1040,128]{2,1,0:T(8,128)(2,1)}, u32[]{:S(2)}) copy-start(bf16[1,1040,128]{2,1,0:T(8,128)(2,1)} %get-tuple-element.41.own) | copy-start | bytes 798724
  29.0 19.2 %collective-permute-start.10 = (bf16[4,256,384]{2,1,0:T(8,128)(2,1)S(1)}, bf16[4,256,384]{2,1,0:T(8,128)(2,1)S(1)}, u32[]{:S(2)}, u32[]{:S(2)}) collective-permute-start(bf16[4,256,384]{2,1,0:T(8,128)(2,1)S(1)} %attention_gradients.2.refs_0_.refs_6_), channel_id=1, source_target_pairs={{0,20},{4,8},{8,28},{12,0},{16,4},{20,24},{24,12},{28,16},{1,21},{... | collective-permute-start | bytes 2359304 | tf_op jit(solution)/shard_map/ppermute | solution.py:128
  30.6 20.5 %collective-permute-start.8 = (bf16[4,256,384]{2,1,0:T(8,128)(2,1)S(1)}, bf16[4,256,384]{2,1,0:T(8,128)(2,1)S(1)}, u32[]{:S(2)}, u32[]{:S(2)}) collective-permute-start(bf16[4,256,384]{2,1,0:T(8,128)(2,1)S(1)} %attention_gradients.2.refs_0_.refs_6_), channel_id=1, source_target_pairs={{0,8},{4,20},{8,0},{12,28},{16,24},{20,4},{24,16},{28,12},{1,9},{5... | collective-permute-start | bytes 2359304 | tf_op jit(solution)/shard_map/ppermute | solution.py:128
  31.1 21.2 %collective-permute-start.6 = (bf16[4,256,384]{2,1,0:T(8,128)(2,1)S(1)}, bf16[4,256,384]{2,1,0:T(8,128)(2,1)S(1)}, u32[]{:S(2)}, u32[]{:S(2)}) collective-permute-start(bf16[4,256,384]{2,1,0:T(8,128)(2,1)S(1)} %attention_gradients.2.refs_0_.refs_6_), channel_id=1, source_target_pairs={{4,0},{12,8},{20,16},{28,24},{5,1},{13,9},{21,17},{29,25},{6,2},{1... | collective-permute-start | bytes 2359304 | tf_op jit(solution)/shard_map/ppermute | solution.py:128
  32.5 5.6 %collective-permute-start.12 = (bf16[2,256,384]{2,1,0:T(8,128)(2,1)S(1)}, bf16[2,256,384]{2,1,0:T(8,128)(2,1)S(1)}, u32[]{:S(2)}, u32[]{:S(2)}) collective-permute-start(bf16[2,256,384]{2,1,0:T(8,128)(2,1)S(1)} %pad_maximum_fusion.refs_0_), channel_id=1, source_target_pairs={{4,0},{12,8},{20,16},{28,24},{5,1},{13,9},{21,17},{29,25},{6,2},{1... | collective-permute-start | bytes 1179656 | tf_op jit(solution)/shard_map/ppermute | solution.py:128
  38.1 17.4 %collective-permute-start.11 = (bf16[2,256,384]{2,1,0:T(8,128)(2,1)S(1)}, bf16[2,256,384]{2,1,0:T(8,128)(2,1)S(1)}, u32[]{:S(2)}, u32[]{:S(2)}) collective-permute-start(bf16[2,256,384]{2,1,0:T(8,128)(2,1)S(1)} %attention_gradients.3.refs_1_.refs_7_), channel_id=1, source_target_pairs={{0,20},{4,8},{8,28},{12,0},{16,4},{20,24},{24,12},{28,16},{1,21},{... | collective-permute-start | bytes 1179656 | tf_op jit(solution)/shard_map/ppermute | solution.py:128
  48.2 9.2 %collective-permute-start.9 = (bf16[2,256,384]{2,1,0:T(8,128)(2,1)S(1)}, bf16[2,256,384]{2,1,0:T(8,128)(2,1)S(1)}, u32[]{:S(2)}, u32[]{:S(2)}) collective-permute-start(bf16[2,256,384]{2,1,0:T(8,128)(2,1)S(1)} %attention_gradients.3.refs_1_.refs_7_), channel_id=1, source_target_pairs={{0,8},{4,20},{8,0},{12,28},{16,24},{20,4},{24,16},{28,12},{1,9},{5... | collective-permute-start | bytes 1179656 | tf_op jit(solution)/shard_map/ppermute | solution.py:128
  51.1 6.3 %collective-permute-start.7 = (bf16[2,256,384]{2,1,0:T(8,128)(2,1)S(1)}, bf16[2,256,384]{2,1,0:T(8,128)(2,1)S(1)}, u32[]{:S(2)}, u32[]{:S(2)}) collective-permute-start(bf16[2,256,384]{2,1,0:T(8,128)(2,1)S(1)} %attention_gradients.3.refs_1_.refs_7_), channel_id=1, source_target_pairs={{4,0},{12,8},{20,16},{28,24},{5,1},{13,9},{21,17},{29,25},{6,2},{1... | collective-permute-start | bytes 1179656 | tf_op jit(solution)/shard_map/ppermute | solution.py:128
  52.4 16.9 %collective-permute-start.15 = (bf16[4,256,384]{2,1,0:T(8,128)(2,1)S(1)}, bf16[4,256,384]{2,1,0:T(8,128)(2,1)S(1)}, u32[]{:S(2)}, u32[]{:S(2)}) collective-permute-start(bf16[4,256,384]{2,1,0:T(8,128)(2,1)S(1)} %collective-permute-done.8.refs_4_.refs_10_), channel_id=1, source_target_pairs={{0,20},{8,28},{16,4},{24,12},{1,21},{9,29},{17,5},{25,13},{2,22},{... | collective-permute-start | bytes 2359304 | tf_op jit(solution)/shard_map/ppermute | solution.py:128
  55.5 13.7 %collective-permute-start.13 = (bf16[4,256,384]{2,1,0:T(8,128)(2,1)S(1)}, bf16[4,256,384]{2,1,0:T(8,128)(2,1)S(1)}, u32[]{:S(2)}, u32[]{:S(2)}) collective-permute-start(bf16[4,256,384]{2,1,0:T(8,128)(2,1)S(1)} %collective-permute-done.8.refs_4_.refs_10_), channel_id=1, source_target_pairs={{4,12},{12,4},{20,28},{28,20},{5,13},{13,5},{21,29},{29,21},{6,14}... | collective-permute-start | bytes 2359304 | tf_op jit(solution)/shard_map/ppermute | solution.py:128
  57.3 11.9 %collective-permute-start.16 = (bf16[2,256,384]{2,1,0:T(8,128)(2,1)S(1)}, bf16[2,256,384]{2,1,0:T(8,128)(2,1)S(1)}, u32[]{:S(2)}, u32[]{:S(2)}) collective-permute-start(bf16[2,256,384]{2,1,0:T(8,128)(2,1)S(1)} %collective-permute-done.9.refs_5_.refs_11_), channel_id=1, source_target_pairs={{0,20},{8,28},{16,4},{24,12},{1,21},{9,29},{17,5},{25,13},{2,22},{... | collective-permute-start | bytes 1179656 | tf_op jit(solution)/shard_map/ppermute | solution.py:128
  61.1 8.2 %collective-permute-start.14 = (bf16[2,256,384]{2,1,0:T(8,128)(2,1)S(1)}, bf16[2,256,384]{2,1,0:T(8,128)(2,1)S(1)}, u32[]{:S(2)}, u32[]{:S(2)}) collective-permute-start(bf16[2,256,384]{2,1,0:T(8,128)(2,1)S(1)} %collective-permute-done.9.refs_5_.refs_11_), channel_id=1, source_target_pairs={{4,12},{12,4},{20,28},{28,20},{5,13},{13,5},{21,29},{29,21},{6,14}... | collective-permute-start | bytes 1179656 | tf_op jit(solution)/shard_map/ppermute | solution.py:128
  73.9 10.2 %collective-permute-start.20 = (bf16[256,768]{1,0:T(8,128)(2,1)S(1)}, bf16[256,768]{1,0:T(8,128)(2,1)S(1)}, u32[]{:S(2)}, u32[]{:S(2)}) collective-permute-start(bf16[256,768]{1,0:T(8,128)(2,1)S(1)} %get-tuple-element.48), channel_id=1, source_target_pairs={{0,1},{3,2},{4,5},{7,6},{8,9},{11,10},{12,13},{15,14},{16,17},{19,... | collective-permute-start | bytes 1179656 | tf_op jit(solution)/shard_map/ppermute | solution.py:556
  76.3 19.6 %collective-permute-start.19 = (bf16[256,768]{1,0:T(8,128)(2,1)S(1)}, bf16[256,768]{1,0:T(8,128)(2,1)S(1)}, u32[]{:S(2)}, u32[]{:S(2)}) collective-permute-start(bf16[256,768]{1,0:T(8,128)(2,1)S(1)} %get-tuple-element.48), channel_id=1, source_target_pairs={{1,2},{2,1},{5,6},{6,5},{9,10},{10,9},{13,14},{14,13},{17,18},{18,... | collective-permute-start | bytes 1179656 | tf_op jit(solution)/shard_map/ppermute | solution.py:558
  77.0 18.9 %collective-permute-start.18 = (bf16[256,768]{1,0:T(8,128)(2,1)S(1)}, bf16[256,768]{1,0:T(8,128)(2,1)S(1)}, u32[]{:S(2)}, u32[]{:S(2)}) collective-permute-start(bf16[256,768]{1,0:T(8,128)(2,1)S(1)} %get-tuple-element.47), channel_id=1, source_target_pairs={{0,1},{1,0},{2,3},{3,2},{4,5},{5,4},{6,7},{7,6},{8,9},{9,8},{10,11... | collective-permute-start | bytes 1179656 | tf_op jit(solution)/shard_map/ppermute | solution.py:557
  78.1 9.9 %collective-permute-start.22 = (bf16[2,256,384]{2,1,0:T(8,128)(2,1)S(1)}, bf16[2,256,384]{2,1,0:T(8,128)(2,1)S(1)}, u32[]{:S(2)}, u32[]{:S(2)}) collective-permute-start(bf16[2,256,384]{2,1,0:T(8,128)(2,1)S(1)} %get-tuple-element.50), channel_id=1, source_target_pairs={{0,8},{4,20},{8,0},{12,28},{16,24},{20,4},{24,16},{28,12},{1,9},{5... | collective-permute-start | bytes 1179656 | tf_op jit(solution)/shard_map/ppermute | solution.py:128
  79.0 11.2 %collective-permute-start.23 = (bf16[2,256,384]{2,1,0:T(8,128)(2,1)S(1)}, bf16[2,256,384]{2,1,0:T(8,128)(2,1)S(1)}, u32[]{:S(2)}, u32[]{:S(2)}) collective-permute-start(bf16[2,256,384]{2,1,0:T(8,128)(2,1)S(1)} %get-tuple-element.51), channel_id=1, source_target_pairs={{0,20},{4,8},{8,28},{12,0},{16,4},{20,24},{24,12},{28,16},{1,21},{... | collective-permute-start | bytes 1179656 | tf_op jit(solution)/shard_map/ppermute | solution.py:128
  84.2 16.8 %collective-permute-start.21 = (bf16[256,768]{1,0:T(8,128)(2,1)S(1)}, bf16[256,768]{1,0:T(8,128)(2,1)S(1)}, u32[]{:S(2)}, u32[]{:S(2)}) collective-permute-start(bf16[256,768]{1,0:T(8,128)(2,1)S(1)} %add_convert_fusion.1), channel_id=1, source_target_pairs={{0,2},{1,3},{2,0},{3,1},{4,6},{5,7},{6,4},{7,5},{8,10},{9,11},{10,... | collective-permute-start | bytes 1179656 | tf_op jit(solution)/shard_map/ppermute | solution.py:560
  90.2 13.8 %collective-permute-start.25 = (bf16[2,256,384]{2,1,0:T(8,128)(2,1)S(1)}, bf16[2,256,384]{2,1,0:T(8,128)(2,1)S(1)}, u32[]{:S(2)}, u32[]{:S(2)}) collective-permute-start(bf16[2,256,384]{2,1,0:T(8,128)(2,1)S(1)} %pad_maximum_fusion.3), channel_id=1, source_target_pairs={{0,28},{8,20},{16,12},{24,4},{1,29},{9,21},{17,13},{25,5},{2,30},{... | collective-permute-start | bytes 1179656 | tf_op jit(solution)/shard_map/ppermute | solution.py:128
  95.2 8.8 %collective-permute-start.24 = (bf16[2,256,384]{2,1,0:T(8,128)(2,1)S(1)}, bf16[2,256,384]{2,1,0:T(8,128)(2,1)S(1)}, u32[]{:S(2)}, u32[]{:S(2)}) collective-permute-start(bf16[2,256,384]{2,1,0:T(8,128)(2,1)S(1)} %pad_maximum_fusion.3), channel_id=1, source_target_pairs={{4,28},{12,20},{20,12},{28,4},{5,29},{13,21},{21,13},{29,5},{6,30}... | collective-permute-start | bytes 1179656 | tf_op jit(solution)/shard_map/ppermute | solution.py:128
  104.0 13.7 %collective-permute-start.26 = (bf16[256,768]{1,0:T(8,128)(2,1)S(1)}, bf16[256,768]{1,0:T(8,128)(2,1)S(1)}, u32[]{:S(2)}, u32[]{:S(2)}) collective-permute-start(bf16[256,768]{1,0:T(8,128)(2,1)S(1)} %add_convert_fusion), channel_id=1, source_target_pairs={{0,0},{1,5},{2,10},{3,15},{4,20},{5,17},{6,30},{7,27},{8,8},{9,13}... | collective-permute-start | bytes 1179656 | tf_op jit(solution)/shard_map/ppermute | solution.py:583
  111.3 8.3 %collective-permute-start.28 = (bf16[384,768]{1,0:T(8,128)(2,1)S(1)}, bf16[384,768]{1,0:T(8,128)(2,1)S(1)}, u32[]{:S(2)}, u32[]{:S(2)}) collective-permute-start(bf16[384,768]{1,0:T(8,128)(2,1)S(1)} %get-tuple-element.55), channel_id=1, source_target_pairs={{0,4},{4,0},{8,12},{12,8},{16,20},{20,16},{24,28},{28,24},{1,5},{5... | collective-permute-start | bytes 1769480 | tf_op jit(solution)/shard_map/ppermute | solution.py:128
  111.4 8.3 %collective-permute-start.29 = (bf16[384,768]{1,0:T(8,128)(2,1)S(1)}, bf16[384,768]{1,0:T(8,128)(2,1)S(1)}, u32[]{:S(2)}, u32[]{:S(2)}) collective-permute-start(bf16[384,768]{1,0:T(8,128)(2,1)S(1)} %get-tuple-element.56), channel_id=1, source_target_pairs={{0,4},{4,0},{8,12},{12,8},{16,20},{20,16},{24,28},{28,24},{1,5},{5... | collective-permute-start | bytes 1769480 | tf_op jit(solution)/shard_map/ppermute | solution.py:128
  111.9 7.8 %collective-permute-start.30 = (bf16[384,768]{1,0:T(8,128)(2,1)S(1)}, bf16[384,768]{1,0:T(8,128)(2,1)S(1)}, u32[]{:S(2)}, u32[]{:S(2)}) collective-permute-start(bf16[384,768]{1,0:T(8,128)(2,1)S(1)} %get-tuple-element.57), channel_id=1, source_target_pairs={{0,4},{4,0},{8,12},{12,8},{16,20},{20,16},{24,28},{28,24},{1,5},{5... | collective-permute-start | bytes 1769480 | tf_op jit(solution)/shard_map/ppermute | solution.py:128
  117.7 14.8 %collective-permute-start.27 = (bf16[256,768]{1,0:T(8,128)(2,1)S(1)}, bf16[256,768]{1,0:T(8,128)(2,1)S(1)}, u32[]{:S(2)}, u32[]{:S(2)}) collective-permute-start(bf16[256,768]{1,0:T(8,128)(2,1)S(1)} %collective-permute-done.26), channel_id=1, source_target_pairs={{0,0},{5,4},{10,8},{15,12},{20,20},{17,16},{30,28},{27,24},{8,9},{... | collective-permute-start | bytes 1179656 | tf_op jit(solution)/shard_map/ppermute | solution.py:592

commit v16 on v13

--- a/solution.py
+++ b/solution.py
@@ -531,8 +531,6 @@
     to_straight = columns(jnp.where(core == 0, toward_x, toward_y))
     to_crossed = columns(jnp.where(core == 0, toward_y, toward_x))
     to_corner = columns(jnp.bitwise_xor(chip, 3))
-    mate_here = moved(here, only(1, mate))
-
     own_weights, turn = None, place
     parts = []
     for kept, sources in sets:
@@ -544,7 +542,7 @@
         ahead = moved(made, straight)
         aside = moved(made, crossed)
         inward = moved(made, only(1, mate))
-        (sent,) = after((ahead,), aside, inward, mate_here, to_straight, to_crossed, to_corner)
+        (sent,) = after((ahead,), aside, inward, here, to_straight, to_crossed, to_corner)
         relay_x = moved(sent, only(1, along_x))
         relay_y = moved(sent, only(0, across_y))
         parts.append((made, inward, ahead, aside, relay_x, relay_y))
@@ -565,7 +563,8 @@
     to_straight, to_crossed = after((to_straight, to_crossed), *slots)
     normed_ahead = moved(to_straight, straight)
     normed_aside = moved(to_crossed, crossed)
-    (to_corner,) = after((to_corner,), normed_ahead, normed_aside)
+    to_corner, sent = after((to_corner, here), normed_ahead, normed_aside)
+    mate_here = moved(sent, only(1, mate))
     tokens = (
         here,
         mate_here,
@@ -574,7 +573,7 @@
         moved(to_corner, corner_same),
         moved(to_corner, corner_cross),
     )
-    (total,) = after((total,), tokens[4], tokens[5])
+    (total,) = after((total,), *tokens)
 
     def spot(y, v, z):
         return (y * views + v) * groups + z

time: 131 us -> 133 us (1.015)
  waiting for transfers between devices: 56.6 us -> 50 us
  Pallas kernels: 25.7 us -> 30 us
  local copies, waits for them, and re-layouts: 1.98 us -> 4.57 us
  starting transfers between devices: 43.9 us -> 45.8 us
    ppermute x25, waiting for transfers between devices: 35 us -> 31 us  [moved(): return lax.ppermute(value, ('dp', 'view'), pairs)]
    unnamed x15 -> x19, local copies, waits for them, and re-layouts: 1.72 us -> 4.32 us
    ppermute x1, starting transfers between devices: 4.43 us -> 6.69 us  [gather_body(): lax.ppermute(total, ('dp', 'view', 'head'), [(spot(y, v, z), spot(y ^ v %...]
    pallas_call x2, Pallas kernels: 7.54 us -> 9.42 us  [weight_product(): pl.pallas_call(functools.partial(weight_kernel, mine, mean_scale, len(gra...]
  transfers between devices with their start and end apart: 31 -> 31, of which waited for: 13 -> 13; matrix products, arithmetic and copies ran while one was open for 1% -> 1% of each run, Pallas kernels for 14% -> 16%
where the time goes in v16:
time: 133 us; the launch traced here: 132 us
  waiting for transfers between devices  50 us (38%)
  starting transfers between devices  45.8 us (34%)
  Pallas kernels  30 us (23%)
  local copies, waits for them, and re-layouts  4.57 us (3%)
    ppermute x25, waiting for transfers between devices, moved(): return lax.ppermute(value, ('dp', 'view'), pairs)  31 us
    ppermute x25, starting transfers between devices, moved(): return lax.ppermute(value, ('dp', 'view'), pairs)  30.6 us
    pallas_call x2, Pallas kernels, weight_product(): pl.pallas_call(functools.partial(weight_kernel, mine, mean_scale, len(gra...  9.42 us
    pallas_call x2, Pallas kernels, attention(): pl.pallas_call(functools.partial(attention_kernel, HD ** (-0.5), kept), o...  9.35 us
    ppermute x1, waiting for transfers between devices, gather_body(): lax.ppermute(beside, ('dp', 'view', 'head'), [(spot(y ^ v % 2, v ^ z, z),...  7.08 us
    ppermute x1, starting transfers between devices, gather_body(): lax.ppermute(total, ('dp', 'view', 'head'), [(spot(y, v, z), spot(y ^ v %...  6.69 us
    pallas_call x1, Pallas kernels, input_product(): pl.pallas_call(functools.partial(input_kernel, len(grads) // 6), out_shap...  5.56 us
    ppermute x1, waiting for transfers between devices, gather_body(): lax.ppermute(total, ('dp', 'view', 'head'), [(spot(y, v, z), spot(y ^ v %...  5.14 us
  transfers between devices with their start and end apart: 31, of which 13 were waited for; matrix products, arithmetic and copies ran while one was open for 1% of the time, Pallas kernels for 16%

profile of v16, /device:TPU:26, one launch (start us, length us, event | category | flops | bytes accessed | tf_op | source)
XLA Modules:
  0.0 132.4 jit_solution(4668223946138527747)
XLA Ops:
  0.6 0.6 pad_add_fusion.place_ref
  1.3 2.8 %pack_heads.1 = (bf16[1,1040,128]{2,1,0:T(8,128)(2,1)}, bf16[1,1040,128]{2,1,0:T(8,128)(2,1)}, bf16[1,1040,128]{2,1,0:T(8,128)(2,1)}, bf16[1,1040,128]{2,1,0:T(8...) custom-call(s32[4]{0:T(128)} %pad_add_fusion.place_ref, s32[1,2]{1,0:T(1,128)} %links_ref.1, ...), custom_call_target="tpu_custom_call" | custom-call | tf_op jit(solution)/shard_map/pack_heads/pallas_call | solution.py:215
  4.0 0.5 collective-permute-start.1
  4.6 0.0 collective-permute-start
  4.6 1.6 %collective-permute-start.2 = (bf16[1,1040,128]{2,1,0:T(8,128)(2,1)}, bf16[1,1040,128]{2,1,0:T(8,128)(2,1)S(1)}, u32[]{:S(2)}, u32[]{:S(2)}) collective-permute-start(bf16[1,1040,128]{2,1,0:T(8,128)(2,1)} %get-tuple-element.37), channel_id=1, source_target_pairs={{0,12},{4,8},{8,4},{12,0},{16,28},{20,24},{24,20},{28,16},{1,13},{... | collective-permute-start | bytes 798728 | tf_op jit(solution)/shard_map/ppermute | solution.py:128
  6.2 0.0 collective-permute-start.3
  6.2 7.3 %collective-permute-done.1.x_in = bf16[1,1040,128]{2,1,0:T(8,128)(2,1)S(1)} collective-permute-done((bf16[1,1040,128]{2,1,0:T(8,128)(2,1)}, bf16[1,1040,128]{2,1,0:T(8,128)(2,1)S(1)}, u32[]{:S(2)}, u32[]{:S(2)}) %collective-permute-start.1) | collective-permute-done | bytes 266272 | tf_op jit(solution)/shard_map/ppermute | solution.py:128
  13.5 0.5 collective-permute-start.4
  14.1 0.0 collective-permute-done.mate_in
  14.1 3.3 %collective-permute-done.2.far_in = bf16[1,1040,128]{2,1,0:T(8,128)(2,1)S(1)} collective-permute-done((bf16[1,1040,128]{2,1,0:T(8,128)(2,1)}, bf16[1,1040,128]{2,1,0:T(8,128)(2,1)S(1)}, u32[]{:S(2)}, u32[]{:S(2)}) %collective-permute-start.2) | collective-permute-done | bytes 266272 | tf_op jit(solution)/shard_map/ppermute | solution.py:128
  17.4 0.9 copy-done.7
  18.4 4.4 %attention_gradients.2.refs_0_.refs_6_ = bf16[4,256,384]{2,1,0:T(8,128)(2,1)S(1)} custom-call(s32[4]{0:T(128)S(1)} %copy-done.3, bf16[1,1040,128]{2,1,0:T(8,128)(2,1)S(1)} %copy-done.7, bf16[1,1040,128]{2,1,0:T(8,128)(2,1)S(1)} %collective-permute-done.mate_in, bf16[1,1040,128]{2,1,0:T(8,128)(2,1)S(1)} %collective-permute-done.1.x_in, ...), custom_call_target="tpu_custom_call" | custom-call | flops 2013265920 | bytes 1835008 | tf_op jit(solution)/shard_map/attention_gradients/pallas_call | solution.py:304
  22.8 1.1 turn_weights.1.own_ref
  23.9 1.7 %collective-permute-start.16 = (bf16[2304,384]{1,0:T(8,128)(2,1)S(1)}, bf16[2304,384]{1,0:T(8,128)(2,1)}, u32[]{:S(2)}, u32[]{:S(2)}) collective-permute-start(bf16[2304,384]{1,0:T(8,128)(2,1)S(1)} %turn_weights.1.own_ref), channel_id=1, source_target_pairs={{0,4},{4,0},{8,12},{12,8},{16,20},{20,16},{24,28},{28,24},{1,5},{5... | collective-permute-start | bytes 5308424 | tf_op jit(solution)/shard_map/ppermute | solution.py:128
  25.6 0.1 collective-permute-start.5
  25.7 1.5 %collective-permute-start.10 = (bf16[4,256,384]{2,1,0:T(8,128)(2,1)S(1)}, bf16[4,256,384]{2,1,0:T(8,128)(2,1)S(1)}, u32[]{:S(2)}, u32[]{:S(2)}) collective-permute-start(bf16[4,256,384]{2,1,0:T(8,128)(2,1)S(1)} %attention_gradients.2.refs_0_.refs_6_), channel_id=1, source_target_pairs={{0,20},{4,8},{8,28},{12,0},{16,4},{20,24},{24,12},{28,16},{1,21},{... | collective-permute-start | bytes 2359304 | tf_op jit(solution)/shard_map/ppermute | solution.py:128
  27.3 0.5 collective-permute-start.8
  27.8 0.7 copy-done.5
  28.5 1.3 collective-permute-start.6
  29.9 0.9 copy-done.4
  30.8 0.9 copy-done.6
  31.8 4.9 %attention_gradients.3.refs_1_.refs_7_ = bf16[2,256,384]{2,1,0:T(8,128)(2,1)S(1)} custom-call(s32[4]{0:T(128)S(1)} %copy-done.3, bf16[1,1040,128]{2,1,0:T(8,128)(2,1)S(1)} %copy-done.4, bf16[1,1040,128]{2,1,0:T(8,128)(2,1)S(1)} %copy-done.6, bf16[1,1040,128]{2,1,0:T(8,128)(2,1)} %collective-permute-done.4.x_in, ...), custom_call_target="tpu_custom_call" | custom-call | flops 2013265920 | bytes 1835008 | tf_op jit(solution)/shard_map/attention_gradients/pallas_call | solution.py:304
  36.7 2.1 %collective-permute-start.11 = (bf16[2,256,384]{2,1,0:T(8,128)(2,1)S(1)}, bf16[2,256,384]{2,1,0:T(8,128)(2,1)S(1)}, u32[]{:S(2)}, u32[]{:S(2)}) collective-permute-start(bf16[2,256,384]{2,1,0:T(8,128)(2,1)S(1)} %attention_gradients.3.refs_1_.refs_7_), channel_id=1, source_target_pairs={{0,20},{4,8},{8,28},{12,0},{16,4},{20,24},{24,12},{28,16},{1,21},{... | collective-permute-start | bytes 1179656 | tf_op jit(solution)/shard_map/ppermute | solution.py:128
  38.8 0.3 dynamic-slice_bitcast_fusion.1
  39.1 0.1 pad_maximum_fusion.2
  39.2 0.1 pad_maximum_fusion
  39.3 5.6 %collective-permute-done.10.refs_6_.refs_12_ = bf16[4,256,384]{2,1,0:T(8,128)(2,1)S(1)} collective-permute-done((bf16[4,256,384]{2,1,0:T(8,128)(2,1)S(1)}, bf16[4,256,384]{2,1,0:T(8,128)(2,1)S(1)}, u32[]{:S(2)}, u32[]{:S(2)}) %collective-permute-start.10) | collective-permute-done | bytes 786464 | tf_op jit(solution)/shard_map/ppermute | solution.py:128
  44.8 0.3 collective-permute-start.9
  45.2 2.7 %collective-permute-done.8.refs_4_.refs_10_ = bf16[4,256,384]{2,1,0:T(8,128)(2,1)} collective-permute-done((bf16[4,256,384]{2,1,0:T(8,128)(2,1)S(1)}, bf16[4,256,384]{2,1,0:T(8,128)(2,1)}, u32[]{:S(2)}, u32[]{:S(2)}) %collective-permute-start.8) | collective-permute-done | bytes 786464 | tf_op jit(solution)/shard_map/ppermute | solution.py:128
  47.8 1.3 collective-permute-start.7
  49.1 3.2 %collective-permute-start.14 = (bf16[4,256,384]{2,1,0:T(8,128)(2,1)}, bf16[4,256,384]{2,1,0:T(8,128)(2,1)S(1)}, u32[]{:S(2)}, u32[]{:S(2)}) collective-permute-start(bf16[4,256,384]{2,1,0:T(8,128)(2,1)} %collective-permute-done.8.refs_4_.refs_10_), channel_id=1, source_target_pairs={{0,20},{8,28},{16,4},{24,12},{1,21},{9,29},{17,5},{25,13},{2,22},{... | collective-permute-start | bytes 2359304 | tf_op jit(solution)/shard_map/ppermute | solution.py:128
  52.3 0.7 collective-permute-start.12
  53.0 0.9 collective-permute-done.9.refs_5_.refs_11_
  54.0 3.6 %collective-permute-start.15 = (bf16[2,256,384]{2,1,0:T(8,128)(2,1)S(1)}, bf16[2,256,384]{2,1,0:T(8,128)(2,1)S(1)}, u32[]{:S(2)}, u32[]{:S(2)}) collective-permute-start(bf16[2,256,384]{2,1,0:T(8,128)(2,1)S(1)} %collective-permute-done.9.refs_5_.refs_11_), channel_id=1, source_target_pairs={{0,20},{8,28},{16,4},{24,12},{1,21},{9,29},{17,5},{25,13},{2,22},{... | collective-permute-start | bytes 1179656 | tf_op jit(solution)/shard_map/ppermute | solution.py:128
  57.6 0.7 collective-permute-start.13
  58.3 1.8 %join_weights.1.refs_12_ = bf16[2304,768]{1,0:T(8,128)(2,1)S(1)} custom-call(s32[4]{0:T(128)S(1)} %copy-done.3, bf16[2304,384]{1,0:T(8,128)(2,1)S(1)} %turn_weights.1.own_ref, bf16[2304,384]{1,0:T(8,128)(2,1)} %collective-permute-done.16.mate_ref), custom_call_target="tpu_custom_call" | custom-call | tf_op jit(solution)/shard_map/join_weights/pallas_call | solution.py:351
  60.1 6.1 %collective-permute-done.15.refs_11_.refs_17_ = bf16[2,256,384]{2,1,0:T(8,128)(2,1)S(1)} collective-permute-done((bf16[2,256,384]{2,1,0:T(8,128)(2,1)S(1)}, bf16[2,256,384]{2,1,0:T(8,128)(2,1)S(1)}, u32[]{:S(2)}, u32[]{:S(2)}) %collective-permute-start.15) | collective-permute-done | bytes 393248 | tf_op jit(solution)/shard_map/ppermute | solution.py:128
  66.2 5.6 %input_gradient.1 = (bf16[256,768]{1,0:T(8,128)(2,1)S(1)}, bf16[256,768]{1,0:T(8,128)(2,1)S(1)}, bf16[256,768]{1,0:T(8,128)(2,1)S(1)}, bf16[256,768]{1,0:T(8,128)(2,1)S(1)}) custom-call(s32[4]{0:T(128)S(1)} %copy-done.3, bf16[4,256,384]{2,1,0:T(8,128)(2,1)S(1)} %attention_gradients.2.refs_0_.refs_6_, ...), custom_call_target="tpu_custom_call" | custom-call | flops 3623878656 | bytes 9830400 | tf_op jit(solution)/shard_map/input_gradient/pallas_call | solution.py:408
  71.8 2.4 %collective-permute-start.19 = (bf16[256,768]{1,0:T(8,128)(2,1)S(1)}, bf16[256,768]{1,0:T(8,128)(2,1)S(1)}, u32[]{:S(2)}, u32[]{:S(2)}) collective-permute-start(bf16[256,768]{1,0:T(8,128)(2,1)S(1)} %get-tuple-element.49), channel_id=1, source_target_pairs={{0,1},{3,2},{4,5},{7,6},{8,9},{11,10},{12,13},{15,14},{16,17},{19,... | collective-permute-start | bytes 1179656 | tf_op jit(solution)/shard_map/ppermute | solution.py:554
  74.1 0.7 collective-permute-start.18
  74.8 1.1 collective-permute-start.17
  75.9 0.6 collective-permute-start.21
  76.6 2.7 %collective-permute-start.22 = (bf16[2,256,384]{2,1,0:T(8,128)(2,1)S(1)}, bf16[2,256,384]{2,1,0:T(8,128)(2,1)S(1)}, u32[]{:S(2)}, u32[]{:S(2)}) collective-permute-start(bf16[2,256,384]{2,1,0:T(8,128)(2,1)S(1)} %get-tuple-element.52), channel_id=1, source_target_pairs={{0,20},{4,8},{8,28},{12,0},{16,4},{20,24},{24,12},{28,16},{1,21},{... | collective-permute-start | bytes 1179656 | tf_op jit(solution)/shard_map/ppermute | solution.py:128
  79.3 2.7 %collective-permute-done.19 = bf16[256,768]{1,0:T(8,128)(2,1)S(1)} collective-permute-done((bf16[256,768]{1,0:T(8,128)(2,1)S(1)}, bf16[256,768]{1,0:T(8,128)(2,1)S(1)}, u32[]{:S(2)}, u32[]{:S(2)}) %collective-permute-start.19) | collective-permute-done | bytes 393248 | tf_op jit(solution)/shard_map/ppermute | solution.py:554
  82.0 0.1 add_convert_fusion.1
  82.1 2.4 %collective-permute-start.20 = (bf16[256,768]{1,0:T(8,128)(2,1)S(1)}, bf16[256,768]{1,0:T(8,128)(2,1)S(1)}, u32[]{:S(2)}, u32[]{:S(2)}) collective-permute-start(bf16[256,768]{1,0:T(8,128)(2,1)S(1)} %add_convert_fusion.1), channel_id=1, source_target_pairs={{0,2},{1,3},{2,0},{3,1},{4,6},{5,7},{6,4},{7,5},{8,10},{9,11},{10,... | collective-permute-start | bytes 1179656 | tf_op jit(solution)/shard_map/ppermute | solution.py:558
  84.5 1.6 %collective-permute-done.21.refs_2_ = bf16[2,256,384]{2,1,0:T(8,128)(2,1)S(1)} collective-permute-done((bf16[2,256,384]{2,1,0:T(8,128)(2,1)S(1)}, bf16[2,256,384]{2,1,0:T(8,128)(2,1)S(1)}, u32[]{:S(2)}, u32[]{:S(2)}) %collective-permute-start.21) | collective-permute-done | bytes 393248 | tf_op jit(solution)/shard_map/ppermute | solution.py:128
  86.1 1.9 %collective-permute-done.22.refs_3_ = bf16[2,256,384]{2,1,0:T(8,128)(2,1)S(1)} collective-permute-done((bf16[2,256,384]{2,1,0:T(8,128)(2,1)S(1)}, bf16[2,256,384]{2,1,0:T(8,128)(2,1)S(1)}, u32[]{:S(2)}, u32[]{:S(2)}) %collective-permute-start.22) | collective-permute-done | bytes 393248 | tf_op jit(solution)/shard_map/ppermute | solution.py:128
  87.9 1.3 collective-permute-start.23
  89.2 4.9 %collective-permute-start.25 = (bf16[2,256,384]{2,1,0:T(8,128)(2,1)S(1)}, bf16[2,256,384]{2,1,0:T(8,128)(2,1)S(1)}, u32[]{:S(2)}, u32[]{:S(2)}) collective-permute-start(bf16[2,256,384]{2,1,0:T(8,128)(2,1)S(1)} %get-tuple-element.54), channel_id=1, source_target_pairs={{0,28},{8,20},{16,12},{24,4},{1,29},{9,21},{17,13},{25,5},{2,30},{... | collective-permute-start | bytes 1179656 | tf_op jit(solution)/shard_map/ppermute | solution.py:128
  94.2 0.7 collective-permute-start.24
  94.9 4.0 %collective-permute-done.20 = bf16[256,768]{1,0:T(8,128)(2,1)S(1)} collective-permute-done((bf16[256,768]{1,0:T(8,128)(2,1)S(1)}, bf16[256,768]{1,0:T(8,128)(2,1)S(1)}, u32[]{:S(2)}, u32[]{:S(2)}) %collective-permute-start.20) | collective-permute-done | bytes 393248 | tf_op jit(solution)/shard_map/ppermute | solution.py:558
  98.9 0.2 add_convert_fusion
  99.1 1.6 %collective-permute-done.25.refs_5_ = bf16[2,256,384]{2,1,0:T(8,128)(2,1)S(1)} collective-permute-done((bf16[2,256,384]{2,1,0:T(8,128)(2,1)S(1)}, bf16[2,256,384]{2,1,0:T(8,128)(2,1)S(1)}, u32[]{:S(2)}, u32[]{:S(2)}) %collective-permute-start.25) | collective-permute-done | bytes 393248 | tf_op jit(solution)/shard_map/ppermute | solution.py:128
  100.7 6.7 %collective-permute-start.26 = (bf16[256,768]{1,0:T(8,128)(2,1)S(1)}, bf16[256,768]{1,0:T(8,128)(2,1)S(1)}, u32[]{:S(2)}, u32[]{:S(2)}) collective-permute-start(bf16[256,768]{1,0:T(8,128)(2,1)S(1)} %add_convert_fusion), channel_id=1, source_target_pairs={{0,0},{1,5},{2,10},{3,15},{4,20},{5,17},{6,30},{7,27},{8,8},{9,13}... | collective-permute-start | bytes 1179656 | tf_op jit(solution)/shard_map/ppermute | solution.py:582
  107.4 3.7 %weight_gradient_mate.1 = (bf16[384,768]{1,0:T(8,128)(2,1)S(1)}, bf16[384,768]{1,0:T(8,128)(2,1)S(1)}, bf16[384,768]{1,0:T(8,128)(2,1)S(1)}) custom-call(s32[4]{0:T(128)S(1)} %copy-done.3, bf16[2,256,384]{2,1,0:T(8,128)(2,1)S(1)} %get-tuple-element.53.refs_0_, bf16[2,256,384]{2,1,0:T(8,128)(2,1)S(1)} %collective-permute-done.23.refs_1_, ...), custom_call_target="tpu_custom_call" | custom-call | flops 1811939328 | bytes 9043968 | tf_op jit(solution)/shard_map/weight_gradient_mate/pallas_call | solution.py:457
  111.1 0.1 collective-permute-start.28
  111.2 0.5 collective-permute-start.29
  111.7 0.1 collective-permute-start.30
  111.8 5.1 %collective-permute-done.26 = bf16[256,768]{1,0:T(8,128)(2,1)S(1)} collective-permute-done((bf16[256,768]{1,0:T(8,128)(2,1)S(1)}, bf16[256,768]{1,0:T(8,128)(2,1)S(1)}, u32[]{:S(2)}, u32[]{:S(2)}) %collective-permute-start.26) | collective-permute-done | bytes 393248 | tf_op jit(solution)/shard_map/ppermute | solution.py:582
  116.9 1.9 %collective-permute-start.27 = (bf16[256,768]{1,0:T(8,128)(2,1)S(1)}, bf16[256,768]{1,0:T(8,128)(2,1)S(1)}, u32[]{:S(2)}, u32[]{:S(2)}) collective-permute-start(bf16[256,768]{1,0:T(8,128)(2,1)S(1)} %collective-permute-done.26), channel_id=1, source_target_pairs={{0,0},{5,4},{10,8},{15,12},{20,20},{17,16},{30,28},{27,24},{8,9},{... | collective-permute-start | bytes 1179656 | tf_op jit(solution)/shard_map/ppermute | solution.py:591
  118.8 5.7 %weight_gradient_own.1 = (f32[384,768]{1,0:T(8,128)}, f32[384,768]{1,0:T(8,128)}, f32[384,768]{1,0:T(8,128)}) custom-call(s32[4]{0:T(128)S(1)} %copy-done.3, bf16[2,256,384]{2,1,0:T(8,128)(2,1)S(1)} %get-tuple-element.53.refs_0_, bf16[2,256,384]{2,1,0:T(8,128)(2,1)S(1)} %collective-permute-done.23.refs_1_, ...), custom_call_target="tpu_custom_call" | custom-call | flops 1811939328 | bytes 9043968 | tf_op jit(solution)/shard_map/weight_gradient_own/pallas_call | solution.py:457
  124.6 7.1 %collective-permute-done.27 = bf16[256,768]{1,0:T(8,128)(2,1)S(1)} collective-permute-done((bf16[256,768]{1,0:T(8,128)(2,1)S(1)}, bf16[256,768]{1,0:T(8,128)(2,1)S(1)}, u32[]{:S(2)}, u32[]{:S(2)}) %collective-permute-start.27) | collective-permute-done | bytes 393248 | tf_op jit(solution)/shard_map/ppermute | solution.py:591
  131.7 0.7 copy.14
  (31 shorter events, 0.1 us)
Async XLA Ops:
  1.3 16.1 %copy-start.3 = (s32[4]{0:T(128)S(1)}, s32[4]{0:T(128)}, u32[]{:S(2)}) copy-start(s32[4]{0:T(128)} %pad_add_fusion.place_ref) | copy-start | bytes 52
  4.0 9.5 %collective-permute-start.1 = (bf16[1,1040,128]{2,1,0:T(8,128)(2,1)}, bf16[1,1040,128]{2,1,0:T(8,128)(2,1)S(1)}, u32[]{:S(2)}, u32[]{:S(2)}) collective-permute-start(bf16[1,1040,128]{2,1,0:T(8,128)(2,1)} %get-tuple-element.36), channel_id=1, source_target_pairs={{0,8},{4,12},{8,0},{12,4},{16,24},{20,28},{24,16},{28,20},{1,9},{5... | collective-permute-start | bytes 798728 | tf_op jit(solution)/shard_map/ppermute | solution.py:128
  4.6 9.5 %collective-permute-start = (bf16[1,1040,128]{2,1,0:T(8,128)(2,1)}, bf16[1,1040,128]{2,1,0:T(8,128)(2,1)S(1)}, u32[]{:S(2)}, u32[]{:S(2)}) collective-permute-start(bf16[1,1040,128]{2,1,0:T(8,128)(2,1)} %get-tuple-element.35), channel_id=1, source_target_pairs={{0,4},{4,0},{8,12},{12,8},{16,20},{20,16},{24,28},{28,24},{1,5},{5... | collective-permute-start | bytes 798728 | tf_op jit(solution)/shard_map/ppermute | solution.py:128
  4.6 12.8 %collective-permute-start.2 = (bf16[1,1040,128]{2,1,0:T(8,128)(2,1)}, bf16[1,1040,128]{2,1,0:T(8,128)(2,1)S(1)}, u32[]{:S(2)}, u32[]{:S(2)}) collective-permute-start(bf16[1,1040,128]{2,1,0:T(8,128)(2,1)} %get-tuple-element.37), channel_id=1, source_target_pairs={{0,12},{4,8},{8,4},{12,0},{16,28},{20,24},{24,20},{28,16},{1,13},{... | collective-permute-start | bytes 798728 | tf_op jit(solution)/shard_map/ppermute | solution.py:128
  6.2 21.6 %collective-permute-start.3 = (bf16[1,1040,128]{2,1,0:T(8,128)(2,1)}, bf16[1,1040,128]{2,1,0:T(8,128)(2,1)S(1)}, u32[]{:S(2)}, u32[]{:S(2)}) collective-permute-start(bf16[1,1040,128]{2,1,0:T(8,128)(2,1)} %get-tuple-element.42.own), channel_id=1, source_target_pairs={{0,4},{4,0},{8,12},{12,8},{16,20},{20,16},{24,28},{28,24},{1,5},{5... | collective-permute-start | bytes 798728 | tf_op jit(solution)/shard_map/ppermute | solution.py:128
  13.5 12.1 %collective-permute-start.4 = (bf16[1,1040,128]{2,1,0:T(8,128)(2,1)}, bf16[1,1040,128]{2,1,0:T(8,128)(2,1)}, u32[]{:S(2)}, u32[]{:S(2)}) collective-permute-start(bf16[1,1040,128]{2,1,0:T(8,128)(2,1)} %get-tuple-element.44), channel_id=1, source_target_pairs={{0,8},{4,12},{8,0},{12,4},{16,24},{20,28},{24,16},{28,20},{1,9},{5... | collective-permute-start | bytes 798728 | tf_op jit(solution)/shard_map/ppermute | solution.py:128
  17.4 1.0 copy-start.7
  18.4 4.5 %copy-start = (bf16[384,768]{1,0:T(8,128)(2,1)S(1)}, bf16[384,768]{1,0:T(8,128)(2,1)}, u32[]{:S(2)}) copy-start(bf16[384,768]{1,0:T(8,128)(2,1)} %q_ref) | copy-start | bytes 1769476
  18.4 4.5 %copy-start.1 = (bf16[384,768]{1,0:T(8,128)(2,1)S(1)}, bf16[384,768]{1,0:T(8,128)(2,1)}, u32[]{:S(2)}) copy-start(bf16[384,768]{1,0:T(8,128)(2,1)} %k_ref) | copy-start | bytes 1769476
  18.4 4.5 %copy-start.2 = (bf16[384,768]{1,0:T(8,128)(2,1)S(1)}, bf16[384,768]{1,0:T(8,128)(2,1)}, u32[]{:S(2)}) copy-start(bf16[384,768]{1,0:T(8,128)(2,1)} %v_ref) | copy-start | bytes 1769476
  23.9 34.4 %collective-permute-start.16 = (bf16[2304,384]{1,0:T(8,128)(2,1)S(1)}, bf16[2304,384]{1,0:T(8,128)(2,1)}, u32[]{:S(2)}, u32[]{:S(2)}) collective-permute-start(bf16[2304,384]{1,0:T(8,128)(2,1)S(1)} %turn_weights.1.own_ref), channel_id=1, source_target_pairs={{0,4},{4,0},{8,12},{12,8},{16,20},{20,16},{24,28},{28,24},{1,5},{5... | collective-permute-start | bytes 5308424 | tf_op jit(solution)/shard_map/ppermute | solution.py:128
  25.6 4.2 %collective-permute-start.5 = (bf16[1,1040,128]{2,1,0:T(8,128)(2,1)}, bf16[1,1040,128]{2,1,0:T(8,128)(2,1)}, u32[]{:S(2)}, u32[]{:S(2)}) collective-permute-start(bf16[1,1040,128]{2,1,0:T(8,128)(2,1)} %collective-permute-done.4.x_in), channel_id=1, source_target_pairs={{0,4},{4,0},{8,12},{12,8},{16,20},{20,16},{24,28},{28,24},{1,5},{5... | collective-permute-start | bytes 798728 | tf_op jit(solution)/shard_map/ppermute | solution.py:128
  25.7 19.1 %collective-permute-start.10 = (bf16[4,256,384]{2,1,0:T(8,128)(2,1)S(1)}, bf16[4,256,384]{2,1,0:T(8,128)(2,1)S(1)}, u32[]{:S(2)}, u32[]{:S(2)}) collective-permute-start(bf16[4,256,384]{2,1,0:T(8,128)(2,1)S(1)} %attention_gradients.2.refs_0_.refs_6_), channel_id=1, source_target_pairs={{0,20},{4,8},{8,28},{12,0},{16,4},{20,24},{24,12},{28,16},{1,21},{... | collective-permute-start | bytes 2359304 | tf_op jit(solution)/shard_map/ppermute | solution.py:128
  27.3 20.6 %collective-permute-start.8 = (bf16[4,256,384]{2,1,0:T(8,128)(2,1)S(1)}, bf16[4,256,384]{2,1,0:T(8,128)(2,1)}, u32[]{:S(2)}, u32[]{:S(2)}) collective-permute-start(bf16[4,256,384]{2,1,0:T(8,128)(2,1)S(1)} %attention_gradients.2.refs_0_.refs_6_), channel_id=1, source_target_pairs={{0,8},{4,20},{8,0},{12,28},{16,24},{20,4},{24,16},{28,12},{1,9},{5... | collective-permute-start | bytes 2359304 | tf_op jit(solution)/shard_map/ppermute | solution.py:128
  27.8 0.7 copy-start.5
  28.5 20.6 %collective-permute-start.6 = (bf16[4,256,384]{2,1,0:T(8,128)(2,1)S(1)}, bf16[4,256,384]{2,1,0:T(8,128)(2,1)}, u32[]{:S(2)}, u32[]{:S(2)}) collective-permute-start(bf16[4,256,384]{2,1,0:T(8,128)(2,1)S(1)} %attention_gradients.2.refs_0_.refs_6_), channel_id=1, source_target_pairs={{4,0},{12,8},{20,16},{28,24},{5,1},{13,9},{21,17},{29,25},{6,2},{1... | collective-permute-start | bytes 2359304 | tf_op jit(solution)/shard_map/ppermute | solution.py:128
  29.9 1.0 copy-start.4
  30.8 1.0 copy-start.6
  31.8 7.0 %copy-start.8 = (bf16[1,1,256,3072]{3,2,1,0:T(8,128)(2,1)S(1)}, bf16[1,1,256,3072]{3,2,1,0:T(8,128)(2,1)}, u32[]{:S(2)}) copy-start(bf16[1,1,256,3072]{3,2,1,0:T(8,128)(2,1)} %param.9) | copy-start | bytes 4718596
  36.7 15.6 %collective-permute-start.11 = (bf16[2,256,384]{2,1,0:T(8,128)(2,1)S(1)}, bf16[2,256,384]{2,1,0:T(8,128)(2,1)S(1)}, u32[]{:S(2)}, u32[]{:S(2)}) collective-permute-start(bf16[2,256,384]{2,1,0:T(8,128)(2,1)S(1)} %attention_gradients.3.refs_1_.refs_7_), channel_id=1, source_target_pairs={{0,20},{4,8},{8,28},{12,0},{16,4},{20,24},{24,12},{28,16},{1,21},{... | collective-permute-start | bytes 1179656 | tf_op jit(solution)/shard_map/ppermute | solution.py:128
  44.8 9.1 %collective-permute-start.9 = (bf16[2,256,384]{2,1,0:T(8,128)(2,1)S(1)}, bf16[2,256,384]{2,1,0:T(8,128)(2,1)S(1)}, u32[]{:S(2)}, u32[]{:S(2)}) collective-permute-start(bf16[2,256,384]{2,1,0:T(8,128)(2,1)S(1)} %attention_gradients.3.refs_1_.refs_7_), channel_id=1, source_target_pairs={{0,8},{4,20},{8,0},{12,28},{16,24},{20,4},{24,16},{28,12},{1,9},{5... | collective-permute-start | bytes 1179656 | tf_op jit(solution)/shard_map/ppermute | solution.py:128
  47.8 6.1 %collective-permute-start.7 = (bf16[2,256,384]{2,1,0:T(8,128)(2,1)S(1)}, bf16[2,256,384]{2,1,0:T(8,128)(2,1)S(1)}, u32[]{:S(2)}, u32[]{:S(2)}) collective-permute-start(bf16[2,256,384]{2,1,0:T(8,128)(2,1)S(1)} %attention_gradients.3.refs_1_.refs_7_), channel_id=1, source_target_pairs={{4,0},{12,8},{20,16},{28,24},{5,1},{13,9},{21,17},{29,25},{6,2},{1... | collective-permute-start | bytes 1179656 | tf_op jit(solution)/shard_map/ppermute | solution.py:128
  49.1 17.0 %collective-permute-start.14 = (bf16[4,256,384]{2,1,0:T(8,128)(2,1)}, bf16[4,256,384]{2,1,0:T(8,128)(2,1)S(1)}, u32[]{:S(2)}, u32[]{:S(2)}) collective-permute-start(bf16[4,256,384]{2,1,0:T(8,128)(2,1)} %collective-permute-done.8.refs_4_.refs_10_), channel_id=1, source_target_pairs={{0,20},{8,28},{16,4},{24,12},{1,21},{9,29},{17,5},{25,13},{2,22},{... | collective-permute-start | bytes 2359304 | tf_op jit(solution)/shard_map/ppermute | solution.py:128
  52.3 13.9 %collective-permute-start.12 = (bf16[4,256,384]{2,1,0:T(8,128)(2,1)}, bf16[4,256,384]{2,1,0:T(8,128)(2,1)S(1)}, u32[]{:S(2)}, u32[]{:S(2)}) collective-permute-start(bf16[4,256,384]{2,1,0:T(8,128)(2,1)} %collective-permute-done.8.refs_4_.refs_10_), channel_id=1, source_target_pairs={{4,12},{12,4},{20,28},{28,20},{5,13},{13,5},{21,29},{29,21},{6,14}... | collective-permute-start | bytes 2359304 | tf_op jit(solution)/shard_map/ppermute | solution.py:128
  54.0 12.2 %collective-permute-start.15 = (bf16[2,256,384]{2,1,0:T(8,128)(2,1)S(1)}, bf16[2,256,384]{2,1,0:T(8,128)(2,1)S(1)}, u32[]{:S(2)}, u32[]{:S(2)}) collective-permute-start(bf16[2,256,384]{2,1,0:T(8,128)(2,1)S(1)} %collective-permute-done.9.refs_5_.refs_11_), channel_id=1, source_target_pairs={{0,20},{8,28},{16,4},{24,12},{1,21},{9,29},{17,5},{25,13},{2,22},{... | collective-permute-start | bytes 1179656 | tf_op jit(solution)/shard_map/ppermute | solution.py:128
  57.6 8.6 %collective-permute-start.13 = (bf16[2,256,384]{2,1,0:T(8,128)(2,1)S(1)}, bf16[2,256,384]{2,1,0:T(8,128)(2,1)S(1)}, u32[]{:S(2)}, u32[]{:S(2)}) collective-permute-start(bf16[2,256,384]{2,1,0:T(8,128)(2,1)S(1)} %collective-permute-done.9.refs_5_.refs_11_), channel_id=1, source_target_pairs={{4,12},{12,4},{20,28},{28,20},{5,13},{13,5},{21,29},{29,21},{6,14}... | collective-permute-start | bytes 1179656 | tf_op jit(solution)/shard_map/ppermute | solution.py:128
  71.8 10.2 %collective-permute-start.19 = (bf16[256,768]{1,0:T(8,128)(2,1)S(1)}, bf16[256,768]{1,0:T(8,128)(2,1)S(1)}, u32[]{:S(2)}, u32[]{:S(2)}) collective-permute-start(bf16[256,768]{1,0:T(8,128)(2,1)S(1)} %get-tuple-element.49), channel_id=1, source_target_pairs={{0,1},{3,2},{4,5},{7,6},{8,9},{11,10},{12,13},{15,14},{16,17},{19,... | collective-permute-start | bytes 1179656 | tf_op jit(solution)/shard_map/ppermute | solution.py:554
  74.1 20.7 %collective-permute-start.18 = (bf16[256,768]{1,0:T(8,128)(2,1)S(1)}, bf16[256,768]{1,0:T(8,128)(2,1)S(1)}, u32[]{:S(2)}, u32[]{:S(2)}) collective-permute-start(bf16[256,768]{1,0:T(8,128)(2,1)S(1)} %get-tuple-element.49), channel_id=1, source_target_pairs={{1,2},{2,1},{5,6},{6,5},{9,10},{10,9},{13,14},{14,13},{17,18},{18,... | collective-permute-start | bytes 1179656 | tf_op jit(solution)/shard_map/ppermute | solution.py:556
  74.8 19.3 %collective-permute-start.17 = (bf16[256,768]{1,0:T(8,128)(2,1)S(1)}, bf16[256,768]{1,0:T(8,128)(2,1)S(1)}, u32[]{:S(2)}, u32[]{:S(2)}) collective-permute-start(bf16[256,768]{1,0:T(8,128)(2,1)S(1)} %get-tuple-element.48), channel_id=1, source_target_pairs={{0,1},{1,0},{2,3},{3,2},{4,5},{5,4},{6,7},{7,6},{8,9},{9,8},{10,11... | collective-permute-start | bytes 1179656 | tf_op jit(solution)/shard_map/ppermute | solution.py:555
  75.9 10.1 %collective-permute-start.21 = (bf16[2,256,384]{2,1,0:T(8,128)(2,1)S(1)}, bf16[2,256,384]{2,1,0:T(8,128)(2,1)S(1)}, u32[]{:S(2)}, u32[]{:S(2)}) collective-permute-start(bf16[2,256,384]{2,1,0:T(8,128)(2,1)S(1)} %get-tuple-element.51), channel_id=1, source_target_pairs={{0,8},{4,20},{8,0},{12,28},{16,24},{20,4},{24,16},{28,12},{1,9},{5... | collective-permute-start | bytes 1179656 | tf_op jit(solution)/shard_map/ppermute | solution.py:128
  76.6 11.4 %collective-permute-start.22 = (bf16[2,256,384]{2,1,0:T(8,128)(2,1)S(1)}, bf16[2,256,384]{2,1,0:T(8,128)(2,1)S(1)}, u32[]{:S(2)}, u32[]{:S(2)}) collective-permute-start(bf16[2,256,384]{2,1,0:T(8,128)(2,1)S(1)} %get-tuple-element.52), channel_id=1, source_target_pairs={{0,20},{4,8},{8,28},{12,0},{16,4},{20,24},{24,12},{28,16},{1,21},{... | collective-permute-start | bytes 1179656 | tf_op jit(solution)/shard_map/ppermute | solution.py:128
  82.1 16.8 %collective-permute-start.20 = (bf16[256,768]{1,0:T(8,128)(2,1)S(1)}, bf16[256,768]{1,0:T(8,128)(2,1)S(1)}, u32[]{:S(2)}, u32[]{:S(2)}) collective-permute-start(bf16[256,768]{1,0:T(8,128)(2,1)S(1)} %add_convert_fusion.1), channel_id=1, source_target_pairs={{0,2},{1,3},{2,0},{3,1},{4,6},{5,7},{6,4},{7,5},{8,10},{9,11},{10,... | collective-permute-start | bytes 1179656 | tf_op jit(solution)/shard_map/ppermute | solution.py:558
  87.9 11.1 %collective-permute-start.23 = (bf16[2,256,384]{2,1,0:T(8,128)(2,1)S(1)}, bf16[2,256,384]{2,1,0:T(8,128)(2,1)S(1)}, u32[]{:S(2)}, u32[]{:S(2)}) collective-permute-start(bf16[2,256,384]{2,1,0:T(8,128)(2,1)S(1)} %get-tuple-element.53.refs_0_), channel_id=1, source_target_pairs={{4,0},{12,8},{20,16},{28,24},{5,1},{13,9},{21,17},{29,25},{6,2},{1... | collective-permute-start | bytes 1179656 | tf_op jit(solution)/shard_map/ppermute | solution.py:128
  89.2 11.5 %collective-permute-start.25 = (bf16[2,256,384]{2,1,0:T(8,128)(2,1)S(1)}, bf16[2,256,384]{2,1,0:T(8,128)(2,1)S(1)}, u32[]{:S(2)}, u32[]{:S(2)}) collective-permute-start(bf16[2,256,384]{2,1,0:T(8,128)(2,1)S(1)} %get-tuple-element.54), channel_id=1, source_target_pairs={{0,28},{8,20},{16,12},{24,4},{1,29},{9,21},{17,13},{25,5},{2,30},{... | collective-permute-start | bytes 1179656 | tf_op jit(solution)/shard_map/ppermute | solution.py:128
  94.2 6.6 %collective-permute-start.24 = (bf16[2,256,384]{2,1,0:T(8,128)(2,1)S(1)}, bf16[2,256,384]{2,1,0:T(8,128)(2,1)S(1)}, u32[]{:S(2)}, u32[]{:S(2)}) collective-permute-start(bf16[2,256,384]{2,1,0:T(8,128)(2,1)S(1)} %get-tuple-element.54), channel_id=1, source_target_pairs={{4,28},{12,20},{20,12},{28,4},{5,29},{13,21},{21,13},{29,5},{6,30}... | collective-permute-start | bytes 1179656 | tf_op jit(solution)/shard_map/ppermute | solution.py:128
  100.7 16.2 %collective-permute-start.26 = (bf16[256,768]{1,0:T(8,128)(2,1)S(1)}, bf16[256,768]{1,0:T(8,128)(2,1)S(1)}, u32[]{:S(2)}, u32[]{:S(2)}) collective-permute-start(bf16[256,768]{1,0:T(8,128)(2,1)S(1)} %add_convert_fusion), channel_id=1, source_target_pairs={{0,0},{1,5},{2,10},{3,15},{4,20},{5,17},{6,30},{7,27},{8,8},{9,13}... | collective-permute-start | bytes 1179656 | tf_op jit(solution)/shard_map/ppermute | solution.py:582
  111.1 7.7 %collective-permute-start.28 = (bf16[384,768]{1,0:T(8,128)(2,1)S(1)}, bf16[384,768]{1,0:T(8,128)(2,1)S(1)}, u32[]{:S(2)}, u32[]{:S(2)}) collective-permute-start(bf16[384,768]{1,0:T(8,128)(2,1)S(1)} %get-tuple-element.57), channel_id=1, source_target_pairs={{0,4},{4,0},{8,12},{12,8},{16,20},{20,16},{24,28},{28,24},{1,5},{5... | collective-permute-start | bytes 1769480 | tf_op jit(solution)/shard_map/ppermute | solution.py:128
  111.2 7.6 %collective-permute-start.29 = (bf16[384,768]{1,0:T(8,128)(2,1)S(1)}, bf16[384,768]{1,0:T(8,128)(2,1)S(1)}, u32[]{:S(2)}, u32[]{:S(2)}) collective-permute-start(bf16[384,768]{1,0:T(8,128)(2,1)S(1)} %get-tuple-element.58), channel_id=1, source_target_pairs={{0,4},{4,0},{8,12},{12,8},{16,20},{20,16},{24,28},{28,24},{1,5},{5... | collective-permute-start | bytes 1769480 | tf_op jit(solution)/shard_map/ppermute | solution.py:128
  111.7 7.2 %collective-permute-start.30 = (bf16[384,768]{1,0:T(8,128)(2,1)S(1)}, bf16[384,768]{1,0:T(8,128)(2,1)S(1)}, u32[]{:S(2)}, u32[]{:S(2)}) collective-permute-start(bf16[384,768]{1,0:T(8,128)(2,1)S(1)} %get-tuple-element.59), channel_id=1, source_target_pairs={{0,4},{4,0},{8,12},{12,8},{16,20},{20,16},{24,28},{28,24},{1,5},{5... | collective-permute-start | bytes 1769480 | tf_op jit(solution)/shard_map/ppermute | solution.py:128
  116.9 14.8 %collective-permute-start.27 = (bf16[256,768]{1,0:T(8,128)(2,1)S(1)}, bf16[256,768]{1,0:T(8,128)(2,1)S(1)}, u32[]{:S(2)}, u32[]{:S(2)}) collective-permute-start(bf16[256,768]{1,0:T(8,128)(2,1)S(1)} %collective-permute-done.26), channel_id=1, source_target_pairs={{0,0},{5,4},{10,8},{15,12},{20,20},{17,16},{30,28},{27,24},{8,9},{... | collective-permute-start | bytes 1179656 | tf_op jit(solution)/shard_map/ppermute | solution.py:591

commit v17 on v16

--- a/solution.py
+++ b/solution.py
@@ -308,7 +308,7 @@
         out_specs=whole(),
         scratch_shapes=[pltpu.VMEM((6 * length, HD), jnp.bfloat16)] * 2
         + [pltpu.VMEM((6 * length, HD), jnp.float32)] * 2,
-        compiler_params=pltpu.CompilerParams(vmem_limit_bytes=12 * MIB),
+        compiler_params=pltpu.CompilerParams(vmem_limit_bytes=8 * MIB),
         cost_estimate=pl.CostEstimate(
             flops=heads * 4 * 5 * 2 * length * 3 * length * HD * 2,
             bytes_accessed=heads * 2 * length * 7 * HD * 4,
@@ -411,7 +411,7 @@
         in_specs=[whole(pltpu.SMEM)] + [whole()] * (len(grads) + 1),
         out_specs=[whole()] * 4,
         scratch_shapes=[pltpu.VMEM((4, length, rows), jnp.bfloat16)],
-        compiler_params=pltpu.CompilerParams(vmem_limit_bytes=16 * MIB),
+        compiler_params=pltpu.CompilerParams(vmem_limit_bytes=12 * MIB),
         cost_estimate=pl.CostEstimate(
             flops=8 * length * rows * depth,
             bytes_accessed=8 * length * (rows + depth) + 2 * rows * depth,
@@ -460,7 +460,7 @@
         in_specs=[whole(pltpu.SMEM)] + [whole()] * (6 + len(grads) + len(received)),
         out_specs=[whole()] * 3,
         scratch_shapes=[pltpu.VMEM((rows, 4 * length), jnp.bfloat16)],
-        compiler_params=pltpu.CompilerParams(vmem_limit_bytes=16 * MIB),
+        compiler_params=pltpu.CompilerParams(vmem_limit_bytes=12 * MIB),
         cost_estimate=pl.CostEstimate(
             flops=8 * rows * 3 * cols * length,
             bytes_accessed=8 * length * (rows + 3 * cols) + 12 * rows * cols,

time: 133 us -> 133 us (level)
  no operation moved by 1% of the time
where the time goes in v17:
time: 133 us; the launch traced here: 132 us
  waiting for transfers between devices  50 us (38%)
  starting transfers between devices  45.8 us (34%)
  Pallas kernels  30 us (23%)
  local copies, waits for them, and re-layouts  4.57 us (3%)
    ppermute x25, waiting for transfers between devices, moved(): return lax.ppermute(value, ('dp', 'view'), pairs)  31 us
    ppermute x25, starting transfers between devices, moved(): return lax.ppermute(value, ('dp', 'view'), pairs)  30.6 us
    pallas_call x2, Pallas kernels, weight_product(): pl.pallas_call(functools.partial(weight_kernel, mine, mean_scale, len(gra...  9.42 us
    pallas_call x2, Pallas kernels, attention(): pl.pallas_call(functools.partial(attention_kernel, HD ** (-0.5), kept), o...  9.35 us
    ppermute x1, waiting for transfers between devices, gather_body(): lax.ppermute(beside, ('dp', 'view', 'head'), [(spot(y ^ v % 2, v ^ z, z),...  7.08 us
    ppermute x1, starting transfers between devices, gather_body(): lax.ppermute(total, ('dp', 'view', 'head'), [(spot(y, v, z), spot(y ^ v %...  6.69 us
    pallas_call x1, Pallas kernels, input_product(): pl.pallas_call(functools.partial(input_kernel, len(grads) // 6), out_shap...  5.56 us
    ppermute x1, waiting for transfers between devices, gather_body(): lax.ppermute(total, ('dp', 'view', 'head'), [(spot(y, v, z), spot(y ^ v %...  5.14 us
  transfers between devices with their start and end apart: 31, of which 13 were waited for; matrix products, arithmetic and copies ran while one was open for 1% of the time, Pallas kernels for 16%

profile of v17, /device:TPU:26, one launch (start us, length us, event | category | flops | bytes accessed | tf_op | source)
XLA Modules:
  0.0 132.4 jit_solution(8505841352663253035)
XLA Ops:
  0.6 0.6 pad_add_fusion.place_ref
  1.3 2.8 %pack_heads.1 = (bf16[1,1040,128]{2,1,0:T(8,128)(2,1)}, bf16[1,1040,128]{2,1,0:T(8,128)(2,1)}, bf16[1,1040,128]{2,1,0:T(8,128)(2,1)}, bf16[1,1040,128]{2,1,0:T(8...) custom-call(s32[4]{0:T(128)} %pad_add_fusion.place_ref, s32[1,2]{1,0:T(1,128)} %links_ref.1, ...), custom_call_target="tpu_custom_call" | custom-call | tf_op jit(solution)/shard_map/pack_heads/pallas_call | solution.py:215
  4.0 0.5 collective-permute-start.1
  4.6 0.0 collective-permute-start
  4.6 1.6 %collective-permute-start.2 = (bf16[1,1040,128]{2,1,0:T(8,128)(2,1)}, bf16[1,1040,128]{2,1,0:T(8,128)(2,1)S(1)}, u32[]{:S(2)}, u32[]{:S(2)}) collective-permute-start(bf16[1,1040,128]{2,1,0:T(8,128)(2,1)} %get-tuple-element.37), channel_id=1, source_target_pairs={{0,12},{4,8},{8,4},{12,0},{16,28},{20,24},{24,20},{28,16},{1,13},{... | collective-permute-start | bytes 798728 | tf_op jit(solution)/shard_map/ppermute | solution.py:128
  6.2 0.0 collective-permute-start.3
  6.2 7.3 %collective-permute-done.1.x_in = bf16[1,1040,128]{2,1,0:T(8,128)(2,1)S(1)} collective-permute-done((bf16[1,1040,128]{2,1,0:T(8,128)(2,1)}, bf16[1,1040,128]{2,1,0:T(8,128)(2,1)S(1)}, u32[]{:S(2)}, u32[]{:S(2)}) %collective-permute-start.1) | collective-permute-done | bytes 266272 | tf_op jit(solution)/shard_map/ppermute | solution.py:128
  13.5 0.5 collective-permute-start.4
  14.1 0.0 collective-permute-done.mate_in
  14.1 3.3 %collective-permute-done.2.far_in = bf16[1,1040,128]{2,1,0:T(8,128)(2,1)S(1)} collective-permute-done((bf16[1,1040,128]{2,1,0:T(8,128)(2,1)}, bf16[1,1040,128]{2,1,0:T(8,128)(2,1)S(1)}, u32[]{:S(2)}, u32[]{:S(2)}) %collective-permute-start.2) | collective-permute-done | bytes 266272 | tf_op jit(solution)/shard_map/ppermute | solution.py:128
  17.4 0.9 copy-done.7
  18.4 4.4 %attention_gradients.2.refs_0_.refs_6_ = bf16[4,256,384]{2,1,0:T(8,128)(2,1)S(1)} custom-call(s32[4]{0:T(128)S(1)} %copy-done.3, bf16[1,1040,128]{2,1,0:T(8,128)(2,1)S(1)} %copy-done.7, bf16[1,1040,128]{2,1,0:T(8,128)(2,1)S(1)} %collective-permute-done.mate_in, bf16[1,1040,128]{2,1,0:T(8,128)(2,1)S(1)} %collective-permute-done.1.x_in, ...), custom_call_target="tpu_custom_call" | custom-call | flops 2013265920 | bytes 1835008 | tf_op jit(solution)/shard_map/attention_gradients/pallas_call | solution.py:304
  22.8 1.1 turn_weights.1.own_ref
  23.9 1.7 %collective-permute-start.16 = (bf16[2304,384]{1,0:T(8,128)(2,1)S(1)}, bf16[2304,384]{1,0:T(8,128)(2,1)}, u32[]{:S(2)}, u32[]{:S(2)}) collective-permute-start(bf16[2304,384]{1,0:T(8,128)(2,1)S(1)} %turn_weights.1.own_ref), channel_id=1, source_target_pairs={{0,4},{4,0},{8,12},{12,8},{16,20},{20,16},{24,28},{28,24},{1,5},{5... | collective-permute-start | bytes 5308424 | tf_op jit(solution)/shard_map/ppermute | solution.py:128
  25.6 0.1 collective-permute-start.5
  25.7 1.5 %collective-permute-start.10 = (bf16[4,256,384]{2,1,0:T(8,128)(2,1)S(1)}, bf16[4,256,384]{2,1,0:T(8,128)(2,1)S(1)}, u32[]{:S(2)}, u32[]{:S(2)}) collective-permute-start(bf16[4,256,384]{2,1,0:T(8,128)(2,1)S(1)} %attention_gradients.2.refs_0_.refs_6_), channel_id=1, source_target_pairs={{0,20},{4,8},{8,28},{12,0},{16,4},{20,24},{24,12},{28,16},{1,21},{... | collective-permute-start | bytes 2359304 | tf_op jit(solution)/shard_map/ppermute | solution.py:128
  27.3 0.5 collective-permute-start.8
  27.8 0.7 copy-done.5
  28.5 1.3 collective-permute-start.6
  29.9 0.9 copy-done.4
  30.8 0.9 copy-done.6
  31.8 4.9 %attention_gradients.3.refs_1_.refs_7_ = bf16[2,256,384]{2,1,0:T(8,128)(2,1)S(1)} custom-call(s32[4]{0:T(128)S(1)} %copy-done.3, bf16[1,1040,128]{2,1,0:T(8,128)(2,1)S(1)} %copy-done.4, bf16[1,1040,128]{2,1,0:T(8,128)(2,1)S(1)} %copy-done.6, bf16[1,1040,128]{2,1,0:T(8,128)(2,1)} %collective-permute-done.4.x_in, ...), custom_call_target="tpu_custom_call" | custom-call | flops 2013265920 | bytes 1835008 | tf_op jit(solution)/shard_map/attention_gradients/pallas_call | solution.py:304
  36.7 2.1 %collective-permute-start.11 = (bf16[2,256,384]{2,1,0:T(8,128)(2,1)S(1)}, bf16[2,256,384]{2,1,0:T(8,128)(2,1)S(1)}, u32[]{:S(2)}, u32[]{:S(2)}) collective-permute-start(bf16[2,256,384]{2,1,0:T(8,128)(2,1)S(1)} %attention_gradients.3.refs_1_.refs_7_), channel_id=1, source_target_pairs={{0,20},{4,8},{8,28},{12,0},{16,4},{20,24},{24,12},{28,16},{1,21},{... | collective-permute-start | bytes 1179656 | tf_op jit(solution)/shard_map/ppermute | solution.py:128
  38.8 0.3 dynamic-slice_bitcast_fusion.1
  39.1 0.1 pad_maximum_fusion.2
  39.2 0.1 pad_maximum_fusion
  39.3 5.6 %collective-permute-done.10.refs_6_.refs_12_ = bf16[4,256,384]{2,1,0:T(8,128)(2,1)S(1)} collective-permute-done((bf16[4,256,384]{2,1,0:T(8,128)(2,1)S(1)}, bf16[4,256,384]{2,1,0:T(8,128)(2,1)S(1)}, u32[]{:S(2)}, u32[]{:S(2)}) %collective-permute-start.10) | collective-permute-done | bytes 786464 | tf_op jit(solution)/shard_map/ppermute | solution.py:128
  44.8 0.3 collective-permute-start.9
  45.2 2.7 %collective-permute-done.8.refs_4_.refs_10_ = bf16[4,256,384]{2,1,0:T(8,128)(2,1)} collective-permute-done((bf16[4,256,384]{2,1,0:T(8,128)(2,1)S(1)}, bf16[4,256,384]{2,1,0:T(8,128)(2,1)}, u32[]{:S(2)}, u32[]{:S(2)}) %collective-permute-start.8) | collective-permute-done | bytes 786464 | tf_op jit(solution)/shard_map/ppermute | solution.py:128
  47.8 1.3 collective-permute-start.7
  49.1 3.2 %collective-permute-start.14 = (bf16[4,256,384]{2,1,0:T(8,128)(2,1)}, bf16[4,256,384]{2,1,0:T(8,128)(2,1)S(1)}, u32[]{:S(2)}, u32[]{:S(2)}) collective-permute-start(bf16[4,256,384]{2,1,0:T(8,128)(2,1)} %collective-permute-done.8.refs_4_.refs_10_), channel_id=1, source_target_pairs={{0,20},{8,28},{16,4},{24,12},{1,21},{9,29},{17,5},{25,13},{2,22},{... | collective-permute-start | bytes 2359304 | tf_op jit(solution)/shard_map/ppermute | solution.py:128
  52.3 0.7 collective-permute-start.12
  53.0 0.9 collective-permute-done.9.refs_5_.refs_11_
  54.0 3.6 %collective-permute-start.15 = (bf16[2,256,384]{2,1,0:T(8,128)(2,1)S(1)}, bf16[2,256,384]{2,1,0:T(8,128)(2,1)S(1)}, u32[]{:S(2)}, u32[]{:S(2)}) collective-permute-start(bf16[2,256,384]{2,1,0:T(8,128)(2,1)S(1)} %collective-permute-done.9.refs_5_.refs_11_), channel_id=1, source_target_pairs={{0,20},{8,28},{16,4},{24,12},{1,21},{9,29},{17,5},{25,13},{2,22},{... | collective-permute-start | bytes 1179656 | tf_op jit(solution)/shard_map/ppermute | solution.py:128
  57.6 0.7 collective-permute-start.13
  58.3 1.8 %join_weights.1.refs_12_ = bf16[2304,768]{1,0:T(8,128)(2,1)S(1)} custom-call(s32[4]{0:T(128)S(1)} %copy-done.3, bf16[2304,384]{1,0:T(8,128)(2,1)S(1)} %turn_weights.1.own_ref, bf16[2304,384]{1,0:T(8,128)(2,1)} %collective-permute-done.16.mate_ref), custom_call_target="tpu_custom_call" | custom-call | tf_op jit(solution)/shard_map/join_weights/pallas_call | solution.py:351
  60.1 6.1 %collective-permute-done.15.refs_11_.refs_17_ = bf16[2,256,384]{2,1,0:T(8,128)(2,1)S(1)} collective-permute-done((bf16[2,256,384]{2,1,0:T(8,128)(2,1)S(1)}, bf16[2,256,384]{2,1,0:T(8,128)(2,1)S(1)}, u32[]{:S(2)}, u32[]{:S(2)}) %collective-permute-start.15) | collective-permute-done | bytes 393248 | tf_op jit(solution)/shard_map/ppermute | solution.py:128
  66.2 5.6 %input_gradient.1 = (bf16[256,768]{1,0:T(8,128)(2,1)S(1)}, bf16[256,768]{1,0:T(8,128)(2,1)S(1)}, bf16[256,768]{1,0:T(8,128)(2,1)S(1)}, bf16[256,768]{1,0:T(8,128)(2,1)S(1)}) custom-call(s32[4]{0:T(128)S(1)} %copy-done.3, bf16[4,256,384]{2,1,0:T(8,128)(2,1)S(1)} %attention_gradients.2.refs_0_.refs_6_, ...), custom_call_target="tpu_custom_call" | custom-call | flops 3623878656 | bytes 9830400 | tf_op jit(solution)/shard_map/input_gradient/pallas_call | solution.py:408
  71.8 2.4 %collective-permute-start.19 = (bf16[256,768]{1,0:T(8,128)(2,1)S(1)}, bf16[256,768]{1,0:T(8,128)(2,1)S(1)}, u32[]{:S(2)}, u32[]{:S(2)}) collective-permute-start(bf16[256,768]{1,0:T(8,128)(2,1)S(1)} %get-tuple-element.49), channel_id=1, source_target_pairs={{0,1},{3,2},{4,5},{7,6},{8,9},{11,10},{12,13},{15,14},{16,17},{19,... | collective-permute-start | bytes 1179656 | tf_op jit(solution)/shard_map/ppermute | solution.py:554
  74.1 0.7 collective-permute-start.18
  74.8 1.1 collective-permute-start.17
  75.9 0.6 collective-permute-start.21
  76.6 2.7 %collective-permute-start.22 = (bf16[2,256,384]{2,1,0:T(8,128)(2,1)S(1)}, bf16[2,256,384]{2,1,0:T(8,128)(2,1)S(1)}, u32[]{:S(2)}, u32[]{:S(2)}) collective-permute-start(bf16[2,256,384]{2,1,0:T(8,128)(2,1)S(1)} %get-tuple-element.52), channel_id=1, source_target_pairs={{0,20},{4,8},{8,28},{12,0},{16,4},{20,24},{24,12},{28,16},{1,21},{... | collective-permute-start | bytes 1179656 | tf_op jit(solution)/shard_map/ppermute | solution.py:128
  79.3 2.7 %collective-permute-done.19 = bf16[256,768]{1,0:T(8,128)(2,1)S(1)} collective-permute-done((bf16[256,768]{1,0:T(8,128)(2,1)S(1)}, bf16[256,768]{1,0:T(8,128)(2,1)S(1)}, u32[]{:S(2)}, u32[]{:S(2)}) %collective-permute-start.19) | collective-permute-done | bytes 393248 | tf_op jit(solution)/shard_map/ppermute | solution.py:554
  82.0 0.1 add_convert_fusion.1
  82.1 2.4 %collective-permute-start.20 = (bf16[256,768]{1,0:T(8,128)(2,1)S(1)}, bf16[256,768]{1,0:T(8,128)(2,1)S(1)}, u32[]{:S(2)}, u32[]{:S(2)}) collective-permute-start(bf16[256,768]{1,0:T(8,128)(2,1)S(1)} %add_convert_fusion.1), channel_id=1, source_target_pairs={{0,2},{1,3},{2,0},{3,1},{4,6},{5,7},{6,4},{7,5},{8,10},{9,11},{10,... | collective-permute-start | bytes 1179656 | tf_op jit(solution)/shard_map/ppermute | solution.py:558
  84.5 1.6 %collective-permute-done.21.refs_2_ = bf16[2,256,384]{2,1,0:T(8,128)(2,1)S(1)} collective-permute-done((bf16[2,256,384]{2,1,0:T(8,128)(2,1)S(1)}, bf16[2,256,384]{2,1,0:T(8,128)(2,1)S(1)}, u32[]{:S(2)}, u32[]{:S(2)}) %collective-permute-start.21) | collective-permute-done | bytes 393248 | tf_op jit(solution)/shard_map/ppermute | solution.py:128
  86.1 1.9 %collective-permute-done.22.refs_3_ = bf16[2,256,384]{2,1,0:T(8,128)(2,1)S(1)} collective-permute-done((bf16[2,256,384]{2,1,0:T(8,128)(2,1)S(1)}, bf16[2,256,384]{2,1,0:T(8,128)(2,1)S(1)}, u32[]{:S(2)}, u32[]{:S(2)}) %collective-permute-start.22) | collective-permute-done | bytes 393248 | tf_op jit(solution)/shard_map/ppermute | solution.py:128
  87.9 1.3 collective-permute-start.23
  89.2 4.9 %collective-permute-start.25 = (bf16[2,256,384]{2,1,0:T(8,128)(2,1)S(1)}, bf16[2,256,384]{2,1,0:T(8,128)(2,1)S(1)}, u32[]{:S(2)}, u32[]{:S(2)}) collective-permute-start(bf16[2,256,384]{2,1,0:T(8,128)(2,1)S(1)} %get-tuple-element.54), channel_id=1, source_target_pairs={{0,28},{8,20},{16,12},{24,4},{1,29},{9,21},{17,13},{25,5},{2,30},{... | collective-permute-start | bytes 1179656 | tf_op jit(solution)/shard_map/ppermute | solution.py:128
  94.2 0.7 collective-permute-start.24
  94.9 4.0 %collective-permute-done.20 = bf16[256,768]{1,0:T(8,128)(2,1)S(1)} collective-permute-done((bf16[256,768]{1,0:T(8,128)(2,1)S(1)}, bf16[256,768]{1,0:T(8,128)(2,1)S(1)}, u32[]{:S(2)}, u32[]{:S(2)}) %collective-permute-start.20) | collective-permute-done | bytes 393248 | tf_op jit(solution)/shard_map/ppermute | solution.py:558
  98.9 0.2 add_convert_fusion
  99.1 1.6 %collective-permute-done.25.refs_5_ = bf16[2,256,384]{2,1,0:T(8,128)(2,1)S(1)} collective-permute-done((bf16[2,256,384]{2,1,0:T(8,128)(2,1)S(1)}, bf16[2,256,384]{2,1,0:T(8,128)(2,1)S(1)}, u32[]{:S(2)}, u32[]{:S(2)}) %collective-permute-start.25) | collective-permute-done | bytes 393248 | tf_op jit(solution)/shard_map/ppermute | solution.py:128
  100.7 6.7 %collective-permute-start.26 = (bf16[256,768]{1,0:T(8,128)(2,1)S(1)}, bf16[256,768]{1,0:T(8,128)(2,1)S(1)}, u32[]{:S(2)}, u32[]{:S(2)}) collective-permute-start(bf16[256,768]{1,0:T(8,128)(2,1)S(1)} %add_convert_fusion), channel_id=1, source_target_pairs={{0,0},{1,5},{2,10},{3,15},{4,20},{5,17},{6,30},{7,27},{8,8},{9,13}... | collective-permute-start | bytes 1179656 | tf_op jit(solution)/shard_map/ppermute | solution.py:582
  107.4 3.7 %weight_gradient_mate.1 = (bf16[384,768]{1,0:T(8,128)(2,1)S(1)}, bf16[384,768]{1,0:T(8,128)(2,1)S(1)}, bf16[384,768]{1,0:T(8,128)(2,1)S(1)}) custom-call(s32[4]{0:T(128)S(1)} %copy-done.3, bf16[2,256,384]{2,1,0:T(8,128)(2,1)S(1)} %get-tuple-element.53.refs_0_, bf16[2,256,384]{2,1,0:T(8,128)(2,1)S(1)} %collective-permute-done.23.refs_1_, ...), custom_call_target="tpu_custom_call" | custom-call | flops 1811939328 | bytes 9043968 | tf_op jit(solution)/shard_map/weight_gradient_mate/pallas_call | solution.py:457
  111.1 0.1 collective-permute-start.28
  111.2 0.5 collective-permute-start.29
  111.7 0.1 collective-permute-start.30
  111.8 5.1 %collective-permute-done.26 = bf16[256,768]{1,0:T(8,128)(2,1)S(1)} collective-permute-done((bf16[256,768]{1,0:T(8,128)(2,1)S(1)}, bf16[256,768]{1,0:T(8,128)(2,1)S(1)}, u32[]{:S(2)}, u32[]{:S(2)}) %collective-permute-start.26) | collective-permute-done | bytes 393248 | tf_op jit(solution)/shard_map/ppermute | solution.py:582
  116.9 1.9 %collective-permute-start.27 = (bf16[256,768]{1,0:T(8,128)(2,1)S(1)}, bf16[256,768]{1,0:T(8,128)(2,1)S(1)}, u32[]{:S(2)}, u32[]{:S(2)}) collective-permute-start(bf16[256,768]{1,0:T(8,128)(2,1)S(1)} %collective-permute-done.26), channel_id=1, source_target_pairs={{0,0},{5,4},{10,8},{15,12},{20,20},{17,16},{30,28},{27,24},{8,9},{... | collective-permute-start | bytes 1179656 | tf_op jit(solution)/shard_map/ppermute | solution.py:591
  118.8 5.7 %weight_gradient_own.1 = (f32[384,768]{1,0:T(8,128)}, f32[384,768]{1,0:T(8,128)}, f32[384,768]{1,0:T(8,128)}) custom-call(s32[4]{0:T(128)S(1)} %copy-done.3, bf16[2,256,384]{2,1,0:T(8,128)(2,1)S(1)} %get-tuple-element.53.refs_0_, bf16[2,256,384]{2,1,0:T(8,128)(2,1)S(1)} %collective-permute-done.23.refs_1_, ...), custom_call_target="tpu_custom_call" | custom-call | flops 1811939328 | bytes 9043968 | tf_op jit(solution)/shard_map/weight_gradient_own/pallas_call | solution.py:457
  124.6 7.1 %collective-permute-done.27 = bf16[256,768]{1,0:T(8,128)(2,1)S(1)} collective-permute-done((bf16[256,768]{1,0:T(8,128)(2,1)S(1)}, bf16[256,768]{1,0:T(8,128)(2,1)S(1)}, u32[]{:S(2)}, u32[]{:S(2)}) %collective-permute-start.27) | collective-permute-done | bytes 393248 | tf_op jit(solution)/shard_map/ppermute | solution.py:591
  131.7 0.7 copy.14
  (31 shorter events, 0.1 us)
Async XLA Ops:
  1.3 16.1 %copy-start.3 = (s32[4]{0:T(128)S(1)}, s32[4]{0:T(128)}, u32[]{:S(2)}) copy-start(s32[4]{0:T(128)} %pad_add_fusion.place_ref) | copy-start | bytes 52
  4.0 9.5 %collective-permute-start.1 = (bf16[1,1040,128]{2,1,0:T(8,128)(2,1)}, bf16[1,1040,128]{2,1,0:T(8,128)(2,1)S(1)}, u32[]{:S(2)}, u32[]{:S(2)}) collective-permute-start(bf16[1,1040,128]{2,1,0:T(8,128)(2,1)} %get-tuple-element.36), channel_id=1, source_target_pairs={{0,8},{4,12},{8,0},{12,4},{16,24},{20,28},{24,16},{28,20},{1,9},{5... | collective-permute-start | bytes 798728 | tf_op jit(solution)/shard_map/ppermute | solution.py:128
  4.6 9.5 %collective-permute-start = (bf16[1,1040,128]{2,1,0:T(8,128)(2,1)}, bf16[1,1040,128]{2,1,0:T(8,128)(2,1)S(1)}, u32[]{:S(2)}, u32[]{:S(2)}) collective-permute-start(bf16[1,1040,128]{2,1,0:T(8,128)(2,1)} %get-tuple-element.35), channel_id=1, source_target_pairs={{0,4},{4,0},{8,12},{12,8},{16,20},{20,16},{24,28},{28,24},{1,5},{5... | collective-permute-start | bytes 798728 | tf_op jit(solution)/shard_map/ppermute | solution.py:128
  4.6 12.8 %collective-permute-start.2 = (bf16[1,1040,128]{2,1,0:T(8,128)(2,1)}, bf16[1,1040,128]{2,1,0:T(8,128)(2,1)S(1)}, u32[]{:S(2)}, u32[]{:S(2)}) collective-permute-start(bf16[1,1040,128]{2,1,0:T(8,128)(2,1)} %get-tuple-element.37), channel_id=1, source_target_pairs={{0,12},{4,8},{8,4},{12,0},{16,28},{20,24},{24,20},{28,16},{1,13},{... | collective-permute-start | bytes 798728 | tf_op jit(solution)/shard_map/ppermute | solution.py:128
  6.2 21.6 %collective-permute-start.3 = (bf16[1,1040,128]{2,1,0:T(8,128)(2,1)}, bf16[1,1040,128]{2,1,0:T(8,128)(2,1)S(1)}, u32[]{:S(2)}, u32[]{:S(2)}) collective-permute-start(bf16[1,1040,128]{2,1,0:T(8,128)(2,1)} %get-tuple-element.42.own), channel_id=1, source_target_pairs={{0,4},{4,0},{8,12},{12,8},{16,20},{20,16},{24,28},{28,24},{1,5},{5... | collective-permute-start | bytes 798728 | tf_op jit(solution)/shard_map/ppermute | solution.py:128
  13.5 12.1 %collective-permute-start.4 = (bf16[1,1040,128]{2,1,0:T(8,128)(2,1)}, bf16[1,1040,128]{2,1,0:T(8,128)(2,1)}, u32[]{:S(2)}, u32[]{:S(2)}) collective-permute-start(bf16[1,1040,128]{2,1,0:T(8,128)(2,1)} %get-tuple-element.44), channel_id=1, source_target_pairs={{0,8},{4,12},{8,0},{12,4},{16,24},{20,28},{24,16},{28,20},{1,9},{5... | collective-permute-start | bytes 798728 | tf_op jit(solution)/shard_map/ppermute | solution.py:128
  17.4 1.0 copy-start.7
  18.4 4.5 %copy-start = (bf16[384,768]{1,0:T(8,128)(2,1)S(1)}, bf16[384,768]{1,0:T(8,128)(2,1)}, u32[]{:S(2)}) copy-start(bf16[384,768]{1,0:T(8,128)(2,1)} %q_ref) | copy-start | bytes 1769476
  18.4 4.5 %copy-start.1 = (bf16[384,768]{1,0:T(8,128)(2,1)S(1)}, bf16[384,768]{1,0:T(8,128)(2,1)}, u32[]{:S(2)}) copy-start(bf16[384,768]{1,0:T(8,128)(2,1)} %k_ref) | copy-start | bytes 1769476
  18.4 4.5 %copy-start.2 = (bf16[384,768]{1,0:T(8,128)(2,1)S(1)}, bf16[384,768]{1,0:T(8,128)(2,1)}, u32[]{:S(2)}) copy-start(bf16[384,768]{1,0:T(8,128)(2,1)} %v_ref) | copy-start | bytes 1769476
  23.9 34.4 %collective-permute-start.16 = (bf16[2304,384]{1,0:T(8,128)(2,1)S(1)}, bf16[2304,384]{1,0:T(8,128)(2,1)}, u32[]{:S(2)}, u32[]{:S(2)}) collective-permute-start(bf16[2304,384]{1,0:T(8,128)(2,1)S(1)} %turn_weights.1.own_ref), channel_id=1, source_target_pairs={{0,4},{4,0},{8,12},{12,8},{16,20},{20,16},{24,28},{28,24},{1,5},{5... | collective-permute-start | bytes 5308424 | tf_op jit(solution)/shard_map/ppermute | solution.py:128
  25.6 4.2 %collective-permute-start.5 = (bf16[1,1040,128]{2,1,0:T(8,128)(2,1)}, bf16[1,1040,128]{2,1,0:T(8,128)(2,1)}, u32[]{:S(2)}, u32[]{:S(2)}) collective-permute-start(bf16[1,1040,128]{2,1,0:T(8,128)(2,1)} %collective-permute-done.4.x_in), channel_id=1, source_target_pairs={{0,4},{4,0},{8,12},{12,8},{16,20},{20,16},{24,28},{28,24},{1,5},{5... | collective-permute-start | bytes 798728 | tf_op jit(solution)/shard_map/ppermute | solution.py:128
  25.7 19.1 %collective-permute-start.10 = (bf16[4,256,384]{2,1,0:T(8,128)(2,1)S(1)}, bf16[4,256,384]{2,1,0:T(8,128)(2,1)S(1)}, u32[]{:S(2)}, u32[]{:S(2)}) collective-permute-start(bf16[4,256,384]{2,1,0:T(8,128)(2,1)S(1)} %attention_gradients.2.refs_0_.refs_6_), channel_id=1, source_target_pairs={{0,20},{4,8},{8,28},{12,0},{16,4},{20,24},{24,12},{28,16},{1,21},{... | collective-permute-start | bytes 2359304 | tf_op jit(solution)/shard_map/ppermute | solution.py:128
  27.3 20.6 %collective-permute-start.8 = (bf16[4,256,384]{2,1,0:T(8,128)(2,1)S(1)}, bf16[4,256,384]{2,1,0:T(8,128)(2,1)}, u32[]{:S(2)}, u32[]{:S(2)}) collective-permute-start(bf16[4,256,384]{2,1,0:T(8,128)(2,1)S(1)} %attention_gradients.2.refs_0_.refs_6_), channel_id=1, source_target_pairs={{0,8},{4,20},{8,0},{12,28},{16,24},{20,4},{24,16},{28,12},{1,9},{5... | collective-permute-start | bytes 2359304 | tf_op jit(solution)/shard_map/ppermute | solution.py:128
  27.8 0.7 copy-start.5
  28.5 20.6 %collective-permute-start.6 = (bf16[4,256,384]{2,1,0:T(8,128)(2,1)S(1)}, bf16[4,256,384]{2,1,0:T(8,128)(2,1)}, u32[]{:S(2)}, u32[]{:S(2)}) collective-permute-start(bf16[4,256,384]{2,1,0:T(8,128)(2,1)S(1)} %attention_gradients.2.refs_0_.refs_6_), channel_id=1, source_target_pairs={{4,0},{12,8},{20,16},{28,24},{5,1},{13,9},{21,17},{29,25},{6,2},{1... | collective-permute-start | bytes 2359304 | tf_op jit(solution)/shard_map/ppermute | solution.py:128
  29.9 1.0 copy-start.4
  30.8 1.0 copy-start.6
  31.8 7.0 %copy-start.8 = (bf16[1,1,256,3072]{3,2,1,0:T(8,128)(2,1)S(1)}, bf16[1,1,256,3072]{3,2,1,0:T(8,128)(2,1)}, u32[]{:S(2)}) copy-start(bf16[1,1,256,3072]{3,2,1,0:T(8,128)(2,1)} %param.9) | copy-start | bytes 4718596
  36.7 15.6 %collective-permute-start.11 = (bf16[2,256,384]{2,1,0:T(8,128)(2,1)S(1)}, bf16[2,256,384]{2,1,0:T(8,128)(2,1)S(1)}, u32[]{:S(2)}, u32[]{:S(2)}) collective-permute-start(bf16[2,256,384]{2,1,0:T(8,128)(2,1)S(1)} %attention_gradients.3.refs_1_.refs_7_), channel_id=1, source_target_pairs={{0,20},{4,8},{8,28},{12,0},{16,4},{20,24},{24,12},{28,16},{1,21},{... | collective-permute-start | bytes 1179656 | tf_op jit(solution)/shard_map/ppermute | solution.py:128
  44.8 9.1 %collective-permute-start.9 = (bf16[2,256,384]{2,1,0:T(8,128)(2,1)S(1)}, bf16[2,256,384]{2,1,0:T(8,128)(2,1)S(1)}, u32[]{:S(2)}, u32[]{:S(2)}) collective-permute-start(bf16[2,256,384]{2,1,0:T(8,128)(2,1)S(1)} %attention_gradients.3.refs_1_.refs_7_), channel_id=1, source_target_pairs={{0,8},{4,20},{8,0},{12,28},{16,24},{20,4},{24,16},{28,12},{1,9},{5... | collective-permute-start | bytes 1179656 | tf_op jit(solution)/shard_map/ppermute | solution.py:128
  47.8 6.1 %collective-permute-start.7 = (bf16[2,256,384]{2,1,0:T(8,128)(2,1)S(1)}, bf16[2,256,384]{2,1,0:T(8,128)(2,1)S(1)}, u32[]{:S(2)}, u32[]{:S(2)}) collective-permute-start(bf16[2,256,384]{2,1,0:T(8,128)(2,1)S(1)} %attention_gradients.3.refs_1_.refs_7_), channel_id=1, source_target_pairs={{4,0},{12,8},{20,16},{28,24},{5,1},{13,9},{21,17},{29,25},{6,2},{1... | collective-permute-start | bytes 1179656 | tf_op jit(solution)/shard_map/ppermute | solution.py:128
  49.1 17.0 %collective-permute-start.14 = (bf16[4,256,384]{2,1,0:T(8,128)(2,1)}, bf16[4,256,384]{2,1,0:T(8,128)(2,1)S(1)}, u32[]{:S(2)}, u32[]{:S(2)}) collective-permute-start(bf16[4,256,384]{2,1,0:T(8,128)(2,1)} %collective-permute-done.8.refs_4_.refs_10_), channel_id=1, source_target_pairs={{0,20},{8,28},{16,4},{24,12},{1,21},{9,29},{17,5},{25,13},{2,22},{... | collective-permute-start | bytes 2359304 | tf_op jit(solution)/shard_map/ppermute | solution.py:128
  52.3 13.9 %collective-permute-start.12 = (bf16[4,256,384]{2,1,0:T(8,128)(2,1)}, bf16[4,256,384]{2,1,0:T(8,128)(2,1)S(1)}, u32[]{:S(2)}, u32[]{:S(2)}) collective-permute-start(bf16[4,256,384]{2,1,0:T(8,128)(2,1)} %collective-permute-done.8.refs_4_.refs_10_), channel_id=1, source_target_pairs={{4,12},{12,4},{20,28},{28,20},{5,13},{13,5},{21,29},{29,21},{6,14}... | collective-permute-start | bytes 2359304 | tf_op jit(solution)/shard_map/ppermute | solution.py:128
  54.0 12.2 %collective-permute-start.15 = (bf16[2,256,384]{2,1,0:T(8,128)(2,1)S(1)}, bf16[2,256,384]{2,1,0:T(8,128)(2,1)S(1)}, u32[]{:S(2)}, u32[]{:S(2)}) collective-permute-start(bf16[2,256,384]{2,1,0:T(8,128)(2,1)S(1)} %collective-permute-done.9.refs_5_.refs_11_), channel_id=1, source_target_pairs={{0,20},{8,28},{16,4},{24,12},{1,21},{9,29},{17,5},{25,13},{2,22},{... | collective-permute-start | bytes 1179656 | tf_op jit(solution)/shard_map/ppermute | solution.py:128
  57.6 8.6 %collective-permute-start.13 = (bf16[2,256,384]{2,1,0:T(8,128)(2,1)S(1)}, bf16[2,256,384]{2,1,0:T(8,128)(2,1)S(1)}, u32[]{:S(2)}, u32[]{:S(2)}) collective-permute-start(bf16[2,256,384]{2,1,0:T(8,128)(2,1)S(1)} %collective-permute-done.9.refs_5_.refs_11_), channel_id=1, source_target_pairs={{4,12},{12,4},{20,28},{28,20},{5,13},{13,5},{21,29},{29,21},{6,14}... | collective-permute-start | bytes 1179656 | tf_op jit(solution)/shard_map/ppermute | solution.py:128
  71.8 10.2 %collective-permute-start.19 = (bf16[256,768]{1,0:T(8,128)(2,1)S(1)}, bf16[256,768]{1,0:T(8,128)(2,1)S(1)}, u32[]{:S(2)}, u32[]{:S(2)}) collective-permute-start(bf16[256,768]{1,0:T(8,128)(2,1)S(1)} %get-tuple-element.49), channel_id=1, source_target_pairs={{0,1},{3,2},{4,5},{7,6},{8,9},{11,10},{12,13},{15,14},{16,17},{19,... | collective-permute-start | bytes 1179656 | tf_op jit(solution)/shard_map/ppermute | solution.py:554
  74.1 20.7 %collective-permute-start.18 = (bf16[256,768]{1,0:T(8,128)(2,1)S(1)}, bf16[256,768]{1,0:T(8,128)(2,1)S(1)}, u32[]{:S(2)}, u32[]{:S(2)}) collective-permute-start(bf16[256,768]{1,0:T(8,128)(2,1)S(1)} %get-tuple-element.49), channel_id=1, source_target_pairs={{1,2},{2,1},{5,6},{6,5},{9,10},{10,9},{13,14},{14,13},{17,18},{18,... | collective-permute-start | bytes 1179656 | tf_op jit(solution)/shard_map/ppermute | solution.py:556
  74.8 19.3 %collective-permute-start.17 = (bf16[256,768]{1,0:T(8,128)(2,1)S(1)}, bf16[256,768]{1,0:T(8,128)(2,1)S(1)}, u32[]{:S(2)}, u32[]{:S(2)}) collective-permute-start(bf16[256,768]{1,0:T(8,128)(2,1)S(1)} %get-tuple-element.48), channel_id=1, source_target_pairs={{0,1},{1,0},{2,3},{3,2},{4,5},{5,4},{6,7},{7,6},{8,9},{9,8},{10,11... | collective-permute-start | bytes 1179656 | tf_op jit(solution)/shard_map/ppermute | solution.py:555
  75.9 10.1 %collective-permute-start.21 = (bf16[2,256,384]{2,1,0:T(8,128)(2,1)S(1)}, bf16[2,256,384]{2,1,0:T(8,128)(2,1)S(1)}, u32[]{:S(2)}, u32[]{:S(2)}) collective-permute-start(bf16[2,256,384]{2,1,0:T(8,128)(2,1)S(1)} %get-tuple-element.51), channel_id=1, source_target_pairs={{0,8},{4,20},{8,0},{12,28},{16,24},{20,4},{24,16},{28,12},{1,9},{5... | collective-permute-start | bytes 1179656 | tf_op jit(solution)/shard_map/ppermute | solution.py:128
  76.6 11.4 %collective-permute-start.22 = (bf16[2,256,384]{2,1,0:T(8,128)(2,1)S(1)}, bf16[2,256,384]{2,1,0:T(8,128)(2,1)S(1)}, u32[]{:S(2)}, u32[]{:S(2)}) collective-permute-start(bf16[2,256,384]{2,1,0:T(8,128)(2,1)S(1)} %get-tuple-element.52), channel_id=1, source_target_pairs={{0,20},{4,8},{8,28},{12,0},{16,4},{20,24},{24,12},{28,16},{1,21},{... | collective-permute-start | bytes 1179656 | tf_op jit(solution)/shard_map/ppermute | solution.py:128
  82.1 16.8 %collective-permute-start.20 = (bf16[256,768]{1,0:T(8,128)(2,1)S(1)}, bf16[256,768]{1,0:T(8,128)(2,1)S(1)}, u32[]{:S(2)}, u32[]{:S(2)}) collective-permute-start(bf16[256,768]{1,0:T(8,128)(2,1)S(1)} %add_convert_fusion.1), channel_id=1, source_target_pairs={{0,2},{1,3},{2,0},{3,1},{4,6},{5,7},{6,4},{7,5},{8,10},{9,11},{10,... | collective-permute-start | bytes 1179656 | tf_op jit(solution)/shard_map/ppermute | solution.py:558
  87.9 11.1 %collective-permute-start.23 = (bf16[2,256,384]{2,1,0:T(8,128)(2,1)S(1)}, bf16[2,256,384]{2,1,0:T(8,128)(2,1)S(1)}, u32[]{:S(2)}, u32[]{:S(2)}) collective-permute-start(bf16[2,256,384]{2,1,0:T(8,128)(2,1)S(1)} %get-tuple-element.53.refs_0_), channel_id=1, source_target_pairs={{4,0},{12,8},{20,16},{28,24},{5,1},{13,9},{21,17},{29,25},{6,2},{1... | collective-permute-start | bytes 1179656 | tf_op jit(solution)/shard_map/ppermute | solution.py:128
  89.2 11.5 %collective-permute-start.25 = (bf16[2,256,384]{2,1,0:T(8,128)(2,1)S(1)}, bf16[2,256,384]{2,1,0:T(8,128)(2,1)S(1)}, u32[]{:S(2)}, u32[]{:S(2)}) collective-permute-start(bf16[2,256,384]{2,1,0:T(8,128)(2,1)S(1)} %get-tuple-element.54), channel_id=1, source_target_pairs={{0,28},{8,20},{16,12},{24,4},{1,29},{9,21},{17,13},{25,5},{2,30},{... | collective-permute-start | bytes 1179656 | tf_op jit(solution)/shard_map/ppermute | solution.py:128
  94.2 6.6 %collective-permute-start.24 = (bf16[2,256,384]{2,1,0:T(8,128)(2,1)S(1)}, bf16[2,256,384]{2,1,0:T(8,128)(2,1)S(1)}, u32[]{:S(2)}, u32[]{:S(2)}) collective-permute-start(bf16[2,256,384]{2,1,0:T(8,128)(2,1)S(1)} %get-tuple-element.54), channel_id=1, source_target_pairs={{4,28},{12,20},{20,12},{28,4},{5,29},{13,21},{21,13},{29,5},{6,30}... | collective-permute-start | bytes 1179656 | tf_op jit(solution)/shard_map/ppermute | solution.py:128
  100.7 16.2 %collective-permute-start.26 = (bf16[256,768]{1,0:T(8,128)(2,1)S(1)}, bf16[256,768]{1,0:T(8,128)(2,1)S(1)}, u32[]{:S(2)}, u32[]{:S(2)}) collective-permute-start(bf16[256,768]{1,0:T(8,128)(2,1)S(1)} %add_convert_fusion), channel_id=1, source_target_pairs={{0,0},{1,5},{2,10},{3,15},{4,20},{5,17},{6,30},{7,27},{8,8},{9,13}... | collective-permute-start | bytes 1179656 | tf_op jit(solution)/shard_map/ppermute | solution.py:582
  111.1 7.7 %collective-permute-start.28 = (bf16[384,768]{1,0:T(8,128)(2,1)S(1)}, bf16[384,768]{1,0:T(8,128)(2,1)S(1)}, u32[]{:S(2)}, u32[]{:S(2)}) collective-permute-start(bf16[384,768]{1,0:T(8,128)(2,1)S(1)} %get-tuple-element.57), channel_id=1, source_target_pairs={{0,4},{4,0},{8,12},{12,8},{16,20},{20,16},{24,28},{28,24},{1,5},{5... | collective-permute-start | bytes 1769480 | tf_op jit(solution)/shard_map/ppermute | solution.py:128
  111.2 7.6 %collective-permute-start.29 = (bf16[384,768]{1,0:T(8,128)(2,1)S(1)}, bf16[384,768]{1,0:T(8,128)(2,1)S(1)}, u32[]{:S(2)}, u32[]{:S(2)}) collective-permute-start(bf16[384,768]{1,0:T(8,128)(2,1)S(1)} %get-tuple-element.58), channel_id=1, source_target_pairs={{0,4},{4,0},{8,12},{12,8},{16,20},{20,16},{24,28},{28,24},{1,5},{5... | collective-permute-start | bytes 1769480 | tf_op jit(solution)/shard_map/ppermute | solution.py:128
  111.7 7.2 %collective-permute-start.30 = (bf16[384,768]{1,0:T(8,128)(2,1)S(1)}, bf16[384,768]{1,0:T(8,128)(2,1)S(1)}, u32[]{:S(2)}, u32[]{:S(2)}) collective-permute-start(bf16[384,768]{1,0:T(8,128)(2,1)S(1)} %get-tuple-element.59), channel_id=1, source_target_pairs={{0,4},{4,0},{8,12},{12,8},{16,20},{20,16},{24,28},{28,24},{1,5},{5... | collective-permute-start | bytes 1769480 | tf_op jit(solution)/shard_map/ppermute | solution.py:128
  116.9 14.8 %collective-permute-start.27 = (bf16[256,768]{1,0:T(8,128)(2,1)S(1)}, bf16[256,768]{1,0:T(8,128)(2,1)S(1)}, u32[]{:S(2)}, u32[]{:S(2)}) collective-permute-start(bf16[256,768]{1,0:T(8,128)(2,1)S(1)} %collective-permute-done.26), channel_id=1, source_target_pairs={{0,0},{5,4},{10,8},{15,12},{20,20},{17,16},{30,28},{27,24},{8,9},{... | collective-permute-start | bytes 1179656 | tf_op jit(solution)/shard_map/ppermute | solution.py:591
